TPU v7x, 32 devices: a whole 2x2x4 slice. The times are simulated.
32 devices in a mesh: groups: 2 (over y), shard: 8 (over z, x), owner: 2 (over core).
Axes of the slice: x: 2, y: 2, z: 4, core: 2. Of those that a mesh axis runs over, the one named last changes fastest.
Arguments:
- embeddings: bfloat16 [4096, 768], P(('groups', 'shard', 'owner')), parts along dimension 0, may hold values from -6 to 6
- cluster_id: int32 [4096, 1], P(('groups', 'shard', 'owner')), parts along dimension 0, may hold values from 0 to 7; in each aligned block of 128 rows (0 to 127, 128 to 255, ...) at most 32 rows name the same one
- priority: int32 [4096], P(('groups', 'shard', 'owner')), parts along dimension 0, may hold values from 0 to 2047, each once
Outputs:
- dup_score: float32 [4096], P(('groups', 'shard', 'owner')), parts along dimension 0
- readout: float32 [4096, 768], P(('groups', 'shard', 'owner')), parts along dimension 0
There are 2 independent parts, one for each index of `groups`. A program takes and returns all parts, laid end to end along the dimension named above; each array names one. Nothing has to cross between parts.
Inputs may be any that keep to these rules, and one draw needn't show every extreme that they name: `cluster_id`: among the rows of one device no cluster is named more than 32 times. `priority`: all ranks within one part (one index of groups) are distinct.
All inputs are finite; a program needn't handle non-finite values.
Results may differ from a plain program's by a relative error of at most 0.0041.
Values may be sent and summed in bfloat16 or wider, within the bound.
No kernel may reach another device: no remote copies, remote signals or barrier semaphores. Data moves between devices by JAX's collectives and lax.ppermute only.
A program may use at most 64 MiB of HBM per device.

v0:
```python
import jax
import jax.numpy as jnp
from jax import lax
from jax.sharding import PartitionSpec as P


def make_unit(rows):
    wide = rows.astype(jnp.float32)
    scale = lax.rsqrt(jnp.mean(wide * wide, axis=-1, keepdims=True) + 1e-06) / jnp.sqrt(
        jnp.float32(rows.shape[-1])
    )
    return (wide * scale).astype(jnp.bfloat16)


def score_block(query_unit, query_rank, unit_keys, keys, key_rank):
    cosine = jnp.dot(query_unit, unit_keys.T, preferred_element_type=jnp.float32)
    weight = jax.nn.sigmoid(40.0 * (cosine - 0.05))
    valid = key_rank[None, :] >= 0
    earlier = valid & (key_rank[None, :] < query_rank[:, None])
    others = valid & (key_rank[None, :] != query_rank[:, None])
    dup = jnp.log1p(jnp.sum(jnp.where(earlier, weight, 0.0), axis=1))
    near = jnp.where(others, weight, 0.0)
    total = jnp.sum(near, axis=1)
    mixed = jnp.dot(near.astype(jnp.bfloat16), keys, preferred_element_type=jnp.float32)
    mixed = mixed / jnp.sqrt(1.0 + total)[:, None]
    return (dup, mixed)


def local(embeddings, cluster_id, priority):
    stored = embeddings.shape[0]
    width = embeddings.shape[1]
    shards = lax.axis_size("shard")
    places = max(2, 2 * stored // shards)
    labels = cluster_id[:, 0]
    member = (labels[:, None] == jnp.arange(shards, dtype=jnp.int32)[None, :]).astype(jnp.int32)
    before = jnp.sum(jnp.cumsum(member, axis=0) * member, axis=1) - 1
    slot = labels * places + before
    outbox = jnp.zeros((shards * places, width), jnp.bfloat16).at[slot].set(embeddings)
    outrank = jnp.full((shards * places,), -1, jnp.int32).at[slot].set(priority)
    outbox = outbox.reshape(shards, places, width)
    outrank = outrank.reshape(shards, places)
    lane = lax.axis_index("owner")
    arrived, arrived_rank = (
        lax.all_to_all(outbox, "shard", split_axis=0, concat_axis=0, tiled=True),
        lax.all_to_all(outrank, "shard", split_axis=0, concat_axis=0, tiled=True),
    )
    keys, key_rank = (
        lax.all_gather(arrived, "owner", axis=0, tiled=True),
        lax.all_gather(arrived_rank, "owner", axis=0, tiled=True),
    )
    keys = keys.reshape(-1, width)
    key_rank = key_rank.reshape(-1)
    unit_keys = make_unit(keys)
    query_unit = lax.dynamic_slice_in_dim(unit_keys, lane * shards * places, shards * places, 0)
    query_rank = arrived_rank.reshape(-1)
    queries = shards * places
    blocks = queries // queries

    def one_block(pieces):
        return score_block(pieces[0], pieces[1], unit_keys, keys, key_rank)

    dup, mixed = lax.map(
        one_block, (query_unit.reshape(blocks, queries, width), query_rank.reshape(blocks, queries))
    )
    back_mixed, back_dup = (
        lax.all_to_all(
            mixed.reshape(shards, places, width), "shard", split_axis=0, concat_axis=0, tiled=True
        ),
        lax.all_to_all(
            dup.reshape(shards, places), "shard", split_axis=0, concat_axis=0, tiled=True
        ),
    )
    dup_score = back_dup.reshape(-1)[slot]
    readout = back_mixed.reshape(-1, width)[slot]
    return (dup_score, readout)


def solution(mesh):
    placed = (
        P(("groups", "shard", "owner"), None),
        P(("groups", "shard", "owner"), None),
        P(("groups", "shard", "owner")),
    )
    return jax.shard_map(
        local,
        mesh=mesh,
        in_specs=placed,
        out_specs=(P(("groups", "shard", "owner")), P(("groups", "shard", "owner"), None)),
        check_vma=False,
    )
```

profile of v0, /device:TPU:0, one launch (start us, length us, event | category | flops | bytes accessed | tf_op | source)
XLA Modules:
  0.0 71.3 jit_solution(18283272896060918083)
XLA Ops:
  0.6 0.7 %fusion.18 = s32[128,8]{1,0:T(8,128)S(1)} fusion(s32[128]{0:T(128)} %bitcast.18), kind=kLoop, calls=%fused_computation.30 | loop fusion | flops 2048 | bytes 4608 | tf_op jit(solution)/shard_map/convert_element_type | solution.py:35
  1.4 0.2 reduce_window_sum.11
  1.5 0.8 %select_reduce_fusion.1 = s32[128]{0:T(128)S(1)} fusion(s32[128,8]{1,0:T(8,128)S(1)} %reduce_window_sum.11, s32[128]{0:T(128)} %bitcast.19), kind=kLoop, calls=%fused_computation.28 | loop fusion | flops 2944 | bytes 5120 | tf_op jit(solution)/shard_map/reduce_sum | solution.py:36
  2.4 0.7 fusion.19
  3.0 1.1 %scatter_custom_fusion = s32[256]{0:T(256)S(1)} fusion(s32[128]{0:T(128)S(1)} %fusion.19, s32[128]{0:T(128)} %param.5, s32[]{:T(128)} %constant.20.clone.1), kind=kCustom, calls=%fused_computation.38 | custom fusion | bytes 1536 | tf_op jit(solution)/shard_map/scatter | solution.py:39
  4.2 0.7 all_to_all.18
  4.8 7.3 %all-to-all-start = ((s32[8,1,32]{2,1,0:T(1,128)}), s32[8,1,32]{2,1,0:T(1,128)S(1)}, u32[]{:S(2)}, u32[]{:S(2)}) async-start(s32[8,1,32]{2,1,0:T(1,128)} %all_to_all.18), calls=%async_computation | async-start | bytes 8192 | tf_op jit(solution)/shard_map/all_to_all | solution.py:45
  12.1 2.3 %scatter_custom_fusion.1 = bf16[256,768]{1,0:T(8,128)(2,1)} fusion(s32[128]{0:T(128)S(1)} %fusion.19, bf16[128,768]{1,0:T(8,128)(2,1)} %param.3, bf16[]{:T(256)} %constant.25.clone.1), kind=kCustom, calls=%fused_computation.26 | custom fusion | bytes 393728 | tf_op jit(solution)/shard_map/scatter | solution.py:38
  14.3 4.2 %all-to-all-done = s32[8,1,32]{2,1,0:T(1,128)S(1)} async-done(((s32[8,1,32]{2,1,0:T(1,128)}), s32[8,1,32]{2,1,0:T(1,128)S(1)}, u32[]{:S(2)}, u32[]{:S(2)}) %all-to-all-start) | async-done | bytes 1056 | tf_op jit(solution)/shard_map/all_to_all | solution.py:45
  18.6 3.5 %all-to-all-start.1 = ((bf16[8,32,768]{2,1,0:T(8,128)(2,1)}), bf16[8,32,768]{2,1,0:T(8,128)(2,1)S(1)}, u32[]{:S(2)}, u32[]{:S(2)}) async-start(bf16[8,32,768]{2,1,0:T(8,128)(2,1)} %bitcast.3), calls=%async_computation.1 | async-start | bytes 786432 | tf_op jit(solution)/shard_map/all_to_all | solution.py:44
  22.0 1.8 %all-gather = s32[16,1,32]{2,1,0:T(1,128)S(1)} all-gather(s32[8,1,32]{2,1,0:T(1,128)S(1)} %all-to-all-done), channel_id=2, replica_groups=mesh['groups'=2,'shard'=8,'owner'=2] {'owner'}, dimensions={0}, use_global_device_ids=true | all-gather | bytes 3072 | tf_op jit(solution)/shard_map/all_gather | solution.py:49
  23.8 0.5 broadcast.115
  24.3 0.7 reduce.10
  25.0 0.1 broadcast_in_dim_reshape.6
  25.1 0.7 reduce.11
  25.7 0.1 lt.35
  25.8 6.6 %all-to-all-done.1 = bf16[8,32,768]{2,1,0:T(8,128)(2,1)S(1)} async-done(((bf16[8,32,768]{2,1,0:T(8,128)(2,1)}), bf16[8,32,768]{2,1,0:T(8,128)(2,1)S(1)}, u32[]{:S(2)}, u32[]{:S(2)}) %all-to-all-start.1) | async-done | bytes 393248 | tf_op jit(solution)/shard_map/all_to_all | solution.py:44
  32.5 2.4 %all_gather.7 = bf16[16,32,768]{2,1,0:T(8,128)(2,1)S(1)} all-gather(bf16[8,32,768]{2,1,0:T(8,128)(2,1)S(1)} %all-to-all-done.1), channel_id=1, replica_groups=mesh['groups'=2,'shard'=8,'owner'=2] {'owner'}, dimensions={0}, use_global_device_ids=true | all-gather | bytes 1179648 | tf_op jit(solution)/shard_map/all_gather | solution.py:48
  34.8 0.2 fusion
  35.1 0.1 div.34
  35.1 0.2 fusion.1
  35.3 0.1 dynamic-slice.1
  35.4 0.7 %fusion.7 = (f32[256]{0:T(256)S(1)}, f32[256]{0:T(256)S(1)}, bf16[256,512]{1,0:T(8,128)(2,1)S(1)}) fusion(s32[512]{0:T(512)S(1)} %broadcast_in_dim_reshape.6, s32[256]{0:T(256)S(1)} %lt.35, pred[512]{0:T(512)(128)(4,1)S(1)} %broadcast_compare_fusion, bf16[512,768]{1,0:T(8,128)(2,1)S(1)} %bitcast.17, f32[256]{0:T(256)S(1)} %dynamic-slice.1, ...), kind=kOutput, calls=%fused_computation.18 | convolution fusion | flops 203750912 | bytes 1448452 | tf_op jit(solution)/shard_map/while/body/eval_jaxpr/dot_general | solution.py:16
  36.2 0.7 log1p.16
  36.9 3.7 %all-to-all-start.2 = ((f32[8,1,32]{2,1,0:T(1,128)}), f32[8,1,32]{2,1,0:T(1,128)S(1)}, u32[]{:S(2)}, u32[]{:S(2)}) async-start(f32[8,1,32]{2,1,0:T(1,128)} %log1p.16), calls=%async_computation.2 | async-start | bytes 8192 | tf_op jit(solution)/shard_map/all_to_all | solution.py:69
  40.5 1.3 %convolution_divide_fusion = f32[256,768]{1,0:T(8,128)} fusion(bf16[512,768]{1,0:T(8,128)(2,1)S(1)} %bitcast.16, f32[256]{0:T(256)S(1)} %add_sqrt_fusion, bf16[256,512]{1,0:T(8,128)(2,1)S(1)} %get-tuple-element.20, s32[512]{0:T(512)S(1)} %broadcast_in_dim_reshape.6, s32[256]{0:T(256)S(1)} %lt.35, pred[512]{0:T(512)(128)(4,1)S(1)} %broadcast_compare_fusion), kind=kOutput, calls=%fused_computation.8 | convolution fusion | flops 201916416 | bytes 1839616 | tf_op jit(solution)/shard_map/while/body/eval_jaxpr/dot_general | solution.py:24
  41.8 5.1 %all-to-all-done.2 = f32[8,1,32]{2,1,0:T(1,128)S(1)} async-done(((f32[8,1,32]{2,1,0:T(1,128)}), f32[8,1,32]{2,1,0:T(1,128)S(1)}, u32[]{:S(2)}, u32[]{:S(2)}) %all-to-all-start.2) | async-done | bytes 1056 | tf_op jit(solution)/shard_map/all_to_all | solution.py:69
  46.9 3.5 %all-to-all-start.3 = ((f32[8,32,768]{2,1,0:T(8,128)}), f32[8,32,768]{2,1,0:T(8,128)S(1)}, u32[]{:S(2)}, u32[]{:S(2)}) async-start(f32[8,32,768]{2,1,0:T(8,128)} %bitcast.6), calls=%async_computation.3 | async-start | bytes 1572864 | tf_op jit(solution)/shard_map/all_to_all | solution.py:66
  50.5 0.5 broadcast.117
  51.0 0.7 reduce.12
  51.7 0.1 reshape.98
  51.7 1.8 %gather_fusion = f32[128]{0:T(128)} fusion(f32[256]{0:T(256)S(1)} %reshape.98, s32[1024]{0:T(1024)S(1)} %pad_clamp_fusion), kind=kCustom, calls=%fused_computation | custom fusion | bytes 1536 | tf_op jit(solution)/shard_map/gather | solution.py:73
  53.5 16.3 %all-to-all-done.3 = f32[8,32,768]{2,1,0:T(8,128)S(1)} async-done(((f32[8,32,768]{2,1,0:T(8,128)}), f32[8,32,768]{2,1,0:T(8,128)S(1)}, u32[]{:S(2)}, u32[]{:S(2)}) %all-to-all-start.3) | async-done | bytes 786464 | tf_op jit(solution)/shard_map/all_to_all | solution.py:66
  69.8 1.6 %gather_fusion.1 = f32[128,768]{1,0:T(8,128)} fusion(f32[256,768]{1,0:T(8,128)S(1)} %bitcast.14, s32[1024]{0:T(1024)S(1)} %pad_clamp_fusion), kind=kCustom, calls=%fused_computation.1 | custom fusion | bytes 786944 | tf_op jit(solution)/shard_map/gather | solution.py:74
  (5 shorter events, 0.0 us)
Async XLA Ops:
  4.8 13.7 %all-to-all-start = ((s32[8,1,32]{2,1,0:T(1,128)}), s32[8,1,32]{2,1,0:T(1,128)S(1)}, u32[]{:S(2)}, u32[]{:S(2)}) async-start(s32[8,1,32]{2,1,0:T(1,128)} %all_to_all.18), calls=%async_computation | async-start | bytes 8192 | tf_op jit(solution)/shard_map/all_to_all | solution.py:45
  18.6 13.9 %all-to-all-start.1 = ((bf16[8,32,768]{2,1,0:T(8,128)(2,1)}), bf16[8,32,768]{2,1,0:T(8,128)(2,1)S(1)}, u32[]{:S(2)}, u32[]{:S(2)}) async-start(bf16[8,32,768]{2,1,0:T(8,128)(2,1)} %bitcast.3), calls=%async_computation.1 | async-start | bytes 786432 | tf_op jit(solution)/shard_map/all_to_all | solution.py:44
  36.9 10.1 %all-to-all-start.2 = ((f32[8,1,32]{2,1,0:T(1,128)}), f32[8,1,32]{2,1,0:T(1,128)S(1)}, u32[]{:S(2)}, u32[]{:S(2)}) async-start(f32[8,1,32]{2,1,0:T(1,128)} %log1p.16), calls=%async_computation.2 | async-start | bytes 8192 | tf_op jit(solution)/shard_map/all_to_all | solution.py:69
  46.9 22.9 %all-to-all-start.3 = ((f32[8,32,768]{2,1,0:T(8,128)}), f32[8,32,768]{2,1,0:T(8,128)S(1)}, u32[]{:S(2)}, u32[]{:S(2)}) async-start(f32[8,32,768]{2,1,0:T(8,128)} %bitcast.6), calls=%async_computation.3 | async-start | bytes 1572864 | tf_op jit(solution)/shard_map/all_to_all | solution.py:66
where the time goes:
time: 71.8 us; the launch traced here: 71.3 us
  waiting for transfers between devices  32.2 us (45%)
  starting transfers between devices  17.9 us (25%)
  local copies, waits for them, and re-layouts  9.46 us (13%)
  other arithmetic  4.83 us (7%)
  blocking collectives  4.15 us (6%)
  matrix products  2.04 us (3%)
  between operations  0.74 us (1%)
    all_to_all x1, waiting for transfers between devices, local(): lax.all_to_all(mixed.reshape(shards, places, width), 'shard', split_axis=...  16.3 us
    all_to_all x1, starting transfers between devices, local(): lax.all_to_all(outrank, 'shard', split_axis=0, concat_axis=0, tiled=True)  7.25 us
    all_to_all x1, waiting for transfers between devices, local(): lax.all_to_all(outbox, 'shard', split_axis=0, concat_axis=0, tiled=True)  6.62 us
    all_to_all x1, waiting for transfers between devices, local(): lax.all_to_all(dup.reshape(shards, places), 'shard', split_axis=0, concat...  5.08 us
    all_to_all x1, waiting for transfers between devices, local(): lax.all_to_all(outrank, 'shard', split_axis=0, concat_axis=0, tiled=True)  4.2 us
    all_to_all x1, starting transfers between devices, local(): lax.all_to_all(dup.reshape(shards, places), 'shard', split_axis=0, concat...  3.67 us
    all_to_all x1, starting transfers between devices, local(): lax.all_to_all(mixed.reshape(shards, places, width), 'shard', split_axis=...  3.55 us
    all_to_all x1, starting transfers between devices, local(): lax.all_to_all(outbox, 'shard', split_axis=0, concat_axis=0, tiled=True)  3.45 us
  transfers between devices with their start and end apart: 4, of which 4 were waited for; matrix products, arithmetic and copies ran while one was open for 12% of the time, Pallas kernels for 0%

commit v1 on v0

v1 whole, which is shorter than its diff:
```python
import jax
import jax.numpy as jnp
from jax import lax
from jax.experimental import pallas as pl
from jax.experimental.pallas import tpu as pltpu
from jax.sharding import PartitionSpec as P

EXTRA = 16
VMEM = 48 * 1024 * 1024


def make_unit(rows):
    wide = rows.astype(jnp.float32)
    scale = lax.rsqrt(jnp.mean(wide * wide, axis=-1, keepdims=True) + 1e-06) / jnp.sqrt(
        jnp.float32(rows.shape[-1])
    )
    return (wide * scale).astype(jnp.bfloat16)


def diagonal(count):
    down = lax.broadcasted_iota(jnp.int32, (count, count), 0)
    return down == lax.broadcasted_iota(jnp.int32, (count, count), 1)


def as_row(column):
    return jnp.sum(jnp.where(diagonal(column.shape[0]), column, 0.0), axis=0, keepdims=True)


def as_column(row):
    return jnp.sum(jnp.where(diagonal(row.shape[1]), row, 0.0), axis=1, keepdims=True)


def pack_kernel(rows_ref, label_ref, rank_ref, packed_ref):
    count, width = rows_ref.shape
    packed_ref[:count, :] = rows_ref[...]
    packed_ref[count:, :] = jnp.zeros((EXTRA, width), jnp.bfloat16)
    rank = rank_ref[...]
    high = lax.shift_right_logical(rank, 8)
    low = rank - lax.shift_left(high, 8)
    pieces = (
        as_row(label_ref[...].astype(jnp.float32)),
        high.astype(jnp.float32),
        low.astype(jnp.float32),
    )
    for at, piece in enumerate(pieces):
        packed_ref[count : count + EXTRA, at * count : (at + 1) * count] = jnp.broadcast_to(
            piece, (EXTRA, count)
        ).astype(jnp.bfloat16)


def labels_and_ranks(extra, count):
    line = extra.astype(jnp.float32)[:1]
    label, high, low = (line[:, at * count : (at + 1) * count] for at in range(3))
    return label, high * 256.0 + low


def score_kernel(own_ref, blocks_ref, dup_ref, mixed_ref, unit_ref, side_ref, sums_ref):
    step = pl.program_id(0)
    many, height, width = blocks_ref.shape
    count = height - EXTRA

    @pl.when(step == 0)
    def _():
        unit_ref[...] = make_unit(own_ref[:count, :])
        label, rank = labels_and_ranks(own_ref[count:, :], count)
        side_ref[:, 0:1] = as_column(label)
        side_ref[:, 1:2] = as_column(rank)
        sums_ref[...] = jnp.zeros_like(sums_ref)
        mixed_ref[...] = jnp.zeros_like(mixed_ref)

    own_label = side_ref[:, 0:1]
    own_rank = side_ref[:, 1:2]
    keys = jnp.concatenate([blocks_ref[at, :count, :] for at in range(many)], axis=0)
    sides = [labels_and_ranks(blocks_ref[at, count:, :], count) for at in range(many)]
    label = jnp.concatenate([side[0] for side in sides], axis=1)
    rank = jnp.concatenate([side[1] for side in sides], axis=1)
    cosine = lax.dot_general(
        unit_ref[...],
        make_unit(keys),
        (((1,), (1,)), ((), ())),
        preferred_element_type=jnp.float32,
    )
    weight = 1.0 / (1.0 + jnp.exp(-40.0 * (cosine - 0.05)))
    near = jnp.where((label == own_label) & (rank != own_rank), weight, 0.0)
    sums_ref[:, 0:1] += jnp.sum(jnp.where(rank < own_rank, near, 0.0), axis=1, keepdims=True)
    sums_ref[:, 1:2] += jnp.sum(near, axis=1, keepdims=True)
    mixed_ref[...] += jnp.dot(near.astype(jnp.bfloat16), keys, preferred_element_type=jnp.float32)

    @pl.when(step == pl.num_programs(0) - 1)
    def _():
        dup_ref[...] = as_row(jnp.log1p(sums_ref[:, 0:1]))
        mixed_ref[...] = mixed_ref[...] / jnp.sqrt(1.0 + sums_ref[:, 1:2])


def local(embeddings, cluster_id, priority):
    count, width = embeddings.shape
    packed = pl.pallas_call(
        pack_kernel,
        out_shape=jax.ShapeDtypeStruct((count + EXTRA, width), jnp.bfloat16),
        name="pack",
    )(embeddings, cluster_id, priority[None, :])
    blocks = lax.all_gather(packed, ("shard", "owner"), axis=0, tiled=False)
    total = blocks.shape[0]
    many = 2
    dup, mixed = pl.pallas_call(
        score_kernel,
        grid=(total // many,),
        in_specs=[
            pl.BlockSpec((count + EXTRA, width), lambda i: (0, 0)),
            pl.BlockSpec((many, count + EXTRA, width), lambda i: (i, 0, 0)),
        ],
        out_specs=[
            pl.BlockSpec((1, count), lambda i: (0, 0)),
            pl.BlockSpec((count, width), lambda i: (0, 0)),
        ],
        out_shape=[
            jax.ShapeDtypeStruct((1, count), jnp.float32),
            jax.ShapeDtypeStruct((count, width), jnp.float32),
        ],
        scratch_shapes=[
            pltpu.VMEM((count, width), jnp.bfloat16),
            pltpu.VMEM((count, 128), jnp.float32),
            pltpu.VMEM((count, 128), jnp.float32),
        ],
        compiler_params=pltpu.CompilerParams(vmem_limit_bytes=VMEM),
        name="score",
    )(packed, blocks)
    return dup[0], mixed


def solution(mesh):
    placed = (
        P(("groups", "shard", "owner"), None),
        P(("groups", "shard", "owner"), None),
        P(("groups", "shard", "owner")),
    )
    return jax.shard_map(
        local,
        mesh=mesh,
        in_specs=placed,
        out_specs=(P(("groups", "shard", "owner")), P(("groups", "shard", "owner"), None)),
        check_vma=False,
    )
```

time: 71.8 us -> 77.1 us (1.074)
  waiting for transfers between devices: 32.2 us -> 50.4 us
  starting transfers between devices: 17.9 us -> 0.04 us
  between operations: 0.74 us -> 14 us
  Pallas kernels: 0 us -> 8.1 us
  local copies, waits for them, and re-layouts: 9.46 us -> 4.31 us
  other arithmetic: 4.83 us -> 0 us
  blocking collectives: 4.15 us -> 0 us
  matrix products: 2.04 us -> 0 us
    all_gather x0 -> x1, waiting for transfers between devices: none -> 50.4 us  [local(): blocks = lax.all_gather(packed, ('shard', 'owner'), axis=0, tiled=False)]
    all_to_all x4 -> x0, waiting for transfers between devices: 32.2 us -> none  [the longest x1 16.3 us: local(): lax.all_to_all(mixed.reshape(shards, places, width), 'shard', split_axis=...]
    all_to_all x4 -> x0, starting transfers between devices: 17.9 us -> none  [the longest x1 7.25 us: local(): lax.all_to_all(outrank, 'shard', split_axis=0, concat_axis=0, tiled=True)]
    pallas_call x0 -> x2, Pallas kernels: none -> 8.1 us  [the longest x1 6.36 us: local(): pl.pallas_call(score_kernel, grid=(total // many,), in_specs=[pl.BlockSpe...]
    unnamed x0 -> x5, local copies, waits for them, and re-layouts: none -> 4.31 us
    all_gather x2 -> x0, blocking collectives: 4.15 us -> none  [the longest x1 2.36 us: local(): lax.all_gather(arrived, 'owner', axis=0, tiled=True)]
    scatter x2 -> x0, local copies, waits for them, and re-layouts: 3.36 us -> none  [the longest x1 2.26 us: local(): jnp.zeros((shards * places, width), jnp.bfloat16).at[slot].set(embeddings)]
    gather x2 -> x0, local copies, waits for them, and re-layouts: 3.32 us -> none  [the longest x1 1.76 us: local(): dup_score = back_dup.reshape(-1)[slot]]
  transfers between devices with their start and end apart: 4 -> 1, of which waited for: 4 -> 1; matrix products, arithmetic and copies ran while one was open for 12% -> 0% of each run, Pallas kernels for 0% -> 0%
where the time goes in v1:
time: 77.1 us; the launch traced here: 76.9 us
  waiting for transfers between devices  50.4 us (65%)
  between operations  14 us (18%)
  Pallas kernels  8.1 us (11%)
  local copies, waits for them, and re-layouts  4.31 us (6%)
    all_gather x1, waiting for transfers between devices, local(): blocks = lax.all_gather(packed, ('shard', 'owner'), axis=0, tiled=False)  50.4 us
    pallas_call x1, Pallas kernels, local(): pl.pallas_call(score_kernel, grid=(total // many,), in_specs=[pl.BlockSpe...  6.36 us
    unnamed x5, local copies, waits for them, and re-layouts  4.31 us
    pallas_call x1, Pallas kernels, local(): pl.pallas_call(pack_kernel, out_shape=jax.ShapeDtypeStruct((count + EXTRA...  1.75 us
  transfers between devices with their start and end apart: 1, of which 1 were waited for; matrix products, arithmetic and copies ran while one was open for 0% of the time, Pallas kernels for 0%

profile of v1, /device:TPU:0, one launch (start us, length us, event | category | flops | bytes accessed | tf_op | source)
XLA Modules:
  0.0 76.9 jit_solution(4564028120335023340)
XLA Ops:
  7.2 0.0 all-gather.3.cloned.1.call-start
  7.2 1.4 %copy.5.label_ref = s32[128,1]{1,0:T(8,128)} copy(s32[128,1]{0,1:T(1,128)} %param.4) | data formatting | bytes 1024 | tf_op args[1]
  8.6 1.7 %pack.1.own_ref = bf16[144,768]{1,0:T(8,128)(2,1)} custom-call(bf16[128,768]{1,0:T(8,128)(2,1)} %rows_ref.1, s32[128,1]{1,0:T(8,128)} %copy.5.label_ref, s32[1,128]{1,0:T(1,128)} %bitcast.4), custom_call_target="tpu_custom_call" | custom-call | tf_op jit(solution)/shard_map/pack/pallas_call | solution.py:97
  10.3 0.0 all-gather.3.cloned.1.call-update
  10.4 50.4 %all-gather.3.cloned.1.call-done = bf16[2304,768]{1,0:T(8,128)(2,1)} async-done(((bf16[144,768]{1,0:T(8,128)(2,1)}), bf16[2304,768]{1,0:T(8,128)(2,1)}) %all-gather.3.cloned.1.call-update) | async-done | bytes 3538960 | tf_op jit(solution)/shard_map/all_gather | solution.py:102
  60.8 0.0 copy-start
  60.8 2.0 %copy-done = bf16[2304,768]{1,0:T(8,128)(2,1)S(1)} copy-done((bf16[2304,768]{1,0:T(8,128)(2,1)S(1)}, bf16[2304,768]{1,0:T(8,128)(2,1)}, u32[]{:S(2)}) %copy-start) | copy-done | bytes 3538968
  62.8 0.0 copy-start.1
  62.8 0.9 %copy-done.1 = bf16[144,768]{1,0:T(8,128)(2,1)S(1)} copy-done((bf16[144,768]{1,0:T(8,128)(2,1)S(1)}, bf16[144,768]{1,0:T(8,128)(2,1)}, u32[]{:S(2)}) %copy-start.1) | copy-done | bytes 221208
  63.7 6.4 %score.1 = (f32[1,128]{1,0:T(1,128)}, f32[128,768]{1,0:T(8,128)}) custom-call(bf16[144,768]{1,0:T(8,128)(2,1)S(1)} %copy-done.1, bf16[16,144,768]{2,1,0:T(8,128)(2,1)S(1)} %bitcast.3), custom_call_target="tpu_custom_call" | custom-call | tf_op jit(solution)/shard_map/score/pallas_call | solution.py:105
Async XLA Ops:
  7.2 53.6 %all-gather.3.cloned.1.call-start = ((), (), s32[]{:S(2)}) async-start(), calls=%async_computation | async-start | bytes 3760128 | tf_op jit(solution)/shard_map/all_gather | solution.py:102
  60.8 2.0 %copy-start = (bf16[2304,768]{1,0:T(8,128)(2,1)S(1)}, bf16[2304,768]{1,0:T(8,128)(2,1)}, u32[]{:S(2)}) copy-start(bf16[2304,768]{1,0:T(8,128)(2,1)} %all-gather.3.cloned.1.call-done) | copy-start | bytes 10616836
  62.8 0.9 %copy-start.1 = (bf16[144,768]{1,0:T(8,128)(2,1)S(1)}, bf16[144,768]{1,0:T(8,128)(2,1)}, u32[]{:S(2)}) copy-start(bf16[144,768]{1,0:T(8,128)(2,1)} %pack.1.own_ref) | copy-start | bytes 663556
Sparse Core Ops, SparseCore 0:
  10.9 49.8 all-gather.2

commit v2 on v1

v2 whole, which is shorter than its diff:
```python
import jax
import jax.numpy as jnp
from jax import lax
from jax.experimental import pallas as pl
from jax.experimental.pallas import tpu as pltpu
from jax.sharding import PartitionSpec as P

EXTRA = 16
VMEM = 48 * 1024 * 1024


def make_unit(rows):
    wide = rows.astype(jnp.float32)
    scale = lax.rsqrt(jnp.mean(wide * wide, axis=-1, keepdims=True) + 1e-06) / jnp.sqrt(
        jnp.float32(rows.shape[-1])
    )
    return (wide * scale).astype(jnp.bfloat16)


def diagonal(count):
    down = lax.broadcasted_iota(jnp.int32, (count, count), 0)
    return down == lax.broadcasted_iota(jnp.int32, (count, count), 1)


def as_row(column):
    return jnp.sum(jnp.where(diagonal(column.shape[0]), column, 0.0), axis=0, keepdims=True)


def as_column(row):
    return jnp.sum(jnp.where(diagonal(row.shape[1]), row, 0.0), axis=1, keepdims=True)


def pack_kernel(rows_ref, label_ref, rank_ref, packed_ref):
    count, width = rows_ref.shape
    packed_ref[:count, :] = rows_ref[...]
    packed_ref[count:, :] = jnp.zeros((EXTRA, width), jnp.bfloat16)
    rank = rank_ref[...]
    high = lax.shift_right_logical(rank, 8)
    low = rank - lax.shift_left(high, 8)
    pieces = (
        label_ref[...].astype(jnp.float32),
        high.astype(jnp.float32),
        low.astype(jnp.float32),
    )
    for at, piece in enumerate(pieces):
        packed_ref[count : count + EXTRA, at * count : (at + 1) * count] = jnp.broadcast_to(
            piece, (EXTRA, count)
        ).astype(jnp.bfloat16)


def labels_and_ranks(extra, count):
    line = extra.astype(jnp.float32)[:1]
    label, high, low = (line[:, at * count : (at + 1) * count] for at in range(3))
    return label, high * 256.0 + low


def score_pair(unit, own_label, own_rank, blocks):
    count = blocks[0].shape[0] - EXTRA
    keys = jnp.concatenate([block[:count, :] for block in blocks], axis=0)
    sides = [labels_and_ranks(block[count:, :], count) for block in blocks]
    label = jnp.concatenate([side[0] for side in sides], axis=1)
    rank = jnp.concatenate([side[1] for side in sides], axis=1)
    cosine = lax.dot_general(
        unit, make_unit(keys), (((1,), (1,)), ((), ())), preferred_element_type=jnp.float32
    )
    weight = 1.0 / (1.0 + jnp.exp(-40.0 * (cosine - 0.05)))
    near = jnp.where((label == own_label) & (rank != own_rank), weight, 0.0)
    earlier = jnp.sum(jnp.where(rank < own_rank, near, 0.0), axis=1, keepdims=True)
    every = jnp.sum(near, axis=1, keepdims=True)
    mixed = jnp.dot(near.astype(jnp.bfloat16), keys, preferred_element_type=jnp.float32)
    return earlier, every, mixed


def first_kernel(own_ref, other_ref, *refs):
    blocks, (unit_ref, side_ref, sums_ref, mixed_ref) = refs[:-4], refs[-4:]
    count = own_ref.shape[0] - EXTRA
    side_ref[...] = jnp.zeros_like(side_ref)
    sums_ref[...] = jnp.zeros_like(sums_ref)
    for at, ref in enumerate((own_ref, other_ref)):
        here = slice(at * count, (at + 1) * count)
        unit_ref[here, :] = make_unit(ref[:count, :])
        label, rank = labels_and_ranks(ref[count:, :], count)
        side_ref[here, 0:1] = as_column(label)
        side_ref[here, 1:2] = as_column(rank)
    sums_ref[:, 0:1], sums_ref[:, 1:2], mixed_ref[...] = score_pair(
        unit_ref[...], side_ref[:, 0:1], side_ref[:, 1:2], [own_ref] + list(blocks)
    )


def next_kernel(unit_ref, side_ref, old_sums_ref, old_mixed_ref, *refs):
    blocks, (sums_ref, mixed_ref) = refs[:-2], refs[-2:]
    earlier, every, mixed = score_pair(
        unit_ref[...], side_ref[:, 0:1], side_ref[:, 1:2], blocks
    )
    sums_ref[...] = old_sums_ref[...]
    sums_ref[:, 0:1] += earlier
    sums_ref[:, 1:2] += every
    mixed_ref[...] = old_mixed_ref[...] + mixed


def last_kernel(sums_ref, mixed_ref, other_sums_ref, other_mixed_ref, dup_ref, out_ref):
    earlier = sums_ref[:, 0:1] + other_sums_ref[:, 0:1]
    every = sums_ref[:, 1:2] + other_sums_ref[:, 1:2]
    dup_ref[...] = as_row(jnp.log1p(earlier))
    out_ref[...] = (mixed_ref[...] + other_mixed_ref[...]) / jnp.sqrt(1.0 + every)


def cost(queries, keys, width):
    return pl.CostEstimate(
        flops=4 * queries * keys * width,
        bytes_accessed=8 * queries * width + 2 * keys * width,
        transcendentals=queries * keys,
    )


def local(embeddings, cluster_id, priority):
    count, width = embeddings.shape
    shards = lax.axis_size("shard")
    lanes = lax.axis_size("owner")
    packed = pl.pallas_call(
        pack_kernel,
        out_shape=jax.ShapeDtypeStruct((count + EXTRA, width), jnp.bfloat16),
        name="pack",
    )(embeddings, cluster_id.reshape(1, count), priority.reshape(1, count))

    def across(array):
        return lax.ppermute(array, "shard", [(at, at ^ 1) for at in range(shards)])

    def along(array):
        return lax.ppermute(array, "shard", [(at, (at + 2) % shards) for at in range(shards)])

    def swap(array):
        return lax.ppermute(array, "owner", [(at, lanes - 1 - at) for at in range(lanes)])

    queries = 2 * count
    f32 = jnp.float32
    sums_shape = jax.ShapeDtypeStruct((queries, 128), f32)
    mixed_shape = jax.ShapeDtypeStruct((queries, width), f32)
    params = pltpu.CompilerParams(vmem_limit_bytes=VMEM)

    def first(*blocks):
        return pl.pallas_call(
            first_kernel,
            out_shape=[
                jax.ShapeDtypeStruct((queries, width), jnp.bfloat16),
                jax.ShapeDtypeStruct((queries, 128), f32),
                sums_shape,
                mixed_shape,
            ],
            cost_estimate=cost(queries, (len(blocks) - 1) * count, width),
            compiler_params=params,
            name="first_scores",
        )(*blocks)

    def more(unit, side, sums, mixed, *blocks):
        return pl.pallas_call(
            next_kernel,
            out_shape=[sums_shape, mixed_shape],
            input_output_aliases={2: 0, 3: 1},
            cost_estimate=cost(queries, len(blocks) * count, width),
            compiler_params=params,
            name="more_scores",
        )(unit, side, sums, mixed, *blocks)

    other = swap(packed)
    beside = across(packed)
    rounds = shards // 2
    moved = along(packed)
    moved, beside, other = lax.optimization_barrier((moved, beside, other))
    unit, side, sums, mixed = first(packed, other, beside)
    if rounds <= 4:
        for turn in range(1, rounds):
            beside = across(moved)
            ahead = along(moved) if turn + 1 < rounds else None
            held = moved
            if ahead is not None:
                moved, beside = lax.optimization_barrier((ahead, beside))
            sums, mixed = more(unit, side, sums, mixed, held, beside)
    else:

        def turn_body(turn, state):
            moved, sums, mixed = state
            beside = across(moved)
            ahead = along(moved)
            sums, mixed = more(unit, side, sums, mixed, moved, beside)
            return ahead, sums, mixed

        moved, sums, mixed = lax.fori_loop(1, rounds, turn_body, (moved, sums, mixed))
    other_sums, other_mixed = swap(sums[count:]), swap(mixed[count:])
    dup, out = pl.pallas_call(
        last_kernel,
        out_shape=[
            jax.ShapeDtypeStruct((1, count), f32),
            jax.ShapeDtypeStruct((count, width), f32),
        ],
        compiler_params=params,
        name="combine",
    )(sums[:count], mixed[:count], other_sums, other_mixed)
    return dup[0], out


def solution(mesh):
    placed = (
        P(("groups", "shard", "owner"), None),
        P(("groups", "shard", "owner"), None),
        P(("groups", "shard", "owner")),
    )
    return jax.shard_map(
        local,
        mesh=mesh,
        in_specs=placed,
        out_specs=(P(("groups", "shard", "owner")), P(("groups", "shard", "owner"), None)),
        check_vma=False,
    )
```

time: 77.1 us -> 39 us (0.51)
  waiting for transfers between devices: 50.4 us -> 20.5 us
  between operations: 14 us -> 0.69 us
  starting transfers between devices: 0.04 us -> 10.5 us
  local copies, waits for them, and re-layouts: 4.31 us -> 1 us
  Pallas kernels: 8.1 us -> 6.18 us
    all_gather x1 -> x0, waiting for transfers between devices: 50.4 us -> none  [local(): blocks = lax.all_gather(packed, ('shard', 'owner'), axis=0, tiled=False)]
    ppermute x0 -> x10, waiting for transfers between devices: none -> 20.5 us  [the longest x3 18.2 us: along(): lax.ppermute(array, 'shard', [(at, (at + 2) % shards) for at in range(sha...]
    ppermute x0 -> x10, starting transfers between devices: none -> 10.5 us  [the longest x4 5.72 us: across(): return lax.ppermute(array, 'shard', [(at, at ^ 1) for at in range(shards)])]
    unnamed x5 -> x2, local copies, waits for them, and re-layouts: 4.31 us -> 0.94 us
    pallas_call x1 -> x5, Pallas kernels: 6.36 us -> 4.53 us  [the longest x3 2.73 us: more(): pl.pallas_call(next_kernel, out_shape=[sums_shape, mixed_shape], input_ou...]
  transfers between devices with their start and end apart: 1 -> 10, of which waited for: 1 -> 5; matrix products, arithmetic and copies ran while one was open for 0% -> 0% of each run, Pallas kernels for 0% -> 7%
where the time goes in v2:
time: 39 us; the launch traced here: 38.8 us
  waiting for transfers between devices  20.5 us (53%)
  starting transfers between devices  10.5 us (27%)
  Pallas kernels  6.18 us (16%)
  local copies, waits for them, and re-layouts  1 us (3%)
  between operations  0.69 us (2%)
    ppermute x3, waiting for transfers between devices, along(): lax.ppermute(array, 'shard', [(at, (at + 2) % shards) for at in range(sha...  18.2 us
    ppermute x4, starting transfers between devices, across(): return lax.ppermute(array, 'shard', [(at, at ^ 1) for at in range(shards)])  5.72 us
    ppermute x3, starting transfers between devices, along(): lax.ppermute(array, 'shard', [(at, (at + 2) % shards) for at in range(sha...  4.14 us
    pallas_call x3, Pallas kernels, more(): pl.pallas_call(next_kernel, out_shape=[sums_shape, mixed_shape], input_ou...  2.73 us
    pallas_call x1, Pallas kernels, local(): pl.pallas_call(pack_kernel, out_shape=jax.ShapeDtypeStruct((count + EXTRA...  1.65 us
    ppermute x3, waiting for transfers between devices, swap(): lax.ppermute(array, 'owner', [(at, lanes - 1 - at) for at in range(lanes)])  1.23 us
    ppermute x4, waiting for transfers between devices, across(): return lax.ppermute(array, 'shard', [(at, at ^ 1) for at in range(shards)])  1.01 us
    unnamed x2, local copies, waits for them, and re-layouts  0.94 us
  transfers between devices with their start and end apart: 10, of which 5 were waited for; matrix products, arithmetic and copies ran while one was open for 0% of the time, Pallas kernels for 7%

profile of v2, /device:TPU:0, one launch (start us, length us, event | category | flops | bytes accessed | tf_op | source)
XLA Modules:
  0.0 38.8 jit_solution(10208286164855907392)
XLA Ops:
  0.6 1.6 %pack.1.own_ref = bf16[144,768]{1,0:T(8,128)(2,1)} custom-call(bf16[128,768]{1,0:T(8,128)(2,1)} %rows_ref.1, s32[1,128]{1,0:T(1,128)} %bitcast.3, s32[1,128]{1,0:T(1,128)} %bitcast.4), custom_call_target="tpu_custom_call" | custom-call | tf_op jit(solution)/shard_map/pack/pallas_call | solution.py:120
  2.3 3.0 %collective-permute-start = (bf16[144,768]{1,0:T(8,128)(2,1)}, bf16[144,768]{1,0:T(8,128)(2,1)S(1)}, u32[]{:S(2)}, u32[]{:S(2)}) collective-permute-start(bf16[144,768]{1,0:T(8,128)(2,1)} %pack.1.own_ref), channel_id=1, source_target_pairs={{0,4},{2,6},{4,8},{6,10},{8,12},{10,14},{12,0},{14,2},{1,5},{3,7},... | collective-permute-start | bytes 663560 | tf_op jit(solution)/shard_map/ppermute | solution.py:130
  5.3 1.5 %collective-permute-start.1 = (bf16[144,768]{1,0:T(8,128)(2,1)}, bf16[144,768]{1,0:T(8,128)(2,1)S(1)}, u32[]{:S(2)}, u32[]{:S(2)}) collective-permute-start(bf16[144,768]{1,0:T(8,128)(2,1)} %pack.1.own_ref), channel_id=1, source_target_pairs={{0,2},{2,0},{4,6},{6,4},{8,10},{10,8},{12,14},{14,12},{1,3},{3,1},... | collective-permute-start | bytes 663560 | tf_op jit(solution)/shard_map/ppermute | solution.py:127
  6.8 0.0 collective-permute-start.2
  6.8 6.2 %collective-permute-done.refs_0_ = bf16[144,768]{1,0:T(8,128)(2,1)S(1)} collective-permute-done((bf16[144,768]{1,0:T(8,128)(2,1)}, bf16[144,768]{1,0:T(8,128)(2,1)S(1)}, u32[]{:S(2)}, u32[]{:S(2)}) %collective-permute-start) | collective-permute-done | bytes 221216 | tf_op jit(solution)/shard_map/ppermute | solution.py:130
  13.0 0.0 collective-permute-done.1.refs_0_
  13.0 0.0 collective-permute-done.2.other_ref
  13.0 1.0 %collective-permute-start.3 = (bf16[144,768]{1,0:T(8,128)(2,1)S(1)}, bf16[144,768]{1,0:T(8,128)(2,1)S(1)}, u32[]{:S(2)}, u32[]{:S(2)}) collective-permute-start(bf16[144,768]{1,0:T(8,128)(2,1)S(1)} %collective-permute-done.refs_0_), channel_id=1, source_target_pairs={{0,4},{2,6},{4,8},{6,10},{8,12},{10,14},{12,0},{14,2},{1,5},{3,7},... | collective-permute-start | bytes 663560 | tf_op jit(solution)/shard_map/ppermute | solution.py:130
  14.0 1.5 %collective-permute-start.4 = (bf16[144,768]{1,0:T(8,128)(2,1)S(1)}, bf16[144,768]{1,0:T(8,128)(2,1)S(1)}, u32[]{:S(2)}, u32[]{:S(2)}) collective-permute-start(bf16[144,768]{1,0:T(8,128)(2,1)S(1)} %collective-permute-done.refs_0_), channel_id=1, source_target_pairs={{0,2},{2,0},{4,6},{6,4},{8,10},{10,8},{12,14},{14,12},{1,3},{3,1},... | collective-permute-start | bytes 663560 | tf_op jit(solution)/shard_map/ppermute | solution.py:127
  15.5 5.9 %collective-permute-done.3.refs_0_ = bf16[144,768]{1,0:T(8,128)(2,1)S(1)} collective-permute-done((bf16[144,768]{1,0:T(8,128)(2,1)S(1)}, bf16[144,768]{1,0:T(8,128)(2,1)S(1)}, u32[]{:S(2)}, u32[]{:S(2)}) %collective-permute-start.3) | collective-permute-done | bytes 221216 | tf_op jit(solution)/shard_map/ppermute | solution.py:130
  21.4 0.0 collective-permute-done.4.refs_1_
  21.4 0.1 collective-permute-start.5
  21.5 1.5 %collective-permute-start.6 = (bf16[144,768]{1,0:T(8,128)(2,1)S(1)}, bf16[144,768]{1,0:T(8,128)(2,1)S(1)}, u32[]{:S(2)}, u32[]{:S(2)}) collective-permute-start(bf16[144,768]{1,0:T(8,128)(2,1)S(1)} %collective-permute-done.3.refs_0_), channel_id=1, source_target_pairs={{0,2},{2,0},{4,6},{6,4},{8,10},{10,8},{12,14},{14,12},{1,3},{3,1},... | collective-permute-start | bytes 663560 | tf_op jit(solution)/shard_map/ppermute | solution.py:127
  23.0 6.1 %collective-permute-done.5.refs_0_ = bf16[144,768]{1,0:T(8,128)(2,1)S(1)} collective-permute-done((bf16[144,768]{1,0:T(8,128)(2,1)S(1)}, bf16[144,768]{1,0:T(8,128)(2,1)S(1)}, u32[]{:S(2)}, u32[]{:S(2)}) %collective-permute-start.5) | collective-permute-done | bytes 221216 | tf_op jit(solution)/shard_map/ppermute | solution.py:130
  29.1 0.0 collective-permute-done.6.refs_1_
  29.1 1.2 %collective-permute-start.7 = (bf16[144,768]{1,0:T(8,128)(2,1)S(1)}, bf16[144,768]{1,0:T(8,128)(2,1)S(1)}, u32[]{:S(2)}, u32[]{:S(2)}) collective-permute-start(bf16[144,768]{1,0:T(8,128)(2,1)S(1)} %collective-permute-done.5.refs_0_), channel_id=1, source_target_pairs={{0,2},{2,0},{4,6},{6,4},{8,10},{10,8},{12,14},{14,12},{1,3},{3,1},... | collective-permute-start | bytes 663560 | tf_op jit(solution)/shard_map/ppermute | solution.py:127
  30.4 0.0 copy-start
  30.4 0.9 %copy-done = bf16[144,768]{1,0:T(8,128)(2,1)S(1)} copy-done((bf16[144,768]{1,0:T(8,128)(2,1)S(1)}, bf16[144,768]{1,0:T(8,128)(2,1)}, u32[]{:S(2)}) %copy-start) | copy-done | bytes 221208
  31.3 0.9 %first_scores.1 = (bf16[256,768]{1,0:T(8,128)(2,1)S(1)}, f32[256,128]{1,0:T(8,128)S(1)}, f32[256,128]{1,0:T(8,128)S(1)}, f32[256,768]{1,0:T(8,128)S(1)}) custom-call(bf16[144,768]{1,0:T(8,128)(2,1)S(1)} %copy-done, bf16[144,768]{1,0:T(8,128)(2,1)S(1)} %collective-permute-done.2.other_ref, bf16[144,768]{1,0:T(8,128)(2,1)S(1)} %collective-permute-done.1.refs_0_), custom_call_target="tpu_custom_call" | custom-call | flops 201326592 | bytes 1966080 | tf_op jit(solution)/shard_map/first_scores/pallas_call | solution.py:142
  32.2 0.9 %more_scores.3 = (f32[256,128]{1,0:T(8,128)S(1)}, f32[256,768]{1,0:T(8,128)S(1)}) custom-call(bf16[256,768]{1,0:T(8,128)(2,1)S(1)} %get-tuple-element.23.unit_ref, f32[256,128]{1,0:T(8,128)S(1)} %get-tuple-element.24.side_ref, f32[256,128]{1,0:T(8,128)S(1)} %get-tuple-element.25.old_sums_ref, ...), custom_call_target="tpu_custom_call", output_to_operand_aliasing={{0}: (2, {}), {1}: (3, {})} | custom-call | flops 201326592 | bytes 1966080 | tf_op jit(solution)/shard_map/more_scores/pallas_call | solution.py:156
  33.1 0.9 %more_scores.4 = (f32[256,128]{1,0:T(8,128)S(1)}, f32[256,768]{1,0:T(8,128)S(1)}) custom-call(bf16[256,768]{1,0:T(8,128)(2,1)S(1)} %get-tuple-element.23.unit_ref, f32[256,128]{1,0:T(8,128)S(1)} %get-tuple-element.24.side_ref, f32[256,128]{1,0:T(8,128)S(1)} %get-tuple-element.29.old_sums_ref, ...), custom_call_target="tpu_custom_call", output_to_operand_aliasing={{0}: (2, {}), {1}: (3, {})} | custom-call | flops 201326592 | bytes 1966080 | tf_op jit(solution)/shard_map/more_scores/pallas_call | solution.py:156
  34.1 1.0 %collective-permute-done.7.refs_1_ = bf16[144,768]{1,0:T(8,128)(2,1)S(1)} collective-permute-done((bf16[144,768]{1,0:T(8,128)(2,1)S(1)}, bf16[144,768]{1,0:T(8,128)(2,1)S(1)}, u32[]{:S(2)}, u32[]{:S(2)}) %collective-permute-start.7) | collective-permute-done | bytes 221216 | tf_op jit(solution)/shard_map/ppermute | solution.py:127
  35.1 0.9 %more_scores.5 = (f32[256,128]{1,0:T(8,128)S(1)}, f32[256,768]{1,0:T(8,128)S(1)}) custom-call(bf16[256,768]{1,0:T(8,128)(2,1)S(1)} %get-tuple-element.23.unit_ref, f32[256,128]{1,0:T(8,128)S(1)} %get-tuple-element.24.side_ref, f32[256,128]{1,0:T(8,128)S(1)} %get-tuple-element.33.old_sums_ref, ...), custom_call_target="tpu_custom_call", output_to_operand_aliasing={{0}: (2, {}), {1}: (3, {})} | custom-call | flops 201326592 | bytes 1966080 | tf_op jit(solution)/shard_map/more_scores/pallas_call | solution.py:156
  36.0 0.1 fusion
  36.0 0.1 collective-permute-start.9
  36.1 0.6 %collective-permute-start.8 = (f32[128,128]{1,0:T(8,128)S(1)}, f32[128,128]{1,0:T(8,128)S(1)}, u32[]{:S(2)}, u32[]{:S(2)}) collective-permute-start(f32[128,128]{1,0:T(8,128)S(1)} %get-tuple-element.42), channel_id=1, source_target_pairs={{0,1},{1,0},{2,3},{3,2},{4,5},{5,4},{6,7},{7,6},{8,9},{9,8},{10,11... | collective-permute-start | bytes 196616 | tf_op jit(solution)/shard_map/ppermute | solution.py:133
  36.7 1.2 %collective-permute-done.8.other_sums_ref = f32[128,128]{1,0:T(8,128)S(1)} collective-permute-done((f32[128,128]{1,0:T(8,128)S(1)}, f32[128,128]{1,0:T(8,128)S(1)}, u32[]{:S(2)}, u32[]{:S(2)}) %collective-permute-start.8) | collective-permute-done | bytes 65568 | tf_op jit(solution)/shard_map/ppermute | solution.py:133
  37.9 0.0 collective-permute-done.9.other_mixed_ref
  37.9 0.9 %combine.1 = (f32[1,128]{1,0:T(1,128)}, f32[128,768]{1,0:T(8,128)}) custom-call(f32[128,128]{1,0:T(8,128)S(1)} %get-tuple-element.43.sums_ref, f32[128,768]{1,0:T(8,128)S(1)} %get-tuple-element.41.mixed_ref, f32[128,128]{1,0:T(8,128)S(1)} %collective-permute-done.8.other_sums_ref, f32[128,768]{1,0:T(8,128)S(1)} %collective-permute-done.9.other_mixed_ref), custom_call_target="tpu_custom_call" | custom-call | tf_op jit(solution)/shard_map/combine/pallas_call | solution.py:190
  (1 shorter events, 0.0 us)
Async XLA Ops:
  2.3 10.7 %collective-permute-start = (bf16[144,768]{1,0:T(8,128)(2,1)}, bf16[144,768]{1,0:T(8,128)(2,1)S(1)}, u32[]{:S(2)}, u32[]{:S(2)}) collective-permute-start(bf16[144,768]{1,0:T(8,128)(2,1)} %pack.1.own_ref), channel_id=1, source_target_pairs={{0,4},{2,6},{4,8},{6,10},{8,12},{10,14},{12,0},{14,2},{1,5},{3,7},... | collective-permute-start | bytes 663560 | tf_op jit(solution)/shard_map/ppermute | solution.py:130
  5.3 7.7 %collective-permute-start.1 = (bf16[144,768]{1,0:T(8,128)(2,1)}, bf16[144,768]{1,0:T(8,128)(2,1)S(1)}, u32[]{:S(2)}, u32[]{:S(2)}) collective-permute-start(bf16[144,768]{1,0:T(8,128)(2,1)} %pack.1.own_ref), channel_id=1, source_target_pairs={{0,2},{2,0},{4,6},{6,4},{8,10},{10,8},{12,14},{14,12},{1,3},{3,1},... | collective-permute-start | bytes 663560 | tf_op jit(solution)/shard_map/ppermute | solution.py:127
  6.8 6.2 %collective-permute-start.2 = (bf16[144,768]{1,0:T(8,128)(2,1)}, bf16[144,768]{1,0:T(8,128)(2,1)S(1)}, u32[]{:S(2)}, u32[]{:S(2)}) collective-permute-start(bf16[144,768]{1,0:T(8,128)(2,1)} %pack.1.own_ref), channel_id=1, source_target_pairs={{0,1},{1,0},{2,3},{3,2},{4,5},{5,4},{6,7},{7,6},{8,9},{9,8},{10,11... | collective-permute-start | bytes 663560 | tf_op jit(solution)/shard_map/ppermute | solution.py:133
  13.0 8.4 %collective-permute-start.3 = (bf16[144,768]{1,0:T(8,128)(2,1)S(1)}, bf16[144,768]{1,0:T(8,128)(2,1)S(1)}, u32[]{:S(2)}, u32[]{:S(2)}) collective-permute-start(bf16[144,768]{1,0:T(8,128)(2,1)S(1)} %collective-permute-done.refs_0_), channel_id=1, source_target_pairs={{0,4},{2,6},{4,8},{6,10},{8,12},{10,14},{12,0},{14,2},{1,5},{3,7},... | collective-permute-start | bytes 663560 | tf_op jit(solution)/shard_map/ppermute | solution.py:130
  14.0 7.4 %collective-permute-start.4 = (bf16[144,768]{1,0:T(8,128)(2,1)S(1)}, bf16[144,768]{1,0:T(8,128)(2,1)S(1)}, u32[]{:S(2)}, u32[]{:S(2)}) collective-permute-start(bf16[144,768]{1,0:T(8,128)(2,1)S(1)} %collective-permute-done.refs_0_), channel_id=1, source_target_pairs={{0,2},{2,0},{4,6},{6,4},{8,10},{10,8},{12,14},{14,12},{1,3},{3,1},... | collective-permute-start | bytes 663560 | tf_op jit(solution)/shard_map/ppermute | solution.py:127
  21.4 7.7 %collective-permute-start.5 = (bf16[144,768]{1,0:T(8,128)(2,1)S(1)}, bf16[144,768]{1,0:T(8,128)(2,1)S(1)}, u32[]{:S(2)}, u32[]{:S(2)}) collective-permute-start(bf16[144,768]{1,0:T(8,128)(2,1)S(1)} %collective-permute-done.3.refs_0_), channel_id=1, source_target_pairs={{0,4},{2,6},{4,8},{6,10},{8,12},{10,14},{12,0},{14,2},{1,5},{3,7},... | collective-permute-start | bytes 663560 | tf_op jit(solution)/shard_map/ppermute | solution.py:130
  21.5 7.6 %collective-permute-start.6 = (bf16[144,768]{1,0:T(8,128)(2,1)S(1)}, bf16[144,768]{1,0:T(8,128)(2,1)S(1)}, u32[]{:S(2)}, u32[]{:S(2)}) collective-permute-start(bf16[144,768]{1,0:T(8,128)(2,1)S(1)} %collective-permute-done.3.refs_0_), channel_id=1, source_target_pairs={{0,2},{2,0},{4,6},{6,4},{8,10},{10,8},{12,14},{14,12},{1,3},{3,1},... | collective-permute-start | bytes 663560 | tf_op jit(solution)/shard_map/ppermute | solution.py:127
  29.1 5.9 %collective-permute-start.7 = (bf16[144,768]{1,0:T(8,128)(2,1)S(1)}, bf16[144,768]{1,0:T(8,128)(2,1)S(1)}, u32[]{:S(2)}, u32[]{:S(2)}) collective-permute-start(bf16[144,768]{1,0:T(8,128)(2,1)S(1)} %collective-permute-done.5.refs_0_), channel_id=1, source_target_pairs={{0,2},{2,0},{4,6},{6,4},{8,10},{10,8},{12,14},{14,12},{1,3},{3,1},... | collective-permute-start | bytes 663560 | tf_op jit(solution)/shard_map/ppermute | solution.py:127
  30.4 0.9 %copy-start = (bf16[144,768]{1,0:T(8,128)(2,1)S(1)}, bf16[144,768]{1,0:T(8,128)(2,1)}, u32[]{:S(2)}) copy-start(bf16[144,768]{1,0:T(8,128)(2,1)} %pack.1.own_ref) | copy-start | bytes 663556
  36.0 1.9 %collective-permute-start.9 = (f32[128,768]{1,0:T(8,128)S(1)}, f32[128,768]{1,0:T(8,128)S(1)}, u32[]{:S(2)}, u32[]{:S(2)}) collective-permute-start(f32[128,768]{1,0:T(8,128)S(1)} %get-tuple-element.40), channel_id=1, source_target_pairs={{0,1},{1,0},{2,3},{3,2},{4,5},{5,4},{6,7},{7,6},{8,9},{9,8},{10,11... | collective-permute-start | bytes 1179656 | tf_op jit(solution)/shard_map/ppermute | solution.py:133
  36.1 1.8 %collective-permute-start.8 = (f32[128,128]{1,0:T(8,128)S(1)}, f32[128,128]{1,0:T(8,128)S(1)}, u32[]{:S(2)}, u32[]{:S(2)}) collective-permute-start(f32[128,128]{1,0:T(8,128)S(1)} %get-tuple-element.42), channel_id=1, source_target_pairs={{0,1},{1,0},{2,3},{3,2},{4,5},{5,4},{6,7},{7,6},{8,9},{9,8},{10,11... | collective-permute-start | bytes 196616 | tf_op jit(solution)/shard_map/ppermute | solution.py:133

commit v3 on v2

v3 whole, which is shorter than its diff:
```python
import jax
import jax.numpy as jnp
from jax import lax
from jax.experimental import pallas as pl
from jax.experimental.pallas import tpu as pltpu
from jax.sharding import PartitionSpec as P

EXTRA = 8
VMEM = 48 * 1024 * 1024


def make_unit(rows):
    wide = rows.astype(jnp.float32)
    scale = lax.rsqrt(jnp.mean(wide * wide, axis=-1, keepdims=True) + 1e-06) / jnp.sqrt(
        jnp.float32(rows.shape[-1])
    )
    return (wide * scale).astype(jnp.bfloat16)


def diagonal(count):
    down = lax.broadcasted_iota(jnp.int32, (count, count), 0)
    return down == lax.broadcasted_iota(jnp.int32, (count, count), 1)


def as_row(column):
    return jnp.sum(jnp.where(diagonal(column.shape[0]), column, 0.0), axis=0, keepdims=True)


def as_column(row):
    return jnp.sum(jnp.where(diagonal(row.shape[1]), row, 0.0), axis=1, keepdims=True)


def pack_kernel(rows_ref, label_ref, rank_ref, front_ref, rear_ref):
    count, width = rows_ref.shape
    half = count // 2
    front_ref[:half, :] = rows_ref[:half, :]
    rear_ref[...] = rows_ref[half:, :]
    rank = rank_ref[...]
    high = lax.shift_right_logical(rank, 8)
    low = rank - lax.shift_left(high, 8)
    pieces = [piece.astype(jnp.float32) for piece in (label_ref[...], high, low)]
    pieces.append(jnp.zeros((1, width - 3 * count), jnp.float32))
    line = jnp.concatenate(pieces, axis=1)
    front_ref[half:, :] = jnp.broadcast_to(line, (EXTRA, width)).astype(jnp.bfloat16)


def labels_and_ranks(front):
    half = front.shape[0] - EXTRA
    count = 2 * half
    line = front[half:, :].astype(jnp.float32)[:1]
    label, high, low = (line[:, at * count : (at + 1) * count] for at in range(3))
    return label, high * 256.0 + low


def rows_of(blocks):
    pieces = []
    for front, rear in blocks:
        pieces += [front[: rear.shape[0], :], rear[...]]
    return jnp.concatenate(pieces, axis=0)


def score(unit, side, blocks):
    own_label, own_rank = side[:, 0:1], side[:, 1:2]
    keys = rows_of(blocks)
    sides = [labels_and_ranks(front) for front, _ in blocks]
    label = jnp.concatenate([item[0] for item in sides], axis=1)
    rank = jnp.concatenate([item[1] for item in sides], axis=1)
    cosine = lax.dot_general(
        unit, make_unit(keys), (((1,), (1,)), ((), ())), preferred_element_type=jnp.float32
    )
    weight = 1.0 / (1.0 + jnp.exp(-40.0 * (cosine - 0.05)))
    near = jnp.where((label == own_label) & (rank != own_rank), weight, 0.0)
    earlier = jnp.sum(jnp.where(rank < own_rank, near, 0.0), axis=1, keepdims=True)
    every = jnp.sum(near, axis=1, keepdims=True)
    mixed = jnp.dot(near.astype(jnp.bfloat16), keys, preferred_element_type=jnp.float32)
    return earlier, every, mixed


def pairs(refs):
    return [(refs[at], refs[at + 1]) for at in range(0, len(refs), 2)]


def first_kernel(*refs):
    ins, (unit_ref, side_ref, sums_ref, mixed_ref) = pairs(refs[:-4]), refs[-4:]
    own, other = ins[0], ins[1]
    count = 2 * own[1].shape[0]
    side_ref[...] = jnp.zeros_like(side_ref)
    sums_ref[...] = jnp.zeros_like(sums_ref)
    unit_ref[...] = make_unit(rows_of([own, other]))
    for at, (front, _) in enumerate((own, other)):
        here = slice(at * count, (at + 1) * count)
        label, rank = labels_and_ranks(front)
        side_ref[here, 0:1] = as_column(label)
        side_ref[here, 1:2] = as_column(rank)
    sums_ref[:, 0:1], sums_ref[:, 1:2], mixed_ref[...] = score(
        unit_ref[...], side_ref, [own] + ins[2:]
    )


def next_kernel(unit_ref, side_ref, old_sums_ref, old_mixed_ref, *refs):
    blocks, (sums_ref, mixed_ref) = pairs(refs[:-2]), refs[-2:]
    earlier, every, mixed = score(unit_ref[...], side_ref, blocks)
    sums_ref[...] = old_sums_ref[...]
    sums_ref[:, 0:1] += earlier
    sums_ref[:, 1:2] += every
    mixed_ref[...] = old_mixed_ref[...] + mixed


def last_kernel(sums_ref, mixed_ref, other_sums_ref, other_mixed_ref, dup_ref, out_ref):
    earlier = sums_ref[:, 0:1] + other_sums_ref[:, 0:1]
    every = sums_ref[:, 1:2] + other_sums_ref[:, 1:2]
    dup_ref[...] = as_row(jnp.log1p(earlier))
    out_ref[...] = (mixed_ref[...] + other_mixed_ref[...]) / jnp.sqrt(1.0 + every)


def cost(queries, keys, width):
    return pl.CostEstimate(
        flops=4 * queries * keys * width,
        bytes_accessed=8 * queries * width + 2 * keys * width,
        transcendentals=queries * keys,
    )


def local(embeddings, cluster_id, priority):
    count, width = embeddings.shape
    half = count // 2
    shards = lax.axis_size("shard")
    lanes = lax.axis_size("owner")
    rounds = shards // 2
    bf16, f32 = jnp.bfloat16, jnp.float32
    own = pl.pallas_call(
        pack_kernel,
        out_shape=[
            jax.ShapeDtypeStruct((half + EXTRA, width), bf16),
            jax.ShapeDtypeStruct((half, width), bf16),
        ],
        name="pack",
    )(embeddings, cluster_id.reshape(1, count), priority.reshape(1, count))

    def across(array):
        return lax.ppermute(array, "shard", [(at, at ^ 1) for at in range(shards)])

    def along(array, step=2):
        return lax.ppermute(array, "shard", [(at, (at + step) % shards) for at in range(shards)])

    def swap(array):
        return lax.ppermute(array, "owner", [(at, lanes - 1 - at) for at in range(lanes)])

    queries = 2 * count
    sums_shape = jax.ShapeDtypeStruct((queries, 128), f32)
    mixed_shape = jax.ShapeDtypeStruct((queries, width), f32)
    params = pltpu.CompilerParams(vmem_limit_bytes=VMEM)

    def first(*blocks):
        return pl.pallas_call(
            first_kernel,
            out_shape=[
                jax.ShapeDtypeStruct((queries, width), bf16),
                jax.ShapeDtypeStruct((queries, 128), f32),
                sums_shape,
                mixed_shape,
            ],
            cost_estimate=cost(queries, (len(blocks) - 1) * count, width),
            compiler_params=params,
            name="first_scores",
        )(*[piece for block in blocks for piece in block])

    def more(unit, side, sums, mixed, *blocks):
        return pl.pallas_call(
            next_kernel,
            out_shape=[sums_shape, mixed_shape],
            input_output_aliases={2: 0, 3: 1},
            cost_estimate=cost(queries, len(blocks) * count, width),
            compiler_params=params,
            name="more_scores",
        )(unit, side, sums, mixed, *[piece for block in blocks for piece in block])

    if rounds <= 4:
        moved, beside = ([], []), ([], [])
        for at in range(2):
            moved[at].append(along(own[at]))
            beside[at].append(across(own[at]))
            for turn in range(1, rounds):
                here, there = lax.optimization_barrier((moved[at][-1], beside[at][-1]))
                moved[at][-1], beside[at][-1] = here, there
                if turn + 1 < rounds:
                    moved[at].append(along(here))
                    beside[at].append(across(here))
                elif at == 0:
                    beside[at].append(across(here))
                else:
                    beside[at].append(along(beside[at][0], -2))
        other = [swap(piece) for piece in own]
        moved, beside = list(zip(*moved)), list(zip(*beside))
        unit, side, sums, mixed = first(own, other, beside[0])
        for turn in range(1, rounds - 1):
            sums, mixed = more(unit, side, sums, mixed, moved[turn - 1], beside[turn])
        sums, mixed = more(unit, side, sums, mixed, moved[-1])
        sums, mixed = more(unit, side, sums, mixed, beside[-1])
    else:
        other = [swap(piece) for piece in own]
        unit, side, sums, mixed = first(own, other, [across(piece) for piece in own])

        def turn_body(turn, state):
            moved, sums, mixed = state
            beside = [across(piece) for piece in moved]
            ahead = [along(piece) for piece in moved]
            sums, mixed = more(unit, side, sums, mixed, moved, beside)
            return ahead, sums, mixed

        start = ([along(piece) for piece in own], sums, mixed)
        _, sums, mixed = lax.fori_loop(1, rounds, turn_body, start)
    other_sums, other_mixed = swap(sums[count:]), swap(mixed[count:])
    dup, out = pl.pallas_call(
        last_kernel,
        out_shape=[
            jax.ShapeDtypeStruct((1, count), f32),
            jax.ShapeDtypeStruct((count, width), f32),
        ],
        compiler_params=params,
        name="combine",
    )(sums[:count], mixed[:count], other_sums, other_mixed)
    return dup[0], out


def solution(mesh):
    placed = (
        P(("groups", "shard", "owner"), None),
        P(("groups", "shard", "owner"), None),
        P(("groups", "shard", "owner")),
    )
    return jax.shard_map(
        local,
        mesh=mesh,
        in_specs=placed,
        out_specs=(P(("groups", "shard", "owner")), P(("groups", "shard", "owner"), None)),
        check_vma=False,
    )
```

time: 39 us -> 39 us (level)
  waiting for transfers between devices: 20.5 us -> 8.63 us
  starting transfers between devices: 10.5 us -> 20.8 us
  local copies, waits for them, and re-layouts: 1 us -> 1.85 us
  Pallas kernels: 6.18 us -> 6.75 us
    ppermute x3 -> x7, waiting for transfers between devices: 18.2 us -> 5.3 us  [along(): lax.ppermute(array, 'shard', [(at, (at + step) % shards) for at in range(...]
    ppermute x3 -> x7, starting transfers between devices: 4.14 us -> 11.3 us  [along(): lax.ppermute(array, 'shard', [(at, (at + step) % shards) for at in range(...]
    ppermute x4 -> x7, starting transfers between devices: 5.72 us -> 8.82 us  [across(): return lax.ppermute(array, 'shard', [(at, at ^ 1) for at in range(shards)])]
    ppermute x4 -> x7, waiting for transfers between devices: 1.01 us -> 2.09 us  [across(): return lax.ppermute(array, 'shard', [(at, at ^ 1) for at in range(shards)])]
    unnamed x2 -> x4, local copies, waits for them, and re-layouts: 0.94 us -> 1.79 us
    pallas_call x3 -> x4, Pallas kernels: 2.73 us -> 3.25 us  [more(): pl.pallas_call(next_kernel, out_shape=[sums_shape, mixed_shape], input_ou...]
    ppermute x3 -> x4, waiting for transfers between devices: 1.23 us -> 1.24 us  [swap(): lax.ppermute(array, 'owner', [(at, lanes - 1 - at) for at in range(lanes)])]
  transfers between devices with their start and end apart: 10 -> 18, of which waited for: 5 -> 6; matrix products, arithmetic and copies ran while one was open for 0% -> 0% of each run, Pallas kernels for 7% -> 9%
where the time goes in v3:
time: 39 us; the launch traced here: 38.8 us
  starting transfers between devices  20.8 us (53%)
  waiting for transfers between devices  8.63 us (22%)
  Pallas kernels  6.75 us (17%)
  local copies, waits for them, and re-layouts  1.85 us (5%)
  between operations  0.74 us (2%)
    ppermute x7, starting transfers between devices, along(): lax.ppermute(array, 'shard', [(at, (at + step) % shards) for at in range(...  11.3 us
    ppermute x7, starting transfers between devices, across(): return lax.ppermute(array, 'shard', [(at, at ^ 1) for at in range(shards)])  8.82 us
    ppermute x7, waiting for transfers between devices, along(): lax.ppermute(array, 'shard', [(at, (at + step) % shards) for at in range(...  5.3 us
    pallas_call x4, Pallas kernels, more(): pl.pallas_call(next_kernel, out_shape=[sums_shape, mixed_shape], input_ou...  3.25 us
    ppermute x7, waiting for transfers between devices, across(): return lax.ppermute(array, 'shard', [(at, at ^ 1) for at in range(shards)])  2.09 us
    unnamed x4, local copies, waits for them, and re-layouts  1.79 us
    pallas_call x1, Pallas kernels, local(): pl.pallas_call(pack_kernel, out_shape=[jax.ShapeDtypeStruct((half + EXTRA...  1.64 us
    ppermute x4, waiting for transfers between devices, swap(): lax.ppermute(array, 'owner', [(at, lanes - 1 - at) for at in range(lanes)])  1.24 us
  transfers between devices with their start and end apart: 18, of which 6 were waited for; matrix products, arithmetic and copies ran while one was open for 0% of the time, Pallas kernels for 9%

profile of v3, /device:TPU:0, one launch (start us, length us, event | category | flops | bytes accessed | tf_op | source)
XLA Modules:
  0.0 38.8 jit_solution(15452159190293791821)
XLA Ops:
  0.6 1.6 %pack.1 = (bf16[72,768]{1,0:T(8,128)(2,1)}, bf16[64,768]{1,0:T(8,128)(2,1)}) custom-call(bf16[128,768]{1,0:T(8,128)(2,1)} %rows_ref.1, s32[1,128]{1,0:T(1,128)} %bitcast.3, s32[1,128]{1,0:T(1,128)} %bitcast.4), custom_call_target="tpu_custom_call" | custom-call | tf_op jit(solution)/shard_map/pack/pallas_call | solution.py:131
  2.3 3.0 %collective-permute-start.2 = (bf16[72,768]{1,0:T(8,128)(2,1)}, bf16[72,768]{1,0:T(8,128)(2,1)S(1)}, u32[]{:S(2)}, u32[]{:S(2)}) collective-permute-start(bf16[72,768]{1,0:T(8,128)(2,1)} %get-tuple-element.30.refs_0_), channel_id=1, source_target_pairs={{0,4},{2,6},{4,8},{6,10},{8,12},{10,14},{12,0},{14,2},{1,5},{3,7},... | collective-permute-start | bytes 331784 | tf_op jit(solution)/shard_map/ppermute | solution.py:144
  5.3 1.5 %collective-permute-start.3 = (bf16[72,768]{1,0:T(8,128)(2,1)}, bf16[72,768]{1,0:T(8,128)(2,1)S(1)}, u32[]{:S(2)}, u32[]{:S(2)}) collective-permute-start(bf16[72,768]{1,0:T(8,128)(2,1)} %get-tuple-element.30.refs_0_), channel_id=1, source_target_pairs={{0,2},{2,0},{4,6},{6,4},{8,10},{10,8},{12,14},{14,12},{1,3},{3,1},... | collective-permute-start | bytes 331784 | tf_op jit(solution)/shard_map/ppermute | solution.py:141
  6.8 1.6 %collective-permute-start.4 = (bf16[64,768]{1,0:T(8,128)(2,1)}, bf16[64,768]{1,0:T(8,128)(2,1)S(1)}, u32[]{:S(2)}, u32[]{:S(2)}) collective-permute-start(bf16[64,768]{1,0:T(8,128)(2,1)} %get-tuple-element.31.refs_1_), channel_id=1, source_target_pairs={{0,4},{2,6},{4,8},{6,10},{8,12},{10,14},{12,0},{14,2},{1,5},{3,7},... | collective-permute-start | bytes 294920 | tf_op jit(solution)/shard_map/ppermute | solution.py:144
  8.4 0.5 %collective-permute-start.5 = (bf16[64,768]{1,0:T(8,128)(2,1)}, bf16[64,768]{1,0:T(8,128)(2,1)S(1)}, u32[]{:S(2)}, u32[]{:S(2)}) collective-permute-start(bf16[64,768]{1,0:T(8,128)(2,1)} %get-tuple-element.31.refs_1_), channel_id=1, source_target_pairs={{0,2},{2,0},{4,6},{6,4},{8,10},{10,8},{12,14},{14,12},{1,3},{3,1},... | collective-permute-start | bytes 294920 | tf_op jit(solution)/shard_map/ppermute | solution.py:141
  8.9 1.7 %collective-permute-done.2.refs_0_ = bf16[72,768]{1,0:T(8,128)(2,1)S(1)} collective-permute-done((bf16[72,768]{1,0:T(8,128)(2,1)}, bf16[72,768]{1,0:T(8,128)(2,1)S(1)}, u32[]{:S(2)}, u32[]{:S(2)}) %collective-permute-start.2) | collective-permute-done | bytes 110624 | tf_op jit(solution)/shard_map/ppermute | solution.py:144
  10.6 0.0 collective-permute-done.3.refs_4_
  10.6 1.4 %collective-permute-start.6 = (bf16[72,768]{1,0:T(8,128)(2,1)S(1)}, bf16[72,768]{1,0:T(8,128)(2,1)S(1)}, u32[]{:S(2)}, u32[]{:S(2)}) collective-permute-start(bf16[72,768]{1,0:T(8,128)(2,1)S(1)} %collective-permute-done.2.refs_0_), channel_id=1, source_target_pairs={{0,4},{2,6},{4,8},{6,10},{8,12},{10,14},{12,0},{14,2},{1,5},{3,7},... | collective-permute-start | bytes 331784 | tf_op jit(solution)/shard_map/ppermute | solution.py:144
  12.0 2.4 %collective-permute-start.7 = (bf16[72,768]{1,0:T(8,128)(2,1)S(1)}, bf16[72,768]{1,0:T(8,128)(2,1)S(1)}, u32[]{:S(2)}, u32[]{:S(2)}) collective-permute-start(bf16[72,768]{1,0:T(8,128)(2,1)S(1)} %collective-permute-done.2.refs_0_), channel_id=1, source_target_pairs={{0,2},{2,0},{4,6},{6,4},{8,10},{10,8},{12,14},{14,12},{1,3},{3,1},... | collective-permute-start | bytes 331784 | tf_op jit(solution)/shard_map/ppermute | solution.py:141
  14.4 0.0 collective-permute-done.4.refs_1_
  14.4 0.0 collective-permute-done.5.refs_5_
  14.4 1.4 %collective-permute-start.8 = (bf16[64,768]{1,0:T(8,128)(2,1)S(1)}, bf16[64,768]{1,0:T(8,128)(2,1)S(1)}, u32[]{:S(2)}, u32[]{:S(2)}) collective-permute-start(bf16[64,768]{1,0:T(8,128)(2,1)S(1)} %collective-permute-done.4.refs_1_), channel_id=1, source_target_pairs={{0,4},{2,6},{4,8},{6,10},{8,12},{10,14},{12,0},{14,2},{1,5},{3,7},... | collective-permute-start | bytes 294920 | tf_op jit(solution)/shard_map/ppermute | solution.py:144
  15.7 2.4 %collective-permute-done.6.refs_0_ = bf16[72,768]{1,0:T(8,128)(2,1)S(1)} collective-permute-done((bf16[72,768]{1,0:T(8,128)(2,1)S(1)}, bf16[72,768]{1,0:T(8,128)(2,1)S(1)}, u32[]{:S(2)}, u32[]{:S(2)}) %collective-permute-start.6) | collective-permute-done | bytes 110624 | tf_op jit(solution)/shard_map/ppermute | solution.py:144
  18.2 0.0 collective-permute-done.7.refs_2_
  18.2 1.2 %collective-permute-start.10 = (bf16[72,768]{1,0:T(8,128)(2,1)S(1)}, bf16[72,768]{1,0:T(8,128)(2,1)S(1)}, u32[]{:S(2)}, u32[]{:S(2)}) collective-permute-start(bf16[72,768]{1,0:T(8,128)(2,1)S(1)} %collective-permute-done.6.refs_0_), channel_id=1, source_target_pairs={{0,4},{2,6},{4,8},{6,10},{8,12},{10,14},{12,0},{14,2},{1,5},{3,7},... | collective-permute-start | bytes 331784 | tf_op jit(solution)/shard_map/ppermute | solution.py:144
  19.4 1.5 %collective-permute-start.9 = (bf16[64,768]{1,0:T(8,128)(2,1)S(1)}, bf16[64,768]{1,0:T(8,128)(2,1)S(1)}, u32[]{:S(2)}, u32[]{:S(2)}) collective-permute-start(bf16[64,768]{1,0:T(8,128)(2,1)S(1)} %collective-permute-done.4.refs_1_), channel_id=1, source_target_pairs={{0,2},{2,0},{4,6},{6,4},{8,10},{10,8},{12,14},{14,12},{1,3},{3,1},... | collective-permute-start | bytes 294920 | tf_op jit(solution)/shard_map/ppermute | solution.py:141
  20.9 0.5 %collective-permute-start.11 = (bf16[72,768]{1,0:T(8,128)(2,1)S(1)}, bf16[72,768]{1,0:T(8,128)(2,1)S(1)}, u32[]{:S(2)}, u32[]{:S(2)}) collective-permute-start(bf16[72,768]{1,0:T(8,128)(2,1)S(1)} %collective-permute-done.6.refs_0_), channel_id=1, source_target_pairs={{0,2},{2,0},{4,6},{6,4},{8,10},{10,8},{12,14},{14,12},{1,3},{3,1},... | collective-permute-start | bytes 331784 | tf_op jit(solution)/shard_map/ppermute | solution.py:141
  21.4 0.0 collective-permute-start.1
  21.4 0.4 %collective-permute-done.8.refs_1_ = bf16[64,768]{1,0:T(8,128)(2,1)S(1)} collective-permute-done((bf16[64,768]{1,0:T(8,128)(2,1)S(1)}, bf16[64,768]{1,0:T(8,128)(2,1)S(1)}, u32[]{:S(2)}, u32[]{:S(2)}) %collective-permute-start.8) | collective-permute-done | bytes 98336 | tf_op jit(solution)/shard_map/ppermute | solution.py:144
  21.8 0.1 collective-permute-start
  21.9 2.1 %collective-permute-done.9.refs_3_ = bf16[64,768]{1,0:T(8,128)(2,1)S(1)} collective-permute-done((bf16[64,768]{1,0:T(8,128)(2,1)S(1)}, bf16[64,768]{1,0:T(8,128)(2,1)S(1)}, u32[]{:S(2)}, u32[]{:S(2)}) %collective-permute-start.9) | collective-permute-done | bytes 98336 | tf_op jit(solution)/shard_map/ppermute | solution.py:141
  24.0 0.0 collective-permute-start.12
  24.0 0.7 %collective-permute-done.10.refs_0_ = bf16[72,768]{1,0:T(8,128)(2,1)S(1)} collective-permute-done((bf16[72,768]{1,0:T(8,128)(2,1)S(1)}, bf16[72,768]{1,0:T(8,128)(2,1)S(1)}, u32[]{:S(2)}, u32[]{:S(2)}) %collective-permute-start.10) | collective-permute-done | bytes 110624 | tf_op jit(solution)/shard_map/ppermute | solution.py:144
  24.7 1.9 %collective-permute-start.13 = (bf16[64,768]{1,0:T(8,128)(2,1)S(1)}, bf16[64,768]{1,0:T(8,128)(2,1)S(1)}, u32[]{:S(2)}, u32[]{:S(2)}) collective-permute-start(bf16[64,768]{1,0:T(8,128)(2,1)S(1)} %collective-permute-done.8.refs_1_), channel_id=1, source_target_pairs={{0,2},{2,0},{4,6},{6,4},{8,10},{10,8},{12,14},{14,12},{1,3},{3,1},... | collective-permute-start | bytes 294920 | tf_op jit(solution)/shard_map/ppermute | solution.py:141
  26.6 0.0 collective-permute-done.11.refs_2_
  26.6 0.5 %collective-permute-start.14 = (bf16[72,768]{1,0:T(8,128)(2,1)S(1)}, bf16[72,768]{1,0:T(8,128)(2,1)S(1)}, u32[]{:S(2)}, u32[]{:S(2)}) collective-permute-start(bf16[72,768]{1,0:T(8,128)(2,1)S(1)} %collective-permute-done.10.refs_0_), channel_id=1, source_target_pairs={{0,2},{2,0},{4,6},{6,4},{8,10},{10,8},{12,14},{14,12},{1,3},{3,1},... | collective-permute-start | bytes 331784 | tf_op jit(solution)/shard_map/ppermute | solution.py:141
  27.1 0.0 collective-permute-done.1.refs_3_
  27.1 2.7 %collective-permute-start.15 = (bf16[64,768]{1,0:T(8,128)(2,1)S(1)}, bf16[64,768]{1,0:T(8,128)(2,1)S(1)}, u32[]{:S(2)}, u32[]{:S(2)}) collective-permute-start(bf16[64,768]{1,0:T(8,128)(2,1)S(1)} %collective-permute-done.5.refs_5_), channel_id=1, source_target_pairs={{0,12},{2,14},{4,0},{6,2},{8,4},{10,6},{12,8},{14,10},{1,13},{3,15... | collective-permute-start | bytes 294920 | tf_op jit(solution)/shard_map/ppermute | solution.py:144
  29.8 0.0 collective-permute-done.refs_2_
  29.9 0.0 copy-start
  29.9 0.9 %copy-done = bf16[72,768]{1,0:T(8,128)(2,1)S(1)} copy-done((bf16[72,768]{1,0:T(8,128)(2,1)S(1)}, bf16[72,768]{1,0:T(8,128)(2,1)}, u32[]{:S(2)}) %copy-start) | copy-done | bytes 110616
  30.8 0.0 copy-start.1
  30.8 0.9 %copy-done.1 = bf16[64,768]{1,0:T(8,128)(2,1)S(1)} copy-done((bf16[64,768]{1,0:T(8,128)(2,1)S(1)}, bf16[64,768]{1,0:T(8,128)(2,1)}, u32[]{:S(2)}) %copy-start.1) | copy-done | bytes 98328
  31.6 1.0 %first_scores.1 = (bf16[256,768]{1,0:T(8,128)(2,1)S(1)}, f32[256,128]{1,0:T(8,128)S(1)}, f32[256,128]{1,0:T(8,128)S(1)}, f32[256,768]{1,0:T(8,128)S(1)}) custom-call(bf16[72,768]{1,0:T(8,128)(2,1)S(1)} %copy-done, bf16[64,768]{1,0:T(8,128)(2,1)S(1)} %copy-done.1, bf16[72,768]{1,0:T(8,128)(2,1)S(1)} %collective-permute-done.refs_2_, ...), custom_call_target="tpu_custom_call" | custom-call | flops 201326592 | bytes 1966080 | tf_op jit(solution)/shard_map/first_scores/pallas_call | solution.py:155
  32.6 0.9 %more_scores.4 = (f32[256,128]{1,0:T(8,128)S(1)}, f32[256,768]{1,0:T(8,128)S(1)}) custom-call(bf16[256,768]{1,0:T(8,128)(2,1)S(1)} %get-tuple-element.34.unit_ref, f32[256,128]{1,0:T(8,128)S(1)} %get-tuple-element.35.side_ref, f32[256,128]{1,0:T(8,128)S(1)} %get-tuple-element.36.old_sums_ref, ...), custom_call_target="tpu_custom_call", output_to_operand_aliasing={{0}: (2, {}), {1}: (3, {})} | custom-call | flops 201326592 | bytes 1966080 | tf_op jit(solution)/shard_map/more_scores/pallas_call | solution.py:169
  33.5 0.0 collective-permute-done.12.refs_1_
  33.5 0.0 collective-permute-done.13.refs_3_
  33.5 0.9 %more_scores.5 = (f32[256,128]{1,0:T(8,128)S(1)}, f32[256,768]{1,0:T(8,128)S(1)}) custom-call(bf16[256,768]{1,0:T(8,128)(2,1)S(1)} %get-tuple-element.34.unit_ref, f32[256,128]{1,0:T(8,128)S(1)} %get-tuple-element.35.side_ref, f32[256,128]{1,0:T(8,128)S(1)} %get-tuple-element.42.old_sums_ref, ...), custom_call_target="tpu_custom_call", output_to_operand_aliasing={{0}: (2, {}), {1}: (3, {})} | custom-call | flops 201326592 | bytes 1966080 | tf_op jit(solution)/shard_map/more_scores/pallas_call | solution.py:169
  34.5 0.7 %more_scores.6 = (f32[256,128]{1,0:T(8,128)S(1)}, f32[256,768]{1,0:T(8,128)S(1)}) custom-call(bf16[256,768]{1,0:T(8,128)(2,1)S(1)} %get-tuple-element.34.unit_ref, f32[256,128]{1,0:T(8,128)S(1)} %get-tuple-element.35.side_ref, f32[256,128]{1,0:T(8,128)S(1)} %get-tuple-element.48.old_sums_ref, ...), custom_call_target="tpu_custom_call", output_to_operand_aliasing={{0}: (2, {}), {1}: (3, {})} | custom-call | flops 100663296 | bytes 1769472 | tf_op jit(solution)/shard_map/more_scores/pallas_call | solution.py:169
  35.2 0.0 collective-permute-done.15.refs_1_
  35.2 0.0 collective-permute-done.14.refs_0_
  35.2 0.7 %more_scores.7 = (f32[256,128]{1,0:T(8,128)S(1)}, f32[256,768]{1,0:T(8,128)S(1)}) custom-call(bf16[256,768]{1,0:T(8,128)(2,1)S(1)} %get-tuple-element.34.unit_ref, f32[256,128]{1,0:T(8,128)S(1)} %get-tuple-element.35.side_ref, f32[256,128]{1,0:T(8,128)S(1)} %get-tuple-element.52.old_sums_ref, ...), custom_call_target="tpu_custom_call", output_to_operand_aliasing={{0}: (2, {}), {1}: (3, {})} | custom-call | flops 100663296 | bytes 1769472 | tf_op jit(solution)/shard_map/more_scores/pallas_call | solution.py:169
  35.9 0.1 fusion
  36.0 0.1 collective-permute-start.17
  36.1 0.6 %collective-permute-start.16 = (f32[128,128]{1,0:T(8,128)S(1)}, f32[128,128]{1,0:T(8,128)S(1)}, u32[]{:S(2)}, u32[]{:S(2)}) collective-permute-start(f32[128,128]{1,0:T(8,128)S(1)} %get-tuple-element.60), channel_id=1, source_target_pairs={{0,1},{1,0},{2,3},{3,2},{4,5},{5,4},{6,7},{7,6},{8,9},{9,8},{10,11... | collective-permute-start | bytes 196616 | tf_op jit(solution)/shard_map/ppermute | solution.py:147
  36.7 1.2 %collective-permute-done.16.other_sums_ref = f32[128,128]{1,0:T(8,128)S(1)} collective-permute-done((f32[128,128]{1,0:T(8,128)S(1)}, f32[128,128]{1,0:T(8,128)S(1)}, u32[]{:S(2)}, u32[]{:S(2)}) %collective-permute-start.16) | collective-permute-done | bytes 65568 | tf_op jit(solution)/shard_map/ppermute | solution.py:147
  37.9 0.0 collective-permute-done.17.other_mixed_ref
  37.9 0.9 %combine.1 = (f32[1,128]{1,0:T(1,128)}, f32[128,768]{1,0:T(8,128)}) custom-call(f32[128,128]{1,0:T(8,128)S(1)} %get-tuple-element.61.sums_ref, f32[128,768]{1,0:T(8,128)S(1)} %get-tuple-element.59.mixed_ref, f32[128,128]{1,0:T(8,128)S(1)} %collective-permute-done.16.other_sums_ref, f32[128,768]{1,0:T(8,128)S(1)} %collective-permute-done.17.other_mixed_ref), custom_call_target="tpu_custom_call" | custom-call | tf_op jit(solution)/shard_map/combine/pallas_call | solution.py:214
  (1 shorter events, 0.0 us)
Async XLA Ops:
  2.3 8.3 %collective-permute-start.2 = (bf16[72,768]{1,0:T(8,128)(2,1)}, bf16[72,768]{1,0:T(8,128)(2,1)S(1)}, u32[]{:S(2)}, u32[]{:S(2)}) collective-permute-start(bf16[72,768]{1,0:T(8,128)(2,1)} %get-tuple-element.30.refs_0_), channel_id=1, source_target_pairs={{0,4},{2,6},{4,8},{6,10},{8,12},{10,14},{12,0},{14,2},{1,5},{3,7},... | collective-permute-start | bytes 331784 | tf_op jit(solution)/shard_map/ppermute | solution.py:144
  5.3 5.3 %collective-permute-start.3 = (bf16[72,768]{1,0:T(8,128)(2,1)}, bf16[72,768]{1,0:T(8,128)(2,1)S(1)}, u32[]{:S(2)}, u32[]{:S(2)}) collective-permute-start(bf16[72,768]{1,0:T(8,128)(2,1)} %get-tuple-element.30.refs_0_), channel_id=1, source_target_pairs={{0,2},{2,0},{4,6},{6,4},{8,10},{10,8},{12,14},{14,12},{1,3},{3,1},... | collective-permute-start | bytes 331784 | tf_op jit(solution)/shard_map/ppermute | solution.py:141
  6.8 7.6 %collective-permute-start.4 = (bf16[64,768]{1,0:T(8,128)(2,1)}, bf16[64,768]{1,0:T(8,128)(2,1)S(1)}, u32[]{:S(2)}, u32[]{:S(2)}) collective-permute-start(bf16[64,768]{1,0:T(8,128)(2,1)} %get-tuple-element.31.refs_1_), channel_id=1, source_target_pairs={{0,4},{2,6},{4,8},{6,10},{8,12},{10,14},{12,0},{14,2},{1,5},{3,7},... | collective-permute-start | bytes 294920 | tf_op jit(solution)/shard_map/ppermute | solution.py:144
  8.4 6.0 %collective-permute-start.5 = (bf16[64,768]{1,0:T(8,128)(2,1)}, bf16[64,768]{1,0:T(8,128)(2,1)S(1)}, u32[]{:S(2)}, u32[]{:S(2)}) collective-permute-start(bf16[64,768]{1,0:T(8,128)(2,1)} %get-tuple-element.31.refs_1_), channel_id=1, source_target_pairs={{0,2},{2,0},{4,6},{6,4},{8,10},{10,8},{12,14},{14,12},{1,3},{3,1},... | collective-permute-start | bytes 294920 | tf_op jit(solution)/shard_map/ppermute | solution.py:141
  10.6 7.6 %collective-permute-start.6 = (bf16[72,768]{1,0:T(8,128)(2,1)S(1)}, bf16[72,768]{1,0:T(8,128)(2,1)S(1)}, u32[]{:S(2)}, u32[]{:S(2)}) collective-permute-start(bf16[72,768]{1,0:T(8,128)(2,1)S(1)} %collective-permute-done.2.refs_0_), channel_id=1, source_target_pairs={{0,4},{2,6},{4,8},{6,10},{8,12},{10,14},{12,0},{14,2},{1,5},{3,7},... | collective-permute-start | bytes 331784 | tf_op jit(solution)/shard_map/ppermute | solution.py:144
  12.0 6.2 %collective-permute-start.7 = (bf16[72,768]{1,0:T(8,128)(2,1)S(1)}, bf16[72,768]{1,0:T(8,128)(2,1)S(1)}, u32[]{:S(2)}, u32[]{:S(2)}) collective-permute-start(bf16[72,768]{1,0:T(8,128)(2,1)S(1)} %collective-permute-done.2.refs_0_), channel_id=1, source_target_pairs={{0,2},{2,0},{4,6},{6,4},{8,10},{10,8},{12,14},{14,12},{1,3},{3,1},... | collective-permute-start | bytes 331784 | tf_op jit(solution)/shard_map/ppermute | solution.py:141
  14.4 7.5 %collective-permute-start.8 = (bf16[64,768]{1,0:T(8,128)(2,1)S(1)}, bf16[64,768]{1,0:T(8,128)(2,1)S(1)}, u32[]{:S(2)}, u32[]{:S(2)}) collective-permute-start(bf16[64,768]{1,0:T(8,128)(2,1)S(1)} %collective-permute-done.4.refs_1_), channel_id=1, source_target_pairs={{0,4},{2,6},{4,8},{6,10},{8,12},{10,14},{12,0},{14,2},{1,5},{3,7},... | collective-permute-start | bytes 294920 | tf_op jit(solution)/shard_map/ppermute | solution.py:144
  18.2 6.5 %collective-permute-start.10 = (bf16[72,768]{1,0:T(8,128)(2,1)S(1)}, bf16[72,768]{1,0:T(8,128)(2,1)S(1)}, u32[]{:S(2)}, u32[]{:S(2)}) collective-permute-start(bf16[72,768]{1,0:T(8,128)(2,1)S(1)} %collective-permute-done.6.refs_0_), channel_id=1, source_target_pairs={{0,4},{2,6},{4,8},{6,10},{8,12},{10,14},{12,0},{14,2},{1,5},{3,7},... | collective-permute-start | bytes 331784 | tf_op jit(solution)/shard_map/ppermute | solution.py:144
  19.4 4.6 %collective-permute-start.9 = (bf16[64,768]{1,0:T(8,128)(2,1)S(1)}, bf16[64,768]{1,0:T(8,128)(2,1)S(1)}, u32[]{:S(2)}, u32[]{:S(2)}) collective-permute-start(bf16[64,768]{1,0:T(8,128)(2,1)S(1)} %collective-permute-done.4.refs_1_), channel_id=1, source_target_pairs={{0,2},{2,0},{4,6},{6,4},{8,10},{10,8},{12,14},{14,12},{1,3},{3,1},... | collective-permute-start | bytes 294920 | tf_op jit(solution)/shard_map/ppermute | solution.py:141
  20.9 5.7 %collective-permute-start.11 = (bf16[72,768]{1,0:T(8,128)(2,1)S(1)}, bf16[72,768]{1,0:T(8,128)(2,1)S(1)}, u32[]{:S(2)}, u32[]{:S(2)}) collective-permute-start(bf16[72,768]{1,0:T(8,128)(2,1)S(1)} %collective-permute-done.6.refs_0_), channel_id=1, source_target_pairs={{0,2},{2,0},{4,6},{6,4},{8,10},{10,8},{12,14},{14,12},{1,3},{3,1},... | collective-permute-start | bytes 331784 | tf_op jit(solution)/shard_map/ppermute | solution.py:141
  21.4 5.7 %collective-permute-start.1 = (bf16[64,768]{1,0:T(8,128)(2,1)}, bf16[64,768]{1,0:T(8,128)(2,1)S(1)}, u32[]{:S(2)}, u32[]{:S(2)}) collective-permute-start(bf16[64,768]{1,0:T(8,128)(2,1)} %get-tuple-element.31.refs_1_), channel_id=1, source_target_pairs={{0,1},{1,0},{2,3},{3,2},{4,5},{5,4},{6,7},{7,6},{8,9},{9,8},{10,11... | collective-permute-start | bytes 294920 | tf_op jit(solution)/shard_map/ppermute | solution.py:147
  21.8 8.0 %collective-permute-start = (bf16[72,768]{1,0:T(8,128)(2,1)}, bf16[72,768]{1,0:T(8,128)(2,1)S(1)}, u32[]{:S(2)}, u32[]{:S(2)}) collective-permute-start(bf16[72,768]{1,0:T(8,128)(2,1)} %get-tuple-element.30.refs_0_), channel_id=1, source_target_pairs={{0,1},{1,0},{2,3},{3,2},{4,5},{5,4},{6,7},{7,6},{8,9},{9,8},{10,11... | collective-permute-start | bytes 331784 | tf_op jit(solution)/shard_map/ppermute | solution.py:147
  24.0 9.5 %collective-permute-start.12 = (bf16[64,768]{1,0:T(8,128)(2,1)S(1)}, bf16[64,768]{1,0:T(8,128)(2,1)S(1)}, u32[]{:S(2)}, u32[]{:S(2)}) collective-permute-start(bf16[64,768]{1,0:T(8,128)(2,1)S(1)} %collective-permute-done.8.refs_1_), channel_id=1, source_target_pairs={{0,4},{2,6},{4,8},{6,10},{8,12},{10,14},{12,0},{14,2},{1,5},{3,7},... | collective-permute-start | bytes 294920 | tf_op jit(solution)/shard_map/ppermute | solution.py:144
  24.7 8.8 %collective-permute-start.13 = (bf16[64,768]{1,0:T(8,128)(2,1)S(1)}, bf16[64,768]{1,0:T(8,128)(2,1)S(1)}, u32[]{:S(2)}, u32[]{:S(2)}) collective-permute-start(bf16[64,768]{1,0:T(8,128)(2,1)S(1)} %collective-permute-done.8.refs_1_), channel_id=1, source_target_pairs={{0,2},{2,0},{4,6},{6,4},{8,10},{10,8},{12,14},{14,12},{1,3},{3,1},... | collective-permute-start | bytes 294920 | tf_op jit(solution)/shard_map/ppermute | solution.py:141
  26.6 8.6 %collective-permute-start.14 = (bf16[72,768]{1,0:T(8,128)(2,1)S(1)}, bf16[72,768]{1,0:T(8,128)(2,1)S(1)}, u32[]{:S(2)}, u32[]{:S(2)}) collective-permute-start(bf16[72,768]{1,0:T(8,128)(2,1)S(1)} %collective-permute-done.10.refs_0_), channel_id=1, source_target_pairs={{0,2},{2,0},{4,6},{6,4},{8,10},{10,8},{12,14},{14,12},{1,3},{3,1},... | collective-permute-start | bytes 331784 | tf_op jit(solution)/shard_map/ppermute | solution.py:141
  27.1 8.1 %collective-permute-start.15 = (bf16[64,768]{1,0:T(8,128)(2,1)S(1)}, bf16[64,768]{1,0:T(8,128)(2,1)S(1)}, u32[]{:S(2)}, u32[]{:S(2)}) collective-permute-start(bf16[64,768]{1,0:T(8,128)(2,1)S(1)} %collective-permute-done.5.refs_5_), channel_id=1, source_target_pairs={{0,12},{2,14},{4,0},{6,2},{8,4},{10,6},{12,8},{14,10},{1,13},{3,15... | collective-permute-start | bytes 294920 | tf_op jit(solution)/shard_map/ppermute | solution.py:144
  29.9 0.9 %copy-start = (bf16[72,768]{1,0:T(8,128)(2,1)S(1)}, bf16[72,768]{1,0:T(8,128)(2,1)}, u32[]{:S(2)}) copy-start(bf16[72,768]{1,0:T(8,128)(2,1)} %get-tuple-element.30.refs_0_) | copy-start | bytes 331780
  30.8 0.9 %copy-start.1 = (bf16[64,768]{1,0:T(8,128)(2,1)S(1)}, bf16[64,768]{1,0:T(8,128)(2,1)}, u32[]{:S(2)}) copy-start(bf16[64,768]{1,0:T(8,128)(2,1)} %get-tuple-element.31.refs_1_) | copy-start | bytes 294916
  36.0 1.9 %collective-permute-start.17 = (f32[128,768]{1,0:T(8,128)S(1)}, f32[128,768]{1,0:T(8,128)S(1)}, u32[]{:S(2)}, u32[]{:S(2)}) collective-permute-start(f32[128,768]{1,0:T(8,128)S(1)} %get-tuple-element.58), channel_id=1, source_target_pairs={{0,1},{1,0},{2,3},{3,2},{4,5},{5,4},{6,7},{7,6},{8,9},{9,8},{10,11... | collective-permute-start | bytes 1179656 | tf_op jit(solution)/shard_map/ppermute | solution.py:147
  36.1 1.8 %collective-permute-start.16 = (f32[128,128]{1,0:T(8,128)S(1)}, f32[128,128]{1,0:T(8,128)S(1)}, u32[]{:S(2)}, u32[]{:S(2)}) collective-permute-start(f32[128,128]{1,0:T(8,128)S(1)} %get-tuple-element.60), channel_id=1, source_target_pairs={{0,1},{1,0},{2,3},{3,2},{4,5},{5,4},{6,7},{7,6},{8,9},{9,8},{10,11... | collective-permute-start | bytes 196616 | tf_op jit(solution)/shard_map/ppermute | solution.py:147

commit v4 on v2

v4 whole, which is shorter than its diff:
```python
import jax
import jax.numpy as jnp
from jax import lax
from jax.experimental import pallas as pl
from jax.experimental.pallas import tpu as pltpu
from jax.sharding import PartitionSpec as P

EXTRA = 8
VMEM = 24 * 1024 * 1024


def make_unit(rows):
    wide = rows.astype(jnp.float32)
    scale = lax.rsqrt(jnp.mean(wide * wide, axis=-1, keepdims=True) + 1e-06) / jnp.sqrt(
        jnp.float32(rows.shape[-1])
    )
    return (wide * scale).astype(jnp.bfloat16)


def diagonal(count):
    down = lax.broadcasted_iota(jnp.int32, (count, count), 0)
    return down == lax.broadcasted_iota(jnp.int32, (count, count), 1)


def as_row(column):
    return jnp.sum(jnp.where(diagonal(column.shape[0]), column, 0.0), axis=0, keepdims=True)


def as_column(row):
    return jnp.sum(jnp.where(diagonal(row.shape[1]), row, 0.0), axis=1, keepdims=True)


def halves(value):
    high = value.astype(jnp.bfloat16)
    return high, (value - high.astype(jnp.float32)).astype(jnp.bfloat16)


def pack_kernel(rows_ref, label_ref, rank_ref, packed_ref):
    count, width = rows_ref.shape
    packed_ref[:count, :] = rows_ref[...]
    rank = rank_ref[...]
    high = lax.shift_right_logical(rank, 8)
    low = rank - lax.shift_left(high, 8)
    pieces = [piece.astype(jnp.float32) for piece in (label_ref[...], high, low)]
    pieces.append(jnp.zeros((1, width - 3 * count), jnp.float32))
    line = jnp.concatenate(pieces, axis=1)
    packed_ref[count:, :] = jnp.broadcast_to(line, (EXTRA, width)).astype(jnp.bfloat16)


def labels_and_ranks(block):
    count = block.shape[0] - EXTRA
    line = block[count:, :].astype(jnp.float32)[:1]
    label, high, low = (line[:, at * count : (at + 1) * count] for at in range(3))
    return label, high * 256.0 + low


def rows_of(blocks):
    return jnp.concatenate([block[: block.shape[0] - EXTRA, :] for block in blocks], axis=0)


def score(unit, side, blocks):
    own_label, own_rank = side[:, 0:1], side[:, 1:2]
    keys = rows_of(blocks)
    sides = [labels_and_ranks(block) for block in blocks]
    label = jnp.concatenate([item[0] for item in sides], axis=1)
    rank = jnp.concatenate([item[1] for item in sides], axis=1)
    cosine = lax.dot_general(
        unit, make_unit(keys), (((1,), (1,)), ((), ())), preferred_element_type=jnp.float32
    )
    weight = 1.0 / (1.0 + jnp.exp(-40.0 * (cosine - 0.05)))
    near = jnp.where((label == own_label) & (rank != own_rank), weight, 0.0)
    earlier = jnp.sum(jnp.where(rank < own_rank, near, 0.0), axis=1, keepdims=True)
    every = jnp.sum(near, axis=1, keepdims=True)
    mixed = jnp.dot(near.astype(jnp.bfloat16), keys, preferred_element_type=jnp.float32)
    return earlier, every, mixed


def first_kernel(own_ref, other_ref, *refs):
    blocks, (unit_ref, side_ref, sums_ref, mixed_ref) = refs[:-4], refs[-4:]
    count = own_ref.shape[0] - EXTRA
    side_ref[...] = jnp.zeros_like(side_ref)
    sums_ref[...] = jnp.zeros_like(sums_ref)
    unit_ref[...] = make_unit(rows_of([own_ref, other_ref]))
    for at, ref in enumerate((own_ref, other_ref)):
        here = slice(at * count, (at + 1) * count)
        label, rank = labels_and_ranks(ref)
        side_ref[here, 0:1] = as_column(label)
        side_ref[here, 1:2] = as_column(rank)
    sums_ref[:, 0:1], sums_ref[:, 1:2], mixed_ref[...] = score(
        unit_ref[...], side_ref, (own_ref,) + blocks
    )


def more_kernel(unit_ref, side_ref, old_sums_ref, old_mixed_ref, *refs):
    blocks, (sums_ref, mixed_ref) = refs[:-2], refs[-2:]
    earlier, every, mixed = score(unit_ref[...], side_ref, blocks)
    sums_ref[...] = old_sums_ref[...]
    sums_ref[:, 0:1] += earlier
    sums_ref[:, 1:2] += every
    mixed_ref[...] = old_mixed_ref[...] + mixed


def final_kernel(unit_ref, side_ref, old_sums_ref, old_mixed_ref, *refs):
    blocks, (keep_sums_ref, keep_ref, send_ref) = refs[:-3], refs[-3:]
    count, width = keep_ref.shape
    earlier, every, mixed = score(unit_ref[...], side_ref, blocks)
    earlier += old_sums_ref[:, 0:1]
    every += old_sums_ref[:, 1:2]
    mixed += old_mixed_ref[...]
    keep_sums_ref[...] = jnp.zeros_like(keep_sums_ref)
    keep_sums_ref[:, 0:1] = earlier[:count]
    keep_sums_ref[:, 1:2] = every[:count]
    keep_ref[...] = mixed[:count]
    send_ref[:count, :] = mixed[count:].astype(jnp.bfloat16)
    pieces = halves(as_row(earlier[count:])) + halves(as_row(every[count:]))
    pieces = [piece.astype(jnp.float32) for piece in pieces]
    pieces.append(jnp.zeros((1, width - 4 * count), jnp.float32))
    line = jnp.concatenate(pieces, axis=1)
    send_ref[count:, :] = jnp.broadcast_to(line, (EXTRA, width)).astype(jnp.bfloat16)


def combine_kernel(sums_ref, mixed_ref, got_ref, dup_ref, out_ref):
    count = mixed_ref.shape[0]
    line = got_ref[count:, :].astype(jnp.float32)[:1]
    parts = [line[:, at * count : (at + 1) * count] for at in range(4)]
    every = sums_ref[:, 1:2] + as_column(parts[2] + parts[3])
    dup_ref[...] = jnp.log1p(as_row(sums_ref[:, 0:1]) + parts[0] + parts[1])
    mixed = mixed_ref[...] + got_ref[:count, :].astype(jnp.float32)
    out_ref[...] = mixed / jnp.sqrt(1.0 + every)


def cost(queries, keys, width):
    return pl.CostEstimate(
        flops=400 * queries * keys * width,
        bytes_accessed=8 * queries * width + 2 * keys * width,
        transcendentals=100 * queries * keys,
    )


def local(embeddings, cluster_id, priority):
    count, width = embeddings.shape
    height = count + EXTRA
    shards = lax.axis_size("shard")
    lanes = lax.axis_size("owner")
    rounds = shards // 2
    queries = 2 * count
    bf16, f32 = jnp.bfloat16, jnp.float32
    params = pltpu.CompilerParams(vmem_limit_bytes=VMEM)

    def shape(*dims, dtype=f32):
        return jax.ShapeDtypeStruct(dims, dtype)

    ring = list(range(0, rounds, 2)) + list(range(1, rounds, 2))[::-1]

    def along(array, step):
        pairs = [
            (2 * ring[at] + side, 2 * ring[(at + step) % rounds] + side)
            for at in range(rounds)
            for side in range(2)
        ]
        return lax.ppermute(array, "shard", pairs)

    def across(array):
        return lax.ppermute(array, "shard", [(at, at ^ 1) for at in range(shards)])

    def swap(array):
        return lax.ppermute(array, "owner", [(at, lanes - 1 - at) for at in range(lanes)])

    def first(*blocks):
        return pl.pallas_call(
            first_kernel,
            out_shape=[
                shape(queries, width, dtype=bf16),
                shape(queries, 128),
                shape(queries, 128),
                shape(queries, width),
            ],
            cost_estimate=cost(queries, (len(blocks) - 1) * count, width),
            compiler_params=params,
            name="first_scores",
        )(*blocks)

    def more(unit, side, sums, mixed, *blocks):
        return pl.pallas_call(
            more_kernel,
            out_shape=[shape(queries, 128), shape(queries, width)],
            input_output_aliases={2: 0, 3: 1},
            cost_estimate=cost(queries, len(blocks) * count, width),
            compiler_params=params,
            name="more_scores",
        )(unit, side, sums, mixed, *blocks)

    def final(unit, side, sums, mixed, *blocks):
        return pl.pallas_call(
            final_kernel,
            out_shape=[
                shape(count, 128),
                shape(count, width),
                shape(height, width, dtype=bf16),
            ],
            cost_estimate=cost(queries, len(blocks) * count, width),
            compiler_params=params,
            name="final_scores",
        )(unit, side, sums, mixed, *blocks)

    own = pl.pallas_call(
        pack_kernel,
        out_shape=shape(height, width, dtype=bf16),
        compiler_params=params,
        name="pack",
    )(embeddings, cluster_id.reshape(1, count), priority.reshape(1, count))

    moved, beside = along(own, 1), across(own)
    other = swap(own)
    if rounds == 4:
        moved, beside, other = lax.optimization_barrier((moved, beside, other))
        corner = along(beside, -1)
        moved_1, beside_1 = along(moved, 1), across(moved)
        state = first(own, other, beside)
        unit, side = state[:2]
        moved_1, beside_1 = lax.optimization_barrier((moved_1, beside_1))
        moved_2, beside_2 = along(moved_1, 1), across(moved_1)
        sums, mixed = more(*state, moved, moved_1, beside_1)
        sums, mixed = more(unit, side, sums, mixed, corner)
        moved, beside = moved_2, beside_2
    else:
        unit, side, sums, mixed = first(own, other, beside)

        def turn(at, state):
            moved, sums, mixed = state
            ahead, beside = along(moved, 1), across(moved)
            sums, mixed = more(unit, side, sums, mixed, moved, beside)
            return ahead, sums, mixed

        moved, sums, mixed = lax.fori_loop(1, rounds - 1, turn, (moved, sums, mixed))
        beside = across(moved)
    keep_sums, keep, send = final(unit, side, sums, mixed, moved, beside)
    dup, out = pl.pallas_call(
        combine_kernel,
        out_shape=[shape(1, count), shape(count, width)],
        compiler_params=params,
        name="combine",
    )(keep_sums, keep, swap(send))
    return dup[0], out


def solution(mesh):
    placed = (
        P(("groups", "shard", "owner"), None),
        P(("groups", "shard", "owner"), None),
        P(("groups", "shard", "owner")),
    )
    return jax.shard_map(
        local,
        mesh=mesh,
        in_specs=placed,
        out_specs=(P(("groups", "shard", "owner")), P(("groups", "shard", "owner"), None)),
        check_vma=False,
    )
```

time: 39 us -> 32.8 us (0.84)
  waiting for transfers between devices: 20.5 us -> 12 us
  starting transfers between devices: 10.5 us -> 13.9 us
  Pallas kernels: 6.18 us -> 4.54 us
  local copies, waits for them, and re-layouts: 1 us -> 1.58 us
    ppermute x3 -> x4, waiting for transfers between devices: 18.2 us -> 6.81 us  [along(): return lax.ppermute(array, 'shard', pairs)]
    ppermute x3 -> x4, starting transfers between devices: 4.14 us -> 9.32 us  [along(): return lax.ppermute(array, 'shard', pairs)]
    ppermute x4 -> x3, waiting for transfers between devices: 1.01 us -> 3.75 us  [across(): return lax.ppermute(array, 'shard', [(at, at ^ 1) for at in range(shards)])]
    pallas_call x6, Pallas kernels: 6.18 us -> 4.54 us  [the longest x2 1.76 us: more(): pl.pallas_call(more_kernel, out_shape=[shape(queries, 128), shape(queries...]
    ppermute x4 -> x3, starting transfers between devices: 5.72 us -> 4.47 us  [across(): return lax.ppermute(array, 'shard', [(at, at ^ 1) for at in range(shards)])]
    unnamed x2 -> x6, local copies, waits for them, and re-layouts: 0.94 us -> 1.58 us
    ppermute x3 -> x2, starting transfers between devices: 0.63 us -> 0.07 us  [swap(): lax.ppermute(array, 'owner', [(at, lanes - 1 - at) for at in range(lanes)])]
    ppermute x3 -> x2, waiting for transfers between devices: 1.23 us -> 1.45 us  [swap(): lax.ppermute(array, 'owner', [(at, lanes - 1 - at) for at in range(lanes)])]
  transfers between devices with their start and end apart: 10 -> 9, of which waited for: 5 -> 7; matrix products, arithmetic and copies ran while one was open for 0% -> 0% of each run, Pallas kernels for 7% -> 8%
where the time goes in v4:
time: 32.8 us; the launch traced here: 32.7 us
  starting transfers between devices  13.9 us (42%)
  waiting for transfers between devices  12 us (37%)
  Pallas kernels  4.54 us (14%)
  local copies, waits for them, and re-layouts  1.58 us (5%)
  between operations  0.69 us (2%)
    ppermute x4, starting transfers between devices, along(): return lax.ppermute(array, 'shard', pairs)  9.32 us
    ppermute x4, waiting for transfers between devices, along(): return lax.ppermute(array, 'shard', pairs)  6.81 us
    ppermute x3, starting transfers between devices, across(): return lax.ppermute(array, 'shard', [(at, at ^ 1) for at in range(shards)])  4.47 us
    ppermute x3, waiting for transfers between devices, across(): return lax.ppermute(array, 'shard', [(at, at ^ 1) for at in range(shards)])  3.75 us
    pallas_call x2, Pallas kernels, more(): pl.pallas_call(more_kernel, out_shape=[shape(queries, 128), shape(queries...  1.76 us
    unnamed x6, local copies, waits for them, and re-layouts  1.58 us
    ppermute x2, waiting for transfers between devices, swap(): lax.ppermute(array, 'owner', [(at, lanes - 1 - at) for at in range(lanes)])  1.45 us
    pallas_call x1, Pallas kernels, first(): pl.pallas_call(first_kernel, out_shape=[shape(queries, width, dtype=bf16)...  0.96 us
  transfers between devices with their start and end apart: 9, of which 7 were waited for; matrix products, arithmetic and copies ran while one was open for 0% of the time, Pallas kernels for 8%

profile of v4, /device:TPU:0, one launch (start us, length us, event | category | flops | bytes accessed | tf_op | source)
XLA Modules:
  0.0 32.7 jit_solution(1354550810085825472)
XLA Ops:
  0.6 0.0 copy-start.1
  0.6 0.0 copy-start.2
  0.6 0.6 %copy-done.1 = s32[128,1]{0,1:T(1,128)S(1)} copy-done((s32[128,1]{0,1:T(1,128)S(1)}, s32[128,1]{0,1:T(1,128)}, u32[]{:S(2)}) %copy-start.1) | copy-done | bytes 536
  1.3 0.0 copy-done.2
  1.3 0.0 copy-start
  1.3 0.9 %copy-done = bf16[128,768]{1,0:T(8,128)(2,1)S(1)} copy-done((bf16[128,768]{1,0:T(8,128)(2,1)S(1)}, bf16[128,768]{1,0:T(8,128)(2,1)}, u32[]{:S(2)}) %copy-start) | copy-done | bytes 196632
  2.3 4.1 %collective-permute-start = (bf16[136,768]{1,0:T(8,128)(2,1)S(1)}, bf16[136,768]{1,0:T(8,128)(2,1)S(1)}, u32[]{:S(2)}, u32[]{:S(2)}) collective-permute-start(bf16[136,768]{1,0:T(8,128)(2,1)S(1)} %pack.1.own_ref), channel_id=1, source_target_pairs={{0,8},{2,10},{8,12},{10,14},{12,4},{14,6},{4,0},{6,2},{1,9},{3,11}... | collective-permute-start | bytes 626696 | tf_op jit(solution)/shard_map/ppermute | solution.py:161
  6.3 1.5 %collective-permute-start.1 = (bf16[136,768]{1,0:T(8,128)(2,1)S(1)}, bf16[136,768]{1,0:T(8,128)(2,1)S(1)}, u32[]{:S(2)}, u32[]{:S(2)}) collective-permute-start(bf16[136,768]{1,0:T(8,128)(2,1)S(1)} %pack.1.own_ref), channel_id=1, source_target_pairs={{0,2},{2,0},{4,6},{6,4},{8,10},{10,8},{12,14},{14,12},{1,3},{3,1},... | collective-permute-start | bytes 626696 | tf_op jit(solution)/shard_map/ppermute | solution.py:164
  7.8 0.0 collective-permute-start.2
  7.8 2.9 %collective-permute-done.refs_0_ = bf16[136,768]{1,0:T(8,128)(2,1)S(1)} collective-permute-done((bf16[136,768]{1,0:T(8,128)(2,1)S(1)}, bf16[136,768]{1,0:T(8,128)(2,1)S(1)}, u32[]{:S(2)}, u32[]{:S(2)}) %collective-permute-start) | collective-permute-done | bytes 208928 | tf_op jit(solution)/shard_map/ppermute | solution.py:161
  10.8 2.2 %collective-permute-done.1.refs_0_ = bf16[136,768]{1,0:T(8,128)(2,1)S(1)} collective-permute-done((bf16[136,768]{1,0:T(8,128)(2,1)S(1)}, bf16[136,768]{1,0:T(8,128)(2,1)S(1)}, u32[]{:S(2)}, u32[]{:S(2)}) %collective-permute-start.1) | collective-permute-done | bytes 208928 | tf_op jit(solution)/shard_map/ppermute | solution.py:164
  13.0 0.0 collective-permute-done.2.other_ref
  13.0 1.6 %collective-permute-start.3 = (bf16[136,768]{1,0:T(8,128)(2,1)S(1)}, bf16[136,768]{1,0:T(8,128)(2,1)S(1)}, u32[]{:S(2)}, u32[]{:S(2)}) collective-permute-start(bf16[136,768]{1,0:T(8,128)(2,1)S(1)} %collective-permute-done.refs_0_), channel_id=1, source_target_pairs={{0,8},{2,10},{8,12},{10,14},{12,4},{14,6},{4,0},{6,2},{1,9},{3,11}... | collective-permute-start | bytes 626696 | tf_op jit(solution)/shard_map/ppermute | solution.py:161
  14.5 1.5 %collective-permute-start.4 = (bf16[136,768]{1,0:T(8,128)(2,1)S(1)}, bf16[136,768]{1,0:T(8,128)(2,1)S(1)}, u32[]{:S(2)}, u32[]{:S(2)}) collective-permute-start(bf16[136,768]{1,0:T(8,128)(2,1)S(1)} %collective-permute-done.refs_0_), channel_id=1, source_target_pairs={{0,2},{2,0},{4,6},{6,4},{8,10},{10,8},{12,14},{14,12},{1,3},{3,1},... | collective-permute-start | bytes 626696 | tf_op jit(solution)/shard_map/ppermute | solution.py:164
  16.0 0.4 %collective-permute-start.5 = (bf16[136,768]{1,0:T(8,128)(2,1)S(1)}, bf16[136,768]{1,0:T(8,128)(2,1)S(1)}, u32[]{:S(2)}, u32[]{:S(2)}) collective-permute-start(bf16[136,768]{1,0:T(8,128)(2,1)S(1)} %collective-permute-done.1.refs_0_), channel_id=1, source_target_pairs={{0,4},{2,6},{8,0},{10,2},{12,8},{14,10},{4,12},{6,14},{1,5},{3,7},... | collective-permute-start | bytes 626696 | tf_op jit(solution)/shard_map/ppermute | solution.py:161
  16.5 1.0 %first_scores.1 = (bf16[256,768]{1,0:T(8,128)(2,1)S(1)}, f32[256,128]{1,0:T(8,128)S(1)}, f32[256,128]{1,0:T(8,128)S(1)}, f32[256,768]{1,0:T(8,128)S(1)}) custom-call(bf16[136,768]{1,0:T(8,128)(2,1)S(1)} %pack.1.own_ref, bf16[136,768]{1,0:T(8,128)(2,1)S(1)} %collective-permute-done.2.other_ref, bf16[136,768]{1,0:T(8,128)(2,1)S(1)} %collective-permute-done.1.refs_0_), custom_call_target="tpu_custom_call" | custom-call | flops 20132659200 | bytes 1966080 | tf_op jit(solution)/shard_map/first_scores/pallas_call | solution.py:170
  17.5 2.7 %collective-permute-done.3.refs_1_ = bf16[136,768]{1,0:T(8,128)(2,1)S(1)} collective-permute-done((bf16[136,768]{1,0:T(8,128)(2,1)S(1)}, bf16[136,768]{1,0:T(8,128)(2,1)S(1)}, u32[]{:S(2)}, u32[]{:S(2)}) %collective-permute-start.3) | collective-permute-done | bytes 208928 | tf_op jit(solution)/shard_map/ppermute | solution.py:161
  20.2 0.2 collective-permute-done.4.refs_2_
  20.3 3.2 %collective-permute-start.6 = (bf16[136,768]{1,0:T(8,128)(2,1)S(1)}, bf16[136,768]{1,0:T(8,128)(2,1)S(1)}, u32[]{:S(2)}, u32[]{:S(2)}) collective-permute-start(bf16[136,768]{1,0:T(8,128)(2,1)S(1)} %collective-permute-done.3.refs_1_), channel_id=1, source_target_pairs={{0,8},{2,10},{8,12},{10,14},{12,4},{14,6},{4,0},{6,2},{1,9},{3,11}... | collective-permute-start | bytes 626696 | tf_op jit(solution)/shard_map/ppermute | solution.py:161
  23.6 1.5 %collective-permute-start.7 = (bf16[136,768]{1,0:T(8,128)(2,1)S(1)}, bf16[136,768]{1,0:T(8,128)(2,1)S(1)}, u32[]{:S(2)}, u32[]{:S(2)}) collective-permute-start(bf16[136,768]{1,0:T(8,128)(2,1)S(1)} %collective-permute-done.3.refs_1_), channel_id=1, source_target_pairs={{0,2},{2,0},{4,6},{6,4},{8,10},{10,8},{12,14},{14,12},{1,3},{3,1},... | collective-permute-start | bytes 626696 | tf_op jit(solution)/shard_map/ppermute | solution.py:164
  25.0 1.1 %more_scores.2 = (f32[256,128]{1,0:T(8,128)S(1)}, f32[256,768]{1,0:T(8,128)S(1)}) custom-call(bf16[256,768]{1,0:T(8,128)(2,1)S(1)} %get-tuple-element.22.unit_ref, f32[256,128]{1,0:T(8,128)S(1)} %get-tuple-element.23.side_ref, f32[256,128]{1,0:T(8,128)S(1)} %get-tuple-element.24.old_sums_ref, ...), custom_call_target="tpu_custom_call", output_to_operand_aliasing={{0}: (2, {}), {1}: (3, {})} | custom-call | flops 30198988800 | bytes 2162688 | tf_op jit(solution)/shard_map/more_scores/pallas_call | solution.py:184
  26.1 0.0 collective-permute-done.5.refs_0_
  26.2 0.7 %more_scores.3 = (f32[256,128]{1,0:T(8,128)S(1)}, f32[256,768]{1,0:T(8,128)S(1)}) custom-call(bf16[256,768]{1,0:T(8,128)(2,1)S(1)} %get-tuple-element.22.unit_ref, f32[256,128]{1,0:T(8,128)S(1)} %get-tuple-element.23.side_ref, f32[256,128]{1,0:T(8,128)S(1)} %get-tuple-element.29.old_sums_ref, ...), custom_call_target="tpu_custom_call", output_to_operand_aliasing={{0}: (2, {}), {1}: (3, {})} | custom-call | flops 10066329600 | bytes 1769472 | tf_op jit(solution)/shard_map/more_scores/pallas_call | solution.py:184
  26.9 1.1 %collective-permute-done.6.refs_0_ = bf16[136,768]{1,0:T(8,128)(2,1)S(1)} collective-permute-done((bf16[136,768]{1,0:T(8,128)(2,1)S(1)}, bf16[136,768]{1,0:T(8,128)(2,1)S(1)}, u32[]{:S(2)}, u32[]{:S(2)}) %collective-permute-start.6) | collective-permute-done | bytes 208928 | tf_op jit(solution)/shard_map/ppermute | solution.py:161
  28.0 1.4 %collective-permute-done.7.refs_1_ = bf16[136,768]{1,0:T(8,128)(2,1)S(1)} collective-permute-done((bf16[136,768]{1,0:T(8,128)(2,1)S(1)}, bf16[136,768]{1,0:T(8,128)(2,1)S(1)}, u32[]{:S(2)}, u32[]{:S(2)}) %collective-permute-start.7) | collective-permute-done | bytes 208928 | tf_op jit(solution)/shard_map/ppermute | solution.py:164
  29.4 0.9 %final_scores.1 = (f32[128,128]{1,0:T(8,128)S(1)}, f32[128,768]{1,0:T(8,128)S(1)}, bf16[136,768]{1,0:T(8,128)(2,1)S(1)}) custom-call(bf16[256,768]{1,0:T(8,128)(2,1)S(1)} %get-tuple-element.22.unit_ref, f32[256,128]{1,0:T(8,128)S(1)} %get-tuple-element.23.side_ref, f32[256,128]{1,0:T(8,128)S(1)} %get-tuple-element.31.old_sums_ref, ...), custom_call_target="tpu_custom_call" | custom-call | flops 20132659200 | bytes 1966080 | tf_op jit(solution)/shard_map/final_scores/pallas_call | solution.py:194
  30.2 0.1 collective-permute-start.8
  30.3 1.4 %collective-permute-done.8.got_ref = bf16[136,768]{1,0:T(8,128)(2,1)S(1)} collective-permute-done((bf16[136,768]{1,0:T(8,128)(2,1)S(1)}, bf16[136,768]{1,0:T(8,128)(2,1)S(1)}, u32[]{:S(2)}, u32[]{:S(2)}) %collective-permute-start.8) | collective-permute-done | bytes 208928 | tf_op jit(solution)/shard_map/ppermute | solution.py:167
  31.7 1.0 %combine.1 = (f32[1,128]{1,0:T(1,128)}, f32[128,768]{1,0:T(8,128)}) custom-call(f32[128,128]{1,0:T(8,128)S(1)} %get-tuple-element.33.sums_ref, f32[128,768]{1,0:T(8,128)S(1)} %get-tuple-element.34.mixed_ref, bf16[136,768]{1,0:T(8,128)(2,1)S(1)} %collective-permute-done.8.got_ref), custom_call_target="tpu_custom_call" | custom-call | tf_op jit(solution)/shard_map/combine/pallas_call | solution.py:238
  (1 shorter events, 0.0 us)
Async XLA Ops:
  0.6 0.7 %copy-start.1 = (s32[128,1]{0,1:T(1,128)S(1)}, s32[128,1]{0,1:T(1,128)}, u32[]{:S(2)}) copy-start(s32[128,1]{0,1:T(1,128)} %param.4) | copy-start | bytes 1540
  0.6 0.7 %copy-start.2 = (s32[128]{0:T(128)S(1)}, s32[128]{0:T(128)}, u32[]{:S(2)}) copy-start(s32[128]{0:T(128)} %param.5) | copy-start | bytes 1540
  1.3 0.9 %copy-start = (bf16[128,768]{1,0:T(8,128)(2,1)S(1)}, bf16[128,768]{1,0:T(8,128)(2,1)}, u32[]{:S(2)}) copy-start(bf16[128,768]{1,0:T(8,128)(2,1)} %rows_ref.1) | copy-start | bytes 589828
  2.3 8.5 %collective-permute-start = (bf16[136,768]{1,0:T(8,128)(2,1)S(1)}, bf16[136,768]{1,0:T(8,128)(2,1)S(1)}, u32[]{:S(2)}, u32[]{:S(2)}) collective-permute-start(bf16[136,768]{1,0:T(8,128)(2,1)S(1)} %pack.1.own_ref), channel_id=1, source_target_pairs={{0,8},{2,10},{8,12},{10,14},{12,4},{14,6},{4,0},{6,2},{1,9},{3,11}... | collective-permute-start | bytes 626696 | tf_op jit(solution)/shard_map/ppermute | solution.py:161
  6.3 6.6 %collective-permute-start.1 = (bf16[136,768]{1,0:T(8,128)(2,1)S(1)}, bf16[136,768]{1,0:T(8,128)(2,1)S(1)}, u32[]{:S(2)}, u32[]{:S(2)}) collective-permute-start(bf16[136,768]{1,0:T(8,128)(2,1)S(1)} %pack.1.own_ref), channel_id=1, source_target_pairs={{0,2},{2,0},{4,6},{6,4},{8,10},{10,8},{12,14},{14,12},{1,3},{3,1},... | collective-permute-start | bytes 626696 | tf_op jit(solution)/shard_map/ppermute | solution.py:164
  7.8 5.1 %collective-permute-start.2 = (bf16[136,768]{1,0:T(8,128)(2,1)S(1)}, bf16[136,768]{1,0:T(8,128)(2,1)S(1)}, u32[]{:S(2)}, u32[]{:S(2)}) collective-permute-start(bf16[136,768]{1,0:T(8,128)(2,1)S(1)} %pack.1.own_ref), channel_id=1, source_target_pairs={{0,1},{1,0},{2,3},{3,2},{4,5},{5,4},{6,7},{7,6},{8,9},{9,8},{10,11... | collective-permute-start | bytes 626696 | tf_op jit(solution)/shard_map/ppermute | solution.py:167
  13.0 7.2 %collective-permute-start.3 = (bf16[136,768]{1,0:T(8,128)(2,1)S(1)}, bf16[136,768]{1,0:T(8,128)(2,1)S(1)}, u32[]{:S(2)}, u32[]{:S(2)}) collective-permute-start(bf16[136,768]{1,0:T(8,128)(2,1)S(1)} %collective-permute-done.refs_0_), channel_id=1, source_target_pairs={{0,8},{2,10},{8,12},{10,14},{12,4},{14,6},{4,0},{6,2},{1,9},{3,11}... | collective-permute-start | bytes 626696 | tf_op jit(solution)/shard_map/ppermute | solution.py:161
  14.5 5.8 %collective-permute-start.4 = (bf16[136,768]{1,0:T(8,128)(2,1)S(1)}, bf16[136,768]{1,0:T(8,128)(2,1)S(1)}, u32[]{:S(2)}, u32[]{:S(2)}) collective-permute-start(bf16[136,768]{1,0:T(8,128)(2,1)S(1)} %collective-permute-done.refs_0_), channel_id=1, source_target_pairs={{0,2},{2,0},{4,6},{6,4},{8,10},{10,8},{12,14},{14,12},{1,3},{3,1},... | collective-permute-start | bytes 626696 | tf_op jit(solution)/shard_map/ppermute | solution.py:164
  16.0 10.1 %collective-permute-start.5 = (bf16[136,768]{1,0:T(8,128)(2,1)S(1)}, bf16[136,768]{1,0:T(8,128)(2,1)S(1)}, u32[]{:S(2)}, u32[]{:S(2)}) collective-permute-start(bf16[136,768]{1,0:T(8,128)(2,1)S(1)} %collective-permute-done.1.refs_0_), channel_id=1, source_target_pairs={{0,4},{2,6},{8,0},{10,2},{12,8},{14,10},{4,12},{6,14},{1,5},{3,7},... | collective-permute-start | bytes 626696 | tf_op jit(solution)/shard_map/ppermute | solution.py:161
  20.3 7.6 %collective-permute-start.6 = (bf16[136,768]{1,0:T(8,128)(2,1)S(1)}, bf16[136,768]{1,0:T(8,128)(2,1)S(1)}, u32[]{:S(2)}, u32[]{:S(2)}) collective-permute-start(bf16[136,768]{1,0:T(8,128)(2,1)S(1)} %collective-permute-done.3.refs_1_), channel_id=1, source_target_pairs={{0,8},{2,10},{8,12},{10,14},{12,4},{14,6},{4,0},{6,2},{1,9},{3,11}... | collective-permute-start | bytes 626696 | tf_op jit(solution)/shard_map/ppermute | solution.py:161
  23.6 5.8 %collective-permute-start.7 = (bf16[136,768]{1,0:T(8,128)(2,1)S(1)}, bf16[136,768]{1,0:T(8,128)(2,1)S(1)}, u32[]{:S(2)}, u32[]{:S(2)}) collective-permute-start(bf16[136,768]{1,0:T(8,128)(2,1)S(1)} %collective-permute-done.3.refs_1_), channel_id=1, source_target_pairs={{0,2},{2,0},{4,6},{6,4},{8,10},{10,8},{12,14},{14,12},{1,3},{3,1},... | collective-permute-start | bytes 626696 | tf_op jit(solution)/shard_map/ppermute | solution.py:164
  30.2 1.5 %collective-permute-start.8 = (bf16[136,768]{1,0:T(8,128)(2,1)S(1)}, bf16[136,768]{1,0:T(8,128)(2,1)S(1)}, u32[]{:S(2)}, u32[]{:S(2)}) collective-permute-start(bf16[136,768]{1,0:T(8,128)(2,1)S(1)} %get-tuple-element.35), channel_id=1, source_target_pairs={{0,1},{1,0},{2,3},{3,2},{4,5},{5,4},{6,7},{7,6},{8,9},{9,8},{10,11... | collective-permute-start | bytes 626696 | tf_op jit(solution)/shard_map/ppermute | solution.py:167

commit v5 on v4

--- a/solution.py
+++ b/solution.py
@@ -213,16 +213,17 @@
     moved, beside = along(own, 1), across(own)
     other = swap(own)
     if rounds == 4:
+        ahead = along(own, -1)
         moved, beside, other = lax.optimization_barrier((moved, beside, other))
-        corner = along(beside, -1)
-        moved_1, beside_1 = along(moved, 1), across(moved)
-        state = first(own, other, beside)
+        opposite = along(moved, 1)
+        moved_beside = across(moved)
+        ahead_beside = along(beside, -1)
+        state = first(own, other, beside, ahead)
         unit, side = state[:2]
-        moved_1, beside_1 = lax.optimization_barrier((moved_1, beside_1))
-        moved_2, beside_2 = along(moved_1, 1), across(moved_1)
-        sums, mixed = more(*state, moved, moved_1, beside_1)
-        sums, mixed = more(unit, side, sums, mixed, corner)
-        moved, beside = moved_2, beside_2
+        opposite, moved_beside = lax.optimization_barrier((opposite, moved_beside))
+        last = [across(opposite)]
+        sums, mixed = more(*state, moved, moved_beside)
+        sums, mixed = more(unit, side, sums, mixed, opposite, ahead_beside)
     else:
         unit, side, sums, mixed = first(own, other, beside)
 
@@ -233,8 +234,8 @@
             return ahead, sums, mixed
 
         moved, sums, mixed = lax.fori_loop(1, rounds - 1, turn, (moved, sums, mixed))
-        beside = across(moved)
-    keep_sums, keep, send = final(unit, side, sums, mixed, moved, beside)
+        last = [moved, across(moved)]
+    keep_sums, keep, send = final(unit, side, sums, mixed, *last)
     dup, out = pl.pallas_call(
         combine_kernel,
         out_shape=[shape(1, count), shape(count, width)],

time: 32.8 us -> 32.3 us (0.985)
  starting transfers between devices: 13.9 us -> 11.6 us
  waiting for transfers between devices: 12 us -> 13.7 us
    ppermute x4, starting transfers between devices: 9.32 us -> 6.42 us  [along(): return lax.ppermute(array, 'shard', pairs)]
    ppermute x4, waiting for transfers between devices: 6.81 us -> 9.1 us  [along(): return lax.ppermute(array, 'shard', pairs)]
    ppermute x3, starting transfers between devices: 4.47 us -> 5.14 us  [across(): return lax.ppermute(array, 'shard', [(at, at ^ 1) for at in range(shards)])]
    ppermute x3, waiting for transfers between devices: 3.75 us -> 3.13 us  [across(): return lax.ppermute(array, 'shard', [(at, at ^ 1) for at in range(shards)])]
  transfers between devices with their start and end apart: 9 -> 9, of which waited for: 7 -> 7; matrix products, arithmetic and copies ran while one was open for 0% -> 0% of each run, Pallas kernels for 8% -> 9%
where the time goes in v5:
time: 32.3 us; the launch traced here: 32.1 us
  waiting for transfers between devices  13.7 us (42%)
  starting transfers between devices  11.6 us (36%)
  Pallas kernels  4.55 us (14%)
  local copies, waits for them, and re-layouts  1.58 us (5%)
  between operations  0.69 us (2%)
    ppermute x4, waiting for transfers between devices, along(): return lax.ppermute(array, 'shard', pairs)  9.1 us
    ppermute x4, starting transfers between devices, along(): return lax.ppermute(array, 'shard', pairs)  6.42 us
    ppermute x3, starting transfers between devices, across(): return lax.ppermute(array, 'shard', [(at, at ^ 1) for at in range(shards)])  5.14 us
    ppermute x3, waiting for transfers between devices, across(): return lax.ppermute(array, 'shard', [(at, at ^ 1) for at in range(shards)])  3.13 us
    pallas_call x2, Pallas kernels, more(): pl.pallas_call(more_kernel, out_shape=[shape(queries, 128), shape(queries...  1.81 us
    unnamed x6, local copies, waits for them, and re-layouts  1.58 us
    ppermute x2, waiting for transfers between devices, swap(): lax.ppermute(array, 'owner', [(at, lanes - 1 - at) for at in range(lanes)])  1.45 us
    pallas_call x1, Pallas kernels, first(): pl.pallas_call(first_kernel, out_shape=[shape(queries, width, dtype=bf16)...  1.14 us
  transfers between devices with their start and end apart: 9, of which 7 were waited for; matrix products, arithmetic and copies ran while one was open for 0% of the time, Pallas kernels for 9%

profile of v5, /device:TPU:0, one launch (start us, length us, event | category | flops | bytes accessed | tf_op | source)
XLA Modules:
  0.0 32.1 jit_solution(13704156798720330466)
XLA Ops:
  0.6 0.0 copy-start.1
  0.6 0.0 copy-start.2
  0.6 0.6 %copy-done.1 = s32[128,1]{0,1:T(1,128)S(1)} copy-done((s32[128,1]{0,1:T(1,128)S(1)}, s32[128,1]{0,1:T(1,128)}, u32[]{:S(2)}) %copy-start.1) | copy-done | bytes 536
  1.3 0.0 copy-done.2
  1.3 0.0 copy-start
  1.3 0.9 %copy-done = bf16[128,768]{1,0:T(8,128)(2,1)S(1)} copy-done((bf16[128,768]{1,0:T(8,128)(2,1)S(1)}, bf16[128,768]{1,0:T(8,128)(2,1)}, u32[]{:S(2)}) %copy-start) | copy-done | bytes 196632
  2.3 4.1 %collective-permute-start = (bf16[136,768]{1,0:T(8,128)(2,1)S(1)}, bf16[136,768]{1,0:T(8,128)(2,1)S(1)}, u32[]{:S(2)}, u32[]{:S(2)}) collective-permute-start(bf16[136,768]{1,0:T(8,128)(2,1)S(1)} %pack.1.own_ref), channel_id=1, source_target_pairs={{0,8},{2,10},{8,12},{10,14},{12,4},{14,6},{4,0},{6,2},{1,9},{3,11}... | collective-permute-start | bytes 626696 | tf_op jit(solution)/shard_map/ppermute | solution.py:161
  6.3 1.5 %collective-permute-start.1 = (bf16[136,768]{1,0:T(8,128)(2,1)S(1)}, bf16[136,768]{1,0:T(8,128)(2,1)S(1)}, u32[]{:S(2)}, u32[]{:S(2)}) collective-permute-start(bf16[136,768]{1,0:T(8,128)(2,1)S(1)} %pack.1.own_ref), channel_id=1, source_target_pairs={{0,2},{2,0},{4,6},{6,4},{8,10},{10,8},{12,14},{14,12},{1,3},{3,1},... | collective-permute-start | bytes 626696 | tf_op jit(solution)/shard_map/ppermute | solution.py:164
  7.8 0.0 collective-permute-start.2
  7.8 0.0 collective-permute-start.3
  7.8 4.1 %collective-permute-done.refs_0_ = bf16[136,768]{1,0:T(8,128)(2,1)S(1)} collective-permute-done((bf16[136,768]{1,0:T(8,128)(2,1)S(1)}, bf16[136,768]{1,0:T(8,128)(2,1)S(1)}, u32[]{:S(2)}, u32[]{:S(2)}) %collective-permute-start) | collective-permute-done | bytes 208928 | tf_op jit(solution)/shard_map/ppermute | solution.py:161
  11.9 1.1 %collective-permute-done.1.refs_0_ = bf16[136,768]{1,0:T(8,128)(2,1)S(1)} collective-permute-done((bf16[136,768]{1,0:T(8,128)(2,1)S(1)}, bf16[136,768]{1,0:T(8,128)(2,1)S(1)}, u32[]{:S(2)}, u32[]{:S(2)}) %collective-permute-start.1) | collective-permute-done | bytes 208928 | tf_op jit(solution)/shard_map/ppermute | solution.py:164
  13.0 0.0 collective-permute-done.2.other_ref
  13.0 2.3 %collective-permute-start.4 = (bf16[136,768]{1,0:T(8,128)(2,1)S(1)}, bf16[136,768]{1,0:T(8,128)(2,1)S(1)}, u32[]{:S(2)}, u32[]{:S(2)}) collective-permute-start(bf16[136,768]{1,0:T(8,128)(2,1)S(1)} %collective-permute-done.refs_0_), channel_id=1, source_target_pairs={{0,8},{2,10},{8,12},{10,14},{12,4},{14,6},{4,0},{6,2},{1,9},{3,11}... | collective-permute-start | bytes 626696 | tf_op jit(solution)/shard_map/ppermute | solution.py:161
  15.3 1.5 %collective-permute-start.5 = (bf16[136,768]{1,0:T(8,128)(2,1)S(1)}, bf16[136,768]{1,0:T(8,128)(2,1)S(1)}, u32[]{:S(2)}, u32[]{:S(2)}) collective-permute-start(bf16[136,768]{1,0:T(8,128)(2,1)S(1)} %collective-permute-done.refs_0_), channel_id=1, source_target_pairs={{0,2},{2,0},{4,6},{6,4},{8,10},{10,8},{12,14},{14,12},{1,3},{3,1},... | collective-permute-start | bytes 626696 | tf_op jit(solution)/shard_map/ppermute | solution.py:164
  16.8 0.0 collective-permute-start.6
  16.8 0.8 %collective-permute-done.3.refs_1_ = bf16[136,768]{1,0:T(8,128)(2,1)S(1)} collective-permute-done((bf16[136,768]{1,0:T(8,128)(2,1)S(1)}, bf16[136,768]{1,0:T(8,128)(2,1)S(1)}, u32[]{:S(2)}, u32[]{:S(2)}) %collective-permute-start.3) | collective-permute-done | bytes 208928 | tf_op jit(solution)/shard_map/ppermute | solution.py:161
  17.6 1.1 %first_scores.1 = (bf16[256,768]{1,0:T(8,128)(2,1)S(1)}, f32[256,128]{1,0:T(8,128)S(1)}, f32[256,128]{1,0:T(8,128)S(1)}, f32[256,768]{1,0:T(8,128)S(1)}) custom-call(bf16[136,768]{1,0:T(8,128)(2,1)S(1)} %pack.1.own_ref, bf16[136,768]{1,0:T(8,128)(2,1)S(1)} %collective-permute-done.2.other_ref, bf16[136,768]{1,0:T(8,128)(2,1)S(1)} %collective-permute-done.1.refs_0_, ...), custom_call_target="tpu_custom_call" | custom-call | flops 30198988800 | bytes 2162688 | tf_op jit(solution)/shard_map/first_scores/pallas_call | solution.py:170
  18.8 3.2 %collective-permute-done.4.refs_0_ = bf16[136,768]{1,0:T(8,128)(2,1)S(1)} collective-permute-done((bf16[136,768]{1,0:T(8,128)(2,1)S(1)}, bf16[136,768]{1,0:T(8,128)(2,1)S(1)}, u32[]{:S(2)}, u32[]{:S(2)}) %collective-permute-start.4) | collective-permute-done | bytes 208928 | tf_op jit(solution)/shard_map/ppermute | solution.py:161
  22.0 0.0 collective-permute-done.5.refs_1_
  22.0 2.1 %collective-permute-start.7 = (bf16[136,768]{1,0:T(8,128)(2,1)S(1)}, bf16[136,768]{1,0:T(8,128)(2,1)S(1)}, u32[]{:S(2)}, u32[]{:S(2)}) collective-permute-start(bf16[136,768]{1,0:T(8,128)(2,1)S(1)} %collective-permute-done.4.refs_0_), channel_id=1, source_target_pairs={{0,2},{2,0},{4,6},{6,4},{8,10},{10,8},{12,14},{14,12},{1,3},{3,1},... | collective-permute-start | bytes 626696 | tf_op jit(solution)/shard_map/ppermute | solution.py:164
  24.2 0.9 %more_scores.2 = (f32[256,128]{1,0:T(8,128)S(1)}, f32[256,768]{1,0:T(8,128)S(1)}) custom-call(bf16[256,768]{1,0:T(8,128)(2,1)S(1)} %get-tuple-element.22.unit_ref, f32[256,128]{1,0:T(8,128)S(1)} %get-tuple-element.23.side_ref, f32[256,128]{1,0:T(8,128)S(1)} %get-tuple-element.24.old_sums_ref, ...), custom_call_target="tpu_custom_call", output_to_operand_aliasing={{0}: (2, {}), {1}: (3, {})} | custom-call | flops 20132659200 | bytes 1966080 | tf_op jit(solution)/shard_map/more_scores/pallas_call | solution.py:184
  25.1 1.0 %collective-permute-done.6.refs_1_ = bf16[136,768]{1,0:T(8,128)(2,1)S(1)} collective-permute-done((bf16[136,768]{1,0:T(8,128)(2,1)S(1)}, bf16[136,768]{1,0:T(8,128)(2,1)S(1)}, u32[]{:S(2)}, u32[]{:S(2)}) %collective-permute-start.6) | collective-permute-done | bytes 208928 | tf_op jit(solution)/shard_map/ppermute | solution.py:161
  26.0 0.9 %more_scores.3 = (f32[256,128]{1,0:T(8,128)S(1)}, f32[256,768]{1,0:T(8,128)S(1)}) custom-call(bf16[256,768]{1,0:T(8,128)(2,1)S(1)} %get-tuple-element.22.unit_ref, f32[256,128]{1,0:T(8,128)S(1)} %get-tuple-element.23.side_ref, f32[256,128]{1,0:T(8,128)S(1)} %get-tuple-element.28.old_sums_ref, ...), custom_call_target="tpu_custom_call", output_to_operand_aliasing={{0}: (2, {}), {1}: (3, {})} | custom-call | flops 20132659200 | bytes 1966080 | tf_op jit(solution)/shard_map/more_scores/pallas_call | solution.py:184
  27.0 2.1 %collective-permute-done.7.refs_0_ = bf16[136,768]{1,0:T(8,128)(2,1)S(1)} collective-permute-done((bf16[136,768]{1,0:T(8,128)(2,1)S(1)}, bf16[136,768]{1,0:T(8,128)(2,1)S(1)}, u32[]{:S(2)}, u32[]{:S(2)}) %collective-permute-start.7) | collective-permute-done | bytes 208928 | tf_op jit(solution)/shard_map/ppermute | solution.py:164
  29.0 0.6 %final_scores.1 = (f32[128,128]{1,0:T(8,128)S(1)}, f32[128,768]{1,0:T(8,128)S(1)}, bf16[136,768]{1,0:T(8,128)(2,1)S(1)}) custom-call(bf16[256,768]{1,0:T(8,128)(2,1)S(1)} %get-tuple-element.22.unit_ref, f32[256,128]{1,0:T(8,128)S(1)} %get-tuple-element.23.side_ref, f32[256,128]{1,0:T(8,128)S(1)} %get-tuple-element.31.old_sums_ref, ...), custom_call_target="tpu_custom_call" | custom-call | flops 10066329600 | bytes 1769472 | tf_op jit(solution)/shard_map/final_scores/pallas_call | solution.py:194
  29.7 0.1 collective-permute-start.8
  29.7 1.4 %collective-permute-done.8.got_ref = bf16[136,768]{1,0:T(8,128)(2,1)S(1)} collective-permute-done((bf16[136,768]{1,0:T(8,128)(2,1)S(1)}, bf16[136,768]{1,0:T(8,128)(2,1)S(1)}, u32[]{:S(2)}, u32[]{:S(2)}) %collective-permute-start.8) | collective-permute-done | bytes 208928 | tf_op jit(solution)/shard_map/ppermute | solution.py:167
  31.2 1.0 %combine.1 = (f32[1,128]{1,0:T(1,128)}, f32[128,768]{1,0:T(8,128)}) custom-call(f32[128,128]{1,0:T(8,128)S(1)} %get-tuple-element.33.sums_ref, f32[128,768]{1,0:T(8,128)S(1)} %get-tuple-element.34.mixed_ref, bf16[136,768]{1,0:T(8,128)(2,1)S(1)} %collective-permute-done.8.got_ref), custom_call_target="tpu_custom_call" | custom-call | tf_op jit(solution)/shard_map/combine/pallas_call | solution.py:239
  (1 shorter events, 0.0 us)
Async XLA Ops:
  0.6 0.7 %copy-start.1 = (s32[128,1]{0,1:T(1,128)S(1)}, s32[128,1]{0,1:T(1,128)}, u32[]{:S(2)}) copy-start(s32[128,1]{0,1:T(1,128)} %param.4) | copy-start | bytes 1540
  0.6 0.7 %copy-start.2 = (s32[128]{0:T(128)S(1)}, s32[128]{0:T(128)}, u32[]{:S(2)}) copy-start(s32[128]{0:T(128)} %param.5) | copy-start | bytes 1540
  1.3 0.9 %copy-start = (bf16[128,768]{1,0:T(8,128)(2,1)S(1)}, bf16[128,768]{1,0:T(8,128)(2,1)}, u32[]{:S(2)}) copy-start(bf16[128,768]{1,0:T(8,128)(2,1)} %rows_ref.1) | copy-start | bytes 589828
  2.3 9.7 %collective-permute-start = (bf16[136,768]{1,0:T(8,128)(2,1)S(1)}, bf16[136,768]{1,0:T(8,128)(2,1)S(1)}, u32[]{:S(2)}, u32[]{:S(2)}) collective-permute-start(bf16[136,768]{1,0:T(8,128)(2,1)S(1)} %pack.1.own_ref), channel_id=1, source_target_pairs={{0,8},{2,10},{8,12},{10,14},{12,4},{14,6},{4,0},{6,2},{1,9},{3,11}... | collective-permute-start | bytes 626696 | tf_op jit(solution)/shard_map/ppermute | solution.py:161
  6.3 6.6 %collective-permute-start.1 = (bf16[136,768]{1,0:T(8,128)(2,1)S(1)}, bf16[136,768]{1,0:T(8,128)(2,1)S(1)}, u32[]{:S(2)}, u32[]{:S(2)}) collective-permute-start(bf16[136,768]{1,0:T(8,128)(2,1)S(1)} %pack.1.own_ref), channel_id=1, source_target_pairs={{0,2},{2,0},{4,6},{6,4},{8,10},{10,8},{12,14},{14,12},{1,3},{3,1},... | collective-permute-start | bytes 626696 | tf_op jit(solution)/shard_map/ppermute | solution.py:164
  7.8 5.1 %collective-permute-start.2 = (bf16[136,768]{1,0:T(8,128)(2,1)S(1)}, bf16[136,768]{1,0:T(8,128)(2,1)S(1)}, u32[]{:S(2)}, u32[]{:S(2)}) collective-permute-start(bf16[136,768]{1,0:T(8,128)(2,1)S(1)} %pack.1.own_ref), channel_id=1, source_target_pairs={{0,1},{1,0},{2,3},{3,2},{4,5},{5,4},{6,7},{7,6},{8,9},{9,8},{10,11... | collective-permute-start | bytes 626696 | tf_op jit(solution)/shard_map/ppermute | solution.py:167
  7.8 9.8 %collective-permute-start.3 = (bf16[136,768]{1,0:T(8,128)(2,1)S(1)}, bf16[136,768]{1,0:T(8,128)(2,1)S(1)}, u32[]{:S(2)}, u32[]{:S(2)}) collective-permute-start(bf16[136,768]{1,0:T(8,128)(2,1)S(1)} %pack.1.own_ref), channel_id=1, source_target_pairs={{0,4},{2,6},{8,0},{10,2},{12,8},{14,10},{4,12},{6,14},{1,5},{3,7},... | collective-permute-start | bytes 626696 | tf_op jit(solution)/shard_map/ppermute | solution.py:161
  13.0 9.1 %collective-permute-start.4 = (bf16[136,768]{1,0:T(8,128)(2,1)S(1)}, bf16[136,768]{1,0:T(8,128)(2,1)S(1)}, u32[]{:S(2)}, u32[]{:S(2)}) collective-permute-start(bf16[136,768]{1,0:T(8,128)(2,1)S(1)} %collective-permute-done.refs_0_), channel_id=1, source_target_pairs={{0,8},{2,10},{8,12},{10,14},{12,4},{14,6},{4,0},{6,2},{1,9},{3,11}... | collective-permute-start | bytes 626696 | tf_op jit(solution)/shard_map/ppermute | solution.py:161
  15.3 6.7 %collective-permute-start.5 = (bf16[136,768]{1,0:T(8,128)(2,1)S(1)}, bf16[136,768]{1,0:T(8,128)(2,1)S(1)}, u32[]{:S(2)}, u32[]{:S(2)}) collective-permute-start(bf16[136,768]{1,0:T(8,128)(2,1)S(1)} %collective-permute-done.refs_0_), channel_id=1, source_target_pairs={{0,2},{2,0},{4,6},{6,4},{8,10},{10,8},{12,14},{14,12},{1,3},{3,1},... | collective-permute-start | bytes 626696 | tf_op jit(solution)/shard_map/ppermute | solution.py:164
  16.8 9.2 %collective-permute-start.6 = (bf16[136,768]{1,0:T(8,128)(2,1)S(1)}, bf16[136,768]{1,0:T(8,128)(2,1)S(1)}, u32[]{:S(2)}, u32[]{:S(2)}) collective-permute-start(bf16[136,768]{1,0:T(8,128)(2,1)S(1)} %collective-permute-done.1.refs_0_), channel_id=1, source_target_pairs={{0,4},{2,6},{8,0},{10,2},{12,8},{14,10},{4,12},{6,14},{1,5},{3,7},... | collective-permute-start | bytes 626696 | tf_op jit(solution)/shard_map/ppermute | solution.py:161
  22.0 7.0 %collective-permute-start.7 = (bf16[136,768]{1,0:T(8,128)(2,1)S(1)}, bf16[136,768]{1,0:T(8,128)(2,1)S(1)}, u32[]{:S(2)}, u32[]{:S(2)}) collective-permute-start(bf16[136,768]{1,0:T(8,128)(2,1)S(1)} %collective-permute-done.4.refs_0_), channel_id=1, source_target_pairs={{0,2},{2,0},{4,6},{6,4},{8,10},{10,8},{12,14},{14,12},{1,3},{3,1},... | collective-permute-start | bytes 626696 | tf_op jit(solution)/shard_map/ppermute | solution.py:164
  29.7 1.5 %collective-permute-start.8 = (bf16[136,768]{1,0:T(8,128)(2,1)S(1)}, bf16[136,768]{1,0:T(8,128)(2,1)S(1)}, u32[]{:S(2)}, u32[]{:S(2)}) collective-permute-start(bf16[136,768]{1,0:T(8,128)(2,1)S(1)} %get-tuple-element.35), channel_id=1, source_target_pairs={{0,1},{1,0},{2,3},{3,2},{4,5},{5,4},{6,7},{7,6},{8,9},{9,8},{10,11... | collective-permute-start | bytes 626696 | tf_op jit(solution)/shard_map/ppermute | solution.py:167

commit v6 on v5

--- a/solution.py
+++ b/solution.py
@@ -163,6 +163,16 @@
     def across(array):
         return lax.ppermute(array, "shard", [(at, at ^ 1) for at in range(shards)])
 
+    def corner(beside, ahead):
+        pairs = []
+        for at in range(rounds):
+            for side in range(2):
+                here = 2 * ring[at] + side
+                pairs.append((here * lanes, (2 * ring[at - 1] + side) * lanes))
+                pairs += [(here * lanes + lane, (here ^ 1) * lanes + lane) for lane in range(1, lanes)]
+        source = jnp.where(lax.axis_index("owner") == 0, beside, ahead)
+        return lax.ppermute(source, ("shard", "owner"), pairs)
+
     def swap(array):
         return lax.ppermute(array, "owner", [(at, lanes - 1 - at) for at in range(lanes)])
 
@@ -214,13 +224,13 @@
     other = swap(own)
     if rounds == 4:
         ahead = along(own, -1)
-        moved, beside, other = lax.optimization_barrier((moved, beside, other))
+        other, beside, moved = lax.optimization_barrier((other, beside, moved))
         opposite = along(moved, 1)
         moved_beside = across(moved)
-        ahead_beside = along(beside, -1)
+        ahead_beside = corner(beside, ahead)
         state = first(own, other, beside, ahead)
         unit, side = state[:2]
-        opposite, moved_beside = lax.optimization_barrier((opposite, moved_beside))
+        moved_beside, opposite = lax.optimization_barrier((moved_beside, opposite))
         last = [across(opposite)]
         sums, mixed = more(*state, moved, moved_beside)
         sums, mixed = more(unit, side, sums, mixed, opposite, ahead_beside)

time: 32.3 us -> 31.9 us (0.988)
  waiting for transfers between devices: 13.7 us -> 12.6 us
  starting transfers between devices: 11.6 us -> 12.3 us
    ppermute x4 -> x3, waiting for transfers between devices: 9.1 us -> 6.33 us  [along(): return lax.ppermute(array, 'shard', pairs)]
    ppermute x0 -> x1, starting transfers between devices: none -> 1.27 us  [corner(): return lax.ppermute(source, ('shard', 'owner'), pairs)]
    ppermute x3, waiting for transfers between devices: 3.13 us -> 4.33 us  [across(): return lax.ppermute(array, 'shard', [(at, at ^ 1) for at in range(shards)])]
    ppermute x3, starting transfers between devices: 5.14 us -> 4.5 us  [across(): return lax.ppermute(array, 'shard', [(at, at ^ 1) for at in range(shards)])]
    ppermute x0 -> x1, waiting for transfers between devices: none -> 0.5 us  [corner(): return lax.ppermute(source, ('shard', 'owner'), pairs)]
    ppermute x4 -> x3, starting transfers between devices: 6.42 us -> 6.42 us  [along(): return lax.ppermute(array, 'shard', pairs)]
where the time goes in v6:
time: 31.9 us; the launch traced here: 31.7 us
  waiting for transfers between devices  12.6 us (39%)
  starting transfers between devices  12.3 us (39%)
  Pallas kernels  4.56 us (14%)
  local copies, waits for them, and re-layouts  1.58 us (5%)
  between operations  0.7 us (2%)
    ppermute x3, starting transfers between devices, along(): return lax.ppermute(array, 'shard', pairs)  6.42 us
    ppermute x3, waiting for transfers between devices, along(): return lax.ppermute(array, 'shard', pairs)  6.33 us
    ppermute x3, starting transfers between devices, across(): return lax.ppermute(array, 'shard', [(at, at ^ 1) for at in range(shards)])  4.5 us
    ppermute x3, waiting for transfers between devices, across(): return lax.ppermute(array, 'shard', [(at, at ^ 1) for at in range(shards)])  4.33 us
    pallas_call x2, Pallas kernels, more(): pl.pallas_call(more_kernel, out_shape=[shape(queries, 128), shape(queries...  1.81 us
    unnamed x6, local copies, waits for them, and re-layouts  1.58 us
    ppermute x2, waiting for transfers between devices, swap(): lax.ppermute(array, 'owner', [(at, lanes - 1 - at) for at in range(lanes)])  1.45 us
    ppermute x1, starting transfers between devices, corner(): return lax.ppermute(source, ('shard', 'owner'), pairs)  1.27 us
  transfers between devices with their start and end apart: 9, of which 7 were waited for; matrix products, arithmetic and copies ran while one was open for 0% of the time, Pallas kernels for 9%

profile of v6, /device:TPU:0, one launch (start us, length us, event | category | flops | bytes accessed | tf_op | source)
XLA Modules:
  0.0 31.7 jit_solution(8825826955170696614)
XLA Ops:
  0.6 0.0 copy-start.1
  0.6 0.0 copy-start.2
  0.6 0.6 %copy-done.1 = s32[128,1]{0,1:T(1,128)S(1)} copy-done((s32[128,1]{0,1:T(1,128)S(1)}, s32[128,1]{0,1:T(1,128)}, u32[]{:S(2)}) %copy-start.1) | copy-done | bytes 536
  1.3 0.0 copy-done.2
  1.3 0.0 copy-start
  1.3 0.9 %copy-done = bf16[128,768]{1,0:T(8,128)(2,1)S(1)} copy-done((bf16[128,768]{1,0:T(8,128)(2,1)S(1)}, bf16[128,768]{1,0:T(8,128)(2,1)}, u32[]{:S(2)}) %copy-start) | copy-done | bytes 196632
  2.3 4.1 %collective-permute-start.2 = (bf16[136,768]{1,0:T(8,128)(2,1)S(1)}, bf16[136,768]{1,0:T(8,128)(2,1)S(1)}, u32[]{:S(2)}, u32[]{:S(2)}) collective-permute-start(bf16[136,768]{1,0:T(8,128)(2,1)S(1)} %pack.1.own_ref), channel_id=1, source_target_pairs={{0,8},{2,10},{8,12},{10,14},{12,4},{14,6},{4,0},{6,2},{1,9},{3,11}... | collective-permute-start | bytes 626696 | tf_op jit(solution)/shard_map/ppermute | solution.py:161
  6.3 1.5 %collective-permute-start.1 = (bf16[136,768]{1,0:T(8,128)(2,1)S(1)}, bf16[136,768]{1,0:T(8,128)(2,1)S(1)}, u32[]{:S(2)}, u32[]{:S(2)}) collective-permute-start(bf16[136,768]{1,0:T(8,128)(2,1)S(1)} %pack.1.own_ref), channel_id=1, source_target_pairs={{0,2},{2,0},{4,6},{6,4},{8,10},{10,8},{12,14},{14,12},{1,3},{3,1},... | collective-permute-start | bytes 626696 | tf_op jit(solution)/shard_map/ppermute | solution.py:164
  7.8 0.0 collective-permute-start
  7.8 0.0 collective-permute-start.3
  7.8 4.1 %collective-permute-done.2.refs_0_ = bf16[136,768]{1,0:T(8,128)(2,1)S(1)} collective-permute-done((bf16[136,768]{1,0:T(8,128)(2,1)S(1)}, bf16[136,768]{1,0:T(8,128)(2,1)S(1)}, u32[]{:S(2)}, u32[]{:S(2)}) %collective-permute-start.2) | collective-permute-done | bytes 208928 | tf_op jit(solution)/shard_map/ppermute | solution.py:161
  11.9 1.1 %collective-permute-done.1.refs_0_ = bf16[136,768]{1,0:T(8,128)(2,1)S(1)} collective-permute-done((bf16[136,768]{1,0:T(8,128)(2,1)S(1)}, bf16[136,768]{1,0:T(8,128)(2,1)S(1)}, u32[]{:S(2)}, u32[]{:S(2)}) %collective-permute-start.1) | collective-permute-done | bytes 208928 | tf_op jit(solution)/shard_map/ppermute | solution.py:164
  13.0 0.0 collective-permute-done.other_ref
  13.0 2.3 %collective-permute-start.5 = (bf16[136,768]{1,0:T(8,128)(2,1)S(1)}, bf16[136,768]{1,0:T(8,128)(2,1)S(1)}, u32[]{:S(2)}, u32[]{:S(2)}) collective-permute-start(bf16[136,768]{1,0:T(8,128)(2,1)S(1)} %collective-permute-done.2.refs_0_), channel_id=1, source_target_pairs={{0,8},{2,10},{8,12},{10,14},{12,4},{14,6},{4,0},{6,2},{1,9},{3,11}... | collective-permute-start | bytes 626696 | tf_op jit(solution)/shard_map/ppermute | solution.py:161
  15.3 1.5 %collective-permute-start.4 = (bf16[136,768]{1,0:T(8,128)(2,1)S(1)}, bf16[136,768]{1,0:T(8,128)(2,1)S(1)}, u32[]{:S(2)}, u32[]{:S(2)}) collective-permute-start(bf16[136,768]{1,0:T(8,128)(2,1)S(1)} %collective-permute-done.2.refs_0_), channel_id=1, source_target_pairs={{0,2},{2,0},{4,6},{6,4},{8,10},{10,8},{12,14},{14,12},{1,3},{3,1},... | collective-permute-start | bytes 626696 | tf_op jit(solution)/shard_map/ppermute | solution.py:164
  16.8 0.8 %collective-permute-done.3.refs_1_ = bf16[136,768]{1,0:T(8,128)(2,1)S(1)} collective-permute-done((bf16[136,768]{1,0:T(8,128)(2,1)S(1)}, bf16[136,768]{1,0:T(8,128)(2,1)S(1)}, u32[]{:S(2)}, u32[]{:S(2)}) %collective-permute-start.3) | collective-permute-done | bytes 208928 | tf_op jit(solution)/shard_map/ppermute | solution.py:161
  17.7 1.3 %collective-permute-start.6 = (bf16[136,768]{1,0:T(8,128)(2,1)S(1)}, bf16[136,768]{1,0:T(8,128)(2,1)S(1)}, u32[]{:S(2)}, u32[]{:S(2)}) collective-permute-start(bf16[136,768]{1,0:T(8,128)(2,1)S(1)} %broadcast_select_fusion), channel_id=1, source_target_pairs={{0,4},{1,3},{2,6},{3,1},{8,0},{9,11},{10,2},{11,9},{12,8},{13,15},... | collective-permute-start | bytes 626696 | tf_op jit(solution)/shard_map/ppermute | solution.py:174
  18.9 1.1 %first_scores.1 = (bf16[256,768]{1,0:T(8,128)(2,1)S(1)}, f32[256,128]{1,0:T(8,128)S(1)}, f32[256,128]{1,0:T(8,128)S(1)}, f32[256,768]{1,0:T(8,128)S(1)}) custom-call(bf16[136,768]{1,0:T(8,128)(2,1)S(1)} %pack.1.own_ref, bf16[136,768]{1,0:T(8,128)(2,1)S(1)} %collective-permute-done.other_ref, bf16[136,768]{1,0:T(8,128)(2,1)S(1)} %collective-permute-done.1.refs_0_, ...), custom_call_target="tpu_custom_call" | custom-call | flops 30198988800 | bytes 2162688 | tf_op jit(solution)/shard_map/first_scores/pallas_call | solution.py:180
  20.1 1.4 %collective-permute-done.5.refs_0_ = bf16[136,768]{1,0:T(8,128)(2,1)S(1)} collective-permute-done((bf16[136,768]{1,0:T(8,128)(2,1)S(1)}, bf16[136,768]{1,0:T(8,128)(2,1)S(1)}, u32[]{:S(2)}, u32[]{:S(2)}) %collective-permute-start.5) | collective-permute-done | bytes 208928 | tf_op jit(solution)/shard_map/ppermute | solution.py:161
  21.5 0.0 collective-permute-done.4.refs_1_
  21.5 1.5 %collective-permute-start.7 = (bf16[136,768]{1,0:T(8,128)(2,1)S(1)}, bf16[136,768]{1,0:T(8,128)(2,1)S(1)}, u32[]{:S(2)}, u32[]{:S(2)}) collective-permute-start(bf16[136,768]{1,0:T(8,128)(2,1)S(1)} %collective-permute-done.5.refs_0_), channel_id=1, source_target_pairs={{0,2},{2,0},{4,6},{6,4},{8,10},{10,8},{12,14},{14,12},{1,3},{3,1},... | collective-permute-start | bytes 626696 | tf_op jit(solution)/shard_map/ppermute | solution.py:164
  23.0 0.9 %more_scores.2 = (f32[256,128]{1,0:T(8,128)S(1)}, f32[256,768]{1,0:T(8,128)S(1)}) custom-call(bf16[256,768]{1,0:T(8,128)(2,1)S(1)} %get-tuple-element.22.unit_ref, f32[256,128]{1,0:T(8,128)S(1)} %get-tuple-element.23.side_ref, f32[256,128]{1,0:T(8,128)S(1)} %get-tuple-element.24.old_sums_ref, ...), custom_call_target="tpu_custom_call", output_to_operand_aliasing={{0}: (2, {}), {1}: (3, {})} | custom-call | flops 20132659200 | bytes 1966080 | tf_op jit(solution)/shard_map/more_scores/pallas_call | solution.py:194
  23.9 0.5 %collective-permute-done.6.refs_1_ = bf16[136,768]{1,0:T(8,128)(2,1)S(1)} collective-permute-done((bf16[136,768]{1,0:T(8,128)(2,1)S(1)}, bf16[136,768]{1,0:T(8,128)(2,1)S(1)}, u32[]{:S(2)}, u32[]{:S(2)}) %collective-permute-start.6) | collective-permute-done | bytes 208928 | tf_op jit(solution)/shard_map/ppermute | solution.py:174
  24.4 0.9 %more_scores.3 = (f32[256,128]{1,0:T(8,128)S(1)}, f32[256,768]{1,0:T(8,128)S(1)}) custom-call(bf16[256,768]{1,0:T(8,128)(2,1)S(1)} %get-tuple-element.22.unit_ref, f32[256,128]{1,0:T(8,128)S(1)} %get-tuple-element.23.side_ref, f32[256,128]{1,0:T(8,128)S(1)} %get-tuple-element.28.old_sums_ref, ...), custom_call_target="tpu_custom_call", output_to_operand_aliasing={{0}: (2, {}), {1}: (3, {})} | custom-call | flops 20132659200 | bytes 1966080 | tf_op jit(solution)/shard_map/more_scores/pallas_call | solution.py:194
  25.3 3.3 %collective-permute-done.7.refs_0_ = bf16[136,768]{1,0:T(8,128)(2,1)S(1)} collective-permute-done((bf16[136,768]{1,0:T(8,128)(2,1)S(1)}, bf16[136,768]{1,0:T(8,128)(2,1)S(1)}, u32[]{:S(2)}, u32[]{:S(2)}) %collective-permute-start.7) | collective-permute-done | bytes 208928 | tf_op jit(solution)/shard_map/ppermute | solution.py:164
  28.6 0.6 %final_scores.1 = (f32[128,128]{1,0:T(8,128)S(1)}, f32[128,768]{1,0:T(8,128)S(1)}, bf16[136,768]{1,0:T(8,128)(2,1)S(1)}) custom-call(bf16[256,768]{1,0:T(8,128)(2,1)S(1)} %get-tuple-element.22.unit_ref, f32[256,128]{1,0:T(8,128)S(1)} %get-tuple-element.23.side_ref, f32[256,128]{1,0:T(8,128)S(1)} %get-tuple-element.31.old_sums_ref, ...), custom_call_target="tpu_custom_call" | custom-call | flops 10066329600 | bytes 1769472 | tf_op jit(solution)/shard_map/final_scores/pallas_call | solution.py:204
  29.2 0.1 collective-permute-start.8
  29.3 1.4 %collective-permute-done.8.got_ref = bf16[136,768]{1,0:T(8,128)(2,1)S(1)} collective-permute-done((bf16[136,768]{1,0:T(8,128)(2,1)S(1)}, bf16[136,768]{1,0:T(8,128)(2,1)S(1)}, u32[]{:S(2)}, u32[]{:S(2)}) %collective-permute-start.8) | collective-permute-done | bytes 208928 | tf_op jit(solution)/shard_map/ppermute | solution.py:177
  30.8 1.0 %combine.1 = (f32[1,128]{1,0:T(1,128)}, f32[128,768]{1,0:T(8,128)}) custom-call(f32[128,128]{1,0:T(8,128)S(1)} %get-tuple-element.33.sums_ref, f32[128,768]{1,0:T(8,128)S(1)} %get-tuple-element.34.mixed_ref, bf16[136,768]{1,0:T(8,128)(2,1)S(1)} %collective-permute-done.8.got_ref), custom_call_target="tpu_custom_call" | custom-call | tf_op jit(solution)/shard_map/combine/pallas_call | solution.py:249
  (2 shorter events, 0.0 us)
Async XLA Ops:
  0.6 0.7 %copy-start.1 = (s32[128,1]{0,1:T(1,128)S(1)}, s32[128,1]{0,1:T(1,128)}, u32[]{:S(2)}) copy-start(s32[128,1]{0,1:T(1,128)} %param.4) | copy-start | bytes 1540
  0.6 0.7 %copy-start.2 = (s32[128]{0:T(128)S(1)}, s32[128]{0:T(128)}, u32[]{:S(2)}) copy-start(s32[128]{0:T(128)} %param.5) | copy-start | bytes 1540
  1.3 0.9 %copy-start = (bf16[128,768]{1,0:T(8,128)(2,1)S(1)}, bf16[128,768]{1,0:T(8,128)(2,1)}, u32[]{:S(2)}) copy-start(bf16[128,768]{1,0:T(8,128)(2,1)} %rows_ref.1) | copy-start | bytes 589828
  2.3 9.7 %collective-permute-start.2 = (bf16[136,768]{1,0:T(8,128)(2,1)S(1)}, bf16[136,768]{1,0:T(8,128)(2,1)S(1)}, u32[]{:S(2)}, u32[]{:S(2)}) collective-permute-start(bf16[136,768]{1,0:T(8,128)(2,1)S(1)} %pack.1.own_ref), channel_id=1, source_target_pairs={{0,8},{2,10},{8,12},{10,14},{12,4},{14,6},{4,0},{6,2},{1,9},{3,11}... | collective-permute-start | bytes 626696 | tf_op jit(solution)/shard_map/ppermute | solution.py:161
  6.3 6.6 %collective-permute-start.1 = (bf16[136,768]{1,0:T(8,128)(2,1)S(1)}, bf16[136,768]{1,0:T(8,128)(2,1)S(1)}, u32[]{:S(2)}, u32[]{:S(2)}) collective-permute-start(bf16[136,768]{1,0:T(8,128)(2,1)S(1)} %pack.1.own_ref), channel_id=1, source_target_pairs={{0,2},{2,0},{4,6},{6,4},{8,10},{10,8},{12,14},{14,12},{1,3},{3,1},... | collective-permute-start | bytes 626696 | tf_op jit(solution)/shard_map/ppermute | solution.py:164
  7.8 5.1 %collective-permute-start = (bf16[136,768]{1,0:T(8,128)(2,1)S(1)}, bf16[136,768]{1,0:T(8,128)(2,1)S(1)}, u32[]{:S(2)}, u32[]{:S(2)}) collective-permute-start(bf16[136,768]{1,0:T(8,128)(2,1)S(1)} %pack.1.own_ref), channel_id=1, source_target_pairs={{0,1},{1,0},{2,3},{3,2},{4,5},{5,4},{6,7},{7,6},{8,9},{9,8},{10,11... | collective-permute-start | bytes 626696 | tf_op jit(solution)/shard_map/ppermute | solution.py:177
  7.8 9.8 %collective-permute-start.3 = (bf16[136,768]{1,0:T(8,128)(2,1)S(1)}, bf16[136,768]{1,0:T(8,128)(2,1)S(1)}, u32[]{:S(2)}, u32[]{:S(2)}) collective-permute-start(bf16[136,768]{1,0:T(8,128)(2,1)S(1)} %pack.1.own_ref), channel_id=1, source_target_pairs={{0,4},{2,6},{8,0},{10,2},{12,8},{14,10},{4,12},{6,14},{1,5},{3,7},... | collective-permute-start | bytes 626696 | tf_op jit(solution)/shard_map/ppermute | solution.py:161
  13.0 8.6 %collective-permute-start.5 = (bf16[136,768]{1,0:T(8,128)(2,1)S(1)}, bf16[136,768]{1,0:T(8,128)(2,1)S(1)}, u32[]{:S(2)}, u32[]{:S(2)}) collective-permute-start(bf16[136,768]{1,0:T(8,128)(2,1)S(1)} %collective-permute-done.2.refs_0_), channel_id=1, source_target_pairs={{0,8},{2,10},{8,12},{10,14},{12,4},{14,6},{4,0},{6,2},{1,9},{3,11}... | collective-permute-start | bytes 626696 | tf_op jit(solution)/shard_map/ppermute | solution.py:161
  15.3 6.2 %collective-permute-start.4 = (bf16[136,768]{1,0:T(8,128)(2,1)S(1)}, bf16[136,768]{1,0:T(8,128)(2,1)S(1)}, u32[]{:S(2)}, u32[]{:S(2)}) collective-permute-start(bf16[136,768]{1,0:T(8,128)(2,1)S(1)} %collective-permute-done.2.refs_0_), channel_id=1, source_target_pairs={{0,2},{2,0},{4,6},{6,4},{8,10},{10,8},{12,14},{14,12},{1,3},{3,1},... | collective-permute-start | bytes 626696 | tf_op jit(solution)/shard_map/ppermute | solution.py:164
  17.7 6.8 %collective-permute-start.6 = (bf16[136,768]{1,0:T(8,128)(2,1)S(1)}, bf16[136,768]{1,0:T(8,128)(2,1)S(1)}, u32[]{:S(2)}, u32[]{:S(2)}) collective-permute-start(bf16[136,768]{1,0:T(8,128)(2,1)S(1)} %broadcast_select_fusion), channel_id=1, source_target_pairs={{0,4},{1,3},{2,6},{3,1},{8,0},{9,11},{10,2},{11,9},{12,8},{13,15},... | collective-permute-start | bytes 626696 | tf_op jit(solution)/shard_map/ppermute | solution.py:174
  21.5 7.1 %collective-permute-start.7 = (bf16[136,768]{1,0:T(8,128)(2,1)S(1)}, bf16[136,768]{1,0:T(8,128)(2,1)S(1)}, u32[]{:S(2)}, u32[]{:S(2)}) collective-permute-start(bf16[136,768]{1,0:T(8,128)(2,1)S(1)} %collective-permute-done.5.refs_0_), channel_id=1, source_target_pairs={{0,2},{2,0},{4,6},{6,4},{8,10},{10,8},{12,14},{14,12},{1,3},{3,1},... | collective-permute-start | bytes 626696 | tf_op jit(solution)/shard_map/ppermute | solution.py:164
  29.2 1.5 %collective-permute-start.8 = (bf16[136,768]{1,0:T(8,128)(2,1)S(1)}, bf16[136,768]{1,0:T(8,128)(2,1)S(1)}, u32[]{:S(2)}, u32[]{:S(2)}) collective-permute-start(bf16[136,768]{1,0:T(8,128)(2,1)S(1)} %get-tuple-element.35), channel_id=1, source_target_pairs={{0,1},{1,0},{2,3},{3,2},{4,5},{5,4},{6,7},{7,6},{8,9},{9,8},{10,11... | collective-permute-start | bytes 626696 | tf_op jit(solution)/shard_map/ppermute | solution.py:177

commit v7 on v5

--- a/solution.py
+++ b/solution.py
@@ -210,38 +210,34 @@
         name="pack",
     )(embeddings, cluster_id.reshape(1, count), priority.reshape(1, count))
 
-    moved, beside = along(own, 1), across(own)
-    other = swap(own)
+    moved, other, guest = along(own, 1), swap(own), across(own)
     if rounds == 4:
         ahead = along(own, -1)
-        moved, beside, other = lax.optimization_barrier((moved, beside, other))
-        opposite = along(moved, 1)
-        moved_beside = across(moved)
-        ahead_beside = along(beside, -1)
-        state = first(own, other, beside, ahead)
-        unit, side = state[:2]
-        opposite, moved_beside = lax.optimization_barrier((opposite, moved_beside))
-        last = [across(opposite)]
-        sums, mixed = more(*state, moved, moved_beside)
-        sums, mixed = more(unit, side, sums, mixed, opposite, ahead_beside)
+        other, guest, moved = lax.optimization_barrier((other, guest, moved))
+        last = along(moved, 1)
+        far = swap(moved)
+        unit, side, sums, mixed = first(own, guest, other, moved)
+        sums, far, last = lax.optimization_barrier((sums, far, last))
+        blocks = [far, ahead, swap(ahead), last]
     else:
-        unit, side, sums, mixed = first(own, other, beside)
+        unit, side, sums, mixed = first(own, guest, other)
 
         def turn(at, state):
             moved, sums, mixed = state
-            ahead, beside = along(moved, 1), across(moved)
-            sums, mixed = more(unit, side, sums, mixed, moved, beside)
+            ahead = along(moved, 1)
+            sums, mixed = more(unit, side, sums, mixed, moved, swap(moved))
             return ahead, sums, mixed
 
-        moved, sums, mixed = lax.fori_loop(1, rounds - 1, turn, (moved, sums, mixed))
-        last = [moved, across(moved)]
-    keep_sums, keep, send = final(unit, side, sums, mixed, *last)
+        last, sums, mixed = lax.fori_loop(1, rounds - 1, turn, (moved, sums, mixed))
+        blocks = [last]
+    sums, mixed = more(unit, side, sums, mixed, *blocks)
+    keep_sums, keep, send = final(unit, side, sums, mixed, swap(last))
     dup, out = pl.pallas_call(
         combine_kernel,
         out_shape=[shape(1, count), shape(count, width)],
         compiler_params=params,
         name="combine",
-    )(keep_sums, keep, swap(send))
+    )(keep_sums, keep, across(send))
     return dup[0], out
 
 

time: 32.3 us -> 32 us (level)
  waiting for transfers between devices: 13.7 us -> 16.3 us
  starting transfers between devices: 11.6 us -> 9.5 us
  Pallas kernels: 4.55 us -> 3.8 us
    ppermute x3 -> x2, waiting for transfers between devices: 3.13 us -> 6.77 us  [across(): return lax.ppermute(array, 'shard', [(at, at ^ 1) for at in range(shards)])]
    ppermute x3 -> x2, starting transfers between devices: 5.14 us -> 3.05 us  [across(): return lax.ppermute(array, 'shard', [(at, at ^ 1) for at in range(shards)])]
    ppermute x2 -> x4, waiting for transfers between devices: 1.45 us -> 0.38 us  [swap(): lax.ppermute(array, 'owner', [(at, lanes - 1 - at) for at in range(lanes)])]
    pallas_call x2 -> x1, Pallas kernels: 1.81 us -> 1.06 us  [more(): pl.pallas_call(more_kernel, out_shape=[shape(queries, 128), shape(queries...]
    ppermute x4 -> x3, waiting for transfers between devices: 9.1 us -> 9.14 us  [along(): return lax.ppermute(array, 'shard', pairs)]
    ppermute x4 -> x3, starting transfers between devices: 6.42 us -> 6.42 us  [along(): return lax.ppermute(array, 'shard', pairs)]
  transfers between devices with their start and end apart: 9 -> 9, of which waited for: 7 -> 6; matrix products, arithmetic and copies ran while one was open for 0% -> 0% of each run, Pallas kernels for 9% -> 7%
where the time goes in v7:
time: 32 us; the launch traced here: 31.8 us
  waiting for transfers between devices  16.3 us (51%)
  starting transfers between devices  9.5 us (30%)
  Pallas kernels  3.8 us (12%)
  local copies, waits for them, and re-layouts  1.58 us (5%)
  between operations  0.68 us (2%)
    ppermute x3, waiting for transfers between devices, along(): return lax.ppermute(array, 'shard', pairs)  9.14 us
    ppermute x2, waiting for transfers between devices, across(): return lax.ppermute(array, 'shard', [(at, at ^ 1) for at in range(shards)])  6.77 us
    ppermute x3, starting transfers between devices, along(): return lax.ppermute(array, 'shard', pairs)  6.42 us
    ppermute x2, starting transfers between devices, across(): return lax.ppermute(array, 'shard', [(at, at ^ 1) for at in range(shards)])  3.05 us
    unnamed x6, local copies, waits for them, and re-layouts  1.58 us
    pallas_call x1, Pallas kernels, first(): pl.pallas_call(first_kernel, out_shape=[shape(queries, width, dtype=bf16)...  1.14 us
    pallas_call x1, Pallas kernels, more(): pl.pallas_call(more_kernel, out_shape=[shape(queries, 128), shape(queries...  1.06 us
    pallas_call x1, Pallas kernels, local(): pl.pallas_call(combine_kernel, out_shape=[shape(1, count), shape(count, w...  0.95 us
  transfers between devices with their start and end apart: 9, of which 6 were waited for; matrix products, arithmetic and copies ran while one was open for 0% of the time, Pallas kernels for 7%

profile of v7, /device:TPU:0, one launch (start us, length us, event | category | flops | bytes accessed | tf_op | source)
XLA Modules:
  0.0 31.8 jit_solution(2806334639363723798)
XLA Ops:
  0.6 0.0 copy-start.1
  0.6 0.0 copy-start.2
  0.6 0.6 %copy-done.1 = s32[128,1]{0,1:T(1,128)S(1)} copy-done((s32[128,1]{0,1:T(1,128)S(1)}, s32[128,1]{0,1:T(1,128)}, u32[]{:S(2)}) %copy-start.1) | copy-done | bytes 536
  1.3 0.0 copy-done.2
  1.3 0.0 copy-start
  1.3 0.9 %copy-done = bf16[128,768]{1,0:T(8,128)(2,1)S(1)} copy-done((bf16[128,768]{1,0:T(8,128)(2,1)S(1)}, bf16[128,768]{1,0:T(8,128)(2,1)}, u32[]{:S(2)}) %copy-start) | copy-done | bytes 196632
  2.3 4.1 %collective-permute-start.2 = (bf16[136,768]{1,0:T(8,128)(2,1)S(1)}, bf16[136,768]{1,0:T(8,128)(2,1)S(1)}, u32[]{:S(2)}, u32[]{:S(2)}) collective-permute-start(bf16[136,768]{1,0:T(8,128)(2,1)S(1)} %pack.1.own_ref), channel_id=1, source_target_pairs={{0,8},{2,10},{8,12},{10,14},{12,4},{14,6},{4,0},{6,2},{1,9},{3,11}... | collective-permute-start | bytes 626696 | tf_op jit(solution)/shard_map/ppermute | solution.py:161
  6.3 1.5 %collective-permute-start.1 = (bf16[136,768]{1,0:T(8,128)(2,1)S(1)}, bf16[136,768]{1,0:T(8,128)(2,1)S(1)}, u32[]{:S(2)}, u32[]{:S(2)}) collective-permute-start(bf16[136,768]{1,0:T(8,128)(2,1)S(1)} %pack.1.own_ref), channel_id=1, source_target_pairs={{0,2},{2,0},{4,6},{6,4},{8,10},{10,8},{12,14},{14,12},{1,3},{3,1},... | collective-permute-start | bytes 626696 | tf_op jit(solution)/shard_map/ppermute | solution.py:164
  7.8 0.0 collective-permute-start
  7.8 0.0 collective-permute-start.5
  7.8 4.1 %collective-permute-done.2.refs_1_ = bf16[136,768]{1,0:T(8,128)(2,1)S(1)} collective-permute-done((bf16[136,768]{1,0:T(8,128)(2,1)S(1)}, bf16[136,768]{1,0:T(8,128)(2,1)S(1)}, u32[]{:S(2)}, u32[]{:S(2)}) %collective-permute-start.2) | collective-permute-done | bytes 208928 | tf_op jit(solution)/shard_map/ppermute | solution.py:161
  11.9 1.1 %collective-permute-done.1.other_ref = bf16[136,768]{1,0:T(8,128)(2,1)S(1)} collective-permute-done((bf16[136,768]{1,0:T(8,128)(2,1)S(1)}, bf16[136,768]{1,0:T(8,128)(2,1)S(1)}, u32[]{:S(2)}, u32[]{:S(2)}) %collective-permute-start.1) | collective-permute-done | bytes 208928 | tf_op jit(solution)/shard_map/ppermute | solution.py:164
  13.0 0.0 collective-permute-done.refs_0_
  13.0 2.3 %collective-permute-start.4 = (bf16[136,768]{1,0:T(8,128)(2,1)S(1)}, bf16[136,768]{1,0:T(8,128)(2,1)S(1)}, u32[]{:S(2)}, u32[]{:S(2)}) collective-permute-start(bf16[136,768]{1,0:T(8,128)(2,1)S(1)} %collective-permute-done.2.refs_1_), channel_id=1, source_target_pairs={{0,8},{2,10},{8,12},{10,14},{12,4},{14,6},{4,0},{6,2},{1,9},{3,11}... | collective-permute-start | bytes 626696 | tf_op jit(solution)/shard_map/ppermute | solution.py:161
  15.3 0.0 collective-permute-start.3
  15.3 2.3 %collective-permute-done.5.refs_1_ = bf16[136,768]{1,0:T(8,128)(2,1)S(1)} collective-permute-done((bf16[136,768]{1,0:T(8,128)(2,1)S(1)}, bf16[136,768]{1,0:T(8,128)(2,1)S(1)}, u32[]{:S(2)}, u32[]{:S(2)}) %collective-permute-start.5) | collective-permute-done | bytes 208928 | tf_op jit(solution)/shard_map/ppermute | solution.py:161
  17.6 0.0 collective-permute-start.6
  17.7 1.1 %first_scores.1 = (bf16[256,768]{1,0:T(8,128)(2,1)S(1)}, f32[256,128]{1,0:T(8,128)S(1)}, f32[256,128]{1,0:T(8,128)S(1)}, f32[256,768]{1,0:T(8,128)S(1)}) custom-call(bf16[136,768]{1,0:T(8,128)(2,1)S(1)} %pack.1.own_ref, bf16[136,768]{1,0:T(8,128)(2,1)S(1)} %collective-permute-done.1.other_ref, bf16[136,768]{1,0:T(8,128)(2,1)S(1)} %collective-permute-done.refs_0_, ...), custom_call_target="tpu_custom_call" | custom-call | flops 30198988800 | bytes 2162688 | tf_op jit(solution)/shard_map/first_scores/pallas_call | solution.py:170
  18.8 2.7 %collective-permute-done.4.refs_3_ = bf16[136,768]{1,0:T(8,128)(2,1)S(1)} collective-permute-done((bf16[136,768]{1,0:T(8,128)(2,1)S(1)}, bf16[136,768]{1,0:T(8,128)(2,1)S(1)}, u32[]{:S(2)}, u32[]{:S(2)}) %collective-permute-start.4) | collective-permute-done | bytes 208928 | tf_op jit(solution)/shard_map/ppermute | solution.py:161
  21.5 0.0 collective-permute-done.3.refs_0_
  21.5 0.0 collective-permute-start.7
  21.5 0.0 collective-permute-done.6.refs_2_
  21.5 1.1 %more_scores.1 = (f32[256,128]{1,0:T(8,128)S(1)}, f32[256,768]{1,0:T(8,128)S(1)}) custom-call(bf16[256,768]{1,0:T(8,128)(2,1)S(1)} %get-tuple-element.22.unit_ref, f32[256,128]{1,0:T(8,128)S(1)} %get-tuple-element.23.side_ref, f32[256,128]{1,0:T(8,128)S(1)} %get-tuple-element.25.old_sums_ref, ...), custom_call_target="tpu_custom_call", output_to_operand_aliasing={{0}: (2, {}), {1}: (3, {})} | custom-call | flops 40265318400 | bytes 2359296 | tf_op jit(solution)/shard_map/more_scores/pallas_call | solution.py:184
  22.6 0.4 %collective-permute-done.7.refs_0_ = bf16[136,768]{1,0:T(8,128)(2,1)S(1)} collective-permute-done((bf16[136,768]{1,0:T(8,128)(2,1)S(1)}, bf16[136,768]{1,0:T(8,128)(2,1)S(1)}, u32[]{:S(2)}, u32[]{:S(2)}) %collective-permute-start.7) | collective-permute-done | bytes 208928 | tf_op jit(solution)/shard_map/ppermute | solution.py:167
  23.0 0.6 %final_scores.1 = (f32[128,128]{1,0:T(8,128)S(1)}, f32[128,768]{1,0:T(8,128)S(1)}, bf16[136,768]{1,0:T(8,128)(2,1)S(1)}) custom-call(bf16[256,768]{1,0:T(8,128)(2,1)S(1)} %get-tuple-element.22.unit_ref, f32[256,128]{1,0:T(8,128)S(1)} %get-tuple-element.23.side_ref, f32[256,128]{1,0:T(8,128)S(1)} %get-tuple-element.29.old_sums_ref, ...), custom_call_target="tpu_custom_call" | custom-call | flops 10066329600 | bytes 1769472 | tf_op jit(solution)/shard_map/final_scores/pallas_call | solution.py:194
  23.6 1.6 %collective-permute-start.8 = (bf16[136,768]{1,0:T(8,128)(2,1)S(1)}, bf16[136,768]{1,0:T(8,128)(2,1)S(1)}, u32[]{:S(2)}, u32[]{:S(2)}) collective-permute-start(bf16[136,768]{1,0:T(8,128)(2,1)S(1)} %get-tuple-element.33), channel_id=1, source_target_pairs={{0,2},{2,0},{4,6},{6,4},{8,10},{10,8},{12,14},{14,12},{1,3},{3,1},... | collective-permute-start | bytes 626696 | tf_op jit(solution)/shard_map/ppermute | solution.py:164
  25.2 5.7 %collective-permute-done.8.got_ref = bf16[136,768]{1,0:T(8,128)(2,1)S(1)} collective-permute-done((bf16[136,768]{1,0:T(8,128)(2,1)S(1)}, bf16[136,768]{1,0:T(8,128)(2,1)S(1)}, u32[]{:S(2)}, u32[]{:S(2)}) %collective-permute-start.8) | collective-permute-done | bytes 208928 | tf_op jit(solution)/shard_map/ppermute | solution.py:164
  30.9 1.0 %combine.1 = (f32[1,128]{1,0:T(1,128)}, f32[128,768]{1,0:T(8,128)}) custom-call(f32[128,128]{1,0:T(8,128)S(1)} %get-tuple-element.31.sums_ref, f32[128,768]{1,0:T(8,128)S(1)} %get-tuple-element.32.mixed_ref, bf16[136,768]{1,0:T(8,128)(2,1)S(1)} %collective-permute-done.8.got_ref), custom_call_target="tpu_custom_call" | custom-call | tf_op jit(solution)/shard_map/combine/pallas_call | solution.py:235
  (1 shorter events, 0.0 us)
Async XLA Ops:
  0.6 0.7 %copy-start.1 = (s32[128,1]{0,1:T(1,128)S(1)}, s32[128,1]{0,1:T(1,128)}, u32[]{:S(2)}) copy-start(s32[128,1]{0,1:T(1,128)} %param.4) | copy-start | bytes 1540
  0.6 0.7 %copy-start.2 = (s32[128]{0:T(128)S(1)}, s32[128]{0:T(128)}, u32[]{:S(2)}) copy-start(s32[128]{0:T(128)} %param.5) | copy-start | bytes 1540
  1.3 0.9 %copy-start = (bf16[128,768]{1,0:T(8,128)(2,1)S(1)}, bf16[128,768]{1,0:T(8,128)(2,1)}, u32[]{:S(2)}) copy-start(bf16[128,768]{1,0:T(8,128)(2,1)} %rows_ref.1) | copy-start | bytes 589828
  2.3 9.7 %collective-permute-start.2 = (bf16[136,768]{1,0:T(8,128)(2,1)S(1)}, bf16[136,768]{1,0:T(8,128)(2,1)S(1)}, u32[]{:S(2)}, u32[]{:S(2)}) collective-permute-start(bf16[136,768]{1,0:T(8,128)(2,1)S(1)} %pack.1.own_ref), channel_id=1, source_target_pairs={{0,8},{2,10},{8,12},{10,14},{12,4},{14,6},{4,0},{6,2},{1,9},{3,11}... | collective-permute-start | bytes 626696 | tf_op jit(solution)/shard_map/ppermute | solution.py:161
  6.3 6.6 %collective-permute-start.1 = (bf16[136,768]{1,0:T(8,128)(2,1)S(1)}, bf16[136,768]{1,0:T(8,128)(2,1)S(1)}, u32[]{:S(2)}, u32[]{:S(2)}) collective-permute-start(bf16[136,768]{1,0:T(8,128)(2,1)S(1)} %pack.1.own_ref), channel_id=1, source_target_pairs={{0,2},{2,0},{4,6},{6,4},{8,10},{10,8},{12,14},{14,12},{1,3},{3,1},... | collective-permute-start | bytes 626696 | tf_op jit(solution)/shard_map/ppermute | solution.py:164
  7.8 5.1 %collective-permute-start = (bf16[136,768]{1,0:T(8,128)(2,1)S(1)}, bf16[136,768]{1,0:T(8,128)(2,1)S(1)}, u32[]{:S(2)}, u32[]{:S(2)}) collective-permute-start(bf16[136,768]{1,0:T(8,128)(2,1)S(1)} %pack.1.own_ref), channel_id=1, source_target_pairs={{0,1},{1,0},{2,3},{3,2},{4,5},{5,4},{6,7},{7,6},{8,9},{9,8},{10,11... | collective-permute-start | bytes 626696 | tf_op jit(solution)/shard_map/ppermute | solution.py:167
  7.8 9.8 %collective-permute-start.5 = (bf16[136,768]{1,0:T(8,128)(2,1)S(1)}, bf16[136,768]{1,0:T(8,128)(2,1)S(1)}, u32[]{:S(2)}, u32[]{:S(2)}) collective-permute-start(bf16[136,768]{1,0:T(8,128)(2,1)S(1)} %pack.1.own_ref), channel_id=1, source_target_pairs={{0,4},{2,6},{8,0},{10,2},{12,8},{14,10},{4,12},{6,14},{1,5},{3,7},... | collective-permute-start | bytes 626696 | tf_op jit(solution)/shard_map/ppermute | solution.py:161
  13.0 8.6 %collective-permute-start.4 = (bf16[136,768]{1,0:T(8,128)(2,1)S(1)}, bf16[136,768]{1,0:T(8,128)(2,1)S(1)}, u32[]{:S(2)}, u32[]{:S(2)}) collective-permute-start(bf16[136,768]{1,0:T(8,128)(2,1)S(1)} %collective-permute-done.2.refs_1_), channel_id=1, source_target_pairs={{0,8},{2,10},{8,12},{10,14},{12,4},{14,6},{4,0},{6,2},{1,9},{3,11}... | collective-permute-start | bytes 626696 | tf_op jit(solution)/shard_map/ppermute | solution.py:161
  15.3 6.2 %collective-permute-start.3 = (bf16[136,768]{1,0:T(8,128)(2,1)S(1)}, bf16[136,768]{1,0:T(8,128)(2,1)S(1)}, u32[]{:S(2)}, u32[]{:S(2)}) collective-permute-start(bf16[136,768]{1,0:T(8,128)(2,1)S(1)} %collective-permute-done.2.refs_1_), channel_id=1, source_target_pairs={{0,1},{1,0},{2,3},{3,2},{4,5},{5,4},{6,7},{7,6},{8,9},{9,8},{10,11... | collective-permute-start | bytes 626696 | tf_op jit(solution)/shard_map/ppermute | solution.py:167
  17.6 3.9 %collective-permute-start.6 = (bf16[136,768]{1,0:T(8,128)(2,1)S(1)}, bf16[136,768]{1,0:T(8,128)(2,1)S(1)}, u32[]{:S(2)}, u32[]{:S(2)}) collective-permute-start(bf16[136,768]{1,0:T(8,128)(2,1)S(1)} %collective-permute-done.5.refs_1_), channel_id=1, source_target_pairs={{0,1},{1,0},{2,3},{3,2},{4,5},{5,4},{6,7},{7,6},{8,9},{9,8},{10,11... | collective-permute-start | bytes 626696 | tf_op jit(solution)/shard_map/ppermute | solution.py:167
  21.5 1.5 %collective-permute-start.7 = (bf16[136,768]{1,0:T(8,128)(2,1)S(1)}, bf16[136,768]{1,0:T(8,128)(2,1)S(1)}, u32[]{:S(2)}, u32[]{:S(2)}) collective-permute-start(bf16[136,768]{1,0:T(8,128)(2,1)S(1)} %collective-permute-done.4.refs_3_), channel_id=1, source_target_pairs={{0,1},{1,0},{2,3},{3,2},{4,5},{5,4},{6,7},{7,6},{8,9},{9,8},{10,11... | collective-permute-start | bytes 626696 | tf_op jit(solution)/shard_map/ppermute | solution.py:167
  23.6 7.3 %collective-permute-start.8 = (bf16[136,768]{1,0:T(8,128)(2,1)S(1)}, bf16[136,768]{1,0:T(8,128)(2,1)S(1)}, u32[]{:S(2)}, u32[]{:S(2)}) collective-permute-start(bf16[136,768]{1,0:T(8,128)(2,1)S(1)} %get-tuple-element.33), channel_id=1, source_target_pairs={{0,2},{2,0},{4,6},{6,4},{8,10},{10,8},{12,14},{14,12},{1,3},{3,1},... | collective-permute-start | bytes 626696 | tf_op jit(solution)/shard_map/ppermute | solution.py:164

commit v8 on v6

--- a/solution.py
+++ b/solution.py
@@ -163,14 +163,14 @@
     def across(array):
         return lax.ppermute(array, "shard", [(at, at ^ 1) for at in range(shards)])
 
-    def corner(beside, ahead):
+    def two_ways(by_ring, step, by_side):
         pairs = []
         for at in range(rounds):
             for side in range(2):
-                here = 2 * ring[at] + side
-                pairs.append((here * lanes, (2 * ring[at - 1] + side) * lanes))
+                here, there = 2 * ring[at] + side, 2 * ring[(at + step) % rounds] + side
+                pairs.append((here * lanes, there * lanes))
                 pairs += [(here * lanes + lane, (here ^ 1) * lanes + lane) for lane in range(1, lanes)]
-        source = jnp.where(lax.axis_index("owner") == 0, beside, ahead)
+        source = jnp.where(lax.axis_index("owner") == 0, by_ring, by_side)
         return lax.ppermute(source, ("shard", "owner"), pairs)
 
     def swap(array):
@@ -227,11 +227,11 @@
         other, beside, moved = lax.optimization_barrier((other, beside, moved))
         opposite = along(moved, 1)
         moved_beside = across(moved)
-        ahead_beside = corner(beside, ahead)
+        ahead_beside = two_ways(beside, -1, ahead)
         state = first(own, other, beside, ahead)
         unit, side = state[:2]
         moved_beside, opposite = lax.optimization_barrier((moved_beside, opposite))
-        last = [across(opposite)]
+        last = [two_ways(moved_beside, 1, opposite)]
         sums, mixed = more(*state, moved, moved_beside)
         sums, mixed = more(unit, side, sums, mixed, opposite, ahead_beside)
     else:

time: 31.9 us -> 30.7 us (0.962)
  waiting for transfers between devices: 12.6 us -> 11.2 us
    ppermute x3 -> x2, waiting for transfers between devices: 4.33 us -> 1.06 us  [across(): return lax.ppermute(array, 'shard', [(at, at ^ 1) for at in range(shards)])]
    ppermute x1 -> x2, waiting for transfers between devices: 0.5 us -> 2.36 us  [two_ways(): return lax.ppermute(source, ('shard', 'owner'), pairs)]
    ppermute x1 -> x2, starting transfers between devices: 1.27 us -> 2.95 us  [two_ways(): return lax.ppermute(source, ('shard', 'owner'), pairs)]
    ppermute x3 -> x2, starting transfers between devices: 4.5 us -> 3 us  [across(): return lax.ppermute(array, 'shard', [(at, at ^ 1) for at in range(shards)])]
  transfers between devices with their start and end apart: 9 -> 9, of which waited for: 7 -> 7; matrix products, arithmetic and copies ran while one was open for 0% -> 0% of each run, Pallas kernels for 9% -> 10%
where the time goes in v8:
time: 30.7 us; the launch traced here: 30.5 us
  starting transfers between devices  12.4 us (40%)
  waiting for transfers between devices  11.2 us (36%)
  Pallas kernels  4.55 us (15%)
  local copies, waits for them, and re-layouts  1.58 us (5%)
  between operations  0.7 us (2%)
    ppermute x3, starting transfers between devices, along(): return lax.ppermute(array, 'shard', pairs)  6.42 us
    ppermute x3, waiting for transfers between devices, along(): return lax.ppermute(array, 'shard', pairs)  6.33 us
    ppermute x2, starting transfers between devices, across(): return lax.ppermute(array, 'shard', [(at, at ^ 1) for at in range(shards)])  3 us
    ppermute x2, starting transfers between devices, two_ways(): return lax.ppermute(source, ('shard', 'owner'), pairs)  2.95 us
    ppermute x2, waiting for transfers between devices, two_ways(): return lax.ppermute(source, ('shard', 'owner'), pairs)  2.36 us
    pallas_call x2, Pallas kernels, more(): pl.pallas_call(more_kernel, out_shape=[shape(queries, 128), shape(queries...  1.81 us
    unnamed x6, local copies, waits for them, and re-layouts  1.58 us
    ppermute x2, waiting for transfers between devices, swap(): lax.ppermute(array, 'owner', [(at, lanes - 1 - at) for at in range(lanes)])  1.45 us
  transfers between devices with their start and end apart: 9, of which 7 were waited for; matrix products, arithmetic and copies ran while one was open for 0% of the time, Pallas kernels for 10%

profile of v8, /device:TPU:0, one launch (start us, length us, event | category | flops | bytes accessed | tf_op | source)
XLA Modules:
  0.0 30.5 jit_solution(2992351316779307254)
XLA Ops:
  0.6 0.0 copy-start.1
  0.6 0.0 copy-start.2
  0.6 0.6 %copy-done.1 = s32[128,1]{0,1:T(1,128)S(1)} copy-done((s32[128,1]{0,1:T(1,128)S(1)}, s32[128,1]{0,1:T(1,128)}, u32[]{:S(2)}) %copy-start.1) | copy-done | bytes 536
  1.3 0.0 copy-done.2
  1.3 0.0 copy-start
  1.3 0.9 %copy-done = bf16[128,768]{1,0:T(8,128)(2,1)S(1)} copy-done((bf16[128,768]{1,0:T(8,128)(2,1)S(1)}, bf16[128,768]{1,0:T(8,128)(2,1)}, u32[]{:S(2)}) %copy-start) | copy-done | bytes 196632
  2.3 4.1 %collective-permute-start.2 = (bf16[136,768]{1,0:T(8,128)(2,1)S(1)}, bf16[136,768]{1,0:T(8,128)(2,1)S(1)}, u32[]{:S(2)}, u32[]{:S(2)}) collective-permute-start(bf16[136,768]{1,0:T(8,128)(2,1)S(1)} %pack.1.own_ref), channel_id=1, source_target_pairs={{0,8},{2,10},{8,12},{10,14},{12,4},{14,6},{4,0},{6,2},{1,9},{3,11}... | collective-permute-start | bytes 626696 | tf_op jit(solution)/shard_map/ppermute | solution.py:161
  6.3 1.5 %collective-permute-start.1 = (bf16[136,768]{1,0:T(8,128)(2,1)S(1)}, bf16[136,768]{1,0:T(8,128)(2,1)S(1)}, u32[]{:S(2)}, u32[]{:S(2)}) collective-permute-start(bf16[136,768]{1,0:T(8,128)(2,1)S(1)} %pack.1.own_ref), channel_id=1, source_target_pairs={{0,2},{2,0},{4,6},{6,4},{8,10},{10,8},{12,14},{14,12},{1,3},{3,1},... | collective-permute-start | bytes 626696 | tf_op jit(solution)/shard_map/ppermute | solution.py:164
  7.8 0.0 collective-permute-start
  7.8 0.0 collective-permute-start.3
  7.8 4.1 %collective-permute-done.2.refs_0_ = bf16[136,768]{1,0:T(8,128)(2,1)S(1)} collective-permute-done((bf16[136,768]{1,0:T(8,128)(2,1)S(1)}, bf16[136,768]{1,0:T(8,128)(2,1)S(1)}, u32[]{:S(2)}, u32[]{:S(2)}) %collective-permute-start.2) | collective-permute-done | bytes 208928 | tf_op jit(solution)/shard_map/ppermute | solution.py:161
  11.9 1.1 %collective-permute-done.1.refs_0_ = bf16[136,768]{1,0:T(8,128)(2,1)S(1)} collective-permute-done((bf16[136,768]{1,0:T(8,128)(2,1)S(1)}, bf16[136,768]{1,0:T(8,128)(2,1)S(1)}, u32[]{:S(2)}, u32[]{:S(2)}) %collective-permute-start.1) | collective-permute-done | bytes 208928 | tf_op jit(solution)/shard_map/ppermute | solution.py:164
  13.0 0.0 collective-permute-done.other_ref
  13.0 2.3 %collective-permute-start.5 = (bf16[136,768]{1,0:T(8,128)(2,1)S(1)}, bf16[136,768]{1,0:T(8,128)(2,1)S(1)}, u32[]{:S(2)}, u32[]{:S(2)}) collective-permute-start(bf16[136,768]{1,0:T(8,128)(2,1)S(1)} %collective-permute-done.2.refs_0_), channel_id=1, source_target_pairs={{0,8},{2,10},{8,12},{10,14},{12,4},{14,6},{4,0},{6,2},{1,9},{3,11}... | collective-permute-start | bytes 626696 | tf_op jit(solution)/shard_map/ppermute | solution.py:161
  15.3 1.5 %collective-permute-start.4 = (bf16[136,768]{1,0:T(8,128)(2,1)S(1)}, bf16[136,768]{1,0:T(8,128)(2,1)S(1)}, u32[]{:S(2)}, u32[]{:S(2)}) collective-permute-start(bf16[136,768]{1,0:T(8,128)(2,1)S(1)} %collective-permute-done.2.refs_0_), channel_id=1, source_target_pairs={{0,2},{2,0},{4,6},{6,4},{8,10},{10,8},{12,14},{14,12},{1,3},{3,1},... | collective-permute-start | bytes 626696 | tf_op jit(solution)/shard_map/ppermute | solution.py:164
  16.8 0.8 %collective-permute-done.3.refs_1_ = bf16[136,768]{1,0:T(8,128)(2,1)S(1)} collective-permute-done((bf16[136,768]{1,0:T(8,128)(2,1)S(1)}, bf16[136,768]{1,0:T(8,128)(2,1)S(1)}, u32[]{:S(2)}, u32[]{:S(2)}) %collective-permute-start.3) | collective-permute-done | bytes 208928 | tf_op jit(solution)/shard_map/ppermute | solution.py:161
  17.7 1.3 %collective-permute-start.6 = (bf16[136,768]{1,0:T(8,128)(2,1)S(1)}, bf16[136,768]{1,0:T(8,128)(2,1)S(1)}, u32[]{:S(2)}, u32[]{:S(2)}) collective-permute-start(bf16[136,768]{1,0:T(8,128)(2,1)S(1)} %broadcast_select_fusion.1), channel_id=1, source_target_pairs={{0,4},{1,3},{2,6},{3,1},{8,0},{9,11},{10,2},{11,9},{12,8},{13,15},... | collective-permute-start | bytes 626696 | tf_op jit(solution)/shard_map/ppermute | solution.py:174
  18.9 1.1 %first_scores.1 = (bf16[256,768]{1,0:T(8,128)(2,1)S(1)}, f32[256,128]{1,0:T(8,128)S(1)}, f32[256,128]{1,0:T(8,128)S(1)}, f32[256,768]{1,0:T(8,128)S(1)}) custom-call(bf16[136,768]{1,0:T(8,128)(2,1)S(1)} %pack.1.own_ref, bf16[136,768]{1,0:T(8,128)(2,1)S(1)} %collective-permute-done.other_ref, bf16[136,768]{1,0:T(8,128)(2,1)S(1)} %collective-permute-done.1.refs_0_, ...), custom_call_target="tpu_custom_call" | custom-call | flops 30198988800 | bytes 2162688 | tf_op jit(solution)/shard_map/first_scores/pallas_call | solution.py:180
  20.1 1.4 %collective-permute-done.5.refs_0_ = bf16[136,768]{1,0:T(8,128)(2,1)S(1)} collective-permute-done((bf16[136,768]{1,0:T(8,128)(2,1)S(1)}, bf16[136,768]{1,0:T(8,128)(2,1)S(1)}, u32[]{:S(2)}, u32[]{:S(2)}) %collective-permute-start.5) | collective-permute-done | bytes 208928 | tf_op jit(solution)/shard_map/ppermute | solution.py:161
  21.5 0.0 collective-permute-done.4.refs_1_
  21.6 1.7 %collective-permute-start.7 = (bf16[136,768]{1,0:T(8,128)(2,1)S(1)}, bf16[136,768]{1,0:T(8,128)(2,1)S(1)}, u32[]{:S(2)}, u32[]{:S(2)}) collective-permute-start(bf16[136,768]{1,0:T(8,128)(2,1)S(1)} %broadcast_select_fusion), channel_id=1, source_target_pairs={{0,8},{1,3},{2,10},{3,1},{8,12},{9,11},{10,14},{11,9},{12,4},{13,1... | collective-permute-start | bytes 626696 | tf_op jit(solution)/shard_map/ppermute | solution.py:174
  23.2 0.9 %more_scores.2 = (f32[256,128]{1,0:T(8,128)S(1)}, f32[256,768]{1,0:T(8,128)S(1)}) custom-call(bf16[256,768]{1,0:T(8,128)(2,1)S(1)} %get-tuple-element.22.unit_ref, f32[256,128]{1,0:T(8,128)S(1)} %get-tuple-element.23.side_ref, f32[256,128]{1,0:T(8,128)S(1)} %get-tuple-element.24.old_sums_ref, ...), custom_call_target="tpu_custom_call", output_to_operand_aliasing={{0}: (2, {}), {1}: (3, {})} | custom-call | flops 20132659200 | bytes 1966080 | tf_op jit(solution)/shard_map/more_scores/pallas_call | solution.py:194
  24.1 0.3 collective-permute-done.6.refs_1_
  24.4 0.9 %more_scores.3 = (f32[256,128]{1,0:T(8,128)S(1)}, f32[256,768]{1,0:T(8,128)S(1)}) custom-call(bf16[256,768]{1,0:T(8,128)(2,1)S(1)} %get-tuple-element.22.unit_ref, f32[256,128]{1,0:T(8,128)S(1)} %get-tuple-element.23.side_ref, f32[256,128]{1,0:T(8,128)S(1)} %get-tuple-element.28.old_sums_ref, ...), custom_call_target="tpu_custom_call", output_to_operand_aliasing={{0}: (2, {}), {1}: (3, {})} | custom-call | flops 20132659200 | bytes 1966080 | tf_op jit(solution)/shard_map/more_scores/pallas_call | solution.py:194
  25.3 2.1 %collective-permute-done.7.refs_0_ = bf16[136,768]{1,0:T(8,128)(2,1)S(1)} collective-permute-done((bf16[136,768]{1,0:T(8,128)(2,1)S(1)}, bf16[136,768]{1,0:T(8,128)(2,1)S(1)}, u32[]{:S(2)}, u32[]{:S(2)}) %collective-permute-start.7) | collective-permute-done | bytes 208928 | tf_op jit(solution)/shard_map/ppermute | solution.py:174
  27.4 0.6 %final_scores.1 = (f32[128,128]{1,0:T(8,128)S(1)}, f32[128,768]{1,0:T(8,128)S(1)}, bf16[136,768]{1,0:T(8,128)(2,1)S(1)}) custom-call(bf16[256,768]{1,0:T(8,128)(2,1)S(1)} %get-tuple-element.22.unit_ref, f32[256,128]{1,0:T(8,128)S(1)} %get-tuple-element.23.side_ref, f32[256,128]{1,0:T(8,128)S(1)} %get-tuple-element.31.old_sums_ref, ...), custom_call_target="tpu_custom_call" | custom-call | flops 10066329600 | bytes 1769472 | tf_op jit(solution)/shard_map/final_scores/pallas_call | solution.py:204
  28.0 0.1 collective-permute-start.8
  28.1 1.4 %collective-permute-done.8.got_ref = bf16[136,768]{1,0:T(8,128)(2,1)S(1)} collective-permute-done((bf16[136,768]{1,0:T(8,128)(2,1)S(1)}, bf16[136,768]{1,0:T(8,128)(2,1)S(1)}, u32[]{:S(2)}, u32[]{:S(2)}) %collective-permute-start.8) | collective-permute-done | bytes 208928 | tf_op jit(solution)/shard_map/ppermute | solution.py:177
  29.6 1.0 %combine.1 = (f32[1,128]{1,0:T(1,128)}, f32[128,768]{1,0:T(8,128)}) custom-call(f32[128,128]{1,0:T(8,128)S(1)} %get-tuple-element.33.sums_ref, f32[128,768]{1,0:T(8,128)S(1)} %get-tuple-element.34.mixed_ref, bf16[136,768]{1,0:T(8,128)(2,1)S(1)} %collective-permute-done.8.got_ref), custom_call_target="tpu_custom_call" | custom-call | tf_op jit(solution)/shard_map/combine/pallas_call | solution.py:249
  (3 shorter events, 0.1 us)
Async XLA Ops:
  0.6 0.7 %copy-start.1 = (s32[128,1]{0,1:T(1,128)S(1)}, s32[128,1]{0,1:T(1,128)}, u32[]{:S(2)}) copy-start(s32[128,1]{0,1:T(1,128)} %param.4) | copy-start | bytes 1540
  0.6 0.7 %copy-start.2 = (s32[128]{0:T(128)S(1)}, s32[128]{0:T(128)}, u32[]{:S(2)}) copy-start(s32[128]{0:T(128)} %param.5) | copy-start | bytes 1540
  1.3 0.9 %copy-start = (bf16[128,768]{1,0:T(8,128)(2,1)S(1)}, bf16[128,768]{1,0:T(8,128)(2,1)}, u32[]{:S(2)}) copy-start(bf16[128,768]{1,0:T(8,128)(2,1)} %rows_ref.1) | copy-start | bytes 589828
  2.3 9.7 %collective-permute-start.2 = (bf16[136,768]{1,0:T(8,128)(2,1)S(1)}, bf16[136,768]{1,0:T(8,128)(2,1)S(1)}, u32[]{:S(2)}, u32[]{:S(2)}) collective-permute-start(bf16[136,768]{1,0:T(8,128)(2,1)S(1)} %pack.1.own_ref), channel_id=1, source_target_pairs={{0,8},{2,10},{8,12},{10,14},{12,4},{14,6},{4,0},{6,2},{1,9},{3,11}... | collective-permute-start | bytes 626696 | tf_op jit(solution)/shard_map/ppermute | solution.py:161
  6.3 6.6 %collective-permute-start.1 = (bf16[136,768]{1,0:T(8,128)(2,1)S(1)}, bf16[136,768]{1,0:T(8,128)(2,1)S(1)}, u32[]{:S(2)}, u32[]{:S(2)}) collective-permute-start(bf16[136,768]{1,0:T(8,128)(2,1)S(1)} %pack.1.own_ref), channel_id=1, source_target_pairs={{0,2},{2,0},{4,6},{6,4},{8,10},{10,8},{12,14},{14,12},{1,3},{3,1},... | collective-permute-start | bytes 626696 | tf_op jit(solution)/shard_map/ppermute | solution.py:164
  7.8 5.1 %collective-permute-start = (bf16[136,768]{1,0:T(8,128)(2,1)S(1)}, bf16[136,768]{1,0:T(8,128)(2,1)S(1)}, u32[]{:S(2)}, u32[]{:S(2)}) collective-permute-start(bf16[136,768]{1,0:T(8,128)(2,1)S(1)} %pack.1.own_ref), channel_id=1, source_target_pairs={{0,1},{1,0},{2,3},{3,2},{4,5},{5,4},{6,7},{7,6},{8,9},{9,8},{10,11... | collective-permute-start | bytes 626696 | tf_op jit(solution)/shard_map/ppermute | solution.py:177
  7.8 9.8 %collective-permute-start.3 = (bf16[136,768]{1,0:T(8,128)(2,1)S(1)}, bf16[136,768]{1,0:T(8,128)(2,1)S(1)}, u32[]{:S(2)}, u32[]{:S(2)}) collective-permute-start(bf16[136,768]{1,0:T(8,128)(2,1)S(1)} %pack.1.own_ref), channel_id=1, source_target_pairs={{0,4},{2,6},{8,0},{10,2},{12,8},{14,10},{4,12},{6,14},{1,5},{3,7},... | collective-permute-start | bytes 626696 | tf_op jit(solution)/shard_map/ppermute | solution.py:161
  13.0 8.6 %collective-permute-start.5 = (bf16[136,768]{1,0:T(8,128)(2,1)S(1)}, bf16[136,768]{1,0:T(8,128)(2,1)S(1)}, u32[]{:S(2)}, u32[]{:S(2)}) collective-permute-start(bf16[136,768]{1,0:T(8,128)(2,1)S(1)} %collective-permute-done.2.refs_0_), channel_id=1, source_target_pairs={{0,8},{2,10},{8,12},{10,14},{12,4},{14,6},{4,0},{6,2},{1,9},{3,11}... | collective-permute-start | bytes 626696 | tf_op jit(solution)/shard_map/ppermute | solution.py:161
  15.3 6.2 %collective-permute-start.4 = (bf16[136,768]{1,0:T(8,128)(2,1)S(1)}, bf16[136,768]{1,0:T(8,128)(2,1)S(1)}, u32[]{:S(2)}, u32[]{:S(2)}) collective-permute-start(bf16[136,768]{1,0:T(8,128)(2,1)S(1)} %collective-permute-done.2.refs_0_), channel_id=1, source_target_pairs={{0,2},{2,0},{4,6},{6,4},{8,10},{10,8},{12,14},{14,12},{1,3},{3,1},... | collective-permute-start | bytes 626696 | tf_op jit(solution)/shard_map/ppermute | solution.py:164
  17.7 6.8 %collective-permute-start.6 = (bf16[136,768]{1,0:T(8,128)(2,1)S(1)}, bf16[136,768]{1,0:T(8,128)(2,1)S(1)}, u32[]{:S(2)}, u32[]{:S(2)}) collective-permute-start(bf16[136,768]{1,0:T(8,128)(2,1)S(1)} %broadcast_select_fusion.1), channel_id=1, source_target_pairs={{0,4},{1,3},{2,6},{3,1},{8,0},{9,11},{10,2},{11,9},{12,8},{13,15},... | collective-permute-start | bytes 626696 | tf_op jit(solution)/shard_map/ppermute | solution.py:174
  21.6 5.9 %collective-permute-start.7 = (bf16[136,768]{1,0:T(8,128)(2,1)S(1)}, bf16[136,768]{1,0:T(8,128)(2,1)S(1)}, u32[]{:S(2)}, u32[]{:S(2)}) collective-permute-start(bf16[136,768]{1,0:T(8,128)(2,1)S(1)} %broadcast_select_fusion), channel_id=1, source_target_pairs={{0,8},{1,3},{2,10},{3,1},{8,12},{9,11},{10,14},{11,9},{12,4},{13,1... | collective-permute-start | bytes 626696 | tf_op jit(solution)/shard_map/ppermute | solution.py:174
  28.0 1.5 %collective-permute-start.8 = (bf16[136,768]{1,0:T(8,128)(2,1)S(1)}, bf16[136,768]{1,0:T(8,128)(2,1)S(1)}, u32[]{:S(2)}, u32[]{:S(2)}) collective-permute-start(bf16[136,768]{1,0:T(8,128)(2,1)S(1)} %get-tuple-element.35), channel_id=1, source_target_pairs={{0,1},{1,0},{2,3},{3,2},{4,5},{5,4},{6,7},{7,6},{8,9},{9,8},{10,11... | collective-permute-start | bytes 626696 | tf_op jit(solution)/shard_map/ppermute | solution.py:177

commit v9 on v8

--- a/solution.py
+++ b/solution.py
@@ -1,3 +1,5 @@
+import functools
+
 import jax
 import jax.numpy as jnp
 from jax import lax
@@ -35,35 +37,16 @@
     return high, (value - high.astype(jnp.float32)).astype(jnp.bfloat16)
 
 
-def pack_kernel(rows_ref, label_ref, rank_ref, packed_ref):
-    count, width = rows_ref.shape
-    packed_ref[:count, :] = rows_ref[...]
-    rank = rank_ref[...]
-    high = lax.shift_right_logical(rank, 8)
-    low = rank - lax.shift_left(high, 8)
-    pieces = [piece.astype(jnp.float32) for piece in (label_ref[...], high, low)]
-    pieces.append(jnp.zeros((1, width - 3 * count), jnp.float32))
-    line = jnp.concatenate(pieces, axis=1)
-    packed_ref[count:, :] = jnp.broadcast_to(line, (EXTRA, width)).astype(jnp.bfloat16)
-
-
-def labels_and_ranks(block):
-    count = block.shape[0] - EXTRA
-    line = block[count:, :].astype(jnp.float32)[:1]
-    label, high, low = (line[:, at * count : (at + 1) * count] for at in range(3))
-    return label, high * 256.0 + low
-
-
-def rows_of(blocks):
-    return jnp.concatenate([block[: block.shape[0] - EXTRA, :] for block in blocks], axis=0)
-
-
-def score(unit, side, blocks):
+def tags_kernel(label_ref, rank_ref, tags_ref):
+    tags_ref[0:1, :] = label_ref[...]
+    tags_ref[1:2, :] = rank_ref[...]
+
+
+def score(unit, side, blocks, tags):
     own_label, own_rank = side[:, 0:1], side[:, 1:2]
-    keys = rows_of(blocks)
-    sides = [labels_and_ranks(block) for block in blocks]
-    label = jnp.concatenate([item[0] for item in sides], axis=1)
-    rank = jnp.concatenate([item[1] for item in sides], axis=1)
+    keys = jnp.concatenate([block[...] for block in blocks], axis=0)
+    label = jnp.concatenate([tag[0:1] for tag in tags], axis=1)
+    rank = jnp.concatenate([tag[1:2] for tag in tags], axis=1)
     cosine = lax.dot_general(
         unit, make_unit(keys), (((1,), (1,)), ((), ())), preferred_element_type=jnp.float32
     )
@@ -75,35 +58,44 @@
     return earlier, every, mixed
 
 
-def first_kernel(own_ref, other_ref, *refs):
-    blocks, (unit_ref, side_ref, sums_ref, mixed_ref) = refs[:-4], refs[-4:]
-    count = own_ref.shape[0] - EXTRA
+def tags_of(tags_ref, order):
+    tags = tags_ref[...].astype(jnp.float32)
+    return [tags[2 * at : 2 * at + 2] for at in order]
+
+
+def first_kernel(own_ref, other_ref, beside_ref, tags_ref, other_tags_ref, *outs):
+    unit_ref, side_ref, sums_ref, mixed_ref = outs
+    count = own_ref.shape[0]
     side_ref[...] = jnp.zeros_like(side_ref)
     sums_ref[...] = jnp.zeros_like(sums_ref)
-    unit_ref[...] = make_unit(rows_of([own_ref, other_ref]))
-    for at, ref in enumerate((own_ref, other_ref)):
+    tags = tags_of(tags_ref, (0, 1))
+    for at, (ref, tag) in enumerate(
+        ((own_ref, tags[0]), (other_ref, tags_of(other_tags_ref, (0,))[0]))
+    ):
         here = slice(at * count, (at + 1) * count)
-        label, rank = labels_and_ranks(ref)
-        side_ref[here, 0:1] = as_column(label)
-        side_ref[here, 1:2] = as_column(rank)
+        unit_ref[here, :] = make_unit(ref[...])
+        side_ref[here, 0:1] = as_column(tag[0:1])
+        side_ref[here, 1:2] = as_column(tag[1:2])
     sums_ref[:, 0:1], sums_ref[:, 1:2], mixed_ref[...] = score(
-        unit_ref[...], side_ref, (own_ref,) + blocks
-    )
-
-
-def more_kernel(unit_ref, side_ref, old_sums_ref, old_mixed_ref, *refs):
+        unit_ref[...], side_ref, (own_ref, beside_ref), tags
+    )
+
+
+def more_kernel(order, unit_ref, side_ref, old_sums_ref, old_mixed_ref, tags_ref, *refs):
     blocks, (sums_ref, mixed_ref) = refs[:-2], refs[-2:]
-    earlier, every, mixed = score(unit_ref[...], side_ref, blocks)
+    tags = tags_of(tags_ref, order)
+    earlier, every, mixed = score(unit_ref[...], side_ref, blocks, tags)
     sums_ref[...] = old_sums_ref[...]
     sums_ref[:, 0:1] += earlier
     sums_ref[:, 1:2] += every
     mixed_ref[...] = old_mixed_ref[...] + mixed
 
 
-def final_kernel(unit_ref, side_ref, old_sums_ref, old_mixed_ref, *refs):
+def final_kernel(order, unit_ref, side_ref, old_sums_ref, old_mixed_ref, tags_ref, *refs):
     blocks, (keep_sums_ref, keep_ref, send_ref) = refs[:-3], refs[-3:]
     count, width = keep_ref.shape
-    earlier, every, mixed = score(unit_ref[...], side_ref, blocks)
+    tags = tags_of(tags_ref, order)
+    earlier, every, mixed = score(unit_ref[...], side_ref, blocks, tags)
     earlier += old_sums_ref[:, 0:1]
     every += old_sums_ref[:, 1:2]
     mixed += old_mixed_ref[...]
@@ -139,7 +131,6 @@
 
 def local(embeddings, cluster_id, priority):
     count, width = embeddings.shape
-    height = count + EXTRA
     shards = lax.axis_size("shard")
     lanes = lax.axis_size("owner")
     rounds = shards // 2
@@ -176,7 +167,7 @@
     def swap(array):
         return lax.ppermute(array, "owner", [(at, lanes - 1 - at) for at in range(lanes)])
 
-    def first(*blocks):
+    def first(own, other, beside, tags, other_tags):
         return pl.pallas_call(
             first_kernel,
             out_shape=[
@@ -185,67 +176,71 @@
                 shape(queries, 128),
                 shape(queries, width),
             ],
-            cost_estimate=cost(queries, (len(blocks) - 1) * count, width),
+            cost_estimate=cost(queries, 3 * count, width),
             compiler_params=params,
             name="first_scores",
-        )(*blocks)
-
-    def more(unit, side, sums, mixed, *blocks):
+        )(own, other, beside, tags, other_tags)
+
+    def more(unit, side, sums, mixed, tags, order, *blocks):
         return pl.pallas_call(
-            more_kernel,
+            functools.partial(more_kernel, order),
             out_shape=[shape(queries, 128), shape(queries, width)],
             input_output_aliases={2: 0, 3: 1},
             cost_estimate=cost(queries, len(blocks) * count, width),
             compiler_params=params,
             name="more_scores",
-        )(unit, side, sums, mixed, *blocks)
-
-    def final(unit, side, sums, mixed, *blocks):
+        )(unit, side, sums, mixed, tags, *blocks)
+
+    def final(unit, side, sums, mixed, tags, order, *blocks):
         return pl.pallas_call(
-            final_kernel,
+            functools.partial(final_kernel, order),
             out_shape=[
                 shape(count, 128),
                 shape(count, width),
-                shape(height, width, dtype=bf16),
+                shape(count + EXTRA, width, dtype=bf16),
             ],
             cost_estimate=cost(queries, len(blocks) * count, width),
             compiler_params=params,
             name="final_scores",
-        )(unit, side, sums, mixed, *blocks)
-
-    own = pl.pallas_call(
-        pack_kernel,
-        out_shape=shape(height, width, dtype=bf16),
-        compiler_params=params,
-        name="pack",
-    )(embeddings, cluster_id.reshape(1, count), priority.reshape(1, count))
-
-    moved, beside = along(own, 1), across(own)
-    other = swap(own)
+        )(unit, side, sums, mixed, tags, *blocks)
+
+    own = embeddings
+    moved, beside, other = along(own, 1), across(own), swap(own)
+    if rounds == 4:
+        other, cluster_id, priority = lax.optimization_barrier((other, cluster_id, priority))
+    tags = pl.pallas_call(
+        tags_kernel, out_shape=shape(2, count, dtype=jnp.int32), compiler_params=params, name="tags"
+    )(cluster_id.reshape(1, count), priority.reshape(1, count))
+    other_tags = swap(tags)
+    pair = jnp.concatenate([tags, across(tags)], axis=0)
+    moved_tags = along(pair, 1)
     if rounds == 4:
         ahead = along(own, -1)
-        other, beside, moved = lax.optimization_barrier((other, beside, moved))
+        moved, beside = lax.optimization_barrier((moved, beside))
         opposite = along(moved, 1)
         moved_beside = across(moved)
+        ahead, moved_tags = lax.optimization_barrier((ahead, moved_tags))
         ahead_beside = two_ways(beside, -1, ahead)
-        state = first(own, other, beside, ahead)
-        unit, side = state[:2]
-        moved_beside, opposite = lax.optimization_barrier((moved_beside, opposite))
-        last = [two_ways(moved_beside, 1, opposite)]
-        sums, mixed = more(*state, moved, moved_beside)
-        sums, mixed = more(unit, side, sums, mixed, opposite, ahead_beside)
+        unit, side, sums, mixed = first(own, other, beside, pair, other_tags)
+        far_tags = along(jnp.concatenate([pair, moved_tags], axis=0), 2)
+        opposite, moved_beside = lax.optimization_barrier((opposite, moved_beside))
+        last = two_ways(moved_beside, 1, opposite)
+        sums, mixed = more(unit, side, sums, mixed, moved_tags, (0, 1), moved, moved_beside)
+        sums, mixed = more(unit, side, sums, mixed, far_tags, (2, 3, 0), ahead, ahead_beside, opposite)
+        outcome = final(unit, side, sums, mixed, far_tags, (1,), last)
     else:
-        unit, side, sums, mixed = first(own, other, beside)
+        unit, side, sums, mixed = first(own, other, beside, pair, other_tags)
 
         def turn(at, state):
-            moved, sums, mixed = state
-            ahead, beside = along(moved, 1), across(moved)
-            sums, mixed = more(unit, side, sums, mixed, moved, beside)
-            return ahead, sums, mixed
-
-        moved, sums, mixed = lax.fori_loop(1, rounds - 1, turn, (moved, sums, mixed))
-        last = [moved, across(moved)]
-    keep_sums, keep, send = final(unit, side, sums, mixed, *last)
+            moved, tags, sums, mixed = state
+            ahead, ahead_tags, beside = along(moved, 1), along(tags, 1), across(moved)
+            sums, mixed = more(unit, side, sums, mixed, tags, (0, 1), moved, beside)
+            return ahead, ahead_tags, sums, mixed
+
+        state = (moved, moved_tags, sums, mixed)
+        moved, moved_tags, sums, mixed = lax.fori_loop(1, rounds - 1, turn, state)
+        outcome = final(unit, side, sums, mixed, moved_tags, (0, 1), moved, across(moved))
+    keep_sums, keep, send = outcome
     dup, out = pl.pallas_call(
         combine_kernel,
         out_shape=[shape(1, count), shape(count, width)],

time: 30.7 us -> 35.8 us (1.17)
  starting transfers between devices: 12.4 us -> 15.3 us
  waiting for transfers between devices: 11.2 us -> 13.4 us
    ppermute x2, waiting for transfers between devices: 2.36 us -> 4.79 us  [two_ways(): return lax.ppermute(source, ('shard', 'owner'), pairs)]
    ppermute x3 -> x5, starting transfers between devices: 6.42 us -> 8.22 us  [along(): return lax.ppermute(array, 'shard', pairs)]
    ppermute x3 -> x5, waiting for transfers between devices: 6.33 us -> 5.52 us  [along(): return lax.ppermute(array, 'shard', pairs)]
    ppermute x2 -> x3, waiting for transfers between devices: 1.06 us -> 1.65 us  [across(): return lax.ppermute(array, 'shard', [(at, at ^ 1) for at in range(shards)])]
    ppermute x2 -> x3, starting transfers between devices: 0.07 us -> 0.59 us  [swap(): lax.ppermute(array, 'owner', [(at, lanes - 1 - at) for at in range(lanes)])]
    ppermute x2 -> x3, starting transfers between devices: 3 us -> 3.52 us  [across(): return lax.ppermute(array, 'shard', [(at, at ^ 1) for at in range(shards)])]
    ppermute x2 -> x3, waiting for transfers between devices: 1.45 us -> 1.45 us  [swap(): lax.ppermute(array, 'owner', [(at, lanes - 1 - at) for at in range(lanes)])]
  transfers between devices with their start and end apart: 9 -> 13, of which waited for: 7 -> 5; matrix products, arithmetic and copies ran while one was open for 0% -> 0% of each run, Pallas kernels for 10% -> 8%
where the time goes in v9:
time: 35.8 us; the launch traced here: 35.6 us
  starting transfers between devices  15.3 us (43%)
  waiting for transfers between devices  13.4 us (37%)
  Pallas kernels  4.47 us (12%)
  local copies, waits for them, and re-layouts  1.6 us (4%)
  between operations  0.74 us (2%)
    ppermute x5, starting transfers between devices, along(): return lax.ppermute(array, 'shard', pairs)  8.22 us
    ppermute x5, waiting for transfers between devices, along(): return lax.ppermute(array, 'shard', pairs)  5.52 us
    ppermute x2, waiting for transfers between devices, two_ways(): return lax.ppermute(source, ('shard', 'owner'), pairs)  4.79 us
    ppermute x3, starting transfers between devices, across(): return lax.ppermute(array, 'shard', [(at, at ^ 1) for at in range(shards)])  3.52 us
    ppermute x2, starting transfers between devices, two_ways(): return lax.ppermute(source, ('shard', 'owner'), pairs)  3 us
    pallas_call x2, Pallas kernels, more(): pl.pallas_call(functools.partial(more_kernel, order), out_shape=[shape(qu...  1.97 us
    ppermute x3, waiting for transfers between devices, across(): return lax.ppermute(array, 'shard', [(at, at ^ 1) for at in range(shards)])  1.65 us
    unnamed x6, local copies, waits for them, and re-layouts  1.6 us
  transfers between devices with their start and end apart: 13, of which 5 were waited for; matrix products, arithmetic and copies ran while one was open for 0% of the time, Pallas kernels for 8%

profile of v9, /device:TPU:0, one launch (start us, length us, event | category | flops | bytes accessed | tf_op | source)
XLA Modules:
  0.0 35.6 jit_solution(14268542721719087942)
XLA Ops:
  0.6 0.5 %collective-permute-start = (bf16[128,768]{1,0:T(8,128)(2,1)}, bf16[128,768]{1,0:T(8,128)(2,1)S(1)}, u32[]{:S(2)}, u32[]{:S(2)}) collective-permute-start(bf16[128,768]{1,0:T(8,128)(2,1)} %own_ref.1), channel_id=1, source_target_pairs={{0,1},{1,0},{2,3},{3,2},{4,5},{5,4},{6,7},{7,6},{8,9},{9,8},{10,11... | collective-permute-start | bytes 589832 | tf_op jit(solution)/shard_map/ppermute | solution.py:168
  1.1 3.7 %collective-permute-start.1 = (bf16[128,768]{1,0:T(8,128)(2,1)}, bf16[128,768]{1,0:T(8,128)(2,1)S(1)}, u32[]{:S(2)}, u32[]{:S(2)}) collective-permute-start(bf16[128,768]{1,0:T(8,128)(2,1)} %own_ref.1), channel_id=1, source_target_pairs={{0,8},{2,10},{8,12},{10,14},{12,4},{14,6},{4,0},{6,2},{1,9},{3,11}... | collective-permute-start | bytes 589832 | tf_op jit(solution)/shard_map/ppermute | solution.py:152
  4.8 1.5 %collective-permute-start.2 = (bf16[128,768]{1,0:T(8,128)(2,1)}, bf16[128,768]{1,0:T(8,128)(2,1)S(1)}, u32[]{:S(2)}, u32[]{:S(2)}) collective-permute-start(bf16[128,768]{1,0:T(8,128)(2,1)} %own_ref.1), channel_id=1, source_target_pairs={{0,2},{2,0},{4,6},{6,4},{8,10},{10,8},{12,14},{14,12},{1,3},{3,1},... | collective-permute-start | bytes 589832 | tf_op jit(solution)/shard_map/ppermute | solution.py:155
  6.3 0.0 collective-permute-done.other_ref
  6.3 0.0 copy-start
  6.3 0.0 copy-start.1
  6.3 0.7 %copy-done = s32[128,1]{0,1:T(1,128)S(1)} copy-done((s32[128,1]{0,1:T(1,128)S(1)}, s32[128,1]{0,1:T(1,128)}, u32[]{:S(2)}) %copy-start) | copy-done | bytes 536
  7.0 0.0 copy-done.1
  7.0 0.5 %collective-permute-start.3 = (s32[2,128]{1,0:T(2,128)S(1)}, s32[2,128]{1,0:T(2,128)S(1)}, u32[]{:S(2)}, u32[]{:S(2)}) collective-permute-start(s32[2,128]{1,0:T(2,128)S(1)} %tags.1), channel_id=1, source_target_pairs={{0,2},{2,0},{4,6},{6,4},{8,10},{10,8},{12,14},{14,12},{1,3},{3,1},... | collective-permute-start | bytes 3080 | tf_op jit(solution)/shard_map/ppermute | solution.py:155
  7.5 0.0 collective-permute-start.5
  7.5 0.0 collective-permute-start.4
  7.5 2.8 %collective-permute-done.1.refs_0_ = bf16[128,768]{1,0:T(8,128)(2,1)S(1)} collective-permute-done((bf16[128,768]{1,0:T(8,128)(2,1)}, bf16[128,768]{1,0:T(8,128)(2,1)S(1)}, u32[]{:S(2)}, u32[]{:S(2)}) %collective-permute-start.1) | collective-permute-done | bytes 196640 | tf_op jit(solution)/shard_map/ppermute | solution.py:152
  10.3 1.6 %collective-permute-done.2.beside_ref = bf16[128,768]{1,0:T(8,128)(2,1)S(1)} collective-permute-done((bf16[128,768]{1,0:T(8,128)(2,1)}, bf16[128,768]{1,0:T(8,128)(2,1)S(1)}, u32[]{:S(2)}, u32[]{:S(2)}) %collective-permute-start.2) | collective-permute-done | bytes 196640 | tf_op jit(solution)/shard_map/ppermute | solution.py:155
  12.0 1.6 %collective-permute-start.7 = (bf16[128,768]{1,0:T(8,128)(2,1)S(1)}, bf16[128,768]{1,0:T(8,128)(2,1)S(1)}, u32[]{:S(2)}, u32[]{:S(2)}) collective-permute-start(bf16[128,768]{1,0:T(8,128)(2,1)S(1)} %collective-permute-done.1.refs_0_), channel_id=1, source_target_pairs={{0,8},{2,10},{8,12},{10,14},{12,4},{14,6},{4,0},{6,2},{1,9},{3,11}... | collective-permute-start | bytes 589832 | tf_op jit(solution)/shard_map/ppermute | solution.py:152
  13.6 1.5 %collective-permute-start.8 = (bf16[128,768]{1,0:T(8,128)(2,1)S(1)}, bf16[128,768]{1,0:T(8,128)(2,1)S(1)}, u32[]{:S(2)}, u32[]{:S(2)}) collective-permute-start(bf16[128,768]{1,0:T(8,128)(2,1)S(1)} %collective-permute-done.1.refs_0_), channel_id=1, source_target_pairs={{0,2},{2,0},{4,6},{6,4},{8,10},{10,8},{12,14},{14,12},{1,3},{3,1},... | collective-permute-start | bytes 589832 | tf_op jit(solution)/shard_map/ppermute | solution.py:155
  15.1 0.0 collective-permute-done.3
  15.1 0.4 %collective-permute-start.6 = (s32[4,128]{1,0:T(4,128)S(1)}, s32[4,128]{1,0:T(4,128)S(1)}, u32[]{:S(2)}, u32[]{:S(2)}) collective-permute-start(s32[4,128]{1,0:T(4,128)S(1)} %pad_add_fusion.1.tags_ref), channel_id=1, source_target_pairs={{0,8},{2,10},{8,12},{10,14},{12,4},{14,6},{4,0},{6,2},{1,9},{3,11}... | collective-permute-start | bytes 6152 | tf_op jit(solution)/shard_map/ppermute | solution.py:152
  15.5 0.0 collective-permute-done.4.other_tags_ref
  15.5 0.0 copy-start.2
  15.5 0.9 %copy-done.2 = bf16[128,768]{1,0:T(8,128)(2,1)S(1)} copy-done((bf16[128,768]{1,0:T(8,128)(2,1)S(1)}, bf16[128,768]{1,0:T(8,128)(2,1)}, u32[]{:S(2)}) %copy-start.2) | copy-done | bytes 196632
  16.4 0.9 %first_scores.1 = (bf16[256,768]{1,0:T(8,128)(2,1)S(1)}, f32[256,128]{1,0:T(8,128)S(1)}, f32[256,128]{1,0:T(8,128)S(1)}, f32[256,768]{1,0:T(8,128)S(1)}) custom-call(bf16[128,768]{1,0:T(8,128)(2,1)S(1)} %copy-done.2, bf16[128,768]{1,0:T(8,128)(2,1)S(1)} %collective-permute-done.other_ref, bf16[128,768]{1,0:T(8,128)(2,1)S(1)} %collective-permute-done.2.beside_ref, ...), custom_call_target="tpu_custom_call" | custom-call | flops 30198988800 | bytes 2162688 | tf_op jit(solution)/shard_map/first_scores/pallas_call | solution.py:171
  17.3 0.0 collective-permute-done.5.refs_0_
  17.3 2.7 %collective-permute-done.6.tags_ref = s32[4,128]{1,0:T(4,128)S(1)} collective-permute-done((s32[4,128]{1,0:T(4,128)S(1)}, s32[4,128]{1,0:T(4,128)S(1)}, u32[]{:S(2)}, u32[]{:S(2)}) %collective-permute-start.6) | collective-permute-done | bytes 2080 | tf_op jit(solution)/shard_map/ppermute | solution.py:152
  20.1 2.5 %collective-permute-start.9 = (s32[8,128]{1,0:T(8,128)S(1)}, s32[8,128]{1,0:T(8,128)S(1)}, u32[]{:S(2)}, u32[]{:S(2)}) collective-permute-start(s32[8,128]{1,0:T(8,128)S(1)} %pad_add_fusion), channel_id=1, source_target_pairs={{0,12},{2,14},{8,4},{10,6},{12,0},{14,2},{4,8},{6,10},{1,13},{3,15... | collective-permute-start | bytes 12296 | tf_op jit(solution)/shard_map/ppermute | solution.py:152
  22.6 0.1 collective-permute-start.10
  22.7 0.0 collective-permute-done.7.refs_2_
  22.7 0.0 collective-permute-done.8.refs_1_
  22.7 2.9 %collective-permute-start.11 = (bf16[128,768]{1,0:T(8,128)(2,1)S(1)}, bf16[128,768]{1,0:T(8,128)(2,1)S(1)}, u32[]{:S(2)}, u32[]{:S(2)}) collective-permute-start(bf16[128,768]{1,0:T(8,128)(2,1)S(1)} %broadcast_select_fusion), channel_id=1, source_target_pairs={{0,8},{1,3},{2,10},{3,1},{8,12},{9,11},{10,14},{11,9},{12,4},{13,1... | collective-permute-start | bytes 589832 | tf_op jit(solution)/shard_map/ppermute | solution.py:165
  25.7 0.9 %more_scores.2 = (f32[256,128]{1,0:T(8,128)S(1)}, f32[256,768]{1,0:T(8,128)S(1)}) custom-call(bf16[256,768]{1,0:T(8,128)(2,1)S(1)} %get-tuple-element.28.unit_ref, f32[256,128]{1,0:T(8,128)S(1)} %get-tuple-element.29.side_ref, f32[256,128]{1,0:T(8,128)S(1)} %get-tuple-element.30.old_sums_ref, ...), custom_call_target="tpu_custom_call", output_to_operand_aliasing={{0}: (2, {}), {1}: (3, {})} | custom-call | flops 20132659200 | bytes 1966080 | tf_op jit(solution)/shard_map/more_scores/pallas_call | solution.py:185
  26.6 0.0 collective-permute-done.9.tags_ref
  26.6 4.8 %collective-permute-done.10.refs_1_ = bf16[128,768]{1,0:T(8,128)(2,1)S(1)} collective-permute-done((bf16[128,768]{1,0:T(8,128)(2,1)S(1)}, bf16[128,768]{1,0:T(8,128)(2,1)S(1)}, u32[]{:S(2)}, u32[]{:S(2)}) %collective-permute-start.10) | collective-permute-done | bytes 196640 | tf_op jit(solution)/shard_map/ppermute | solution.py:165
  31.4 1.1 %more_scores.3 = (f32[256,128]{1,0:T(8,128)S(1)}, f32[256,768]{1,0:T(8,128)S(1)}) custom-call(bf16[256,768]{1,0:T(8,128)(2,1)S(1)} %get-tuple-element.28.unit_ref, f32[256,128]{1,0:T(8,128)S(1)} %get-tuple-element.29.side_ref, f32[256,128]{1,0:T(8,128)S(1)} %get-tuple-element.35.old_sums_ref, ...), custom_call_target="tpu_custom_call", output_to_operand_aliasing={{0}: (2, {}), {1}: (3, {})} | custom-call | flops 30198988800 | bytes 2162688 | tf_op jit(solution)/shard_map/more_scores/pallas_call | solution.py:185
  32.5 0.0 collective-permute-done.11.refs_0_
  32.5 0.6 %final_scores.1 = (f32[128,128]{1,0:T(8,128)S(1)}, f32[128,768]{1,0:T(8,128)S(1)}, bf16[136,768]{1,0:T(8,128)(2,1)S(1)}) custom-call(bf16[256,768]{1,0:T(8,128)(2,1)S(1)} %get-tuple-element.28.unit_ref, f32[256,128]{1,0:T(8,128)S(1)} %get-tuple-element.29.side_ref, f32[256,128]{1,0:T(8,128)S(1)} %get-tuple-element.39.old_sums_ref, ...), custom_call_target="tpu_custom_call" | custom-call | flops 10066329600 | bytes 1769472 | tf_op jit(solution)/shard_map/final_scores/pallas_call | solution.py:195
  33.1 0.1 collective-permute-start.12
  33.2 1.4 %collective-permute-done.12.got_ref = bf16[136,768]{1,0:T(8,128)(2,1)S(1)} collective-permute-done((bf16[136,768]{1,0:T(8,128)(2,1)S(1)}, bf16[136,768]{1,0:T(8,128)(2,1)S(1)}, u32[]{:S(2)}, u32[]{:S(2)}) %collective-permute-start.12) | collective-permute-done | bytes 208928 | tf_op jit(solution)/shard_map/ppermute | solution.py:168
  34.6 1.0 %combine.1 = (f32[1,128]{1,0:T(1,128)}, f32[128,768]{1,0:T(8,128)}) custom-call(f32[128,128]{1,0:T(8,128)S(1)} %get-tuple-element.41.sums_ref, f32[128,768]{1,0:T(8,128)S(1)} %get-tuple-element.42.mixed_ref, bf16[136,768]{1,0:T(8,128)(2,1)S(1)} %collective-permute-done.12.got_ref), custom_call_target="tpu_custom_call" | custom-call | tf_op jit(solution)/shard_map/combine/pallas_call | solution.py:244
  (5 shorter events, 0.1 us)
Async XLA Ops:
  0.6 5.7 %collective-permute-start = (bf16[128,768]{1,0:T(8,128)(2,1)}, bf16[128,768]{1,0:T(8,128)(2,1)S(1)}, u32[]{:S(2)}, u32[]{:S(2)}) collective-permute-start(bf16[128,768]{1,0:T(8,128)(2,1)} %own_ref.1), channel_id=1, source_target_pairs={{0,1},{1,0},{2,3},{3,2},{4,5},{5,4},{6,7},{7,6},{8,9},{9,8},{10,11... | collective-permute-start | bytes 589832 | tf_op jit(solution)/shard_map/ppermute | solution.py:168
  1.1 9.2 %collective-permute-start.1 = (bf16[128,768]{1,0:T(8,128)(2,1)}, bf16[128,768]{1,0:T(8,128)(2,1)S(1)}, u32[]{:S(2)}, u32[]{:S(2)}) collective-permute-start(bf16[128,768]{1,0:T(8,128)(2,1)} %own_ref.1), channel_id=1, source_target_pairs={{0,8},{2,10},{8,12},{10,14},{12,4},{14,6},{4,0},{6,2},{1,9},{3,11}... | collective-permute-start | bytes 589832 | tf_op jit(solution)/shard_map/ppermute | solution.py:152
  4.8 7.2 %collective-permute-start.2 = (bf16[128,768]{1,0:T(8,128)(2,1)}, bf16[128,768]{1,0:T(8,128)(2,1)S(1)}, u32[]{:S(2)}, u32[]{:S(2)}) collective-permute-start(bf16[128,768]{1,0:T(8,128)(2,1)} %own_ref.1), channel_id=1, source_target_pairs={{0,2},{2,0},{4,6},{6,4},{8,10},{10,8},{12,14},{14,12},{1,3},{3,1},... | collective-permute-start | bytes 589832 | tf_op jit(solution)/shard_map/ppermute | solution.py:155
  6.3 0.7 %copy-start = (s32[128,1]{0,1:T(1,128)S(1)}, s32[128,1]{0,1:T(1,128)}, u32[]{:S(2)}) copy-start(s32[128,1]{0,1:T(1,128)} %param.4) | copy-start | bytes 1540
  6.3 0.7 %copy-start.1 = (s32[128]{0:T(128)S(1)}, s32[128]{0:T(128)}, u32[]{:S(2)}) copy-start(s32[128]{0:T(128)} %param.5) | copy-start | bytes 1540
  7.0 8.1 %collective-permute-start.3 = (s32[2,128]{1,0:T(2,128)S(1)}, s32[2,128]{1,0:T(2,128)S(1)}, u32[]{:S(2)}, u32[]{:S(2)}) collective-permute-start(s32[2,128]{1,0:T(2,128)S(1)} %tags.1), channel_id=1, source_target_pairs={{0,2},{2,0},{4,6},{6,4},{8,10},{10,8},{12,14},{14,12},{1,3},{3,1},... | collective-permute-start | bytes 3080 | tf_op jit(solution)/shard_map/ppermute | solution.py:155
  7.5 9.8 %collective-permute-start.5 = (bf16[128,768]{1,0:T(8,128)(2,1)}, bf16[128,768]{1,0:T(8,128)(2,1)S(1)}, u32[]{:S(2)}, u32[]{:S(2)}) collective-permute-start(bf16[128,768]{1,0:T(8,128)(2,1)} %own_ref.1), channel_id=1, source_target_pairs={{0,4},{2,6},{8,0},{10,2},{12,8},{14,10},{4,12},{6,14},{1,5},{3,7},... | collective-permute-start | bytes 589832 | tf_op jit(solution)/shard_map/ppermute | solution.py:152
  7.5 8.0 %collective-permute-start.4 = (s32[2,128]{1,0:T(2,128)S(1)}, s32[2,128]{1,0:T(2,128)S(1)}, u32[]{:S(2)}, u32[]{:S(2)}) collective-permute-start(s32[2,128]{1,0:T(2,128)S(1)} %tags.1), channel_id=1, source_target_pairs={{0,1},{1,0},{2,3},{3,2},{4,5},{5,4},{6,7},{7,6},{8,9},{9,8},{10,11... | collective-permute-start | bytes 3080 | tf_op jit(solution)/shard_map/ppermute | solution.py:168
  12.0 10.7 %collective-permute-start.7 = (bf16[128,768]{1,0:T(8,128)(2,1)S(1)}, bf16[128,768]{1,0:T(8,128)(2,1)S(1)}, u32[]{:S(2)}, u32[]{:S(2)}) collective-permute-start(bf16[128,768]{1,0:T(8,128)(2,1)S(1)} %collective-permute-done.1.refs_0_), channel_id=1, source_target_pairs={{0,8},{2,10},{8,12},{10,14},{12,4},{14,6},{4,0},{6,2},{1,9},{3,11}... | collective-permute-start | bytes 589832 | tf_op jit(solution)/shard_map/ppermute | solution.py:152
  13.6 9.1 %collective-permute-start.8 = (bf16[128,768]{1,0:T(8,128)(2,1)S(1)}, bf16[128,768]{1,0:T(8,128)(2,1)S(1)}, u32[]{:S(2)}, u32[]{:S(2)}) collective-permute-start(bf16[128,768]{1,0:T(8,128)(2,1)S(1)} %collective-permute-done.1.refs_0_), channel_id=1, source_target_pairs={{0,2},{2,0},{4,6},{6,4},{8,10},{10,8},{12,14},{14,12},{1,3},{3,1},... | collective-permute-start | bytes 589832 | tf_op jit(solution)/shard_map/ppermute | solution.py:155
  15.1 4.9 %collective-permute-start.6 = (s32[4,128]{1,0:T(4,128)S(1)}, s32[4,128]{1,0:T(4,128)S(1)}, u32[]{:S(2)}, u32[]{:S(2)}) collective-permute-start(s32[4,128]{1,0:T(4,128)S(1)} %pad_add_fusion.1.tags_ref), channel_id=1, source_target_pairs={{0,8},{2,10},{8,12},{10,14},{12,4},{14,6},{4,0},{6,2},{1,9},{3,11}... | collective-permute-start | bytes 6152 | tf_op jit(solution)/shard_map/ppermute | solution.py:152
  15.5 0.9 %copy-start.2 = (bf16[128,768]{1,0:T(8,128)(2,1)S(1)}, bf16[128,768]{1,0:T(8,128)(2,1)}, u32[]{:S(2)}) copy-start(bf16[128,768]{1,0:T(8,128)(2,1)} %own_ref.1) | copy-start | bytes 589828
  20.1 6.5 %collective-permute-start.9 = (s32[8,128]{1,0:T(8,128)S(1)}, s32[8,128]{1,0:T(8,128)S(1)}, u32[]{:S(2)}, u32[]{:S(2)}) collective-permute-start(s32[8,128]{1,0:T(8,128)S(1)} %pad_add_fusion), channel_id=1, source_target_pairs={{0,12},{2,14},{8,4},{10,6},{12,0},{14,2},{4,8},{6,10},{1,13},{3,15... | collective-permute-start | bytes 12296 | tf_op jit(solution)/shard_map/ppermute | solution.py:152
  22.6 8.8 %collective-permute-start.10 = (bf16[128,768]{1,0:T(8,128)(2,1)S(1)}, bf16[128,768]{1,0:T(8,128)(2,1)S(1)}, u32[]{:S(2)}, u32[]{:S(2)}) collective-permute-start(bf16[128,768]{1,0:T(8,128)(2,1)S(1)} %broadcast_select_fusion.1), channel_id=1, source_target_pairs={{0,4},{1,3},{2,6},{3,1},{8,0},{9,11},{10,2},{11,9},{12,8},{13,15},... | collective-permute-start | bytes 589832 | tf_op jit(solution)/shard_map/ppermute | solution.py:165
  22.7 9.7 %collective-permute-start.11 = (bf16[128,768]{1,0:T(8,128)(2,1)S(1)}, bf16[128,768]{1,0:T(8,128)(2,1)S(1)}, u32[]{:S(2)}, u32[]{:S(2)}) collective-permute-start(bf16[128,768]{1,0:T(8,128)(2,1)S(1)} %broadcast_select_fusion), channel_id=1, source_target_pairs={{0,8},{1,3},{2,10},{3,1},{8,12},{9,11},{10,14},{11,9},{12,4},{13,1... | collective-permute-start | bytes 589832 | tf_op jit(solution)/shard_map/ppermute | solution.py:165
  33.1 1.5 %collective-permute-start.12 = (bf16[136,768]{1,0:T(8,128)(2,1)S(1)}, bf16[136,768]{1,0:T(8,128)(2,1)S(1)}, u32[]{:S(2)}, u32[]{:S(2)}) collective-permute-start(bf16[136,768]{1,0:T(8,128)(2,1)S(1)} %get-tuple-element.43), channel_id=1, source_target_pairs={{0,1},{1,0},{2,3},{3,2},{4,5},{5,4},{6,7},{7,6},{8,9},{9,8},{10,11... | collective-permute-start | bytes 626696 | tf_op jit(solution)/shard_map/ppermute | solution.py:168

commit v10 on v8

--- a/solution.py
+++ b/solution.py
@@ -7,6 +7,7 @@
 
 EXTRA = 8
 VMEM = 24 * 1024 * 1024
+PACK_VMEM = 62 * 1024 * 1024
 
 
 def make_unit(rows):
@@ -35,16 +36,27 @@
     return high, (value - high.astype(jnp.float32)).astype(jnp.bfloat16)
 
 
-def pack_kernel(rows_ref, label_ref, rank_ref, packed_ref):
+def pack_kernel(rows_ref, label_ref, rank_ref, packed_ref, label, rank, line, sems):
     count, width = rows_ref.shape
-    packed_ref[:count, :] = rows_ref[...]
-    rank = rank_ref[...]
-    high = lax.shift_right_logical(rank, 8)
-    low = rank - lax.shift_left(high, 8)
-    pieces = [piece.astype(jnp.float32) for piece in (label_ref[...], high, low)]
+    copies = [
+        pltpu.make_async_copy(label_ref, label, sems.at[0]),
+        pltpu.make_async_copy(rank_ref, rank, sems.at[1]),
+        pltpu.make_async_copy(rows_ref, packed_ref.at[pl.ds(0, count), :], sems.at[2]),
+    ]
+    for copy in copies:
+        copy.start()
+    for copy in copies[:2]:
+        copy.wait()
+    high = lax.shift_right_logical(rank[...], 8)
+    low = rank[...] - lax.shift_left(high, 8)
+    pieces = [piece.astype(jnp.float32) for piece in (label[...], high, low)]
     pieces.append(jnp.zeros((1, width - 3 * count), jnp.float32))
-    line = jnp.concatenate(pieces, axis=1)
-    packed_ref[count:, :] = jnp.broadcast_to(line, (EXTRA, width)).astype(jnp.bfloat16)
+    row = jnp.concatenate(pieces, axis=1)
+    line[...] = jnp.broadcast_to(row, (EXTRA, width)).astype(jnp.bfloat16)
+    added = pltpu.make_async_copy(line, packed_ref.at[pl.ds(count, EXTRA), :], sems.at[3])
+    added.start()
+    added.wait()
+    copies[2].wait()
 
 
 def labels_and_ranks(block):
@@ -163,14 +175,16 @@
     def across(array):
         return lax.ppermute(array, "shard", [(at, at ^ 1) for at in range(shards)])
 
-    def two_ways(by_ring, step, by_side):
+    def two_ways(by_ring, step, by_side, ring_lane):
         pairs = []
         for at in range(rounds):
             for side in range(2):
                 here, there = 2 * ring[at] + side, 2 * ring[(at + step) % rounds] + side
-                pairs.append((here * lanes, there * lanes))
-                pairs += [(here * lanes + lane, (here ^ 1) * lanes + lane) for lane in range(1, lanes)]
-        source = jnp.where(lax.axis_index("owner") == 0, by_ring, by_side)
+                pairs += [
+                    (here * lanes + lane, (there if lane == ring_lane else here ^ 1) * lanes + lane)
+                    for lane in range(lanes)
+                ]
+        source = jnp.where(lax.axis_index("owner") == ring_lane, by_ring, by_side)
         return lax.ppermute(source, ("shard", "owner"), pairs)
 
     def swap(array):
@@ -215,8 +229,16 @@
 
     own = pl.pallas_call(
         pack_kernel,
+        in_specs=[pl.BlockSpec(memory_space=pl.ANY)] * 3,
+        out_specs=pl.BlockSpec(memory_space=pl.ANY),
         out_shape=shape(height, width, dtype=bf16),
-        compiler_params=params,
+        scratch_shapes=[
+            pltpu.VMEM((1, count), jnp.int32),
+            pltpu.VMEM((1, count), jnp.int32),
+            pltpu.VMEM((EXTRA, width), bf16),
+            pltpu.SemaphoreType.DMA((4,)),
+        ],
+        compiler_params=pltpu.CompilerParams(vmem_limit_bytes=PACK_VMEM),
         name="pack",
     )(embeddings, cluster_id.reshape(1, count), priority.reshape(1, count))
 
@@ -227,11 +249,11 @@
         other, beside, moved = lax.optimization_barrier((other, beside, moved))
         opposite = along(moved, 1)
         moved_beside = across(moved)
-        ahead_beside = two_ways(beside, -1, ahead)
+        ahead_beside = two_ways(beside, -1, ahead, 0)
         state = first(own, other, beside, ahead)
         unit, side = state[:2]
         moved_beside, opposite = lax.optimization_barrier((moved_beside, opposite))
-        last = [two_ways(moved_beside, 1, opposite)]
+        last = [two_ways(moved_beside, 1, opposite, lanes - 1)]
         sums, mixed = more(*state, moved, moved_beside)
         sums, mixed = more(unit, side, sums, mixed, opposite, ahead_beside)
     else:

time: 30.7 us -> 36.4 us (1.19)
  Pallas kernels: 4.55 us -> 11.6 us
  local copies, waits for them, and re-layouts: 1.58 us -> 0.01 us
    pallas_call x1, Pallas kernels: 0.02 us -> 7.09 us  [local(): pl.pallas_call(pack_kernel, in_specs=[pl.BlockSpec(memory_space=pl.ANY)]...]
    unnamed x6 -> x2, local copies, waits for them, and re-layouts: 1.58 us -> 0.01 us
  transfers between devices with their start and end apart: 9 -> 9, of which waited for: 7 -> 7; matrix products, arithmetic and copies ran while one was open for 0% -> 0% of each run, Pallas kernels for 10% -> 8%
where the time goes in v10:
time: 36.4 us; the launch traced here: 36.2 us
  starting transfers between devices  12.3 us (34%)
  Pallas kernels  11.6 us (32%)
  waiting for transfers between devices  11.5 us (32%)
  between operations  0.69 us (2%)
    pallas_call x1, Pallas kernels, local(): pl.pallas_call(pack_kernel, in_specs=[pl.BlockSpec(memory_space=pl.ANY)]...  7.09 us
    ppermute x3, waiting for transfers between devices, along(): return lax.ppermute(array, 'shard', pairs)  6.64 us
    ppermute x3, starting transfers between devices, along(): return lax.ppermute(array, 'shard', pairs)  6.42 us
    ppermute x2, starting transfers between devices, across(): return lax.ppermute(array, 'shard', [(at, at ^ 1) for at in range(shards)])  3 us
    ppermute x2, starting transfers between devices, two_ways(): return lax.ppermute(source, ('shard', 'owner'), pairs)  2.81 us
    ppermute x2, waiting for transfers between devices, two_ways(): return lax.ppermute(source, ('shard', 'owner'), pairs)  2.49 us
    pallas_call x2, Pallas kernels, more(): pl.pallas_call(more_kernel, out_shape=[shape(queries, 128), shape(queries...  1.81 us
    ppermute x2, waiting for transfers between devices, swap(): lax.ppermute(array, 'owner', [(at, lanes - 1 - at) for at in range(lanes)])  1.45 us
  transfers between devices with their start and end apart: 9, of which 7 were waited for; matrix products, arithmetic and copies ran while one was open for 0% of the time, Pallas kernels for 8%

profile of v10, /device:TPU:0, one launch (start us, length us, event | category | flops | bytes accessed | tf_op | source)
XLA Modules:
  0.0 36.2 jit_solution(64978432791600118)
XLA Ops:
  0.6 7.1 %pack.1.own_ref = bf16[136,768]{1,0:T(8,128)(2,1)} custom-call(bf16[128,768]{1,0:T(8,128)(2,1)} %rows_ref.1, s32[1,128]{1,0:T(1,128)} %bitcast.3, s32[1,128]{1,0:T(1,128)} %bitcast.4), custom_call_target="tpu_custom_call" | custom-call | tf_op jit(solution)/shard_map/pack/pallas_call | solution.py:230
  7.7 4.1 %collective-permute-start.2 = (bf16[136,768]{1,0:T(8,128)(2,1)}, bf16[136,768]{1,0:T(8,128)(2,1)S(1)}, u32[]{:S(2)}, u32[]{:S(2)}) collective-permute-start(bf16[136,768]{1,0:T(8,128)(2,1)} %pack.1.own_ref), channel_id=1, source_target_pairs={{0,8},{2,10},{8,12},{10,14},{12,4},{14,6},{4,0},{6,2},{1,9},{3,11}... | collective-permute-start | bytes 626696 | tf_op jit(solution)/shard_map/ppermute | solution.py:173
  11.8 1.5 %collective-permute-start.1 = (bf16[136,768]{1,0:T(8,128)(2,1)}, bf16[136,768]{1,0:T(8,128)(2,1)S(1)}, u32[]{:S(2)}, u32[]{:S(2)}) collective-permute-start(bf16[136,768]{1,0:T(8,128)(2,1)} %pack.1.own_ref), channel_id=1, source_target_pairs={{0,2},{2,0},{4,6},{6,4},{8,10},{10,8},{12,14},{14,12},{1,3},{3,1},... | collective-permute-start | bytes 626696 | tf_op jit(solution)/shard_map/ppermute | solution.py:176
  13.3 0.0 collective-permute-start
  13.3 0.0 collective-permute-start.3
  13.3 0.0 copy-start
  13.3 4.4 %collective-permute-done.2.refs_0_ = bf16[136,768]{1,0:T(8,128)(2,1)S(1)} collective-permute-done((bf16[136,768]{1,0:T(8,128)(2,1)}, bf16[136,768]{1,0:T(8,128)(2,1)S(1)}, u32[]{:S(2)}, u32[]{:S(2)}) %collective-permute-start.2) | collective-permute-done | bytes 208928 | tf_op jit(solution)/shard_map/ppermute | solution.py:173
  17.7 0.9 %collective-permute-done.1.refs_0_ = bf16[136,768]{1,0:T(8,128)(2,1)S(1)} collective-permute-done((bf16[136,768]{1,0:T(8,128)(2,1)}, bf16[136,768]{1,0:T(8,128)(2,1)S(1)}, u32[]{:S(2)}, u32[]{:S(2)}) %collective-permute-start.1) | collective-permute-done | bytes 208928 | tf_op jit(solution)/shard_map/ppermute | solution.py:176
  18.7 0.0 collective-permute-done.other_ref
  18.7 2.3 %collective-permute-start.5 = (bf16[136,768]{1,0:T(8,128)(2,1)S(1)}, bf16[136,768]{1,0:T(8,128)(2,1)S(1)}, u32[]{:S(2)}, u32[]{:S(2)}) collective-permute-start(bf16[136,768]{1,0:T(8,128)(2,1)S(1)} %collective-permute-done.2.refs_0_), channel_id=1, source_target_pairs={{0,8},{2,10},{8,12},{10,14},{12,4},{14,6},{4,0},{6,2},{1,9},{3,11}... | collective-permute-start | bytes 626696 | tf_op jit(solution)/shard_map/ppermute | solution.py:173
  21.0 1.5 %collective-permute-start.4 = (bf16[136,768]{1,0:T(8,128)(2,1)S(1)}, bf16[136,768]{1,0:T(8,128)(2,1)S(1)}, u32[]{:S(2)}, u32[]{:S(2)}) collective-permute-start(bf16[136,768]{1,0:T(8,128)(2,1)S(1)} %collective-permute-done.2.refs_0_), channel_id=1, source_target_pairs={{0,2},{2,0},{4,6},{6,4},{8,10},{10,8},{12,14},{14,12},{1,3},{3,1},... | collective-permute-start | bytes 626696 | tf_op jit(solution)/shard_map/ppermute | solution.py:176
  22.5 0.8 %collective-permute-done.3.refs_1_ = bf16[136,768]{1,0:T(8,128)(2,1)S(1)} collective-permute-done((bf16[136,768]{1,0:T(8,128)(2,1)}, bf16[136,768]{1,0:T(8,128)(2,1)S(1)}, u32[]{:S(2)}, u32[]{:S(2)}) %collective-permute-start.3) | collective-permute-done | bytes 208928 | tf_op jit(solution)/shard_map/ppermute | solution.py:173
  23.4 1.3 %collective-permute-start.6 = (bf16[136,768]{1,0:T(8,128)(2,1)S(1)}, bf16[136,768]{1,0:T(8,128)(2,1)S(1)}, u32[]{:S(2)}, u32[]{:S(2)}) collective-permute-start(bf16[136,768]{1,0:T(8,128)(2,1)S(1)} %broadcast_select_fusion.1), channel_id=1, source_target_pairs={{0,4},{1,3},{2,6},{3,1},{8,0},{9,11},{10,2},{11,9},{12,8},{13,15},... | collective-permute-start | bytes 626696 | tf_op jit(solution)/shard_map/ppermute | solution.py:188
  24.6 0.0 copy-done
  24.6 1.1 %first_scores.1 = (bf16[256,768]{1,0:T(8,128)(2,1)S(1)}, f32[256,128]{1,0:T(8,128)S(1)}, f32[256,128]{1,0:T(8,128)S(1)}, f32[256,768]{1,0:T(8,128)S(1)}) custom-call(bf16[136,768]{1,0:T(8,128)(2,1)S(1)} %copy-done, bf16[136,768]{1,0:T(8,128)(2,1)S(1)} %collective-permute-done.other_ref, bf16[136,768]{1,0:T(8,128)(2,1)S(1)} %collective-permute-done.1.refs_0_, ...), custom_call_target="tpu_custom_call" | custom-call | flops 30198988800 | bytes 2162688 | tf_op jit(solution)/shard_map/first_scores/pallas_call | solution.py:194
  25.8 1.4 %collective-permute-done.5.refs_0_ = bf16[136,768]{1,0:T(8,128)(2,1)S(1)} collective-permute-done((bf16[136,768]{1,0:T(8,128)(2,1)S(1)}, bf16[136,768]{1,0:T(8,128)(2,1)S(1)}, u32[]{:S(2)}, u32[]{:S(2)}) %collective-permute-start.5) | collective-permute-done | bytes 208928 | tf_op jit(solution)/shard_map/ppermute | solution.py:173
  27.2 0.0 collective-permute-done.4.refs_1_
  27.3 1.5 %collective-permute-start.7 = (bf16[136,768]{1,0:T(8,128)(2,1)S(1)}, bf16[136,768]{1,0:T(8,128)(2,1)S(1)}, u32[]{:S(2)}, u32[]{:S(2)}) collective-permute-start(bf16[136,768]{1,0:T(8,128)(2,1)S(1)} %broadcast_select_fusion), channel_id=1, source_target_pairs={{0,2},{1,9},{2,0},{3,11},{8,10},{9,13},{10,8},{11,15},{12,14},{13,... | collective-permute-start | bytes 626696 | tf_op jit(solution)/shard_map/ppermute | solution.py:188
  28.8 0.9 %more_scores.2 = (f32[256,128]{1,0:T(8,128)S(1)}, f32[256,768]{1,0:T(8,128)S(1)}) custom-call(bf16[256,768]{1,0:T(8,128)(2,1)S(1)} %get-tuple-element.22.unit_ref, f32[256,128]{1,0:T(8,128)S(1)} %get-tuple-element.23.side_ref, f32[256,128]{1,0:T(8,128)S(1)} %get-tuple-element.24.old_sums_ref, ...), custom_call_target="tpu_custom_call", output_to_operand_aliasing={{0}: (2, {}), {1}: (3, {})} | custom-call | flops 20132659200 | bytes 1966080 | tf_op jit(solution)/shard_map/more_scores/pallas_call | solution.py:208
  29.7 0.4 %collective-permute-done.6.refs_1_ = bf16[136,768]{1,0:T(8,128)(2,1)S(1)} collective-permute-done((bf16[136,768]{1,0:T(8,128)(2,1)S(1)}, bf16[136,768]{1,0:T(8,128)(2,1)S(1)}, u32[]{:S(2)}, u32[]{:S(2)}) %collective-permute-start.6) | collective-permute-done | bytes 208928 | tf_op jit(solution)/shard_map/ppermute | solution.py:188
  30.1 0.9 %more_scores.3 = (f32[256,128]{1,0:T(8,128)S(1)}, f32[256,768]{1,0:T(8,128)S(1)}) custom-call(bf16[256,768]{1,0:T(8,128)(2,1)S(1)} %get-tuple-element.22.unit_ref, f32[256,128]{1,0:T(8,128)S(1)} %get-tuple-element.23.side_ref, f32[256,128]{1,0:T(8,128)S(1)} %get-tuple-element.28.old_sums_ref, ...), custom_call_target="tpu_custom_call", output_to_operand_aliasing={{0}: (2, {}), {1}: (3, {})} | custom-call | flops 20132659200 | bytes 1966080 | tf_op jit(solution)/shard_map/more_scores/pallas_call | solution.py:208
  31.1 2.0 %collective-permute-done.7.refs_0_ = bf16[136,768]{1,0:T(8,128)(2,1)S(1)} collective-permute-done((bf16[136,768]{1,0:T(8,128)(2,1)S(1)}, bf16[136,768]{1,0:T(8,128)(2,1)S(1)}, u32[]{:S(2)}, u32[]{:S(2)}) %collective-permute-start.7) | collective-permute-done | bytes 208928 | tf_op jit(solution)/shard_map/ppermute | solution.py:188
  33.1 0.6 %final_scores.1 = (f32[128,128]{1,0:T(8,128)S(1)}, f32[128,768]{1,0:T(8,128)S(1)}, bf16[136,768]{1,0:T(8,128)(2,1)S(1)}) custom-call(bf16[256,768]{1,0:T(8,128)(2,1)S(1)} %get-tuple-element.22.unit_ref, f32[256,128]{1,0:T(8,128)S(1)} %get-tuple-element.23.side_ref, f32[256,128]{1,0:T(8,128)S(1)} %get-tuple-element.31.old_sums_ref, ...), custom_call_target="tpu_custom_call" | custom-call | flops 10066329600 | bytes 1769472 | tf_op jit(solution)/shard_map/final_scores/pallas_call | solution.py:218
  33.7 0.1 collective-permute-start.8
  33.8 1.4 %collective-permute-done.8.got_ref = bf16[136,768]{1,0:T(8,128)(2,1)S(1)} collective-permute-done((bf16[136,768]{1,0:T(8,128)(2,1)S(1)}, bf16[136,768]{1,0:T(8,128)(2,1)S(1)}, u32[]{:S(2)}, u32[]{:S(2)}) %collective-permute-start.8) | collective-permute-done | bytes 208928 | tf_op jit(solution)/shard_map/ppermute | solution.py:191
  35.3 1.0 %combine.1 = (f32[1,128]{1,0:T(1,128)}, f32[128,768]{1,0:T(8,128)}) custom-call(f32[128,128]{1,0:T(8,128)S(1)} %get-tuple-element.33.sums_ref, f32[128,768]{1,0:T(8,128)S(1)} %get-tuple-element.34.mixed_ref, bf16[136,768]{1,0:T(8,128)(2,1)S(1)} %collective-permute-done.8.got_ref), custom_call_target="tpu_custom_call" | custom-call | tf_op jit(solution)/shard_map/combine/pallas_call | solution.py:271
  (2 shorter events, 0.1 us)
Async XLA Ops:
  7.7 10.0 %collective-permute-start.2 = (bf16[136,768]{1,0:T(8,128)(2,1)}, bf16[136,768]{1,0:T(8,128)(2,1)S(1)}, u32[]{:S(2)}, u32[]{:S(2)}) collective-permute-start(bf16[136,768]{1,0:T(8,128)(2,1)} %pack.1.own_ref), channel_id=1, source_target_pairs={{0,8},{2,10},{8,12},{10,14},{12,4},{14,6},{4,0},{6,2},{1,9},{3,11}... | collective-permute-start | bytes 626696 | tf_op jit(solution)/shard_map/ppermute | solution.py:173
  11.8 6.8 %collective-permute-start.1 = (bf16[136,768]{1,0:T(8,128)(2,1)}, bf16[136,768]{1,0:T(8,128)(2,1)S(1)}, u32[]{:S(2)}, u32[]{:S(2)}) collective-permute-start(bf16[136,768]{1,0:T(8,128)(2,1)} %pack.1.own_ref), channel_id=1, source_target_pairs={{0,2},{2,0},{4,6},{6,4},{8,10},{10,8},{12,14},{14,12},{1,3},{3,1},... | collective-permute-start | bytes 626696 | tf_op jit(solution)/shard_map/ppermute | solution.py:176
  13.3 5.3 %collective-permute-start = (bf16[136,768]{1,0:T(8,128)(2,1)}, bf16[136,768]{1,0:T(8,128)(2,1)S(1)}, u32[]{:S(2)}, u32[]{:S(2)}) collective-permute-start(bf16[136,768]{1,0:T(8,128)(2,1)} %pack.1.own_ref), channel_id=1, source_target_pairs={{0,1},{1,0},{2,3},{3,2},{4,5},{5,4},{6,7},{7,6},{8,9},{9,8},{10,11... | collective-permute-start | bytes 626696 | tf_op jit(solution)/shard_map/ppermute | solution.py:191
  13.3 10.0 %collective-permute-start.3 = (bf16[136,768]{1,0:T(8,128)(2,1)}, bf16[136,768]{1,0:T(8,128)(2,1)S(1)}, u32[]{:S(2)}, u32[]{:S(2)}) collective-permute-start(bf16[136,768]{1,0:T(8,128)(2,1)} %pack.1.own_ref), channel_id=1, source_target_pairs={{0,4},{2,6},{8,0},{10,2},{12,8},{14,10},{4,12},{6,14},{1,5},{3,7},... | collective-permute-start | bytes 626696 | tf_op jit(solution)/shard_map/ppermute | solution.py:173
  13.3 11.3 %copy-start = (bf16[136,768]{1,0:T(8,128)(2,1)S(1)}, bf16[136,768]{1,0:T(8,128)(2,1)}, u32[]{:S(2)}) copy-start(bf16[136,768]{1,0:T(8,128)(2,1)} %pack.1.own_ref) | copy-start | bytes 626692
  18.7 8.6 %collective-permute-start.5 = (bf16[136,768]{1,0:T(8,128)(2,1)S(1)}, bf16[136,768]{1,0:T(8,128)(2,1)S(1)}, u32[]{:S(2)}, u32[]{:S(2)}) collective-permute-start(bf16[136,768]{1,0:T(8,128)(2,1)S(1)} %collective-permute-done.2.refs_0_), channel_id=1, source_target_pairs={{0,8},{2,10},{8,12},{10,14},{12,4},{14,6},{4,0},{6,2},{1,9},{3,11}... | collective-permute-start | bytes 626696 | tf_op jit(solution)/shard_map/ppermute | solution.py:173
  21.0 6.2 %collective-permute-start.4 = (bf16[136,768]{1,0:T(8,128)(2,1)S(1)}, bf16[136,768]{1,0:T(8,128)(2,1)S(1)}, u32[]{:S(2)}, u32[]{:S(2)}) collective-permute-start(bf16[136,768]{1,0:T(8,128)(2,1)S(1)} %collective-permute-done.2.refs_0_), channel_id=1, source_target_pairs={{0,2},{2,0},{4,6},{6,4},{8,10},{10,8},{12,14},{14,12},{1,3},{3,1},... | collective-permute-start | bytes 626696 | tf_op jit(solution)/shard_map/ppermute | solution.py:176
  23.4 6.8 %collective-permute-start.6 = (bf16[136,768]{1,0:T(8,128)(2,1)S(1)}, bf16[136,768]{1,0:T(8,128)(2,1)S(1)}, u32[]{:S(2)}, u32[]{:S(2)}) collective-permute-start(bf16[136,768]{1,0:T(8,128)(2,1)S(1)} %broadcast_select_fusion.1), channel_id=1, source_target_pairs={{0,4},{1,3},{2,6},{3,1},{8,0},{9,11},{10,2},{11,9},{12,8},{13,15},... | collective-permute-start | bytes 626696 | tf_op jit(solution)/shard_map/ppermute | solution.py:188
  27.3 5.9 %collective-permute-start.7 = (bf16[136,768]{1,0:T(8,128)(2,1)S(1)}, bf16[136,768]{1,0:T(8,128)(2,1)S(1)}, u32[]{:S(2)}, u32[]{:S(2)}) collective-permute-start(bf16[136,768]{1,0:T(8,128)(2,1)S(1)} %broadcast_select_fusion), channel_id=1, source_target_pairs={{0,2},{1,9},{2,0},{3,11},{8,10},{9,13},{10,8},{11,15},{12,14},{13,... | collective-permute-start | bytes 626696 | tf_op jit(solution)/shard_map/ppermute | solution.py:188
  33.7 1.5 %collective-permute-start.8 = (bf16[136,768]{1,0:T(8,128)(2,1)S(1)}, bf16[136,768]{1,0:T(8,128)(2,1)S(1)}, u32[]{:S(2)}, u32[]{:S(2)}) collective-permute-start(bf16[136,768]{1,0:T(8,128)(2,1)S(1)} %get-tuple-element.35), channel_id=1, source_target_pairs={{0,1},{1,0},{2,3},{3,2},{4,5},{5,4},{6,7},{7,6},{8,9},{9,8},{10,11... | collective-permute-start | bytes 626696 | tf_op jit(solution)/shard_map/ppermute | solution.py:191

commit v11 on v8

--- a/solution.py
+++ b/solution.py
@@ -224,16 +224,14 @@
     other = swap(own)
     if rounds == 4:
         ahead = along(own, -1)
-        other, beside, moved = lax.optimization_barrier((other, beside, moved))
+        moved, beside, other = lax.optimization_barrier((moved, beside, other))
         opposite = along(moved, 1)
         moved_beside = across(moved)
         ahead_beside = two_ways(beside, -1, ahead)
-        state = first(own, other, beside, ahead)
-        unit, side = state[:2]
-        moved_beside, opposite = lax.optimization_barrier((moved_beside, opposite))
+        other, opposite, moved_beside = lax.optimization_barrier((other, opposite, moved_beside))
         last = [two_ways(moved_beside, 1, opposite)]
-        sums, mixed = more(*state, moved, moved_beside)
-        sums, mixed = more(unit, side, sums, mixed, opposite, ahead_beside)
+        unit, side, sums, mixed = first(own, other, beside, ahead, ahead_beside)
+        sums, mixed = more(unit, side, sums, mixed, moved, moved_beside, opposite)
     else:
         unit, side, sums, mixed = first(own, other, beside)
 

time: 30.7 us -> 30.7 us (level)
  Pallas kernels: 4.55 us -> 3.8 us
  waiting for transfers between devices: 11.2 us -> 11.9 us
    ppermute x3, waiting for transfers between devices: 6.33 us -> 7.48 us  [along(): return lax.ppermute(array, 'shard', pairs)]
    pallas_call x2 -> x1, Pallas kernels: 1.81 us -> 1.06 us  [more(): pl.pallas_call(more_kernel, out_shape=[shape(queries, 128), shape(queries...]
    ppermute x2, waiting for transfers between devices: 2.36 us -> 1.96 us  [two_ways(): return lax.ppermute(source, ('shard', 'owner'), pairs)]
  transfers between devices with their start and end apart: 9 -> 9, of which waited for: 7 -> 7; matrix products, arithmetic and copies ran while one was open for 0% -> 0% of each run, Pallas kernels for 10% -> 7%
where the time goes in v11:
time: 30.7 us; the launch traced here: 30.5 us
  starting transfers between devices  12.4 us (40%)
  waiting for transfers between devices  11.9 us (39%)
  Pallas kernels  3.8 us (12%)
  local copies, waits for them, and re-layouts  1.58 us (5%)
  between operations  0.69 us (2%)
    ppermute x3, waiting for transfers between devices, along(): return lax.ppermute(array, 'shard', pairs)  7.48 us
    ppermute x3, starting transfers between devices, along(): return lax.ppermute(array, 'shard', pairs)  6.42 us
    ppermute x2, starting transfers between devices, across(): return lax.ppermute(array, 'shard', [(at, at ^ 1) for at in range(shards)])  3 us
    ppermute x2, starting transfers between devices, two_ways(): return lax.ppermute(source, ('shard', 'owner'), pairs)  2.95 us
    ppermute x2, waiting for transfers between devices, two_ways(): return lax.ppermute(source, ('shard', 'owner'), pairs)  1.96 us
    unnamed x6, local copies, waits for them, and re-layouts  1.58 us
    ppermute x2, waiting for transfers between devices, swap(): lax.ppermute(array, 'owner', [(at, lanes - 1 - at) for at in range(lanes)])  1.45 us
    pallas_call x1, Pallas kernels, first(): pl.pallas_call(first_kernel, out_shape=[shape(queries, width, dtype=bf16)...  1.14 us
  transfers between devices with their start and end apart: 9, of which 7 were waited for; matrix products, arithmetic and copies ran while one was open for 0% of the time, Pallas kernels for 7%

profile of v11, /device:TPU:0, one launch (start us, length us, event | category | flops | bytes accessed | tf_op | source)
XLA Modules:
  0.0 30.5 jit_solution(7634794421844388064)
XLA Ops:
  0.6 0.0 copy-start.1
  0.6 0.0 copy-start.2
  0.6 0.6 %copy-done.1 = s32[128,1]{0,1:T(1,128)S(1)} copy-done((s32[128,1]{0,1:T(1,128)S(1)}, s32[128,1]{0,1:T(1,128)}, u32[]{:S(2)}) %copy-start.1) | copy-done | bytes 536
  1.3 0.0 copy-done.2
  1.3 0.0 copy-start
  1.3 0.9 %copy-done = bf16[128,768]{1,0:T(8,128)(2,1)S(1)} copy-done((bf16[128,768]{1,0:T(8,128)(2,1)S(1)}, bf16[128,768]{1,0:T(8,128)(2,1)}, u32[]{:S(2)}) %copy-start) | copy-done | bytes 196632
  2.3 4.1 %collective-permute-start = (bf16[136,768]{1,0:T(8,128)(2,1)S(1)}, bf16[136,768]{1,0:T(8,128)(2,1)S(1)}, u32[]{:S(2)}, u32[]{:S(2)}) collective-permute-start(bf16[136,768]{1,0:T(8,128)(2,1)S(1)} %pack.1.own_ref), channel_id=1, source_target_pairs={{0,8},{2,10},{8,12},{10,14},{12,4},{14,6},{4,0},{6,2},{1,9},{3,11}... | collective-permute-start | bytes 626696 | tf_op jit(solution)/shard_map/ppermute | solution.py:161
  6.3 1.5 %collective-permute-start.1 = (bf16[136,768]{1,0:T(8,128)(2,1)S(1)}, bf16[136,768]{1,0:T(8,128)(2,1)S(1)}, u32[]{:S(2)}, u32[]{:S(2)}) collective-permute-start(bf16[136,768]{1,0:T(8,128)(2,1)S(1)} %pack.1.own_ref), channel_id=1, source_target_pairs={{0,2},{2,0},{4,6},{6,4},{8,10},{10,8},{12,14},{14,12},{1,3},{3,1},... | collective-permute-start | bytes 626696 | tf_op jit(solution)/shard_map/ppermute | solution.py:164
  7.8 0.0 collective-permute-start.2
  7.8 0.0 collective-permute-start.5
  7.8 4.1 %collective-permute-done.refs_0_ = bf16[136,768]{1,0:T(8,128)(2,1)S(1)} collective-permute-done((bf16[136,768]{1,0:T(8,128)(2,1)S(1)}, bf16[136,768]{1,0:T(8,128)(2,1)S(1)}, u32[]{:S(2)}, u32[]{:S(2)}) %collective-permute-start) | collective-permute-done | bytes 208928 | tf_op jit(solution)/shard_map/ppermute | solution.py:161
  11.9 1.1 %collective-permute-done.1.refs_0_ = bf16[136,768]{1,0:T(8,128)(2,1)S(1)} collective-permute-done((bf16[136,768]{1,0:T(8,128)(2,1)S(1)}, bf16[136,768]{1,0:T(8,128)(2,1)S(1)}, u32[]{:S(2)}, u32[]{:S(2)}) %collective-permute-start.1) | collective-permute-done | bytes 208928 | tf_op jit(solution)/shard_map/ppermute | solution.py:164
  13.0 0.0 collective-permute-done.2.other_ref
  13.0 2.3 %collective-permute-start.3 = (bf16[136,768]{1,0:T(8,128)(2,1)S(1)}, bf16[136,768]{1,0:T(8,128)(2,1)S(1)}, u32[]{:S(2)}, u32[]{:S(2)}) collective-permute-start(bf16[136,768]{1,0:T(8,128)(2,1)S(1)} %collective-permute-done.refs_0_), channel_id=1, source_target_pairs={{0,8},{2,10},{8,12},{10,14},{12,4},{14,6},{4,0},{6,2},{1,9},{3,11}... | collective-permute-start | bytes 626696 | tf_op jit(solution)/shard_map/ppermute | solution.py:161
  15.3 1.5 %collective-permute-start.4 = (bf16[136,768]{1,0:T(8,128)(2,1)S(1)}, bf16[136,768]{1,0:T(8,128)(2,1)S(1)}, u32[]{:S(2)}, u32[]{:S(2)}) collective-permute-start(bf16[136,768]{1,0:T(8,128)(2,1)S(1)} %collective-permute-done.refs_0_), channel_id=1, source_target_pairs={{0,2},{2,0},{4,6},{6,4},{8,10},{10,8},{12,14},{14,12},{1,3},{3,1},... | collective-permute-start | bytes 626696 | tf_op jit(solution)/shard_map/ppermute | solution.py:164
  16.8 0.8 %collective-permute-done.5.refs_1_ = bf16[136,768]{1,0:T(8,128)(2,1)S(1)} collective-permute-done((bf16[136,768]{1,0:T(8,128)(2,1)S(1)}, bf16[136,768]{1,0:T(8,128)(2,1)S(1)}, u32[]{:S(2)}, u32[]{:S(2)}) %collective-permute-start.5) | collective-permute-done | bytes 208928 | tf_op jit(solution)/shard_map/ppermute | solution.py:161
  17.7 1.3 %collective-permute-start.6 = (bf16[136,768]{1,0:T(8,128)(2,1)S(1)}, bf16[136,768]{1,0:T(8,128)(2,1)S(1)}, u32[]{:S(2)}, u32[]{:S(2)}) collective-permute-start(bf16[136,768]{1,0:T(8,128)(2,1)S(1)} %broadcast_select_fusion.1), channel_id=1, source_target_pairs={{0,4},{1,3},{2,6},{3,1},{8,0},{9,11},{10,2},{11,9},{12,8},{13,15},... | collective-permute-start | bytes 626696 | tf_op jit(solution)/shard_map/ppermute | solution.py:174
  18.9 2.6 %collective-permute-done.3.refs_2_ = bf16[136,768]{1,0:T(8,128)(2,1)S(1)} collective-permute-done((bf16[136,768]{1,0:T(8,128)(2,1)S(1)}, bf16[136,768]{1,0:T(8,128)(2,1)S(1)}, u32[]{:S(2)}, u32[]{:S(2)}) %collective-permute-start.3) | collective-permute-done | bytes 208928 | tf_op jit(solution)/shard_map/ppermute | solution.py:161
  21.5 0.0 collective-permute-done.4.refs_1_
  21.6 1.7 %collective-permute-start.7 = (bf16[136,768]{1,0:T(8,128)(2,1)S(1)}, bf16[136,768]{1,0:T(8,128)(2,1)S(1)}, u32[]{:S(2)}, u32[]{:S(2)}) collective-permute-start(bf16[136,768]{1,0:T(8,128)(2,1)S(1)} %broadcast_select_fusion), channel_id=1, source_target_pairs={{0,8},{1,3},{2,10},{3,1},{8,12},{9,11},{10,14},{11,9},{12,4},{13,1... | collective-permute-start | bytes 626696 | tf_op jit(solution)/shard_map/ppermute | solution.py:174
  23.2 1.2 %collective-permute-done.6.refs_2_ = bf16[136,768]{1,0:T(8,128)(2,1)S(1)} collective-permute-done((bf16[136,768]{1,0:T(8,128)(2,1)S(1)}, bf16[136,768]{1,0:T(8,128)(2,1)S(1)}, u32[]{:S(2)}, u32[]{:S(2)}) %collective-permute-start.6) | collective-permute-done | bytes 208928 | tf_op jit(solution)/shard_map/ppermute | solution.py:174
  24.4 1.1 %first_scores.1 = (bf16[256,768]{1,0:T(8,128)(2,1)S(1)}, f32[256,128]{1,0:T(8,128)S(1)}, f32[256,128]{1,0:T(8,128)S(1)}, f32[256,768]{1,0:T(8,128)S(1)}) custom-call(bf16[136,768]{1,0:T(8,128)(2,1)S(1)} %pack.1.own_ref, bf16[136,768]{1,0:T(8,128)(2,1)S(1)} %collective-permute-done.2.other_ref, bf16[136,768]{1,0:T(8,128)(2,1)S(1)} %collective-permute-done.1.refs_0_, ...), custom_call_target="tpu_custom_call" | custom-call | flops 40265318400 | bytes 2359296 | tf_op jit(solution)/shard_map/first_scores/pallas_call | solution.py:180
  25.6 1.1 %more_scores.1 = (f32[256,128]{1,0:T(8,128)S(1)}, f32[256,768]{1,0:T(8,128)S(1)}) custom-call(bf16[256,768]{1,0:T(8,128)(2,1)S(1)} %get-tuple-element.23.unit_ref, f32[256,128]{1,0:T(8,128)S(1)} %get-tuple-element.24.side_ref, f32[256,128]{1,0:T(8,128)S(1)} %get-tuple-element.25.old_sums_ref, ...), custom_call_target="tpu_custom_call", output_to_operand_aliasing={{0}: (2, {}), {1}: (3, {})} | custom-call | flops 30198988800 | bytes 2162688 | tf_op jit(solution)/shard_map/more_scores/pallas_call | solution.py:194
  26.6 0.8 %collective-permute-done.7.refs_0_ = bf16[136,768]{1,0:T(8,128)(2,1)S(1)} collective-permute-done((bf16[136,768]{1,0:T(8,128)(2,1)S(1)}, bf16[136,768]{1,0:T(8,128)(2,1)S(1)}, u32[]{:S(2)}, u32[]{:S(2)}) %collective-permute-start.7) | collective-permute-done | bytes 208928 | tf_op jit(solution)/shard_map/ppermute | solution.py:174
  27.4 0.6 %final_scores.1 = (f32[128,128]{1,0:T(8,128)S(1)}, f32[128,768]{1,0:T(8,128)S(1)}, bf16[136,768]{1,0:T(8,128)(2,1)S(1)}) custom-call(bf16[256,768]{1,0:T(8,128)(2,1)S(1)} %get-tuple-element.23.unit_ref, f32[256,128]{1,0:T(8,128)S(1)} %get-tuple-element.24.side_ref, f32[256,128]{1,0:T(8,128)S(1)} %get-tuple-element.29.old_sums_ref, ...), custom_call_target="tpu_custom_call" | custom-call | flops 10066329600 | bytes 1769472 | tf_op jit(solution)/shard_map/final_scores/pallas_call | solution.py:204
  28.0 0.1 collective-permute-start.8
  28.1 1.4 %collective-permute-done.8.got_ref = bf16[136,768]{1,0:T(8,128)(2,1)S(1)} collective-permute-done((bf16[136,768]{1,0:T(8,128)(2,1)S(1)}, bf16[136,768]{1,0:T(8,128)(2,1)S(1)}, u32[]{:S(2)}, u32[]{:S(2)}) %collective-permute-start.8) | collective-permute-done | bytes 208928 | tf_op jit(solution)/shard_map/ppermute | solution.py:177
  29.6 1.0 %combine.1 = (f32[1,128]{1,0:T(1,128)}, f32[128,768]{1,0:T(8,128)}) custom-call(f32[128,128]{1,0:T(8,128)S(1)} %get-tuple-element.31.sums_ref, f32[128,768]{1,0:T(8,128)S(1)} %get-tuple-element.32.mixed_ref, bf16[136,768]{1,0:T(8,128)(2,1)S(1)} %collective-permute-done.8.got_ref), custom_call_target="tpu_custom_call" | custom-call | tf_op jit(solution)/shard_map/combine/pallas_call | solution.py:247
  (3 shorter events, 0.1 us)
Async XLA Ops:
  0.6 0.7 %copy-start.1 = (s32[128,1]{0,1:T(1,128)S(1)}, s32[128,1]{0,1:T(1,128)}, u32[]{:S(2)}) copy-start(s32[128,1]{0,1:T(1,128)} %param.4) | copy-start | bytes 1540
  0.6 0.7 %copy-start.2 = (s32[128]{0:T(128)S(1)}, s32[128]{0:T(128)}, u32[]{:S(2)}) copy-start(s32[128]{0:T(128)} %param.5) | copy-start | bytes 1540
  1.3 0.9 %copy-start = (bf16[128,768]{1,0:T(8,128)(2,1)S(1)}, bf16[128,768]{1,0:T(8,128)(2,1)}, u32[]{:S(2)}) copy-start(bf16[128,768]{1,0:T(8,128)(2,1)} %rows_ref.1) | copy-start | bytes 589828
  2.3 9.7 %collective-permute-start = (bf16[136,768]{1,0:T(8,128)(2,1)S(1)}, bf16[136,768]{1,0:T(8,128)(2,1)S(1)}, u32[]{:S(2)}, u32[]{:S(2)}) collective-permute-start(bf16[136,768]{1,0:T(8,128)(2,1)S(1)} %pack.1.own_ref), channel_id=1, source_target_pairs={{0,8},{2,10},{8,12},{10,14},{12,4},{14,6},{4,0},{6,2},{1,9},{3,11}... | collective-permute-start | bytes 626696 | tf_op jit(solution)/shard_map/ppermute | solution.py:161
  6.3 6.6 %collective-permute-start.1 = (bf16[136,768]{1,0:T(8,128)(2,1)S(1)}, bf16[136,768]{1,0:T(8,128)(2,1)S(1)}, u32[]{:S(2)}, u32[]{:S(2)}) collective-permute-start(bf16[136,768]{1,0:T(8,128)(2,1)S(1)} %pack.1.own_ref), channel_id=1, source_target_pairs={{0,2},{2,0},{4,6},{6,4},{8,10},{10,8},{12,14},{14,12},{1,3},{3,1},... | collective-permute-start | bytes 626696 | tf_op jit(solution)/shard_map/ppermute | solution.py:164
  7.8 5.1 %collective-permute-start.2 = (bf16[136,768]{1,0:T(8,128)(2,1)S(1)}, bf16[136,768]{1,0:T(8,128)(2,1)S(1)}, u32[]{:S(2)}, u32[]{:S(2)}) collective-permute-start(bf16[136,768]{1,0:T(8,128)(2,1)S(1)} %pack.1.own_ref), channel_id=1, source_target_pairs={{0,1},{1,0},{2,3},{3,2},{4,5},{5,4},{6,7},{7,6},{8,9},{9,8},{10,11... | collective-permute-start | bytes 626696 | tf_op jit(solution)/shard_map/ppermute | solution.py:177
  7.8 9.8 %collective-permute-start.5 = (bf16[136,768]{1,0:T(8,128)(2,1)S(1)}, bf16[136,768]{1,0:T(8,128)(2,1)S(1)}, u32[]{:S(2)}, u32[]{:S(2)}) collective-permute-start(bf16[136,768]{1,0:T(8,128)(2,1)S(1)} %pack.1.own_ref), channel_id=1, source_target_pairs={{0,4},{2,6},{8,0},{10,2},{12,8},{14,10},{4,12},{6,14},{1,5},{3,7},... | collective-permute-start | bytes 626696 | tf_op jit(solution)/shard_map/ppermute | solution.py:161
  13.0 8.6 %collective-permute-start.3 = (bf16[136,768]{1,0:T(8,128)(2,1)S(1)}, bf16[136,768]{1,0:T(8,128)(2,1)S(1)}, u32[]{:S(2)}, u32[]{:S(2)}) collective-permute-start(bf16[136,768]{1,0:T(8,128)(2,1)S(1)} %collective-permute-done.refs_0_), channel_id=1, source_target_pairs={{0,8},{2,10},{8,12},{10,14},{12,4},{14,6},{4,0},{6,2},{1,9},{3,11}... | collective-permute-start | bytes 626696 | tf_op jit(solution)/shard_map/ppermute | solution.py:161
  15.3 6.2 %collective-permute-start.4 = (bf16[136,768]{1,0:T(8,128)(2,1)S(1)}, bf16[136,768]{1,0:T(8,128)(2,1)S(1)}, u32[]{:S(2)}, u32[]{:S(2)}) collective-permute-start(bf16[136,768]{1,0:T(8,128)(2,1)S(1)} %collective-permute-done.refs_0_), channel_id=1, source_target_pairs={{0,2},{2,0},{4,6},{6,4},{8,10},{10,8},{12,14},{14,12},{1,3},{3,1},... | collective-permute-start | bytes 626696 | tf_op jit(solution)/shard_map/ppermute | solution.py:164
  17.7 6.8 %collective-permute-start.6 = (bf16[136,768]{1,0:T(8,128)(2,1)S(1)}, bf16[136,768]{1,0:T(8,128)(2,1)S(1)}, u32[]{:S(2)}, u32[]{:S(2)}) collective-permute-start(bf16[136,768]{1,0:T(8,128)(2,1)S(1)} %broadcast_select_fusion.1), channel_id=1, source_target_pairs={{0,4},{1,3},{2,6},{3,1},{8,0},{9,11},{10,2},{11,9},{12,8},{13,15},... | collective-permute-start | bytes 626696 | tf_op jit(solution)/shard_map/ppermute | solution.py:174
  21.6 5.9 %collective-permute-start.7 = (bf16[136,768]{1,0:T(8,128)(2,1)S(1)}, bf16[136,768]{1,0:T(8,128)(2,1)S(1)}, u32[]{:S(2)}, u32[]{:S(2)}) collective-permute-start(bf16[136,768]{1,0:T(8,128)(2,1)S(1)} %broadcast_select_fusion), channel_id=1, source_target_pairs={{0,8},{1,3},{2,10},{3,1},{8,12},{9,11},{10,14},{11,9},{12,4},{13,1... | collective-permute-start | bytes 626696 | tf_op jit(solution)/shard_map/ppermute | solution.py:174
  28.0 1.5 %collective-permute-start.8 = (bf16[136,768]{1,0:T(8,128)(2,1)S(1)}, bf16[136,768]{1,0:T(8,128)(2,1)S(1)}, u32[]{:S(2)}, u32[]{:S(2)}) collective-permute-start(bf16[136,768]{1,0:T(8,128)(2,1)S(1)} %get-tuple-element.33), channel_id=1, source_target_pairs={{0,1},{1,0},{2,3},{3,2},{4,5},{5,4},{6,7},{7,6},{8,9},{9,8},{10,11... | collective-permute-start | bytes 626696 | tf_op jit(solution)/shard_map/ppermute | solution.py:177

commit v12 on v11

--- a/solution.py
+++ b/solution.py
@@ -5,6 +5,7 @@
 from jax.experimental.pallas import tpu as pltpu
 from jax.sharding import PartitionSpec as P
 
+SUB, LANE = 8, 128
 EXTRA = 8
 VMEM = 24 * 1024 * 1024
 
@@ -35,37 +36,42 @@
     return high, (value - high.astype(jnp.float32)).astype(jnp.bfloat16)
 
 
-def pack_kernel(rows_ref, label_ref, rank_ref, packed_ref):
-    count, width = rows_ref.shape
-    packed_ref[:count, :] = rows_ref[...]
+def pack_kernel(tiles_ref, label_ref, rank_ref, packed_ref):
+    many = tiles_ref.shape[0]
+    packed_ref[:many] = tiles_ref[...]
     rank = rank_ref[...]
     high = lax.shift_right_logical(rank, 8)
     low = rank - lax.shift_left(high, 8)
-    pieces = [piece.astype(jnp.float32) for piece in (label_ref[...], high, low)]
-    pieces.append(jnp.zeros((1, width - 3 * count), jnp.float32))
-    line = jnp.concatenate(pieces, axis=1)
-    packed_ref[count:, :] = jnp.broadcast_to(line, (EXTRA, width)).astype(jnp.bfloat16)
+    lines = [line.astype(jnp.float32) for line in (label_ref[...], high, low)]
+    lines.append(jnp.zeros((SUB - len(lines), LANE), jnp.float32))
+    packed_ref[many] = jnp.concatenate(lines, axis=0).astype(jnp.bfloat16)
 
 
 def labels_and_ranks(block):
-    count = block.shape[0] - EXTRA
-    line = block[count:, :].astype(jnp.float32)[:1]
-    label, high, low = (line[:, at * count : (at + 1) * count] for at in range(3))
-    return label, high * 256.0 + low
-
-
-def rows_of(blocks):
-    return jnp.concatenate([block[: block.shape[0] - EXTRA, :] for block in blocks], axis=0)
+    tile = block[block.shape[0] - 1].astype(jnp.float32)
+    return tile[0:1], tile[1:2] * 256.0 + tile[2:3]
+
+
+def rows_of(blocks, width):
+    across = width // LANE
+    wide = []
+    for block in blocks:
+        tiles = block[: block.shape[0] - 1].astype(jnp.float32)
+        tiles = tiles.reshape(-1, across, SUB, LANE)
+        pieces = [tiles[:, at].reshape(-1, LANE) for at in range(across)]
+        wide.append(jnp.concatenate(pieces, axis=1))
+    return jnp.concatenate(wide, axis=0)
 
 
 def score(unit, side, blocks):
     own_label, own_rank = side[:, 0:1], side[:, 1:2]
-    keys = rows_of(blocks)
+    wide = rows_of(blocks, unit.shape[1])
+    keys = wide.astype(jnp.bfloat16)
     sides = [labels_and_ranks(block) for block in blocks]
     label = jnp.concatenate([item[0] for item in sides], axis=1)
     rank = jnp.concatenate([item[1] for item in sides], axis=1)
     cosine = lax.dot_general(
-        unit, make_unit(keys), (((1,), (1,)), ((), ())), preferred_element_type=jnp.float32
+        unit, make_unit(wide), (((1,), (1,)), ((), ())), preferred_element_type=jnp.float32
     )
     weight = 1.0 / (1.0 + jnp.exp(-40.0 * (cosine - 0.05)))
     near = jnp.where((label == own_label) & (rank != own_rank), weight, 0.0)
@@ -77,10 +83,10 @@
 
 def first_kernel(own_ref, other_ref, *refs):
     blocks, (unit_ref, side_ref, sums_ref, mixed_ref) = refs[:-4], refs[-4:]
-    count = own_ref.shape[0] - EXTRA
+    count = own_ref.shape[0] // (unit_ref.shape[1] // LANE) * SUB
     side_ref[...] = jnp.zeros_like(side_ref)
     sums_ref[...] = jnp.zeros_like(sums_ref)
-    unit_ref[...] = make_unit(rows_of([own_ref, other_ref]))
+    unit_ref[...] = make_unit(rows_of([own_ref, other_ref], unit_ref.shape[1]))
     for at, ref in enumerate((own_ref, other_ref)):
         here = slice(at * count, (at + 1) * count)
         label, rank = labels_and_ranks(ref)
@@ -139,7 +145,7 @@
 
 def local(embeddings, cluster_id, priority):
     count, width = embeddings.shape
-    height = count + EXTRA
+    tiles = count // SUB * (width // LANE)
     shards = lax.axis_size("shard")
     lanes = lax.axis_size("owner")
     rounds = shards // 2
@@ -206,19 +212,20 @@
             out_shape=[
                 shape(count, 128),
                 shape(count, width),
-                shape(height, width, dtype=bf16),
+                shape(count + EXTRA, width, dtype=bf16),
             ],
             cost_estimate=cost(queries, len(blocks) * count, width),
             compiler_params=params,
             name="final_scores",
         )(unit, side, sums, mixed, *blocks)
 
+    pieces = embeddings.reshape(count // SUB, SUB, width // LANE, LANE).transpose(0, 2, 1, 3)
     own = pl.pallas_call(
         pack_kernel,
-        out_shape=shape(height, width, dtype=bf16),
+        out_shape=shape(tiles + 1, SUB, LANE, dtype=bf16),
         compiler_params=params,
         name="pack",
-    )(embeddings, cluster_id.reshape(1, count), priority.reshape(1, count))
+    )(pieces.reshape(tiles, SUB, LANE), cluster_id.reshape(1, count), priority.reshape(1, count))
 
     moved, beside = along(own, 1), across(own)
     other = swap(own)

time: 30.7 us -> 30.4 us (level)
    ppermute x3, waiting for transfers between devices: 7.48 us -> 6.58 us  [along(): return lax.ppermute(array, 'shard', pairs)]
    ppermute x2, waiting for transfers between devices: 1.06 us -> 1.48 us  [across(): return lax.ppermute(array, 'shard', [(at, at ^ 1) for at in range(shards)])]
  transfers between devices with their start and end apart: 9 -> 9, of which waited for: 7 -> 8; matrix products, arithmetic and copies ran while one was open for 0% -> 0% of each run, Pallas kernels for 7% -> 7%
where the time goes in v12:
time: 30.4 us; the launch traced here: 30.2 us
  starting transfers between devices  12.2 us (40%)
  waiting for transfers between devices  11.7 us (38%)
  Pallas kernels  3.84 us (13%)
  local copies, waits for them, and re-layouts  1.58 us (5%)
  between operations  0.69 us (2%)
    ppermute x3, waiting for transfers between devices, along(): return lax.ppermute(array, 'shard', pairs)  6.58 us
    ppermute x3, starting transfers between devices, along(): return lax.ppermute(array, 'shard', pairs)  6.42 us
    ppermute x2, starting transfers between devices, across(): return lax.ppermute(array, 'shard', [(at, at ^ 1) for at in range(shards)])  2.98 us
    ppermute x2, starting transfers between devices, two_ways(): return lax.ppermute(source, ('shard', 'owner'), pairs)  2.74 us
    ppermute x2, waiting for transfers between devices, two_ways(): return lax.ppermute(source, ('shard', 'owner'), pairs)  2.24 us
    unnamed x6, local copies, waits for them, and re-layouts  1.58 us
    ppermute x2, waiting for transfers between devices, across(): return lax.ppermute(array, 'shard', [(at, at ^ 1) for at in range(shards)])  1.48 us
    ppermute x2, waiting for transfers between devices, swap(): lax.ppermute(array, 'owner', [(at, lanes - 1 - at) for at in range(lanes)])  1.45 us
  transfers between devices with their start and end apart: 9, of which 8 were waited for; matrix products, arithmetic and copies ran while one was open for 0% of the time, Pallas kernels for 7%

profile of v12, /device:TPU:0, one launch (start us, length us, event | category | flops | bytes accessed | tf_op | source)
XLA Modules:
  0.0 30.2 jit_solution(4118524020373106054)
XLA Ops:
  0.6 0.0 copy-start.1
  0.6 0.0 copy-start.2
  0.6 0.6 %copy-done.1 = s32[128,1]{0,1:T(1,128)S(1)} copy-done((s32[128,1]{0,1:T(1,128)S(1)}, s32[128,1]{0,1:T(1,128)}, u32[]{:S(2)}) %copy-start.1) | copy-done | bytes 536
  1.3 0.0 copy-done.2
  1.3 0.0 copy-start
  1.3 0.9 %copy-done = bf16[128,768]{1,0:T(8,128)(2,1)S(1)} copy-done((bf16[128,768]{1,0:T(8,128)(2,1)S(1)}, bf16[128,768]{1,0:T(8,128)(2,1)}, u32[]{:S(2)}) %copy-start) | copy-done | bytes 196632
  2.3 4.1 %collective-permute-start = (bf16[97,8,128]{2,1,0:T(8,128)(2,1)S(1)}, bf16[97,8,128]{2,1,0:T(8,128)(2,1)S(1)}, u32[]{:S(2)}, u32[]{:S(2)}) collective-permute-start(bf16[97,8,128]{2,1,0:T(8,128)(2,1)S(1)} %pack.1.own_ref), channel_id=1, source_target_pairs={{0,8},{2,10},{8,12},{10,14},{12,4},{14,6},{4,0},{6,2},{1,9},{3,11}... | collective-permute-start | bytes 595976 | tf_op jit(solution)/shard_map/ppermute | solution.py:167
  6.3 1.5 %collective-permute-start.1 = (bf16[97,8,128]{2,1,0:T(8,128)(2,1)S(1)}, bf16[97,8,128]{2,1,0:T(8,128)(2,1)S(1)}, u32[]{:S(2)}, u32[]{:S(2)}) collective-permute-start(bf16[97,8,128]{2,1,0:T(8,128)(2,1)S(1)} %pack.1.own_ref), channel_id=1, source_target_pairs={{0,2},{2,0},{4,6},{6,4},{8,10},{10,8},{12,14},{14,12},{1,3},{3,1},... | collective-permute-start | bytes 595976 | tf_op jit(solution)/shard_map/ppermute | solution.py:170
  7.8 0.0 collective-permute-start.2
  7.8 0.0 collective-permute-start.5
  7.8 3.9 %collective-permute-done.refs_0_ = bf16[97,8,128]{2,1,0:T(8,128)(2,1)S(1)} collective-permute-done((bf16[97,8,128]{2,1,0:T(8,128)(2,1)S(1)}, bf16[97,8,128]{2,1,0:T(8,128)(2,1)S(1)}, u32[]{:S(2)}, u32[]{:S(2)}) %collective-permute-start) | collective-permute-done | bytes 198688 | tf_op jit(solution)/shard_map/ppermute | solution.py:167
  11.7 1.1 %collective-permute-done.1.refs_0_ = bf16[97,8,128]{2,1,0:T(8,128)(2,1)S(1)} collective-permute-done((bf16[97,8,128]{2,1,0:T(8,128)(2,1)S(1)}, bf16[97,8,128]{2,1,0:T(8,128)(2,1)S(1)}, u32[]{:S(2)}, u32[]{:S(2)}) %collective-permute-start.1) | collective-permute-done | bytes 198688 | tf_op jit(solution)/shard_map/ppermute | solution.py:170
  12.7 0.0 collective-permute-done.2.other_ref
  12.8 2.3 %collective-permute-start.3 = (bf16[97,8,128]{2,1,0:T(8,128)(2,1)S(1)}, bf16[97,8,128]{2,1,0:T(8,128)(2,1)S(1)}, u32[]{:S(2)}, u32[]{:S(2)}) collective-permute-start(bf16[97,8,128]{2,1,0:T(8,128)(2,1)S(1)} %collective-permute-done.refs_0_), channel_id=1, source_target_pairs={{0,8},{2,10},{8,12},{10,14},{12,4},{14,6},{4,0},{6,2},{1,9},{3,11}... | collective-permute-start | bytes 595976 | tf_op jit(solution)/shard_map/ppermute | solution.py:167
  15.1 1.5 %collective-permute-start.4 = (bf16[97,8,128]{2,1,0:T(8,128)(2,1)S(1)}, bf16[97,8,128]{2,1,0:T(8,128)(2,1)S(1)}, u32[]{:S(2)}, u32[]{:S(2)}) collective-permute-start(bf16[97,8,128]{2,1,0:T(8,128)(2,1)S(1)} %collective-permute-done.refs_0_), channel_id=1, source_target_pairs={{0,2},{2,0},{4,6},{6,4},{8,10},{10,8},{12,14},{14,12},{1,3},{3,1},... | collective-permute-start | bytes 595976 | tf_op jit(solution)/shard_map/ppermute | solution.py:170
  16.6 0.4 %collective-permute-done.5.refs_1_ = bf16[97,8,128]{2,1,0:T(8,128)(2,1)S(1)} collective-permute-done((bf16[97,8,128]{2,1,0:T(8,128)(2,1)S(1)}, bf16[97,8,128]{2,1,0:T(8,128)(2,1)S(1)}, u32[]{:S(2)}, u32[]{:S(2)}) %collective-permute-start.5) | collective-permute-done | bytes 198688 | tf_op jit(solution)/shard_map/ppermute | solution.py:167
  17.0 0.1 broadcast_select_fusion.1
  17.1 1.5 %collective-permute-start.6 = (bf16[97,8,128]{2,1,0:T(8,128)(2,1)S(1)}, bf16[97,8,128]{2,1,0:T(8,128)(2,1)S(1)}, u32[]{:S(2)}, u32[]{:S(2)}) collective-permute-start(bf16[97,8,128]{2,1,0:T(8,128)(2,1)S(1)} %broadcast_select_fusion.1), channel_id=1, source_target_pairs={{0,4},{1,3},{2,6},{3,1},{8,0},{9,11},{10,2},{11,9},{12,8},{13,15},... | collective-permute-start | bytes 595976 | tf_op jit(solution)/shard_map/ppermute | solution.py:180
  18.5 2.3 %collective-permute-done.3.refs_2_ = bf16[97,8,128]{2,1,0:T(8,128)(2,1)S(1)} collective-permute-done((bf16[97,8,128]{2,1,0:T(8,128)(2,1)S(1)}, bf16[97,8,128]{2,1,0:T(8,128)(2,1)S(1)}, u32[]{:S(2)}, u32[]{:S(2)}) %collective-permute-start.3) | collective-permute-done | bytes 198688 | tf_op jit(solution)/shard_map/ppermute | solution.py:167
  20.9 0.4 %collective-permute-done.4.refs_1_ = bf16[97,8,128]{2,1,0:T(8,128)(2,1)S(1)} collective-permute-done((bf16[97,8,128]{2,1,0:T(8,128)(2,1)S(1)}, bf16[97,8,128]{2,1,0:T(8,128)(2,1)S(1)}, u32[]{:S(2)}, u32[]{:S(2)}) %collective-permute-start.4) | collective-permute-done | bytes 198688 | tf_op jit(solution)/shard_map/ppermute | solution.py:170
  21.3 0.1 broadcast_select_fusion
  21.3 1.3 %collective-permute-start.7 = (bf16[97,8,128]{2,1,0:T(8,128)(2,1)S(1)}, bf16[97,8,128]{2,1,0:T(8,128)(2,1)S(1)}, u32[]{:S(2)}, u32[]{:S(2)}) collective-permute-start(bf16[97,8,128]{2,1,0:T(8,128)(2,1)S(1)} %broadcast_select_fusion), channel_id=1, source_target_pairs={{0,8},{1,3},{2,10},{3,1},{8,12},{9,11},{10,14},{11,9},{12,4},{13,1... | collective-permute-start | bytes 595976 | tf_op jit(solution)/shard_map/ppermute | solution.py:180
  22.6 1.1 %collective-permute-done.6.refs_2_ = bf16[97,8,128]{2,1,0:T(8,128)(2,1)S(1)} collective-permute-done((bf16[97,8,128]{2,1,0:T(8,128)(2,1)S(1)}, bf16[97,8,128]{2,1,0:T(8,128)(2,1)S(1)}, u32[]{:S(2)}, u32[]{:S(2)}) %collective-permute-start.6) | collective-permute-done | bytes 198688 | tf_op jit(solution)/shard_map/ppermute | solution.py:180
  23.7 1.2 %first_scores.1 = (bf16[256,768]{1,0:T(8,128)(2,1)S(1)}, f32[256,128]{1,0:T(8,128)S(1)}, f32[256,128]{1,0:T(8,128)S(1)}, f32[256,768]{1,0:T(8,128)S(1)}) custom-call(bf16[97,8,128]{2,1,0:T(8,128)(2,1)S(1)} %pack.1.own_ref, bf16[97,8,128]{2,1,0:T(8,128)(2,1)S(1)} %collective-permute-done.2.other_ref, bf16[97,8,128]{2,1,0:T(8,128)(2,1)S(1)} %collective-permute-done.1.refs_0_, ...), custom_call_target="tpu_custom_call" | custom-call | flops 40265318400 | bytes 2359296 | tf_op jit(solution)/shard_map/first_scores/pallas_call | solution.py:186
  24.9 1.1 %more_scores.1 = (f32[256,128]{1,0:T(8,128)S(1)}, f32[256,768]{1,0:T(8,128)S(1)}) custom-call(bf16[256,768]{1,0:T(8,128)(2,1)S(1)} %get-tuple-element.23.unit_ref, f32[256,128]{1,0:T(8,128)S(1)} %get-tuple-element.24.side_ref, f32[256,128]{1,0:T(8,128)S(1)} %get-tuple-element.25.old_sums_ref, ...), custom_call_target="tpu_custom_call", output_to_operand_aliasing={{0}: (2, {}), {1}: (3, {})} | custom-call | flops 30198988800 | bytes 2162688 | tf_op jit(solution)/shard_map/more_scores/pallas_call | solution.py:200
  26.0 1.1 %collective-permute-done.7.refs_0_ = bf16[97,8,128]{2,1,0:T(8,128)(2,1)S(1)} collective-permute-done((bf16[97,8,128]{2,1,0:T(8,128)(2,1)S(1)}, bf16[97,8,128]{2,1,0:T(8,128)(2,1)S(1)}, u32[]{:S(2)}, u32[]{:S(2)}) %collective-permute-start.7) | collective-permute-done | bytes 198688 | tf_op jit(solution)/shard_map/ppermute | solution.py:180
  27.1 0.6 %final_scores.1 = (f32[128,128]{1,0:T(8,128)S(1)}, f32[128,768]{1,0:T(8,128)S(1)}, bf16[136,768]{1,0:T(8,128)(2,1)S(1)}) custom-call(bf16[256,768]{1,0:T(8,128)(2,1)S(1)} %get-tuple-element.23.unit_ref, f32[256,128]{1,0:T(8,128)S(1)} %get-tuple-element.24.side_ref, f32[256,128]{1,0:T(8,128)S(1)} %get-tuple-element.29.old_sums_ref, ...), custom_call_target="tpu_custom_call" | custom-call | flops 10066329600 | bytes 1769472 | tf_op jit(solution)/shard_map/final_scores/pallas_call | solution.py:210
  27.7 0.1 collective-permute-start.8
  27.8 1.4 %collective-permute-done.8.got_ref = bf16[136,768]{1,0:T(8,128)(2,1)S(1)} collective-permute-done((bf16[136,768]{1,0:T(8,128)(2,1)S(1)}, bf16[136,768]{1,0:T(8,128)(2,1)S(1)}, u32[]{:S(2)}, u32[]{:S(2)}) %collective-permute-start.8) | collective-permute-done | bytes 208928 | tf_op jit(solution)/shard_map/ppermute | solution.py:183
  29.3 1.0 %combine.1 = (f32[1,128]{1,0:T(1,128)}, f32[128,768]{1,0:T(8,128)}) custom-call(f32[128,128]{1,0:T(8,128)S(1)} %get-tuple-element.31.sums_ref, f32[128,768]{1,0:T(8,128)S(1)} %get-tuple-element.32.mixed_ref, bf16[136,768]{1,0:T(8,128)(2,1)S(1)} %collective-permute-done.8.got_ref), custom_call_target="tpu_custom_call" | custom-call | tf_op jit(solution)/shard_map/combine/pallas_call | solution.py:254
  (1 shorter events, 0.0 us)
Async XLA Ops:
  0.6 0.7 %copy-start.1 = (s32[128,1]{0,1:T(1,128)S(1)}, s32[128,1]{0,1:T(1,128)}, u32[]{:S(2)}) copy-start(s32[128,1]{0,1:T(1,128)} %param.4) | copy-start | bytes 1540
  0.6 0.7 %copy-start.2 = (s32[128]{0:T(128)S(1)}, s32[128]{0:T(128)}, u32[]{:S(2)}) copy-start(s32[128]{0:T(128)} %param.5) | copy-start | bytes 1540
  1.3 0.9 %copy-start = (bf16[128,768]{1,0:T(8,128)(2,1)S(1)}, bf16[128,768]{1,0:T(8,128)(2,1)}, u32[]{:S(2)}) copy-start(bf16[128,768]{1,0:T(8,128)(2,1)} %param.3) | copy-start | bytes 589828
  2.3 9.4 %collective-permute-start = (bf16[97,8,128]{2,1,0:T(8,128)(2,1)S(1)}, bf16[97,8,128]{2,1,0:T(8,128)(2,1)S(1)}, u32[]{:S(2)}, u32[]{:S(2)}) collective-permute-start(bf16[97,8,128]{2,1,0:T(8,128)(2,1)S(1)} %pack.1.own_ref), channel_id=1, source_target_pairs={{0,8},{2,10},{8,12},{10,14},{12,4},{14,6},{4,0},{6,2},{1,9},{3,11}... | collective-permute-start | bytes 595976 | tf_op jit(solution)/shard_map/ppermute | solution.py:167
  6.3 6.4 %collective-permute-start.1 = (bf16[97,8,128]{2,1,0:T(8,128)(2,1)S(1)}, bf16[97,8,128]{2,1,0:T(8,128)(2,1)S(1)}, u32[]{:S(2)}, u32[]{:S(2)}) collective-permute-start(bf16[97,8,128]{2,1,0:T(8,128)(2,1)S(1)} %pack.1.own_ref), channel_id=1, source_target_pairs={{0,2},{2,0},{4,6},{6,4},{8,10},{10,8},{12,14},{14,12},{1,3},{3,1},... | collective-permute-start | bytes 595976 | tf_op jit(solution)/shard_map/ppermute | solution.py:170
  7.8 4.9 %collective-permute-start.2 = (bf16[97,8,128]{2,1,0:T(8,128)(2,1)S(1)}, bf16[97,8,128]{2,1,0:T(8,128)(2,1)S(1)}, u32[]{:S(2)}, u32[]{:S(2)}) collective-permute-start(bf16[97,8,128]{2,1,0:T(8,128)(2,1)S(1)} %pack.1.own_ref), channel_id=1, source_target_pairs={{0,1},{1,0},{2,3},{3,2},{4,5},{5,4},{6,7},{7,6},{8,9},{9,8},{10,11... | collective-permute-start | bytes 595976 | tf_op jit(solution)/shard_map/ppermute | solution.py:183
  7.8 9.2 %collective-permute-start.5 = (bf16[97,8,128]{2,1,0:T(8,128)(2,1)S(1)}, bf16[97,8,128]{2,1,0:T(8,128)(2,1)S(1)}, u32[]{:S(2)}, u32[]{:S(2)}) collective-permute-start(bf16[97,8,128]{2,1,0:T(8,128)(2,1)S(1)} %pack.1.own_ref), channel_id=1, source_target_pairs={{0,4},{2,6},{8,0},{10,2},{12,8},{14,10},{4,12},{6,14},{1,5},{3,7},... | collective-permute-start | bytes 595976 | tf_op jit(solution)/shard_map/ppermute | solution.py:167
  12.8 8.1 %collective-permute-start.3 = (bf16[97,8,128]{2,1,0:T(8,128)(2,1)S(1)}, bf16[97,8,128]{2,1,0:T(8,128)(2,1)S(1)}, u32[]{:S(2)}, u32[]{:S(2)}) collective-permute-start(bf16[97,8,128]{2,1,0:T(8,128)(2,1)S(1)} %collective-permute-done.refs_0_), channel_id=1, source_target_pairs={{0,8},{2,10},{8,12},{10,14},{12,4},{14,6},{4,0},{6,2},{1,9},{3,11}... | collective-permute-start | bytes 595976 | tf_op jit(solution)/shard_map/ppermute | solution.py:167
  15.1 6.2 %collective-permute-start.4 = (bf16[97,8,128]{2,1,0:T(8,128)(2,1)S(1)}, bf16[97,8,128]{2,1,0:T(8,128)(2,1)S(1)}, u32[]{:S(2)}, u32[]{:S(2)}) collective-permute-start(bf16[97,8,128]{2,1,0:T(8,128)(2,1)S(1)} %collective-permute-done.refs_0_), channel_id=1, source_target_pairs={{0,2},{2,0},{4,6},{6,4},{8,10},{10,8},{12,14},{14,12},{1,3},{3,1},... | collective-permute-start | bytes 595976 | tf_op jit(solution)/shard_map/ppermute | solution.py:170
  17.1 6.6 %collective-permute-start.6 = (bf16[97,8,128]{2,1,0:T(8,128)(2,1)S(1)}, bf16[97,8,128]{2,1,0:T(8,128)(2,1)S(1)}, u32[]{:S(2)}, u32[]{:S(2)}) collective-permute-start(bf16[97,8,128]{2,1,0:T(8,128)(2,1)S(1)} %broadcast_select_fusion.1), channel_id=1, source_target_pairs={{0,4},{1,3},{2,6},{3,1},{8,0},{9,11},{10,2},{11,9},{12,8},{13,15},... | collective-permute-start | bytes 595976 | tf_op jit(solution)/shard_map/ppermute | solution.py:180
  21.3 5.7 %collective-permute-start.7 = (bf16[97,8,128]{2,1,0:T(8,128)(2,1)S(1)}, bf16[97,8,128]{2,1,0:T(8,128)(2,1)S(1)}, u32[]{:S(2)}, u32[]{:S(2)}) collective-permute-start(bf16[97,8,128]{2,1,0:T(8,128)(2,1)S(1)} %broadcast_select_fusion), channel_id=1, source_target_pairs={{0,8},{1,3},{2,10},{3,1},{8,12},{9,11},{10,14},{11,9},{12,4},{13,1... | collective-permute-start | bytes 595976 | tf_op jit(solution)/shard_map/ppermute | solution.py:180
  27.7 1.5 %collective-permute-start.8 = (bf16[136,768]{1,0:T(8,128)(2,1)S(1)}, bf16[136,768]{1,0:T(8,128)(2,1)S(1)}, u32[]{:S(2)}, u32[]{:S(2)}) collective-permute-start(bf16[136,768]{1,0:T(8,128)(2,1)S(1)} %get-tuple-element.33), channel_id=1, source_target_pairs={{0,1},{1,0},{2,3},{3,2},{4,5},{5,4},{6,7},{7,6},{8,9},{9,8},{10,11... | collective-permute-start | bytes 626696 | tf_op jit(solution)/shard_map/ppermute | solution.py:183

commit v13 on v12

--- a/solution.py
+++ b/solution.py
@@ -234,8 +234,8 @@
         moved, beside, other = lax.optimization_barrier((moved, beside, other))
         opposite = along(moved, 1)
         moved_beside = across(moved)
-        ahead_beside = two_ways(beside, -1, ahead)
-        other, opposite, moved_beside = lax.optimization_barrier((other, opposite, moved_beside))
+        ahead_beside = across(ahead)
+        other, moved_beside, opposite = lax.optimization_barrier((other, moved_beside, opposite))
         last = [two_ways(moved_beside, 1, opposite)]
         unit, side, sums, mixed = first(own, other, beside, ahead, ahead_beside)
         sums, mixed = more(unit, side, sums, mixed, moved, moved_beside, opposite)

time: 30.4 us -> 30.5 us (level)
  starting transfers between devices: 12.2 us -> 14.1 us
  waiting for transfers between devices: 11.7 us -> 10 us
    ppermute x2 -> x3, starting transfers between devices: 2.98 us -> 5.29 us  [across(): return lax.ppermute(array, 'shard', [(at, at ^ 1) for at in range(shards)])]
    ppermute x2 -> x1, waiting for transfers between devices: 2.24 us -> 0.01 us  [two_ways(): return lax.ppermute(source, ('shard', 'owner'), pairs)]
    ppermute x2 -> x3, waiting for transfers between devices: 1.48 us -> 2.77 us  [across(): return lax.ppermute(array, 'shard', [(at, at ^ 1) for at in range(shards)])]
    ppermute x3, waiting for transfers between devices: 6.58 us -> 5.83 us  [along(): return lax.ppermute(array, 'shard', pairs)]
    ppermute x2 -> x1, starting transfers between devices: 2.74 us -> 2.35 us  [two_ways(): return lax.ppermute(source, ('shard', 'owner'), pairs)]
  transfers between devices with their start and end apart: 9 -> 9, of which waited for: 8 -> 6; matrix products, arithmetic and copies ran while one was open for 0% -> 0% of each run, Pallas kernels for 7% -> 7%
where the time goes in v13:
time: 30.5 us; the launch traced here: 30.4 us
  starting transfers between devices  14.1 us (46%)
  waiting for transfers between devices  10 us (33%)
  Pallas kernels  3.84 us (13%)
  local copies, waits for them, and re-layouts  1.58 us (5%)
  between operations  0.7 us (2%)
    ppermute x3, starting transfers between devices, along(): return lax.ppermute(array, 'shard', pairs)  6.42 us
    ppermute x3, waiting for transfers between devices, along(): return lax.ppermute(array, 'shard', pairs)  5.83 us
    ppermute x3, starting transfers between devices, across(): return lax.ppermute(array, 'shard', [(at, at ^ 1) for at in range(shards)])  5.29 us
    ppermute x3, waiting for transfers between devices, across(): return lax.ppermute(array, 'shard', [(at, at ^ 1) for at in range(shards)])  2.77 us
    ppermute x1, starting transfers between devices, two_ways(): return lax.ppermute(source, ('shard', 'owner'), pairs)  2.35 us
    unnamed x6, local copies, waits for them, and re-layouts  1.58 us
    ppermute x2, waiting for transfers between devices, swap(): lax.ppermute(array, 'owner', [(at, lanes - 1 - at) for at in range(lanes)])  1.45 us
    pallas_call x1, Pallas kernels, first(): pl.pallas_call(first_kernel, out_shape=[shape(queries, width, dtype=bf16)...  1.18 us
  transfers between devices with their start and end apart: 9, of which 6 were waited for; matrix products, arithmetic and copies ran while one was open for 0% of the time, Pallas kernels for 7%

profile of v13, /device:TPU:0, one launch (start us, length us, event | category | flops | bytes accessed | tf_op | source)
XLA Modules:
  0.0 30.4 jit_solution(17788659601089950486)
XLA Ops:
  0.6 0.0 copy-start.1
  0.6 0.0 copy-start.2
  0.6 0.6 %copy-done.1 = s32[128,1]{0,1:T(1,128)S(1)} copy-done((s32[128,1]{0,1:T(1,128)S(1)}, s32[128,1]{0,1:T(1,128)}, u32[]{:S(2)}) %copy-start.1) | copy-done | bytes 536
  1.3 0.0 copy-done.2
  1.3 0.0 copy-start
  1.3 0.9 %copy-done = bf16[128,768]{1,0:T(8,128)(2,1)S(1)} copy-done((bf16[128,768]{1,0:T(8,128)(2,1)S(1)}, bf16[128,768]{1,0:T(8,128)(2,1)}, u32[]{:S(2)}) %copy-start) | copy-done | bytes 196632
  2.3 4.1 %collective-permute-start = (bf16[97,8,128]{2,1,0:T(8,128)(2,1)S(1)}, bf16[97,8,128]{2,1,0:T(8,128)(2,1)S(1)}, u32[]{:S(2)}, u32[]{:S(2)}) collective-permute-start(bf16[97,8,128]{2,1,0:T(8,128)(2,1)S(1)} %pack.1.own_ref), channel_id=1, source_target_pairs={{0,8},{2,10},{8,12},{10,14},{12,4},{14,6},{4,0},{6,2},{1,9},{3,11}... | collective-permute-start | bytes 595976 | tf_op jit(solution)/shard_map/ppermute | solution.py:167
  6.3 1.5 %collective-permute-start.1 = (bf16[97,8,128]{2,1,0:T(8,128)(2,1)S(1)}, bf16[97,8,128]{2,1,0:T(8,128)(2,1)S(1)}, u32[]{:S(2)}, u32[]{:S(2)}) collective-permute-start(bf16[97,8,128]{2,1,0:T(8,128)(2,1)S(1)} %pack.1.own_ref), channel_id=1, source_target_pairs={{0,2},{2,0},{4,6},{6,4},{8,10},{10,8},{12,14},{14,12},{1,3},{3,1},... | collective-permute-start | bytes 595976 | tf_op jit(solution)/shard_map/ppermute | solution.py:170
  7.8 0.0 collective-permute-start.2
  7.8 0.0 collective-permute-start.5
  7.8 3.9 %collective-permute-done.refs_0_ = bf16[97,8,128]{2,1,0:T(8,128)(2,1)S(1)} collective-permute-done((bf16[97,8,128]{2,1,0:T(8,128)(2,1)S(1)}, bf16[97,8,128]{2,1,0:T(8,128)(2,1)S(1)}, u32[]{:S(2)}, u32[]{:S(2)}) %collective-permute-start) | collective-permute-done | bytes 198688 | tf_op jit(solution)/shard_map/ppermute | solution.py:167
  11.7 1.1 %collective-permute-done.1.refs_0_ = bf16[97,8,128]{2,1,0:T(8,128)(2,1)S(1)} collective-permute-done((bf16[97,8,128]{2,1,0:T(8,128)(2,1)S(1)}, bf16[97,8,128]{2,1,0:T(8,128)(2,1)S(1)}, u32[]{:S(2)}, u32[]{:S(2)}) %collective-permute-start.1) | collective-permute-done | bytes 198688 | tf_op jit(solution)/shard_map/ppermute | solution.py:170
  12.7 0.0 collective-permute-done.2.other_ref
  12.8 1.5 %collective-permute-start.3 = (bf16[97,8,128]{2,1,0:T(8,128)(2,1)S(1)}, bf16[97,8,128]{2,1,0:T(8,128)(2,1)S(1)}, u32[]{:S(2)}, u32[]{:S(2)}) collective-permute-start(bf16[97,8,128]{2,1,0:T(8,128)(2,1)S(1)} %collective-permute-done.refs_0_), channel_id=1, source_target_pairs={{0,2},{2,0},{4,6},{6,4},{8,10},{10,8},{12,14},{14,12},{1,3},{3,1},... | collective-permute-start | bytes 595976 | tf_op jit(solution)/shard_map/ppermute | solution.py:170
  14.2 2.3 %collective-permute-start.4 = (bf16[97,8,128]{2,1,0:T(8,128)(2,1)S(1)}, bf16[97,8,128]{2,1,0:T(8,128)(2,1)S(1)}, u32[]{:S(2)}, u32[]{:S(2)}) collective-permute-start(bf16[97,8,128]{2,1,0:T(8,128)(2,1)S(1)} %collective-permute-done.refs_0_), channel_id=1, source_target_pairs={{0,8},{2,10},{8,12},{10,14},{12,4},{14,6},{4,0},{6,2},{1,9},{3,11}... | collective-permute-start | bytes 595976 | tf_op jit(solution)/shard_map/ppermute | solution.py:167
  16.6 0.4 %collective-permute-done.5.refs_1_ = bf16[97,8,128]{2,1,0:T(8,128)(2,1)S(1)} collective-permute-done((bf16[97,8,128]{2,1,0:T(8,128)(2,1)S(1)}, bf16[97,8,128]{2,1,0:T(8,128)(2,1)S(1)}, u32[]{:S(2)}, u32[]{:S(2)}) %collective-permute-start.5) | collective-permute-done | bytes 198688 | tf_op jit(solution)/shard_map/ppermute | solution.py:167
  16.9 2.3 %collective-permute-start.6 = (bf16[97,8,128]{2,1,0:T(8,128)(2,1)S(1)}, bf16[97,8,128]{2,1,0:T(8,128)(2,1)S(1)}, u32[]{:S(2)}, u32[]{:S(2)}) collective-permute-start(bf16[97,8,128]{2,1,0:T(8,128)(2,1)S(1)} %collective-permute-done.5.refs_1_), channel_id=1, source_target_pairs={{0,2},{2,0},{4,6},{6,4},{8,10},{10,8},{12,14},{14,12},{1,3},{3,1},... | collective-permute-start | bytes 595976 | tf_op jit(solution)/shard_map/ppermute | solution.py:170
  19.2 0.0 collective-permute-done.3.refs_1_
  19.2 1.6 %collective-permute-done.4.refs_2_ = bf16[97,8,128]{2,1,0:T(8,128)(2,1)S(1)} collective-permute-done((bf16[97,8,128]{2,1,0:T(8,128)(2,1)S(1)}, bf16[97,8,128]{2,1,0:T(8,128)(2,1)S(1)}, u32[]{:S(2)}, u32[]{:S(2)}) %collective-permute-start.4) | collective-permute-done | bytes 198688 | tf_op jit(solution)/shard_map/ppermute | solution.py:167
  20.9 0.1 broadcast_select_fusion
  20.9 2.4 %collective-permute-start.7 = (bf16[97,8,128]{2,1,0:T(8,128)(2,1)S(1)}, bf16[97,8,128]{2,1,0:T(8,128)(2,1)S(1)}, u32[]{:S(2)}, u32[]{:S(2)}) collective-permute-start(bf16[97,8,128]{2,1,0:T(8,128)(2,1)S(1)} %broadcast_select_fusion), channel_id=1, source_target_pairs={{0,8},{1,3},{2,10},{3,1},{8,12},{9,11},{10,14},{11,9},{12,4},{13,1... | collective-permute-start | bytes 595976 | tf_op jit(solution)/shard_map/ppermute | solution.py:180
  23.3 1.7 %collective-permute-done.6.refs_2_ = bf16[97,8,128]{2,1,0:T(8,128)(2,1)S(1)} collective-permute-done((bf16[97,8,128]{2,1,0:T(8,128)(2,1)S(1)}, bf16[97,8,128]{2,1,0:T(8,128)(2,1)S(1)}, u32[]{:S(2)}, u32[]{:S(2)}) %collective-permute-start.6) | collective-permute-done | bytes 198688 | tf_op jit(solution)/shard_map/ppermute | solution.py:170
  25.0 1.2 %first_scores.1 = (bf16[256,768]{1,0:T(8,128)(2,1)S(1)}, f32[256,128]{1,0:T(8,128)S(1)}, f32[256,128]{1,0:T(8,128)S(1)}, f32[256,768]{1,0:T(8,128)S(1)}) custom-call(bf16[97,8,128]{2,1,0:T(8,128)(2,1)S(1)} %pack.1.own_ref, bf16[97,8,128]{2,1,0:T(8,128)(2,1)S(1)} %collective-permute-done.2.other_ref, bf16[97,8,128]{2,1,0:T(8,128)(2,1)S(1)} %collective-permute-done.1.refs_0_, ...), custom_call_target="tpu_custom_call" | custom-call | flops 40265318400 | bytes 2359296 | tf_op jit(solution)/shard_map/first_scores/pallas_call | solution.py:186
  26.2 1.1 %more_scores.1 = (f32[256,128]{1,0:T(8,128)S(1)}, f32[256,768]{1,0:T(8,128)S(1)}) custom-call(bf16[256,768]{1,0:T(8,128)(2,1)S(1)} %get-tuple-element.23.unit_ref, f32[256,128]{1,0:T(8,128)S(1)} %get-tuple-element.24.side_ref, f32[256,128]{1,0:T(8,128)S(1)} %get-tuple-element.25.old_sums_ref, ...), custom_call_target="tpu_custom_call", output_to_operand_aliasing={{0}: (2, {}), {1}: (3, {})} | custom-call | flops 30198988800 | bytes 2162688 | tf_op jit(solution)/shard_map/more_scores/pallas_call | solution.py:200
  27.2 0.0 collective-permute-done.7.refs_0_
  27.3 0.6 %final_scores.1 = (f32[128,128]{1,0:T(8,128)S(1)}, f32[128,768]{1,0:T(8,128)S(1)}, bf16[136,768]{1,0:T(8,128)(2,1)S(1)}) custom-call(bf16[256,768]{1,0:T(8,128)(2,1)S(1)} %get-tuple-element.23.unit_ref, f32[256,128]{1,0:T(8,128)S(1)} %get-tuple-element.24.side_ref, f32[256,128]{1,0:T(8,128)S(1)} %get-tuple-element.29.old_sums_ref, ...), custom_call_target="tpu_custom_call" | custom-call | flops 10066329600 | bytes 1769472 | tf_op jit(solution)/shard_map/final_scores/pallas_call | solution.py:210
  27.9 0.1 collective-permute-start.8
  28.0 1.4 %collective-permute-done.8.got_ref = bf16[136,768]{1,0:T(8,128)(2,1)S(1)} collective-permute-done((bf16[136,768]{1,0:T(8,128)(2,1)S(1)}, bf16[136,768]{1,0:T(8,128)(2,1)S(1)}, u32[]{:S(2)}, u32[]{:S(2)}) %collective-permute-start.8) | collective-permute-done | bytes 208928 | tf_op jit(solution)/shard_map/ppermute | solution.py:183
  29.4 1.0 %combine.1 = (f32[1,128]{1,0:T(1,128)}, f32[128,768]{1,0:T(8,128)}) custom-call(f32[128,128]{1,0:T(8,128)S(1)} %get-tuple-element.31.sums_ref, f32[128,768]{1,0:T(8,128)S(1)} %get-tuple-element.32.mixed_ref, bf16[136,768]{1,0:T(8,128)(2,1)S(1)} %collective-permute-done.8.got_ref), custom_call_target="tpu_custom_call" | custom-call | tf_op jit(solution)/shard_map/combine/pallas_call | solution.py:254
  (1 shorter events, 0.0 us)
Async XLA Ops:
  0.6 0.7 %copy-start.1 = (s32[128,1]{0,1:T(1,128)S(1)}, s32[128,1]{0,1:T(1,128)}, u32[]{:S(2)}) copy-start(s32[128,1]{0,1:T(1,128)} %param.4) | copy-start | bytes 1540
  0.6 0.7 %copy-start.2 = (s32[128]{0:T(128)S(1)}, s32[128]{0:T(128)}, u32[]{:S(2)}) copy-start(s32[128]{0:T(128)} %param.5) | copy-start | bytes 1540
  1.3 0.9 %copy-start = (bf16[128,768]{1,0:T(8,128)(2,1)S(1)}, bf16[128,768]{1,0:T(8,128)(2,1)}, u32[]{:S(2)}) copy-start(bf16[128,768]{1,0:T(8,128)(2,1)} %param.3) | copy-start | bytes 589828
  2.3 9.4 %collective-permute-start = (bf16[97,8,128]{2,1,0:T(8,128)(2,1)S(1)}, bf16[97,8,128]{2,1,0:T(8,128)(2,1)S(1)}, u32[]{:S(2)}, u32[]{:S(2)}) collective-permute-start(bf16[97,8,128]{2,1,0:T(8,128)(2,1)S(1)} %pack.1.own_ref), channel_id=1, source_target_pairs={{0,8},{2,10},{8,12},{10,14},{12,4},{14,6},{4,0},{6,2},{1,9},{3,11}... | collective-permute-start | bytes 595976 | tf_op jit(solution)/shard_map/ppermute | solution.py:167
  6.3 6.4 %collective-permute-start.1 = (bf16[97,8,128]{2,1,0:T(8,128)(2,1)S(1)}, bf16[97,8,128]{2,1,0:T(8,128)(2,1)S(1)}, u32[]{:S(2)}, u32[]{:S(2)}) collective-permute-start(bf16[97,8,128]{2,1,0:T(8,128)(2,1)S(1)} %pack.1.own_ref), channel_id=1, source_target_pairs={{0,2},{2,0},{4,6},{6,4},{8,10},{10,8},{12,14},{14,12},{1,3},{3,1},... | collective-permute-start | bytes 595976 | tf_op jit(solution)/shard_map/ppermute | solution.py:170
  7.8 4.9 %collective-permute-start.2 = (bf16[97,8,128]{2,1,0:T(8,128)(2,1)S(1)}, bf16[97,8,128]{2,1,0:T(8,128)(2,1)S(1)}, u32[]{:S(2)}, u32[]{:S(2)}) collective-permute-start(bf16[97,8,128]{2,1,0:T(8,128)(2,1)S(1)} %pack.1.own_ref), channel_id=1, source_target_pairs={{0,1},{1,0},{2,3},{3,2},{4,5},{5,4},{6,7},{7,6},{8,9},{9,8},{10,11... | collective-permute-start | bytes 595976 | tf_op jit(solution)/shard_map/ppermute | solution.py:183
  7.8 9.1 %collective-permute-start.5 = (bf16[97,8,128]{2,1,0:T(8,128)(2,1)S(1)}, bf16[97,8,128]{2,1,0:T(8,128)(2,1)S(1)}, u32[]{:S(2)}, u32[]{:S(2)}) collective-permute-start(bf16[97,8,128]{2,1,0:T(8,128)(2,1)S(1)} %pack.1.own_ref), channel_id=1, source_target_pairs={{0,4},{2,6},{8,0},{10,2},{12,8},{14,10},{4,12},{6,14},{1,5},{3,7},... | collective-permute-start | bytes 595976 | tf_op jit(solution)/shard_map/ppermute | solution.py:167
  12.8 6.5 %collective-permute-start.3 = (bf16[97,8,128]{2,1,0:T(8,128)(2,1)S(1)}, bf16[97,8,128]{2,1,0:T(8,128)(2,1)S(1)}, u32[]{:S(2)}, u32[]{:S(2)}) collective-permute-start(bf16[97,8,128]{2,1,0:T(8,128)(2,1)S(1)} %collective-permute-done.refs_0_), channel_id=1, source_target_pairs={{0,2},{2,0},{4,6},{6,4},{8,10},{10,8},{12,14},{14,12},{1,3},{3,1},... | collective-permute-start | bytes 595976 | tf_op jit(solution)/shard_map/ppermute | solution.py:170
  14.2 6.6 %collective-permute-start.4 = (bf16[97,8,128]{2,1,0:T(8,128)(2,1)S(1)}, bf16[97,8,128]{2,1,0:T(8,128)(2,1)S(1)}, u32[]{:S(2)}, u32[]{:S(2)}) collective-permute-start(bf16[97,8,128]{2,1,0:T(8,128)(2,1)S(1)} %collective-permute-done.refs_0_), channel_id=1, source_target_pairs={{0,8},{2,10},{8,12},{10,14},{12,4},{14,6},{4,0},{6,2},{1,9},{3,11}... | collective-permute-start | bytes 595976 | tf_op jit(solution)/shard_map/ppermute | solution.py:167
  16.9 8.1 %collective-permute-start.6 = (bf16[97,8,128]{2,1,0:T(8,128)(2,1)S(1)}, bf16[97,8,128]{2,1,0:T(8,128)(2,1)S(1)}, u32[]{:S(2)}, u32[]{:S(2)}) collective-permute-start(bf16[97,8,128]{2,1,0:T(8,128)(2,1)S(1)} %collective-permute-done.5.refs_1_), channel_id=1, source_target_pairs={{0,2},{2,0},{4,6},{6,4},{8,10},{10,8},{12,14},{14,12},{1,3},{3,1},... | collective-permute-start | bytes 595976 | tf_op jit(solution)/shard_map/ppermute | solution.py:170
  20.9 6.3 %collective-permute-start.7 = (bf16[97,8,128]{2,1,0:T(8,128)(2,1)S(1)}, bf16[97,8,128]{2,1,0:T(8,128)(2,1)S(1)}, u32[]{:S(2)}, u32[]{:S(2)}) collective-permute-start(bf16[97,8,128]{2,1,0:T(8,128)(2,1)S(1)} %broadcast_select_fusion), channel_id=1, source_target_pairs={{0,8},{1,3},{2,10},{3,1},{8,12},{9,11},{10,14},{11,9},{12,4},{13,1... | collective-permute-start | bytes 595976 | tf_op jit(solution)/shard_map/ppermute | solution.py:180
  27.9 1.5 %collective-permute-start.8 = (bf16[136,768]{1,0:T(8,128)(2,1)S(1)}, bf16[136,768]{1,0:T(8,128)(2,1)S(1)}, u32[]{:S(2)}, u32[]{:S(2)}) collective-permute-start(bf16[136,768]{1,0:T(8,128)(2,1)S(1)} %get-tuple-element.33), channel_id=1, source_target_pairs={{0,1},{1,0},{2,3},{3,2},{4,5},{5,4},{6,7},{7,6},{8,9},{9,8},{10,11... | collective-permute-start | bytes 626696 | tf_op jit(solution)/shard_map/ppermute | solution.py:183

commit v14 on v13

--- a/solution.py
+++ b/solution.py
@@ -234,7 +234,7 @@
         moved, beside, other = lax.optimization_barrier((moved, beside, other))
         opposite = along(moved, 1)
         moved_beside = across(moved)
-        ahead_beside = across(ahead)
+        ahead_beside = two_ways(beside, -1, ahead)
         other, moved_beside, opposite = lax.optimization_barrier((other, moved_beside, opposite))
         last = [two_ways(moved_beside, 1, opposite)]
         unit, side, sums, mixed = first(own, other, beside, ahead, ahead_beside)

time: 30.5 us -> 29.9 us (0.980)
  starting transfers between devices: 14.1 us -> 12.7 us
  waiting for transfers between devices: 10 us -> 10.9 us
    ppermute x3 -> x2, starting transfers between devices: 5.29 us -> 2.98 us  [across(): return lax.ppermute(array, 'shard', [(at, at ^ 1) for at in range(shards)])]
    ppermute x1 -> x2, waiting for transfers between devices: 0.01 us -> 1.14 us  [two_ways(): return lax.ppermute(source, ('shard', 'owner'), pairs)]
    ppermute x3 -> x2, waiting for transfers between devices: 2.77 us -> 1.66 us  [across(): return lax.ppermute(array, 'shard', [(at, at ^ 1) for at in range(shards)])]
    ppermute x1 -> x2, starting transfers between devices: 2.35 us -> 3.19 us  [two_ways(): return lax.ppermute(source, ('shard', 'owner'), pairs)]
    ppermute x3, waiting for transfers between devices: 5.83 us -> 6.63 us  [along(): return lax.ppermute(array, 'shard', pairs)]
  transfers between devices with their start and end apart: 9 -> 9, of which waited for: 6 -> 8; matrix products, arithmetic and copies ran while one was open for 0% -> 0% of each run, Pallas kernels for 7% -> 8%
where the time goes in v14:
time: 29.9 us; the launch traced here: 29.8 us
  starting transfers between devices  12.7 us (42%)
  waiting for transfers between devices  10.9 us (36%)
  Pallas kernels  3.84 us (13%)
  local copies, waits for them, and re-layouts  1.58 us (5%)
  between operations  0.69 us (2%)
    ppermute x3, waiting for transfers between devices, along(): return lax.ppermute(array, 'shard', pairs)  6.63 us
    ppermute x3, starting transfers between devices, along(): return lax.ppermute(array, 'shard', pairs)  6.42 us
    ppermute x2, starting transfers between devices, two_ways(): return lax.ppermute(source, ('shard', 'owner'), pairs)  3.19 us
    ppermute x2, starting transfers between devices, across(): return lax.ppermute(array, 'shard', [(at, at ^ 1) for at in range(shards)])  2.98 us
    ppermute x2, waiting for transfers between devices, across(): return lax.ppermute(array, 'shard', [(at, at ^ 1) for at in range(shards)])  1.66 us
    unnamed x6, local copies, waits for them, and re-layouts  1.58 us
    ppermute x2, waiting for transfers between devices, swap(): lax.ppermute(array, 'owner', [(at, lanes - 1 - at) for at in range(lanes)])  1.45 us
    pallas_call x1, Pallas kernels, first(): pl.pallas_call(first_kernel, out_shape=[shape(queries, width, dtype=bf16)...  1.18 us
  transfers between devices with their start and end apart: 9, of which 8 were waited for; matrix products, arithmetic and copies ran while one was open for 0% of the time, Pallas kernels for 8%

profile of v14, /device:TPU:0, one launch (start us, length us, event | category | flops | bytes accessed | tf_op | source)
XLA Modules:
  0.0 29.8 jit_solution(3757161919218838013)
XLA Ops:
  0.6 0.0 copy-start.1
  0.6 0.0 copy-start.2
  0.6 0.6 %copy-done.1 = s32[128,1]{0,1:T(1,128)S(1)} copy-done((s32[128,1]{0,1:T(1,128)S(1)}, s32[128,1]{0,1:T(1,128)}, u32[]{:S(2)}) %copy-start.1) | copy-done | bytes 536
  1.3 0.0 copy-done.2
  1.3 0.0 copy-start
  1.3 0.9 %copy-done = bf16[128,768]{1,0:T(8,128)(2,1)S(1)} copy-done((bf16[128,768]{1,0:T(8,128)(2,1)S(1)}, bf16[128,768]{1,0:T(8,128)(2,1)}, u32[]{:S(2)}) %copy-start) | copy-done | bytes 196632
  2.3 4.1 %collective-permute-start = (bf16[97,8,128]{2,1,0:T(8,128)(2,1)S(1)}, bf16[97,8,128]{2,1,0:T(8,128)(2,1)S(1)}, u32[]{:S(2)}, u32[]{:S(2)}) collective-permute-start(bf16[97,8,128]{2,1,0:T(8,128)(2,1)S(1)} %pack.1.own_ref), channel_id=1, source_target_pairs={{0,8},{2,10},{8,12},{10,14},{12,4},{14,6},{4,0},{6,2},{1,9},{3,11}... | collective-permute-start | bytes 595976 | tf_op jit(solution)/shard_map/ppermute | solution.py:167
  6.3 1.5 %collective-permute-start.1 = (bf16[97,8,128]{2,1,0:T(8,128)(2,1)S(1)}, bf16[97,8,128]{2,1,0:T(8,128)(2,1)S(1)}, u32[]{:S(2)}, u32[]{:S(2)}) collective-permute-start(bf16[97,8,128]{2,1,0:T(8,128)(2,1)S(1)} %pack.1.own_ref), channel_id=1, source_target_pairs={{0,2},{2,0},{4,6},{6,4},{8,10},{10,8},{12,14},{14,12},{1,3},{3,1},... | collective-permute-start | bytes 595976 | tf_op jit(solution)/shard_map/ppermute | solution.py:170
  7.8 0.0 collective-permute-start.2
  7.8 0.0 collective-permute-start.5
  7.8 3.9 %collective-permute-done.refs_0_ = bf16[97,8,128]{2,1,0:T(8,128)(2,1)S(1)} collective-permute-done((bf16[97,8,128]{2,1,0:T(8,128)(2,1)S(1)}, bf16[97,8,128]{2,1,0:T(8,128)(2,1)S(1)}, u32[]{:S(2)}, u32[]{:S(2)}) %collective-permute-start) | collective-permute-done | bytes 198688 | tf_op jit(solution)/shard_map/ppermute | solution.py:167
  11.7 1.1 %collective-permute-done.1.refs_0_ = bf16[97,8,128]{2,1,0:T(8,128)(2,1)S(1)} collective-permute-done((bf16[97,8,128]{2,1,0:T(8,128)(2,1)S(1)}, bf16[97,8,128]{2,1,0:T(8,128)(2,1)S(1)}, u32[]{:S(2)}, u32[]{:S(2)}) %collective-permute-start.1) | collective-permute-done | bytes 198688 | tf_op jit(solution)/shard_map/ppermute | solution.py:170
  12.7 0.0 collective-permute-done.2.other_ref
  12.8 1.5 %collective-permute-start.3 = (bf16[97,8,128]{2,1,0:T(8,128)(2,1)S(1)}, bf16[97,8,128]{2,1,0:T(8,128)(2,1)S(1)}, u32[]{:S(2)}, u32[]{:S(2)}) collective-permute-start(bf16[97,8,128]{2,1,0:T(8,128)(2,1)S(1)} %collective-permute-done.refs_0_), channel_id=1, source_target_pairs={{0,2},{2,0},{4,6},{6,4},{8,10},{10,8},{12,14},{14,12},{1,3},{3,1},... | collective-permute-start | bytes 595976 | tf_op jit(solution)/shard_map/ppermute | solution.py:170
  14.2 2.3 %collective-permute-start.4 = (bf16[97,8,128]{2,1,0:T(8,128)(2,1)S(1)}, bf16[97,8,128]{2,1,0:T(8,128)(2,1)S(1)}, u32[]{:S(2)}, u32[]{:S(2)}) collective-permute-start(bf16[97,8,128]{2,1,0:T(8,128)(2,1)S(1)} %collective-permute-done.refs_0_), channel_id=1, source_target_pairs={{0,8},{2,10},{8,12},{10,14},{12,4},{14,6},{4,0},{6,2},{1,9},{3,11}... | collective-permute-start | bytes 595976 | tf_op jit(solution)/shard_map/ppermute | solution.py:167
  16.6 0.4 %collective-permute-done.5.refs_1_ = bf16[97,8,128]{2,1,0:T(8,128)(2,1)S(1)} collective-permute-done((bf16[97,8,128]{2,1,0:T(8,128)(2,1)S(1)}, bf16[97,8,128]{2,1,0:T(8,128)(2,1)S(1)}, u32[]{:S(2)}, u32[]{:S(2)}) %collective-permute-start.5) | collective-permute-done | bytes 198688 | tf_op jit(solution)/shard_map/ppermute | solution.py:167
  16.9 0.1 broadcast_select_fusion.1
  17.0 0.8 %collective-permute-start.6 = (bf16[97,8,128]{2,1,0:T(8,128)(2,1)S(1)}, bf16[97,8,128]{2,1,0:T(8,128)(2,1)S(1)}, u32[]{:S(2)}, u32[]{:S(2)}) collective-permute-start(bf16[97,8,128]{2,1,0:T(8,128)(2,1)S(1)} %broadcast_select_fusion.1), channel_id=1, source_target_pairs={{0,4},{1,3},{2,6},{3,1},{8,0},{9,11},{10,2},{11,9},{12,8},{13,15},... | collective-permute-start | bytes 595976 | tf_op jit(solution)/shard_map/ppermute | solution.py:180
  17.8 0.6 %collective-permute-done.3.refs_1_ = bf16[97,8,128]{2,1,0:T(8,128)(2,1)S(1)} collective-permute-done((bf16[97,8,128]{2,1,0:T(8,128)(2,1)S(1)}, bf16[97,8,128]{2,1,0:T(8,128)(2,1)S(1)}, u32[]{:S(2)}, u32[]{:S(2)}) %collective-permute-start.3) | collective-permute-done | bytes 198688 | tf_op jit(solution)/shard_map/ppermute | solution.py:170
  18.4 2.4 %collective-permute-done.4.refs_2_ = bf16[97,8,128]{2,1,0:T(8,128)(2,1)S(1)} collective-permute-done((bf16[97,8,128]{2,1,0:T(8,128)(2,1)S(1)}, bf16[97,8,128]{2,1,0:T(8,128)(2,1)S(1)}, u32[]{:S(2)}, u32[]{:S(2)}) %collective-permute-start.4) | collective-permute-done | bytes 198688 | tf_op jit(solution)/shard_map/ppermute | solution.py:167
  20.9 0.1 broadcast_select_fusion
  20.9 2.4 %collective-permute-start.7 = (bf16[97,8,128]{2,1,0:T(8,128)(2,1)S(1)}, bf16[97,8,128]{2,1,0:T(8,128)(2,1)S(1)}, u32[]{:S(2)}, u32[]{:S(2)}) collective-permute-start(bf16[97,8,128]{2,1,0:T(8,128)(2,1)S(1)} %broadcast_select_fusion), channel_id=1, source_target_pairs={{0,8},{1,3},{2,10},{3,1},{8,12},{9,11},{10,14},{11,9},{12,4},{13,1... | collective-permute-start | bytes 595976 | tf_op jit(solution)/shard_map/ppermute | solution.py:180
  23.3 0.4 %collective-permute-done.6.refs_2_ = bf16[97,8,128]{2,1,0:T(8,128)(2,1)S(1)} collective-permute-done((bf16[97,8,128]{2,1,0:T(8,128)(2,1)S(1)}, bf16[97,8,128]{2,1,0:T(8,128)(2,1)S(1)}, u32[]{:S(2)}, u32[]{:S(2)}) %collective-permute-start.6) | collective-permute-done | bytes 198688 | tf_op jit(solution)/shard_map/ppermute | solution.py:180
  23.7 1.2 %first_scores.1 = (bf16[256,768]{1,0:T(8,128)(2,1)S(1)}, f32[256,128]{1,0:T(8,128)S(1)}, f32[256,128]{1,0:T(8,128)S(1)}, f32[256,768]{1,0:T(8,128)S(1)}) custom-call(bf16[97,8,128]{2,1,0:T(8,128)(2,1)S(1)} %pack.1.own_ref, bf16[97,8,128]{2,1,0:T(8,128)(2,1)S(1)} %collective-permute-done.2.other_ref, bf16[97,8,128]{2,1,0:T(8,128)(2,1)S(1)} %collective-permute-done.1.refs_0_, ...), custom_call_target="tpu_custom_call" | custom-call | flops 40265318400 | bytes 2359296 | tf_op jit(solution)/shard_map/first_scores/pallas_call | solution.py:186
  24.9 1.1 %more_scores.1 = (f32[256,128]{1,0:T(8,128)S(1)}, f32[256,768]{1,0:T(8,128)S(1)}) custom-call(bf16[256,768]{1,0:T(8,128)(2,1)S(1)} %get-tuple-element.23.unit_ref, f32[256,128]{1,0:T(8,128)S(1)} %get-tuple-element.24.side_ref, f32[256,128]{1,0:T(8,128)S(1)} %get-tuple-element.25.old_sums_ref, ...), custom_call_target="tpu_custom_call", output_to_operand_aliasing={{0}: (2, {}), {1}: (3, {})} | custom-call | flops 30198988800 | bytes 2162688 | tf_op jit(solution)/shard_map/more_scores/pallas_call | solution.py:200
  26.0 0.7 %collective-permute-done.7.refs_0_ = bf16[97,8,128]{2,1,0:T(8,128)(2,1)S(1)} collective-permute-done((bf16[97,8,128]{2,1,0:T(8,128)(2,1)S(1)}, bf16[97,8,128]{2,1,0:T(8,128)(2,1)S(1)}, u32[]{:S(2)}, u32[]{:S(2)}) %collective-permute-start.7) | collective-permute-done | bytes 198688 | tf_op jit(solution)/shard_map/ppermute | solution.py:180
  26.7 0.6 %final_scores.1 = (f32[128,128]{1,0:T(8,128)S(1)}, f32[128,768]{1,0:T(8,128)S(1)}, bf16[136,768]{1,0:T(8,128)(2,1)S(1)}) custom-call(bf16[256,768]{1,0:T(8,128)(2,1)S(1)} %get-tuple-element.23.unit_ref, f32[256,128]{1,0:T(8,128)S(1)} %get-tuple-element.24.side_ref, f32[256,128]{1,0:T(8,128)S(1)} %get-tuple-element.29.old_sums_ref, ...), custom_call_target="tpu_custom_call" | custom-call | flops 10066329600 | bytes 1769472 | tf_op jit(solution)/shard_map/final_scores/pallas_call | solution.py:210
  27.3 0.1 collective-permute-start.8
  27.4 1.4 %collective-permute-done.8.got_ref = bf16[136,768]{1,0:T(8,128)(2,1)S(1)} collective-permute-done((bf16[136,768]{1,0:T(8,128)(2,1)S(1)}, bf16[136,768]{1,0:T(8,128)(2,1)S(1)}, u32[]{:S(2)}, u32[]{:S(2)}) %collective-permute-start.8) | collective-permute-done | bytes 208928 | tf_op jit(solution)/shard_map/ppermute | solution.py:183
  28.8 1.0 %combine.1 = (f32[1,128]{1,0:T(1,128)}, f32[128,768]{1,0:T(8,128)}) custom-call(f32[128,128]{1,0:T(8,128)S(1)} %get-tuple-element.31.sums_ref, f32[128,768]{1,0:T(8,128)S(1)} %get-tuple-element.32.mixed_ref, bf16[136,768]{1,0:T(8,128)(2,1)S(1)} %collective-permute-done.8.got_ref), custom_call_target="tpu_custom_call" | custom-call | tf_op jit(solution)/shard_map/combine/pallas_call | solution.py:254
  (1 shorter events, 0.0 us)
Async XLA Ops:
  0.6 0.7 %copy-start.1 = (s32[128,1]{0,1:T(1,128)S(1)}, s32[128,1]{0,1:T(1,128)}, u32[]{:S(2)}) copy-start(s32[128,1]{0,1:T(1,128)} %param.4) | copy-start | bytes 1540
  0.6 0.7 %copy-start.2 = (s32[128]{0:T(128)S(1)}, s32[128]{0:T(128)}, u32[]{:S(2)}) copy-start(s32[128]{0:T(128)} %param.5) | copy-start | bytes 1540
  1.3 0.9 %copy-start = (bf16[128,768]{1,0:T(8,128)(2,1)S(1)}, bf16[128,768]{1,0:T(8,128)(2,1)}, u32[]{:S(2)}) copy-start(bf16[128,768]{1,0:T(8,128)(2,1)} %param.3) | copy-start | bytes 589828
  2.3 9.4 %collective-permute-start = (bf16[97,8,128]{2,1,0:T(8,128)(2,1)S(1)}, bf16[97,8,128]{2,1,0:T(8,128)(2,1)S(1)}, u32[]{:S(2)}, u32[]{:S(2)}) collective-permute-start(bf16[97,8,128]{2,1,0:T(8,128)(2,1)S(1)} %pack.1.own_ref), channel_id=1, source_target_pairs={{0,8},{2,10},{8,12},{10,14},{12,4},{14,6},{4,0},{6,2},{1,9},{3,11}... | collective-permute-start | bytes 595976 | tf_op jit(solution)/shard_map/ppermute | solution.py:167
  6.3 6.4 %collective-permute-start.1 = (bf16[97,8,128]{2,1,0:T(8,128)(2,1)S(1)}, bf16[97,8,128]{2,1,0:T(8,128)(2,1)S(1)}, u32[]{:S(2)}, u32[]{:S(2)}) collective-permute-start(bf16[97,8,128]{2,1,0:T(8,128)(2,1)S(1)} %pack.1.own_ref), channel_id=1, source_target_pairs={{0,2},{2,0},{4,6},{6,4},{8,10},{10,8},{12,14},{14,12},{1,3},{3,1},... | collective-permute-start | bytes 595976 | tf_op jit(solution)/shard_map/ppermute | solution.py:170
  7.8 4.9 %collective-permute-start.2 = (bf16[97,8,128]{2,1,0:T(8,128)(2,1)S(1)}, bf16[97,8,128]{2,1,0:T(8,128)(2,1)S(1)}, u32[]{:S(2)}, u32[]{:S(2)}) collective-permute-start(bf16[97,8,128]{2,1,0:T(8,128)(2,1)S(1)} %pack.1.own_ref), channel_id=1, source_target_pairs={{0,1},{1,0},{2,3},{3,2},{4,5},{5,4},{6,7},{7,6},{8,9},{9,8},{10,11... | collective-permute-start | bytes 595976 | tf_op jit(solution)/shard_map/ppermute | solution.py:183
  7.8 9.1 %collective-permute-start.5 = (bf16[97,8,128]{2,1,0:T(8,128)(2,1)S(1)}, bf16[97,8,128]{2,1,0:T(8,128)(2,1)S(1)}, u32[]{:S(2)}, u32[]{:S(2)}) collective-permute-start(bf16[97,8,128]{2,1,0:T(8,128)(2,1)S(1)} %pack.1.own_ref), channel_id=1, source_target_pairs={{0,4},{2,6},{8,0},{10,2},{12,8},{14,10},{4,12},{6,14},{1,5},{3,7},... | collective-permute-start | bytes 595976 | tf_op jit(solution)/shard_map/ppermute | solution.py:167
  12.8 5.7 %collective-permute-start.3 = (bf16[97,8,128]{2,1,0:T(8,128)(2,1)S(1)}, bf16[97,8,128]{2,1,0:T(8,128)(2,1)S(1)}, u32[]{:S(2)}, u32[]{:S(2)}) collective-permute-start(bf16[97,8,128]{2,1,0:T(8,128)(2,1)S(1)} %collective-permute-done.refs_0_), channel_id=1, source_target_pairs={{0,2},{2,0},{4,6},{6,4},{8,10},{10,8},{12,14},{14,12},{1,3},{3,1},... | collective-permute-start | bytes 595976 | tf_op jit(solution)/shard_map/ppermute | solution.py:170
  14.2 6.6 %collective-permute-start.4 = (bf16[97,8,128]{2,1,0:T(8,128)(2,1)S(1)}, bf16[97,8,128]{2,1,0:T(8,128)(2,1)S(1)}, u32[]{:S(2)}, u32[]{:S(2)}) collective-permute-start(bf16[97,8,128]{2,1,0:T(8,128)(2,1)S(1)} %collective-permute-done.refs_0_), channel_id=1, source_target_pairs={{0,8},{2,10},{8,12},{10,14},{12,4},{14,6},{4,0},{6,2},{1,9},{3,11}... | collective-permute-start | bytes 595976 | tf_op jit(solution)/shard_map/ppermute | solution.py:167
  17.0 6.7 %collective-permute-start.6 = (bf16[97,8,128]{2,1,0:T(8,128)(2,1)S(1)}, bf16[97,8,128]{2,1,0:T(8,128)(2,1)S(1)}, u32[]{:S(2)}, u32[]{:S(2)}) collective-permute-start(bf16[97,8,128]{2,1,0:T(8,128)(2,1)S(1)} %broadcast_select_fusion.1), channel_id=1, source_target_pairs={{0,4},{1,3},{2,6},{3,1},{8,0},{9,11},{10,2},{11,9},{12,8},{13,15},... | collective-permute-start | bytes 595976 | tf_op jit(solution)/shard_map/ppermute | solution.py:180
  20.9 5.7 %collective-permute-start.7 = (bf16[97,8,128]{2,1,0:T(8,128)(2,1)S(1)}, bf16[97,8,128]{2,1,0:T(8,128)(2,1)S(1)}, u32[]{:S(2)}, u32[]{:S(2)}) collective-permute-start(bf16[97,8,128]{2,1,0:T(8,128)(2,1)S(1)} %broadcast_select_fusion), channel_id=1, source_target_pairs={{0,8},{1,3},{2,10},{3,1},{8,12},{9,11},{10,14},{11,9},{12,4},{13,1... | collective-permute-start | bytes 595976 | tf_op jit(solution)/shard_map/ppermute | solution.py:180
  27.3 1.5 %collective-permute-start.8 = (bf16[136,768]{1,0:T(8,128)(2,1)S(1)}, bf16[136,768]{1,0:T(8,128)(2,1)S(1)}, u32[]{:S(2)}, u32[]{:S(2)}) collective-permute-start(bf16[136,768]{1,0:T(8,128)(2,1)S(1)} %get-tuple-element.33), channel_id=1, source_target_pairs={{0,1},{1,0},{2,3},{3,2},{4,5},{5,4},{6,7},{7,6},{8,9},{9,8},{10,11... | collective-permute-start | bytes 626696 | tf_op jit(solution)/shard_map/ppermute | solution.py:183

commit v15 on v14

--- a/solution.py
+++ b/solution.py
@@ -169,14 +169,16 @@
     def across(array):
         return lax.ppermute(array, "shard", [(at, at ^ 1) for at in range(shards)])
 
-    def two_ways(by_ring, step, by_side):
+    def two_ways(by_ring, step, by_side, ring_lane):
         pairs = []
         for at in range(rounds):
             for side in range(2):
                 here, there = 2 * ring[at] + side, 2 * ring[(at + step) % rounds] + side
-                pairs.append((here * lanes, there * lanes))
-                pairs += [(here * lanes + lane, (here ^ 1) * lanes + lane) for lane in range(1, lanes)]
-        source = jnp.where(lax.axis_index("owner") == 0, by_ring, by_side)
+                pairs += [
+                    (here * lanes + lane, (there if lane == ring_lane else here ^ 1) * lanes + lane)
+                    for lane in range(lanes)
+                ]
+        source = jnp.where(lax.axis_index("owner") == ring_lane, by_ring, by_side)
         return lax.ppermute(source, ("shard", "owner"), pairs)
 
     def swap(array):
@@ -234,9 +236,9 @@
         moved, beside, other = lax.optimization_barrier((moved, beside, other))
         opposite = along(moved, 1)
         moved_beside = across(moved)
-        ahead_beside = two_ways(beside, -1, ahead)
+        ahead_beside = two_ways(beside, -1, ahead, lanes - 1)
         other, moved_beside, opposite = lax.optimization_barrier((other, moved_beside, opposite))
-        last = [two_ways(moved_beside, 1, opposite)]
+        last = [two_ways(moved_beside, 1, opposite, lanes - 1)]
         unit, side, sums, mixed = first(own, other, beside, ahead, ahead_beside)
         sums, mixed = more(unit, side, sums, mixed, moved, moved_beside, opposite)
     else:

time: 29.9 us -> 30.9 us (1.033)
  waiting for transfers between devices: 10.9 us -> 12.1 us
    ppermute x2, waiting for transfers between devices: 1.14 us -> 2.91 us  [two_ways(): return lax.ppermute(source, ('shard', 'owner'), pairs)]
    ppermute x2, waiting for transfers between devices: 1.66 us -> 1.06 us  [across(): return lax.ppermute(array, 'shard', [(at, at ^ 1) for at in range(shards)])]
  transfers between devices with their start and end apart: 9 -> 9, of which waited for: 8 -> 7; matrix products, arithmetic and copies ran while one was open for 0% -> 0% of each run, Pallas kernels for 8% -> 7%
where the time goes in v15:
time: 30.9 us; the launch traced here: 30.7 us
  starting transfers between devices  12.4 us (40%)
  waiting for transfers between devices  12.1 us (39%)
  Pallas kernels  3.84 us (12%)
  local copies, waits for them, and re-layouts  1.58 us (5%)
  between operations  0.69 us (2%)
    ppermute x3, waiting for transfers between devices, along(): return lax.ppermute(array, 'shard', pairs)  6.67 us
    ppermute x3, starting transfers between devices, along(): return lax.ppermute(array, 'shard', pairs)  6.42 us
    ppermute x2, starting transfers between devices, across(): return lax.ppermute(array, 'shard', [(at, at ^ 1) for at in range(shards)])  2.98 us
    ppermute x2, starting transfers between devices, two_ways(): return lax.ppermute(source, ('shard', 'owner'), pairs)  2.94 us
    ppermute x2, waiting for transfers between devices, two_ways(): return lax.ppermute(source, ('shard', 'owner'), pairs)  2.91 us
    unnamed x6, local copies, waits for them, and re-layouts  1.58 us
    ppermute x2, waiting for transfers between devices, swap(): lax.ppermute(array, 'owner', [(at, lanes - 1 - at) for at in range(lanes)])  1.45 us
    pallas_call x1, Pallas kernels, first(): pl.pallas_call(first_kernel, out_shape=[shape(queries, width, dtype=bf16)...  1.18 us
  transfers between devices with their start and end apart: 9, of which 7 were waited for; matrix products, arithmetic and copies ran while one was open for 0% of the time, Pallas kernels for 7%

profile of v15, /device:TPU:0, one launch (start us, length us, event | category | flops | bytes accessed | tf_op | source)
XLA Modules:
  0.0 30.7 jit_solution(12625494353319262926)
XLA Ops:
  0.6 0.0 copy-start.1
  0.6 0.0 copy-start.2
  0.6 0.6 %copy-done.1 = s32[128,1]{0,1:T(1,128)S(1)} copy-done((s32[128,1]{0,1:T(1,128)S(1)}, s32[128,1]{0,1:T(1,128)}, u32[]{:S(2)}) %copy-start.1) | copy-done | bytes 536
  1.3 0.0 copy-done.2
  1.3 0.0 copy-start
  1.3 0.9 %copy-done = bf16[128,768]{1,0:T(8,128)(2,1)S(1)} copy-done((bf16[128,768]{1,0:T(8,128)(2,1)S(1)}, bf16[128,768]{1,0:T(8,128)(2,1)}, u32[]{:S(2)}) %copy-start) | copy-done | bytes 196632
  2.3 4.1 %collective-permute-start = (bf16[97,8,128]{2,1,0:T(8,128)(2,1)S(1)}, bf16[97,8,128]{2,1,0:T(8,128)(2,1)S(1)}, u32[]{:S(2)}, u32[]{:S(2)}) collective-permute-start(bf16[97,8,128]{2,1,0:T(8,128)(2,1)S(1)} %pack.1.own_ref), channel_id=1, source_target_pairs={{0,8},{2,10},{8,12},{10,14},{12,4},{14,6},{4,0},{6,2},{1,9},{3,11}... | collective-permute-start | bytes 595976 | tf_op jit(solution)/shard_map/ppermute | solution.py:167
  6.3 1.5 %collective-permute-start.1 = (bf16[97,8,128]{2,1,0:T(8,128)(2,1)S(1)}, bf16[97,8,128]{2,1,0:T(8,128)(2,1)S(1)}, u32[]{:S(2)}, u32[]{:S(2)}) collective-permute-start(bf16[97,8,128]{2,1,0:T(8,128)(2,1)S(1)} %pack.1.own_ref), channel_id=1, source_target_pairs={{0,2},{2,0},{4,6},{6,4},{8,10},{10,8},{12,14},{14,12},{1,3},{3,1},... | collective-permute-start | bytes 595976 | tf_op jit(solution)/shard_map/ppermute | solution.py:170
  7.8 0.0 collective-permute-start.2
  7.8 0.0 collective-permute-start.5
  7.8 3.9 %collective-permute-done.refs_0_ = bf16[97,8,128]{2,1,0:T(8,128)(2,1)S(1)} collective-permute-done((bf16[97,8,128]{2,1,0:T(8,128)(2,1)S(1)}, bf16[97,8,128]{2,1,0:T(8,128)(2,1)S(1)}, u32[]{:S(2)}, u32[]{:S(2)}) %collective-permute-start) | collective-permute-done | bytes 198688 | tf_op jit(solution)/shard_map/ppermute | solution.py:167
  11.7 1.1 %collective-permute-done.1.refs_0_ = bf16[97,8,128]{2,1,0:T(8,128)(2,1)S(1)} collective-permute-done((bf16[97,8,128]{2,1,0:T(8,128)(2,1)S(1)}, bf16[97,8,128]{2,1,0:T(8,128)(2,1)S(1)}, u32[]{:S(2)}, u32[]{:S(2)}) %collective-permute-start.1) | collective-permute-done | bytes 198688 | tf_op jit(solution)/shard_map/ppermute | solution.py:170
  12.7 0.0 collective-permute-done.2.other_ref
  12.8 1.5 %collective-permute-start.3 = (bf16[97,8,128]{2,1,0:T(8,128)(2,1)S(1)}, bf16[97,8,128]{2,1,0:T(8,128)(2,1)S(1)}, u32[]{:S(2)}, u32[]{:S(2)}) collective-permute-start(bf16[97,8,128]{2,1,0:T(8,128)(2,1)S(1)} %collective-permute-done.refs_0_), channel_id=1, source_target_pairs={{0,2},{2,0},{4,6},{6,4},{8,10},{10,8},{12,14},{14,12},{1,3},{3,1},... | collective-permute-start | bytes 595976 | tf_op jit(solution)/shard_map/ppermute | solution.py:170
  14.2 2.3 %collective-permute-start.4 = (bf16[97,8,128]{2,1,0:T(8,128)(2,1)S(1)}, bf16[97,8,128]{2,1,0:T(8,128)(2,1)S(1)}, u32[]{:S(2)}, u32[]{:S(2)}) collective-permute-start(bf16[97,8,128]{2,1,0:T(8,128)(2,1)S(1)} %collective-permute-done.refs_0_), channel_id=1, source_target_pairs={{0,8},{2,10},{8,12},{10,14},{12,4},{14,6},{4,0},{6,2},{1,9},{3,11}... | collective-permute-start | bytes 595976 | tf_op jit(solution)/shard_map/ppermute | solution.py:167
  16.6 0.4 %collective-permute-done.5.refs_1_ = bf16[97,8,128]{2,1,0:T(8,128)(2,1)S(1)} collective-permute-done((bf16[97,8,128]{2,1,0:T(8,128)(2,1)S(1)}, bf16[97,8,128]{2,1,0:T(8,128)(2,1)S(1)}, u32[]{:S(2)}, u32[]{:S(2)}) %collective-permute-start.5) | collective-permute-done | bytes 198688 | tf_op jit(solution)/shard_map/ppermute | solution.py:167
  16.9 0.1 broadcast_select_fusion.1
  17.0 2.4 %collective-permute-start.6 = (bf16[97,8,128]{2,1,0:T(8,128)(2,1)S(1)}, bf16[97,8,128]{2,1,0:T(8,128)(2,1)S(1)}, u32[]{:S(2)}, u32[]{:S(2)}) collective-permute-start(bf16[97,8,128]{2,1,0:T(8,128)(2,1)S(1)} %broadcast_select_fusion.1), channel_id=1, source_target_pairs={{0,2},{1,5},{2,0},{3,7},{8,10},{9,1},{10,8},{11,3},{12,14},{13,9},... | collective-permute-start | bytes 595976 | tf_op jit(solution)/shard_map/ppermute | solution.py:182
  19.4 0.0 collective-permute-done.3.refs_1_
  19.4 2.5 %collective-permute-done.4.refs_2_ = bf16[97,8,128]{2,1,0:T(8,128)(2,1)S(1)} collective-permute-done((bf16[97,8,128]{2,1,0:T(8,128)(2,1)S(1)}, bf16[97,8,128]{2,1,0:T(8,128)(2,1)S(1)}, u32[]{:S(2)}, u32[]{:S(2)}) %collective-permute-start.4) | collective-permute-done | bytes 198688 | tf_op jit(solution)/shard_map/ppermute | solution.py:167
  21.8 0.1 broadcast_select_fusion
  21.9 0.6 %collective-permute-start.7 = (bf16[97,8,128]{2,1,0:T(8,128)(2,1)S(1)}, bf16[97,8,128]{2,1,0:T(8,128)(2,1)S(1)}, u32[]{:S(2)}, u32[]{:S(2)}) collective-permute-start(bf16[97,8,128]{2,1,0:T(8,128)(2,1)S(1)} %broadcast_select_fusion), channel_id=1, source_target_pairs={{0,2},{1,9},{2,0},{3,11},{8,10},{9,13},{10,8},{11,15},{12,14},{13,... | collective-permute-start | bytes 595976 | tf_op jit(solution)/shard_map/ppermute | solution.py:182
  22.5 0.6 %collective-permute-done.6.refs_2_ = bf16[97,8,128]{2,1,0:T(8,128)(2,1)S(1)} collective-permute-done((bf16[97,8,128]{2,1,0:T(8,128)(2,1)S(1)}, bf16[97,8,128]{2,1,0:T(8,128)(2,1)S(1)}, u32[]{:S(2)}, u32[]{:S(2)}) %collective-permute-start.6) | collective-permute-done | bytes 198688 | tf_op jit(solution)/shard_map/ppermute | solution.py:182
  23.0 1.2 %first_scores.1 = (bf16[256,768]{1,0:T(8,128)(2,1)S(1)}, f32[256,128]{1,0:T(8,128)S(1)}, f32[256,128]{1,0:T(8,128)S(1)}, f32[256,768]{1,0:T(8,128)S(1)}) custom-call(bf16[97,8,128]{2,1,0:T(8,128)(2,1)S(1)} %pack.1.own_ref, bf16[97,8,128]{2,1,0:T(8,128)(2,1)S(1)} %collective-permute-done.2.other_ref, bf16[97,8,128]{2,1,0:T(8,128)(2,1)S(1)} %collective-permute-done.1.refs_0_, ...), custom_call_target="tpu_custom_call" | custom-call | flops 40265318400 | bytes 2359296 | tf_op jit(solution)/shard_map/first_scores/pallas_call | solution.py:188
  24.2 1.1 %more_scores.1 = (f32[256,128]{1,0:T(8,128)S(1)}, f32[256,768]{1,0:T(8,128)S(1)}) custom-call(bf16[256,768]{1,0:T(8,128)(2,1)S(1)} %get-tuple-element.23.unit_ref, f32[256,128]{1,0:T(8,128)S(1)} %get-tuple-element.24.side_ref, f32[256,128]{1,0:T(8,128)S(1)} %get-tuple-element.25.old_sums_ref, ...), custom_call_target="tpu_custom_call", output_to_operand_aliasing={{0}: (2, {}), {1}: (3, {})} | custom-call | flops 30198988800 | bytes 2162688 | tf_op jit(solution)/shard_map/more_scores/pallas_call | solution.py:202
  25.3 2.3 %collective-permute-done.7.refs_0_ = bf16[97,8,128]{2,1,0:T(8,128)(2,1)S(1)} collective-permute-done((bf16[97,8,128]{2,1,0:T(8,128)(2,1)S(1)}, bf16[97,8,128]{2,1,0:T(8,128)(2,1)S(1)}, u32[]{:S(2)}, u32[]{:S(2)}) %collective-permute-start.7) | collective-permute-done | bytes 198688 | tf_op jit(solution)/shard_map/ppermute | solution.py:182
  27.6 0.6 %final_scores.1 = (f32[128,128]{1,0:T(8,128)S(1)}, f32[128,768]{1,0:T(8,128)S(1)}, bf16[136,768]{1,0:T(8,128)(2,1)S(1)}) custom-call(bf16[256,768]{1,0:T(8,128)(2,1)S(1)} %get-tuple-element.23.unit_ref, f32[256,128]{1,0:T(8,128)S(1)} %get-tuple-element.24.side_ref, f32[256,128]{1,0:T(8,128)S(1)} %get-tuple-element.29.old_sums_ref, ...), custom_call_target="tpu_custom_call" | custom-call | flops 10066329600 | bytes 1769472 | tf_op jit(solution)/shard_map/final_scores/pallas_call | solution.py:212
  28.3 0.1 collective-permute-start.8
  28.3 1.4 %collective-permute-done.8.got_ref = bf16[136,768]{1,0:T(8,128)(2,1)S(1)} collective-permute-done((bf16[136,768]{1,0:T(8,128)(2,1)S(1)}, bf16[136,768]{1,0:T(8,128)(2,1)S(1)}, u32[]{:S(2)}, u32[]{:S(2)}) %collective-permute-start.8) | collective-permute-done | bytes 208928 | tf_op jit(solution)/shard_map/ppermute | solution.py:185
  29.8 1.0 %combine.1 = (f32[1,128]{1,0:T(1,128)}, f32[128,768]{1,0:T(8,128)}) custom-call(f32[128,128]{1,0:T(8,128)S(1)} %get-tuple-element.31.sums_ref, f32[128,768]{1,0:T(8,128)S(1)} %get-tuple-element.32.mixed_ref, bf16[136,768]{1,0:T(8,128)(2,1)S(1)} %collective-permute-done.8.got_ref), custom_call_target="tpu_custom_call" | custom-call | tf_op jit(solution)/shard_map/combine/pallas_call | solution.py:256
  (1 shorter events, 0.0 us)
Async XLA Ops:
  0.6 0.7 %copy-start.1 = (s32[128,1]{0,1:T(1,128)S(1)}, s32[128,1]{0,1:T(1,128)}, u32[]{:S(2)}) copy-start(s32[128,1]{0,1:T(1,128)} %param.4) | copy-start | bytes 1540
  0.6 0.7 %copy-start.2 = (s32[128]{0:T(128)S(1)}, s32[128]{0:T(128)}, u32[]{:S(2)}) copy-start(s32[128]{0:T(128)} %param.5) | copy-start | bytes 1540
  1.3 0.9 %copy-start = (bf16[128,768]{1,0:T(8,128)(2,1)S(1)}, bf16[128,768]{1,0:T(8,128)(2,1)}, u32[]{:S(2)}) copy-start(bf16[128,768]{1,0:T(8,128)(2,1)} %param.3) | copy-start | bytes 589828
  2.3 9.4 %collective-permute-start = (bf16[97,8,128]{2,1,0:T(8,128)(2,1)S(1)}, bf16[97,8,128]{2,1,0:T(8,128)(2,1)S(1)}, u32[]{:S(2)}, u32[]{:S(2)}) collective-permute-start(bf16[97,8,128]{2,1,0:T(8,128)(2,1)S(1)} %pack.1.own_ref), channel_id=1, source_target_pairs={{0,8},{2,10},{8,12},{10,14},{12,4},{14,6},{4,0},{6,2},{1,9},{3,11}... | collective-permute-start | bytes 595976 | tf_op jit(solution)/shard_map/ppermute | solution.py:167
  6.3 6.4 %collective-permute-start.1 = (bf16[97,8,128]{2,1,0:T(8,128)(2,1)S(1)}, bf16[97,8,128]{2,1,0:T(8,128)(2,1)S(1)}, u32[]{:S(2)}, u32[]{:S(2)}) collective-permute-start(bf16[97,8,128]{2,1,0:T(8,128)(2,1)S(1)} %pack.1.own_ref), channel_id=1, source_target_pairs={{0,2},{2,0},{4,6},{6,4},{8,10},{10,8},{12,14},{14,12},{1,3},{3,1},... | collective-permute-start | bytes 595976 | tf_op jit(solution)/shard_map/ppermute | solution.py:170
  7.8 4.9 %collective-permute-start.2 = (bf16[97,8,128]{2,1,0:T(8,128)(2,1)S(1)}, bf16[97,8,128]{2,1,0:T(8,128)(2,1)S(1)}, u32[]{:S(2)}, u32[]{:S(2)}) collective-permute-start(bf16[97,8,128]{2,1,0:T(8,128)(2,1)S(1)} %pack.1.own_ref), channel_id=1, source_target_pairs={{0,1},{1,0},{2,3},{3,2},{4,5},{5,4},{6,7},{7,6},{8,9},{9,8},{10,11... | collective-permute-start | bytes 595976 | tf_op jit(solution)/shard_map/ppermute | solution.py:185
  7.8 9.1 %collective-permute-start.5 = (bf16[97,8,128]{2,1,0:T(8,128)(2,1)S(1)}, bf16[97,8,128]{2,1,0:T(8,128)(2,1)S(1)}, u32[]{:S(2)}, u32[]{:S(2)}) collective-permute-start(bf16[97,8,128]{2,1,0:T(8,128)(2,1)S(1)} %pack.1.own_ref), channel_id=1, source_target_pairs={{0,4},{2,6},{8,0},{10,2},{12,8},{14,10},{4,12},{6,14},{1,5},{3,7},... | collective-permute-start | bytes 595976 | tf_op jit(solution)/shard_map/ppermute | solution.py:167
  12.8 6.6 %collective-permute-start.3 = (bf16[97,8,128]{2,1,0:T(8,128)(2,1)S(1)}, bf16[97,8,128]{2,1,0:T(8,128)(2,1)S(1)}, u32[]{:S(2)}, u32[]{:S(2)}) collective-permute-start(bf16[97,8,128]{2,1,0:T(8,128)(2,1)S(1)} %collective-permute-done.refs_0_), channel_id=1, source_target_pairs={{0,2},{2,0},{4,6},{6,4},{8,10},{10,8},{12,14},{14,12},{1,3},{3,1},... | collective-permute-start | bytes 595976 | tf_op jit(solution)/shard_map/ppermute | solution.py:170
  14.2 7.6 %collective-permute-start.4 = (bf16[97,8,128]{2,1,0:T(8,128)(2,1)S(1)}, bf16[97,8,128]{2,1,0:T(8,128)(2,1)S(1)}, u32[]{:S(2)}, u32[]{:S(2)}) collective-permute-start(bf16[97,8,128]{2,1,0:T(8,128)(2,1)S(1)} %collective-permute-done.refs_0_), channel_id=1, source_target_pairs={{0,8},{2,10},{8,12},{10,14},{12,4},{14,6},{4,0},{6,2},{1,9},{3,11}... | collective-permute-start | bytes 595976 | tf_op jit(solution)/shard_map/ppermute | solution.py:167
  17.0 6.0 %collective-permute-start.6 = (bf16[97,8,128]{2,1,0:T(8,128)(2,1)S(1)}, bf16[97,8,128]{2,1,0:T(8,128)(2,1)S(1)}, u32[]{:S(2)}, u32[]{:S(2)}) collective-permute-start(bf16[97,8,128]{2,1,0:T(8,128)(2,1)S(1)} %broadcast_select_fusion.1), channel_id=1, source_target_pairs={{0,2},{1,5},{2,0},{3,7},{8,10},{9,1},{10,8},{11,3},{12,14},{13,9},... | collective-permute-start | bytes 595976 | tf_op jit(solution)/shard_map/ppermute | solution.py:182
  21.9 5.7 %collective-permute-start.7 = (bf16[97,8,128]{2,1,0:T(8,128)(2,1)S(1)}, bf16[97,8,128]{2,1,0:T(8,128)(2,1)S(1)}, u32[]{:S(2)}, u32[]{:S(2)}) collective-permute-start(bf16[97,8,128]{2,1,0:T(8,128)(2,1)S(1)} %broadcast_select_fusion), channel_id=1, source_target_pairs={{0,2},{1,9},{2,0},{3,11},{8,10},{9,13},{10,8},{11,15},{12,14},{13,... | collective-permute-start | bytes 595976 | tf_op jit(solution)/shard_map/ppermute | solution.py:182
  28.3 1.5 %collective-permute-start.8 = (bf16[136,768]{1,0:T(8,128)(2,1)S(1)}, bf16[136,768]{1,0:T(8,128)(2,1)S(1)}, u32[]{:S(2)}, u32[]{:S(2)}) collective-permute-start(bf16[136,768]{1,0:T(8,128)(2,1)S(1)} %get-tuple-element.33), channel_id=1, source_target_pairs={{0,1},{1,0},{2,3},{3,2},{4,5},{5,4},{6,7},{7,6},{8,9},{9,8},{10,11... | collective-permute-start | bytes 626696 | tf_op jit(solution)/shard_map/ppermute | solution.py:185

commit v16 on v15

--- a/solution.py
+++ b/solution.py
@@ -236,7 +236,7 @@
         moved, beside, other = lax.optimization_barrier((moved, beside, other))
         opposite = along(moved, 1)
         moved_beside = across(moved)
-        ahead_beside = two_ways(beside, -1, ahead, lanes - 1)
+        ahead_beside = two_ways(beside, -1, ahead, 0)
         other, moved_beside, opposite = lax.optimization_barrier((other, moved_beside, opposite))
         last = [two_ways(moved_beside, 1, opposite, lanes - 1)]
         unit, side, sums, mixed = first(own, other, beside, ahead, ahead_beside)

time: 30.9 us -> 31 us (level)
  the two profiles are of different devices: /device:TPU:0 before, /device:TPU:3 now
where the time goes in v16:
time: 31 us; the launch traced here: 30.8 us
  waiting for transfers between devices  15.6 us (50%)
  starting transfers between devices  9 us (29%)
  Pallas kernels  3.84 us (12%)
  local copies, waits for them, and re-layouts  1.58 us (5%)
  between operations  0.7 us (2%)
    ppermute x3, waiting for transfers between devices, along(): return lax.ppermute(array, 'shard', pairs)  9.24 us
    ppermute x2, starting transfers between devices, swap(): lax.ppermute(array, 'owner', [(at, lanes - 1 - at) for at in range(lanes)])  4.25 us
    ppermute x3, starting transfers between devices, along(): return lax.ppermute(array, 'shard', pairs)  3.66 us
    ppermute x2, waiting for transfers between devices, two_ways(): return lax.ppermute(source, ('shard', 'owner'), pairs)  3.36 us
    ppermute x2, waiting for transfers between devices, across(): return lax.ppermute(array, 'shard', [(at, at ^ 1) for at in range(shards)])  1.88 us
    unnamed x6, local copies, waits for them, and re-layouts  1.58 us
    pallas_call x1, Pallas kernels, first(): pl.pallas_call(first_kernel, out_shape=[shape(queries, width, dtype=bf16)...  1.18 us
    ppermute x2, waiting for transfers between devices, swap(): lax.ppermute(array, 'owner', [(at, lanes - 1 - at) for at in range(lanes)])  1.09 us
  transfers between devices with their start and end apart: 9, of which 7 were waited for; matrix products, arithmetic and copies ran while one was open for 0% of the time, Pallas kernels for 7%

profile of v16, /device:TPU:3, one launch (start us, length us, event | category | flops | bytes accessed | tf_op | source)
XLA Modules:
  0.0 30.8 jit_solution(7274161780361882565)
XLA Ops:
  0.6 0.0 copy-start.1
  0.6 0.0 copy-start.2
  0.6 0.6 %copy-done.1 = s32[128,1]{0,1:T(1,128)S(1)} copy-done((s32[128,1]{0,1:T(1,128)S(1)}, s32[128,1]{0,1:T(1,128)}, u32[]{:S(2)}) %copy-start.1) | copy-done | bytes 536
  1.3 0.0 copy-done.2
  1.3 0.0 copy-start
  1.3 0.9 %copy-done = bf16[128,768]{1,0:T(8,128)(2,1)S(1)} copy-done((bf16[128,768]{1,0:T(8,128)(2,1)S(1)}, bf16[128,768]{1,0:T(8,128)(2,1)}, u32[]{:S(2)}) %copy-start) | copy-done | bytes 196632
  2.3 2.4 %collective-permute-start = (bf16[97,8,128]{2,1,0:T(8,128)(2,1)S(1)}, bf16[97,8,128]{2,1,0:T(8,128)(2,1)S(1)}, u32[]{:S(2)}, u32[]{:S(2)}) collective-permute-start(bf16[97,8,128]{2,1,0:T(8,128)(2,1)S(1)} %pack.1.own_ref), channel_id=1, source_target_pairs={{0,8},{2,10},{8,12},{10,14},{12,4},{14,6},{4,0},{6,2},{1,9},{3,11}... | collective-permute-start | bytes 595976 | tf_op jit(solution)/shard_map/ppermute | solution.py:167
  4.6 0.3 collective-permute-start.1
  4.9 1.2 %collective-permute-start.2 = (bf16[97,8,128]{2,1,0:T(8,128)(2,1)S(1)}, bf16[97,8,128]{2,1,0:T(8,128)(2,1)S(1)}, u32[]{:S(2)}, u32[]{:S(2)}) collective-permute-start(bf16[97,8,128]{2,1,0:T(8,128)(2,1)S(1)} %pack.1.own_ref), channel_id=1, source_target_pairs={{0,1},{1,0},{2,3},{3,2},{4,5},{5,4},{6,7},{7,6},{8,9},{9,8},{10,11... | collective-permute-start | bytes 595976 | tf_op jit(solution)/shard_map/ppermute | solution.py:185
  6.1 0.0 collective-permute-start.5
  6.1 2.1 %collective-permute-done.refs_0_ = bf16[97,8,128]{2,1,0:T(8,128)(2,1)S(1)} collective-permute-done((bf16[97,8,128]{2,1,0:T(8,128)(2,1)S(1)}, bf16[97,8,128]{2,1,0:T(8,128)(2,1)S(1)}, u32[]{:S(2)}, u32[]{:S(2)}) %collective-permute-start) | collective-permute-done | bytes 198688 | tf_op jit(solution)/shard_map/ppermute | solution.py:167
  8.2 1.9 %collective-permute-done.1.refs_0_ = bf16[97,8,128]{2,1,0:T(8,128)(2,1)S(1)} collective-permute-done((bf16[97,8,128]{2,1,0:T(8,128)(2,1)S(1)}, bf16[97,8,128]{2,1,0:T(8,128)(2,1)S(1)}, u32[]{:S(2)}, u32[]{:S(2)}) %collective-permute-start.1) | collective-permute-done | bytes 198688 | tf_op jit(solution)/shard_map/ppermute | solution.py:170
  10.1 0.0 collective-permute-done.2.other_ref
  10.1 0.3 collective-permute-start.3
  10.4 1.3 %collective-permute-start.4 = (bf16[97,8,128]{2,1,0:T(8,128)(2,1)S(1)}, bf16[97,8,128]{2,1,0:T(8,128)(2,1)S(1)}, u32[]{:S(2)}, u32[]{:S(2)}) collective-permute-start(bf16[97,8,128]{2,1,0:T(8,128)(2,1)S(1)} %collective-permute-done.refs_0_), channel_id=1, source_target_pairs={{0,8},{2,10},{8,12},{10,14},{12,4},{14,6},{4,0},{6,2},{1,9},{3,11}... | collective-permute-start | bytes 595976 | tf_op jit(solution)/shard_map/ppermute | solution.py:167
  11.7 4.8 %collective-permute-done.5.refs_1_ = bf16[97,8,128]{2,1,0:T(8,128)(2,1)S(1)} collective-permute-done((bf16[97,8,128]{2,1,0:T(8,128)(2,1)S(1)}, bf16[97,8,128]{2,1,0:T(8,128)(2,1)S(1)}, u32[]{:S(2)}, u32[]{:S(2)}) %collective-permute-start.5) | collective-permute-done | bytes 198688 | tf_op jit(solution)/shard_map/ppermute | solution.py:167
  16.4 0.1 broadcast_select_fusion.1
  16.5 0.1 collective-permute-start.6
  16.6 0.0 collective-permute-done.3.refs_1_
  16.6 2.3 %collective-permute-done.4.refs_2_ = bf16[97,8,128]{2,1,0:T(8,128)(2,1)S(1)} collective-permute-done((bf16[97,8,128]{2,1,0:T(8,128)(2,1)S(1)}, bf16[97,8,128]{2,1,0:T(8,128)(2,1)S(1)}, u32[]{:S(2)}, u32[]{:S(2)}) %collective-permute-start.4) | collective-permute-done | bytes 198688 | tf_op jit(solution)/shard_map/ppermute | solution.py:167
  18.9 0.1 broadcast_select_fusion
  19.0 0.5 %collective-permute-start.7 = (bf16[97,8,128]{2,1,0:T(8,128)(2,1)S(1)}, bf16[97,8,128]{2,1,0:T(8,128)(2,1)S(1)}, u32[]{:S(2)}, u32[]{:S(2)}) collective-permute-start(bf16[97,8,128]{2,1,0:T(8,128)(2,1)S(1)} %broadcast_select_fusion), channel_id=1, source_target_pairs={{0,2},{1,9},{2,0},{3,11},{8,10},{9,13},{10,8},{11,15},{12,14},{13,... | collective-permute-start | bytes 595976 | tf_op jit(solution)/shard_map/ppermute | solution.py:182
  19.5 1.9 %collective-permute-done.6.refs_2_ = bf16[97,8,128]{2,1,0:T(8,128)(2,1)S(1)} collective-permute-done((bf16[97,8,128]{2,1,0:T(8,128)(2,1)S(1)}, bf16[97,8,128]{2,1,0:T(8,128)(2,1)S(1)}, u32[]{:S(2)}, u32[]{:S(2)}) %collective-permute-start.6) | collective-permute-done | bytes 198688 | tf_op jit(solution)/shard_map/ppermute | solution.py:182
  21.4 1.2 %first_scores.1 = (bf16[256,768]{1,0:T(8,128)(2,1)S(1)}, f32[256,128]{1,0:T(8,128)S(1)}, f32[256,128]{1,0:T(8,128)S(1)}, f32[256,768]{1,0:T(8,128)S(1)}) custom-call(bf16[97,8,128]{2,1,0:T(8,128)(2,1)S(1)} %pack.1.own_ref, bf16[97,8,128]{2,1,0:T(8,128)(2,1)S(1)} %collective-permute-done.2.other_ref, bf16[97,8,128]{2,1,0:T(8,128)(2,1)S(1)} %collective-permute-done.1.refs_0_, ...), custom_call_target="tpu_custom_call" | custom-call | flops 40265318400 | bytes 2359296 | tf_op jit(solution)/shard_map/first_scores/pallas_call | solution.py:188
  22.6 1.1 %more_scores.1 = (f32[256,128]{1,0:T(8,128)S(1)}, f32[256,768]{1,0:T(8,128)S(1)}) custom-call(bf16[256,768]{1,0:T(8,128)(2,1)S(1)} %get-tuple-element.23.unit_ref, f32[256,128]{1,0:T(8,128)S(1)} %get-tuple-element.24.side_ref, f32[256,128]{1,0:T(8,128)S(1)} %get-tuple-element.25.old_sums_ref, ...), custom_call_target="tpu_custom_call", output_to_operand_aliasing={{0}: (2, {}), {1}: (3, {})} | custom-call | flops 30198988800 | bytes 2162688 | tf_op jit(solution)/shard_map/more_scores/pallas_call | solution.py:202
  23.7 1.5 %collective-permute-done.7.refs_0_ = bf16[97,8,128]{2,1,0:T(8,128)(2,1)S(1)} collective-permute-done((bf16[97,8,128]{2,1,0:T(8,128)(2,1)S(1)}, bf16[97,8,128]{2,1,0:T(8,128)(2,1)S(1)}, u32[]{:S(2)}, u32[]{:S(2)}) %collective-permute-start.7) | collective-permute-done | bytes 198688 | tf_op jit(solution)/shard_map/ppermute | solution.py:182
  25.1 0.6 %final_scores.1 = (f32[128,128]{1,0:T(8,128)S(1)}, f32[128,768]{1,0:T(8,128)S(1)}, bf16[136,768]{1,0:T(8,128)(2,1)S(1)}) custom-call(bf16[256,768]{1,0:T(8,128)(2,1)S(1)} %get-tuple-element.23.unit_ref, f32[256,128]{1,0:T(8,128)S(1)} %get-tuple-element.24.side_ref, f32[256,128]{1,0:T(8,128)S(1)} %get-tuple-element.29.old_sums_ref, ...), custom_call_target="tpu_custom_call" | custom-call | flops 10066329600 | bytes 1769472 | tf_op jit(solution)/shard_map/final_scores/pallas_call | solution.py:212
  25.8 3.0 %collective-permute-start.8 = (bf16[136,768]{1,0:T(8,128)(2,1)S(1)}, bf16[136,768]{1,0:T(8,128)(2,1)S(1)}, u32[]{:S(2)}, u32[]{:S(2)}) collective-permute-start(bf16[136,768]{1,0:T(8,128)(2,1)S(1)} %get-tuple-element.33), channel_id=1, source_target_pairs={{0,1},{1,0},{2,3},{3,2},{4,5},{5,4},{6,7},{7,6},{8,9},{9,8},{10,11... | collective-permute-start | bytes 626696 | tf_op jit(solution)/shard_map/ppermute | solution.py:185
  28.8 1.1 %collective-permute-done.8.got_ref = bf16[136,768]{1,0:T(8,128)(2,1)S(1)} collective-permute-done((bf16[136,768]{1,0:T(8,128)(2,1)S(1)}, bf16[136,768]{1,0:T(8,128)(2,1)S(1)}, u32[]{:S(2)}, u32[]{:S(2)}) %collective-permute-start.8) | collective-permute-done | bytes 208928 | tf_op jit(solution)/shard_map/ppermute | solution.py:185
  29.9 1.0 %combine.1 = (f32[1,128]{1,0:T(1,128)}, f32[128,768]{1,0:T(8,128)}) custom-call(f32[128,128]{1,0:T(8,128)S(1)} %get-tuple-element.31.sums_ref, f32[128,768]{1,0:T(8,128)S(1)} %get-tuple-element.32.mixed_ref, bf16[136,768]{1,0:T(8,128)(2,1)S(1)} %collective-permute-done.8.got_ref), custom_call_target="tpu_custom_call" | custom-call | tf_op jit(solution)/shard_map/combine/pallas_call | solution.py:256
  (1 shorter events, 0.0 us)
Async XLA Ops:
  0.6 0.7 %copy-start.1 = (s32[128,1]{0,1:T(1,128)S(1)}, s32[128,1]{0,1:T(1,128)}, u32[]{:S(2)}) copy-start(s32[128,1]{0,1:T(1,128)} %param.4) | copy-start | bytes 1540
  0.6 0.7 %copy-start.2 = (s32[128]{0:T(128)S(1)}, s32[128]{0:T(128)}, u32[]{:S(2)}) copy-start(s32[128]{0:T(128)} %param.5) | copy-start | bytes 1540
  1.3 0.9 %copy-start = (bf16[128,768]{1,0:T(8,128)(2,1)S(1)}, bf16[128,768]{1,0:T(8,128)(2,1)}, u32[]{:S(2)}) copy-start(bf16[128,768]{1,0:T(8,128)(2,1)} %param.3) | copy-start | bytes 589828
  2.3 6.0 %collective-permute-start = (bf16[97,8,128]{2,1,0:T(8,128)(2,1)S(1)}, bf16[97,8,128]{2,1,0:T(8,128)(2,1)S(1)}, u32[]{:S(2)}, u32[]{:S(2)}) collective-permute-start(bf16[97,8,128]{2,1,0:T(8,128)(2,1)S(1)} %pack.1.own_ref), channel_id=1, source_target_pairs={{0,8},{2,10},{8,12},{10,14},{12,4},{14,6},{4,0},{6,2},{1,9},{3,11}... | collective-permute-start | bytes 595976 | tf_op jit(solution)/shard_map/ppermute | solution.py:167
  4.6 5.5 %collective-permute-start.1 = (bf16[97,8,128]{2,1,0:T(8,128)(2,1)S(1)}, bf16[97,8,128]{2,1,0:T(8,128)(2,1)S(1)}, u32[]{:S(2)}, u32[]{:S(2)}) collective-permute-start(bf16[97,8,128]{2,1,0:T(8,128)(2,1)S(1)} %pack.1.own_ref), channel_id=1, source_target_pairs={{0,2},{2,0},{4,6},{6,4},{8,10},{10,8},{12,14},{14,12},{1,3},{3,1},... | collective-permute-start | bytes 595976 | tf_op jit(solution)/shard_map/ppermute | solution.py:170
  4.9 5.2 %collective-permute-start.2 = (bf16[97,8,128]{2,1,0:T(8,128)(2,1)S(1)}, bf16[97,8,128]{2,1,0:T(8,128)(2,1)S(1)}, u32[]{:S(2)}, u32[]{:S(2)}) collective-permute-start(bf16[97,8,128]{2,1,0:T(8,128)(2,1)S(1)} %pack.1.own_ref), channel_id=1, source_target_pairs={{0,1},{1,0},{2,3},{3,2},{4,5},{5,4},{6,7},{7,6},{8,9},{9,8},{10,11... | collective-permute-start | bytes 595976 | tf_op jit(solution)/shard_map/ppermute | solution.py:185
  6.1 10.3 %collective-permute-start.5 = (bf16[97,8,128]{2,1,0:T(8,128)(2,1)S(1)}, bf16[97,8,128]{2,1,0:T(8,128)(2,1)S(1)}, u32[]{:S(2)}, u32[]{:S(2)}) collective-permute-start(bf16[97,8,128]{2,1,0:T(8,128)(2,1)S(1)} %pack.1.own_ref), channel_id=1, source_target_pairs={{0,4},{2,6},{8,0},{10,2},{12,8},{14,10},{4,12},{6,14},{1,5},{3,7},... | collective-permute-start | bytes 595976 | tf_op jit(solution)/shard_map/ppermute | solution.py:167
  10.1 6.5 %collective-permute-start.3 = (bf16[97,8,128]{2,1,0:T(8,128)(2,1)S(1)}, bf16[97,8,128]{2,1,0:T(8,128)(2,1)S(1)}, u32[]{:S(2)}, u32[]{:S(2)}) collective-permute-start(bf16[97,8,128]{2,1,0:T(8,128)(2,1)S(1)} %collective-permute-done.refs_0_), channel_id=1, source_target_pairs={{0,2},{2,0},{4,6},{6,4},{8,10},{10,8},{12,14},{14,12},{1,3},{3,1},... | collective-permute-start | bytes 595976 | tf_op jit(solution)/shard_map/ppermute | solution.py:170
  10.4 8.6 %collective-permute-start.4 = (bf16[97,8,128]{2,1,0:T(8,128)(2,1)S(1)}, bf16[97,8,128]{2,1,0:T(8,128)(2,1)S(1)}, u32[]{:S(2)}, u32[]{:S(2)}) collective-permute-start(bf16[97,8,128]{2,1,0:T(8,128)(2,1)S(1)} %collective-permute-done.refs_0_), channel_id=1, source_target_pairs={{0,8},{2,10},{8,12},{10,14},{12,4},{14,6},{4,0},{6,2},{1,9},{3,11}... | collective-permute-start | bytes 595976 | tf_op jit(solution)/shard_map/ppermute | solution.py:167
  16.5 4.9 %collective-permute-start.6 = (bf16[97,8,128]{2,1,0:T(8,128)(2,1)S(1)}, bf16[97,8,128]{2,1,0:T(8,128)(2,1)S(1)}, u32[]{:S(2)}, u32[]{:S(2)}) collective-permute-start(bf16[97,8,128]{2,1,0:T(8,128)(2,1)S(1)} %broadcast_select_fusion.1), channel_id=1, source_target_pairs={{0,4},{1,3},{2,6},{3,1},{8,0},{9,11},{10,2},{11,9},{12,8},{13,15},... | collective-permute-start | bytes 595976 | tf_op jit(solution)/shard_map/ppermute | solution.py:182
  19.0 6.1 %collective-permute-start.7 = (bf16[97,8,128]{2,1,0:T(8,128)(2,1)S(1)}, bf16[97,8,128]{2,1,0:T(8,128)(2,1)S(1)}, u32[]{:S(2)}, u32[]{:S(2)}) collective-permute-start(bf16[97,8,128]{2,1,0:T(8,128)(2,1)S(1)} %broadcast_select_fusion), channel_id=1, source_target_pairs={{0,2},{1,9},{2,0},{3,11},{8,10},{9,13},{10,8},{11,15},{12,14},{13,... | collective-permute-start | bytes 595976 | tf_op jit(solution)/shard_map/ppermute | solution.py:182
  25.8 4.1 %collective-permute-start.8 = (bf16[136,768]{1,0:T(8,128)(2,1)S(1)}, bf16[136,768]{1,0:T(8,128)(2,1)S(1)}, u32[]{:S(2)}, u32[]{:S(2)}) collective-permute-start(bf16[136,768]{1,0:T(8,128)(2,1)S(1)} %get-tuple-element.33), channel_id=1, source_target_pairs={{0,1},{1,0},{2,3},{3,2},{4,5},{5,4},{6,7},{7,6},{8,9},{9,8},{10,11... | collective-permute-start | bytes 626696 | tf_op jit(solution)/shard_map/ppermute | solution.py:185

commit v17 on v13

--- a/solution.py
+++ b/solution.py
@@ -106,23 +106,28 @@
     mixed_ref[...] = old_mixed_ref[...] + mixed
 
 
-def final_kernel(unit_ref, side_ref, old_sums_ref, old_mixed_ref, *refs):
-    blocks, (keep_sums_ref, keep_ref, send_ref) = refs[:-3], refs[-3:]
-    count, width = keep_ref.shape
-    earlier, every, mixed = score(unit_ref[...], side_ref, blocks)
-    earlier += old_sums_ref[:, 0:1]
-    every += old_sums_ref[:, 1:2]
-    mixed += old_mixed_ref[...]
-    keep_sums_ref[...] = jnp.zeros_like(keep_sums_ref)
-    keep_sums_ref[:, 0:1] = earlier[:count]
-    keep_sums_ref[:, 1:2] = every[:count]
-    keep_ref[...] = mixed[:count]
-    send_ref[:count, :] = mixed[count:].astype(jnp.bfloat16)
-    pieces = halves(as_row(earlier[count:])) + halves(as_row(every[count:]))
+def send_kernel(unit_ref, side_ref, old_sums_ref, old_mixed_ref, *refs):
+    blocks, send_ref = refs[:-1], refs[-1]
+    count, width = send_ref.shape[0] - EXTRA, send_ref.shape[1]
+    earlier, every, mixed = score(unit_ref[count:, :], side_ref[count:, :], blocks)
+    earlier += old_sums_ref[count:, 0:1]
+    every += old_sums_ref[count:, 1:2]
+    send_ref[:count, :] = (mixed + old_mixed_ref[count:, :]).astype(jnp.bfloat16)
+    pieces = halves(as_row(earlier)) + halves(as_row(every))
     pieces = [piece.astype(jnp.float32) for piece in pieces]
     pieces.append(jnp.zeros((1, width - 4 * count), jnp.float32))
     line = jnp.concatenate(pieces, axis=1)
     send_ref[count:, :] = jnp.broadcast_to(line, (EXTRA, width)).astype(jnp.bfloat16)
+
+
+def keep_kernel(unit_ref, side_ref, old_sums_ref, old_mixed_ref, *refs):
+    blocks, (sums_ref, mixed_ref) = refs[:-2], refs[-2:]
+    count = mixed_ref.shape[0]
+    earlier, every, mixed = score(unit_ref[:count, :], side_ref[:count, :], blocks)
+    sums_ref[...] = old_sums_ref[:count, :]
+    sums_ref[:, 0:1] += earlier
+    sums_ref[:, 1:2] += every
+    mixed_ref[...] = old_mixed_ref[:count, :] + mixed
 
 
 def combine_kernel(sums_ref, mixed_ref, got_ref, dup_ref, out_ref):
@@ -207,17 +212,21 @@
         )(unit, side, sums, mixed, *blocks)
 
     def final(unit, side, sums, mixed, *blocks):
-        return pl.pallas_call(
-            final_kernel,
-            out_shape=[
-                shape(count, 128),
-                shape(count, width),
-                shape(count + EXTRA, width, dtype=bf16),
-            ],
-            cost_estimate=cost(queries, len(blocks) * count, width),
-            compiler_params=params,
-            name="final_scores",
+        send = pl.pallas_call(
+            send_kernel,
+            out_shape=shape(count + EXTRA, width, dtype=bf16),
+            cost_estimate=cost(count, len(blocks) * count, width),
+            compiler_params=params,
+            name="send_scores",
         )(unit, side, sums, mixed, *blocks)
+        keep_sums, keep = pl.pallas_call(
+            keep_kernel,
+            out_shape=[shape(count, 128), shape(count, width)],
+            cost_estimate=cost(count, len(blocks) * count, width),
+            compiler_params=params,
+            name="keep_scores",
+        )(unit, side, sums, mixed, *blocks)
+        return keep_sums, keep, send
 
     pieces = embeddings.reshape(count // SUB, SUB, width // LANE, LANE).transpose(0, 2, 1, 3)
     own = pl.pallas_call(
@@ -237,8 +246,8 @@
         ahead_beside = across(ahead)
         other, moved_beside, opposite = lax.optimization_barrier((other, moved_beside, opposite))
         last = [two_ways(moved_beside, 1, opposite)]
-        unit, side, sums, mixed = first(own, other, beside, ahead, ahead_beside)
-        sums, mixed = more(unit, side, sums, mixed, moved, moved_beside, opposite)
+        unit, side, sums, mixed = first(own, other, beside, moved, moved_beside)
+        sums, mixed = more(unit, side, sums, mixed, ahead, opposite, ahead_beside)
     else:
         unit, side, sums, mixed = first(own, other, beside)
 

time: 30.5 us -> 29.8 us (0.977)
  waiting for transfers between devices: 10 us -> 8.96 us
  Pallas kernels: 3.84 us -> 4.24 us
    ppermute x3, waiting for transfers between devices: 2.77 us -> 1.58 us  [across(): return lax.ppermute(array, 'shard', [(at, at ^ 1) for at in range(shards)])]
    ppermute x1, waiting for transfers between devices: 0.01 us -> 0.62 us  [two_ways(): return lax.ppermute(source, ('shard', 'owner'), pairs)]
    ppermute x2, waiting for transfers between devices: 1.45 us -> 0.93 us  [swap(): lax.ppermute(array, 'owner', [(at, lanes - 1 - at) for at in range(lanes)])]
    pallas_call x1 -> x2, Pallas kernels: 0.63 us -> 1.04 us  [the longest x1 0.53 us: final(): pl.pallas_call(send_kernel, out_shape=shape(count + EXTRA, width, dtype=b...]
  transfers between devices with their start and end apart: 9 -> 9, of which waited for: 6 -> 7; matrix products, arithmetic and copies ran while one was open for 0% -> 0% of each run, Pallas kernels for 7% -> 9%
where the time goes in v17:
time: 29.8 us; the launch traced here: 29.7 us
  starting transfers between devices  14.1 us (47%)
  waiting for transfers between devices  8.96 us (30%)
  Pallas kernels  4.24 us (14%)
  local copies, waits for them, and re-layouts  1.58 us (5%)
  between operations  0.69 us (2%)
    ppermute x3, starting transfers between devices, along(): return lax.ppermute(array, 'shard', pairs)  6.42 us
    ppermute x3, waiting for transfers between devices, along(): return lax.ppermute(array, 'shard', pairs)  5.83 us
    ppermute x3, starting transfers between devices, across(): return lax.ppermute(array, 'shard', [(at, at ^ 1) for at in range(shards)])  5.29 us
    ppermute x1, starting transfers between devices, two_ways(): return lax.ppermute(source, ('shard', 'owner'), pairs)  2.35 us
    ppermute x3, waiting for transfers between devices, across(): return lax.ppermute(array, 'shard', [(at, at ^ 1) for at in range(shards)])  1.58 us
    unnamed x6, local copies, waits for them, and re-layouts  1.58 us
    pallas_call x1, Pallas kernels, first(): pl.pallas_call(first_kernel, out_shape=[shape(queries, width, dtype=bf16)...  1.18 us
    pallas_call x1, Pallas kernels, more(): pl.pallas_call(more_kernel, out_shape=[shape(queries, 128), shape(queries...  1.05 us
  transfers between devices with their start and end apart: 9, of which 7 were waited for; matrix products, arithmetic and copies ran while one was open for 0% of the time, Pallas kernels for 9%

profile of v17, /device:TPU:0, one launch (start us, length us, event | category | flops | bytes accessed | tf_op | source)
XLA Modules:
  0.0 29.7 jit_solution(8966017771339052277)
XLA Ops:
  0.6 0.0 copy-start.1
  0.6 0.0 copy-start.2
  0.6 0.6 %copy-done.1 = s32[128,1]{0,1:T(1,128)S(1)} copy-done((s32[128,1]{0,1:T(1,128)S(1)}, s32[128,1]{0,1:T(1,128)}, u32[]{:S(2)}) %copy-start.1) | copy-done | bytes 536
  1.3 0.0 copy-done.2
  1.3 0.0 copy-start
  1.3 0.9 %copy-done = bf16[128,768]{1,0:T(8,128)(2,1)S(1)} copy-done((bf16[128,768]{1,0:T(8,128)(2,1)S(1)}, bf16[128,768]{1,0:T(8,128)(2,1)}, u32[]{:S(2)}) %copy-start) | copy-done | bytes 196632
  2.3 4.1 %collective-permute-start = (bf16[97,8,128]{2,1,0:T(8,128)(2,1)S(1)}, bf16[97,8,128]{2,1,0:T(8,128)(2,1)S(1)}, u32[]{:S(2)}, u32[]{:S(2)}) collective-permute-start(bf16[97,8,128]{2,1,0:T(8,128)(2,1)S(1)} %pack.1.own_ref), channel_id=1, source_target_pairs={{0,8},{2,10},{8,12},{10,14},{12,4},{14,6},{4,0},{6,2},{1,9},{3,11}... | collective-permute-start | bytes 595976 | tf_op jit(solution)/shard_map/ppermute | solution.py:172
  6.3 1.5 %collective-permute-start.1 = (bf16[97,8,128]{2,1,0:T(8,128)(2,1)S(1)}, bf16[97,8,128]{2,1,0:T(8,128)(2,1)S(1)}, u32[]{:S(2)}, u32[]{:S(2)}) collective-permute-start(bf16[97,8,128]{2,1,0:T(8,128)(2,1)S(1)} %pack.1.own_ref), channel_id=1, source_target_pairs={{0,2},{2,0},{4,6},{6,4},{8,10},{10,8},{12,14},{14,12},{1,3},{3,1},... | collective-permute-start | bytes 595976 | tf_op jit(solution)/shard_map/ppermute | solution.py:175
  7.8 0.0 collective-permute-start.2
  7.8 0.0 collective-permute-start.5
  7.8 3.9 %collective-permute-done.refs_1_ = bf16[97,8,128]{2,1,0:T(8,128)(2,1)S(1)} collective-permute-done((bf16[97,8,128]{2,1,0:T(8,128)(2,1)S(1)}, bf16[97,8,128]{2,1,0:T(8,128)(2,1)S(1)}, u32[]{:S(2)}, u32[]{:S(2)}) %collective-permute-start) | collective-permute-done | bytes 198688 | tf_op jit(solution)/shard_map/ppermute | solution.py:172
  11.7 1.1 %collective-permute-done.1.refs_0_ = bf16[97,8,128]{2,1,0:T(8,128)(2,1)S(1)} collective-permute-done((bf16[97,8,128]{2,1,0:T(8,128)(2,1)S(1)}, bf16[97,8,128]{2,1,0:T(8,128)(2,1)S(1)}, u32[]{:S(2)}, u32[]{:S(2)}) %collective-permute-start.1) | collective-permute-done | bytes 198688 | tf_op jit(solution)/shard_map/ppermute | solution.py:175
  12.7 0.0 collective-permute-done.2.other_ref
  12.8 1.5 %collective-permute-start.3 = (bf16[97,8,128]{2,1,0:T(8,128)(2,1)S(1)}, bf16[97,8,128]{2,1,0:T(8,128)(2,1)S(1)}, u32[]{:S(2)}, u32[]{:S(2)}) collective-permute-start(bf16[97,8,128]{2,1,0:T(8,128)(2,1)S(1)} %collective-permute-done.refs_1_), channel_id=1, source_target_pairs={{0,2},{2,0},{4,6},{6,4},{8,10},{10,8},{12,14},{14,12},{1,3},{3,1},... | collective-permute-start | bytes 595976 | tf_op jit(solution)/shard_map/ppermute | solution.py:175
  14.2 2.3 %collective-permute-start.4 = (bf16[97,8,128]{2,1,0:T(8,128)(2,1)S(1)}, bf16[97,8,128]{2,1,0:T(8,128)(2,1)S(1)}, u32[]{:S(2)}, u32[]{:S(2)}) collective-permute-start(bf16[97,8,128]{2,1,0:T(8,128)(2,1)S(1)} %collective-permute-done.refs_1_), channel_id=1, source_target_pairs={{0,8},{2,10},{8,12},{10,14},{12,4},{14,6},{4,0},{6,2},{1,9},{3,11}... | collective-permute-start | bytes 595976 | tf_op jit(solution)/shard_map/ppermute | solution.py:172
  16.6 0.4 %collective-permute-done.5.refs_0_ = bf16[97,8,128]{2,1,0:T(8,128)(2,1)S(1)} collective-permute-done((bf16[97,8,128]{2,1,0:T(8,128)(2,1)S(1)}, bf16[97,8,128]{2,1,0:T(8,128)(2,1)S(1)}, u32[]{:S(2)}, u32[]{:S(2)}) %collective-permute-start.5) | collective-permute-done | bytes 198688 | tf_op jit(solution)/shard_map/ppermute | solution.py:172
  16.9 2.3 %collective-permute-start.6 = (bf16[97,8,128]{2,1,0:T(8,128)(2,1)S(1)}, bf16[97,8,128]{2,1,0:T(8,128)(2,1)S(1)}, u32[]{:S(2)}, u32[]{:S(2)}) collective-permute-start(bf16[97,8,128]{2,1,0:T(8,128)(2,1)S(1)} %collective-permute-done.5.refs_0_), channel_id=1, source_target_pairs={{0,2},{2,0},{4,6},{6,4},{8,10},{10,8},{12,14},{14,12},{1,3},{3,1},... | collective-permute-start | bytes 595976 | tf_op jit(solution)/shard_map/ppermute | solution.py:175
  19.2 0.0 collective-permute-done.3.refs_2_
  19.2 1.6 %collective-permute-done.4.refs_1_ = bf16[97,8,128]{2,1,0:T(8,128)(2,1)S(1)} collective-permute-done((bf16[97,8,128]{2,1,0:T(8,128)(2,1)S(1)}, bf16[97,8,128]{2,1,0:T(8,128)(2,1)S(1)}, u32[]{:S(2)}, u32[]{:S(2)}) %collective-permute-start.4) | collective-permute-done | bytes 198688 | tf_op jit(solution)/shard_map/ppermute | solution.py:172
  20.9 0.1 broadcast_select_fusion
  20.9 2.4 %collective-permute-start.7 = (bf16[97,8,128]{2,1,0:T(8,128)(2,1)S(1)}, bf16[97,8,128]{2,1,0:T(8,128)(2,1)S(1)}, u32[]{:S(2)}, u32[]{:S(2)}) collective-permute-start(bf16[97,8,128]{2,1,0:T(8,128)(2,1)S(1)} %broadcast_select_fusion), channel_id=1, source_target_pairs={{0,8},{1,3},{2,10},{3,1},{8,12},{9,11},{10,14},{11,9},{12,4},{13,1... | collective-permute-start | bytes 595976 | tf_op jit(solution)/shard_map/ppermute | solution.py:185
  23.3 1.2 %first_scores.1 = (bf16[256,768]{1,0:T(8,128)(2,1)S(1)}, f32[256,128]{1,0:T(8,128)S(1)}, f32[256,128]{1,0:T(8,128)S(1)}, f32[256,768]{1,0:T(8,128)S(1)}) custom-call(bf16[97,8,128]{2,1,0:T(8,128)(2,1)S(1)} %pack.1.own_ref, bf16[97,8,128]{2,1,0:T(8,128)(2,1)S(1)} %collective-permute-done.2.other_ref, bf16[97,8,128]{2,1,0:T(8,128)(2,1)S(1)} %collective-permute-done.1.refs_0_, ...), custom_call_target="tpu_custom_call" | custom-call | flops 40265318400 | bytes 2359296 | tf_op jit(solution)/shard_map/first_scores/pallas_call | solution.py:191
  24.5 0.5 %collective-permute-done.6.refs_2_ = bf16[97,8,128]{2,1,0:T(8,128)(2,1)S(1)} collective-permute-done((bf16[97,8,128]{2,1,0:T(8,128)(2,1)S(1)}, bf16[97,8,128]{2,1,0:T(8,128)(2,1)S(1)}, u32[]{:S(2)}, u32[]{:S(2)}) %collective-permute-start.6) | collective-permute-done | bytes 198688 | tf_op jit(solution)/shard_map/ppermute | solution.py:175
  25.0 1.0 %more_scores.1 = (f32[256,128]{1,0:T(8,128)S(1)}, f32[256,768]{1,0:T(8,128)S(1)}) custom-call(bf16[256,768]{1,0:T(8,128)(2,1)S(1)} %get-tuple-element.23.unit_ref, f32[256,128]{1,0:T(8,128)S(1)} %get-tuple-element.24.side_ref, f32[256,128]{1,0:T(8,128)S(1)} %get-tuple-element.25.old_sums_ref, ...), custom_call_target="tpu_custom_call", output_to_operand_aliasing={{0}: (2, {}), {1}: (3, {})} | custom-call | flops 30198988800 | bytes 2162688 | tf_op jit(solution)/shard_map/more_scores/pallas_call | solution.py:205
  26.0 0.6 %collective-permute-done.7.refs_0_ = bf16[97,8,128]{2,1,0:T(8,128)(2,1)S(1)} collective-permute-done((bf16[97,8,128]{2,1,0:T(8,128)(2,1)S(1)}, bf16[97,8,128]{2,1,0:T(8,128)(2,1)S(1)}, u32[]{:S(2)}, u32[]{:S(2)}) %collective-permute-start.7) | collective-permute-done | bytes 198688 | tf_op jit(solution)/shard_map/ppermute | solution.py:185
  26.7 0.5 %send_scores.1 = bf16[136,768]{1,0:T(8,128)(2,1)S(1)} custom-call(bf16[256,768]{1,0:T(8,128)(2,1)S(1)} %get-tuple-element.23.unit_ref, f32[256,128]{1,0:T(8,128)S(1)} %get-tuple-element.24.side_ref, f32[256,128]{1,0:T(8,128)S(1)} %get-tuple-element.28.old_sums_ref, f32[256,768]{1,0:T(8,128)S(1)} %get-tuple-element.29.old_mixed_ref, ...), custom_call_target="tpu_custom_call" | custom-call | flops 5033164800 | bytes 983040 | tf_op jit(solution)/shard_map/send_scores/pallas_call | solution.py:215
  27.2 0.1 collective-permute-start.8
  27.3 0.5 %keep_scores.1 = (f32[128,128]{1,0:T(8,128)S(1)}, f32[128,768]{1,0:T(8,128)S(1)}) custom-call(bf16[256,768]{1,0:T(8,128)(2,1)S(1)} %get-tuple-element.23.unit_ref, f32[256,128]{1,0:T(8,128)S(1)} %get-tuple-element.24.side_ref, f32[256,128]{1,0:T(8,128)S(1)} %get-tuple-element.28.old_sums_ref, f32[256,768]{1,0:T(8,128)S(1)} %get-tuple-element.29.old_mixed_ref, ...), custom_call_target="tpu_custom_call" | custom-call | flops 5033164800 | bytes 983040 | tf_op jit(solution)/shard_map/keep_scores/pallas_call | solution.py:222
  27.8 0.9 %collective-permute-done.8.got_ref = bf16[136,768]{1,0:T(8,128)(2,1)S(1)} collective-permute-done((bf16[136,768]{1,0:T(8,128)(2,1)S(1)}, bf16[136,768]{1,0:T(8,128)(2,1)S(1)}, u32[]{:S(2)}, u32[]{:S(2)}) %collective-permute-start.8) | collective-permute-done | bytes 208928 | tf_op jit(solution)/shard_map/ppermute | solution.py:188
  28.7 1.0 %combine.1 = (f32[1,128]{1,0:T(1,128)}, f32[128,768]{1,0:T(8,128)}) custom-call(f32[128,128]{1,0:T(8,128)S(1)} %get-tuple-element.30.sums_ref, f32[128,768]{1,0:T(8,128)S(1)} %get-tuple-element.31.mixed_ref, bf16[136,768]{1,0:T(8,128)(2,1)S(1)} %collective-permute-done.8.got_ref), custom_call_target="tpu_custom_call" | custom-call | tf_op jit(solution)/shard_map/combine/pallas_call | solution.py:263
  (1 shorter events, 0.0 us)
Async XLA Ops:
  0.6 0.7 %copy-start.1 = (s32[128,1]{0,1:T(1,128)S(1)}, s32[128,1]{0,1:T(1,128)}, u32[]{:S(2)}) copy-start(s32[128,1]{0,1:T(1,128)} %param.4) | copy-start | bytes 1540
  0.6 0.7 %copy-start.2 = (s32[128]{0:T(128)S(1)}, s32[128]{0:T(128)}, u32[]{:S(2)}) copy-start(s32[128]{0:T(128)} %param.5) | copy-start | bytes 1540
  1.3 0.9 %copy-start = (bf16[128,768]{1,0:T(8,128)(2,1)S(1)}, bf16[128,768]{1,0:T(8,128)(2,1)}, u32[]{:S(2)}) copy-start(bf16[128,768]{1,0:T(8,128)(2,1)} %param.3) | copy-start | bytes 589828
  2.3 9.4 %collective-permute-start = (bf16[97,8,128]{2,1,0:T(8,128)(2,1)S(1)}, bf16[97,8,128]{2,1,0:T(8,128)(2,1)S(1)}, u32[]{:S(2)}, u32[]{:S(2)}) collective-permute-start(bf16[97,8,128]{2,1,0:T(8,128)(2,1)S(1)} %pack.1.own_ref), channel_id=1, source_target_pairs={{0,8},{2,10},{8,12},{10,14},{12,4},{14,6},{4,0},{6,2},{1,9},{3,11}... | collective-permute-start | bytes 595976 | tf_op jit(solution)/shard_map/ppermute | solution.py:172
  6.3 6.4 %collective-permute-start.1 = (bf16[97,8,128]{2,1,0:T(8,128)(2,1)S(1)}, bf16[97,8,128]{2,1,0:T(8,128)(2,1)S(1)}, u32[]{:S(2)}, u32[]{:S(2)}) collective-permute-start(bf16[97,8,128]{2,1,0:T(8,128)(2,1)S(1)} %pack.1.own_ref), channel_id=1, source_target_pairs={{0,2},{2,0},{4,6},{6,4},{8,10},{10,8},{12,14},{14,12},{1,3},{3,1},... | collective-permute-start | bytes 595976 | tf_op jit(solution)/shard_map/ppermute | solution.py:175
  7.8 4.9 %collective-permute-start.2 = (bf16[97,8,128]{2,1,0:T(8,128)(2,1)S(1)}, bf16[97,8,128]{2,1,0:T(8,128)(2,1)S(1)}, u32[]{:S(2)}, u32[]{:S(2)}) collective-permute-start(bf16[97,8,128]{2,1,0:T(8,128)(2,1)S(1)} %pack.1.own_ref), channel_id=1, source_target_pairs={{0,1},{1,0},{2,3},{3,2},{4,5},{5,4},{6,7},{7,6},{8,9},{9,8},{10,11... | collective-permute-start | bytes 595976 | tf_op jit(solution)/shard_map/ppermute | solution.py:188
  7.8 9.1 %collective-permute-start.5 = (bf16[97,8,128]{2,1,0:T(8,128)(2,1)S(1)}, bf16[97,8,128]{2,1,0:T(8,128)(2,1)S(1)}, u32[]{:S(2)}, u32[]{:S(2)}) collective-permute-start(bf16[97,8,128]{2,1,0:T(8,128)(2,1)S(1)} %pack.1.own_ref), channel_id=1, source_target_pairs={{0,4},{2,6},{8,0},{10,2},{12,8},{14,10},{4,12},{6,14},{1,5},{3,7},... | collective-permute-start | bytes 595976 | tf_op jit(solution)/shard_map/ppermute | solution.py:172
  12.8 6.5 %collective-permute-start.3 = (bf16[97,8,128]{2,1,0:T(8,128)(2,1)S(1)}, bf16[97,8,128]{2,1,0:T(8,128)(2,1)S(1)}, u32[]{:S(2)}, u32[]{:S(2)}) collective-permute-start(bf16[97,8,128]{2,1,0:T(8,128)(2,1)S(1)} %collective-permute-done.refs_1_), channel_id=1, source_target_pairs={{0,2},{2,0},{4,6},{6,4},{8,10},{10,8},{12,14},{14,12},{1,3},{3,1},... | collective-permute-start | bytes 595976 | tf_op jit(solution)/shard_map/ppermute | solution.py:175
  14.2 6.6 %collective-permute-start.4 = (bf16[97,8,128]{2,1,0:T(8,128)(2,1)S(1)}, bf16[97,8,128]{2,1,0:T(8,128)(2,1)S(1)}, u32[]{:S(2)}, u32[]{:S(2)}) collective-permute-start(bf16[97,8,128]{2,1,0:T(8,128)(2,1)S(1)} %collective-permute-done.refs_1_), channel_id=1, source_target_pairs={{0,8},{2,10},{8,12},{10,14},{12,4},{14,6},{4,0},{6,2},{1,9},{3,11}... | collective-permute-start | bytes 595976 | tf_op jit(solution)/shard_map/ppermute | solution.py:172
  16.9 8.1 %collective-permute-start.6 = (bf16[97,8,128]{2,1,0:T(8,128)(2,1)S(1)}, bf16[97,8,128]{2,1,0:T(8,128)(2,1)S(1)}, u32[]{:S(2)}, u32[]{:S(2)}) collective-permute-start(bf16[97,8,128]{2,1,0:T(8,128)(2,1)S(1)} %collective-permute-done.5.refs_0_), channel_id=1, source_target_pairs={{0,2},{2,0},{4,6},{6,4},{8,10},{10,8},{12,14},{14,12},{1,3},{3,1},... | collective-permute-start | bytes 595976 | tf_op jit(solution)/shard_map/ppermute | solution.py:175
  20.9 5.7 %collective-permute-start.7 = (bf16[97,8,128]{2,1,0:T(8,128)(2,1)S(1)}, bf16[97,8,128]{2,1,0:T(8,128)(2,1)S(1)}, u32[]{:S(2)}, u32[]{:S(2)}) collective-permute-start(bf16[97,8,128]{2,1,0:T(8,128)(2,1)S(1)} %broadcast_select_fusion), channel_id=1, source_target_pairs={{0,8},{1,3},{2,10},{3,1},{8,12},{9,11},{10,14},{11,9},{12,4},{13,1... | collective-permute-start | bytes 595976 | tf_op jit(solution)/shard_map/ppermute | solution.py:185
  27.2 1.5 %collective-permute-start.8 = (bf16[136,768]{1,0:T(8,128)(2,1)S(1)}, bf16[136,768]{1,0:T(8,128)(2,1)S(1)}, u32[]{:S(2)}, u32[]{:S(2)}) collective-permute-start(bf16[136,768]{1,0:T(8,128)(2,1)S(1)} %send_scores.1), channel_id=1, source_target_pairs={{0,1},{1,0},{2,3},{3,2},{4,5},{5,4},{6,7},{7,6},{8,9},{9,8},{10,11... | collective-permute-start | bytes 626696 | tf_op jit(solution)/shard_map/ppermute | solution.py:188

commit v18 on v17

--- a/solution.py
+++ b/solution.py
@@ -36,14 +36,18 @@
     return high, (value - high.astype(jnp.float32)).astype(jnp.bfloat16)
 
 
-def pack_kernel(tiles_ref, label_ref, rank_ref, packed_ref):
+def base_kernel(base_ref):
+    base_ref[...] = jnp.zeros_like(base_ref)
+
+
+def pack_kernel(tiles_ref, label_ref, rank_ref, base_ref, packed_ref):
     many = tiles_ref.shape[0]
     packed_ref[:many] = tiles_ref[...]
     rank = rank_ref[...]
     high = lax.shift_right_logical(rank, 8)
     low = rank - lax.shift_left(high, 8)
     lines = [line.astype(jnp.float32) for line in (label_ref[...], high, low)]
-    lines.append(jnp.zeros((SUB - len(lines), LANE), jnp.float32))
+    lines.append(base_ref[len(lines) :, :])
     packed_ref[many] = jnp.concatenate(lines, axis=0).astype(jnp.bfloat16)
 
 
@@ -229,12 +233,19 @@
         return keep_sums, keep, send
 
     pieces = embeddings.reshape(count // SUB, SUB, width // LANE, LANE).transpose(0, 2, 1, 3)
+    base = pl.pallas_call(
+        base_kernel,
+        out_shape=shape(SUB, LANE),
+        cost_estimate=pl.CostEstimate(flops=1000000000, bytes_accessed=0, transcendentals=0),
+        compiler_params=params,
+        name="base",
+    )()
     own = pl.pallas_call(
         pack_kernel,
         out_shape=shape(tiles + 1, SUB, LANE, dtype=bf16),
         compiler_params=params,
         name="pack",
-    )(pieces.reshape(tiles, SUB, LANE), cluster_id.reshape(1, count), priority.reshape(1, count))
+    )(pieces.reshape(tiles, SUB, LANE), cluster_id.reshape(1, count), priority.reshape(1, count), base)
 
     moved, beside = along(own, 1), across(own)
     other = swap(own)

time: 29.8 us -> 29.2 us (0.980)
  local copies, waits for them, and re-layouts: 1.58 us -> 0.9 us
    unnamed x6, local copies, waits for them, and re-layouts: 1.58 us -> 0.9 us
where the time goes in v18:
time: 29.2 us; the launch traced here: 29 us
  starting transfers between devices  14.1 us (48%)
  waiting for transfers between devices  8.96 us (31%)
  Pallas kernels  4.24 us (15%)
  local copies, waits for them, and re-layouts  0.9 us (3%)
  between operations  0.71 us (2%)
    ppermute x3, starting transfers between devices, along(): return lax.ppermute(array, 'shard', pairs)  6.42 us
    ppermute x3, waiting for transfers between devices, along(): return lax.ppermute(array, 'shard', pairs)  5.83 us
    ppermute x3, starting transfers between devices, across(): return lax.ppermute(array, 'shard', [(at, at ^ 1) for at in range(shards)])  5.29 us
    ppermute x1, starting transfers between devices, two_ways(): return lax.ppermute(source, ('shard', 'owner'), pairs)  2.35 us
    ppermute x3, waiting for transfers between devices, across(): return lax.ppermute(array, 'shard', [(at, at ^ 1) for at in range(shards)])  1.59 us
    pallas_call x1, Pallas kernels, first(): pl.pallas_call(first_kernel, out_shape=[shape(queries, width, dtype=bf16)...  1.18 us
    pallas_call x1, Pallas kernels, more(): pl.pallas_call(more_kernel, out_shape=[shape(queries, 128), shape(queries...  1.04 us
    pallas_call x1, Pallas kernels, local(): pl.pallas_call(combine_kernel, out_shape=[shape(1, count), shape(count, w...  0.95 us
  transfers between devices with their start and end apart: 9, of which 7 were waited for; matrix products, arithmetic and copies ran while one was open for 0% of the time, Pallas kernels for 9%

profile of v18, /device:TPU:0, one launch (start us, length us, event | category | flops | bytes accessed | tf_op | source)
XLA Modules:
  0.0 29.0 jit_solution(10484236036641816430)
XLA Ops:
  0.6 0.0 copy-start
  0.6 0.0 copy-start.1
  0.7 0.0 copy-start.2
  0.7 0.9 %copy-done = bf16[128,768]{1,0:T(8,128)(2,1)S(1)} copy-done((bf16[128,768]{1,0:T(8,128)(2,1)S(1)}, bf16[128,768]{1,0:T(8,128)(2,1)}, u32[]{:S(2)}) %copy-start) | copy-done | bytes 196632
  1.6 0.0 copy-done.1
  1.6 0.0 copy-done.2
  1.6 4.1 %collective-permute-start = (bf16[97,8,128]{2,1,0:T(8,128)(2,1)S(1)}, bf16[97,8,128]{2,1,0:T(8,128)(2,1)S(1)}, u32[]{:S(2)}, u32[]{:S(2)}) collective-permute-start(bf16[97,8,128]{2,1,0:T(8,128)(2,1)S(1)} %pack.1.own_ref), channel_id=1, source_target_pairs={{0,8},{2,10},{8,12},{10,14},{12,4},{14,6},{4,0},{6,2},{1,9},{3,11}... | collective-permute-start | bytes 595976 | tf_op jit(solution)/shard_map/ppermute | solution.py:176
  5.7 1.5 %collective-permute-start.1 = (bf16[97,8,128]{2,1,0:T(8,128)(2,1)S(1)}, bf16[97,8,128]{2,1,0:T(8,128)(2,1)S(1)}, u32[]{:S(2)}, u32[]{:S(2)}) collective-permute-start(bf16[97,8,128]{2,1,0:T(8,128)(2,1)S(1)} %pack.1.own_ref), channel_id=1, source_target_pairs={{0,2},{2,0},{4,6},{6,4},{8,10},{10,8},{12,14},{14,12},{1,3},{3,1},... | collective-permute-start | bytes 595976 | tf_op jit(solution)/shard_map/ppermute | solution.py:179
  7.2 0.0 collective-permute-start.2
  7.2 0.0 collective-permute-start.5
  7.2 3.9 %collective-permute-done.refs_1_ = bf16[97,8,128]{2,1,0:T(8,128)(2,1)S(1)} collective-permute-done((bf16[97,8,128]{2,1,0:T(8,128)(2,1)S(1)}, bf16[97,8,128]{2,1,0:T(8,128)(2,1)S(1)}, u32[]{:S(2)}, u32[]{:S(2)}) %collective-permute-start) | collective-permute-done | bytes 198688 | tf_op jit(solution)/shard_map/ppermute | solution.py:176
  11.0 1.1 %collective-permute-done.1.refs_0_ = bf16[97,8,128]{2,1,0:T(8,128)(2,1)S(1)} collective-permute-done((bf16[97,8,128]{2,1,0:T(8,128)(2,1)S(1)}, bf16[97,8,128]{2,1,0:T(8,128)(2,1)S(1)}, u32[]{:S(2)}, u32[]{:S(2)}) %collective-permute-start.1) | collective-permute-done | bytes 198688 | tf_op jit(solution)/shard_map/ppermute | solution.py:179
  12.1 0.0 collective-permute-done.2.other_ref
  12.1 1.5 %collective-permute-start.3 = (bf16[97,8,128]{2,1,0:T(8,128)(2,1)S(1)}, bf16[97,8,128]{2,1,0:T(8,128)(2,1)S(1)}, u32[]{:S(2)}, u32[]{:S(2)}) collective-permute-start(bf16[97,8,128]{2,1,0:T(8,128)(2,1)S(1)} %collective-permute-done.refs_1_), channel_id=1, source_target_pairs={{0,2},{2,0},{4,6},{6,4},{8,10},{10,8},{12,14},{14,12},{1,3},{3,1},... | collective-permute-start | bytes 595976 | tf_op jit(solution)/shard_map/ppermute | solution.py:179
  13.6 2.3 %collective-permute-start.4 = (bf16[97,8,128]{2,1,0:T(8,128)(2,1)S(1)}, bf16[97,8,128]{2,1,0:T(8,128)(2,1)S(1)}, u32[]{:S(2)}, u32[]{:S(2)}) collective-permute-start(bf16[97,8,128]{2,1,0:T(8,128)(2,1)S(1)} %collective-permute-done.refs_1_), channel_id=1, source_target_pairs={{0,8},{2,10},{8,12},{10,14},{12,4},{14,6},{4,0},{6,2},{1,9},{3,11}... | collective-permute-start | bytes 595976 | tf_op jit(solution)/shard_map/ppermute | solution.py:176
  15.9 0.4 %collective-permute-done.5.refs_0_ = bf16[97,8,128]{2,1,0:T(8,128)(2,1)S(1)} collective-permute-done((bf16[97,8,128]{2,1,0:T(8,128)(2,1)S(1)}, bf16[97,8,128]{2,1,0:T(8,128)(2,1)S(1)}, u32[]{:S(2)}, u32[]{:S(2)}) %collective-permute-start.5) | collective-permute-done | bytes 198688 | tf_op jit(solution)/shard_map/ppermute | solution.py:176
  16.3 2.3 %collective-permute-start.6 = (bf16[97,8,128]{2,1,0:T(8,128)(2,1)S(1)}, bf16[97,8,128]{2,1,0:T(8,128)(2,1)S(1)}, u32[]{:S(2)}, u32[]{:S(2)}) collective-permute-start(bf16[97,8,128]{2,1,0:T(8,128)(2,1)S(1)} %collective-permute-done.5.refs_0_), channel_id=1, source_target_pairs={{0,2},{2,0},{4,6},{6,4},{8,10},{10,8},{12,14},{14,12},{1,3},{3,1},... | collective-permute-start | bytes 595976 | tf_op jit(solution)/shard_map/ppermute | solution.py:179
  18.6 0.0 collective-permute-done.3.refs_2_
  18.6 1.6 %collective-permute-done.4.refs_1_ = bf16[97,8,128]{2,1,0:T(8,128)(2,1)S(1)} collective-permute-done((bf16[97,8,128]{2,1,0:T(8,128)(2,1)S(1)}, bf16[97,8,128]{2,1,0:T(8,128)(2,1)S(1)}, u32[]{:S(2)}, u32[]{:S(2)}) %collective-permute-start.4) | collective-permute-done | bytes 198688 | tf_op jit(solution)/shard_map/ppermute | solution.py:176
  20.2 0.1 broadcast_select_fusion
  20.3 2.4 %collective-permute-start.7 = (bf16[97,8,128]{2,1,0:T(8,128)(2,1)S(1)}, bf16[97,8,128]{2,1,0:T(8,128)(2,1)S(1)}, u32[]{:S(2)}, u32[]{:S(2)}) collective-permute-start(bf16[97,8,128]{2,1,0:T(8,128)(2,1)S(1)} %broadcast_select_fusion), channel_id=1, source_target_pairs={{0,8},{1,3},{2,10},{3,1},{8,12},{9,11},{10,14},{11,9},{12,4},{13,1... | collective-permute-start | bytes 595976 | tf_op jit(solution)/shard_map/ppermute | solution.py:189
  22.6 1.2 %first_scores.1 = (bf16[256,768]{1,0:T(8,128)(2,1)S(1)}, f32[256,128]{1,0:T(8,128)S(1)}, f32[256,128]{1,0:T(8,128)S(1)}, f32[256,768]{1,0:T(8,128)S(1)}) custom-call(bf16[97,8,128]{2,1,0:T(8,128)(2,1)S(1)} %pack.1.own_ref, bf16[97,8,128]{2,1,0:T(8,128)(2,1)S(1)} %collective-permute-done.2.other_ref, bf16[97,8,128]{2,1,0:T(8,128)(2,1)S(1)} %collective-permute-done.1.refs_0_, ...), custom_call_target="tpu_custom_call" | custom-call | flops 40265318400 | bytes 2359296 | tf_op jit(solution)/shard_map/first_scores/pallas_call | solution.py:195
  23.8 0.5 %collective-permute-done.6.refs_2_ = bf16[97,8,128]{2,1,0:T(8,128)(2,1)S(1)} collective-permute-done((bf16[97,8,128]{2,1,0:T(8,128)(2,1)S(1)}, bf16[97,8,128]{2,1,0:T(8,128)(2,1)S(1)}, u32[]{:S(2)}, u32[]{:S(2)}) %collective-permute-start.6) | collective-permute-done | bytes 198688 | tf_op jit(solution)/shard_map/ppermute | solution.py:179
  24.3 1.0 %more_scores.1 = (f32[256,128]{1,0:T(8,128)S(1)}, f32[256,768]{1,0:T(8,128)S(1)}) custom-call(bf16[256,768]{1,0:T(8,128)(2,1)S(1)} %get-tuple-element.23.unit_ref, f32[256,128]{1,0:T(8,128)S(1)} %get-tuple-element.24.side_ref, f32[256,128]{1,0:T(8,128)S(1)} %get-tuple-element.25.old_sums_ref, ...), custom_call_target="tpu_custom_call", output_to_operand_aliasing={{0}: (2, {}), {1}: (3, {})} | custom-call | flops 30198988800 | bytes 2162688 | tf_op jit(solution)/shard_map/more_scores/pallas_call | solution.py:209
  25.4 0.6 %collective-permute-done.7.refs_0_ = bf16[97,8,128]{2,1,0:T(8,128)(2,1)S(1)} collective-permute-done((bf16[97,8,128]{2,1,0:T(8,128)(2,1)S(1)}, bf16[97,8,128]{2,1,0:T(8,128)(2,1)S(1)}, u32[]{:S(2)}, u32[]{:S(2)}) %collective-permute-start.7) | collective-permute-done | bytes 198688 | tf_op jit(solution)/shard_map/ppermute | solution.py:189
  26.0 0.5 %send_scores.1 = bf16[136,768]{1,0:T(8,128)(2,1)S(1)} custom-call(bf16[256,768]{1,0:T(8,128)(2,1)S(1)} %get-tuple-element.23.unit_ref, f32[256,128]{1,0:T(8,128)S(1)} %get-tuple-element.24.side_ref, f32[256,128]{1,0:T(8,128)S(1)} %get-tuple-element.28.old_sums_ref, f32[256,768]{1,0:T(8,128)S(1)} %get-tuple-element.29.old_mixed_ref, ...), custom_call_target="tpu_custom_call" | custom-call | flops 5033164800 | bytes 983040 | tf_op jit(solution)/shard_map/send_scores/pallas_call | solution.py:219
  26.5 0.1 collective-permute-start.8
  26.6 0.5 %keep_scores.1 = (f32[128,128]{1,0:T(8,128)S(1)}, f32[128,768]{1,0:T(8,128)S(1)}) custom-call(bf16[256,768]{1,0:T(8,128)(2,1)S(1)} %get-tuple-element.23.unit_ref, f32[256,128]{1,0:T(8,128)S(1)} %get-tuple-element.24.side_ref, f32[256,128]{1,0:T(8,128)S(1)} %get-tuple-element.28.old_sums_ref, f32[256,768]{1,0:T(8,128)S(1)} %get-tuple-element.29.old_mixed_ref, ...), custom_call_target="tpu_custom_call" | custom-call | flops 5033164800 | bytes 983040 | tf_op jit(solution)/shard_map/keep_scores/pallas_call | solution.py:226
  27.1 0.9 %collective-permute-done.8.got_ref = bf16[136,768]{1,0:T(8,128)(2,1)S(1)} collective-permute-done((bf16[136,768]{1,0:T(8,128)(2,1)S(1)}, bf16[136,768]{1,0:T(8,128)(2,1)S(1)}, u32[]{:S(2)}, u32[]{:S(2)}) %collective-permute-start.8) | collective-permute-done | bytes 208928 | tf_op jit(solution)/shard_map/ppermute | solution.py:192
  28.1 1.0 %combine.1 = (f32[1,128]{1,0:T(1,128)}, f32[128,768]{1,0:T(8,128)}) custom-call(f32[128,128]{1,0:T(8,128)S(1)} %get-tuple-element.30.sums_ref, f32[128,768]{1,0:T(8,128)S(1)} %get-tuple-element.31.mixed_ref, bf16[136,768]{1,0:T(8,128)(2,1)S(1)} %collective-permute-done.8.got_ref), custom_call_target="tpu_custom_call" | custom-call | tf_op jit(solution)/shard_map/combine/pallas_call | solution.py:274
  (2 shorter events, 0.0 us)
Async XLA Ops:
  0.6 0.9 %copy-start = (bf16[128,768]{1,0:T(8,128)(2,1)S(1)}, bf16[128,768]{1,0:T(8,128)(2,1)}, u32[]{:S(2)}) copy-start(bf16[128,768]{1,0:T(8,128)(2,1)} %param.3) | copy-start | bytes 589828
  0.6 0.9 %copy-start.1 = (s32[128,1]{0,1:T(1,128)S(1)}, s32[128,1]{0,1:T(1,128)}, u32[]{:S(2)}) copy-start(s32[128,1]{0,1:T(1,128)} %param.4) | copy-start | bytes 1540
  0.7 0.9 %copy-start.2 = (s32[128]{0:T(128)S(1)}, s32[128]{0:T(128)}, u32[]{:S(2)}) copy-start(s32[128]{0:T(128)} %param.5) | copy-start | bytes 1540
  1.6 9.4 %collective-permute-start = (bf16[97,8,128]{2,1,0:T(8,128)(2,1)S(1)}, bf16[97,8,128]{2,1,0:T(8,128)(2,1)S(1)}, u32[]{:S(2)}, u32[]{:S(2)}) collective-permute-start(bf16[97,8,128]{2,1,0:T(8,128)(2,1)S(1)} %pack.1.own_ref), channel_id=1, source_target_pairs={{0,8},{2,10},{8,12},{10,14},{12,4},{14,6},{4,0},{6,2},{1,9},{3,11}... | collective-permute-start | bytes 595976 | tf_op jit(solution)/shard_map/ppermute | solution.py:176
  5.7 6.4 %collective-permute-start.1 = (bf16[97,8,128]{2,1,0:T(8,128)(2,1)S(1)}, bf16[97,8,128]{2,1,0:T(8,128)(2,1)S(1)}, u32[]{:S(2)}, u32[]{:S(2)}) collective-permute-start(bf16[97,8,128]{2,1,0:T(8,128)(2,1)S(1)} %pack.1.own_ref), channel_id=1, source_target_pairs={{0,2},{2,0},{4,6},{6,4},{8,10},{10,8},{12,14},{14,12},{1,3},{3,1},... | collective-permute-start | bytes 595976 | tf_op jit(solution)/shard_map/ppermute | solution.py:179
  7.2 4.9 %collective-permute-start.2 = (bf16[97,8,128]{2,1,0:T(8,128)(2,1)S(1)}, bf16[97,8,128]{2,1,0:T(8,128)(2,1)S(1)}, u32[]{:S(2)}, u32[]{:S(2)}) collective-permute-start(bf16[97,8,128]{2,1,0:T(8,128)(2,1)S(1)} %pack.1.own_ref), channel_id=1, source_target_pairs={{0,1},{1,0},{2,3},{3,2},{4,5},{5,4},{6,7},{7,6},{8,9},{9,8},{10,11... | collective-permute-start | bytes 595976 | tf_op jit(solution)/shard_map/ppermute | solution.py:192
  7.2 9.1 %collective-permute-start.5 = (bf16[97,8,128]{2,1,0:T(8,128)(2,1)S(1)}, bf16[97,8,128]{2,1,0:T(8,128)(2,1)S(1)}, u32[]{:S(2)}, u32[]{:S(2)}) collective-permute-start(bf16[97,8,128]{2,1,0:T(8,128)(2,1)S(1)} %pack.1.own_ref), channel_id=1, source_target_pairs={{0,4},{2,6},{8,0},{10,2},{12,8},{14,10},{4,12},{6,14},{1,5},{3,7},... | collective-permute-start | bytes 595976 | tf_op jit(solution)/shard_map/ppermute | solution.py:176
  12.1 6.5 %collective-permute-start.3 = (bf16[97,8,128]{2,1,0:T(8,128)(2,1)S(1)}, bf16[97,8,128]{2,1,0:T(8,128)(2,1)S(1)}, u32[]{:S(2)}, u32[]{:S(2)}) collective-permute-start(bf16[97,8,128]{2,1,0:T(8,128)(2,1)S(1)} %collective-permute-done.refs_1_), channel_id=1, source_target_pairs={{0,2},{2,0},{4,6},{6,4},{8,10},{10,8},{12,14},{14,12},{1,3},{3,1},... | collective-permute-start | bytes 595976 | tf_op jit(solution)/shard_map/ppermute | solution.py:179
  13.6 6.6 %collective-permute-start.4 = (bf16[97,8,128]{2,1,0:T(8,128)(2,1)S(1)}, bf16[97,8,128]{2,1,0:T(8,128)(2,1)S(1)}, u32[]{:S(2)}, u32[]{:S(2)}) collective-permute-start(bf16[97,8,128]{2,1,0:T(8,128)(2,1)S(1)} %collective-permute-done.refs_1_), channel_id=1, source_target_pairs={{0,8},{2,10},{8,12},{10,14},{12,4},{14,6},{4,0},{6,2},{1,9},{3,11}... | collective-permute-start | bytes 595976 | tf_op jit(solution)/shard_map/ppermute | solution.py:176
  16.3 8.1 %collective-permute-start.6 = (bf16[97,8,128]{2,1,0:T(8,128)(2,1)S(1)}, bf16[97,8,128]{2,1,0:T(8,128)(2,1)S(1)}, u32[]{:S(2)}, u32[]{:S(2)}) collective-permute-start(bf16[97,8,128]{2,1,0:T(8,128)(2,1)S(1)} %collective-permute-done.5.refs_0_), channel_id=1, source_target_pairs={{0,2},{2,0},{4,6},{6,4},{8,10},{10,8},{12,14},{14,12},{1,3},{3,1},... | collective-permute-start | bytes 595976 | tf_op jit(solution)/shard_map/ppermute | solution.py:179
  20.3 5.7 %collective-permute-start.7 = (bf16[97,8,128]{2,1,0:T(8,128)(2,1)S(1)}, bf16[97,8,128]{2,1,0:T(8,128)(2,1)S(1)}, u32[]{:S(2)}, u32[]{:S(2)}) collective-permute-start(bf16[97,8,128]{2,1,0:T(8,128)(2,1)S(1)} %broadcast_select_fusion), channel_id=1, source_target_pairs={{0,8},{1,3},{2,10},{3,1},{8,12},{9,11},{10,14},{11,9},{12,4},{13,1... | collective-permute-start | bytes 595976 | tf_op jit(solution)/shard_map/ppermute | solution.py:189
  26.5 1.5 %collective-permute-start.8 = (bf16[136,768]{1,0:T(8,128)(2,1)S(1)}, bf16[136,768]{1,0:T(8,128)(2,1)S(1)}, u32[]{:S(2)}, u32[]{:S(2)}) collective-permute-start(bf16[136,768]{1,0:T(8,128)(2,1)S(1)} %send_scores.1), channel_id=1, source_target_pairs={{0,1},{1,0},{2,3},{3,2},{4,5},{5,4},{6,7},{7,6},{8,9},{9,8},{10,11... | collective-permute-start | bytes 626696 | tf_op jit(solution)/shard_map/ppermute | solution.py:192

commit v19 on v18

--- a/solution.py
+++ b/solution.py
@@ -178,15 +178,14 @@
     def across(array):
         return lax.ppermute(array, "shard", [(at, at ^ 1) for at in range(shards)])
 
-    def two_ways(by_ring, step, by_side):
+    def one_lane(array, lane, step):
         pairs = []
         for at in range(rounds):
             for side in range(2):
                 here, there = 2 * ring[at] + side, 2 * ring[(at + step) % rounds] + side
-                pairs.append((here * lanes, there * lanes))
-                pairs += [(here * lanes + lane, (here ^ 1) * lanes + lane) for lane in range(1, lanes)]
-        source = jnp.where(lax.axis_index("owner") == 0, by_ring, by_side)
-        return lax.ppermute(source, ("shard", "owner"), pairs)
+                there = there if step else here ^ 1
+                pairs.append((here * lanes + lane, there * lanes + lane))
+        return lax.ppermute(array, ("shard", "owner"), pairs)
 
     def swap(array):
         return lax.ppermute(array, "owner", [(at, lanes - 1 - at) for at in range(lanes)])
@@ -255,10 +254,11 @@
         opposite = along(moved, 1)
         moved_beside = across(moved)
         ahead_beside = across(ahead)
-        other, moved_beside, opposite = lax.optimization_barrier((other, moved_beside, opposite))
-        last = [two_ways(moved_beside, 1, opposite)]
+        by_ring = one_lane(moved_beside, 0, 1)
+        by_side = one_lane(opposite, lanes - 1, 0)
         unit, side, sums, mixed = first(own, other, beside, moved, moved_beside)
         sums, mixed = more(unit, side, sums, mixed, ahead, opposite, ahead_beside)
+        last = [jnp.where(lax.axis_index("owner") == 0, by_ring, by_side)]
     else:
         unit, side, sums, mixed = first(own, other, beside)
 

time: 29.2 us -> 29.7 us (1.017)
  starting transfers between devices: 14.1 us -> 17.1 us
  waiting for transfers between devices: 8.96 us -> 6.44 us
    ppermute x1 -> x2, starting transfers between devices: 2.35 us -> 5.34 us  [one_lane(): return lax.ppermute(array, ('shard', 'owner'), pairs)]
    ppermute x3, waiting for transfers between devices: 5.83 us -> 4.22 us  [along(): return lax.ppermute(array, 'shard', pairs)]
    ppermute x3, waiting for transfers between devices: 1.59 us -> 1.06 us  [across(): return lax.ppermute(array, 'shard', [(at, at ^ 1) for at in range(shards)])]
    ppermute x1 -> x2, waiting for transfers between devices: 0.62 us -> 0.23 us  [one_lane(): return lax.ppermute(array, ('shard', 'owner'), pairs)]
  transfers between devices with their start and end apart: 9 -> 10, of which waited for: 7 -> 5; matrix products, arithmetic and copies ran while one was open for 0% -> 0% of each run, Pallas kernels for 9% -> 9%
where the time goes in v19:
time: 29.7 us; the launch traced here: 29.5 us
  starting transfers between devices  17.1 us (58%)
  waiting for transfers between devices  6.44 us (22%)
  Pallas kernels  4.26 us (14%)
  local copies, waits for them, and re-layouts  0.9 us (3%)
  between operations  0.74 us (2%)
    ppermute x3, starting transfers between devices, along(): return lax.ppermute(array, 'shard', pairs)  6.42 us
    ppermute x2, starting transfers between devices, one_lane(): return lax.ppermute(array, ('shard', 'owner'), pairs)  5.34 us
    ppermute x3, starting transfers between devices, across(): return lax.ppermute(array, 'shard', [(at, at ^ 1) for at in range(shards)])  5.29 us
    ppermute x3, waiting for transfers between devices, along(): return lax.ppermute(array, 'shard', pairs)  4.22 us
    pallas_call x1, Pallas kernels, first(): pl.pallas_call(first_kernel, out_shape=[shape(queries, width, dtype=bf16)...  1.19 us
    ppermute x3, waiting for transfers between devices, across(): return lax.ppermute(array, 'shard', [(at, at ^ 1) for at in range(shards)])  1.06 us
    pallas_call x1, Pallas kernels, more(): pl.pallas_call(more_kernel, out_shape=[shape(queries, 128), shape(queries...  1.05 us
    pallas_call x1, Pallas kernels, local(): pl.pallas_call(combine_kernel, out_shape=[shape(1, count), shape(count, w...  0.95 us
  transfers between devices with their start and end apart: 10, of which 5 were waited for; matrix products, arithmetic and copies ran while one was open for 0% of the time, Pallas kernels for 9%

profile of v19, /device:TPU:0, one launch (start us, length us, event | category | flops | bytes accessed | tf_op | source)
XLA Modules:
  0.0 29.5 jit_solution(17883293352545192546)
XLA Ops:
  0.6 0.0 copy-start
  0.6 0.0 copy-start.1
  0.7 0.0 copy-start.2
  0.7 0.9 %copy-done = bf16[128,768]{1,0:T(8,128)(2,1)S(1)} copy-done((bf16[128,768]{1,0:T(8,128)(2,1)S(1)}, bf16[128,768]{1,0:T(8,128)(2,1)}, u32[]{:S(2)}) %copy-start) | copy-done | bytes 196632
  1.6 0.0 copy-done.1
  1.6 0.0 copy-done.2
  1.6 4.1 %collective-permute-start = (bf16[97,8,128]{2,1,0:T(8,128)(2,1)S(1)}, bf16[97,8,128]{2,1,0:T(8,128)(2,1)S(1)}, u32[]{:S(2)}, u32[]{:S(2)}) collective-permute-start(bf16[97,8,128]{2,1,0:T(8,128)(2,1)S(1)} %pack.1.own_ref), channel_id=1, source_target_pairs={{0,8},{2,10},{8,12},{10,14},{12,4},{14,6},{4,0},{6,2},{1,9},{3,11}... | collective-permute-start | bytes 595976 | tf_op jit(solution)/shard_map/ppermute | solution.py:176
  5.7 1.5 %collective-permute-start.1 = (bf16[97,8,128]{2,1,0:T(8,128)(2,1)S(1)}, bf16[97,8,128]{2,1,0:T(8,128)(2,1)S(1)}, u32[]{:S(2)}, u32[]{:S(2)}) collective-permute-start(bf16[97,8,128]{2,1,0:T(8,128)(2,1)S(1)} %pack.1.own_ref), channel_id=1, source_target_pairs={{0,2},{2,0},{4,6},{6,4},{8,10},{10,8},{12,14},{14,12},{1,3},{3,1},... | collective-permute-start | bytes 595976 | tf_op jit(solution)/shard_map/ppermute | solution.py:179
  7.2 0.0 collective-permute-start.2
  7.2 0.0 collective-permute-start.4
  7.2 3.9 %collective-permute-done.refs_1_ = bf16[97,8,128]{2,1,0:T(8,128)(2,1)S(1)} collective-permute-done((bf16[97,8,128]{2,1,0:T(8,128)(2,1)S(1)}, bf16[97,8,128]{2,1,0:T(8,128)(2,1)S(1)}, u32[]{:S(2)}, u32[]{:S(2)}) %collective-permute-start) | collective-permute-done | bytes 198688 | tf_op jit(solution)/shard_map/ppermute | solution.py:176
  11.0 1.1 %collective-permute-done.1.refs_0_ = bf16[97,8,128]{2,1,0:T(8,128)(2,1)S(1)} collective-permute-done((bf16[97,8,128]{2,1,0:T(8,128)(2,1)S(1)}, bf16[97,8,128]{2,1,0:T(8,128)(2,1)S(1)}, u32[]{:S(2)}, u32[]{:S(2)}) %collective-permute-start.1) | collective-permute-done | bytes 198688 | tf_op jit(solution)/shard_map/ppermute | solution.py:179
  12.1 0.0 collective-permute-done.2.other_ref
  12.1 1.5 %collective-permute-start.3 = (bf16[97,8,128]{2,1,0:T(8,128)(2,1)S(1)}, bf16[97,8,128]{2,1,0:T(8,128)(2,1)S(1)}, u32[]{:S(2)}, u32[]{:S(2)}) collective-permute-start(bf16[97,8,128]{2,1,0:T(8,128)(2,1)S(1)} %collective-permute-done.refs_1_), channel_id=1, source_target_pairs={{0,2},{2,0},{4,6},{6,4},{8,10},{10,8},{12,14},{14,12},{1,3},{3,1},... | collective-permute-start | bytes 595976 | tf_op jit(solution)/shard_map/ppermute | solution.py:179
  13.6 2.3 %collective-permute-start.5 = (bf16[97,8,128]{2,1,0:T(8,128)(2,1)S(1)}, bf16[97,8,128]{2,1,0:T(8,128)(2,1)S(1)}, u32[]{:S(2)}, u32[]{:S(2)}) collective-permute-start(bf16[97,8,128]{2,1,0:T(8,128)(2,1)S(1)} %collective-permute-done.refs_1_), channel_id=1, source_target_pairs={{0,8},{2,10},{8,12},{10,14},{12,4},{14,6},{4,0},{6,2},{1,9},{3,11}... | collective-permute-start | bytes 595976 | tf_op jit(solution)/shard_map/ppermute | solution.py:176
  15.9 0.4 %collective-permute-done.4.refs_0_ = bf16[97,8,128]{2,1,0:T(8,128)(2,1)S(1)} collective-permute-done((bf16[97,8,128]{2,1,0:T(8,128)(2,1)S(1)}, bf16[97,8,128]{2,1,0:T(8,128)(2,1)S(1)}, u32[]{:S(2)}, u32[]{:S(2)}) %collective-permute-start.4) | collective-permute-done | bytes 198688 | tf_op jit(solution)/shard_map/ppermute | solution.py:176
  16.3 2.3 %collective-permute-start.6 = (bf16[97,8,128]{2,1,0:T(8,128)(2,1)S(1)}, bf16[97,8,128]{2,1,0:T(8,128)(2,1)S(1)}, u32[]{:S(2)}, u32[]{:S(2)}) collective-permute-start(bf16[97,8,128]{2,1,0:T(8,128)(2,1)S(1)} %collective-permute-done.4.refs_0_), channel_id=1, source_target_pairs={{0,2},{2,0},{4,6},{6,4},{8,10},{10,8},{12,14},{14,12},{1,3},{3,1},... | collective-permute-start | bytes 595976 | tf_op jit(solution)/shard_map/ppermute | solution.py:179
  18.6 0.0 collective-permute-done.3.refs_2_
  18.6 4.7 %collective-permute-start.7 = (bf16[97,8,128]{2,1,0:T(8,128)(2,1)S(1)}, bf16[97,8,128]{2,1,0:T(8,128)(2,1)S(1)}, u32[]{:S(2)}, u32[]{:S(2)}) collective-permute-start(bf16[97,8,128]{2,1,0:T(8,128)(2,1)S(1)} %collective-permute-done.3.refs_2_), channel_id=1, source_target_pairs={{0,8},{2,10},{8,12},{10,14},{12,4},{14,6},{4,0},{6,2},{16,24},{18,... | collective-permute-start | bytes 595976 | tf_op jit(solution)/shard_map/ppermute | solution.py:188
  23.3 0.0 collective-permute-done.5.refs_1_
  23.3 0.7 %collective-permute-start.8 = (bf16[97,8,128]{2,1,0:T(8,128)(2,1)S(1)}, bf16[97,8,128]{2,1,0:T(8,128)(2,1)S(1)}, u32[]{:S(2)}, u32[]{:S(2)}) collective-permute-start(bf16[97,8,128]{2,1,0:T(8,128)(2,1)S(1)} %collective-permute-done.5.refs_1_), channel_id=1, source_target_pairs={{1,3},{3,1},{9,11},{11,9},{13,15},{15,13},{5,7},{7,5},{17,19},{19,... | collective-permute-start | bytes 595976 | tf_op jit(solution)/shard_map/ppermute | solution.py:188
  23.9 1.2 %first_scores.1 = (bf16[256,768]{1,0:T(8,128)(2,1)S(1)}, f32[256,128]{1,0:T(8,128)S(1)}, f32[256,128]{1,0:T(8,128)S(1)}, f32[256,768]{1,0:T(8,128)S(1)}) custom-call(bf16[97,8,128]{2,1,0:T(8,128)(2,1)S(1)} %pack.1.own_ref, bf16[97,8,128]{2,1,0:T(8,128)(2,1)S(1)} %collective-permute-done.2.other_ref, bf16[97,8,128]{2,1,0:T(8,128)(2,1)S(1)} %collective-permute-done.1.refs_0_, ...), custom_call_target="tpu_custom_call" | custom-call | flops 40265318400 | bytes 2359296 | tf_op jit(solution)/shard_map/first_scores/pallas_call | solution.py:194
  25.1 0.0 collective-permute-done.6.refs_2_
  25.1 1.1 %more_scores.1 = (f32[256,128]{1,0:T(8,128)S(1)}, f32[256,768]{1,0:T(8,128)S(1)}) custom-call(bf16[256,768]{1,0:T(8,128)(2,1)S(1)} %get-tuple-element.18.unit_ref, f32[256,128]{1,0:T(8,128)S(1)} %get-tuple-element.19.side_ref, f32[256,128]{1,0:T(8,128)S(1)} %get-tuple-element.20.old_sums_ref, ...), custom_call_target="tpu_custom_call", output_to_operand_aliasing={{0}: (2, {}), {1}: (3, {})} | custom-call | flops 30198988800 | bytes 2162688 | tf_op jit(solution)/shard_map/more_scores/pallas_call | solution.py:208
  26.2 0.2 collective-permute-done.7
  26.4 0.0 collective-permute-done.8
  26.4 0.1 broadcast_select_fusion.refs_0_
  26.5 0.5 %send_scores.1 = bf16[136,768]{1,0:T(8,128)(2,1)S(1)} custom-call(bf16[256,768]{1,0:T(8,128)(2,1)S(1)} %get-tuple-element.18.unit_ref, f32[256,128]{1,0:T(8,128)S(1)} %get-tuple-element.19.side_ref, f32[256,128]{1,0:T(8,128)S(1)} %get-tuple-element.22.old_sums_ref, f32[256,768]{1,0:T(8,128)S(1)} %get-tuple-element.23.old_mixed_ref, ...), custom_call_target="tpu_custom_call" | custom-call | flops 5033164800 | bytes 983040 | tf_op jit(solution)/shard_map/send_scores/pallas_call | solution.py:218
  27.0 0.1 collective-permute-start.9
  27.1 0.5 %keep_scores.1 = (f32[128,128]{1,0:T(8,128)S(1)}, f32[128,768]{1,0:T(8,128)S(1)}) custom-call(bf16[256,768]{1,0:T(8,128)(2,1)S(1)} %get-tuple-element.18.unit_ref, f32[256,128]{1,0:T(8,128)S(1)} %get-tuple-element.19.side_ref, f32[256,128]{1,0:T(8,128)S(1)} %get-tuple-element.22.old_sums_ref, f32[256,768]{1,0:T(8,128)S(1)} %get-tuple-element.23.old_mixed_ref, ...), custom_call_target="tpu_custom_call" | custom-call | flops 5033164800 | bytes 983040 | tf_op jit(solution)/shard_map/keep_scores/pallas_call | solution.py:225
  27.6 0.9 %collective-permute-done.9.got_ref = bf16[136,768]{1,0:T(8,128)(2,1)S(1)} collective-permute-done((bf16[136,768]{1,0:T(8,128)(2,1)S(1)}, bf16[136,768]{1,0:T(8,128)(2,1)S(1)}, u32[]{:S(2)}, u32[]{:S(2)}) %collective-permute-start.9) | collective-permute-done | bytes 208928 | tf_op jit(solution)/shard_map/ppermute | solution.py:191
  28.6 1.0 %combine.1 = (f32[1,128]{1,0:T(1,128)}, f32[128,768]{1,0:T(8,128)}) custom-call(f32[128,128]{1,0:T(8,128)S(1)} %get-tuple-element.24.sums_ref, f32[128,768]{1,0:T(8,128)S(1)} %get-tuple-element.25.mixed_ref, bf16[136,768]{1,0:T(8,128)(2,1)S(1)} %collective-permute-done.9.got_ref), custom_call_target="tpu_custom_call" | custom-call | tf_op jit(solution)/shard_map/combine/pallas_call | solution.py:274
  (2 shorter events, 0.0 us)
Async XLA Ops:
  0.6 0.9 %copy-start = (bf16[128,768]{1,0:T(8,128)(2,1)S(1)}, bf16[128,768]{1,0:T(8,128)(2,1)}, u32[]{:S(2)}) copy-start(bf16[128,768]{1,0:T(8,128)(2,1)} %param.3) | copy-start | bytes 589828
  0.6 0.9 %copy-start.1 = (s32[128,1]{0,1:T(1,128)S(1)}, s32[128,1]{0,1:T(1,128)}, u32[]{:S(2)}) copy-start(s32[128,1]{0,1:T(1,128)} %param.4) | copy-start | bytes 1540
  0.7 0.9 %copy-start.2 = (s32[128]{0:T(128)S(1)}, s32[128]{0:T(128)}, u32[]{:S(2)}) copy-start(s32[128]{0:T(128)} %param.5) | copy-start | bytes 1540
  1.6 9.4 %collective-permute-start = (bf16[97,8,128]{2,1,0:T(8,128)(2,1)S(1)}, bf16[97,8,128]{2,1,0:T(8,128)(2,1)S(1)}, u32[]{:S(2)}, u32[]{:S(2)}) collective-permute-start(bf16[97,8,128]{2,1,0:T(8,128)(2,1)S(1)} %pack.1.own_ref), channel_id=1, source_target_pairs={{0,8},{2,10},{8,12},{10,14},{12,4},{14,6},{4,0},{6,2},{1,9},{3,11}... | collective-permute-start | bytes 595976 | tf_op jit(solution)/shard_map/ppermute | solution.py:176
  5.7 6.4 %collective-permute-start.1 = (bf16[97,8,128]{2,1,0:T(8,128)(2,1)S(1)}, bf16[97,8,128]{2,1,0:T(8,128)(2,1)S(1)}, u32[]{:S(2)}, u32[]{:S(2)}) collective-permute-start(bf16[97,8,128]{2,1,0:T(8,128)(2,1)S(1)} %pack.1.own_ref), channel_id=1, source_target_pairs={{0,2},{2,0},{4,6},{6,4},{8,10},{10,8},{12,14},{14,12},{1,3},{3,1},... | collective-permute-start | bytes 595976 | tf_op jit(solution)/shard_map/ppermute | solution.py:179
  7.2 4.9 %collective-permute-start.2 = (bf16[97,8,128]{2,1,0:T(8,128)(2,1)S(1)}, bf16[97,8,128]{2,1,0:T(8,128)(2,1)S(1)}, u32[]{:S(2)}, u32[]{:S(2)}) collective-permute-start(bf16[97,8,128]{2,1,0:T(8,128)(2,1)S(1)} %pack.1.own_ref), channel_id=1, source_target_pairs={{0,1},{1,0},{2,3},{3,2},{4,5},{5,4},{6,7},{7,6},{8,9},{9,8},{10,11... | collective-permute-start | bytes 595976 | tf_op jit(solution)/shard_map/ppermute | solution.py:191
  7.2 9.1 %collective-permute-start.4 = (bf16[97,8,128]{2,1,0:T(8,128)(2,1)S(1)}, bf16[97,8,128]{2,1,0:T(8,128)(2,1)S(1)}, u32[]{:S(2)}, u32[]{:S(2)}) collective-permute-start(bf16[97,8,128]{2,1,0:T(8,128)(2,1)S(1)} %pack.1.own_ref), channel_id=1, source_target_pairs={{0,4},{2,6},{8,0},{10,2},{12,8},{14,10},{4,12},{6,14},{1,5},{3,7},... | collective-permute-start | bytes 595976 | tf_op jit(solution)/shard_map/ppermute | solution.py:176
  12.1 6.5 %collective-permute-start.3 = (bf16[97,8,128]{2,1,0:T(8,128)(2,1)S(1)}, bf16[97,8,128]{2,1,0:T(8,128)(2,1)S(1)}, u32[]{:S(2)}, u32[]{:S(2)}) collective-permute-start(bf16[97,8,128]{2,1,0:T(8,128)(2,1)S(1)} %collective-permute-done.refs_1_), channel_id=1, source_target_pairs={{0,2},{2,0},{4,6},{6,4},{8,10},{10,8},{12,14},{14,12},{1,3},{3,1},... | collective-permute-start | bytes 595976 | tf_op jit(solution)/shard_map/ppermute | solution.py:179
  13.6 9.7 %collective-permute-start.5 = (bf16[97,8,128]{2,1,0:T(8,128)(2,1)S(1)}, bf16[97,8,128]{2,1,0:T(8,128)(2,1)S(1)}, u32[]{:S(2)}, u32[]{:S(2)}) collective-permute-start(bf16[97,8,128]{2,1,0:T(8,128)(2,1)S(1)} %collective-permute-done.refs_1_), channel_id=1, source_target_pairs={{0,8},{2,10},{8,12},{10,14},{12,4},{14,6},{4,0},{6,2},{1,9},{3,11}... | collective-permute-start | bytes 595976 | tf_op jit(solution)/shard_map/ppermute | solution.py:176
  16.3 8.9 %collective-permute-start.6 = (bf16[97,8,128]{2,1,0:T(8,128)(2,1)S(1)}, bf16[97,8,128]{2,1,0:T(8,128)(2,1)S(1)}, u32[]{:S(2)}, u32[]{:S(2)}) collective-permute-start(bf16[97,8,128]{2,1,0:T(8,128)(2,1)S(1)} %collective-permute-done.4.refs_0_), channel_id=1, source_target_pairs={{0,2},{2,0},{4,6},{6,4},{8,10},{10,8},{12,14},{14,12},{1,3},{3,1},... | collective-permute-start | bytes 595976 | tf_op jit(solution)/shard_map/ppermute | solution.py:179
  18.6 7.9 %collective-permute-start.7 = (bf16[97,8,128]{2,1,0:T(8,128)(2,1)S(1)}, bf16[97,8,128]{2,1,0:T(8,128)(2,1)S(1)}, u32[]{:S(2)}, u32[]{:S(2)}) collective-permute-start(bf16[97,8,128]{2,1,0:T(8,128)(2,1)S(1)} %collective-permute-done.3.refs_2_), channel_id=1, source_target_pairs={{0,8},{2,10},{8,12},{10,14},{12,4},{14,6},{4,0},{6,2},{16,24},{18,... | collective-permute-start | bytes 595976 | tf_op jit(solution)/shard_map/ppermute | solution.py:188
  23.3 3.2 %collective-permute-start.8 = (bf16[97,8,128]{2,1,0:T(8,128)(2,1)S(1)}, bf16[97,8,128]{2,1,0:T(8,128)(2,1)S(1)}, u32[]{:S(2)}, u32[]{:S(2)}) collective-permute-start(bf16[97,8,128]{2,1,0:T(8,128)(2,1)S(1)} %collective-permute-done.5.refs_1_), channel_id=1, source_target_pairs={{1,3},{3,1},{9,11},{11,9},{13,15},{15,13},{5,7},{7,5},{17,19},{19,... | collective-permute-start | bytes 595976 | tf_op jit(solution)/shard_map/ppermute | solution.py:188
  27.0 1.5 %collective-permute-start.9 = (bf16[136,768]{1,0:T(8,128)(2,1)S(1)}, bf16[136,768]{1,0:T(8,128)(2,1)S(1)}, u32[]{:S(2)}, u32[]{:S(2)}) collective-permute-start(bf16[136,768]{1,0:T(8,128)(2,1)S(1)} %send_scores.1), channel_id=1, source_target_pairs={{0,1},{1,0},{2,3},{3,2},{4,5},{5,4},{6,7},{7,6},{8,9},{9,8},{10,11... | collective-permute-start | bytes 626696 | tf_op jit(solution)/shard_map/ppermute | solution.py:191

commit v20 on v18

--- a/solution.py
+++ b/solution.py
@@ -7,6 +7,7 @@
 
 SUB, LANE = 8, 128
 EXTRA = 8
+PIECES = 8
 VMEM = 24 * 1024 * 1024
 
 
@@ -134,14 +135,25 @@
     mixed_ref[...] = old_mixed_ref[:count, :] + mixed
 
 
-def combine_kernel(sums_ref, mixed_ref, got_ref, dup_ref, out_ref):
+def combine_kernel(sums_ref, mixed_ref, got_ref, dup_ref, out_ref, dup_here, out_here, sems):
     count = mixed_ref.shape[0]
+    step = count // PIECES
     line = got_ref[count:, :].astype(jnp.float32)[:1]
     parts = [line[:, at * count : (at + 1) * count] for at in range(4)]
     every = sums_ref[:, 1:2] + as_column(parts[2] + parts[3])
-    dup_ref[...] = jnp.log1p(as_row(sums_ref[:, 0:1]) + parts[0] + parts[1])
-    mixed = mixed_ref[...] + got_ref[:count, :].astype(jnp.float32)
-    out_ref[...] = mixed / jnp.sqrt(1.0 + every)
+    root = jnp.sqrt(1.0 + every)
+    copies = []
+    for at in range(PIECES):
+        here = pl.ds(at * step, step)
+        mixed = mixed_ref[here, :] + got_ref[here, :].astype(jnp.float32)
+        out_here[here, :] = mixed / root[at * step : (at + 1) * step]
+        copies.append(pltpu.make_async_copy(out_here.at[here, :], out_ref.at[here, :], sems.at[at]))
+        copies[-1].start()
+    dup_here[...] = jnp.log1p(as_row(sums_ref[:, 0:1]) + parts[0] + parts[1])
+    copies.append(pltpu.make_async_copy(dup_here, dup_ref, sems.at[PIECES]))
+    copies[-1].start()
+    for copy in copies:
+        copy.wait()
 
 
 def cost(queries, keys, width):
@@ -274,6 +286,12 @@
     dup, out = pl.pallas_call(
         combine_kernel,
         out_shape=[shape(1, count), shape(count, width)],
+        out_specs=[pl.BlockSpec(memory_space=pl.ANY)] * 2,
+        scratch_shapes=[
+            pltpu.VMEM((1, count), f32),
+            pltpu.VMEM((count, width), f32),
+            pltpu.SemaphoreType.DMA((PIECES + 1,)),
+        ],
         compiler_params=params,
         name="combine",
     )(keep_sums, keep, swap(send))

time: 29.2 us -> 29.2 us (level)
  no operation moved by 1% of the time
where the time goes in v20:
time: 29.2 us; the launch traced here: 29 us
  starting transfers between devices  14.1 us (48%)
  waiting for transfers between devices  8.96 us (31%)
  Pallas kernels  4.29 us (15%)
  local copies, waits for them, and re-layouts  0.9 us (3%)
  between operations  0.71 us (2%)
    ppermute x3, starting transfers between devices, along(): return lax.ppermute(array, 'shard', pairs)  6.42 us
    ppermute x3, waiting for transfers between devices, along(): return lax.ppermute(array, 'shard', pairs)  5.83 us
    ppermute x3, starting transfers between devices, across(): return lax.ppermute(array, 'shard', [(at, at ^ 1) for at in range(shards)])  5.29 us
    ppermute x1, starting transfers between devices, two_ways(): return lax.ppermute(source, ('shard', 'owner'), pairs)  2.35 us
    ppermute x3, waiting for transfers between devices, across(): return lax.ppermute(array, 'shard', [(at, at ^ 1) for at in range(shards)])  1.59 us
    pallas_call x1, Pallas kernels, first(): pl.pallas_call(first_kernel, out_shape=[shape(queries, width, dtype=bf16)...  1.18 us
    pallas_call x1, Pallas kernels, more(): pl.pallas_call(more_kernel, out_shape=[shape(queries, 128), shape(queries...  1.04 us
    pallas_call x1, Pallas kernels, local(): pl.pallas_call(combine_kernel, out_shape=[shape(1, count), shape(count, w...  0.99 us
  transfers between devices with their start and end apart: 9, of which 7 were waited for; matrix products, arithmetic and copies ran while one was open for 0% of the time, Pallas kernels for 9%

profile of v20, /device:TPU:0, one launch (start us, length us, event | category | flops | bytes accessed | tf_op | source)
XLA Modules:
  0.0 29.0 jit_solution(16261315071043891434)
XLA Ops:
  0.6 0.0 copy-start
  0.6 0.0 copy-start.1
  0.7 0.0 copy-start.2
  0.7 0.9 %copy-done = bf16[128,768]{1,0:T(8,128)(2,1)S(1)} copy-done((bf16[128,768]{1,0:T(8,128)(2,1)S(1)}, bf16[128,768]{1,0:T(8,128)(2,1)}, u32[]{:S(2)}) %copy-start) | copy-done | bytes 196632
  1.6 0.0 copy-done.1
  1.6 0.0 copy-done.2
  1.6 4.1 %collective-permute-start = (bf16[97,8,128]{2,1,0:T(8,128)(2,1)S(1)}, bf16[97,8,128]{2,1,0:T(8,128)(2,1)S(1)}, u32[]{:S(2)}, u32[]{:S(2)}) collective-permute-start(bf16[97,8,128]{2,1,0:T(8,128)(2,1)S(1)} %pack.1.own_ref), channel_id=1, source_target_pairs={{0,8},{2,10},{8,12},{10,14},{12,4},{14,6},{4,0},{6,2},{1,9},{3,11}... | collective-permute-start | bytes 595976 | tf_op jit(solution)/shard_map/ppermute | solution.py:188
  5.7 1.5 %collective-permute-start.1 = (bf16[97,8,128]{2,1,0:T(8,128)(2,1)S(1)}, bf16[97,8,128]{2,1,0:T(8,128)(2,1)S(1)}, u32[]{:S(2)}, u32[]{:S(2)}) collective-permute-start(bf16[97,8,128]{2,1,0:T(8,128)(2,1)S(1)} %pack.1.own_ref), channel_id=1, source_target_pairs={{0,2},{2,0},{4,6},{6,4},{8,10},{10,8},{12,14},{14,12},{1,3},{3,1},... | collective-permute-start | bytes 595976 | tf_op jit(solution)/shard_map/ppermute | solution.py:191
  7.2 0.0 collective-permute-start.2
  7.2 0.0 collective-permute-start.5
  7.2 3.9 %collective-permute-done.refs_1_ = bf16[97,8,128]{2,1,0:T(8,128)(2,1)S(1)} collective-permute-done((bf16[97,8,128]{2,1,0:T(8,128)(2,1)S(1)}, bf16[97,8,128]{2,1,0:T(8,128)(2,1)S(1)}, u32[]{:S(2)}, u32[]{:S(2)}) %collective-permute-start) | collective-permute-done | bytes 198688 | tf_op jit(solution)/shard_map/ppermute | solution.py:188
  11.0 1.1 %collective-permute-done.1.refs_0_ = bf16[97,8,128]{2,1,0:T(8,128)(2,1)S(1)} collective-permute-done((bf16[97,8,128]{2,1,0:T(8,128)(2,1)S(1)}, bf16[97,8,128]{2,1,0:T(8,128)(2,1)S(1)}, u32[]{:S(2)}, u32[]{:S(2)}) %collective-permute-start.1) | collective-permute-done | bytes 198688 | tf_op jit(solution)/shard_map/ppermute | solution.py:191
  12.1 0.0 collective-permute-done.2.other_ref
  12.1 1.5 %collective-permute-start.3 = (bf16[97,8,128]{2,1,0:T(8,128)(2,1)S(1)}, bf16[97,8,128]{2,1,0:T(8,128)(2,1)S(1)}, u32[]{:S(2)}, u32[]{:S(2)}) collective-permute-start(bf16[97,8,128]{2,1,0:T(8,128)(2,1)S(1)} %collective-permute-done.refs_1_), channel_id=1, source_target_pairs={{0,2},{2,0},{4,6},{6,4},{8,10},{10,8},{12,14},{14,12},{1,3},{3,1},... | collective-permute-start | bytes 595976 | tf_op jit(solution)/shard_map/ppermute | solution.py:191
  13.6 2.3 %collective-permute-start.4 = (bf16[97,8,128]{2,1,0:T(8,128)(2,1)S(1)}, bf16[97,8,128]{2,1,0:T(8,128)(2,1)S(1)}, u32[]{:S(2)}, u32[]{:S(2)}) collective-permute-start(bf16[97,8,128]{2,1,0:T(8,128)(2,1)S(1)} %collective-permute-done.refs_1_), channel_id=1, source_target_pairs={{0,8},{2,10},{8,12},{10,14},{12,4},{14,6},{4,0},{6,2},{1,9},{3,11}... | collective-permute-start | bytes 595976 | tf_op jit(solution)/shard_map/ppermute | solution.py:188
  15.9 0.4 %collective-permute-done.5.refs_0_ = bf16[97,8,128]{2,1,0:T(8,128)(2,1)S(1)} collective-permute-done((bf16[97,8,128]{2,1,0:T(8,128)(2,1)S(1)}, bf16[97,8,128]{2,1,0:T(8,128)(2,1)S(1)}, u32[]{:S(2)}, u32[]{:S(2)}) %collective-permute-start.5) | collective-permute-done | bytes 198688 | tf_op jit(solution)/shard_map/ppermute | solution.py:188
  16.3 2.3 %collective-permute-start.6 = (bf16[97,8,128]{2,1,0:T(8,128)(2,1)S(1)}, bf16[97,8,128]{2,1,0:T(8,128)(2,1)S(1)}, u32[]{:S(2)}, u32[]{:S(2)}) collective-permute-start(bf16[97,8,128]{2,1,0:T(8,128)(2,1)S(1)} %collective-permute-done.5.refs_0_), channel_id=1, source_target_pairs={{0,2},{2,0},{4,6},{6,4},{8,10},{10,8},{12,14},{14,12},{1,3},{3,1},... | collective-permute-start | bytes 595976 | tf_op jit(solution)/shard_map/ppermute | solution.py:191
  18.6 0.0 collective-permute-done.3.refs_2_
  18.6 1.6 %collective-permute-done.4.refs_1_ = bf16[97,8,128]{2,1,0:T(8,128)(2,1)S(1)} collective-permute-done((bf16[97,8,128]{2,1,0:T(8,128)(2,1)S(1)}, bf16[97,8,128]{2,1,0:T(8,128)(2,1)S(1)}, u32[]{:S(2)}, u32[]{:S(2)}) %collective-permute-start.4) | collective-permute-done | bytes 198688 | tf_op jit(solution)/shard_map/ppermute | solution.py:188
  20.2 0.1 broadcast_select_fusion
  20.3 2.4 %collective-permute-start.7 = (bf16[97,8,128]{2,1,0:T(8,128)(2,1)S(1)}, bf16[97,8,128]{2,1,0:T(8,128)(2,1)S(1)}, u32[]{:S(2)}, u32[]{:S(2)}) collective-permute-start(bf16[97,8,128]{2,1,0:T(8,128)(2,1)S(1)} %broadcast_select_fusion), channel_id=1, source_target_pairs={{0,8},{1,3},{2,10},{3,1},{8,12},{9,11},{10,14},{11,9},{12,4},{13,1... | collective-permute-start | bytes 595976 | tf_op jit(solution)/shard_map/ppermute | solution.py:201
  22.6 1.2 %first_scores.1 = (bf16[256,768]{1,0:T(8,128)(2,1)S(1)}, f32[256,128]{1,0:T(8,128)S(1)}, f32[256,128]{1,0:T(8,128)S(1)}, f32[256,768]{1,0:T(8,128)S(1)}) custom-call(bf16[97,8,128]{2,1,0:T(8,128)(2,1)S(1)} %pack.1.own_ref, bf16[97,8,128]{2,1,0:T(8,128)(2,1)S(1)} %collective-permute-done.2.other_ref, bf16[97,8,128]{2,1,0:T(8,128)(2,1)S(1)} %collective-permute-done.1.refs_0_, ...), custom_call_target="tpu_custom_call" | custom-call | flops 40265318400 | bytes 2359296 | tf_op jit(solution)/shard_map/first_scores/pallas_call | solution.py:207
  23.8 0.5 %collective-permute-done.6.refs_2_ = bf16[97,8,128]{2,1,0:T(8,128)(2,1)S(1)} collective-permute-done((bf16[97,8,128]{2,1,0:T(8,128)(2,1)S(1)}, bf16[97,8,128]{2,1,0:T(8,128)(2,1)S(1)}, u32[]{:S(2)}, u32[]{:S(2)}) %collective-permute-start.6) | collective-permute-done | bytes 198688 | tf_op jit(solution)/shard_map/ppermute | solution.py:191
  24.3 1.0 %more_scores.1 = (f32[256,128]{1,0:T(8,128)S(1)}, f32[256,768]{1,0:T(8,128)S(1)}) custom-call(bf16[256,768]{1,0:T(8,128)(2,1)S(1)} %get-tuple-element.23.unit_ref, f32[256,128]{1,0:T(8,128)S(1)} %get-tuple-element.24.side_ref, f32[256,128]{1,0:T(8,128)S(1)} %get-tuple-element.25.old_sums_ref, ...), custom_call_target="tpu_custom_call", output_to_operand_aliasing={{0}: (2, {}), {1}: (3, {})} | custom-call | flops 30198988800 | bytes 2162688 | tf_op jit(solution)/shard_map/more_scores/pallas_call | solution.py:221
  25.4 0.6 %collective-permute-done.7.refs_0_ = bf16[97,8,128]{2,1,0:T(8,128)(2,1)S(1)} collective-permute-done((bf16[97,8,128]{2,1,0:T(8,128)(2,1)S(1)}, bf16[97,8,128]{2,1,0:T(8,128)(2,1)S(1)}, u32[]{:S(2)}, u32[]{:S(2)}) %collective-permute-start.7) | collective-permute-done | bytes 198688 | tf_op jit(solution)/shard_map/ppermute | solution.py:201
  26.0 0.5 %send_scores.1 = bf16[136,768]{1,0:T(8,128)(2,1)S(1)} custom-call(bf16[256,768]{1,0:T(8,128)(2,1)S(1)} %get-tuple-element.23.unit_ref, f32[256,128]{1,0:T(8,128)S(1)} %get-tuple-element.24.side_ref, f32[256,128]{1,0:T(8,128)S(1)} %get-tuple-element.28.old_sums_ref, f32[256,768]{1,0:T(8,128)S(1)} %get-tuple-element.29.old_mixed_ref, ...), custom_call_target="tpu_custom_call" | custom-call | flops 5033164800 | bytes 983040 | tf_op jit(solution)/shard_map/send_scores/pallas_call | solution.py:231
  26.5 0.1 collective-permute-start.8
  26.6 0.5 %keep_scores.1 = (f32[128,128]{1,0:T(8,128)S(1)}, f32[128,768]{1,0:T(8,128)S(1)}) custom-call(bf16[256,768]{1,0:T(8,128)(2,1)S(1)} %get-tuple-element.23.unit_ref, f32[256,128]{1,0:T(8,128)S(1)} %get-tuple-element.24.side_ref, f32[256,128]{1,0:T(8,128)S(1)} %get-tuple-element.28.old_sums_ref, f32[256,768]{1,0:T(8,128)S(1)} %get-tuple-element.29.old_mixed_ref, ...), custom_call_target="tpu_custom_call" | custom-call | flops 5033164800 | bytes 983040 | tf_op jit(solution)/shard_map/keep_scores/pallas_call | solution.py:238
  27.1 0.9 %collective-permute-done.8.got_ref = bf16[136,768]{1,0:T(8,128)(2,1)S(1)} collective-permute-done((bf16[136,768]{1,0:T(8,128)(2,1)S(1)}, bf16[136,768]{1,0:T(8,128)(2,1)S(1)}, u32[]{:S(2)}, u32[]{:S(2)}) %collective-permute-start.8) | collective-permute-done | bytes 208928 | tf_op jit(solution)/shard_map/ppermute | solution.py:204
  28.1 1.0 %combine.1 = (f32[1,128]{1,0:T(1,128)}, f32[128,768]{1,0:T(8,128)}) custom-call(f32[128,128]{1,0:T(8,128)S(1)} %get-tuple-element.30.sums_ref, f32[128,768]{1,0:T(8,128)S(1)} %get-tuple-element.31.mixed_ref, bf16[136,768]{1,0:T(8,128)(2,1)S(1)} %collective-permute-done.8.got_ref), custom_call_target="tpu_custom_call" | custom-call | tf_op jit(solution)/shard_map/combine/pallas_call | solution.py:286
  (2 shorter events, 0.0 us)
Async XLA Ops:
  0.6 0.9 %copy-start = (bf16[128,768]{1,0:T(8,128)(2,1)S(1)}, bf16[128,768]{1,0:T(8,128)(2,1)}, u32[]{:S(2)}) copy-start(bf16[128,768]{1,0:T(8,128)(2,1)} %param.3) | copy-start | bytes 589828
  0.6 0.9 %copy-start.1 = (s32[128,1]{0,1:T(1,128)S(1)}, s32[128,1]{0,1:T(1,128)}, u32[]{:S(2)}) copy-start(s32[128,1]{0,1:T(1,128)} %param.4) | copy-start | bytes 1540
  0.7 0.9 %copy-start.2 = (s32[128]{0:T(128)S(1)}, s32[128]{0:T(128)}, u32[]{:S(2)}) copy-start(s32[128]{0:T(128)} %param.5) | copy-start | bytes 1540
  1.6 9.4 %collective-permute-start = (bf16[97,8,128]{2,1,0:T(8,128)(2,1)S(1)}, bf16[97,8,128]{2,1,0:T(8,128)(2,1)S(1)}, u32[]{:S(2)}, u32[]{:S(2)}) collective-permute-start(bf16[97,8,128]{2,1,0:T(8,128)(2,1)S(1)} %pack.1.own_ref), channel_id=1, source_target_pairs={{0,8},{2,10},{8,12},{10,14},{12,4},{14,6},{4,0},{6,2},{1,9},{3,11}... | collective-permute-start | bytes 595976 | tf_op jit(solution)/shard_map/ppermute | solution.py:188
  5.7 6.4 %collective-permute-start.1 = (bf16[97,8,128]{2,1,0:T(8,128)(2,1)S(1)}, bf16[97,8,128]{2,1,0:T(8,128)(2,1)S(1)}, u32[]{:S(2)}, u32[]{:S(2)}) collective-permute-start(bf16[97,8,128]{2,1,0:T(8,128)(2,1)S(1)} %pack.1.own_ref), channel_id=1, source_target_pairs={{0,2},{2,0},{4,6},{6,4},{8,10},{10,8},{12,14},{14,12},{1,3},{3,1},... | collective-permute-start | bytes 595976 | tf_op jit(solution)/shard_map/ppermute | solution.py:191
  7.2 4.9 %collective-permute-start.2 = (bf16[97,8,128]{2,1,0:T(8,128)(2,1)S(1)}, bf16[97,8,128]{2,1,0:T(8,128)(2,1)S(1)}, u32[]{:S(2)}, u32[]{:S(2)}) collective-permute-start(bf16[97,8,128]{2,1,0:T(8,128)(2,1)S(1)} %pack.1.own_ref), channel_id=1, source_target_pairs={{0,1},{1,0},{2,3},{3,2},{4,5},{5,4},{6,7},{7,6},{8,9},{9,8},{10,11... | collective-permute-start | bytes 595976 | tf_op jit(solution)/shard_map/ppermute | solution.py:204
  7.2 9.1 %collective-permute-start.5 = (bf16[97,8,128]{2,1,0:T(8,128)(2,1)S(1)}, bf16[97,8,128]{2,1,0:T(8,128)(2,1)S(1)}, u32[]{:S(2)}, u32[]{:S(2)}) collective-permute-start(bf16[97,8,128]{2,1,0:T(8,128)(2,1)S(1)} %pack.1.own_ref), channel_id=1, source_target_pairs={{0,4},{2,6},{8,0},{10,2},{12,8},{14,10},{4,12},{6,14},{1,5},{3,7},... | collective-permute-start | bytes 595976 | tf_op jit(solution)/shard_map/ppermute | solution.py:188
  12.1 6.5 %collective-permute-start.3 = (bf16[97,8,128]{2,1,0:T(8,128)(2,1)S(1)}, bf16[97,8,128]{2,1,0:T(8,128)(2,1)S(1)}, u32[]{:S(2)}, u32[]{:S(2)}) collective-permute-start(bf16[97,8,128]{2,1,0:T(8,128)(2,1)S(1)} %collective-permute-done.refs_1_), channel_id=1, source_target_pairs={{0,2},{2,0},{4,6},{6,4},{8,10},{10,8},{12,14},{14,12},{1,3},{3,1},... | collective-permute-start | bytes 595976 | tf_op jit(solution)/shard_map/ppermute | solution.py:191
  13.6 6.6 %collective-permute-start.4 = (bf16[97,8,128]{2,1,0:T(8,128)(2,1)S(1)}, bf16[97,8,128]{2,1,0:T(8,128)(2,1)S(1)}, u32[]{:S(2)}, u32[]{:S(2)}) collective-permute-start(bf16[97,8,128]{2,1,0:T(8,128)(2,1)S(1)} %collective-permute-done.refs_1_), channel_id=1, source_target_pairs={{0,8},{2,10},{8,12},{10,14},{12,4},{14,6},{4,0},{6,2},{1,9},{3,11}... | collective-permute-start | bytes 595976 | tf_op jit(solution)/shard_map/ppermute | solution.py:188
  16.3 8.1 %collective-permute-start.6 = (bf16[97,8,128]{2,1,0:T(8,128)(2,1)S(1)}, bf16[97,8,128]{2,1,0:T(8,128)(2,1)S(1)}, u32[]{:S(2)}, u32[]{:S(2)}) collective-permute-start(bf16[97,8,128]{2,1,0:T(8,128)(2,1)S(1)} %collective-permute-done.5.refs_0_), channel_id=1, source_target_pairs={{0,2},{2,0},{4,6},{6,4},{8,10},{10,8},{12,14},{14,12},{1,3},{3,1},... | collective-permute-start | bytes 595976 | tf_op jit(solution)/shard_map/ppermute | solution.py:191
  20.3 5.7 %collective-permute-start.7 = (bf16[97,8,128]{2,1,0:T(8,128)(2,1)S(1)}, bf16[97,8,128]{2,1,0:T(8,128)(2,1)S(1)}, u32[]{:S(2)}, u32[]{:S(2)}) collective-permute-start(bf16[97,8,128]{2,1,0:T(8,128)(2,1)S(1)} %broadcast_select_fusion), channel_id=1, source_target_pairs={{0,8},{1,3},{2,10},{3,1},{8,12},{9,11},{10,14},{11,9},{12,4},{13,1... | collective-permute-start | bytes 595976 | tf_op jit(solution)/shard_map/ppermute | solution.py:201
  26.5 1.5 %collective-permute-start.8 = (bf16[136,768]{1,0:T(8,128)(2,1)S(1)}, bf16[136,768]{1,0:T(8,128)(2,1)S(1)}, u32[]{:S(2)}, u32[]{:S(2)}) collective-permute-start(bf16[136,768]{1,0:T(8,128)(2,1)S(1)} %send_scores.1), channel_id=1, source_target_pairs={{0,1},{1,0},{2,3},{3,2},{4,5},{5,4},{6,7},{7,6},{8,9},{9,8},{10,11... | collective-permute-start | bytes 626696 | tf_op jit(solution)/shard_map/ppermute | solution.py:204

commit v21 on v19

--- a/solution.py
+++ b/solution.py
@@ -177,15 +177,6 @@
 
     def across(array):
         return lax.ppermute(array, "shard", [(at, at ^ 1) for at in range(shards)])
-
-    def one_lane(array, lane, step):
-        pairs = []
-        for at in range(rounds):
-            for side in range(2):
-                here, there = 2 * ring[at] + side, 2 * ring[(at + step) % rounds] + side
-                there = there if step else here ^ 1
-                pairs.append((here * lanes + lane, there * lanes + lane))
-        return lax.ppermute(array, ("shard", "owner"), pairs)
 
     def swap(array):
         return lax.ppermute(array, "owner", [(at, lanes - 1 - at) for at in range(lanes)])
@@ -254,11 +245,9 @@
         opposite = along(moved, 1)
         moved_beside = across(moved)
         ahead_beside = across(ahead)
-        by_ring = one_lane(moved_beside, 0, 1)
-        by_side = one_lane(opposite, lanes - 1, 0)
+        last = [along(moved_beside, 1)]
         unit, side, sums, mixed = first(own, other, beside, moved, moved_beside)
         sums, mixed = more(unit, side, sums, mixed, ahead, opposite, ahead_beside)
-        last = [jnp.where(lax.axis_index("owner") == 0, by_ring, by_side)]
     else:
         unit, side, sums, mixed = first(own, other, beside)
 

time: 29.7 us -> 28.3 us (0.953)
  starting transfers between devices: 17.1 us -> 14.6 us
  waiting for transfers between devices: 6.44 us -> 7.71 us
    ppermute x2 -> x0, starting transfers between devices: 5.34 us -> none  [one_lane(): return lax.ppermute(array, ('shard', 'owner'), pairs)]
    ppermute x3 -> x4, starting transfers between devices: 6.42 us -> 9.19 us  [along(): return lax.ppermute(array, 'shard', pairs)]
    ppermute x3, waiting for transfers between devices: 1.06 us -> 2.16 us  [across(): return lax.ppermute(array, 'shard', [(at, at ^ 1) for at in range(shards)])]
    ppermute x3 -> x4, waiting for transfers between devices: 4.22 us -> 4.62 us  [along(): return lax.ppermute(array, 'shard', pairs)]
  transfers between devices with their start and end apart: 10 -> 9, of which waited for: 5 -> 6; matrix products, arithmetic and copies ran while one was open for 0% -> 0% of each run, Pallas kernels for 9% -> 10%
where the time goes in v21:
time: 28.3 us; the launch traced here: 28.1 us
  starting transfers between devices  14.6 us (52%)
  waiting for transfers between devices  7.71 us (27%)
  Pallas kernels  4.26 us (15%)
  local copies, waits for them, and re-layouts  0.9 us (3%)
  between operations  0.71 us (3%)
    ppermute x4, starting transfers between devices, along(): return lax.ppermute(array, 'shard', pairs)  9.19 us
    ppermute x3, starting transfers between devices, across(): return lax.ppermute(array, 'shard', [(at, at ^ 1) for at in range(shards)])  5.29 us
    ppermute x4, waiting for transfers between devices, along(): return lax.ppermute(array, 'shard', pairs)  4.62 us
    ppermute x3, waiting for transfers between devices, across(): return lax.ppermute(array, 'shard', [(at, at ^ 1) for at in range(shards)])  2.16 us
    pallas_call x1, Pallas kernels, first(): pl.pallas_call(first_kernel, out_shape=[shape(queries, width, dtype=bf16)...  1.19 us
    pallas_call x1, Pallas kernels, more(): pl.pallas_call(more_kernel, out_shape=[shape(queries, 128), shape(queries...  1.05 us
    pallas_call x1, Pallas kernels, local(): pl.pallas_call(combine_kernel, out_shape=[shape(1, count), shape(count, w...  0.95 us
    ppermute x2, waiting for transfers between devices, swap(): lax.ppermute(array, 'owner', [(at, lanes - 1 - at) for at in range(lanes)])  0.93 us
  transfers between devices with their start and end apart: 9, of which 6 were waited for; matrix products, arithmetic and copies ran while one was open for 0% of the time, Pallas kernels for 10%

profile of v21, /device:TPU:0, one launch (start us, length us, event | category | flops | bytes accessed | tf_op | source)
XLA Modules:
  0.0 28.1 jit_solution(17769755666828250198)
XLA Ops:
  0.6 0.0 copy-start
  0.6 0.0 copy-start.1
  0.7 0.0 copy-start.2
  0.7 0.9 %copy-done = bf16[128,768]{1,0:T(8,128)(2,1)S(1)} copy-done((bf16[128,768]{1,0:T(8,128)(2,1)S(1)}, bf16[128,768]{1,0:T(8,128)(2,1)}, u32[]{:S(2)}) %copy-start) | copy-done | bytes 196632
  1.6 0.0 copy-done.1
  1.6 0.0 copy-done.2
  1.6 4.1 %collective-permute-start = (bf16[97,8,128]{2,1,0:T(8,128)(2,1)S(1)}, bf16[97,8,128]{2,1,0:T(8,128)(2,1)S(1)}, u32[]{:S(2)}, u32[]{:S(2)}) collective-permute-start(bf16[97,8,128]{2,1,0:T(8,128)(2,1)S(1)} %pack.1.own_ref), channel_id=1, source_target_pairs={{0,8},{2,10},{8,12},{10,14},{12,4},{14,6},{4,0},{6,2},{1,9},{3,11}... | collective-permute-start | bytes 595976 | tf_op jit(solution)/shard_map/ppermute | solution.py:176
  5.7 1.5 %collective-permute-start.1 = (bf16[97,8,128]{2,1,0:T(8,128)(2,1)S(1)}, bf16[97,8,128]{2,1,0:T(8,128)(2,1)S(1)}, u32[]{:S(2)}, u32[]{:S(2)}) collective-permute-start(bf16[97,8,128]{2,1,0:T(8,128)(2,1)S(1)} %pack.1.own_ref), channel_id=1, source_target_pairs={{0,2},{2,0},{4,6},{6,4},{8,10},{10,8},{12,14},{14,12},{1,3},{3,1},... | collective-permute-start | bytes 595976 | tf_op jit(solution)/shard_map/ppermute | solution.py:179
  7.2 0.0 collective-permute-start.2
  7.2 0.0 collective-permute-start.4
  7.2 3.9 %collective-permute-done.refs_1_ = bf16[97,8,128]{2,1,0:T(8,128)(2,1)S(1)} collective-permute-done((bf16[97,8,128]{2,1,0:T(8,128)(2,1)S(1)}, bf16[97,8,128]{2,1,0:T(8,128)(2,1)S(1)}, u32[]{:S(2)}, u32[]{:S(2)}) %collective-permute-start) | collective-permute-done | bytes 198688 | tf_op jit(solution)/shard_map/ppermute | solution.py:176
  11.0 1.1 %collective-permute-done.1.refs_0_ = bf16[97,8,128]{2,1,0:T(8,128)(2,1)S(1)} collective-permute-done((bf16[97,8,128]{2,1,0:T(8,128)(2,1)S(1)}, bf16[97,8,128]{2,1,0:T(8,128)(2,1)S(1)}, u32[]{:S(2)}, u32[]{:S(2)}) %collective-permute-start.1) | collective-permute-done | bytes 198688 | tf_op jit(solution)/shard_map/ppermute | solution.py:179
  12.1 0.0 collective-permute-done.2.other_ref
  12.1 1.5 %collective-permute-start.3 = (bf16[97,8,128]{2,1,0:T(8,128)(2,1)S(1)}, bf16[97,8,128]{2,1,0:T(8,128)(2,1)S(1)}, u32[]{:S(2)}, u32[]{:S(2)}) collective-permute-start(bf16[97,8,128]{2,1,0:T(8,128)(2,1)S(1)} %collective-permute-done.refs_1_), channel_id=1, source_target_pairs={{0,2},{2,0},{4,6},{6,4},{8,10},{10,8},{12,14},{14,12},{1,3},{3,1},... | collective-permute-start | bytes 595976 | tf_op jit(solution)/shard_map/ppermute | solution.py:179
  13.6 2.3 %collective-permute-start.5 = (bf16[97,8,128]{2,1,0:T(8,128)(2,1)S(1)}, bf16[97,8,128]{2,1,0:T(8,128)(2,1)S(1)}, u32[]{:S(2)}, u32[]{:S(2)}) collective-permute-start(bf16[97,8,128]{2,1,0:T(8,128)(2,1)S(1)} %collective-permute-done.refs_1_), channel_id=1, source_target_pairs={{0,8},{2,10},{8,12},{10,14},{12,4},{14,6},{4,0},{6,2},{1,9},{3,11}... | collective-permute-start | bytes 595976 | tf_op jit(solution)/shard_map/ppermute | solution.py:176
  15.9 0.4 %collective-permute-done.4.refs_0_ = bf16[97,8,128]{2,1,0:T(8,128)(2,1)S(1)} collective-permute-done((bf16[97,8,128]{2,1,0:T(8,128)(2,1)S(1)}, bf16[97,8,128]{2,1,0:T(8,128)(2,1)S(1)}, u32[]{:S(2)}, u32[]{:S(2)}) %collective-permute-start.4) | collective-permute-done | bytes 198688 | tf_op jit(solution)/shard_map/ppermute | solution.py:176
  16.3 2.3 %collective-permute-start.6 = (bf16[97,8,128]{2,1,0:T(8,128)(2,1)S(1)}, bf16[97,8,128]{2,1,0:T(8,128)(2,1)S(1)}, u32[]{:S(2)}, u32[]{:S(2)}) collective-permute-start(bf16[97,8,128]{2,1,0:T(8,128)(2,1)S(1)} %collective-permute-done.4.refs_0_), channel_id=1, source_target_pairs={{0,2},{2,0},{4,6},{6,4},{8,10},{10,8},{12,14},{14,12},{1,3},{3,1},... | collective-permute-start | bytes 595976 | tf_op jit(solution)/shard_map/ppermute | solution.py:179
  18.6 0.0 collective-permute-done.3.refs_2_
  18.6 2.8 %collective-permute-start.7 = (bf16[97,8,128]{2,1,0:T(8,128)(2,1)S(1)}, bf16[97,8,128]{2,1,0:T(8,128)(2,1)S(1)}, u32[]{:S(2)}, u32[]{:S(2)}) collective-permute-start(bf16[97,8,128]{2,1,0:T(8,128)(2,1)S(1)} %collective-permute-done.3.refs_2_), channel_id=1, source_target_pairs={{0,8},{2,10},{8,12},{10,14},{12,4},{14,6},{4,0},{6,2},{1,9},{3,11}... | collective-permute-start | bytes 595976 | tf_op jit(solution)/shard_map/ppermute | solution.py:176
  21.3 1.2 %first_scores.1 = (bf16[256,768]{1,0:T(8,128)(2,1)S(1)}, f32[256,128]{1,0:T(8,128)S(1)}, f32[256,128]{1,0:T(8,128)S(1)}, f32[256,768]{1,0:T(8,128)S(1)}) custom-call(bf16[97,8,128]{2,1,0:T(8,128)(2,1)S(1)} %pack.1.own_ref, bf16[97,8,128]{2,1,0:T(8,128)(2,1)S(1)} %collective-permute-done.2.other_ref, bf16[97,8,128]{2,1,0:T(8,128)(2,1)S(1)} %collective-permute-done.1.refs_0_, ...), custom_call_target="tpu_custom_call" | custom-call | flops 40265318400 | bytes 2359296 | tf_op jit(solution)/shard_map/first_scores/pallas_call | solution.py:185
  22.5 0.0 collective-permute-done.5.refs_1_
  22.6 1.1 %collective-permute-done.6.refs_2_ = bf16[97,8,128]{2,1,0:T(8,128)(2,1)S(1)} collective-permute-done((bf16[97,8,128]{2,1,0:T(8,128)(2,1)S(1)}, bf16[97,8,128]{2,1,0:T(8,128)(2,1)S(1)}, u32[]{:S(2)}, u32[]{:S(2)}) %collective-permute-start.6) | collective-permute-done | bytes 198688 | tf_op jit(solution)/shard_map/ppermute | solution.py:179
  23.7 1.1 %more_scores.1 = (f32[256,128]{1,0:T(8,128)S(1)}, f32[256,768]{1,0:T(8,128)S(1)}) custom-call(bf16[256,768]{1,0:T(8,128)(2,1)S(1)} %get-tuple-element.18.unit_ref, f32[256,128]{1,0:T(8,128)S(1)} %get-tuple-element.19.side_ref, f32[256,128]{1,0:T(8,128)S(1)} %get-tuple-element.20.old_sums_ref, ...), custom_call_target="tpu_custom_call", output_to_operand_aliasing={{0}: (2, {}), {1}: (3, {})} | custom-call | flops 30198988800 | bytes 2162688 | tf_op jit(solution)/shard_map/more_scores/pallas_call | solution.py:199
  24.7 0.4 %collective-permute-done.7.refs_0_ = bf16[97,8,128]{2,1,0:T(8,128)(2,1)S(1)} collective-permute-done((bf16[97,8,128]{2,1,0:T(8,128)(2,1)S(1)}, bf16[97,8,128]{2,1,0:T(8,128)(2,1)S(1)}, u32[]{:S(2)}, u32[]{:S(2)}) %collective-permute-start.7) | collective-permute-done | bytes 198688 | tf_op jit(solution)/shard_map/ppermute | solution.py:176
  25.1 0.5 %send_scores.1 = bf16[136,768]{1,0:T(8,128)(2,1)S(1)} custom-call(bf16[256,768]{1,0:T(8,128)(2,1)S(1)} %get-tuple-element.18.unit_ref, f32[256,128]{1,0:T(8,128)S(1)} %get-tuple-element.19.side_ref, f32[256,128]{1,0:T(8,128)S(1)} %get-tuple-element.22.old_sums_ref, f32[256,768]{1,0:T(8,128)S(1)} %get-tuple-element.23.old_mixed_ref, ...), custom_call_target="tpu_custom_call" | custom-call | flops 5033164800 | bytes 983040 | tf_op jit(solution)/shard_map/send_scores/pallas_call | solution.py:209
  25.7 0.1 collective-permute-start.8
  25.7 0.5 %keep_scores.1 = (f32[128,128]{1,0:T(8,128)S(1)}, f32[128,768]{1,0:T(8,128)S(1)}) custom-call(bf16[256,768]{1,0:T(8,128)(2,1)S(1)} %get-tuple-element.18.unit_ref, f32[256,128]{1,0:T(8,128)S(1)} %get-tuple-element.19.side_ref, f32[256,128]{1,0:T(8,128)S(1)} %get-tuple-element.22.old_sums_ref, f32[256,768]{1,0:T(8,128)S(1)} %get-tuple-element.23.old_mixed_ref, ...), custom_call_target="tpu_custom_call" | custom-call | flops 5033164800 | bytes 983040 | tf_op jit(solution)/shard_map/keep_scores/pallas_call | solution.py:216
  26.3 0.9 %collective-permute-done.8.got_ref = bf16[136,768]{1,0:T(8,128)(2,1)S(1)} collective-permute-done((bf16[136,768]{1,0:T(8,128)(2,1)S(1)}, bf16[136,768]{1,0:T(8,128)(2,1)S(1)}, u32[]{:S(2)}, u32[]{:S(2)}) %collective-permute-start.8) | collective-permute-done | bytes 208928 | tf_op jit(solution)/shard_map/ppermute | solution.py:182
  27.2 1.0 %combine.1 = (f32[1,128]{1,0:T(1,128)}, f32[128,768]{1,0:T(8,128)}) custom-call(f32[128,128]{1,0:T(8,128)S(1)} %get-tuple-element.24.sums_ref, f32[128,768]{1,0:T(8,128)S(1)} %get-tuple-element.25.mixed_ref, bf16[136,768]{1,0:T(8,128)(2,1)S(1)} %collective-permute-done.8.got_ref), custom_call_target="tpu_custom_call" | custom-call | tf_op jit(solution)/shard_map/combine/pallas_call | solution.py:263
  (2 shorter events, 0.0 us)
Async XLA Ops:
  0.6 0.9 %copy-start = (bf16[128,768]{1,0:T(8,128)(2,1)S(1)}, bf16[128,768]{1,0:T(8,128)(2,1)}, u32[]{:S(2)}) copy-start(bf16[128,768]{1,0:T(8,128)(2,1)} %param.3) | copy-start | bytes 589828
  0.6 0.9 %copy-start.1 = (s32[128,1]{0,1:T(1,128)S(1)}, s32[128,1]{0,1:T(1,128)}, u32[]{:S(2)}) copy-start(s32[128,1]{0,1:T(1,128)} %param.4) | copy-start | bytes 1540
  0.7 0.9 %copy-start.2 = (s32[128]{0:T(128)S(1)}, s32[128]{0:T(128)}, u32[]{:S(2)}) copy-start(s32[128]{0:T(128)} %param.5) | copy-start | bytes 1540
  1.6 9.4 %collective-permute-start = (bf16[97,8,128]{2,1,0:T(8,128)(2,1)S(1)}, bf16[97,8,128]{2,1,0:T(8,128)(2,1)S(1)}, u32[]{:S(2)}, u32[]{:S(2)}) collective-permute-start(bf16[97,8,128]{2,1,0:T(8,128)(2,1)S(1)} %pack.1.own_ref), channel_id=1, source_target_pairs={{0,8},{2,10},{8,12},{10,14},{12,4},{14,6},{4,0},{6,2},{1,9},{3,11}... | collective-permute-start | bytes 595976 | tf_op jit(solution)/shard_map/ppermute | solution.py:176
  5.7 6.4 %collective-permute-start.1 = (bf16[97,8,128]{2,1,0:T(8,128)(2,1)S(1)}, bf16[97,8,128]{2,1,0:T(8,128)(2,1)S(1)}, u32[]{:S(2)}, u32[]{:S(2)}) collective-permute-start(bf16[97,8,128]{2,1,0:T(8,128)(2,1)S(1)} %pack.1.own_ref), channel_id=1, source_target_pairs={{0,2},{2,0},{4,6},{6,4},{8,10},{10,8},{12,14},{14,12},{1,3},{3,1},... | collective-permute-start | bytes 595976 | tf_op jit(solution)/shard_map/ppermute | solution.py:179
  7.2 4.9 %collective-permute-start.2 = (bf16[97,8,128]{2,1,0:T(8,128)(2,1)S(1)}, bf16[97,8,128]{2,1,0:T(8,128)(2,1)S(1)}, u32[]{:S(2)}, u32[]{:S(2)}) collective-permute-start(bf16[97,8,128]{2,1,0:T(8,128)(2,1)S(1)} %pack.1.own_ref), channel_id=1, source_target_pairs={{0,1},{1,0},{2,3},{3,2},{4,5},{5,4},{6,7},{7,6},{8,9},{9,8},{10,11... | collective-permute-start | bytes 595976 | tf_op jit(solution)/shard_map/ppermute | solution.py:182
  7.2 9.1 %collective-permute-start.4 = (bf16[97,8,128]{2,1,0:T(8,128)(2,1)S(1)}, bf16[97,8,128]{2,1,0:T(8,128)(2,1)S(1)}, u32[]{:S(2)}, u32[]{:S(2)}) collective-permute-start(bf16[97,8,128]{2,1,0:T(8,128)(2,1)S(1)} %pack.1.own_ref), channel_id=1, source_target_pairs={{0,4},{2,6},{8,0},{10,2},{12,8},{14,10},{4,12},{6,14},{1,5},{3,7},... | collective-permute-start | bytes 595976 | tf_op jit(solution)/shard_map/ppermute | solution.py:176
  12.1 6.5 %collective-permute-start.3 = (bf16[97,8,128]{2,1,0:T(8,128)(2,1)S(1)}, bf16[97,8,128]{2,1,0:T(8,128)(2,1)S(1)}, u32[]{:S(2)}, u32[]{:S(2)}) collective-permute-start(bf16[97,8,128]{2,1,0:T(8,128)(2,1)S(1)} %collective-permute-done.refs_1_), channel_id=1, source_target_pairs={{0,2},{2,0},{4,6},{6,4},{8,10},{10,8},{12,14},{14,12},{1,3},{3,1},... | collective-permute-start | bytes 595976 | tf_op jit(solution)/shard_map/ppermute | solution.py:179
  13.6 9.0 %collective-permute-start.5 = (bf16[97,8,128]{2,1,0:T(8,128)(2,1)S(1)}, bf16[97,8,128]{2,1,0:T(8,128)(2,1)S(1)}, u32[]{:S(2)}, u32[]{:S(2)}) collective-permute-start(bf16[97,8,128]{2,1,0:T(8,128)(2,1)S(1)} %collective-permute-done.refs_1_), channel_id=1, source_target_pairs={{0,8},{2,10},{8,12},{10,14},{12,4},{14,6},{4,0},{6,2},{1,9},{3,11}... | collective-permute-start | bytes 595976 | tf_op jit(solution)/shard_map/ppermute | solution.py:176
  16.3 7.4 %collective-permute-start.6 = (bf16[97,8,128]{2,1,0:T(8,128)(2,1)S(1)}, bf16[97,8,128]{2,1,0:T(8,128)(2,1)S(1)}, u32[]{:S(2)}, u32[]{:S(2)}) collective-permute-start(bf16[97,8,128]{2,1,0:T(8,128)(2,1)S(1)} %collective-permute-done.4.refs_0_), channel_id=1, source_target_pairs={{0,2},{2,0},{4,6},{6,4},{8,10},{10,8},{12,14},{14,12},{1,3},{3,1},... | collective-permute-start | bytes 595976 | tf_op jit(solution)/shard_map/ppermute | solution.py:179
  18.6 6.5 %collective-permute-start.7 = (bf16[97,8,128]{2,1,0:T(8,128)(2,1)S(1)}, bf16[97,8,128]{2,1,0:T(8,128)(2,1)S(1)}, u32[]{:S(2)}, u32[]{:S(2)}) collective-permute-start(bf16[97,8,128]{2,1,0:T(8,128)(2,1)S(1)} %collective-permute-done.3.refs_2_), channel_id=1, source_target_pairs={{0,8},{2,10},{8,12},{10,14},{12,4},{14,6},{4,0},{6,2},{1,9},{3,11}... | collective-permute-start | bytes 595976 | tf_op jit(solution)/shard_map/ppermute | solution.py:176
  25.7 1.5 %collective-permute-start.8 = (bf16[136,768]{1,0:T(8,128)(2,1)S(1)}, bf16[136,768]{1,0:T(8,128)(2,1)S(1)}, u32[]{:S(2)}, u32[]{:S(2)}) collective-permute-start(bf16[136,768]{1,0:T(8,128)(2,1)S(1)} %send_scores.1), channel_id=1, source_target_pairs={{0,1},{1,0},{2,3},{3,2},{4,5},{5,4},{6,7},{7,6},{8,9},{9,8},{10,11... | collective-permute-start | bytes 626696 | tf_op jit(solution)/shard_map/ppermute | solution.py:182

commit v22 on v21

--- a/solution.py
+++ b/solution.py
@@ -1,3 +1,5 @@
+import functools
+
 import jax
 import jax.numpy as jnp
 from jax import lax
@@ -40,7 +42,7 @@
     base_ref[...] = jnp.zeros_like(base_ref)
 
 
-def pack_kernel(tiles_ref, label_ref, rank_ref, base_ref, packed_ref):
+def pack_kernel(tiles_ref, label_ref, rank_ref, base_ref, packed_ref, tag_ref):
     many = tiles_ref.shape[0]
     packed_ref[:many] = tiles_ref[...]
     rank = rank_ref[...]
@@ -48,11 +50,14 @@
     low = rank - lax.shift_left(high, 8)
     lines = [line.astype(jnp.float32) for line in (label_ref[...], high, low)]
     lines.append(base_ref[len(lines) :, :])
-    packed_ref[many] = jnp.concatenate(lines, axis=0).astype(jnp.bfloat16)
-
-
-def labels_and_ranks(block):
-    tile = block[block.shape[0] - 1].astype(jnp.float32)
+    tag = jnp.concatenate(lines, axis=0).astype(jnp.bfloat16)
+    packed_ref[many] = tag
+    tag_ref[...] = tag
+
+
+def labels_and_ranks(block, tag=None):
+    tile = block[block.shape[0] - 1] if tag is None else tag
+    tile = tile.astype(jnp.float32)
     return tile[0:1], tile[1:2] * 256.0 + tile[2:3]
 
 
@@ -60,18 +65,24 @@
     across = width // LANE
     wide = []
     for block in blocks:
-        tiles = block[: block.shape[0] - 1].astype(jnp.float32)
+        tiles = block[: block.shape[0] // across * across].astype(jnp.float32)
         tiles = tiles.reshape(-1, across, SUB, LANE)
         pieces = [tiles[:, at].reshape(-1, LANE) for at in range(across)]
         wide.append(jnp.concatenate(pieces, axis=1))
     return jnp.concatenate(wide, axis=0)
 
 
-def score(unit, side, blocks):
+def split(marks, refs):
+    blocks, arrays = refs[: len(marks)], refs[len(marks) :]
+    tags = [None if m is None else arrays[m[0]][m[1] * SUB : (m[1] + 1) * SUB, :] for m in marks]
+    return blocks, tags
+
+
+def score(unit, side, blocks, tags):
     own_label, own_rank = side[:, 0:1], side[:, 1:2]
     wide = rows_of(blocks, unit.shape[1])
     keys = wide.astype(jnp.bfloat16)
-    sides = [labels_and_ranks(block) for block in blocks]
+    sides = [labels_and_ranks(block, tag) for block, tag in zip(blocks, tags)]
     label = jnp.concatenate([item[0] for item in sides], axis=1)
     rank = jnp.concatenate([item[1] for item in sides], axis=1)
     cosine = lax.dot_general(
@@ -85,8 +96,9 @@
     return earlier, every, mixed
 
 
-def first_kernel(own_ref, other_ref, *refs):
-    blocks, (unit_ref, side_ref, sums_ref, mixed_ref) = refs[:-4], refs[-4:]
+def first_kernel(marks, own_ref, other_ref, *refs):
+    unit_ref, side_ref, sums_ref, mixed_ref = refs[-4:]
+    blocks, tags = split(marks, refs[:-4])
     count = own_ref.shape[0] // (unit_ref.shape[1] // LANE) * SUB
     side_ref[...] = jnp.zeros_like(side_ref)
     sums_ref[...] = jnp.zeros_like(sums_ref)
@@ -97,23 +109,25 @@
         side_ref[here, 0:1] = as_column(label)
         side_ref[here, 1:2] = as_column(rank)
     sums_ref[:, 0:1], sums_ref[:, 1:2], mixed_ref[...] = score(
-        unit_ref[...], side_ref, (own_ref,) + blocks
-    )
-
-
-def more_kernel(unit_ref, side_ref, old_sums_ref, old_mixed_ref, *refs):
-    blocks, (sums_ref, mixed_ref) = refs[:-2], refs[-2:]
-    earlier, every, mixed = score(unit_ref[...], side_ref, blocks)
+        unit_ref[...], side_ref, (own_ref,) + blocks, [None] + tags
+    )
+
+
+def more_kernel(marks, unit_ref, side_ref, old_sums_ref, old_mixed_ref, *refs):
+    sums_ref, mixed_ref = refs[-2:]
+    blocks, tags = split(marks, refs[:-2])
+    earlier, every, mixed = score(unit_ref[...], side_ref, blocks, tags)
     sums_ref[...] = old_sums_ref[...]
     sums_ref[:, 0:1] += earlier
     sums_ref[:, 1:2] += every
     mixed_ref[...] = old_mixed_ref[...] + mixed
 
 
-def send_kernel(unit_ref, side_ref, old_sums_ref, old_mixed_ref, *refs):
-    blocks, send_ref = refs[:-1], refs[-1]
+def send_kernel(marks, unit_ref, side_ref, old_sums_ref, old_mixed_ref, *refs):
+    send_ref = refs[-1]
+    blocks, tags = split(marks, refs[:-1])
     count, width = send_ref.shape[0] - EXTRA, send_ref.shape[1]
-    earlier, every, mixed = score(unit_ref[count:, :], side_ref[count:, :], blocks)
+    earlier, every, mixed = score(unit_ref[count:, :], side_ref[count:, :], blocks, tags)
     earlier += old_sums_ref[count:, 0:1]
     every += old_sums_ref[count:, 1:2]
     send_ref[:count, :] = (mixed + old_mixed_ref[count:, :]).astype(jnp.bfloat16)
@@ -124,10 +138,11 @@
     send_ref[count:, :] = jnp.broadcast_to(line, (EXTRA, width)).astype(jnp.bfloat16)
 
 
-def keep_kernel(unit_ref, side_ref, old_sums_ref, old_mixed_ref, *refs):
-    blocks, (sums_ref, mixed_ref) = refs[:-2], refs[-2:]
+def keep_kernel(marks, unit_ref, side_ref, old_sums_ref, old_mixed_ref, *refs):
+    sums_ref, mixed_ref = refs[-2:]
+    blocks, tags = split(marks, refs[:-2])
     count = mixed_ref.shape[0]
-    earlier, every, mixed = score(unit_ref[:count, :], side_ref[:count, :], blocks)
+    earlier, every, mixed = score(unit_ref[:count, :], side_ref[:count, :], blocks, tags)
     sums_ref[...] = old_sums_ref[:count, :]
     sums_ref[:, 0:1] += earlier
     sums_ref[:, 1:2] += every
@@ -146,9 +161,9 @@
 
 def cost(queries, keys, width):
     return pl.CostEstimate(
-        flops=400 * queries * keys * width,
+        flops=4 * queries * keys * width,
         bytes_accessed=8 * queries * width + 2 * keys * width,
-        transcendentals=100 * queries * keys,
+        transcendentals=queries * keys,
     )
 
 
@@ -181,48 +196,49 @@
     def swap(array):
         return lax.ppermute(array, "owner", [(at, lanes - 1 - at) for at in range(lanes)])
 
-    def first(*blocks):
+    def first(marks, own, other, *refs):
         return pl.pallas_call(
-            first_kernel,
+            functools.partial(first_kernel, marks),
             out_shape=[
                 shape(queries, width, dtype=bf16),
                 shape(queries, 128),
                 shape(queries, 128),
                 shape(queries, width),
             ],
-            cost_estimate=cost(queries, (len(blocks) - 1) * count, width),
+            cost_estimate=cost(queries, (len(marks) + 1) * count, width),
             compiler_params=params,
             name="first_scores",
-        )(*blocks)
-
-    def more(unit, side, sums, mixed, *blocks):
+        )(own, other, *refs)
+
+    def more(marks, unit, side, sums, mixed, *refs):
         return pl.pallas_call(
-            more_kernel,
+            functools.partial(more_kernel, marks),
             out_shape=[shape(queries, 128), shape(queries, width)],
             input_output_aliases={2: 0, 3: 1},
-            cost_estimate=cost(queries, len(blocks) * count, width),
+            cost_estimate=cost(queries, len(marks) * count, width),
             compiler_params=params,
             name="more_scores",
-        )(unit, side, sums, mixed, *blocks)
-
-    def final(unit, side, sums, mixed, *blocks):
+        )(unit, side, sums, mixed, *refs)
+
+    def final(marks, unit, side, sums, mixed, *refs):
         send = pl.pallas_call(
-            send_kernel,
+            functools.partial(send_kernel, marks),
             out_shape=shape(count + EXTRA, width, dtype=bf16),
-            cost_estimate=cost(count, len(blocks) * count, width),
+            cost_estimate=cost(count, len(marks) * count, width),
             compiler_params=params,
             name="send_scores",
-        )(unit, side, sums, mixed, *blocks)
+        )(unit, side, sums, mixed, *refs)
         keep_sums, keep = pl.pallas_call(
-            keep_kernel,
+            functools.partial(keep_kernel, marks),
             out_shape=[shape(count, 128), shape(count, width)],
-            cost_estimate=cost(count, len(blocks) * count, width),
+            cost_estimate=cost(count, len(marks) * count, width),
             compiler_params=params,
             name="keep_scores",
-        )(unit, side, sums, mixed, *blocks)
+        )(unit, side, sums, mixed, *refs)
         return keep_sums, keep, send
 
     pieces = embeddings.reshape(count // SUB, SUB, width // LANE, LANE).transpose(0, 2, 1, 3)
+    pieces = pieces.reshape(tiles, SUB, LANE)
     base = pl.pallas_call(
         base_kernel,
         out_shape=shape(SUB, LANE),
@@ -230,36 +246,44 @@
         compiler_params=params,
         name="base",
     )()
-    own = pl.pallas_call(
+    own, own_tag = pl.pallas_call(
         pack_kernel,
-        out_shape=shape(tiles + 1, SUB, LANE, dtype=bf16),
+        out_shape=[shape(tiles + 1, SUB, LANE, dtype=bf16), shape(SUB, LANE, dtype=bf16)],
         compiler_params=params,
         name="pack",
-    )(pieces.reshape(tiles, SUB, LANE), cluster_id.reshape(1, count), priority.reshape(1, count), base)
-
-    moved, beside = along(own, 1), across(own)
-    other = swap(own)
+    )(pieces, cluster_id.reshape(1, count), priority.reshape(1, count), base)
+
+    other, beside = swap(own), across(own)
     if rounds == 4:
+        moved = along(pieces, 1)
         ahead = along(own, -1)
-        moved, beside, other = lax.optimization_barrier((moved, beside, other))
+        other, own_tag = lax.optimization_barrier((other, own_tag))
+        ahead, beside = lax.optimization_barrier((ahead, beside))
         opposite = along(moved, 1)
         moved_beside = across(moved)
         ahead_beside = across(ahead)
-        last = [along(moved_beside, 1)]
-        unit, side, sums, mixed = first(own, other, beside, moved, moved_beside)
-        sums, mixed = more(unit, side, sums, mixed, ahead, opposite, ahead_beside)
+        column = jnp.concatenate([along(own_tag, 1), along(own_tag, 2)], axis=0)
+        tags = (column, across(column))
+        last = along(moved_beside, 1)
+        marks = (None, (0, 0), (1, 0))
+        state = first(marks, own, other, beside, moved, moved_beside, *tags)
+        marks = (None, (0, 1), None)
+        sums, mixed = more(marks, *state, ahead, opposite, ahead_beside, *tags)
+        outcome = final(((1, 1),), *state[:2], sums, mixed, last, *tags)
     else:
-        unit, side, sums, mixed = first(own, other, beside)
+        moved = along(own, 1)
+        unit, side, sums, mixed = first((None,), own, other, beside)
+        marks = (None, None)
 
         def turn(at, state):
             moved, sums, mixed = state
             ahead, beside = along(moved, 1), across(moved)
-            sums, mixed = more(unit, side, sums, mixed, moved, beside)
+            sums, mixed = more(marks, unit, side, sums, mixed, moved, beside)
             return ahead, sums, mixed
 
         moved, sums, mixed = lax.fori_loop(1, rounds - 1, turn, (moved, sums, mixed))
-        last = [moved, across(moved)]
-    keep_sums, keep, send = final(unit, side, sums, mixed, *last)
+        outcome = final(marks, unit, side, sums, mixed, moved, across(moved))
+    keep_sums, keep, send = outcome
     dup, out = pl.pallas_call(
         combine_kernel,
         out_shape=[shape(1, count), shape(count, width)],

time: 28.3 us -> 30.6 us (1.081)
  starting transfers between devices: 14.6 us -> 17.6 us
  waiting for transfers between devices: 7.71 us -> 7.21 us
    ppermute x3 -> x4, starting transfers between devices: 5.29 us -> 7.65 us  [across(): return lax.ppermute(array, 'shard', [(at, at ^ 1) for at in range(shards)])]
    ppermute x4 -> x6, starting transfers between devices: 9.19 us -> 9.75 us  [along(): return lax.ppermute(array, 'shard', pairs)]
    ppermute x4 -> x6, waiting for transfers between devices: 4.62 us -> 4.37 us  [along(): return lax.ppermute(array, 'shard', pairs)]
    ppermute x3 -> x4, waiting for transfers between devices: 2.16 us -> 1.91 us  [across(): return lax.ppermute(array, 'shard', [(at, at ^ 1) for at in range(shards)])]
    unnamed x6 -> x7, local copies, waits for them, and re-layouts: 0.9 us -> 0.67 us
  transfers between devices with their start and end apart: 9 -> 12, of which waited for: 6 -> 5; matrix products, arithmetic and copies ran while one was open for 0% -> 0% of each run, Pallas kernels for 10% -> 9%
where the time goes in v22:
time: 30.6 us; the launch traced here: 30.4 us
  starting transfers between devices  17.6 us (58%)
  waiting for transfers between devices  7.21 us (24%)
  Pallas kernels  4.27 us (14%)
  between operations  0.72 us (2%)
  local copies, waits for them, and re-layouts  0.68 us (2%)
    ppermute x6, starting transfers between devices, along(): return lax.ppermute(array, 'shard', pairs)  9.75 us
    ppermute x4, starting transfers between devices, across(): return lax.ppermute(array, 'shard', [(at, at ^ 1) for at in range(shards)])  7.65 us
    ppermute x6, waiting for transfers between devices, along(): return lax.ppermute(array, 'shard', pairs)  4.37 us
    ppermute x4, waiting for transfers between devices, across(): return lax.ppermute(array, 'shard', [(at, at ^ 1) for at in range(shards)])  1.91 us
    pallas_call x1, Pallas kernels, first(): pl.pallas_call(functools.partial(first_kernel, marks), out_shape=[shape(q...  1.19 us
    pallas_call x1, Pallas kernels, more(): pl.pallas_call(functools.partial(more_kernel, marks), out_shape=[shape(qu...  1.06 us
    pallas_call x1, Pallas kernels, local(): pl.pallas_call(combine_kernel, out_shape=[shape(1, count), shape(count, w...  0.95 us
    ppermute x2, waiting for transfers between devices, swap(): lax.ppermute(array, 'owner', [(at, lanes - 1 - at) for at in range(lanes)])  0.93 us
  transfers between devices with their start and end apart: 12, of which 5 were waited for; matrix products, arithmetic and copies ran while one was open for 0% of the time, Pallas kernels for 9%

profile of v22, /device:TPU:0, one launch (start us, length us, event | category | flops | bytes accessed | tf_op | source)
XLA Modules:
  0.0 30.4 jit_solution(4128224740027152925)
XLA Ops:
  0.6 0.0 copy-start
  0.6 4.1 %collective-permute-start.3 = (bf16[96,8,128]{2,1,0:T(8,128)(2,1)}, bf16[96,8,128]{2,1,0:T(8,128)(2,1)S(1)}, u32[]{:S(2)}, u32[]{:S(2)}) collective-permute-start(bf16[96,8,128]{2,1,0:T(8,128)(2,1)} %bitcast.8), channel_id=1, source_target_pairs={{0,8},{2,10},{8,12},{10,14},{12,4},{14,6},{4,0},{6,2},{1,9},{3,11}... | collective-permute-start | bytes 589832 | tf_op jit(solution)/shard_map/ppermute | solution.py:191
  4.7 0.0 copy-start.1
  4.7 0.0 copy-start.2
  4.7 0.0 copy-done
  4.7 0.6 %copy-done.1 = s32[128,1]{0,1:T(1,128)S(1)} copy-done((s32[128,1]{0,1:T(1,128)S(1)}, s32[128,1]{0,1:T(1,128)}, u32[]{:S(2)}) %copy-start.1) | copy-done | bytes 536
  5.4 0.0 copy-done.2
  5.4 0.1 collective-permute-start
  5.5 0.1 collective-permute-start.1
  5.6 1.6 %collective-permute-start.2 = (bf16[97,8,128]{2,1,0:T(8,128)(2,1)S(1)}, bf16[97,8,128]{2,1,0:T(8,128)(2,1)S(1)}, u32[]{:S(2)}, u32[]{:S(2)}) collective-permute-start(bf16[97,8,128]{2,1,0:T(8,128)(2,1)S(1)} %get-tuple-element.18.own_ref), channel_id=1, source_target_pairs={{0,2},{2,0},{4,6},{6,4},{8,10},{10,8},{12,14},{14,12},{1,3},{3,1},... | collective-permute-start | bytes 595976 | tf_op jit(solution)/shard_map/ppermute | solution.py:194
  7.1 3.2 %collective-permute-done.3.refs_1_ = bf16[96,8,128]{2,1,0:T(8,128)(2,1)S(1)} collective-permute-done((bf16[96,8,128]{2,1,0:T(8,128)(2,1)}, bf16[96,8,128]{2,1,0:T(8,128)(2,1)S(1)}, u32[]{:S(2)}, u32[]{:S(2)}) %collective-permute-start.3) | collective-permute-done | bytes 196640 | tf_op jit(solution)/shard_map/ppermute | solution.py:191
  10.4 1.5 %collective-permute-start.4 = (bf16[96,8,128]{2,1,0:T(8,128)(2,1)S(1)}, bf16[96,8,128]{2,1,0:T(8,128)(2,1)S(1)}, u32[]{:S(2)}, u32[]{:S(2)}) collective-permute-start(bf16[96,8,128]{2,1,0:T(8,128)(2,1)S(1)} %collective-permute-done.3.refs_1_), channel_id=1, source_target_pairs={{0,2},{2,0},{4,6},{6,4},{8,10},{10,8},{12,14},{14,12},{1,3},{3,1},... | collective-permute-start | bytes 589832 | tf_op jit(solution)/shard_map/ppermute | solution.py:194
  11.8 0.0 collective-permute-done.other_ref
  11.8 3.3 %collective-permute-start.5 = (bf16[8,128]{1,0:T(8,128)(2,1)S(1)}, bf16[8,128]{1,0:T(8,128)(2,1)S(1)}, u32[]{:S(2)}, u32[]{:S(2)}) collective-permute-start(bf16[8,128]{1,0:T(8,128)(2,1)S(1)} %get-tuple-element.22), channel_id=1, source_target_pairs={{0,8},{2,10},{8,12},{10,14},{12,4},{14,6},{4,0},{6,2},{1,9},{3,11}... | collective-permute-start | bytes 6152 | tf_op jit(solution)/shard_map/ppermute | solution.py:191
  15.1 0.0 collective-permute-start.8
  15.2 0.5 %collective-permute-done.1.refs_0_ = bf16[97,8,128]{2,1,0:T(8,128)(2,1)S(1)} collective-permute-done((bf16[97,8,128]{2,1,0:T(8,128)(2,1)S(1)}, bf16[97,8,128]{2,1,0:T(8,128)(2,1)S(1)}, u32[]{:S(2)}, u32[]{:S(2)}) %collective-permute-start.1) | collective-permute-done | bytes 198688 | tf_op jit(solution)/shard_map/ppermute | solution.py:191
  15.7 2.1 %collective-permute-start.6 = (bf16[8,128]{1,0:T(8,128)(2,1)S(1)}, bf16[8,128]{1,0:T(8,128)(2,1)S(1)}, u32[]{:S(2)}, u32[]{:S(2)}) collective-permute-start(bf16[8,128]{1,0:T(8,128)(2,1)S(1)} %get-tuple-element.22), channel_id=1, source_target_pairs={{0,12},{2,14},{8,4},{10,6},{12,0},{14,2},{4,8},{6,10},{1,13},{3,15... | collective-permute-start | bytes 6152 | tf_op jit(solution)/shard_map/ppermute | solution.py:191
  17.7 0.0 collective-permute-done.2.refs_0_
  17.7 2.4 %collective-permute-start.9 = (bf16[97,8,128]{2,1,0:T(8,128)(2,1)S(1)}, bf16[97,8,128]{2,1,0:T(8,128)(2,1)S(1)}, u32[]{:S(2)}, u32[]{:S(2)}) collective-permute-start(bf16[97,8,128]{2,1,0:T(8,128)(2,1)S(1)} %collective-permute-done.1.refs_0_), channel_id=1, source_target_pairs={{0,2},{2,0},{4,6},{6,4},{8,10},{10,8},{12,14},{14,12},{1,3},{3,1},... | collective-permute-start | bytes 595976 | tf_op jit(solution)/shard_map/ppermute | solution.py:194
  20.2 0.0 collective-permute-done.4.refs_2_
  20.2 0.2 collective-permute-start.10
  20.4 0.0 collective-permute-done.5
  20.4 0.6 %collective-permute-done.6 = bf16[8,128]{1,0:T(8,128)(2,1)S(1)} collective-permute-done((bf16[8,128]{1,0:T(8,128)(2,1)S(1)}, bf16[8,128]{1,0:T(8,128)(2,1)S(1)}, u32[]{:S(2)}, u32[]{:S(2)}) %collective-permute-start.6) | collective-permute-done | bytes 2080 | tf_op jit(solution)/shard_map/ppermute | solution.py:191
  21.1 2.2 %collective-permute-start.7 = (bf16[16,128]{1,0:T(8,128)(2,1)S(1)}, bf16[16,128]{1,0:T(8,128)(2,1)S(1)}, u32[]{:S(2)}, u32[]{:S(2)}) collective-permute-start(bf16[16,128]{1,0:T(8,128)(2,1)S(1)} %constant_dynamic-update-slice_fusion.refs_3_.refs_1_), channel_id=1, source_target_pairs={{0,2},{2,0},{4,6},{6,4},{8,10},{10,8},{12,14},{14,12},{1,3},{3,1},... | collective-permute-start | bytes 12296 | tf_op jit(solution)/shard_map/ppermute | solution.py:194
  23.2 1.9 %collective-permute-done.7.refs_4_.refs_2_ = bf16[16,128]{1,0:T(8,128)(2,1)S(1)} collective-permute-done((bf16[16,128]{1,0:T(8,128)(2,1)S(1)}, bf16[16,128]{1,0:T(8,128)(2,1)S(1)}, u32[]{:S(2)}, u32[]{:S(2)}) %collective-permute-start.7) | collective-permute-done | bytes 4128 | tf_op jit(solution)/shard_map/ppermute | solution.py:194
  25.1 1.2 %first_scores.1 = (bf16[256,768]{1,0:T(8,128)(2,1)S(1)}, f32[256,128]{1,0:T(8,128)S(1)}, f32[256,128]{1,0:T(8,128)S(1)}, f32[256,768]{1,0:T(8,128)S(1)}) custom-call(bf16[97,8,128]{2,1,0:T(8,128)(2,1)S(1)} %get-tuple-element.18.own_ref, bf16[97,8,128]{2,1,0:T(8,128)(2,1)S(1)} %collective-permute-done.other_ref, ...), custom_call_target="tpu_custom_call" | custom-call | flops 402653184 | bytes 2359296 | tf_op jit(solution)/shard_map/first_scores/pallas_call | solution.py:200
  26.3 0.0 collective-permute-done.8.refs_1_
  26.3 0.0 collective-permute-done.9.refs_2_
  26.3 1.1 %more_scores.1 = (f32[256,128]{1,0:T(8,128)S(1)}, f32[256,768]{1,0:T(8,128)S(1)}) custom-call(bf16[256,768]{1,0:T(8,128)(2,1)S(1)} %get-tuple-element.23.unit_ref, f32[256,128]{1,0:T(8,128)S(1)} %get-tuple-element.24.side_ref, f32[256,128]{1,0:T(8,128)S(1)} %get-tuple-element.25.old_sums_ref, ...), custom_call_target="tpu_custom_call", output_to_operand_aliasing={{0}: (2, {}), {1}: (3, {})} | custom-call | flops 301989888 | bytes 2162688 | tf_op jit(solution)/shard_map/more_scores/pallas_call | solution.py:214
  27.4 0.0 collective-permute-done.10.refs_0_
  27.4 0.5 %send_scores.1 = bf16[136,768]{1,0:T(8,128)(2,1)S(1)} custom-call(bf16[256,768]{1,0:T(8,128)(2,1)S(1)} %get-tuple-element.23.unit_ref, f32[256,128]{1,0:T(8,128)S(1)} %get-tuple-element.24.side_ref, f32[256,128]{1,0:T(8,128)S(1)} %get-tuple-element.28.old_sums_ref, f32[256,768]{1,0:T(8,128)S(1)} %get-tuple-element.29.old_mixed_ref, ...), custom_call_target="tpu_custom_call" | custom-call | flops 50331648 | bytes 983040 | tf_op jit(solution)/shard_map/send_scores/pallas_call | solution.py:224
  28.0 0.1 collective-permute-start.11
  28.0 0.5 %keep_scores.1 = (f32[128,128]{1,0:T(8,128)S(1)}, f32[128,768]{1,0:T(8,128)S(1)}) custom-call(bf16[256,768]{1,0:T(8,128)(2,1)S(1)} %get-tuple-element.23.unit_ref, f32[256,128]{1,0:T(8,128)S(1)} %get-tuple-element.24.side_ref, f32[256,128]{1,0:T(8,128)S(1)} %get-tuple-element.28.old_sums_ref, f32[256,768]{1,0:T(8,128)S(1)} %get-tuple-element.29.old_mixed_ref, ...), custom_call_target="tpu_custom_call" | custom-call | flops 50331648 | bytes 983040 | tf_op jit(solution)/shard_map/keep_scores/pallas_call | solution.py:231
  28.6 0.9 %collective-permute-done.11.got_ref = bf16[136,768]{1,0:T(8,128)(2,1)S(1)} collective-permute-done((bf16[136,768]{1,0:T(8,128)(2,1)S(1)}, bf16[136,768]{1,0:T(8,128)(2,1)S(1)}, u32[]{:S(2)}, u32[]{:S(2)}) %collective-permute-start.11) | collective-permute-done | bytes 208928 | tf_op jit(solution)/shard_map/ppermute | solution.py:197
  29.5 1.0 %combine.1 = (f32[1,128]{1,0:T(1,128)}, f32[128,768]{1,0:T(8,128)}) custom-call(f32[128,128]{1,0:T(8,128)S(1)} %get-tuple-element.30.sums_ref, f32[128,768]{1,0:T(8,128)S(1)} %get-tuple-element.31.mixed_ref, bf16[136,768]{1,0:T(8,128)(2,1)S(1)} %collective-permute-done.11.got_ref), custom_call_target="tpu_custom_call" | custom-call | tf_op jit(solution)/shard_map/combine/pallas_call | solution.py:287
  (4 shorter events, 0.0 us)
Async XLA Ops:
  0.6 4.1 %copy-start = (bf16[128,768]{1,0:T(8,128)(2,1)S(1)}, bf16[128,768]{1,0:T(8,128)(2,1)}, u32[]{:S(2)}) copy-start(bf16[128,768]{1,0:T(8,128)(2,1)} %param.3) | copy-start | bytes 589828
  0.6 9.7 %collective-permute-start.3 = (bf16[96,8,128]{2,1,0:T(8,128)(2,1)}, bf16[96,8,128]{2,1,0:T(8,128)(2,1)S(1)}, u32[]{:S(2)}, u32[]{:S(2)}) collective-permute-start(bf16[96,8,128]{2,1,0:T(8,128)(2,1)} %bitcast.8), channel_id=1, source_target_pairs={{0,8},{2,10},{8,12},{10,14},{12,4},{14,6},{4,0},{6,2},{1,9},{3,11}... | collective-permute-start | bytes 589832 | tf_op jit(solution)/shard_map/ppermute | solution.py:191
  4.7 0.7 %copy-start.1 = (s32[128,1]{0,1:T(1,128)S(1)}, s32[128,1]{0,1:T(1,128)}, u32[]{:S(2)}) copy-start(s32[128,1]{0,1:T(1,128)} %param.4) | copy-start | bytes 1540
  4.7 0.7 %copy-start.2 = (s32[128]{0:T(128)S(1)}, s32[128]{0:T(128)}, u32[]{:S(2)}) copy-start(s32[128]{0:T(128)} %param.5) | copy-start | bytes 1540
  5.4 6.4 %collective-permute-start = (bf16[97,8,128]{2,1,0:T(8,128)(2,1)S(1)}, bf16[97,8,128]{2,1,0:T(8,128)(2,1)S(1)}, u32[]{:S(2)}, u32[]{:S(2)}) collective-permute-start(bf16[97,8,128]{2,1,0:T(8,128)(2,1)S(1)} %get-tuple-element.18.own_ref), channel_id=1, source_target_pairs={{0,1},{1,0},{2,3},{3,2},{4,5},{5,4},{6,7},{7,6},{8,9},{9,8},{10,11... | collective-permute-start | bytes 595976 | tf_op jit(solution)/shard_map/ppermute | solution.py:197
  5.5 10.2 %collective-permute-start.1 = (bf16[97,8,128]{2,1,0:T(8,128)(2,1)S(1)}, bf16[97,8,128]{2,1,0:T(8,128)(2,1)S(1)}, u32[]{:S(2)}, u32[]{:S(2)}) collective-permute-start(bf16[97,8,128]{2,1,0:T(8,128)(2,1)S(1)} %get-tuple-element.18.own_ref), channel_id=1, source_target_pairs={{0,4},{2,6},{8,0},{10,2},{12,8},{14,10},{4,12},{6,14},{1,5},{3,7},... | collective-permute-start | bytes 595976 | tf_op jit(solution)/shard_map/ppermute | solution.py:191
  5.6 12.2 %collective-permute-start.2 = (bf16[97,8,128]{2,1,0:T(8,128)(2,1)S(1)}, bf16[97,8,128]{2,1,0:T(8,128)(2,1)S(1)}, u32[]{:S(2)}, u32[]{:S(2)}) collective-permute-start(bf16[97,8,128]{2,1,0:T(8,128)(2,1)S(1)} %get-tuple-element.18.own_ref), channel_id=1, source_target_pairs={{0,2},{2,0},{4,6},{6,4},{8,10},{10,8},{12,14},{14,12},{1,3},{3,1},... | collective-permute-start | bytes 595976 | tf_op jit(solution)/shard_map/ppermute | solution.py:194
  10.4 9.8 %collective-permute-start.4 = (bf16[96,8,128]{2,1,0:T(8,128)(2,1)S(1)}, bf16[96,8,128]{2,1,0:T(8,128)(2,1)S(1)}, u32[]{:S(2)}, u32[]{:S(2)}) collective-permute-start(bf16[96,8,128]{2,1,0:T(8,128)(2,1)S(1)} %collective-permute-done.3.refs_1_), channel_id=1, source_target_pairs={{0,2},{2,0},{4,6},{6,4},{8,10},{10,8},{12,14},{14,12},{1,3},{3,1},... | collective-permute-start | bytes 589832 | tf_op jit(solution)/shard_map/ppermute | solution.py:194
  11.8 8.6 %collective-permute-start.5 = (bf16[8,128]{1,0:T(8,128)(2,1)S(1)}, bf16[8,128]{1,0:T(8,128)(2,1)S(1)}, u32[]{:S(2)}, u32[]{:S(2)}) collective-permute-start(bf16[8,128]{1,0:T(8,128)(2,1)S(1)} %get-tuple-element.22), channel_id=1, source_target_pairs={{0,8},{2,10},{8,12},{10,14},{12,4},{14,6},{4,0},{6,2},{1,9},{3,11}... | collective-permute-start | bytes 6152 | tf_op jit(solution)/shard_map/ppermute | solution.py:191
  15.1 11.2 %collective-permute-start.8 = (bf16[96,8,128]{2,1,0:T(8,128)(2,1)S(1)}, bf16[96,8,128]{2,1,0:T(8,128)(2,1)S(1)}, u32[]{:S(2)}, u32[]{:S(2)}) collective-permute-start(bf16[96,8,128]{2,1,0:T(8,128)(2,1)S(1)} %collective-permute-done.3.refs_1_), channel_id=1, source_target_pairs={{0,8},{2,10},{8,12},{10,14},{12,4},{14,6},{4,0},{6,2},{1,9},{3,11}... | collective-permute-start | bytes 589832 | tf_op jit(solution)/shard_map/ppermute | solution.py:191
  15.7 5.4 %collective-permute-start.6 = (bf16[8,128]{1,0:T(8,128)(2,1)S(1)}, bf16[8,128]{1,0:T(8,128)(2,1)S(1)}, u32[]{:S(2)}, u32[]{:S(2)}) collective-permute-start(bf16[8,128]{1,0:T(8,128)(2,1)S(1)} %get-tuple-element.22), channel_id=1, source_target_pairs={{0,12},{2,14},{8,4},{10,6},{12,0},{14,2},{4,8},{6,10},{1,13},{3,15... | collective-permute-start | bytes 6152 | tf_op jit(solution)/shard_map/ppermute | solution.py:191
  17.7 8.6 %collective-permute-start.9 = (bf16[97,8,128]{2,1,0:T(8,128)(2,1)S(1)}, bf16[97,8,128]{2,1,0:T(8,128)(2,1)S(1)}, u32[]{:S(2)}, u32[]{:S(2)}) collective-permute-start(bf16[97,8,128]{2,1,0:T(8,128)(2,1)S(1)} %collective-permute-done.1.refs_0_), channel_id=1, source_target_pairs={{0,2},{2,0},{4,6},{6,4},{8,10},{10,8},{12,14},{14,12},{1,3},{3,1},... | collective-permute-start | bytes 595976 | tf_op jit(solution)/shard_map/ppermute | solution.py:194
  20.2 7.2 %collective-permute-start.10 = (bf16[96,8,128]{2,1,0:T(8,128)(2,1)S(1)}, bf16[96,8,128]{2,1,0:T(8,128)(2,1)S(1)}, u32[]{:S(2)}, u32[]{:S(2)}) collective-permute-start(bf16[96,8,128]{2,1,0:T(8,128)(2,1)S(1)} %collective-permute-done.4.refs_2_), channel_id=1, source_target_pairs={{0,8},{2,10},{8,12},{10,14},{12,4},{14,6},{4,0},{6,2},{1,9},{3,11}... | collective-permute-start | bytes 589832 | tf_op jit(solution)/shard_map/ppermute | solution.py:191
  21.1 4.1 %collective-permute-start.7 = (bf16[16,128]{1,0:T(8,128)(2,1)S(1)}, bf16[16,128]{1,0:T(8,128)(2,1)S(1)}, u32[]{:S(2)}, u32[]{:S(2)}) collective-permute-start(bf16[16,128]{1,0:T(8,128)(2,1)S(1)} %constant_dynamic-update-slice_fusion.refs_3_.refs_1_), channel_id=1, source_target_pairs={{0,2},{2,0},{4,6},{6,4},{8,10},{10,8},{12,14},{14,12},{1,3},{3,1},... | collective-permute-start | bytes 12296 | tf_op jit(solution)/shard_map/ppermute | solution.py:194
  28.0 1.5 %collective-permute-start.11 = (bf16[136,768]{1,0:T(8,128)(2,1)S(1)}, bf16[136,768]{1,0:T(8,128)(2,1)S(1)}, u32[]{:S(2)}, u32[]{:S(2)}) collective-permute-start(bf16[136,768]{1,0:T(8,128)(2,1)S(1)} %send_scores.1), channel_id=1, source_target_pairs={{0,1},{1,0},{2,3},{3,2},{4,5},{5,4},{6,7},{7,6},{8,9},{9,8},{10,11... | collective-permute-start | bytes 626696 | tf_op jit(solution)/shard_map/ppermute | solution.py:197

commit v23 on v21

--- a/solution.py
+++ b/solution.py
@@ -244,10 +244,12 @@
         moved, beside, other = lax.optimization_barrier((moved, beside, other))
         opposite = along(moved, 1)
         moved_beside = across(moved)
+        moved_beside, ahead = lax.optimization_barrier((moved_beside, ahead))
+        last_ = along(moved_beside, 1)
         ahead_beside = across(ahead)
-        last = [along(moved_beside, 1)]
+        last = [last_, ahead_beside]
         unit, side, sums, mixed = first(own, other, beside, moved, moved_beside)
-        sums, mixed = more(unit, side, sums, mixed, ahead, opposite, ahead_beside)
+        sums, mixed = more(unit, side, sums, mixed, ahead, opposite)
     else:
         unit, side, sums, mixed = first(own, other, beside)
 

time: 28.3 us -> 29 us (1.025)
  waiting for transfers between devices: 7.71 us -> 9.72 us
  starting transfers between devices: 14.6 us -> 13.3 us
    ppermute x3, waiting for transfers between devices: 2.16 us -> 3.91 us  [across(): return lax.ppermute(array, 'shard', [(at, at ^ 1) for at in range(shards)])]
    ppermute x3, starting transfers between devices: 5.29 us -> 4.47 us  [across(): return lax.ppermute(array, 'shard', [(at, at ^ 1) for at in range(shards)])]
    ppermute x4, starting transfers between devices: 9.19 us -> 8.75 us  [along(): return lax.ppermute(array, 'shard', pairs)]
    ppermute x4, waiting for transfers between devices: 4.62 us -> 5 us  [along(): return lax.ppermute(array, 'shard', pairs)]
  transfers between devices with their start and end apart: 9 -> 9, of which waited for: 6 -> 7; matrix products, arithmetic and copies ran while one was open for 0% -> 0% of each run, Pallas kernels for 10% -> 9%
where the time goes in v23:
time: 29 us; the launch traced here: 28.9 us
  starting transfers between devices  13.3 us (46%)
  waiting for transfers between devices  9.72 us (34%)
  Pallas kernels  4.26 us (15%)
  local copies, waits for them, and re-layouts  0.9 us (3%)
  between operations  0.71 us (2%)
    ppermute x4, starting transfers between devices, along(): return lax.ppermute(array, 'shard', pairs)  8.75 us
    ppermute x4, waiting for transfers between devices, along(): return lax.ppermute(array, 'shard', pairs)  5 us
    ppermute x3, starting transfers between devices, across(): return lax.ppermute(array, 'shard', [(at, at ^ 1) for at in range(shards)])  4.47 us
    ppermute x3, waiting for transfers between devices, across(): return lax.ppermute(array, 'shard', [(at, at ^ 1) for at in range(shards)])  3.91 us
    pallas_call x1, Pallas kernels, first(): pl.pallas_call(first_kernel, out_shape=[shape(queries, width, dtype=bf16)...  1.19 us
    pallas_call x1, Pallas kernels, local(): pl.pallas_call(combine_kernel, out_shape=[shape(1, count), shape(count, w...  0.95 us
    unnamed x6, local copies, waits for them, and re-layouts  0.9 us
    pallas_call x1, Pallas kernels, more(): pl.pallas_call(more_kernel, out_shape=[shape(queries, 128), shape(queries...  0.86 us
  transfers between devices with their start and end apart: 9, of which 7 were waited for; matrix products, arithmetic and copies ran while one was open for 0% of the time, Pallas kernels for 9%

profile of v23, /device:TPU:0, one launch (start us, length us, event | category | flops | bytes accessed | tf_op | source)
XLA Modules:
  0.0 28.9 jit_solution(5692389887007589047)
XLA Ops:
  0.6 0.0 copy-start
  0.6 0.0 copy-start.1
  0.7 0.0 copy-start.2
  0.7 0.9 %copy-done = bf16[128,768]{1,0:T(8,128)(2,1)S(1)} copy-done((bf16[128,768]{1,0:T(8,128)(2,1)S(1)}, bf16[128,768]{1,0:T(8,128)(2,1)}, u32[]{:S(2)}) %copy-start) | copy-done | bytes 196632
  1.6 0.0 copy-done.1
  1.6 0.0 copy-done.2
  1.6 4.1 %collective-permute-start = (bf16[97,8,128]{2,1,0:T(8,128)(2,1)S(1)}, bf16[97,8,128]{2,1,0:T(8,128)(2,1)S(1)}, u32[]{:S(2)}, u32[]{:S(2)}) collective-permute-start(bf16[97,8,128]{2,1,0:T(8,128)(2,1)S(1)} %pack.1.own_ref), channel_id=1, source_target_pairs={{0,8},{2,10},{8,12},{10,14},{12,4},{14,6},{4,0},{6,2},{1,9},{3,11}... | collective-permute-start | bytes 595976 | tf_op jit(solution)/shard_map/ppermute | solution.py:176
  5.7 1.5 %collective-permute-start.1 = (bf16[97,8,128]{2,1,0:T(8,128)(2,1)S(1)}, bf16[97,8,128]{2,1,0:T(8,128)(2,1)S(1)}, u32[]{:S(2)}, u32[]{:S(2)}) collective-permute-start(bf16[97,8,128]{2,1,0:T(8,128)(2,1)S(1)} %pack.1.own_ref), channel_id=1, source_target_pairs={{0,2},{2,0},{4,6},{6,4},{8,10},{10,8},{12,14},{14,12},{1,3},{3,1},... | collective-permute-start | bytes 595976 | tf_op jit(solution)/shard_map/ppermute | solution.py:179
  7.2 0.0 collective-permute-start.2
  7.2 0.0 collective-permute-start.4
  7.2 3.9 %collective-permute-done.refs_1_ = bf16[97,8,128]{2,1,0:T(8,128)(2,1)S(1)} collective-permute-done((bf16[97,8,128]{2,1,0:T(8,128)(2,1)S(1)}, bf16[97,8,128]{2,1,0:T(8,128)(2,1)S(1)}, u32[]{:S(2)}, u32[]{:S(2)}) %collective-permute-start) | collective-permute-done | bytes 198688 | tf_op jit(solution)/shard_map/ppermute | solution.py:176
  11.0 1.1 %collective-permute-done.1.refs_0_ = bf16[97,8,128]{2,1,0:T(8,128)(2,1)S(1)} collective-permute-done((bf16[97,8,128]{2,1,0:T(8,128)(2,1)S(1)}, bf16[97,8,128]{2,1,0:T(8,128)(2,1)S(1)}, u32[]{:S(2)}, u32[]{:S(2)}) %collective-permute-start.1) | collective-permute-done | bytes 198688 | tf_op jit(solution)/shard_map/ppermute | solution.py:179
  12.1 0.0 collective-permute-done.2.other_ref
  12.1 1.5 %collective-permute-start.3 = (bf16[97,8,128]{2,1,0:T(8,128)(2,1)S(1)}, bf16[97,8,128]{2,1,0:T(8,128)(2,1)S(1)}, u32[]{:S(2)}, u32[]{:S(2)}) collective-permute-start(bf16[97,8,128]{2,1,0:T(8,128)(2,1)S(1)} %collective-permute-done.refs_1_), channel_id=1, source_target_pairs={{0,2},{2,0},{4,6},{6,4},{8,10},{10,8},{12,14},{14,12},{1,3},{3,1},... | collective-permute-start | bytes 595976 | tf_op jit(solution)/shard_map/ppermute | solution.py:179
  13.6 2.3 %collective-permute-start.5 = (bf16[97,8,128]{2,1,0:T(8,128)(2,1)S(1)}, bf16[97,8,128]{2,1,0:T(8,128)(2,1)S(1)}, u32[]{:S(2)}, u32[]{:S(2)}) collective-permute-start(bf16[97,8,128]{2,1,0:T(8,128)(2,1)S(1)} %collective-permute-done.refs_1_), channel_id=1, source_target_pairs={{0,8},{2,10},{8,12},{10,14},{12,4},{14,6},{4,0},{6,2},{1,9},{3,11}... | collective-permute-start | bytes 595976 | tf_op jit(solution)/shard_map/ppermute | solution.py:176
  15.9 0.4 %collective-permute-done.4.refs_0_ = bf16[97,8,128]{2,1,0:T(8,128)(2,1)S(1)} collective-permute-done((bf16[97,8,128]{2,1,0:T(8,128)(2,1)S(1)}, bf16[97,8,128]{2,1,0:T(8,128)(2,1)S(1)}, u32[]{:S(2)}, u32[]{:S(2)}) %collective-permute-start.4) | collective-permute-done | bytes 198688 | tf_op jit(solution)/shard_map/ppermute | solution.py:176
  16.3 1.5 %collective-permute-done.3.refs_2_ = bf16[97,8,128]{2,1,0:T(8,128)(2,1)S(1)} collective-permute-done((bf16[97,8,128]{2,1,0:T(8,128)(2,1)S(1)}, bf16[97,8,128]{2,1,0:T(8,128)(2,1)S(1)}, u32[]{:S(2)}, u32[]{:S(2)}) %collective-permute-start.3) | collective-permute-done | bytes 198688 | tf_op jit(solution)/shard_map/ppermute | solution.py:179
  17.8 2.3 %collective-permute-start.6 = (bf16[97,8,128]{2,1,0:T(8,128)(2,1)S(1)}, bf16[97,8,128]{2,1,0:T(8,128)(2,1)S(1)}, u32[]{:S(2)}, u32[]{:S(2)}) collective-permute-start(bf16[97,8,128]{2,1,0:T(8,128)(2,1)S(1)} %collective-permute-done.3.refs_2_), channel_id=1, source_target_pairs={{0,8},{2,10},{8,12},{10,14},{12,4},{14,6},{4,0},{6,2},{1,9},{3,11}... | collective-permute-start | bytes 595976 | tf_op jit(solution)/shard_map/ppermute | solution.py:176
  20.1 1.5 %collective-permute-start.7 = (bf16[97,8,128]{2,1,0:T(8,128)(2,1)S(1)}, bf16[97,8,128]{2,1,0:T(8,128)(2,1)S(1)}, u32[]{:S(2)}, u32[]{:S(2)}) collective-permute-start(bf16[97,8,128]{2,1,0:T(8,128)(2,1)S(1)} %collective-permute-done.4.refs_0_), channel_id=1, source_target_pairs={{0,2},{2,0},{4,6},{6,4},{8,10},{10,8},{12,14},{14,12},{1,3},{3,1},... | collective-permute-start | bytes 595976 | tf_op jit(solution)/shard_map/ppermute | solution.py:179
  21.6 1.2 %first_scores.1 = (bf16[256,768]{1,0:T(8,128)(2,1)S(1)}, f32[256,128]{1,0:T(8,128)S(1)}, f32[256,128]{1,0:T(8,128)S(1)}, f32[256,768]{1,0:T(8,128)S(1)}) custom-call(bf16[97,8,128]{2,1,0:T(8,128)(2,1)S(1)} %pack.1.own_ref, bf16[97,8,128]{2,1,0:T(8,128)(2,1)S(1)} %collective-permute-done.2.other_ref, bf16[97,8,128]{2,1,0:T(8,128)(2,1)S(1)} %collective-permute-done.1.refs_0_, ...), custom_call_target="tpu_custom_call" | custom-call | flops 40265318400 | bytes 2359296 | tf_op jit(solution)/shard_map/first_scores/pallas_call | solution.py:185
  22.8 0.0 collective-permute-done.5.refs_1_
  22.8 0.9 %more_scores.1 = (f32[256,128]{1,0:T(8,128)S(1)}, f32[256,768]{1,0:T(8,128)S(1)}) custom-call(bf16[256,768]{1,0:T(8,128)(2,1)S(1)} %get-tuple-element.21.unit_ref, f32[256,128]{1,0:T(8,128)S(1)} %get-tuple-element.22.side_ref, f32[256,128]{1,0:T(8,128)S(1)} %get-tuple-element.23.old_sums_ref, ...), custom_call_target="tpu_custom_call", output_to_operand_aliasing={{0}: (2, {}), {1}: (3, {})} | custom-call | flops 20132659200 | bytes 1966080 | tf_op jit(solution)/shard_map/more_scores/pallas_call | solution.py:199
  23.7 0.8 %collective-permute-done.6.refs_0_ = bf16[97,8,128]{2,1,0:T(8,128)(2,1)S(1)} collective-permute-done((bf16[97,8,128]{2,1,0:T(8,128)(2,1)S(1)}, bf16[97,8,128]{2,1,0:T(8,128)(2,1)S(1)}, u32[]{:S(2)}, u32[]{:S(2)}) %collective-permute-start.6) | collective-permute-done | bytes 198688 | tf_op jit(solution)/shard_map/ppermute | solution.py:176
  24.5 1.3 %collective-permute-done.7.refs_1_ = bf16[97,8,128]{2,1,0:T(8,128)(2,1)S(1)} collective-permute-done((bf16[97,8,128]{2,1,0:T(8,128)(2,1)S(1)}, bf16[97,8,128]{2,1,0:T(8,128)(2,1)S(1)}, u32[]{:S(2)}, u32[]{:S(2)}) %collective-permute-start.7) | collective-permute-done | bytes 198688 | tf_op jit(solution)/shard_map/ppermute | solution.py:179
  25.8 0.6 %send_scores.1 = bf16[136,768]{1,0:T(8,128)(2,1)S(1)} custom-call(bf16[256,768]{1,0:T(8,128)(2,1)S(1)} %get-tuple-element.21.unit_ref, f32[256,128]{1,0:T(8,128)S(1)} %get-tuple-element.22.side_ref, f32[256,128]{1,0:T(8,128)S(1)} %get-tuple-element.26.old_sums_ref, f32[256,768]{1,0:T(8,128)S(1)} %get-tuple-element.27.old_mixed_ref, ...), custom_call_target="tpu_custom_call" | custom-call | flops 10066329600 | bytes 1179648 | tf_op jit(solution)/shard_map/send_scores/pallas_call | solution.py:209
  26.4 0.1 collective-permute-start.8
  26.5 0.6 %keep_scores.1 = (f32[128,128]{1,0:T(8,128)S(1)}, f32[128,768]{1,0:T(8,128)S(1)}) custom-call(bf16[256,768]{1,0:T(8,128)(2,1)S(1)} %get-tuple-element.21.unit_ref, f32[256,128]{1,0:T(8,128)S(1)} %get-tuple-element.22.side_ref, f32[256,128]{1,0:T(8,128)S(1)} %get-tuple-element.26.old_sums_ref, f32[256,768]{1,0:T(8,128)S(1)} %get-tuple-element.27.old_mixed_ref, ...), custom_call_target="tpu_custom_call" | custom-call | flops 10066329600 | bytes 1179648 | tf_op jit(solution)/shard_map/keep_scores/pallas_call | solution.py:216
  27.1 0.8 %collective-permute-done.8.got_ref = bf16[136,768]{1,0:T(8,128)(2,1)S(1)} collective-permute-done((bf16[136,768]{1,0:T(8,128)(2,1)S(1)}, bf16[136,768]{1,0:T(8,128)(2,1)S(1)}, u32[]{:S(2)}, u32[]{:S(2)}) %collective-permute-start.8) | collective-permute-done | bytes 208928 | tf_op jit(solution)/shard_map/ppermute | solution.py:182
  27.9 1.0 %combine.1 = (f32[1,128]{1,0:T(1,128)}, f32[128,768]{1,0:T(8,128)}) custom-call(f32[128,128]{1,0:T(8,128)S(1)} %get-tuple-element.28.sums_ref, f32[128,768]{1,0:T(8,128)S(1)} %get-tuple-element.29.mixed_ref, bf16[136,768]{1,0:T(8,128)(2,1)S(1)} %collective-permute-done.8.got_ref), custom_call_target="tpu_custom_call" | custom-call | tf_op jit(solution)/shard_map/combine/pallas_call | solution.py:265
  (2 shorter events, 0.0 us)
Async XLA Ops:
  0.6 0.9 %copy-start = (bf16[128,768]{1,0:T(8,128)(2,1)S(1)}, bf16[128,768]{1,0:T(8,128)(2,1)}, u32[]{:S(2)}) copy-start(bf16[128,768]{1,0:T(8,128)(2,1)} %param.3) | copy-start | bytes 589828
  0.6 0.9 %copy-start.1 = (s32[128,1]{0,1:T(1,128)S(1)}, s32[128,1]{0,1:T(1,128)}, u32[]{:S(2)}) copy-start(s32[128,1]{0,1:T(1,128)} %param.4) | copy-start | bytes 1540
  0.7 0.9 %copy-start.2 = (s32[128]{0:T(128)S(1)}, s32[128]{0:T(128)}, u32[]{:S(2)}) copy-start(s32[128]{0:T(128)} %param.5) | copy-start | bytes 1540
  1.6 9.4 %collective-permute-start = (bf16[97,8,128]{2,1,0:T(8,128)(2,1)S(1)}, bf16[97,8,128]{2,1,0:T(8,128)(2,1)S(1)}, u32[]{:S(2)}, u32[]{:S(2)}) collective-permute-start(bf16[97,8,128]{2,1,0:T(8,128)(2,1)S(1)} %pack.1.own_ref), channel_id=1, source_target_pairs={{0,8},{2,10},{8,12},{10,14},{12,4},{14,6},{4,0},{6,2},{1,9},{3,11}... | collective-permute-start | bytes 595976 | tf_op jit(solution)/shard_map/ppermute | solution.py:176
  5.7 6.4 %collective-permute-start.1 = (bf16[97,8,128]{2,1,0:T(8,128)(2,1)S(1)}, bf16[97,8,128]{2,1,0:T(8,128)(2,1)S(1)}, u32[]{:S(2)}, u32[]{:S(2)}) collective-permute-start(bf16[97,8,128]{2,1,0:T(8,128)(2,1)S(1)} %pack.1.own_ref), channel_id=1, source_target_pairs={{0,2},{2,0},{4,6},{6,4},{8,10},{10,8},{12,14},{14,12},{1,3},{3,1},... | collective-permute-start | bytes 595976 | tf_op jit(solution)/shard_map/ppermute | solution.py:179
  7.2 4.9 %collective-permute-start.2 = (bf16[97,8,128]{2,1,0:T(8,128)(2,1)S(1)}, bf16[97,8,128]{2,1,0:T(8,128)(2,1)S(1)}, u32[]{:S(2)}, u32[]{:S(2)}) collective-permute-start(bf16[97,8,128]{2,1,0:T(8,128)(2,1)S(1)} %pack.1.own_ref), channel_id=1, source_target_pairs={{0,1},{1,0},{2,3},{3,2},{4,5},{5,4},{6,7},{7,6},{8,9},{9,8},{10,11... | collective-permute-start | bytes 595976 | tf_op jit(solution)/shard_map/ppermute | solution.py:182
  7.2 9.1 %collective-permute-start.4 = (bf16[97,8,128]{2,1,0:T(8,128)(2,1)S(1)}, bf16[97,8,128]{2,1,0:T(8,128)(2,1)S(1)}, u32[]{:S(2)}, u32[]{:S(2)}) collective-permute-start(bf16[97,8,128]{2,1,0:T(8,128)(2,1)S(1)} %pack.1.own_ref), channel_id=1, source_target_pairs={{0,4},{2,6},{8,0},{10,2},{12,8},{14,10},{4,12},{6,14},{1,5},{3,7},... | collective-permute-start | bytes 595976 | tf_op jit(solution)/shard_map/ppermute | solution.py:176
  12.1 5.7 %collective-permute-start.3 = (bf16[97,8,128]{2,1,0:T(8,128)(2,1)S(1)}, bf16[97,8,128]{2,1,0:T(8,128)(2,1)S(1)}, u32[]{:S(2)}, u32[]{:S(2)}) collective-permute-start(bf16[97,8,128]{2,1,0:T(8,128)(2,1)S(1)} %collective-permute-done.refs_1_), channel_id=1, source_target_pairs={{0,2},{2,0},{4,6},{6,4},{8,10},{10,8},{12,14},{14,12},{1,3},{3,1},... | collective-permute-start | bytes 595976 | tf_op jit(solution)/shard_map/ppermute | solution.py:179
  13.6 9.2 %collective-permute-start.5 = (bf16[97,8,128]{2,1,0:T(8,128)(2,1)S(1)}, bf16[97,8,128]{2,1,0:T(8,128)(2,1)S(1)}, u32[]{:S(2)}, u32[]{:S(2)}) collective-permute-start(bf16[97,8,128]{2,1,0:T(8,128)(2,1)S(1)} %collective-permute-done.refs_1_), channel_id=1, source_target_pairs={{0,8},{2,10},{8,12},{10,14},{12,4},{14,6},{4,0},{6,2},{1,9},{3,11}... | collective-permute-start | bytes 595976 | tf_op jit(solution)/shard_map/ppermute | solution.py:176
  17.8 6.7 %collective-permute-start.6 = (bf16[97,8,128]{2,1,0:T(8,128)(2,1)S(1)}, bf16[97,8,128]{2,1,0:T(8,128)(2,1)S(1)}, u32[]{:S(2)}, u32[]{:S(2)}) collective-permute-start(bf16[97,8,128]{2,1,0:T(8,128)(2,1)S(1)} %collective-permute-done.3.refs_2_), channel_id=1, source_target_pairs={{0,8},{2,10},{8,12},{10,14},{12,4},{14,6},{4,0},{6,2},{1,9},{3,11}... | collective-permute-start | bytes 595976 | tf_op jit(solution)/shard_map/ppermute | solution.py:176
  20.1 5.7 %collective-permute-start.7 = (bf16[97,8,128]{2,1,0:T(8,128)(2,1)S(1)}, bf16[97,8,128]{2,1,0:T(8,128)(2,1)S(1)}, u32[]{:S(2)}, u32[]{:S(2)}) collective-permute-start(bf16[97,8,128]{2,1,0:T(8,128)(2,1)S(1)} %collective-permute-done.4.refs_0_), channel_id=1, source_target_pairs={{0,2},{2,0},{4,6},{6,4},{8,10},{10,8},{12,14},{14,12},{1,3},{3,1},... | collective-permute-start | bytes 595976 | tf_op jit(solution)/shard_map/ppermute | solution.py:179
  26.4 1.5 %collective-permute-start.8 = (bf16[136,768]{1,0:T(8,128)(2,1)S(1)}, bf16[136,768]{1,0:T(8,128)(2,1)S(1)}, u32[]{:S(2)}, u32[]{:S(2)}) collective-permute-start(bf16[136,768]{1,0:T(8,128)(2,1)S(1)} %send_scores.1), channel_id=1, source_target_pairs={{0,1},{1,0},{2,3},{3,2},{4,5},{5,4},{6,7},{7,6},{8,9},{9,8},{10,11... | collective-permute-start | bytes 626696 | tf_op jit(solution)/shard_map/ppermute | solution.py:182

commit v24 on v21

--- a/solution.py
+++ b/solution.py
@@ -177,6 +177,17 @@
 
     def across(array):
         return lax.ppermute(array, "shard", [(at, at ^ 1) for at in range(shards)])
+
+    def two_ways(array, ring_lane):
+        pairs = []
+        for at in range(rounds):
+            for side in range(2):
+                here, there = 2 * ring[at] + side, 2 * ring[(at + 1) % rounds] + side
+                pairs += [
+                    (here * lanes + lane, (there if lane == ring_lane else here ^ 1) * lanes + lane)
+                    for lane in range(lanes)
+                ]
+        return lax.ppermute(array, ("shard", "owner"), pairs)
 
     def swap(array):
         return lax.ppermute(array, "owner", [(at, lanes - 1 - at) for at in range(lanes)])
@@ -242,12 +253,11 @@
     if rounds == 4:
         ahead = along(own, -1)
         moved, beside, other = lax.optimization_barrier((moved, beside, other))
-        opposite = along(moved, 1)
-        moved_beside = across(moved)
+        sooner, later = two_ways(moved, 1), two_ways(moved, 0)
         ahead_beside = across(ahead)
-        last = [along(moved_beside, 1)]
-        unit, side, sums, mixed = first(own, other, beside, moved, moved_beside)
-        sums, mixed = more(unit, side, sums, mixed, ahead, opposite, ahead_beside)
+        last = [two_ways(sooner, 0)]
+        unit, side, sums, mixed = first(own, other, beside, moved, sooner)
+        sums, mixed = more(unit, side, sums, mixed, ahead, later, ahead_beside)
     else:
         unit, side, sums, mixed = first(own, other, beside)
 

time: 28.3 us -> 28.6 us (1.011)
  waiting for transfers between devices: 7.71 us -> 8.14 us
    ppermute x0 -> x3, starting transfers between devices: none -> 6.29 us  [two_ways(): return lax.ppermute(array, ('shard', 'owner'), pairs)]
    ppermute x4 -> x2, starting transfers between devices: 9.19 us -> 4.09 us  [along(): return lax.ppermute(array, 'shard', pairs)]
    ppermute x3 -> x2, starting transfers between devices: 5.29 us -> 3.74 us  [across(): return lax.ppermute(array, 'shard', [(at, at ^ 1) for at in range(shards)])]
    ppermute x3 -> x2, waiting for transfers between devices: 2.16 us -> 2.83 us  [across(): return lax.ppermute(array, 'shard', [(at, at ^ 1) for at in range(shards)])]
    ppermute x4 -> x2, waiting for transfers between devices: 4.62 us -> 4.27 us  [along(): return lax.ppermute(array, 'shard', pairs)]
    ppermute x0 -> x3, waiting for transfers between devices: none -> 0.3 us  [two_ways(): return lax.ppermute(array, ('shard', 'owner'), pairs)]
where the time goes in v24:
time: 28.6 us; the launch traced here: 28.4 us
  starting transfers between devices  14.4 us (50%)
  waiting for transfers between devices  8.14 us (28%)
  Pallas kernels  4.26 us (15%)
  local copies, waits for them, and re-layouts  0.9 us (3%)
  between operations  0.71 us (2%)
    ppermute x3, starting transfers between devices, two_ways(): return lax.ppermute(array, ('shard', 'owner'), pairs)  6.29 us
    ppermute x2, waiting for transfers between devices, along(): return lax.ppermute(array, 'shard', pairs)  4.27 us
    ppermute x2, starting transfers between devices, along(): return lax.ppermute(array, 'shard', pairs)  4.09 us
    ppermute x2, starting transfers between devices, across(): return lax.ppermute(array, 'shard', [(at, at ^ 1) for at in range(shards)])  3.74 us
    ppermute x2, waiting for transfers between devices, across(): return lax.ppermute(array, 'shard', [(at, at ^ 1) for at in range(shards)])  2.83 us
    pallas_call x1, Pallas kernels, first(): pl.pallas_call(first_kernel, out_shape=[shape(queries, width, dtype=bf16)...  1.19 us
    pallas_call x1, Pallas kernels, more(): pl.pallas_call(more_kernel, out_shape=[shape(queries, 128), shape(queries...  1.05 us
    pallas_call x1, Pallas kernels, local(): pl.pallas_call(combine_kernel, out_shape=[shape(1, count), shape(count, w...  0.95 us
  transfers between devices with their start and end apart: 9, of which 6 were waited for; matrix products, arithmetic and copies ran while one was open for 0% of the time, Pallas kernels for 10%

profile of v24, /device:TPU:0, one launch (start us, length us, event | category | flops | bytes accessed | tf_op | source)
XLA Modules:
  0.0 28.4 jit_solution(10202396371332623702)
XLA Ops:
  0.6 0.0 copy-start
  0.6 0.0 copy-start.1
  0.7 0.0 copy-start.2
  0.7 0.9 %copy-done = bf16[128,768]{1,0:T(8,128)(2,1)S(1)} copy-done((bf16[128,768]{1,0:T(8,128)(2,1)S(1)}, bf16[128,768]{1,0:T(8,128)(2,1)}, u32[]{:S(2)}) %copy-start) | copy-done | bytes 196632
  1.6 0.0 copy-done.1
  1.6 0.0 copy-done.2
  1.6 4.1 %collective-permute-start = (bf16[97,8,128]{2,1,0:T(8,128)(2,1)S(1)}, bf16[97,8,128]{2,1,0:T(8,128)(2,1)S(1)}, u32[]{:S(2)}, u32[]{:S(2)}) collective-permute-start(bf16[97,8,128]{2,1,0:T(8,128)(2,1)S(1)} %pack.1.own_ref), channel_id=1, source_target_pairs={{0,8},{2,10},{8,12},{10,14},{12,4},{14,6},{4,0},{6,2},{1,9},{3,11}... | collective-permute-start | bytes 595976 | tf_op jit(solution)/shard_map/ppermute | solution.py:176
  5.7 1.5 %collective-permute-start.1 = (bf16[97,8,128]{2,1,0:T(8,128)(2,1)S(1)}, bf16[97,8,128]{2,1,0:T(8,128)(2,1)S(1)}, u32[]{:S(2)}, u32[]{:S(2)}) collective-permute-start(bf16[97,8,128]{2,1,0:T(8,128)(2,1)S(1)} %pack.1.own_ref), channel_id=1, source_target_pairs={{0,2},{2,0},{4,6},{6,4},{8,10},{10,8},{12,14},{14,12},{1,3},{3,1},... | collective-permute-start | bytes 595976 | tf_op jit(solution)/shard_map/ppermute | solution.py:179
  7.2 0.0 collective-permute-start.2
  7.2 0.0 collective-permute-start.4
  7.2 3.9 %collective-permute-done.refs_1_ = bf16[97,8,128]{2,1,0:T(8,128)(2,1)S(1)} collective-permute-done((bf16[97,8,128]{2,1,0:T(8,128)(2,1)S(1)}, bf16[97,8,128]{2,1,0:T(8,128)(2,1)S(1)}, u32[]{:S(2)}, u32[]{:S(2)}) %collective-permute-start) | collective-permute-done | bytes 198688 | tf_op jit(solution)/shard_map/ppermute | solution.py:176
  11.0 1.1 %collective-permute-done.1.refs_0_ = bf16[97,8,128]{2,1,0:T(8,128)(2,1)S(1)} collective-permute-done((bf16[97,8,128]{2,1,0:T(8,128)(2,1)S(1)}, bf16[97,8,128]{2,1,0:T(8,128)(2,1)S(1)}, u32[]{:S(2)}, u32[]{:S(2)}) %collective-permute-start.1) | collective-permute-done | bytes 198688 | tf_op jit(solution)/shard_map/ppermute | solution.py:179
  12.1 0.0 collective-permute-done.2.other_ref
  12.1 1.5 %collective-permute-start.3 = (bf16[97,8,128]{2,1,0:T(8,128)(2,1)S(1)}, bf16[97,8,128]{2,1,0:T(8,128)(2,1)S(1)}, u32[]{:S(2)}, u32[]{:S(2)}) collective-permute-start(bf16[97,8,128]{2,1,0:T(8,128)(2,1)S(1)} %collective-permute-done.refs_1_), channel_id=1, source_target_pairs={{0,2},{1,9},{2,0},{3,11},{8,10},{9,13},{10,8},{11,15},{12,14},{13,... | collective-permute-start | bytes 595976 | tf_op jit(solution)/shard_map/ppermute | solution.py:190
  13.6 2.3 %collective-permute-start.5 = (bf16[97,8,128]{2,1,0:T(8,128)(2,1)S(1)}, bf16[97,8,128]{2,1,0:T(8,128)(2,1)S(1)}, u32[]{:S(2)}, u32[]{:S(2)}) collective-permute-start(bf16[97,8,128]{2,1,0:T(8,128)(2,1)S(1)} %collective-permute-done.refs_1_), channel_id=1, source_target_pairs={{0,8},{1,3},{2,10},{3,1},{8,12},{9,11},{10,14},{11,9},{12,4},{13,1... | collective-permute-start | bytes 595976 | tf_op jit(solution)/shard_map/ppermute | solution.py:190
  15.9 0.4 %collective-permute-done.4.refs_0_ = bf16[97,8,128]{2,1,0:T(8,128)(2,1)S(1)} collective-permute-done((bf16[97,8,128]{2,1,0:T(8,128)(2,1)S(1)}, bf16[97,8,128]{2,1,0:T(8,128)(2,1)S(1)}, u32[]{:S(2)}, u32[]{:S(2)}) %collective-permute-start.4) | collective-permute-done | bytes 198688 | tf_op jit(solution)/shard_map/ppermute | solution.py:176
  16.3 2.3 %collective-permute-start.6 = (bf16[97,8,128]{2,1,0:T(8,128)(2,1)S(1)}, bf16[97,8,128]{2,1,0:T(8,128)(2,1)S(1)}, u32[]{:S(2)}, u32[]{:S(2)}) collective-permute-start(bf16[97,8,128]{2,1,0:T(8,128)(2,1)S(1)} %collective-permute-done.4.refs_0_), channel_id=1, source_target_pairs={{0,2},{2,0},{4,6},{6,4},{8,10},{10,8},{12,14},{14,12},{1,3},{3,1},... | collective-permute-start | bytes 595976 | tf_op jit(solution)/shard_map/ppermute | solution.py:179
  18.6 0.3 %collective-permute-done.3.refs_2_ = bf16[97,8,128]{2,1,0:T(8,128)(2,1)S(1)} collective-permute-done((bf16[97,8,128]{2,1,0:T(8,128)(2,1)S(1)}, bf16[97,8,128]{2,1,0:T(8,128)(2,1)S(1)}, u32[]{:S(2)}, u32[]{:S(2)}) %collective-permute-start.3) | collective-permute-done | bytes 198688 | tf_op jit(solution)/shard_map/ppermute | solution.py:190
  18.9 2.5 %collective-permute-start.7 = (bf16[97,8,128]{2,1,0:T(8,128)(2,1)S(1)}, bf16[97,8,128]{2,1,0:T(8,128)(2,1)S(1)}, u32[]{:S(2)}, u32[]{:S(2)}) collective-permute-start(bf16[97,8,128]{2,1,0:T(8,128)(2,1)S(1)} %collective-permute-done.3.refs_2_), channel_id=1, source_target_pairs={{0,8},{1,3},{2,10},{3,1},{8,12},{9,11},{10,14},{11,9},{12,4},{13,1... | collective-permute-start | bytes 595976 | tf_op jit(solution)/shard_map/ppermute | solution.py:190
  21.3 1.2 %first_scores.1 = (bf16[256,768]{1,0:T(8,128)(2,1)S(1)}, f32[256,128]{1,0:T(8,128)S(1)}, f32[256,128]{1,0:T(8,128)S(1)}, f32[256,768]{1,0:T(8,128)S(1)}) custom-call(bf16[97,8,128]{2,1,0:T(8,128)(2,1)S(1)} %pack.1.own_ref, bf16[97,8,128]{2,1,0:T(8,128)(2,1)S(1)} %collective-permute-done.2.other_ref, bf16[97,8,128]{2,1,0:T(8,128)(2,1)S(1)} %collective-permute-done.1.refs_0_, ...), custom_call_target="tpu_custom_call" | custom-call | flops 40265318400 | bytes 2359296 | tf_op jit(solution)/shard_map/first_scores/pallas_call | solution.py:196
  22.5 0.0 collective-permute-done.5.refs_1_
  22.6 1.8 %collective-permute-done.6.refs_2_ = bf16[97,8,128]{2,1,0:T(8,128)(2,1)S(1)} collective-permute-done((bf16[97,8,128]{2,1,0:T(8,128)(2,1)S(1)}, bf16[97,8,128]{2,1,0:T(8,128)(2,1)S(1)}, u32[]{:S(2)}, u32[]{:S(2)}) %collective-permute-start.6) | collective-permute-done | bytes 198688 | tf_op jit(solution)/shard_map/ppermute | solution.py:179
  24.3 1.1 %more_scores.1 = (f32[256,128]{1,0:T(8,128)S(1)}, f32[256,768]{1,0:T(8,128)S(1)}) custom-call(bf16[256,768]{1,0:T(8,128)(2,1)S(1)} %get-tuple-element.18.unit_ref, f32[256,128]{1,0:T(8,128)S(1)} %get-tuple-element.19.side_ref, f32[256,128]{1,0:T(8,128)S(1)} %get-tuple-element.20.old_sums_ref, ...), custom_call_target="tpu_custom_call", output_to_operand_aliasing={{0}: (2, {}), {1}: (3, {})} | custom-call | flops 30198988800 | bytes 2162688 | tf_op jit(solution)/shard_map/more_scores/pallas_call | solution.py:210
  25.4 0.0 collective-permute-done.7.refs_0_
  25.4 0.5 %send_scores.1 = bf16[136,768]{1,0:T(8,128)(2,1)S(1)} custom-call(bf16[256,768]{1,0:T(8,128)(2,1)S(1)} %get-tuple-element.18.unit_ref, f32[256,128]{1,0:T(8,128)S(1)} %get-tuple-element.19.side_ref, f32[256,128]{1,0:T(8,128)S(1)} %get-tuple-element.22.old_sums_ref, f32[256,768]{1,0:T(8,128)S(1)} %get-tuple-element.23.old_mixed_ref, ...), custom_call_target="tpu_custom_call" | custom-call | flops 5033164800 | bytes 983040 | tf_op jit(solution)/shard_map/send_scores/pallas_call | solution.py:220
  25.9 0.3 collective-permute-start.8
  26.2 0.5 %keep_scores.1 = (f32[128,128]{1,0:T(8,128)S(1)}, f32[128,768]{1,0:T(8,128)S(1)}) custom-call(bf16[256,768]{1,0:T(8,128)(2,1)S(1)} %get-tuple-element.18.unit_ref, f32[256,128]{1,0:T(8,128)S(1)} %get-tuple-element.19.side_ref, f32[256,128]{1,0:T(8,128)S(1)} %get-tuple-element.22.old_sums_ref, f32[256,768]{1,0:T(8,128)S(1)} %get-tuple-element.23.old_mixed_ref, ...), custom_call_target="tpu_custom_call" | custom-call | flops 5033164800 | bytes 983040 | tf_op jit(solution)/shard_map/keep_scores/pallas_call | solution.py:227
  26.7 0.7 %collective-permute-done.8.got_ref = bf16[136,768]{1,0:T(8,128)(2,1)S(1)} collective-permute-done((bf16[136,768]{1,0:T(8,128)(2,1)S(1)}, bf16[136,768]{1,0:T(8,128)(2,1)S(1)}, u32[]{:S(2)}, u32[]{:S(2)}) %collective-permute-start.8) | collective-permute-done | bytes 208928 | tf_op jit(solution)/shard_map/ppermute | solution.py:193
  27.5 1.0 %combine.1 = (f32[1,128]{1,0:T(1,128)}, f32[128,768]{1,0:T(8,128)}) custom-call(f32[128,128]{1,0:T(8,128)S(1)} %get-tuple-element.24.sums_ref, f32[128,768]{1,0:T(8,128)S(1)} %get-tuple-element.25.mixed_ref, bf16[136,768]{1,0:T(8,128)(2,1)S(1)} %collective-permute-done.8.got_ref), custom_call_target="tpu_custom_call" | custom-call | tf_op jit(solution)/shard_map/combine/pallas_call | solution.py:273
  (2 shorter events, 0.0 us)
Async XLA Ops:
  0.6 0.9 %copy-start = (bf16[128,768]{1,0:T(8,128)(2,1)S(1)}, bf16[128,768]{1,0:T(8,128)(2,1)}, u32[]{:S(2)}) copy-start(bf16[128,768]{1,0:T(8,128)(2,1)} %param.3) | copy-start | bytes 589828
  0.6 0.9 %copy-start.1 = (s32[128,1]{0,1:T(1,128)S(1)}, s32[128,1]{0,1:T(1,128)}, u32[]{:S(2)}) copy-start(s32[128,1]{0,1:T(1,128)} %param.4) | copy-start | bytes 1540
  0.7 0.9 %copy-start.2 = (s32[128]{0:T(128)S(1)}, s32[128]{0:T(128)}, u32[]{:S(2)}) copy-start(s32[128]{0:T(128)} %param.5) | copy-start | bytes 1540
  1.6 9.4 %collective-permute-start = (bf16[97,8,128]{2,1,0:T(8,128)(2,1)S(1)}, bf16[97,8,128]{2,1,0:T(8,128)(2,1)S(1)}, u32[]{:S(2)}, u32[]{:S(2)}) collective-permute-start(bf16[97,8,128]{2,1,0:T(8,128)(2,1)S(1)} %pack.1.own_ref), channel_id=1, source_target_pairs={{0,8},{2,10},{8,12},{10,14},{12,4},{14,6},{4,0},{6,2},{1,9},{3,11}... | collective-permute-start | bytes 595976 | tf_op jit(solution)/shard_map/ppermute | solution.py:176
  5.7 6.4 %collective-permute-start.1 = (bf16[97,8,128]{2,1,0:T(8,128)(2,1)S(1)}, bf16[97,8,128]{2,1,0:T(8,128)(2,1)S(1)}, u32[]{:S(2)}, u32[]{:S(2)}) collective-permute-start(bf16[97,8,128]{2,1,0:T(8,128)(2,1)S(1)} %pack.1.own_ref), channel_id=1, source_target_pairs={{0,2},{2,0},{4,6},{6,4},{8,10},{10,8},{12,14},{14,12},{1,3},{3,1},... | collective-permute-start | bytes 595976 | tf_op jit(solution)/shard_map/ppermute | solution.py:179
  7.2 4.9 %collective-permute-start.2 = (bf16[97,8,128]{2,1,0:T(8,128)(2,1)S(1)}, bf16[97,8,128]{2,1,0:T(8,128)(2,1)S(1)}, u32[]{:S(2)}, u32[]{:S(2)}) collective-permute-start(bf16[97,8,128]{2,1,0:T(8,128)(2,1)S(1)} %pack.1.own_ref), channel_id=1, source_target_pairs={{0,1},{1,0},{2,3},{3,2},{4,5},{5,4},{6,7},{7,6},{8,9},{9,8},{10,11... | collective-permute-start | bytes 595976 | tf_op jit(solution)/shard_map/ppermute | solution.py:193
  7.2 9.2 %collective-permute-start.4 = (bf16[97,8,128]{2,1,0:T(8,128)(2,1)S(1)}, bf16[97,8,128]{2,1,0:T(8,128)(2,1)S(1)}, u32[]{:S(2)}, u32[]{:S(2)}) collective-permute-start(bf16[97,8,128]{2,1,0:T(8,128)(2,1)S(1)} %pack.1.own_ref), channel_id=1, source_target_pairs={{0,4},{2,6},{8,0},{10,2},{12,8},{14,10},{4,12},{6,14},{1,5},{3,7},... | collective-permute-start | bytes 595976 | tf_op jit(solution)/shard_map/ppermute | solution.py:176
  12.1 6.8 %collective-permute-start.3 = (bf16[97,8,128]{2,1,0:T(8,128)(2,1)S(1)}, bf16[97,8,128]{2,1,0:T(8,128)(2,1)S(1)}, u32[]{:S(2)}, u32[]{:S(2)}) collective-permute-start(bf16[97,8,128]{2,1,0:T(8,128)(2,1)S(1)} %collective-permute-done.refs_1_), channel_id=1, source_target_pairs={{0,2},{1,9},{2,0},{3,11},{8,10},{9,13},{10,8},{11,15},{12,14},{13,... | collective-permute-start | bytes 595976 | tf_op jit(solution)/shard_map/ppermute | solution.py:190
  13.6 9.0 %collective-permute-start.5 = (bf16[97,8,128]{2,1,0:T(8,128)(2,1)S(1)}, bf16[97,8,128]{2,1,0:T(8,128)(2,1)S(1)}, u32[]{:S(2)}, u32[]{:S(2)}) collective-permute-start(bf16[97,8,128]{2,1,0:T(8,128)(2,1)S(1)} %collective-permute-done.refs_1_), channel_id=1, source_target_pairs={{0,8},{1,3},{2,10},{3,1},{8,12},{9,11},{10,14},{11,9},{12,4},{13,1... | collective-permute-start | bytes 595976 | tf_op jit(solution)/shard_map/ppermute | solution.py:190
  16.3 8.0 %collective-permute-start.6 = (bf16[97,8,128]{2,1,0:T(8,128)(2,1)S(1)}, bf16[97,8,128]{2,1,0:T(8,128)(2,1)S(1)}, u32[]{:S(2)}, u32[]{:S(2)}) collective-permute-start(bf16[97,8,128]{2,1,0:T(8,128)(2,1)S(1)} %collective-permute-done.4.refs_0_), channel_id=1, source_target_pairs={{0,2},{2,0},{4,6},{6,4},{8,10},{10,8},{12,14},{14,12},{1,3},{3,1},... | collective-permute-start | bytes 595976 | tf_op jit(solution)/shard_map/ppermute | solution.py:179
  18.9 6.5 %collective-permute-start.7 = (bf16[97,8,128]{2,1,0:T(8,128)(2,1)S(1)}, bf16[97,8,128]{2,1,0:T(8,128)(2,1)S(1)}, u32[]{:S(2)}, u32[]{:S(2)}) collective-permute-start(bf16[97,8,128]{2,1,0:T(8,128)(2,1)S(1)} %collective-permute-done.3.refs_2_), channel_id=1, source_target_pairs={{0,8},{1,3},{2,10},{3,1},{8,12},{9,11},{10,14},{11,9},{12,4},{13,1... | collective-permute-start | bytes 595976 | tf_op jit(solution)/shard_map/ppermute | solution.py:190
  25.9 1.5 %collective-permute-start.8 = (bf16[136,768]{1,0:T(8,128)(2,1)S(1)}, bf16[136,768]{1,0:T(8,128)(2,1)S(1)}, u32[]{:S(2)}, u32[]{:S(2)}) collective-permute-start(bf16[136,768]{1,0:T(8,128)(2,1)S(1)} %send_scores.1), channel_id=1, source_target_pairs={{0,1},{1,0},{2,3},{3,2},{4,5},{5,4},{6,7},{7,6},{8,9},{9,8},{10,11... | collective-permute-start | bytes 626696 | tf_op jit(solution)/shard_map/ppermute | solution.py:193

commit v25 on v24

--- a/solution.py
+++ b/solution.py
@@ -255,9 +255,9 @@
         moved, beside, other = lax.optimization_barrier((moved, beside, other))
         sooner, later = two_ways(moved, 1), two_ways(moved, 0)
         ahead_beside = across(ahead)
-        last = [two_ways(sooner, 0)]
+        last = [two_ways(sooner, 0), ahead_beside]
         unit, side, sums, mixed = first(own, other, beside, moved, sooner)
-        sums, mixed = more(unit, side, sums, mixed, ahead, later, ahead_beside)
+        sums, mixed = more(unit, side, sums, mixed, ahead, later)
     else:
         unit, side, sums, mixed = first(own, other, beside)
 

time: 28.6 us -> 28.5 us (level)
  waiting for transfers between devices: 8.14 us -> 7.24 us
  starting transfers between devices: 14.4 us -> 15.2 us
    ppermute x2, waiting for transfers between devices: 2.83 us -> 1.96 us  [across(): return lax.ppermute(array, 'shard', [(at, at ^ 1) for at in range(shards)])]
    ppermute x2, starting transfers between devices: 0.27 us -> 1.11 us  [swap(): lax.ppermute(array, 'owner', [(at, lanes - 1 - at) for at in range(lanes)])]
  transfers between devices with their start and end apart: 9 -> 9, of which waited for: 6 -> 7; matrix products, arithmetic and copies ran while one was open for 0% -> 0% of each run, Pallas kernels for 10% -> 9%
where the time goes in v25:
time: 28.5 us; the launch traced here: 28.3 us
  starting transfers between devices  15.2 us (53%)
  waiting for transfers between devices  7.24 us (25%)
  Pallas kernels  4.26 us (15%)
  local copies, waits for them, and re-layouts  0.9 us (3%)
  between operations  0.71 us (2%)
    ppermute x3, starting transfers between devices, two_ways(): return lax.ppermute(array, ('shard', 'owner'), pairs)  6.29 us
    ppermute x2, waiting for transfers between devices, along(): return lax.ppermute(array, 'shard', pairs)  4.27 us
    ppermute x2, starting transfers between devices, along(): return lax.ppermute(array, 'shard', pairs)  4.09 us
    ppermute x2, starting transfers between devices, across(): return lax.ppermute(array, 'shard', [(at, at ^ 1) for at in range(shards)])  3.74 us
    ppermute x2, waiting for transfers between devices, across(): return lax.ppermute(array, 'shard', [(at, at ^ 1) for at in range(shards)])  1.96 us
    pallas_call x1, Pallas kernels, first(): pl.pallas_call(first_kernel, out_shape=[shape(queries, width, dtype=bf16)...  1.18 us
    ppermute x2, starting transfers between devices, swap(): lax.ppermute(array, 'owner', [(at, lanes - 1 - at) for at in range(lanes)])  1.11 us
    pallas_call x1, Pallas kernels, local(): pl.pallas_call(combine_kernel, out_shape=[shape(1, count), shape(count, w...  0.95 us
  transfers between devices with their start and end apart: 9, of which 7 were waited for; matrix products, arithmetic and copies ran while one was open for 0% of the time, Pallas kernels for 9%

profile of v25, /device:TPU:0, one launch (start us, length us, event | category | flops | bytes accessed | tf_op | source)
XLA Modules:
  0.0 28.3 jit_solution(17015572078335421524)
XLA Ops:
  0.6 0.0 copy-start
  0.6 0.0 copy-start.1
  0.7 0.0 copy-start.2
  0.7 0.9 %copy-done = bf16[128,768]{1,0:T(8,128)(2,1)S(1)} copy-done((bf16[128,768]{1,0:T(8,128)(2,1)S(1)}, bf16[128,768]{1,0:T(8,128)(2,1)}, u32[]{:S(2)}) %copy-start) | copy-done | bytes 196632
  1.6 0.0 copy-done.1
  1.6 0.0 copy-done.2
  1.6 4.1 %collective-permute-start = (bf16[97,8,128]{2,1,0:T(8,128)(2,1)S(1)}, bf16[97,8,128]{2,1,0:T(8,128)(2,1)S(1)}, u32[]{:S(2)}, u32[]{:S(2)}) collective-permute-start(bf16[97,8,128]{2,1,0:T(8,128)(2,1)S(1)} %pack.1.own_ref), channel_id=1, source_target_pairs={{0,8},{2,10},{8,12},{10,14},{12,4},{14,6},{4,0},{6,2},{1,9},{3,11}... | collective-permute-start | bytes 595976 | tf_op jit(solution)/shard_map/ppermute | solution.py:176
  5.7 1.5 %collective-permute-start.1 = (bf16[97,8,128]{2,1,0:T(8,128)(2,1)S(1)}, bf16[97,8,128]{2,1,0:T(8,128)(2,1)S(1)}, u32[]{:S(2)}, u32[]{:S(2)}) collective-permute-start(bf16[97,8,128]{2,1,0:T(8,128)(2,1)S(1)} %pack.1.own_ref), channel_id=1, source_target_pairs={{0,2},{2,0},{4,6},{6,4},{8,10},{10,8},{12,14},{14,12},{1,3},{3,1},... | collective-permute-start | bytes 595976 | tf_op jit(solution)/shard_map/ppermute | solution.py:179
  7.2 0.0 collective-permute-start.2
  7.2 0.0 collective-permute-start.4
  7.2 3.9 %collective-permute-done.refs_1_ = bf16[97,8,128]{2,1,0:T(8,128)(2,1)S(1)} collective-permute-done((bf16[97,8,128]{2,1,0:T(8,128)(2,1)S(1)}, bf16[97,8,128]{2,1,0:T(8,128)(2,1)S(1)}, u32[]{:S(2)}, u32[]{:S(2)}) %collective-permute-start) | collective-permute-done | bytes 198688 | tf_op jit(solution)/shard_map/ppermute | solution.py:176
  11.0 1.1 %collective-permute-done.1.refs_0_ = bf16[97,8,128]{2,1,0:T(8,128)(2,1)S(1)} collective-permute-done((bf16[97,8,128]{2,1,0:T(8,128)(2,1)S(1)}, bf16[97,8,128]{2,1,0:T(8,128)(2,1)S(1)}, u32[]{:S(2)}, u32[]{:S(2)}) %collective-permute-start.1) | collective-permute-done | bytes 198688 | tf_op jit(solution)/shard_map/ppermute | solution.py:179
  12.1 0.0 collective-permute-done.2.other_ref
  12.1 1.5 %collective-permute-start.3 = (bf16[97,8,128]{2,1,0:T(8,128)(2,1)S(1)}, bf16[97,8,128]{2,1,0:T(8,128)(2,1)S(1)}, u32[]{:S(2)}, u32[]{:S(2)}) collective-permute-start(bf16[97,8,128]{2,1,0:T(8,128)(2,1)S(1)} %collective-permute-done.refs_1_), channel_id=1, source_target_pairs={{0,2},{1,9},{2,0},{3,11},{8,10},{9,13},{10,8},{11,15},{12,14},{13,... | collective-permute-start | bytes 595976 | tf_op jit(solution)/shard_map/ppermute | solution.py:190
  13.6 2.3 %collective-permute-start.5 = (bf16[97,8,128]{2,1,0:T(8,128)(2,1)S(1)}, bf16[97,8,128]{2,1,0:T(8,128)(2,1)S(1)}, u32[]{:S(2)}, u32[]{:S(2)}) collective-permute-start(bf16[97,8,128]{2,1,0:T(8,128)(2,1)S(1)} %collective-permute-done.refs_1_), channel_id=1, source_target_pairs={{0,8},{1,3},{2,10},{3,1},{8,12},{9,11},{10,14},{11,9},{12,4},{13,1... | collective-permute-start | bytes 595976 | tf_op jit(solution)/shard_map/ppermute | solution.py:190
  15.9 0.4 %collective-permute-done.4.refs_0_ = bf16[97,8,128]{2,1,0:T(8,128)(2,1)S(1)} collective-permute-done((bf16[97,8,128]{2,1,0:T(8,128)(2,1)S(1)}, bf16[97,8,128]{2,1,0:T(8,128)(2,1)S(1)}, u32[]{:S(2)}, u32[]{:S(2)}) %collective-permute-start.4) | collective-permute-done | bytes 198688 | tf_op jit(solution)/shard_map/ppermute | solution.py:176
  16.3 2.3 %collective-permute-start.7 = (bf16[97,8,128]{2,1,0:T(8,128)(2,1)S(1)}, bf16[97,8,128]{2,1,0:T(8,128)(2,1)S(1)}, u32[]{:S(2)}, u32[]{:S(2)}) collective-permute-start(bf16[97,8,128]{2,1,0:T(8,128)(2,1)S(1)} %collective-permute-done.4.refs_0_), channel_id=1, source_target_pairs={{0,2},{2,0},{4,6},{6,4},{8,10},{10,8},{12,14},{14,12},{1,3},{3,1},... | collective-permute-start | bytes 595976 | tf_op jit(solution)/shard_map/ppermute | solution.py:179
  18.6 0.3 %collective-permute-done.3.refs_2_ = bf16[97,8,128]{2,1,0:T(8,128)(2,1)S(1)} collective-permute-done((bf16[97,8,128]{2,1,0:T(8,128)(2,1)S(1)}, bf16[97,8,128]{2,1,0:T(8,128)(2,1)S(1)}, u32[]{:S(2)}, u32[]{:S(2)}) %collective-permute-start.3) | collective-permute-done | bytes 198688 | tf_op jit(solution)/shard_map/ppermute | solution.py:190
  18.9 2.5 %collective-permute-start.6 = (bf16[97,8,128]{2,1,0:T(8,128)(2,1)S(1)}, bf16[97,8,128]{2,1,0:T(8,128)(2,1)S(1)}, u32[]{:S(2)}, u32[]{:S(2)}) collective-permute-start(bf16[97,8,128]{2,1,0:T(8,128)(2,1)S(1)} %collective-permute-done.3.refs_2_), channel_id=1, source_target_pairs={{0,8},{1,3},{2,10},{3,1},{8,12},{9,11},{10,14},{11,9},{12,4},{13,1... | collective-permute-start | bytes 595976 | tf_op jit(solution)/shard_map/ppermute | solution.py:190
  21.3 1.2 %first_scores.1 = (bf16[256,768]{1,0:T(8,128)(2,1)S(1)}, f32[256,128]{1,0:T(8,128)S(1)}, f32[256,128]{1,0:T(8,128)S(1)}, f32[256,768]{1,0:T(8,128)S(1)}) custom-call(bf16[97,8,128]{2,1,0:T(8,128)(2,1)S(1)} %pack.1.own_ref, bf16[97,8,128]{2,1,0:T(8,128)(2,1)S(1)} %collective-permute-done.2.other_ref, bf16[97,8,128]{2,1,0:T(8,128)(2,1)S(1)} %collective-permute-done.1.refs_0_, ...), custom_call_target="tpu_custom_call" | custom-call | flops 40265318400 | bytes 2359296 | tf_op jit(solution)/shard_map/first_scores/pallas_call | solution.py:196
  22.5 0.0 collective-permute-done.5.refs_1_
  22.5 0.9 %more_scores.1 = (f32[256,128]{1,0:T(8,128)S(1)}, f32[256,768]{1,0:T(8,128)S(1)}) custom-call(bf16[256,768]{1,0:T(8,128)(2,1)S(1)} %get-tuple-element.18.unit_ref, f32[256,128]{1,0:T(8,128)S(1)} %get-tuple-element.19.side_ref, f32[256,128]{1,0:T(8,128)S(1)} %get-tuple-element.20.old_sums_ref, ...), custom_call_target="tpu_custom_call", output_to_operand_aliasing={{0}: (2, {}), {1}: (3, {})} | custom-call | flops 20132659200 | bytes 1966080 | tf_op jit(solution)/shard_map/more_scores/pallas_call | solution.py:210
  23.4 0.9 %collective-permute-done.7.refs_1_ = bf16[97,8,128]{2,1,0:T(8,128)(2,1)S(1)} collective-permute-done((bf16[97,8,128]{2,1,0:T(8,128)(2,1)S(1)}, bf16[97,8,128]{2,1,0:T(8,128)(2,1)S(1)}, u32[]{:S(2)}, u32[]{:S(2)}) %collective-permute-start.7) | collective-permute-done | bytes 198688 | tf_op jit(solution)/shard_map/ppermute | solution.py:179
  24.3 0.2 collective-permute-done.6.refs_0_
  24.6 0.6 %send_scores.1 = bf16[136,768]{1,0:T(8,128)(2,1)S(1)} custom-call(bf16[256,768]{1,0:T(8,128)(2,1)S(1)} %get-tuple-element.18.unit_ref, f32[256,128]{1,0:T(8,128)S(1)} %get-tuple-element.19.side_ref, f32[256,128]{1,0:T(8,128)S(1)} %get-tuple-element.22.old_sums_ref, f32[256,768]{1,0:T(8,128)S(1)} %get-tuple-element.23.old_mixed_ref, ...), custom_call_target="tpu_custom_call" | custom-call | flops 10066329600 | bytes 1179648 | tf_op jit(solution)/shard_map/send_scores/pallas_call | solution.py:220
  25.2 1.1 %collective-permute-start.8 = (bf16[136,768]{1,0:T(8,128)(2,1)S(1)}, bf16[136,768]{1,0:T(8,128)(2,1)S(1)}, u32[]{:S(2)}, u32[]{:S(2)}) collective-permute-start(bf16[136,768]{1,0:T(8,128)(2,1)S(1)} %send_scores.1), channel_id=1, source_target_pairs={{0,1},{1,0},{2,3},{3,2},{4,5},{5,4},{6,7},{7,6},{8,9},{9,8},{10,11... | collective-permute-start | bytes 626696 | tf_op jit(solution)/shard_map/ppermute | solution.py:193
  26.3 0.6 %keep_scores.1 = (f32[128,128]{1,0:T(8,128)S(1)}, f32[128,768]{1,0:T(8,128)S(1)}) custom-call(bf16[256,768]{1,0:T(8,128)(2,1)S(1)} %get-tuple-element.18.unit_ref, f32[256,128]{1,0:T(8,128)S(1)} %get-tuple-element.19.side_ref, f32[256,128]{1,0:T(8,128)S(1)} %get-tuple-element.22.old_sums_ref, f32[256,768]{1,0:T(8,128)S(1)} %get-tuple-element.23.old_mixed_ref, ...), custom_call_target="tpu_custom_call" | custom-call | flops 10066329600 | bytes 1179648 | tf_op jit(solution)/shard_map/keep_scores/pallas_call | solution.py:227
  26.9 0.5 %collective-permute-done.8.got_ref = bf16[136,768]{1,0:T(8,128)(2,1)S(1)} collective-permute-done((bf16[136,768]{1,0:T(8,128)(2,1)S(1)}, bf16[136,768]{1,0:T(8,128)(2,1)S(1)}, u32[]{:S(2)}, u32[]{:S(2)}) %collective-permute-start.8) | collective-permute-done | bytes 208928 | tf_op jit(solution)/shard_map/ppermute | solution.py:193
  27.4 1.0 %combine.1 = (f32[1,128]{1,0:T(1,128)}, f32[128,768]{1,0:T(8,128)}) custom-call(f32[128,128]{1,0:T(8,128)S(1)} %get-tuple-element.24.sums_ref, f32[128,768]{1,0:T(8,128)S(1)} %get-tuple-element.25.mixed_ref, bf16[136,768]{1,0:T(8,128)(2,1)S(1)} %collective-permute-done.8.got_ref), custom_call_target="tpu_custom_call" | custom-call | tf_op jit(solution)/shard_map/combine/pallas_call | solution.py:273
  (2 shorter events, 0.0 us)
Async XLA Ops:
  0.6 0.9 %copy-start = (bf16[128,768]{1,0:T(8,128)(2,1)S(1)}, bf16[128,768]{1,0:T(8,128)(2,1)}, u32[]{:S(2)}) copy-start(bf16[128,768]{1,0:T(8,128)(2,1)} %param.3) | copy-start | bytes 589828
  0.6 0.9 %copy-start.1 = (s32[128,1]{0,1:T(1,128)S(1)}, s32[128,1]{0,1:T(1,128)}, u32[]{:S(2)}) copy-start(s32[128,1]{0,1:T(1,128)} %param.4) | copy-start | bytes 1540
  0.7 0.9 %copy-start.2 = (s32[128]{0:T(128)S(1)}, s32[128]{0:T(128)}, u32[]{:S(2)}) copy-start(s32[128]{0:T(128)} %param.5) | copy-start | bytes 1540
  1.6 9.4 %collective-permute-start = (bf16[97,8,128]{2,1,0:T(8,128)(2,1)S(1)}, bf16[97,8,128]{2,1,0:T(8,128)(2,1)S(1)}, u32[]{:S(2)}, u32[]{:S(2)}) collective-permute-start(bf16[97,8,128]{2,1,0:T(8,128)(2,1)S(1)} %pack.1.own_ref), channel_id=1, source_target_pairs={{0,8},{2,10},{8,12},{10,14},{12,4},{14,6},{4,0},{6,2},{1,9},{3,11}... | collective-permute-start | bytes 595976 | tf_op jit(solution)/shard_map/ppermute | solution.py:176
  5.7 6.4 %collective-permute-start.1 = (bf16[97,8,128]{2,1,0:T(8,128)(2,1)S(1)}, bf16[97,8,128]{2,1,0:T(8,128)(2,1)S(1)}, u32[]{:S(2)}, u32[]{:S(2)}) collective-permute-start(bf16[97,8,128]{2,1,0:T(8,128)(2,1)S(1)} %pack.1.own_ref), channel_id=1, source_target_pairs={{0,2},{2,0},{4,6},{6,4},{8,10},{10,8},{12,14},{14,12},{1,3},{3,1},... | collective-permute-start | bytes 595976 | tf_op jit(solution)/shard_map/ppermute | solution.py:179
  7.2 4.9 %collective-permute-start.2 = (bf16[97,8,128]{2,1,0:T(8,128)(2,1)S(1)}, bf16[97,8,128]{2,1,0:T(8,128)(2,1)S(1)}, u32[]{:S(2)}, u32[]{:S(2)}) collective-permute-start(bf16[97,8,128]{2,1,0:T(8,128)(2,1)S(1)} %pack.1.own_ref), channel_id=1, source_target_pairs={{0,1},{1,0},{2,3},{3,2},{4,5},{5,4},{6,7},{7,6},{8,9},{9,8},{10,11... | collective-permute-start | bytes 595976 | tf_op jit(solution)/shard_map/ppermute | solution.py:193
  7.2 9.2 %collective-permute-start.4 = (bf16[97,8,128]{2,1,0:T(8,128)(2,1)S(1)}, bf16[97,8,128]{2,1,0:T(8,128)(2,1)S(1)}, u32[]{:S(2)}, u32[]{:S(2)}) collective-permute-start(bf16[97,8,128]{2,1,0:T(8,128)(2,1)S(1)} %pack.1.own_ref), channel_id=1, source_target_pairs={{0,4},{2,6},{8,0},{10,2},{12,8},{14,10},{4,12},{6,14},{1,5},{3,7},... | collective-permute-start | bytes 595976 | tf_op jit(solution)/shard_map/ppermute | solution.py:176
  12.1 6.8 %collective-permute-start.3 = (bf16[97,8,128]{2,1,0:T(8,128)(2,1)S(1)}, bf16[97,8,128]{2,1,0:T(8,128)(2,1)S(1)}, u32[]{:S(2)}, u32[]{:S(2)}) collective-permute-start(bf16[97,8,128]{2,1,0:T(8,128)(2,1)S(1)} %collective-permute-done.refs_1_), channel_id=1, source_target_pairs={{0,2},{1,9},{2,0},{3,11},{8,10},{9,13},{10,8},{11,15},{12,14},{13,... | collective-permute-start | bytes 595976 | tf_op jit(solution)/shard_map/ppermute | solution.py:190
  13.6 9.0 %collective-permute-start.5 = (bf16[97,8,128]{2,1,0:T(8,128)(2,1)S(1)}, bf16[97,8,128]{2,1,0:T(8,128)(2,1)S(1)}, u32[]{:S(2)}, u32[]{:S(2)}) collective-permute-start(bf16[97,8,128]{2,1,0:T(8,128)(2,1)S(1)} %collective-permute-done.refs_1_), channel_id=1, source_target_pairs={{0,8},{1,3},{2,10},{3,1},{8,12},{9,11},{10,14},{11,9},{12,4},{13,1... | collective-permute-start | bytes 595976 | tf_op jit(solution)/shard_map/ppermute | solution.py:190
  16.3 8.0 %collective-permute-start.7 = (bf16[97,8,128]{2,1,0:T(8,128)(2,1)S(1)}, bf16[97,8,128]{2,1,0:T(8,128)(2,1)S(1)}, u32[]{:S(2)}, u32[]{:S(2)}) collective-permute-start(bf16[97,8,128]{2,1,0:T(8,128)(2,1)S(1)} %collective-permute-done.4.refs_0_), channel_id=1, source_target_pairs={{0,2},{2,0},{4,6},{6,4},{8,10},{10,8},{12,14},{14,12},{1,3},{3,1},... | collective-permute-start | bytes 595976 | tf_op jit(solution)/shard_map/ppermute | solution.py:179
  18.9 5.7 %collective-permute-start.6 = (bf16[97,8,128]{2,1,0:T(8,128)(2,1)S(1)}, bf16[97,8,128]{2,1,0:T(8,128)(2,1)S(1)}, u32[]{:S(2)}, u32[]{:S(2)}) collective-permute-start(bf16[97,8,128]{2,1,0:T(8,128)(2,1)S(1)} %collective-permute-done.3.refs_2_), channel_id=1, source_target_pairs={{0,8},{1,3},{2,10},{3,1},{8,12},{9,11},{10,14},{11,9},{12,4},{13,1... | collective-permute-start | bytes 595976 | tf_op jit(solution)/shard_map/ppermute | solution.py:190
  25.2 2.2 %collective-permute-start.8 = (bf16[136,768]{1,0:T(8,128)(2,1)S(1)}, bf16[136,768]{1,0:T(8,128)(2,1)S(1)}, u32[]{:S(2)}, u32[]{:S(2)}) collective-permute-start(bf16[136,768]{1,0:T(8,128)(2,1)S(1)} %send_scores.1), channel_id=1, source_target_pairs={{0,1},{1,0},{2,3},{3,2},{4,5},{5,4},{6,7},{7,6},{8,9},{9,8},{10,11... | collective-permute-start | bytes 626696 | tf_op jit(solution)/shard_map/ppermute | solution.py:193

commit v26 on v21

--- a/solution.py
+++ b/solution.py
@@ -165,7 +165,7 @@
     def shape(*dims, dtype=f32):
         return jax.ShapeDtypeStruct(dims, dtype)
 
-    ring = list(range(0, rounds, 2)) + list(range(1, rounds, 2))[::-1]
+    ring = [0] + list(range(1, rounds, 2)) + list(range(2, rounds, 2))[::-1]
 
     def along(array, step):
         pairs = [

time: 28.3 us -> 29.9 us (1.057)
  starting transfers between devices: 14.6 us -> 18.4 us
  waiting for transfers between devices: 7.71 us -> 5.43 us
    ppermute x4, starting transfers between devices: 9.19 us -> 15.3 us  [along(): return lax.ppermute(array, 'shard', pairs)]
    ppermute x3, starting transfers between devices: 5.29 us -> 3.04 us  [across(): return lax.ppermute(array, 'shard', [(at, at ^ 1) for at in range(shards)])]
    ppermute x3, waiting for transfers between devices: 2.16 us -> 0.4 us  [across(): return lax.ppermute(array, 'shard', [(at, at ^ 1) for at in range(shards)])]
    ppermute x4, waiting for transfers between devices: 4.62 us -> 4.1 us  [along(): return lax.ppermute(array, 'shard', pairs)]
  transfers between devices with their start and end apart: 9 -> 9, of which waited for: 6 -> 4; matrix products, arithmetic and copies ran while one was open for 0% -> 0% of each run, Pallas kernels for 10% -> 9%
where the time goes in v26:
time: 29.9 us; the launch traced here: 29.7 us
  starting transfers between devices  18.4 us (62%)
  waiting for transfers between devices  5.43 us (18%)
  Pallas kernels  4.26 us (14%)
  local copies, waits for them, and re-layouts  0.9 us (3%)
  between operations  0.72 us (2%)
    ppermute x4, starting transfers between devices, along(): return lax.ppermute(array, 'shard', pairs)  15.3 us
    ppermute x4, waiting for transfers between devices, along(): return lax.ppermute(array, 'shard', pairs)  4.1 us
    ppermute x3, starting transfers between devices, across(): return lax.ppermute(array, 'shard', [(at, at ^ 1) for at in range(shards)])  3.04 us
    pallas_call x1, Pallas kernels, first(): pl.pallas_call(first_kernel, out_shape=[shape(queries, width, dtype=bf16)...  1.19 us
    pallas_call x1, Pallas kernels, more(): pl.pallas_call(more_kernel, out_shape=[shape(queries, 128), shape(queries...  1.06 us
    pallas_call x1, Pallas kernels, local(): pl.pallas_call(combine_kernel, out_shape=[shape(1, count), shape(count, w...  0.95 us
    ppermute x2, waiting for transfers between devices, swap(): lax.ppermute(array, 'owner', [(at, lanes - 1 - at) for at in range(lanes)])  0.93 us
    unnamed x6, local copies, waits for them, and re-layouts  0.9 us
  transfers between devices with their start and end apart: 9, of which 4 were waited for; matrix products, arithmetic and copies ran while one was open for 0% of the time, Pallas kernels for 9%

profile of v26, /device:TPU:0, one launch (start us, length us, event | category | flops | bytes accessed | tf_op | source)
XLA Modules:
  0.0 29.7 jit_solution(14264054315769689349)
XLA Ops:
  0.6 0.0 copy-start
  0.6 0.0 copy-start.1
  0.7 0.0 copy-start.2
  0.7 0.9 %copy-done = bf16[128,768]{1,0:T(8,128)(2,1)S(1)} copy-done((bf16[128,768]{1,0:T(8,128)(2,1)S(1)}, bf16[128,768]{1,0:T(8,128)(2,1)}, u32[]{:S(2)}) %copy-start) | copy-done | bytes 196632
  1.6 0.0 copy-done.1
  1.6 0.0 copy-done.2
  1.6 3.1 %collective-permute-start = (bf16[97,8,128]{2,1,0:T(8,128)(2,1)S(1)}, bf16[97,8,128]{2,1,0:T(8,128)(2,1)S(1)}, u32[]{:S(2)}, u32[]{:S(2)}) collective-permute-start(bf16[97,8,128]{2,1,0:T(8,128)(2,1)S(1)} %pack.1.own_ref), channel_id=1, source_target_pairs={{0,4},{2,6},{4,12},{6,14},{12,8},{14,10},{8,0},{10,2},{1,5},{3,7},... | collective-permute-start | bytes 595976 | tf_op jit(solution)/shard_map/ppermute | solution.py:176
  4.7 1.5 %collective-permute-start.1 = (bf16[97,8,128]{2,1,0:T(8,128)(2,1)S(1)}, bf16[97,8,128]{2,1,0:T(8,128)(2,1)S(1)}, u32[]{:S(2)}, u32[]{:S(2)}) collective-permute-start(bf16[97,8,128]{2,1,0:T(8,128)(2,1)S(1)} %pack.1.own_ref), channel_id=1, source_target_pairs={{0,2},{2,0},{4,6},{6,4},{8,10},{10,8},{12,14},{14,12},{1,3},{3,1},... | collective-permute-start | bytes 595976 | tf_op jit(solution)/shard_map/ppermute | solution.py:179
  6.2 0.0 collective-permute-start.2
  6.2 1.3 %collective-permute-start.4 = (bf16[97,8,128]{2,1,0:T(8,128)(2,1)S(1)}, bf16[97,8,128]{2,1,0:T(8,128)(2,1)S(1)}, u32[]{:S(2)}, u32[]{:S(2)}) collective-permute-start(bf16[97,8,128]{2,1,0:T(8,128)(2,1)S(1)} %pack.1.own_ref), channel_id=1, source_target_pairs={{0,8},{2,10},{4,0},{6,2},{12,4},{14,6},{8,12},{10,14},{1,9},{3,11}... | collective-permute-start | bytes 595976 | tf_op jit(solution)/shard_map/ppermute | solution.py:176
  7.5 3.2 %collective-permute-done.refs_1_ = bf16[97,8,128]{2,1,0:T(8,128)(2,1)S(1)} collective-permute-done((bf16[97,8,128]{2,1,0:T(8,128)(2,1)S(1)}, bf16[97,8,128]{2,1,0:T(8,128)(2,1)S(1)}, u32[]{:S(2)}, u32[]{:S(2)}) %collective-permute-start) | collective-permute-done | bytes 198688 | tf_op jit(solution)/shard_map/ppermute | solution.py:176
  10.7 0.4 %collective-permute-done.1.refs_0_ = bf16[97,8,128]{2,1,0:T(8,128)(2,1)S(1)} collective-permute-done((bf16[97,8,128]{2,1,0:T(8,128)(2,1)S(1)}, bf16[97,8,128]{2,1,0:T(8,128)(2,1)S(1)}, u32[]{:S(2)}, u32[]{:S(2)}) %collective-permute-start.1) | collective-permute-done | bytes 198688 | tf_op jit(solution)/shard_map/ppermute | solution.py:179
  11.1 0.0 collective-permute-done.2.other_ref
  11.1 1.5 %collective-permute-start.3 = (bf16[97,8,128]{2,1,0:T(8,128)(2,1)S(1)}, bf16[97,8,128]{2,1,0:T(8,128)(2,1)S(1)}, u32[]{:S(2)}, u32[]{:S(2)}) collective-permute-start(bf16[97,8,128]{2,1,0:T(8,128)(2,1)S(1)} %collective-permute-done.refs_1_), channel_id=1, source_target_pairs={{0,2},{2,0},{4,6},{6,4},{8,10},{10,8},{12,14},{14,12},{1,3},{3,1},... | collective-permute-start | bytes 595976 | tf_op jit(solution)/shard_map/ppermute | solution.py:179
  12.6 5.2 %collective-permute-start.5 = (bf16[97,8,128]{2,1,0:T(8,128)(2,1)S(1)}, bf16[97,8,128]{2,1,0:T(8,128)(2,1)S(1)}, u32[]{:S(2)}, u32[]{:S(2)}) collective-permute-start(bf16[97,8,128]{2,1,0:T(8,128)(2,1)S(1)} %collective-permute-done.refs_1_), channel_id=1, source_target_pairs={{0,4},{2,6},{4,12},{6,14},{12,8},{14,10},{8,0},{10,2},{1,5},{3,7},... | collective-permute-start | bytes 595976 | tf_op jit(solution)/shard_map/ppermute | solution.py:176
  17.8 0.0 collective-permute-done.4.refs_0_
  17.8 0.1 collective-permute-start.6
  17.8 0.0 collective-permute-done.3.refs_2_
  17.8 5.7 %collective-permute-start.7 = (bf16[97,8,128]{2,1,0:T(8,128)(2,1)S(1)}, bf16[97,8,128]{2,1,0:T(8,128)(2,1)S(1)}, u32[]{:S(2)}, u32[]{:S(2)}) collective-permute-start(bf16[97,8,128]{2,1,0:T(8,128)(2,1)S(1)} %collective-permute-done.3.refs_2_), channel_id=1, source_target_pairs={{0,4},{2,6},{4,12},{6,14},{12,8},{14,10},{8,0},{10,2},{1,5},{3,7},... | collective-permute-start | bytes 595976 | tf_op jit(solution)/shard_map/ppermute | solution.py:176
  23.5 1.2 %first_scores.1 = (bf16[256,768]{1,0:T(8,128)(2,1)S(1)}, f32[256,128]{1,0:T(8,128)S(1)}, f32[256,128]{1,0:T(8,128)S(1)}, f32[256,768]{1,0:T(8,128)S(1)}) custom-call(bf16[97,8,128]{2,1,0:T(8,128)(2,1)S(1)} %pack.1.own_ref, bf16[97,8,128]{2,1,0:T(8,128)(2,1)S(1)} %collective-permute-done.2.other_ref, bf16[97,8,128]{2,1,0:T(8,128)(2,1)S(1)} %collective-permute-done.1.refs_0_, ...), custom_call_target="tpu_custom_call" | custom-call | flops 40265318400 | bytes 2359296 | tf_op jit(solution)/shard_map/first_scores/pallas_call | solution.py:185
  24.7 0.0 collective-permute-done.5.refs_1_
  24.7 0.0 collective-permute-done.6.refs_2_
  24.7 1.1 %more_scores.1 = (f32[256,128]{1,0:T(8,128)S(1)}, f32[256,768]{1,0:T(8,128)S(1)}) custom-call(bf16[256,768]{1,0:T(8,128)(2,1)S(1)} %get-tuple-element.18.unit_ref, f32[256,128]{1,0:T(8,128)S(1)} %get-tuple-element.19.side_ref, f32[256,128]{1,0:T(8,128)S(1)} %get-tuple-element.20.old_sums_ref, ...), custom_call_target="tpu_custom_call", output_to_operand_aliasing={{0}: (2, {}), {1}: (3, {})} | custom-call | flops 30198988800 | bytes 2162688 | tf_op jit(solution)/shard_map/more_scores/pallas_call | solution.py:199
  25.8 0.9 %collective-permute-done.7.refs_0_ = bf16[97,8,128]{2,1,0:T(8,128)(2,1)S(1)} collective-permute-done((bf16[97,8,128]{2,1,0:T(8,128)(2,1)S(1)}, bf16[97,8,128]{2,1,0:T(8,128)(2,1)S(1)}, u32[]{:S(2)}, u32[]{:S(2)}) %collective-permute-start.7) | collective-permute-done | bytes 198688 | tf_op jit(solution)/shard_map/ppermute | solution.py:176
  26.7 0.5 %send_scores.1 = bf16[136,768]{1,0:T(8,128)(2,1)S(1)} custom-call(bf16[256,768]{1,0:T(8,128)(2,1)S(1)} %get-tuple-element.18.unit_ref, f32[256,128]{1,0:T(8,128)S(1)} %get-tuple-element.19.side_ref, f32[256,128]{1,0:T(8,128)S(1)} %get-tuple-element.22.old_sums_ref, f32[256,768]{1,0:T(8,128)S(1)} %get-tuple-element.23.old_mixed_ref, ...), custom_call_target="tpu_custom_call" | custom-call | flops 5033164800 | bytes 983040 | tf_op jit(solution)/shard_map/send_scores/pallas_call | solution.py:209
  27.2 0.1 collective-permute-start.8
  27.3 0.5 %keep_scores.1 = (f32[128,128]{1,0:T(8,128)S(1)}, f32[128,768]{1,0:T(8,128)S(1)}) custom-call(bf16[256,768]{1,0:T(8,128)(2,1)S(1)} %get-tuple-element.18.unit_ref, f32[256,128]{1,0:T(8,128)S(1)} %get-tuple-element.19.side_ref, f32[256,128]{1,0:T(8,128)S(1)} %get-tuple-element.22.old_sums_ref, f32[256,768]{1,0:T(8,128)S(1)} %get-tuple-element.23.old_mixed_ref, ...), custom_call_target="tpu_custom_call" | custom-call | flops 5033164800 | bytes 983040 | tf_op jit(solution)/shard_map/keep_scores/pallas_call | solution.py:216
  27.8 0.9 %collective-permute-done.8.got_ref = bf16[136,768]{1,0:T(8,128)(2,1)S(1)} collective-permute-done((bf16[136,768]{1,0:T(8,128)(2,1)S(1)}, bf16[136,768]{1,0:T(8,128)(2,1)S(1)}, u32[]{:S(2)}, u32[]{:S(2)}) %collective-permute-start.8) | collective-permute-done | bytes 208928 | tf_op jit(solution)/shard_map/ppermute | solution.py:182
  28.8 1.0 %combine.1 = (f32[1,128]{1,0:T(1,128)}, f32[128,768]{1,0:T(8,128)}) custom-call(f32[128,128]{1,0:T(8,128)S(1)} %get-tuple-element.24.sums_ref, f32[128,768]{1,0:T(8,128)S(1)} %get-tuple-element.25.mixed_ref, bf16[136,768]{1,0:T(8,128)(2,1)S(1)} %collective-permute-done.8.got_ref), custom_call_target="tpu_custom_call" | custom-call | tf_op jit(solution)/shard_map/combine/pallas_call | solution.py:263
  (2 shorter events, 0.0 us)
Async XLA Ops:
  0.6 0.9 %copy-start = (bf16[128,768]{1,0:T(8,128)(2,1)S(1)}, bf16[128,768]{1,0:T(8,128)(2,1)}, u32[]{:S(2)}) copy-start(bf16[128,768]{1,0:T(8,128)(2,1)} %param.3) | copy-start | bytes 589828
  0.6 0.9 %copy-start.1 = (s32[128,1]{0,1:T(1,128)S(1)}, s32[128,1]{0,1:T(1,128)}, u32[]{:S(2)}) copy-start(s32[128,1]{0,1:T(1,128)} %param.4) | copy-start | bytes 1540
  0.7 0.9 %copy-start.2 = (s32[128]{0:T(128)S(1)}, s32[128]{0:T(128)}, u32[]{:S(2)}) copy-start(s32[128]{0:T(128)} %param.5) | copy-start | bytes 1540
  1.6 9.1 %collective-permute-start = (bf16[97,8,128]{2,1,0:T(8,128)(2,1)S(1)}, bf16[97,8,128]{2,1,0:T(8,128)(2,1)S(1)}, u32[]{:S(2)}, u32[]{:S(2)}) collective-permute-start(bf16[97,8,128]{2,1,0:T(8,128)(2,1)S(1)} %pack.1.own_ref), channel_id=1, source_target_pairs={{0,4},{2,6},{4,12},{6,14},{12,8},{14,10},{8,0},{10,2},{1,5},{3,7},... | collective-permute-start | bytes 595976 | tf_op jit(solution)/shard_map/ppermute | solution.py:176
  4.7 6.4 %collective-permute-start.1 = (bf16[97,8,128]{2,1,0:T(8,128)(2,1)S(1)}, bf16[97,8,128]{2,1,0:T(8,128)(2,1)S(1)}, u32[]{:S(2)}, u32[]{:S(2)}) collective-permute-start(bf16[97,8,128]{2,1,0:T(8,128)(2,1)S(1)} %pack.1.own_ref), channel_id=1, source_target_pairs={{0,2},{2,0},{4,6},{6,4},{8,10},{10,8},{12,14},{14,12},{1,3},{3,1},... | collective-permute-start | bytes 595976 | tf_op jit(solution)/shard_map/ppermute | solution.py:179
  6.2 4.9 %collective-permute-start.2 = (bf16[97,8,128]{2,1,0:T(8,128)(2,1)S(1)}, bf16[97,8,128]{2,1,0:T(8,128)(2,1)S(1)}, u32[]{:S(2)}, u32[]{:S(2)}) collective-permute-start(bf16[97,8,128]{2,1,0:T(8,128)(2,1)S(1)} %pack.1.own_ref), channel_id=1, source_target_pairs={{0,1},{1,0},{2,3},{3,2},{4,5},{5,4},{6,7},{7,6},{8,9},{9,8},{10,11... | collective-permute-start | bytes 595976 | tf_op jit(solution)/shard_map/ppermute | solution.py:182
  6.2 11.6 %collective-permute-start.4 = (bf16[97,8,128]{2,1,0:T(8,128)(2,1)S(1)}, bf16[97,8,128]{2,1,0:T(8,128)(2,1)S(1)}, u32[]{:S(2)}, u32[]{:S(2)}) collective-permute-start(bf16[97,8,128]{2,1,0:T(8,128)(2,1)S(1)} %pack.1.own_ref), channel_id=1, source_target_pairs={{0,8},{2,10},{4,0},{6,2},{12,4},{14,6},{8,12},{10,14},{1,9},{3,11}... | collective-permute-start | bytes 595976 | tf_op jit(solution)/shard_map/ppermute | solution.py:176
  11.1 6.7 %collective-permute-start.3 = (bf16[97,8,128]{2,1,0:T(8,128)(2,1)S(1)}, bf16[97,8,128]{2,1,0:T(8,128)(2,1)S(1)}, u32[]{:S(2)}, u32[]{:S(2)}) collective-permute-start(bf16[97,8,128]{2,1,0:T(8,128)(2,1)S(1)} %collective-permute-done.refs_1_), channel_id=1, source_target_pairs={{0,2},{2,0},{4,6},{6,4},{8,10},{10,8},{12,14},{14,12},{1,3},{3,1},... | collective-permute-start | bytes 595976 | tf_op jit(solution)/shard_map/ppermute | solution.py:179
  12.6 12.1 %collective-permute-start.5 = (bf16[97,8,128]{2,1,0:T(8,128)(2,1)S(1)}, bf16[97,8,128]{2,1,0:T(8,128)(2,1)S(1)}, u32[]{:S(2)}, u32[]{:S(2)}) collective-permute-start(bf16[97,8,128]{2,1,0:T(8,128)(2,1)S(1)} %collective-permute-done.refs_1_), channel_id=1, source_target_pairs={{0,4},{2,6},{4,12},{6,14},{12,8},{14,10},{8,0},{10,2},{1,5},{3,7},... | collective-permute-start | bytes 595976 | tf_op jit(solution)/shard_map/ppermute | solution.py:176
  17.8 7.0 %collective-permute-start.6 = (bf16[97,8,128]{2,1,0:T(8,128)(2,1)S(1)}, bf16[97,8,128]{2,1,0:T(8,128)(2,1)S(1)}, u32[]{:S(2)}, u32[]{:S(2)}) collective-permute-start(bf16[97,8,128]{2,1,0:T(8,128)(2,1)S(1)} %collective-permute-done.4.refs_0_), channel_id=1, source_target_pairs={{0,2},{2,0},{4,6},{6,4},{8,10},{10,8},{12,14},{14,12},{1,3},{3,1},... | collective-permute-start | bytes 595976 | tf_op jit(solution)/shard_map/ppermute | solution.py:179
  17.8 8.9 %collective-permute-start.7 = (bf16[97,8,128]{2,1,0:T(8,128)(2,1)S(1)}, bf16[97,8,128]{2,1,0:T(8,128)(2,1)S(1)}, u32[]{:S(2)}, u32[]{:S(2)}) collective-permute-start(bf16[97,8,128]{2,1,0:T(8,128)(2,1)S(1)} %collective-permute-done.3.refs_2_), channel_id=1, source_target_pairs={{0,4},{2,6},{4,12},{6,14},{12,8},{14,10},{8,0},{10,2},{1,5},{3,7},... | collective-permute-start | bytes 595976 | tf_op jit(solution)/shard_map/ppermute | solution.py:176
  27.2 1.5 %collective-permute-start.8 = (bf16[136,768]{1,0:T(8,128)(2,1)S(1)}, bf16[136,768]{1,0:T(8,128)(2,1)S(1)}, u32[]{:S(2)}, u32[]{:S(2)}) collective-permute-start(bf16[136,768]{1,0:T(8,128)(2,1)S(1)} %send_scores.1), channel_id=1, source_target_pairs={{0,1},{1,0},{2,3},{3,2},{4,5},{5,4},{6,7},{7,6},{8,9},{9,8},{10,11... | collective-permute-start | bytes 626696 | tf_op jit(solution)/shard_map/ppermute | solution.py:182

commit v27 on v21

--- a/solution.py
+++ b/solution.py
@@ -111,17 +111,20 @@
 
 
 def send_kernel(unit_ref, side_ref, old_sums_ref, old_mixed_ref, *refs):
-    blocks, send_ref = refs[:-1], refs[-1]
-    count, width = send_ref.shape[0] - EXTRA, send_ref.shape[1]
+    blocks, (front_ref, rear_ref) = refs[:-2], refs[-2:]
+    half, width = front_ref.shape
+    count = 2 * half
     earlier, every, mixed = score(unit_ref[count:, :], side_ref[count:, :], blocks)
     earlier += old_sums_ref[count:, 0:1]
     every += old_sums_ref[count:, 1:2]
-    send_ref[:count, :] = (mixed + old_mixed_ref[count:, :]).astype(jnp.bfloat16)
+    mixed = (mixed + old_mixed_ref[count:, :]).astype(jnp.bfloat16)
+    front_ref[...] = mixed[:half]
+    rear_ref[:half, :] = mixed[half:]
     pieces = halves(as_row(earlier)) + halves(as_row(every))
     pieces = [piece.astype(jnp.float32) for piece in pieces]
     pieces.append(jnp.zeros((1, width - 4 * count), jnp.float32))
     line = jnp.concatenate(pieces, axis=1)
-    send_ref[count:, :] = jnp.broadcast_to(line, (EXTRA, width)).astype(jnp.bfloat16)
+    rear_ref[half:, :] = jnp.broadcast_to(line, (EXTRA, width)).astype(jnp.bfloat16)
 
 
 def keep_kernel(unit_ref, side_ref, old_sums_ref, old_mixed_ref, *refs):
@@ -134,14 +137,17 @@
     mixed_ref[...] = old_mixed_ref[:count, :] + mixed
 
 
-def combine_kernel(sums_ref, mixed_ref, got_ref, dup_ref, out_ref):
+def combine_kernel(sums_ref, mixed_ref, front_ref, rear_ref, dup_ref, out_ref):
     count = mixed_ref.shape[0]
-    line = got_ref[count:, :].astype(jnp.float32)[:1]
+    half = count // 2
+    line = rear_ref[half:, :].astype(jnp.float32)[:1]
     parts = [line[:, at * count : (at + 1) * count] for at in range(4)]
     every = sums_ref[:, 1:2] + as_column(parts[2] + parts[3])
     dup_ref[...] = jnp.log1p(as_row(sums_ref[:, 0:1]) + parts[0] + parts[1])
-    mixed = mixed_ref[...] + got_ref[:count, :].astype(jnp.float32)
-    out_ref[...] = mixed / jnp.sqrt(1.0 + every)
+    root = jnp.sqrt(1.0 + every)
+    out_ref[:half, :] = (mixed_ref[:half, :] + front_ref[...].astype(jnp.float32)) / root[:half]
+    rear = rear_ref[:half, :].astype(jnp.float32)
+    out_ref[half:, :] = (mixed_ref[half:, :] + rear) / root[half:]
 
 
 def cost(queries, keys, width):
@@ -208,7 +214,10 @@
     def final(unit, side, sums, mixed, *blocks):
         send = pl.pallas_call(
             send_kernel,
-            out_shape=shape(count + EXTRA, width, dtype=bf16),
+            out_shape=[
+                shape(count // 2, width, dtype=bf16),
+                shape(count // 2 + EXTRA, width, dtype=bf16),
+            ],
             cost_estimate=cost(count, len(blocks) * count, width),
             compiler_params=params,
             name="send_scores",
@@ -265,7 +274,7 @@
         out_shape=[shape(1, count), shape(count, width)],
         compiler_params=params,
         name="combine",
-    )(keep_sums, keep, swap(send))
+    )(keep_sums, keep, *[swap(piece) for piece in send])
     return dup[0], out
 
 

time: 28.3 us -> 28.3 us (level)
  waiting for transfers between devices: 7.71 us -> 7.22 us
  starting transfers between devices: 14.6 us -> 15 us
    ppermute x2 -> x3, starting transfers between devices: 0.07 us -> 0.57 us  [swap(): lax.ppermute(array, 'owner', [(at, lanes - 1 - at) for at in range(lanes)])]
    ppermute x2 -> x3, waiting for transfers between devices: 0.93 us -> 0.44 us  [swap(): lax.ppermute(array, 'owner', [(at, lanes - 1 - at) for at in range(lanes)])]
  transfers between devices with their start and end apart: 9 -> 10, of which waited for: 6 -> 6; matrix products, arithmetic and copies ran while one was open for 0% -> 0% of each run, Pallas kernels for 10% -> 10%
where the time goes in v27:
time: 28.3 us; the launch traced here: 28.1 us
  starting transfers between devices  15 us (53%)
  waiting for transfers between devices  7.22 us (26%)
  Pallas kernels  4.25 us (15%)
  local copies, waits for them, and re-layouts  0.9 us (3%)
  between operations  0.71 us (3%)
    ppermute x4, starting transfers between devices, along(): return lax.ppermute(array, 'shard', pairs)  9.19 us
    ppermute x3, starting transfers between devices, across(): return lax.ppermute(array, 'shard', [(at, at ^ 1) for at in range(shards)])  5.29 us
    ppermute x4, waiting for transfers between devices, along(): return lax.ppermute(array, 'shard', pairs)  4.62 us
    ppermute x3, waiting for transfers between devices, across(): return lax.ppermute(array, 'shard', [(at, at ^ 1) for at in range(shards)])  2.17 us
    pallas_call x1, Pallas kernels, first(): pl.pallas_call(first_kernel, out_shape=[shape(queries, width, dtype=bf16)...  1.18 us
    pallas_call x1, Pallas kernels, more(): pl.pallas_call(more_kernel, out_shape=[shape(queries, 128), shape(queries...  1.05 us
    pallas_call x1, Pallas kernels, local(): pl.pallas_call(combine_kernel, out_shape=[shape(1, count), shape(count, w...  0.95 us
    unnamed x6, local copies, waits for them, and re-layouts  0.9 us
  transfers between devices with their start and end apart: 10, of which 6 were waited for; matrix products, arithmetic and copies ran while one was open for 0% of the time, Pallas kernels for 10%

profile of v27, /device:TPU:0, one launch (start us, length us, event | category | flops | bytes accessed | tf_op | source)
XLA Modules:
  0.0 28.1 jit_solution(4275258852607193146)
XLA Ops:
  0.6 0.0 copy-start
  0.6 0.0 copy-start.1
  0.7 0.0 copy-start.2
  0.7 0.9 %copy-done = bf16[128,768]{1,0:T(8,128)(2,1)S(1)} copy-done((bf16[128,768]{1,0:T(8,128)(2,1)S(1)}, bf16[128,768]{1,0:T(8,128)(2,1)}, u32[]{:S(2)}) %copy-start) | copy-done | bytes 196632
  1.6 0.0 copy-done.1
  1.6 0.0 copy-done.2
  1.6 4.1 %collective-permute-start = (bf16[97,8,128]{2,1,0:T(8,128)(2,1)S(1)}, bf16[97,8,128]{2,1,0:T(8,128)(2,1)S(1)}, u32[]{:S(2)}, u32[]{:S(2)}) collective-permute-start(bf16[97,8,128]{2,1,0:T(8,128)(2,1)S(1)} %pack.1.own_ref), channel_id=1, source_target_pairs={{0,8},{2,10},{8,12},{10,14},{12,4},{14,6},{4,0},{6,2},{1,9},{3,11}... | collective-permute-start | bytes 595976 | tf_op jit(solution)/shard_map/ppermute | solution.py:182
  5.7 1.5 %collective-permute-start.1 = (bf16[97,8,128]{2,1,0:T(8,128)(2,1)S(1)}, bf16[97,8,128]{2,1,0:T(8,128)(2,1)S(1)}, u32[]{:S(2)}, u32[]{:S(2)}) collective-permute-start(bf16[97,8,128]{2,1,0:T(8,128)(2,1)S(1)} %pack.1.own_ref), channel_id=1, source_target_pairs={{0,2},{2,0},{4,6},{6,4},{8,10},{10,8},{12,14},{14,12},{1,3},{3,1},... | collective-permute-start | bytes 595976 | tf_op jit(solution)/shard_map/ppermute | solution.py:185
  7.2 0.0 collective-permute-start.2
  7.2 0.0 collective-permute-start.4
  7.2 3.9 %collective-permute-done.refs_1_ = bf16[97,8,128]{2,1,0:T(8,128)(2,1)S(1)} collective-permute-done((bf16[97,8,128]{2,1,0:T(8,128)(2,1)S(1)}, bf16[97,8,128]{2,1,0:T(8,128)(2,1)S(1)}, u32[]{:S(2)}, u32[]{:S(2)}) %collective-permute-start) | collective-permute-done | bytes 198688 | tf_op jit(solution)/shard_map/ppermute | solution.py:182
  11.0 1.1 %collective-permute-done.1.refs_0_ = bf16[97,8,128]{2,1,0:T(8,128)(2,1)S(1)} collective-permute-done((bf16[97,8,128]{2,1,0:T(8,128)(2,1)S(1)}, bf16[97,8,128]{2,1,0:T(8,128)(2,1)S(1)}, u32[]{:S(2)}, u32[]{:S(2)}) %collective-permute-start.1) | collective-permute-done | bytes 198688 | tf_op jit(solution)/shard_map/ppermute | solution.py:185
  12.1 0.0 collective-permute-done.2.other_ref
  12.1 1.5 %collective-permute-start.3 = (bf16[97,8,128]{2,1,0:T(8,128)(2,1)S(1)}, bf16[97,8,128]{2,1,0:T(8,128)(2,1)S(1)}, u32[]{:S(2)}, u32[]{:S(2)}) collective-permute-start(bf16[97,8,128]{2,1,0:T(8,128)(2,1)S(1)} %collective-permute-done.refs_1_), channel_id=1, source_target_pairs={{0,2},{2,0},{4,6},{6,4},{8,10},{10,8},{12,14},{14,12},{1,3},{3,1},... | collective-permute-start | bytes 595976 | tf_op jit(solution)/shard_map/ppermute | solution.py:185
  13.6 2.3 %collective-permute-start.5 = (bf16[97,8,128]{2,1,0:T(8,128)(2,1)S(1)}, bf16[97,8,128]{2,1,0:T(8,128)(2,1)S(1)}, u32[]{:S(2)}, u32[]{:S(2)}) collective-permute-start(bf16[97,8,128]{2,1,0:T(8,128)(2,1)S(1)} %collective-permute-done.refs_1_), channel_id=1, source_target_pairs={{0,8},{2,10},{8,12},{10,14},{12,4},{14,6},{4,0},{6,2},{1,9},{3,11}... | collective-permute-start | bytes 595976 | tf_op jit(solution)/shard_map/ppermute | solution.py:182
  15.9 0.4 %collective-permute-done.4.refs_0_ = bf16[97,8,128]{2,1,0:T(8,128)(2,1)S(1)} collective-permute-done((bf16[97,8,128]{2,1,0:T(8,128)(2,1)S(1)}, bf16[97,8,128]{2,1,0:T(8,128)(2,1)S(1)}, u32[]{:S(2)}, u32[]{:S(2)}) %collective-permute-start.4) | collective-permute-done | bytes 198688 | tf_op jit(solution)/shard_map/ppermute | solution.py:182
  16.3 2.3 %collective-permute-start.6 = (bf16[97,8,128]{2,1,0:T(8,128)(2,1)S(1)}, bf16[97,8,128]{2,1,0:T(8,128)(2,1)S(1)}, u32[]{:S(2)}, u32[]{:S(2)}) collective-permute-start(bf16[97,8,128]{2,1,0:T(8,128)(2,1)S(1)} %collective-permute-done.4.refs_0_), channel_id=1, source_target_pairs={{0,2},{2,0},{4,6},{6,4},{8,10},{10,8},{12,14},{14,12},{1,3},{3,1},... | collective-permute-start | bytes 595976 | tf_op jit(solution)/shard_map/ppermute | solution.py:185
  18.6 0.0 collective-permute-done.3.refs_2_
  18.6 2.8 %collective-permute-start.7 = (bf16[97,8,128]{2,1,0:T(8,128)(2,1)S(1)}, bf16[97,8,128]{2,1,0:T(8,128)(2,1)S(1)}, u32[]{:S(2)}, u32[]{:S(2)}) collective-permute-start(bf16[97,8,128]{2,1,0:T(8,128)(2,1)S(1)} %collective-permute-done.3.refs_2_), channel_id=1, source_target_pairs={{0,8},{2,10},{8,12},{10,14},{12,4},{14,6},{4,0},{6,2},{1,9},{3,11}... | collective-permute-start | bytes 595976 | tf_op jit(solution)/shard_map/ppermute | solution.py:182
  21.3 1.2 %first_scores.1 = (bf16[256,768]{1,0:T(8,128)(2,1)S(1)}, f32[256,128]{1,0:T(8,128)S(1)}, f32[256,128]{1,0:T(8,128)S(1)}, f32[256,768]{1,0:T(8,128)S(1)}) custom-call(bf16[97,8,128]{2,1,0:T(8,128)(2,1)S(1)} %pack.1.own_ref, bf16[97,8,128]{2,1,0:T(8,128)(2,1)S(1)} %collective-permute-done.2.other_ref, bf16[97,8,128]{2,1,0:T(8,128)(2,1)S(1)} %collective-permute-done.1.refs_0_, ...), custom_call_target="tpu_custom_call" | custom-call | flops 40265318400 | bytes 2359296 | tf_op jit(solution)/shard_map/first_scores/pallas_call | solution.py:191
  22.5 0.0 collective-permute-done.5.refs_1_
  22.5 1.1 %collective-permute-done.6.refs_2_ = bf16[97,8,128]{2,1,0:T(8,128)(2,1)S(1)} collective-permute-done((bf16[97,8,128]{2,1,0:T(8,128)(2,1)S(1)}, bf16[97,8,128]{2,1,0:T(8,128)(2,1)S(1)}, u32[]{:S(2)}, u32[]{:S(2)}) %collective-permute-start.6) | collective-permute-done | bytes 198688 | tf_op jit(solution)/shard_map/ppermute | solution.py:185
  23.7 1.1 %more_scores.1 = (f32[256,128]{1,0:T(8,128)S(1)}, f32[256,768]{1,0:T(8,128)S(1)}) custom-call(bf16[256,768]{1,0:T(8,128)(2,1)S(1)} %get-tuple-element.20.unit_ref, f32[256,128]{1,0:T(8,128)S(1)} %get-tuple-element.21.side_ref, f32[256,128]{1,0:T(8,128)S(1)} %get-tuple-element.22.old_sums_ref, ...), custom_call_target="tpu_custom_call", output_to_operand_aliasing={{0}: (2, {}), {1}: (3, {})} | custom-call | flops 30198988800 | bytes 2162688 | tf_op jit(solution)/shard_map/more_scores/pallas_call | solution.py:205
  24.7 0.4 %collective-permute-done.7.refs_0_ = bf16[97,8,128]{2,1,0:T(8,128)(2,1)S(1)} collective-permute-done((bf16[97,8,128]{2,1,0:T(8,128)(2,1)S(1)}, bf16[97,8,128]{2,1,0:T(8,128)(2,1)S(1)}, u32[]{:S(2)}, u32[]{:S(2)}) %collective-permute-start.7) | collective-permute-done | bytes 198688 | tf_op jit(solution)/shard_map/ppermute | solution.py:182
  25.1 0.5 %send_scores.1 = (bf16[64,768]{1,0:T(8,128)(2,1)S(1)}, bf16[72,768]{1,0:T(8,128)(2,1)S(1)}) custom-call(bf16[256,768]{1,0:T(8,128)(2,1)S(1)} %get-tuple-element.20.unit_ref, f32[256,128]{1,0:T(8,128)S(1)} %get-tuple-element.21.side_ref, f32[256,128]{1,0:T(8,128)S(1)} %get-tuple-element.24.old_sums_ref, f32[256,768]{1,0:T(8,128)S(1)} %get-tuple-element.25.old_mixed_ref, ...), custom_call_target="tpu_custom_call" | custom-call | flops 5033164800 | bytes 983040 | tf_op jit(solution)/shard_map/send_scores/pallas_call | solution.py:215
  25.7 0.1 collective-permute-start.9
  25.7 0.5 %collective-permute-start.8 = (bf16[64,768]{1,0:T(8,128)(2,1)S(1)}, bf16[64,768]{1,0:T(8,128)(2,1)S(1)}, u32[]{:S(2)}, u32[]{:S(2)}) collective-permute-start(bf16[64,768]{1,0:T(8,128)(2,1)S(1)} %get-tuple-element.28), channel_id=1, source_target_pairs={{0,1},{1,0},{2,3},{3,2},{4,5},{5,4},{6,7},{7,6},{8,9},{9,8},{10,11... | collective-permute-start | bytes 294920 | tf_op jit(solution)/shard_map/ppermute | solution.py:188
  26.2 0.5 %keep_scores.1 = (f32[128,128]{1,0:T(8,128)S(1)}, f32[128,768]{1,0:T(8,128)S(1)}) custom-call(bf16[256,768]{1,0:T(8,128)(2,1)S(1)} %get-tuple-element.20.unit_ref, f32[256,128]{1,0:T(8,128)S(1)} %get-tuple-element.21.side_ref, f32[256,128]{1,0:T(8,128)S(1)} %get-tuple-element.24.old_sums_ref, f32[256,768]{1,0:T(8,128)S(1)} %get-tuple-element.25.old_mixed_ref, ...), custom_call_target="tpu_custom_call" | custom-call | flops 5033164800 | bytes 983040 | tf_op jit(solution)/shard_map/keep_scores/pallas_call | solution.py:225
  26.7 0.4 %collective-permute-done.8.front_ref = bf16[64,768]{1,0:T(8,128)(2,1)S(1)} collective-permute-done((bf16[64,768]{1,0:T(8,128)(2,1)S(1)}, bf16[64,768]{1,0:T(8,128)(2,1)S(1)}, u32[]{:S(2)}, u32[]{:S(2)}) %collective-permute-start.8) | collective-permute-done | bytes 98336 | tf_op jit(solution)/shard_map/ppermute | solution.py:188
  27.2 0.0 collective-permute-done.9.rear_ref
  27.2 1.0 %combine.1 = (f32[1,128]{1,0:T(1,128)}, f32[128,768]{1,0:T(8,128)}) custom-call(f32[128,128]{1,0:T(8,128)S(1)} %get-tuple-element.26.sums_ref, f32[128,768]{1,0:T(8,128)S(1)} %get-tuple-element.27.mixed_ref, bf16[64,768]{1,0:T(8,128)(2,1)S(1)} %collective-permute-done.8.front_ref, bf16[72,768]{1,0:T(8,128)(2,1)S(1)} %collective-permute-done.9.rear_ref), custom_call_target="tpu_custom_call" | custom-call | tf_op jit(solution)/shard_map/combine/pallas_call | solution.py:272
  (2 shorter events, 0.0 us)
Async XLA Ops:
  0.6 0.9 %copy-start = (bf16[128,768]{1,0:T(8,128)(2,1)S(1)}, bf16[128,768]{1,0:T(8,128)(2,1)}, u32[]{:S(2)}) copy-start(bf16[128,768]{1,0:T(8,128)(2,1)} %param.3) | copy-start | bytes 589828
  0.6 0.9 %copy-start.1 = (s32[128,1]{0,1:T(1,128)S(1)}, s32[128,1]{0,1:T(1,128)}, u32[]{:S(2)}) copy-start(s32[128,1]{0,1:T(1,128)} %param.4) | copy-start | bytes 1540
  0.7 0.9 %copy-start.2 = (s32[128]{0:T(128)S(1)}, s32[128]{0:T(128)}, u32[]{:S(2)}) copy-start(s32[128]{0:T(128)} %param.5) | copy-start | bytes 1540
  1.6 9.4 %collective-permute-start = (bf16[97,8,128]{2,1,0:T(8,128)(2,1)S(1)}, bf16[97,8,128]{2,1,0:T(8,128)(2,1)S(1)}, u32[]{:S(2)}, u32[]{:S(2)}) collective-permute-start(bf16[97,8,128]{2,1,0:T(8,128)(2,1)S(1)} %pack.1.own_ref), channel_id=1, source_target_pairs={{0,8},{2,10},{8,12},{10,14},{12,4},{14,6},{4,0},{6,2},{1,9},{3,11}... | collective-permute-start | bytes 595976 | tf_op jit(solution)/shard_map/ppermute | solution.py:182
  5.7 6.4 %collective-permute-start.1 = (bf16[97,8,128]{2,1,0:T(8,128)(2,1)S(1)}, bf16[97,8,128]{2,1,0:T(8,128)(2,1)S(1)}, u32[]{:S(2)}, u32[]{:S(2)}) collective-permute-start(bf16[97,8,128]{2,1,0:T(8,128)(2,1)S(1)} %pack.1.own_ref), channel_id=1, source_target_pairs={{0,2},{2,0},{4,6},{6,4},{8,10},{10,8},{12,14},{14,12},{1,3},{3,1},... | collective-permute-start | bytes 595976 | tf_op jit(solution)/shard_map/ppermute | solution.py:185
  7.2 4.9 %collective-permute-start.2 = (bf16[97,8,128]{2,1,0:T(8,128)(2,1)S(1)}, bf16[97,8,128]{2,1,0:T(8,128)(2,1)S(1)}, u32[]{:S(2)}, u32[]{:S(2)}) collective-permute-start(bf16[97,8,128]{2,1,0:T(8,128)(2,1)S(1)} %pack.1.own_ref), channel_id=1, source_target_pairs={{0,1},{1,0},{2,3},{3,2},{4,5},{5,4},{6,7},{7,6},{8,9},{9,8},{10,11... | collective-permute-start | bytes 595976 | tf_op jit(solution)/shard_map/ppermute | solution.py:188
  7.2 9.1 %collective-permute-start.4 = (bf16[97,8,128]{2,1,0:T(8,128)(2,1)S(1)}, bf16[97,8,128]{2,1,0:T(8,128)(2,1)S(1)}, u32[]{:S(2)}, u32[]{:S(2)}) collective-permute-start(bf16[97,8,128]{2,1,0:T(8,128)(2,1)S(1)} %pack.1.own_ref), channel_id=1, source_target_pairs={{0,4},{2,6},{8,0},{10,2},{12,8},{14,10},{4,12},{6,14},{1,5},{3,7},... | collective-permute-start | bytes 595976 | tf_op jit(solution)/shard_map/ppermute | solution.py:182
  12.1 6.5 %collective-permute-start.3 = (bf16[97,8,128]{2,1,0:T(8,128)(2,1)S(1)}, bf16[97,8,128]{2,1,0:T(8,128)(2,1)S(1)}, u32[]{:S(2)}, u32[]{:S(2)}) collective-permute-start(bf16[97,8,128]{2,1,0:T(8,128)(2,1)S(1)} %collective-permute-done.refs_1_), channel_id=1, source_target_pairs={{0,2},{2,0},{4,6},{6,4},{8,10},{10,8},{12,14},{14,12},{1,3},{3,1},... | collective-permute-start | bytes 595976 | tf_op jit(solution)/shard_map/ppermute | solution.py:185
  13.6 9.0 %collective-permute-start.5 = (bf16[97,8,128]{2,1,0:T(8,128)(2,1)S(1)}, bf16[97,8,128]{2,1,0:T(8,128)(2,1)S(1)}, u32[]{:S(2)}, u32[]{:S(2)}) collective-permute-start(bf16[97,8,128]{2,1,0:T(8,128)(2,1)S(1)} %collective-permute-done.refs_1_), channel_id=1, source_target_pairs={{0,8},{2,10},{8,12},{10,14},{12,4},{14,6},{4,0},{6,2},{1,9},{3,11}... | collective-permute-start | bytes 595976 | tf_op jit(solution)/shard_map/ppermute | solution.py:182
  16.3 7.4 %collective-permute-start.6 = (bf16[97,8,128]{2,1,0:T(8,128)(2,1)S(1)}, bf16[97,8,128]{2,1,0:T(8,128)(2,1)S(1)}, u32[]{:S(2)}, u32[]{:S(2)}) collective-permute-start(bf16[97,8,128]{2,1,0:T(8,128)(2,1)S(1)} %collective-permute-done.4.refs_0_), channel_id=1, source_target_pairs={{0,2},{2,0},{4,6},{6,4},{8,10},{10,8},{12,14},{14,12},{1,3},{3,1},... | collective-permute-start | bytes 595976 | tf_op jit(solution)/shard_map/ppermute | solution.py:185
  18.6 6.5 %collective-permute-start.7 = (bf16[97,8,128]{2,1,0:T(8,128)(2,1)S(1)}, bf16[97,8,128]{2,1,0:T(8,128)(2,1)S(1)}, u32[]{:S(2)}, u32[]{:S(2)}) collective-permute-start(bf16[97,8,128]{2,1,0:T(8,128)(2,1)S(1)} %collective-permute-done.3.refs_2_), channel_id=1, source_target_pairs={{0,8},{2,10},{8,12},{10,14},{12,4},{14,6},{4,0},{6,2},{1,9},{3,11}... | collective-permute-start | bytes 595976 | tf_op jit(solution)/shard_map/ppermute | solution.py:182
  25.7 1.5 %collective-permute-start.9 = (bf16[72,768]{1,0:T(8,128)(2,1)S(1)}, bf16[72,768]{1,0:T(8,128)(2,1)S(1)}, u32[]{:S(2)}, u32[]{:S(2)}) collective-permute-start(bf16[72,768]{1,0:T(8,128)(2,1)S(1)} %get-tuple-element.29), channel_id=1, source_target_pairs={{0,1},{1,0},{2,3},{3,2},{4,5},{5,4},{6,7},{7,6},{8,9},{9,8},{10,11... | collective-permute-start | bytes 331784 | tf_op jit(solution)/shard_map/ppermute | solution.py:188
  25.7 1.4 %collective-permute-start.8 = (bf16[64,768]{1,0:T(8,128)(2,1)S(1)}, bf16[64,768]{1,0:T(8,128)(2,1)S(1)}, u32[]{:S(2)}, u32[]{:S(2)}) collective-permute-start(bf16[64,768]{1,0:T(8,128)(2,1)S(1)} %get-tuple-element.28), channel_id=1, source_target_pairs={{0,1},{1,0},{2,3},{3,2},{4,5},{5,4},{6,7},{7,6},{8,9},{9,8},{10,11... | collective-permute-start | bytes 294920 | tf_op jit(solution)/shard_map/ppermute | solution.py:188

commit v28 on v21

--- a/solution.py
+++ b/solution.py
@@ -244,10 +244,11 @@
         moved, beside, other = lax.optimization_barrier((moved, beside, other))
         opposite = along(moved, 1)
         moved_beside = across(moved)
+        unit, side, sums, mixed = first(own, other, beside, moved, ahead)
+        sums, ahead = lax.optimization_barrier((sums, ahead))
         ahead_beside = across(ahead)
-        last = [along(moved_beside, 1)]
-        unit, side, sums, mixed = first(own, other, beside, moved, moved_beside)
-        sums, mixed = more(unit, side, sums, mixed, ahead, opposite, ahead_beside)
+        last = [along(moved_beside, 1), ahead_beside]
+        sums, mixed = more(unit, side, sums, mixed, moved_beside, opposite)
     else:
         unit, side, sums, mixed = first(own, other, beside)
 

time: 28.3 us -> 29.6 us (1.046)
  waiting for transfers between devices: 7.71 us -> 11.2 us
  starting transfers between devices: 14.6 us -> 12.4 us
    ppermute x3, waiting for transfers between devices: 2.16 us -> 4.7 us  [across(): return lax.ppermute(array, 'shard', [(at, at ^ 1) for at in range(shards)])]
    ppermute x4, starting transfers between devices: 9.19 us -> 6.99 us  [along(): return lax.ppermute(array, 'shard', pairs)]
    ppermute x4, waiting for transfers between devices: 4.62 us -> 5.68 us  [along(): return lax.ppermute(array, 'shard', pairs)]
  transfers between devices with their start and end apart: 9 -> 9, of which waited for: 6 -> 6; matrix products, arithmetic and copies ran while one was open for 0% -> 0% of each run, Pallas kernels for 10% -> 9%
where the time goes in v28:
time: 29.6 us; the launch traced here: 29.5 us
  starting transfers between devices  12.4 us (42%)
  waiting for transfers between devices  11.2 us (38%)
  Pallas kernels  4.26 us (14%)
  local copies, waits for them, and re-layouts  0.9 us (3%)
  between operations  0.71 us (2%)
    ppermute x4, starting transfers between devices, along(): return lax.ppermute(array, 'shard', pairs)  6.99 us
    ppermute x4, waiting for transfers between devices, along(): return lax.ppermute(array, 'shard', pairs)  5.68 us
    ppermute x3, starting transfers between devices, across(): return lax.ppermute(array, 'shard', [(at, at ^ 1) for at in range(shards)])  5.36 us
    ppermute x3, waiting for transfers between devices, across(): return lax.ppermute(array, 'shard', [(at, at ^ 1) for at in range(shards)])  4.7 us
    pallas_call x1, Pallas kernels, first(): pl.pallas_call(first_kernel, out_shape=[shape(queries, width, dtype=bf16)...  1.19 us
    pallas_call x1, Pallas kernels, local(): pl.pallas_call(combine_kernel, out_shape=[shape(1, count), shape(count, w...  0.95 us
    unnamed x6, local copies, waits for them, and re-layouts  0.9 us
    pallas_call x1, Pallas kernels, more(): pl.pallas_call(more_kernel, out_shape=[shape(queries, 128), shape(queries...  0.86 us
  transfers between devices with their start and end apart: 9, of which 6 were waited for; matrix products, arithmetic and copies ran while one was open for 0% of the time, Pallas kernels for 9%

profile of v28, /device:TPU:0, one launch (start us, length us, event | category | flops | bytes accessed | tf_op | source)
XLA Modules:
  0.0 29.5 jit_solution(14013435055710722573)
XLA Ops:
  0.6 0.0 copy-start
  0.6 0.0 copy-start.1
  0.7 0.0 copy-start.2
  0.7 0.9 %copy-done = bf16[128,768]{1,0:T(8,128)(2,1)S(1)} copy-done((bf16[128,768]{1,0:T(8,128)(2,1)S(1)}, bf16[128,768]{1,0:T(8,128)(2,1)}, u32[]{:S(2)}) %copy-start) | copy-done | bytes 196632
  1.6 0.0 copy-done.1
  1.6 0.0 copy-done.2
  1.6 4.1 %collective-permute-start = (bf16[97,8,128]{2,1,0:T(8,128)(2,1)S(1)}, bf16[97,8,128]{2,1,0:T(8,128)(2,1)S(1)}, u32[]{:S(2)}, u32[]{:S(2)}) collective-permute-start(bf16[97,8,128]{2,1,0:T(8,128)(2,1)S(1)} %pack.1.own_ref), channel_id=1, source_target_pairs={{0,8},{2,10},{8,12},{10,14},{12,4},{14,6},{4,0},{6,2},{1,9},{3,11}... | collective-permute-start | bytes 595976 | tf_op jit(solution)/shard_map/ppermute | solution.py:176
  5.7 1.5 %collective-permute-start.1 = (bf16[97,8,128]{2,1,0:T(8,128)(2,1)S(1)}, bf16[97,8,128]{2,1,0:T(8,128)(2,1)S(1)}, u32[]{:S(2)}, u32[]{:S(2)}) collective-permute-start(bf16[97,8,128]{2,1,0:T(8,128)(2,1)S(1)} %pack.1.own_ref), channel_id=1, source_target_pairs={{0,2},{2,0},{4,6},{6,4},{8,10},{10,8},{12,14},{14,12},{1,3},{3,1},... | collective-permute-start | bytes 595976 | tf_op jit(solution)/shard_map/ppermute | solution.py:179
  7.2 0.0 collective-permute-start.2
  7.2 0.0 collective-permute-start.3
  7.2 3.9 %collective-permute-done.refs_1_ = bf16[97,8,128]{2,1,0:T(8,128)(2,1)S(1)} collective-permute-done((bf16[97,8,128]{2,1,0:T(8,128)(2,1)S(1)}, bf16[97,8,128]{2,1,0:T(8,128)(2,1)S(1)}, u32[]{:S(2)}, u32[]{:S(2)}) %collective-permute-start) | collective-permute-done | bytes 198688 | tf_op jit(solution)/shard_map/ppermute | solution.py:176
  11.0 1.1 %collective-permute-done.1.refs_0_ = bf16[97,8,128]{2,1,0:T(8,128)(2,1)S(1)} collective-permute-done((bf16[97,8,128]{2,1,0:T(8,128)(2,1)S(1)}, bf16[97,8,128]{2,1,0:T(8,128)(2,1)S(1)}, u32[]{:S(2)}, u32[]{:S(2)}) %collective-permute-start.1) | collective-permute-done | bytes 198688 | tf_op jit(solution)/shard_map/ppermute | solution.py:179
  12.1 0.0 collective-permute-done.2.other_ref
  12.1 1.5 %collective-permute-start.4 = (bf16[97,8,128]{2,1,0:T(8,128)(2,1)S(1)}, bf16[97,8,128]{2,1,0:T(8,128)(2,1)S(1)}, u32[]{:S(2)}, u32[]{:S(2)}) collective-permute-start(bf16[97,8,128]{2,1,0:T(8,128)(2,1)S(1)} %collective-permute-done.refs_1_), channel_id=1, source_target_pairs={{0,2},{2,0},{4,6},{6,4},{8,10},{10,8},{12,14},{14,12},{1,3},{3,1},... | collective-permute-start | bytes 595976 | tf_op jit(solution)/shard_map/ppermute | solution.py:179
  13.6 2.3 %collective-permute-start.5 = (bf16[97,8,128]{2,1,0:T(8,128)(2,1)S(1)}, bf16[97,8,128]{2,1,0:T(8,128)(2,1)S(1)}, u32[]{:S(2)}, u32[]{:S(2)}) collective-permute-start(bf16[97,8,128]{2,1,0:T(8,128)(2,1)S(1)} %collective-permute-done.refs_1_), channel_id=1, source_target_pairs={{0,8},{2,10},{8,12},{10,14},{12,4},{14,6},{4,0},{6,2},{1,9},{3,11}... | collective-permute-start | bytes 595976 | tf_op jit(solution)/shard_map/ppermute | solution.py:176
  15.9 0.4 %collective-permute-done.3.refs_2_ = bf16[97,8,128]{2,1,0:T(8,128)(2,1)S(1)} collective-permute-done((bf16[97,8,128]{2,1,0:T(8,128)(2,1)S(1)}, bf16[97,8,128]{2,1,0:T(8,128)(2,1)S(1)}, u32[]{:S(2)}, u32[]{:S(2)}) %collective-permute-start.3) | collective-permute-done | bytes 198688 | tf_op jit(solution)/shard_map/ppermute | solution.py:176
  16.3 1.2 %first_scores.1 = (bf16[256,768]{1,0:T(8,128)(2,1)S(1)}, f32[256,128]{1,0:T(8,128)S(1)}, f32[256,128]{1,0:T(8,128)S(1)}, f32[256,768]{1,0:T(8,128)S(1)}) custom-call(bf16[97,8,128]{2,1,0:T(8,128)(2,1)S(1)} %pack.1.own_ref, bf16[97,8,128]{2,1,0:T(8,128)(2,1)S(1)} %collective-permute-done.2.other_ref, bf16[97,8,128]{2,1,0:T(8,128)(2,1)S(1)} %collective-permute-done.1.refs_0_, ...), custom_call_target="tpu_custom_call" | custom-call | flops 40265318400 | bytes 2359296 | tf_op jit(solution)/shard_map/first_scores/pallas_call | solution.py:185
  17.5 2.4 %collective-permute-start.7 = (bf16[97,8,128]{2,1,0:T(8,128)(2,1)S(1)}, bf16[97,8,128]{2,1,0:T(8,128)(2,1)S(1)}, u32[]{:S(2)}, u32[]{:S(2)}) collective-permute-start(bf16[97,8,128]{2,1,0:T(8,128)(2,1)S(1)} %collective-permute-done.3.refs_2_), channel_id=1, source_target_pairs={{0,2},{2,0},{4,6},{6,4},{8,10},{10,8},{12,14},{14,12},{1,3},{3,1},... | collective-permute-start | bytes 595976 | tf_op jit(solution)/shard_map/ppermute | solution.py:179
  19.8 0.0 collective-permute-done.4.refs_0_
  19.8 0.6 %collective-permute-start.6 = (bf16[97,8,128]{2,1,0:T(8,128)(2,1)S(1)}, bf16[97,8,128]{2,1,0:T(8,128)(2,1)S(1)}, u32[]{:S(2)}, u32[]{:S(2)}) collective-permute-start(bf16[97,8,128]{2,1,0:T(8,128)(2,1)S(1)} %collective-permute-done.4.refs_0_), channel_id=1, source_target_pairs={{0,8},{2,10},{8,12},{10,14},{12,4},{14,6},{4,0},{6,2},{1,9},{3,11}... | collective-permute-start | bytes 595976 | tf_op jit(solution)/shard_map/ppermute | solution.py:176
  20.4 0.0 collective-permute-done.5.refs_1_
  20.4 0.9 %more_scores.1 = (f32[256,128]{1,0:T(8,128)S(1)}, f32[256,768]{1,0:T(8,128)S(1)}) custom-call(bf16[256,768]{1,0:T(8,128)(2,1)S(1)} %get-tuple-element.20.unit_ref, f32[256,128]{1,0:T(8,128)S(1)} %get-tuple-element.21.side_ref, f32[256,128]{1,0:T(8,128)S(1)} %get-tuple-element.23.old_sums_ref, ...), custom_call_target="tpu_custom_call", output_to_operand_aliasing={{0}: (2, {}), {1}: (3, {})} | custom-call | flops 20132659200 | bytes 1966080 | tf_op jit(solution)/shard_map/more_scores/pallas_call | solution.py:199
  21.3 3.6 %collective-permute-done.7.refs_1_ = bf16[97,8,128]{2,1,0:T(8,128)(2,1)S(1)} collective-permute-done((bf16[97,8,128]{2,1,0:T(8,128)(2,1)S(1)}, bf16[97,8,128]{2,1,0:T(8,128)(2,1)S(1)}, u32[]{:S(2)}, u32[]{:S(2)}) %collective-permute-start.7) | collective-permute-done | bytes 198688 | tf_op jit(solution)/shard_map/ppermute | solution.py:179
  24.9 1.5 %collective-permute-done.6.refs_0_ = bf16[97,8,128]{2,1,0:T(8,128)(2,1)S(1)} collective-permute-done((bf16[97,8,128]{2,1,0:T(8,128)(2,1)S(1)}, bf16[97,8,128]{2,1,0:T(8,128)(2,1)S(1)}, u32[]{:S(2)}, u32[]{:S(2)}) %collective-permute-start.6) | collective-permute-done | bytes 198688 | tf_op jit(solution)/shard_map/ppermute | solution.py:176
  26.4 0.6 %send_scores.1 = bf16[136,768]{1,0:T(8,128)(2,1)S(1)} custom-call(bf16[256,768]{1,0:T(8,128)(2,1)S(1)} %get-tuple-element.20.unit_ref, f32[256,128]{1,0:T(8,128)S(1)} %get-tuple-element.21.side_ref, f32[256,128]{1,0:T(8,128)S(1)} %get-tuple-element.25.old_sums_ref, f32[256,768]{1,0:T(8,128)S(1)} %get-tuple-element.26.old_mixed_ref, ...), custom_call_target="tpu_custom_call" | custom-call | flops 10066329600 | bytes 1179648 | tf_op jit(solution)/shard_map/send_scores/pallas_call | solution.py:209
  27.0 0.1 collective-permute-start.8
  27.1 0.6 %keep_scores.1 = (f32[128,128]{1,0:T(8,128)S(1)}, f32[128,768]{1,0:T(8,128)S(1)}) custom-call(bf16[256,768]{1,0:T(8,128)(2,1)S(1)} %get-tuple-element.20.unit_ref, f32[256,128]{1,0:T(8,128)S(1)} %get-tuple-element.21.side_ref, f32[256,128]{1,0:T(8,128)S(1)} %get-tuple-element.25.old_sums_ref, f32[256,768]{1,0:T(8,128)S(1)} %get-tuple-element.26.old_mixed_ref, ...), custom_call_target="tpu_custom_call" | custom-call | flops 10066329600 | bytes 1179648 | tf_op jit(solution)/shard_map/keep_scores/pallas_call | solution.py:216
  27.7 0.8 %collective-permute-done.8.got_ref = bf16[136,768]{1,0:T(8,128)(2,1)S(1)} collective-permute-done((bf16[136,768]{1,0:T(8,128)(2,1)S(1)}, bf16[136,768]{1,0:T(8,128)(2,1)S(1)}, u32[]{:S(2)}, u32[]{:S(2)}) %collective-permute-start.8) | collective-permute-done | bytes 208928 | tf_op jit(solution)/shard_map/ppermute | solution.py:182
  28.5 1.0 %combine.1 = (f32[1,128]{1,0:T(1,128)}, f32[128,768]{1,0:T(8,128)}) custom-call(f32[128,128]{1,0:T(8,128)S(1)} %get-tuple-element.28.sums_ref, f32[128,768]{1,0:T(8,128)S(1)} %get-tuple-element.29.mixed_ref, bf16[136,768]{1,0:T(8,128)(2,1)S(1)} %collective-permute-done.8.got_ref), custom_call_target="tpu_custom_call" | custom-call | tf_op jit(solution)/shard_map/combine/pallas_call | solution.py:264
  (2 shorter events, 0.0 us)
Async XLA Ops:
  0.6 0.9 %copy-start = (bf16[128,768]{1,0:T(8,128)(2,1)S(1)}, bf16[128,768]{1,0:T(8,128)(2,1)}, u32[]{:S(2)}) copy-start(bf16[128,768]{1,0:T(8,128)(2,1)} %param.3) | copy-start | bytes 589828
  0.6 0.9 %copy-start.1 = (s32[128,1]{0,1:T(1,128)S(1)}, s32[128,1]{0,1:T(1,128)}, u32[]{:S(2)}) copy-start(s32[128,1]{0,1:T(1,128)} %param.4) | copy-start | bytes 1540
  0.7 0.9 %copy-start.2 = (s32[128]{0:T(128)S(1)}, s32[128]{0:T(128)}, u32[]{:S(2)}) copy-start(s32[128]{0:T(128)} %param.5) | copy-start | bytes 1540
  1.6 9.4 %collective-permute-start = (bf16[97,8,128]{2,1,0:T(8,128)(2,1)S(1)}, bf16[97,8,128]{2,1,0:T(8,128)(2,1)S(1)}, u32[]{:S(2)}, u32[]{:S(2)}) collective-permute-start(bf16[97,8,128]{2,1,0:T(8,128)(2,1)S(1)} %pack.1.own_ref), channel_id=1, source_target_pairs={{0,8},{2,10},{8,12},{10,14},{12,4},{14,6},{4,0},{6,2},{1,9},{3,11}... | collective-permute-start | bytes 595976 | tf_op jit(solution)/shard_map/ppermute | solution.py:176
  5.7 6.4 %collective-permute-start.1 = (bf16[97,8,128]{2,1,0:T(8,128)(2,1)S(1)}, bf16[97,8,128]{2,1,0:T(8,128)(2,1)S(1)}, u32[]{:S(2)}, u32[]{:S(2)}) collective-permute-start(bf16[97,8,128]{2,1,0:T(8,128)(2,1)S(1)} %pack.1.own_ref), channel_id=1, source_target_pairs={{0,2},{2,0},{4,6},{6,4},{8,10},{10,8},{12,14},{14,12},{1,3},{3,1},... | collective-permute-start | bytes 595976 | tf_op jit(solution)/shard_map/ppermute | solution.py:179
  7.2 4.9 %collective-permute-start.2 = (bf16[97,8,128]{2,1,0:T(8,128)(2,1)S(1)}, bf16[97,8,128]{2,1,0:T(8,128)(2,1)S(1)}, u32[]{:S(2)}, u32[]{:S(2)}) collective-permute-start(bf16[97,8,128]{2,1,0:T(8,128)(2,1)S(1)} %pack.1.own_ref), channel_id=1, source_target_pairs={{0,1},{1,0},{2,3},{3,2},{4,5},{5,4},{6,7},{7,6},{8,9},{9,8},{10,11... | collective-permute-start | bytes 595976 | tf_op jit(solution)/shard_map/ppermute | solution.py:182
  7.2 9.1 %collective-permute-start.3 = (bf16[97,8,128]{2,1,0:T(8,128)(2,1)S(1)}, bf16[97,8,128]{2,1,0:T(8,128)(2,1)S(1)}, u32[]{:S(2)}, u32[]{:S(2)}) collective-permute-start(bf16[97,8,128]{2,1,0:T(8,128)(2,1)S(1)} %pack.1.own_ref), channel_id=1, source_target_pairs={{0,4},{2,6},{8,0},{10,2},{12,8},{14,10},{4,12},{6,14},{1,5},{3,7},... | collective-permute-start | bytes 595976 | tf_op jit(solution)/shard_map/ppermute | solution.py:176
  12.1 7.8 %collective-permute-start.4 = (bf16[97,8,128]{2,1,0:T(8,128)(2,1)S(1)}, bf16[97,8,128]{2,1,0:T(8,128)(2,1)S(1)}, u32[]{:S(2)}, u32[]{:S(2)}) collective-permute-start(bf16[97,8,128]{2,1,0:T(8,128)(2,1)S(1)} %collective-permute-done.refs_1_), channel_id=1, source_target_pairs={{0,2},{2,0},{4,6},{6,4},{8,10},{10,8},{12,14},{14,12},{1,3},{3,1},... | collective-permute-start | bytes 595976 | tf_op jit(solution)/shard_map/ppermute | solution.py:179
  13.6 6.8 %collective-permute-start.5 = (bf16[97,8,128]{2,1,0:T(8,128)(2,1)S(1)}, bf16[97,8,128]{2,1,0:T(8,128)(2,1)S(1)}, u32[]{:S(2)}, u32[]{:S(2)}) collective-permute-start(bf16[97,8,128]{2,1,0:T(8,128)(2,1)S(1)} %collective-permute-done.refs_1_), channel_id=1, source_target_pairs={{0,8},{2,10},{8,12},{10,14},{12,4},{14,6},{4,0},{6,2},{1,9},{3,11}... | collective-permute-start | bytes 595976 | tf_op jit(solution)/shard_map/ppermute | solution.py:176
  17.5 7.5 %collective-permute-start.7 = (bf16[97,8,128]{2,1,0:T(8,128)(2,1)S(1)}, bf16[97,8,128]{2,1,0:T(8,128)(2,1)S(1)}, u32[]{:S(2)}, u32[]{:S(2)}) collective-permute-start(bf16[97,8,128]{2,1,0:T(8,128)(2,1)S(1)} %collective-permute-done.3.refs_2_), channel_id=1, source_target_pairs={{0,2},{2,0},{4,6},{6,4},{8,10},{10,8},{12,14},{14,12},{1,3},{3,1},... | collective-permute-start | bytes 595976 | tf_op jit(solution)/shard_map/ppermute | solution.py:179
  19.8 6.5 %collective-permute-start.6 = (bf16[97,8,128]{2,1,0:T(8,128)(2,1)S(1)}, bf16[97,8,128]{2,1,0:T(8,128)(2,1)S(1)}, u32[]{:S(2)}, u32[]{:S(2)}) collective-permute-start(bf16[97,8,128]{2,1,0:T(8,128)(2,1)S(1)} %collective-permute-done.4.refs_0_), channel_id=1, source_target_pairs={{0,8},{2,10},{8,12},{10,14},{12,4},{14,6},{4,0},{6,2},{1,9},{3,11}... | collective-permute-start | bytes 595976 | tf_op jit(solution)/shard_map/ppermute | solution.py:176
  27.0 1.5 %collective-permute-start.8 = (bf16[136,768]{1,0:T(8,128)(2,1)S(1)}, bf16[136,768]{1,0:T(8,128)(2,1)S(1)}, u32[]{:S(2)}, u32[]{:S(2)}) collective-permute-start(bf16[136,768]{1,0:T(8,128)(2,1)S(1)} %send_scores.1), channel_id=1, source_target_pairs={{0,1},{1,0},{2,3},{3,2},{4,5},{5,4},{6,7},{7,6},{8,9},{9,8},{10,11... | collective-permute-start | bytes 626696 | tf_op jit(solution)/shard_map/ppermute | solution.py:182

commit v29 on v21

--- a/solution.py
+++ b/solution.py
@@ -241,7 +241,7 @@
     other = swap(own)
     if rounds == 4:
         ahead = along(own, -1)
-        moved, beside, other = lax.optimization_barrier((moved, beside, other))
+        moved, beside = lax.optimization_barrier((moved, beside))
         opposite = along(moved, 1)
         moved_beside = across(moved)
         ahead_beside = across(ahead)

time: 28.3 us -> 28.3 us (level)
    ppermute x3, starting transfers between devices: 5.29 us -> 4.48 us  [across(): return lax.ppermute(array, 'shard', [(at, at ^ 1) for at in range(shards)])]
    ppermute x4, starting transfers between devices: 9.19 us -> 9.89 us  [along(): return lax.ppermute(array, 'shard', pairs)]
    ppermute x4, waiting for transfers between devices: 4.62 us -> 4.98 us  [along(): return lax.ppermute(array, 'shard', pairs)]
where the time goes in v29:
time: 28.3 us; the launch traced here: 28.2 us
  starting transfers between devices  14.5 us (51%)
  waiting for transfers between devices  7.87 us (28%)
  Pallas kernels  4.26 us (15%)
  local copies, waits for them, and re-layouts  0.9 us (3%)
  between operations  0.71 us (3%)
    ppermute x4, starting transfers between devices, along(): return lax.ppermute(array, 'shard', pairs)  9.89 us
    ppermute x4, waiting for transfers between devices, along(): return lax.ppermute(array, 'shard', pairs)  4.98 us
    ppermute x3, starting transfers between devices, across(): return lax.ppermute(array, 'shard', [(at, at ^ 1) for at in range(shards)])  4.48 us
    ppermute x3, waiting for transfers between devices, across(): return lax.ppermute(array, 'shard', [(at, at ^ 1) for at in range(shards)])  1.96 us
    pallas_call x1, Pallas kernels, first(): pl.pallas_call(first_kernel, out_shape=[shape(queries, width, dtype=bf16)...  1.19 us
    pallas_call x1, Pallas kernels, more(): pl.pallas_call(more_kernel, out_shape=[shape(queries, 128), shape(queries...  1.05 us
    pallas_call x1, Pallas kernels, local(): pl.pallas_call(combine_kernel, out_shape=[shape(1, count), shape(count, w...  0.95 us
    ppermute x2, waiting for transfers between devices, swap(): lax.ppermute(array, 'owner', [(at, lanes - 1 - at) for at in range(lanes)])  0.93 us
  transfers between devices with their start and end apart: 9, of which 6 were waited for; matrix products, arithmetic and copies ran while one was open for 0% of the time, Pallas kernels for 10%

profile of v29, /device:TPU:0, one launch (start us, length us, event | category | flops | bytes accessed | tf_op | source)
XLA Modules:
  0.0 28.2 jit_solution(11867391627211112867)
XLA Ops:
  0.6 0.0 copy-start
  0.6 0.0 copy-start.1
  0.7 0.0 copy-start.2
  0.7 0.9 %copy-done = bf16[128,768]{1,0:T(8,128)(2,1)S(1)} copy-done((bf16[128,768]{1,0:T(8,128)(2,1)S(1)}, bf16[128,768]{1,0:T(8,128)(2,1)}, u32[]{:S(2)}) %copy-start) | copy-done | bytes 196632
  1.6 0.0 copy-done.1
  1.6 0.0 copy-done.2
  1.6 4.1 %collective-permute-start.1 = (bf16[97,8,128]{2,1,0:T(8,128)(2,1)S(1)}, bf16[97,8,128]{2,1,0:T(8,128)(2,1)S(1)}, u32[]{:S(2)}, u32[]{:S(2)}) collective-permute-start(bf16[97,8,128]{2,1,0:T(8,128)(2,1)S(1)} %pack.1.own_ref), channel_id=1, source_target_pairs={{0,8},{2,10},{8,12},{10,14},{12,4},{14,6},{4,0},{6,2},{1,9},{3,11}... | collective-permute-start | bytes 595976 | tf_op jit(solution)/shard_map/ppermute | solution.py:176
  5.7 1.5 %collective-permute-start.2 = (bf16[97,8,128]{2,1,0:T(8,128)(2,1)S(1)}, bf16[97,8,128]{2,1,0:T(8,128)(2,1)S(1)}, u32[]{:S(2)}, u32[]{:S(2)}) collective-permute-start(bf16[97,8,128]{2,1,0:T(8,128)(2,1)S(1)} %pack.1.own_ref), channel_id=1, source_target_pairs={{0,2},{2,0},{4,6},{6,4},{8,10},{10,8},{12,14},{14,12},{1,3},{3,1},... | collective-permute-start | bytes 595976 | tf_op jit(solution)/shard_map/ppermute | solution.py:179
  7.2 0.0 collective-permute-start.4
  7.2 3.9 %collective-permute-done.1.refs_1_ = bf16[97,8,128]{2,1,0:T(8,128)(2,1)S(1)} collective-permute-done((bf16[97,8,128]{2,1,0:T(8,128)(2,1)S(1)}, bf16[97,8,128]{2,1,0:T(8,128)(2,1)S(1)}, u32[]{:S(2)}, u32[]{:S(2)}) %collective-permute-start.1) | collective-permute-done | bytes 198688 | tf_op jit(solution)/shard_map/ppermute | solution.py:176
  11.1 1.0 %collective-permute-done.2.refs_0_ = bf16[97,8,128]{2,1,0:T(8,128)(2,1)S(1)} collective-permute-done((bf16[97,8,128]{2,1,0:T(8,128)(2,1)S(1)}, bf16[97,8,128]{2,1,0:T(8,128)(2,1)S(1)}, u32[]{:S(2)}, u32[]{:S(2)}) %collective-permute-start.2) | collective-permute-done | bytes 198688 | tf_op jit(solution)/shard_map/ppermute | solution.py:179
  12.1 1.5 %collective-permute-start.3 = (bf16[97,8,128]{2,1,0:T(8,128)(2,1)S(1)}, bf16[97,8,128]{2,1,0:T(8,128)(2,1)S(1)}, u32[]{:S(2)}, u32[]{:S(2)}) collective-permute-start(bf16[97,8,128]{2,1,0:T(8,128)(2,1)S(1)} %collective-permute-done.1.refs_1_), channel_id=1, source_target_pairs={{0,2},{2,0},{4,6},{6,4},{8,10},{10,8},{12,14},{14,12},{1,3},{3,1},... | collective-permute-start | bytes 595976 | tf_op jit(solution)/shard_map/ppermute | solution.py:179
  13.6 0.0 collective-permute-start
  13.6 2.4 %collective-permute-start.5 = (bf16[97,8,128]{2,1,0:T(8,128)(2,1)S(1)}, bf16[97,8,128]{2,1,0:T(8,128)(2,1)S(1)}, u32[]{:S(2)}, u32[]{:S(2)}) collective-permute-start(bf16[97,8,128]{2,1,0:T(8,128)(2,1)S(1)} %collective-permute-done.1.refs_1_), channel_id=1, source_target_pairs={{0,8},{2,10},{8,12},{10,14},{12,4},{14,6},{4,0},{6,2},{1,9},{3,11}... | collective-permute-start | bytes 595976 | tf_op jit(solution)/shard_map/ppermute | solution.py:176
  15.9 0.0 collective-permute-done.4.refs_0_
  16.0 1.5 %collective-permute-start.6 = (bf16[97,8,128]{2,1,0:T(8,128)(2,1)S(1)}, bf16[97,8,128]{2,1,0:T(8,128)(2,1)S(1)}, u32[]{:S(2)}, u32[]{:S(2)}) collective-permute-start(bf16[97,8,128]{2,1,0:T(8,128)(2,1)S(1)} %collective-permute-done.4.refs_0_), channel_id=1, source_target_pairs={{0,2},{2,0},{4,6},{6,4},{8,10},{10,8},{12,14},{14,12},{1,3},{3,1},... | collective-permute-start | bytes 595976 | tf_op jit(solution)/shard_map/ppermute | solution.py:179
  17.5 0.3 %collective-permute-done.3.refs_2_ = bf16[97,8,128]{2,1,0:T(8,128)(2,1)S(1)} collective-permute-done((bf16[97,8,128]{2,1,0:T(8,128)(2,1)S(1)}, bf16[97,8,128]{2,1,0:T(8,128)(2,1)S(1)}, u32[]{:S(2)}, u32[]{:S(2)}) %collective-permute-start.3) | collective-permute-done | bytes 198688 | tf_op jit(solution)/shard_map/ppermute | solution.py:179
  17.8 3.4 %collective-permute-start.7 = (bf16[97,8,128]{2,1,0:T(8,128)(2,1)S(1)}, bf16[97,8,128]{2,1,0:T(8,128)(2,1)S(1)}, u32[]{:S(2)}, u32[]{:S(2)}) collective-permute-start(bf16[97,8,128]{2,1,0:T(8,128)(2,1)S(1)} %collective-permute-done.3.refs_2_), channel_id=1, source_target_pairs={{0,8},{2,10},{8,12},{10,14},{12,4},{14,6},{4,0},{6,2},{1,9},{3,11}... | collective-permute-start | bytes 595976 | tf_op jit(solution)/shard_map/ppermute | solution.py:176
  21.2 0.0 collective-permute-done.other_ref
  21.2 1.2 %first_scores.1 = (bf16[256,768]{1,0:T(8,128)(2,1)S(1)}, f32[256,128]{1,0:T(8,128)S(1)}, f32[256,128]{1,0:T(8,128)S(1)}, f32[256,768]{1,0:T(8,128)S(1)}) custom-call(bf16[97,8,128]{2,1,0:T(8,128)(2,1)S(1)} %pack.1.own_ref, bf16[97,8,128]{2,1,0:T(8,128)(2,1)S(1)} %collective-permute-done.other_ref, bf16[97,8,128]{2,1,0:T(8,128)(2,1)S(1)} %collective-permute-done.2.refs_0_, ...), custom_call_target="tpu_custom_call" | custom-call | flops 40265318400 | bytes 2359296 | tf_op jit(solution)/shard_map/first_scores/pallas_call | solution.py:185
  22.4 0.0 collective-permute-done.5.refs_1_
  22.4 0.6 %collective-permute-done.6.refs_2_ = bf16[97,8,128]{2,1,0:T(8,128)(2,1)S(1)} collective-permute-done((bf16[97,8,128]{2,1,0:T(8,128)(2,1)S(1)}, bf16[97,8,128]{2,1,0:T(8,128)(2,1)S(1)}, u32[]{:S(2)}, u32[]{:S(2)}) %collective-permute-start.6) | collective-permute-done | bytes 198688 | tf_op jit(solution)/shard_map/ppermute | solution.py:179
  23.0 1.1 %more_scores.1 = (f32[256,128]{1,0:T(8,128)S(1)}, f32[256,768]{1,0:T(8,128)S(1)}) custom-call(bf16[256,768]{1,0:T(8,128)(2,1)S(1)} %get-tuple-element.16.unit_ref, f32[256,128]{1,0:T(8,128)S(1)} %get-tuple-element.17.side_ref, f32[256,128]{1,0:T(8,128)S(1)} %get-tuple-element.18.old_sums_ref, ...), custom_call_target="tpu_custom_call", output_to_operand_aliasing={{0}: (2, {}), {1}: (3, {})} | custom-call | flops 30198988800 | bytes 2162688 | tf_op jit(solution)/shard_map/more_scores/pallas_call | solution.py:199
  24.1 1.1 %collective-permute-done.7.refs_0_ = bf16[97,8,128]{2,1,0:T(8,128)(2,1)S(1)} collective-permute-done((bf16[97,8,128]{2,1,0:T(8,128)(2,1)S(1)}, bf16[97,8,128]{2,1,0:T(8,128)(2,1)S(1)}, u32[]{:S(2)}, u32[]{:S(2)}) %collective-permute-start.7) | collective-permute-done | bytes 198688 | tf_op jit(solution)/shard_map/ppermute | solution.py:176
  25.2 0.5 %send_scores.1 = bf16[136,768]{1,0:T(8,128)(2,1)S(1)} custom-call(bf16[256,768]{1,0:T(8,128)(2,1)S(1)} %get-tuple-element.16.unit_ref, f32[256,128]{1,0:T(8,128)S(1)} %get-tuple-element.17.side_ref, f32[256,128]{1,0:T(8,128)S(1)} %get-tuple-element.20.old_sums_ref, f32[256,768]{1,0:T(8,128)S(1)} %get-tuple-element.21.old_mixed_ref, ...), custom_call_target="tpu_custom_call" | custom-call | flops 5033164800 | bytes 983040 | tf_op jit(solution)/shard_map/send_scores/pallas_call | solution.py:209
  25.7 0.1 collective-permute-start.8
  25.8 0.5 %keep_scores.1 = (f32[128,128]{1,0:T(8,128)S(1)}, f32[128,768]{1,0:T(8,128)S(1)}) custom-call(bf16[256,768]{1,0:T(8,128)(2,1)S(1)} %get-tuple-element.16.unit_ref, f32[256,128]{1,0:T(8,128)S(1)} %get-tuple-element.17.side_ref, f32[256,128]{1,0:T(8,128)S(1)} %get-tuple-element.20.old_sums_ref, f32[256,768]{1,0:T(8,128)S(1)} %get-tuple-element.21.old_mixed_ref, ...), custom_call_target="tpu_custom_call" | custom-call | flops 5033164800 | bytes 983040 | tf_op jit(solution)/shard_map/keep_scores/pallas_call | solution.py:216
  26.3 0.9 %collective-permute-done.8.got_ref = bf16[136,768]{1,0:T(8,128)(2,1)S(1)} collective-permute-done((bf16[136,768]{1,0:T(8,128)(2,1)S(1)}, bf16[136,768]{1,0:T(8,128)(2,1)S(1)}, u32[]{:S(2)}, u32[]{:S(2)}) %collective-permute-start.8) | collective-permute-done | bytes 208928 | tf_op jit(solution)/shard_map/ppermute | solution.py:182
  27.2 1.0 %combine.1 = (f32[1,128]{1,0:T(1,128)}, f32[128,768]{1,0:T(8,128)}) custom-call(f32[128,128]{1,0:T(8,128)S(1)} %get-tuple-element.22.sums_ref, f32[128,768]{1,0:T(8,128)S(1)} %get-tuple-element.23.mixed_ref, bf16[136,768]{1,0:T(8,128)(2,1)S(1)} %collective-permute-done.8.got_ref), custom_call_target="tpu_custom_call" | custom-call | tf_op jit(solution)/shard_map/combine/pallas_call | solution.py:263
  (2 shorter events, 0.0 us)
Async XLA Ops:
  0.6 0.9 %copy-start = (bf16[128,768]{1,0:T(8,128)(2,1)S(1)}, bf16[128,768]{1,0:T(8,128)(2,1)}, u32[]{:S(2)}) copy-start(bf16[128,768]{1,0:T(8,128)(2,1)} %param.3) | copy-start | bytes 589828
  0.6 0.9 %copy-start.1 = (s32[128,1]{0,1:T(1,128)S(1)}, s32[128,1]{0,1:T(1,128)}, u32[]{:S(2)}) copy-start(s32[128,1]{0,1:T(1,128)} %param.4) | copy-start | bytes 1540
  0.7 0.9 %copy-start.2 = (s32[128]{0:T(128)S(1)}, s32[128]{0:T(128)}, u32[]{:S(2)}) copy-start(s32[128]{0:T(128)} %param.5) | copy-start | bytes 1540
  1.6 9.5 %collective-permute-start.1 = (bf16[97,8,128]{2,1,0:T(8,128)(2,1)S(1)}, bf16[97,8,128]{2,1,0:T(8,128)(2,1)S(1)}, u32[]{:S(2)}, u32[]{:S(2)}) collective-permute-start(bf16[97,8,128]{2,1,0:T(8,128)(2,1)S(1)} %pack.1.own_ref), channel_id=1, source_target_pairs={{0,8},{2,10},{8,12},{10,14},{12,4},{14,6},{4,0},{6,2},{1,9},{3,11}... | collective-permute-start | bytes 595976 | tf_op jit(solution)/shard_map/ppermute | solution.py:176
  5.7 6.4 %collective-permute-start.2 = (bf16[97,8,128]{2,1,0:T(8,128)(2,1)S(1)}, bf16[97,8,128]{2,1,0:T(8,128)(2,1)S(1)}, u32[]{:S(2)}, u32[]{:S(2)}) collective-permute-start(bf16[97,8,128]{2,1,0:T(8,128)(2,1)S(1)} %pack.1.own_ref), channel_id=1, source_target_pairs={{0,2},{2,0},{4,6},{6,4},{8,10},{10,8},{12,14},{14,12},{1,3},{3,1},... | collective-permute-start | bytes 595976 | tf_op jit(solution)/shard_map/ppermute | solution.py:179
  7.2 8.8 %collective-permute-start.4 = (bf16[97,8,128]{2,1,0:T(8,128)(2,1)S(1)}, bf16[97,8,128]{2,1,0:T(8,128)(2,1)S(1)}, u32[]{:S(2)}, u32[]{:S(2)}) collective-permute-start(bf16[97,8,128]{2,1,0:T(8,128)(2,1)S(1)} %pack.1.own_ref), channel_id=1, source_target_pairs={{0,4},{2,6},{8,0},{10,2},{12,8},{14,10},{4,12},{6,14},{1,5},{3,7},... | collective-permute-start | bytes 595976 | tf_op jit(solution)/shard_map/ppermute | solution.py:176
  12.1 5.7 %collective-permute-start.3 = (bf16[97,8,128]{2,1,0:T(8,128)(2,1)S(1)}, bf16[97,8,128]{2,1,0:T(8,128)(2,1)S(1)}, u32[]{:S(2)}, u32[]{:S(2)}) collective-permute-start(bf16[97,8,128]{2,1,0:T(8,128)(2,1)S(1)} %collective-permute-done.1.refs_1_), channel_id=1, source_target_pairs={{0,2},{2,0},{4,6},{6,4},{8,10},{10,8},{12,14},{14,12},{1,3},{3,1},... | collective-permute-start | bytes 595976 | tf_op jit(solution)/shard_map/ppermute | solution.py:179
  13.6 7.6 %collective-permute-start = (bf16[97,8,128]{2,1,0:T(8,128)(2,1)S(1)}, bf16[97,8,128]{2,1,0:T(8,128)(2,1)S(1)}, u32[]{:S(2)}, u32[]{:S(2)}) collective-permute-start(bf16[97,8,128]{2,1,0:T(8,128)(2,1)S(1)} %pack.1.own_ref), channel_id=1, source_target_pairs={{0,1},{1,0},{2,3},{3,2},{4,5},{5,4},{6,7},{7,6},{8,9},{9,8},{10,11... | collective-permute-start | bytes 595976 | tf_op jit(solution)/shard_map/ppermute | solution.py:182
  13.6 8.8 %collective-permute-start.5 = (bf16[97,8,128]{2,1,0:T(8,128)(2,1)S(1)}, bf16[97,8,128]{2,1,0:T(8,128)(2,1)S(1)}, u32[]{:S(2)}, u32[]{:S(2)}) collective-permute-start(bf16[97,8,128]{2,1,0:T(8,128)(2,1)S(1)} %collective-permute-done.1.refs_1_), channel_id=1, source_target_pairs={{0,8},{2,10},{8,12},{10,14},{12,4},{14,6},{4,0},{6,2},{1,9},{3,11}... | collective-permute-start | bytes 595976 | tf_op jit(solution)/shard_map/ppermute | solution.py:176
  16.0 7.1 %collective-permute-start.6 = (bf16[97,8,128]{2,1,0:T(8,128)(2,1)S(1)}, bf16[97,8,128]{2,1,0:T(8,128)(2,1)S(1)}, u32[]{:S(2)}, u32[]{:S(2)}) collective-permute-start(bf16[97,8,128]{2,1,0:T(8,128)(2,1)S(1)} %collective-permute-done.4.refs_0_), channel_id=1, source_target_pairs={{0,2},{2,0},{4,6},{6,4},{8,10},{10,8},{12,14},{14,12},{1,3},{3,1},... | collective-permute-start | bytes 595976 | tf_op jit(solution)/shard_map/ppermute | solution.py:179
  17.8 7.4 %collective-permute-start.7 = (bf16[97,8,128]{2,1,0:T(8,128)(2,1)S(1)}, bf16[97,8,128]{2,1,0:T(8,128)(2,1)S(1)}, u32[]{:S(2)}, u32[]{:S(2)}) collective-permute-start(bf16[97,8,128]{2,1,0:T(8,128)(2,1)S(1)} %collective-permute-done.3.refs_2_), channel_id=1, source_target_pairs={{0,8},{2,10},{8,12},{10,14},{12,4},{14,6},{4,0},{6,2},{1,9},{3,11}... | collective-permute-start | bytes 595976 | tf_op jit(solution)/shard_map/ppermute | solution.py:176
  25.7 1.5 %collective-permute-start.8 = (bf16[136,768]{1,0:T(8,128)(2,1)S(1)}, bf16[136,768]{1,0:T(8,128)(2,1)S(1)}, u32[]{:S(2)}, u32[]{:S(2)}) collective-permute-start(bf16[136,768]{1,0:T(8,128)(2,1)S(1)} %send_scores.1), channel_id=1, source_target_pairs={{0,1},{1,0},{2,3},{3,2},{4,5},{5,4},{6,7},{7,6},{8,9},{9,8},{10,11... | collective-permute-start | bytes 626696 | tf_op jit(solution)/shard_map/ppermute | solution.py:182

commit v30 on v25

--- a/solution.py
+++ b/solution.py
@@ -252,7 +252,7 @@
     other = swap(own)
     if rounds == 4:
         ahead = along(own, -1)
-        moved, beside, other = lax.optimization_barrier((moved, beside, other))
+        moved, beside = lax.optimization_barrier((moved, beside))
         sooner, later = two_ways(moved, 1), two_ways(moved, 0)
         ahead_beside = across(ahead)
         last = [two_ways(sooner, 0), ahead_beside]

time: 28.5 us -> 29 us (1.018)
  waiting for transfers between devices: 7.24 us -> 8.47 us
  starting transfers between devices: 15.2 us -> 14.5 us
    ppermute x2, starting transfers between devices: 3.74 us -> 2.97 us  [across(): return lax.ppermute(array, 'shard', [(at, at ^ 1) for at in range(shards)])]
    ppermute x2, waiting for transfers between devices: 4.27 us -> 5.02 us  [along(): return lax.ppermute(array, 'shard', pairs)]
    ppermute x2, waiting for transfers between devices: 1.96 us -> 2.69 us  [across(): return lax.ppermute(array, 'shard', [(at, at ^ 1) for at in range(shards)])]
  transfers between devices with their start and end apart: 9 -> 9, of which waited for: 7 -> 6; matrix products, arithmetic and copies ran while one was open for 0% -> 0% of each run, Pallas kernels for 9% -> 9%
where the time goes in v30:
time: 29 us; the launch traced here: 28.8 us
  starting transfers between devices  14.5 us (50%)
  waiting for transfers between devices  8.47 us (29%)
  Pallas kernels  4.27 us (15%)
  local copies, waits for them, and re-layouts  0.9 us (3%)
  between operations  0.71 us (2%)
    ppermute x3, starting transfers between devices, two_ways(): return lax.ppermute(array, ('shard', 'owner'), pairs)  6.22 us
    ppermute x2, waiting for transfers between devices, along(): return lax.ppermute(array, 'shard', pairs)  5.02 us
    ppermute x2, starting transfers between devices, along(): return lax.ppermute(array, 'shard', pairs)  4.09 us
    ppermute x2, starting transfers between devices, across(): return lax.ppermute(array, 'shard', [(at, at ^ 1) for at in range(shards)])  2.97 us
    ppermute x2, waiting for transfers between devices, across(): return lax.ppermute(array, 'shard', [(at, at ^ 1) for at in range(shards)])  2.69 us
    ppermute x2, starting transfers between devices, swap(): lax.ppermute(array, 'owner', [(at, lanes - 1 - at) for at in range(lanes)])  1.2 us
    pallas_call x1, Pallas kernels, first(): pl.pallas_call(first_kernel, out_shape=[shape(queries, width, dtype=bf16)...  1.19 us
    pallas_call x1, Pallas kernels, local(): pl.pallas_call(combine_kernel, out_shape=[shape(1, count), shape(count, w...  0.95 us
  transfers between devices with their start and end apart: 9, of which 6 were waited for; matrix products, arithmetic and copies ran while one was open for 0% of the time, Pallas kernels for 9%

profile of v30, /device:TPU:0, one launch (start us, length us, event | category | flops | bytes accessed | tf_op | source)
XLA Modules:
  0.0 28.8 jit_solution(1458237898723915563)
XLA Ops:
  0.6 0.0 copy-start
  0.6 0.0 copy-start.1
  0.7 0.0 copy-start.2
  0.7 0.9 %copy-done = bf16[128,768]{1,0:T(8,128)(2,1)S(1)} copy-done((bf16[128,768]{1,0:T(8,128)(2,1)S(1)}, bf16[128,768]{1,0:T(8,128)(2,1)}, u32[]{:S(2)}) %copy-start) | copy-done | bytes 196632
  1.6 0.0 copy-done.1
  1.6 0.0 copy-done.2
  1.6 4.1 %collective-permute-start.1 = (bf16[97,8,128]{2,1,0:T(8,128)(2,1)S(1)}, bf16[97,8,128]{2,1,0:T(8,128)(2,1)S(1)}, u32[]{:S(2)}, u32[]{:S(2)}) collective-permute-start(bf16[97,8,128]{2,1,0:T(8,128)(2,1)S(1)} %pack.1.own_ref), channel_id=1, source_target_pairs={{0,8},{2,10},{8,12},{10,14},{12,4},{14,6},{4,0},{6,2},{1,9},{3,11}... | collective-permute-start | bytes 595976 | tf_op jit(solution)/shard_map/ppermute | solution.py:176
  5.7 1.5 %collective-permute-start.2 = (bf16[97,8,128]{2,1,0:T(8,128)(2,1)S(1)}, bf16[97,8,128]{2,1,0:T(8,128)(2,1)S(1)}, u32[]{:S(2)}, u32[]{:S(2)}) collective-permute-start(bf16[97,8,128]{2,1,0:T(8,128)(2,1)S(1)} %pack.1.own_ref), channel_id=1, source_target_pairs={{0,2},{2,0},{4,6},{6,4},{8,10},{10,8},{12,14},{14,12},{1,3},{3,1},... | collective-permute-start | bytes 595976 | tf_op jit(solution)/shard_map/ppermute | solution.py:179
  7.2 0.0 collective-permute-start.4
  7.2 3.9 %collective-permute-done.1.refs_1_ = bf16[97,8,128]{2,1,0:T(8,128)(2,1)S(1)} collective-permute-done((bf16[97,8,128]{2,1,0:T(8,128)(2,1)S(1)}, bf16[97,8,128]{2,1,0:T(8,128)(2,1)S(1)}, u32[]{:S(2)}, u32[]{:S(2)}) %collective-permute-start.1) | collective-permute-done | bytes 198688 | tf_op jit(solution)/shard_map/ppermute | solution.py:176
  11.1 1.0 %collective-permute-done.2.refs_0_ = bf16[97,8,128]{2,1,0:T(8,128)(2,1)S(1)} collective-permute-done((bf16[97,8,128]{2,1,0:T(8,128)(2,1)S(1)}, bf16[97,8,128]{2,1,0:T(8,128)(2,1)S(1)}, u32[]{:S(2)}, u32[]{:S(2)}) %collective-permute-start.2) | collective-permute-done | bytes 198688 | tf_op jit(solution)/shard_map/ppermute | solution.py:179
  12.1 1.5 %collective-permute-start.3 = (bf16[97,8,128]{2,1,0:T(8,128)(2,1)S(1)}, bf16[97,8,128]{2,1,0:T(8,128)(2,1)S(1)}, u32[]{:S(2)}, u32[]{:S(2)}) collective-permute-start(bf16[97,8,128]{2,1,0:T(8,128)(2,1)S(1)} %collective-permute-done.1.refs_1_), channel_id=1, source_target_pairs={{0,2},{1,9},{2,0},{3,11},{8,10},{9,13},{10,8},{11,15},{12,14},{13,... | collective-permute-start | bytes 595976 | tf_op jit(solution)/shard_map/ppermute | solution.py:190
  13.6 0.0 collective-permute-start
  13.6 2.4 %collective-permute-start.5 = (bf16[97,8,128]{2,1,0:T(8,128)(2,1)S(1)}, bf16[97,8,128]{2,1,0:T(8,128)(2,1)S(1)}, u32[]{:S(2)}, u32[]{:S(2)}) collective-permute-start(bf16[97,8,128]{2,1,0:T(8,128)(2,1)S(1)} %collective-permute-done.1.refs_1_), channel_id=1, source_target_pairs={{0,8},{1,3},{2,10},{3,1},{8,12},{9,11},{10,14},{11,9},{12,4},{13,1... | collective-permute-start | bytes 595976 | tf_op jit(solution)/shard_map/ppermute | solution.py:190
  15.9 1.1 %collective-permute-done.4.refs_0_ = bf16[97,8,128]{2,1,0:T(8,128)(2,1)S(1)} collective-permute-done((bf16[97,8,128]{2,1,0:T(8,128)(2,1)S(1)}, bf16[97,8,128]{2,1,0:T(8,128)(2,1)S(1)}, u32[]{:S(2)}, u32[]{:S(2)}) %collective-permute-start.4) | collective-permute-done | bytes 198688 | tf_op jit(solution)/shard_map/ppermute | solution.py:176
  17.1 1.5 %collective-permute-start.7 = (bf16[97,8,128]{2,1,0:T(8,128)(2,1)S(1)}, bf16[97,8,128]{2,1,0:T(8,128)(2,1)S(1)}, u32[]{:S(2)}, u32[]{:S(2)}) collective-permute-start(bf16[97,8,128]{2,1,0:T(8,128)(2,1)S(1)} %collective-permute-done.4.refs_0_), channel_id=1, source_target_pairs={{0,2},{2,0},{4,6},{6,4},{8,10},{10,8},{12,14},{14,12},{1,3},{3,1},... | collective-permute-start | bytes 595976 | tf_op jit(solution)/shard_map/ppermute | solution.py:179
  18.6 0.3 %collective-permute-done.3.refs_2_ = bf16[97,8,128]{2,1,0:T(8,128)(2,1)S(1)} collective-permute-done((bf16[97,8,128]{2,1,0:T(8,128)(2,1)S(1)}, bf16[97,8,128]{2,1,0:T(8,128)(2,1)S(1)}, u32[]{:S(2)}, u32[]{:S(2)}) %collective-permute-start.3) | collective-permute-done | bytes 198688 | tf_op jit(solution)/shard_map/ppermute | solution.py:190
  18.9 2.4 %collective-permute-start.6 = (bf16[97,8,128]{2,1,0:T(8,128)(2,1)S(1)}, bf16[97,8,128]{2,1,0:T(8,128)(2,1)S(1)}, u32[]{:S(2)}, u32[]{:S(2)}) collective-permute-start(bf16[97,8,128]{2,1,0:T(8,128)(2,1)S(1)} %collective-permute-done.3.refs_2_), channel_id=1, source_target_pairs={{0,8},{1,3},{2,10},{3,1},{8,12},{9,11},{10,14},{11,9},{12,4},{13,1... | collective-permute-start | bytes 595976 | tf_op jit(solution)/shard_map/ppermute | solution.py:190
  21.2 0.0 collective-permute-done.other_ref
  21.2 1.2 %first_scores.1 = (bf16[256,768]{1,0:T(8,128)(2,1)S(1)}, f32[256,128]{1,0:T(8,128)S(1)}, f32[256,128]{1,0:T(8,128)S(1)}, f32[256,768]{1,0:T(8,128)S(1)}) custom-call(bf16[97,8,128]{2,1,0:T(8,128)(2,1)S(1)} %pack.1.own_ref, bf16[97,8,128]{2,1,0:T(8,128)(2,1)S(1)} %collective-permute-done.other_ref, bf16[97,8,128]{2,1,0:T(8,128)(2,1)S(1)} %collective-permute-done.2.refs_0_, ...), custom_call_target="tpu_custom_call" | custom-call | flops 40265318400 | bytes 2359296 | tf_op jit(solution)/shard_map/first_scores/pallas_call | solution.py:196
  22.4 0.0 collective-permute-done.5.refs_1_
  22.4 0.9 %more_scores.1 = (f32[256,128]{1,0:T(8,128)S(1)}, f32[256,768]{1,0:T(8,128)S(1)}) custom-call(bf16[256,768]{1,0:T(8,128)(2,1)S(1)} %get-tuple-element.16.unit_ref, f32[256,128]{1,0:T(8,128)S(1)} %get-tuple-element.17.side_ref, f32[256,128]{1,0:T(8,128)S(1)} %get-tuple-element.18.old_sums_ref, ...), custom_call_target="tpu_custom_call", output_to_operand_aliasing={{0}: (2, {}), {1}: (3, {})} | custom-call | flops 20132659200 | bytes 1966080 | tf_op jit(solution)/shard_map/more_scores/pallas_call | solution.py:210
  23.3 1.7 %collective-permute-done.7.refs_1_ = bf16[97,8,128]{2,1,0:T(8,128)(2,1)S(1)} collective-permute-done((bf16[97,8,128]{2,1,0:T(8,128)(2,1)S(1)}, bf16[97,8,128]{2,1,0:T(8,128)(2,1)S(1)}, u32[]{:S(2)}, u32[]{:S(2)}) %collective-permute-start.7) | collective-permute-done | bytes 198688 | tf_op jit(solution)/shard_map/ppermute | solution.py:179
  25.0 0.0 collective-permute-done.6.refs_0_
  25.0 0.6 %send_scores.1 = bf16[136,768]{1,0:T(8,128)(2,1)S(1)} custom-call(bf16[256,768]{1,0:T(8,128)(2,1)S(1)} %get-tuple-element.16.unit_ref, f32[256,128]{1,0:T(8,128)S(1)} %get-tuple-element.17.side_ref, f32[256,128]{1,0:T(8,128)S(1)} %get-tuple-element.20.old_sums_ref, f32[256,768]{1,0:T(8,128)S(1)} %get-tuple-element.21.old_mixed_ref, ...), custom_call_target="tpu_custom_call" | custom-call | flops 10066329600 | bytes 1179648 | tf_op jit(solution)/shard_map/send_scores/pallas_call | solution.py:220
  25.6 1.2 %collective-permute-start.8 = (bf16[136,768]{1,0:T(8,128)(2,1)S(1)}, bf16[136,768]{1,0:T(8,128)(2,1)S(1)}, u32[]{:S(2)}, u32[]{:S(2)}) collective-permute-start(bf16[136,768]{1,0:T(8,128)(2,1)S(1)} %send_scores.1), channel_id=1, source_target_pairs={{0,1},{1,0},{2,3},{3,2},{4,5},{5,4},{6,7},{7,6},{8,9},{9,8},{10,11... | collective-permute-start | bytes 626696 | tf_op jit(solution)/shard_map/ppermute | solution.py:193
  26.8 0.6 %keep_scores.1 = (f32[128,128]{1,0:T(8,128)S(1)}, f32[128,768]{1,0:T(8,128)S(1)}) custom-call(bf16[256,768]{1,0:T(8,128)(2,1)S(1)} %get-tuple-element.16.unit_ref, f32[256,128]{1,0:T(8,128)S(1)} %get-tuple-element.17.side_ref, f32[256,128]{1,0:T(8,128)S(1)} %get-tuple-element.20.old_sums_ref, f32[256,768]{1,0:T(8,128)S(1)} %get-tuple-element.21.old_mixed_ref, ...), custom_call_target="tpu_custom_call" | custom-call | flops 10066329600 | bytes 1179648 | tf_op jit(solution)/shard_map/keep_scores/pallas_call | solution.py:227
  27.4 0.5 %collective-permute-done.8.got_ref = bf16[136,768]{1,0:T(8,128)(2,1)S(1)} collective-permute-done((bf16[136,768]{1,0:T(8,128)(2,1)S(1)}, bf16[136,768]{1,0:T(8,128)(2,1)S(1)}, u32[]{:S(2)}, u32[]{:S(2)}) %collective-permute-start.8) | collective-permute-done | bytes 208928 | tf_op jit(solution)/shard_map/ppermute | solution.py:193
  27.9 1.0 %combine.1 = (f32[1,128]{1,0:T(1,128)}, f32[128,768]{1,0:T(8,128)}) custom-call(f32[128,128]{1,0:T(8,128)S(1)} %get-tuple-element.22.sums_ref, f32[128,768]{1,0:T(8,128)S(1)} %get-tuple-element.23.mixed_ref, bf16[136,768]{1,0:T(8,128)(2,1)S(1)} %collective-permute-done.8.got_ref), custom_call_target="tpu_custom_call" | custom-call | tf_op jit(solution)/shard_map/combine/pallas_call | solution.py:273
  (2 shorter events, 0.0 us)
Async XLA Ops:
  0.6 0.9 %copy-start = (bf16[128,768]{1,0:T(8,128)(2,1)S(1)}, bf16[128,768]{1,0:T(8,128)(2,1)}, u32[]{:S(2)}) copy-start(bf16[128,768]{1,0:T(8,128)(2,1)} %param.3) | copy-start | bytes 589828
  0.6 0.9 %copy-start.1 = (s32[128,1]{0,1:T(1,128)S(1)}, s32[128,1]{0,1:T(1,128)}, u32[]{:S(2)}) copy-start(s32[128,1]{0,1:T(1,128)} %param.4) | copy-start | bytes 1540
  0.7 0.9 %copy-start.2 = (s32[128]{0:T(128)S(1)}, s32[128]{0:T(128)}, u32[]{:S(2)}) copy-start(s32[128]{0:T(128)} %param.5) | copy-start | bytes 1540
  1.6 9.5 %collective-permute-start.1 = (bf16[97,8,128]{2,1,0:T(8,128)(2,1)S(1)}, bf16[97,8,128]{2,1,0:T(8,128)(2,1)S(1)}, u32[]{:S(2)}, u32[]{:S(2)}) collective-permute-start(bf16[97,8,128]{2,1,0:T(8,128)(2,1)S(1)} %pack.1.own_ref), channel_id=1, source_target_pairs={{0,8},{2,10},{8,12},{10,14},{12,4},{14,6},{4,0},{6,2},{1,9},{3,11}... | collective-permute-start | bytes 595976 | tf_op jit(solution)/shard_map/ppermute | solution.py:176
  5.7 6.4 %collective-permute-start.2 = (bf16[97,8,128]{2,1,0:T(8,128)(2,1)S(1)}, bf16[97,8,128]{2,1,0:T(8,128)(2,1)S(1)}, u32[]{:S(2)}, u32[]{:S(2)}) collective-permute-start(bf16[97,8,128]{2,1,0:T(8,128)(2,1)S(1)} %pack.1.own_ref), channel_id=1, source_target_pairs={{0,2},{2,0},{4,6},{6,4},{8,10},{10,8},{12,14},{14,12},{1,3},{3,1},... | collective-permute-start | bytes 595976 | tf_op jit(solution)/shard_map/ppermute | solution.py:179
  7.2 9.9 %collective-permute-start.4 = (bf16[97,8,128]{2,1,0:T(8,128)(2,1)S(1)}, bf16[97,8,128]{2,1,0:T(8,128)(2,1)S(1)}, u32[]{:S(2)}, u32[]{:S(2)}) collective-permute-start(bf16[97,8,128]{2,1,0:T(8,128)(2,1)S(1)} %pack.1.own_ref), channel_id=1, source_target_pairs={{0,4},{2,6},{8,0},{10,2},{12,8},{14,10},{4,12},{6,14},{1,5},{3,7},... | collective-permute-start | bytes 595976 | tf_op jit(solution)/shard_map/ppermute | solution.py:176
  12.1 6.8 %collective-permute-start.3 = (bf16[97,8,128]{2,1,0:T(8,128)(2,1)S(1)}, bf16[97,8,128]{2,1,0:T(8,128)(2,1)S(1)}, u32[]{:S(2)}, u32[]{:S(2)}) collective-permute-start(bf16[97,8,128]{2,1,0:T(8,128)(2,1)S(1)} %collective-permute-done.1.refs_1_), channel_id=1, source_target_pairs={{0,2},{1,9},{2,0},{3,11},{8,10},{9,13},{10,8},{11,15},{12,14},{13,... | collective-permute-start | bytes 595976 | tf_op jit(solution)/shard_map/ppermute | solution.py:190
  13.6 7.7 %collective-permute-start = (bf16[97,8,128]{2,1,0:T(8,128)(2,1)S(1)}, bf16[97,8,128]{2,1,0:T(8,128)(2,1)S(1)}, u32[]{:S(2)}, u32[]{:S(2)}) collective-permute-start(bf16[97,8,128]{2,1,0:T(8,128)(2,1)S(1)} %pack.1.own_ref), channel_id=1, source_target_pairs={{0,1},{1,0},{2,3},{3,2},{4,5},{5,4},{6,7},{7,6},{8,9},{9,8},{10,11... | collective-permute-start | bytes 595976 | tf_op jit(solution)/shard_map/ppermute | solution.py:193
  13.6 8.9 %collective-permute-start.5 = (bf16[97,8,128]{2,1,0:T(8,128)(2,1)S(1)}, bf16[97,8,128]{2,1,0:T(8,128)(2,1)S(1)}, u32[]{:S(2)}, u32[]{:S(2)}) collective-permute-start(bf16[97,8,128]{2,1,0:T(8,128)(2,1)S(1)} %collective-permute-done.1.refs_1_), channel_id=1, source_target_pairs={{0,8},{1,3},{2,10},{3,1},{8,12},{9,11},{10,14},{11,9},{12,4},{13,1... | collective-permute-start | bytes 595976 | tf_op jit(solution)/shard_map/ppermute | solution.py:190
  17.1 7.9 %collective-permute-start.7 = (bf16[97,8,128]{2,1,0:T(8,128)(2,1)S(1)}, bf16[97,8,128]{2,1,0:T(8,128)(2,1)S(1)}, u32[]{:S(2)}, u32[]{:S(2)}) collective-permute-start(bf16[97,8,128]{2,1,0:T(8,128)(2,1)S(1)} %collective-permute-done.4.refs_0_), channel_id=1, source_target_pairs={{0,2},{2,0},{4,6},{6,4},{8,10},{10,8},{12,14},{14,12},{1,3},{3,1},... | collective-permute-start | bytes 595976 | tf_op jit(solution)/shard_map/ppermute | solution.py:179
  18.9 6.1 %collective-permute-start.6 = (bf16[97,8,128]{2,1,0:T(8,128)(2,1)S(1)}, bf16[97,8,128]{2,1,0:T(8,128)(2,1)S(1)}, u32[]{:S(2)}, u32[]{:S(2)}) collective-permute-start(bf16[97,8,128]{2,1,0:T(8,128)(2,1)S(1)} %collective-permute-done.3.refs_2_), channel_id=1, source_target_pairs={{0,8},{1,3},{2,10},{3,1},{8,12},{9,11},{10,14},{11,9},{12,4},{13,1... | collective-permute-start | bytes 595976 | tf_op jit(solution)/shard_map/ppermute | solution.py:190
  25.6 2.3 %collective-permute-start.8 = (bf16[136,768]{1,0:T(8,128)(2,1)S(1)}, bf16[136,768]{1,0:T(8,128)(2,1)S(1)}, u32[]{:S(2)}, u32[]{:S(2)}) collective-permute-start(bf16[136,768]{1,0:T(8,128)(2,1)S(1)} %send_scores.1), channel_id=1, source_target_pairs={{0,1},{1,0},{2,3},{3,2},{4,5},{5,4},{6,7},{7,6},{8,9},{9,8},{10,11... | collective-permute-start | bytes 626696 | tf_op jit(solution)/shard_map/ppermute | solution.py:193

commit v31 on v29

--- a/solution.py
+++ b/solution.py
@@ -238,17 +238,19 @@
     )(pieces.reshape(tiles, SUB, LANE), cluster_id.reshape(1, count), priority.reshape(1, count), base)
 
     moved, beside = along(own, 1), across(own)
-    other = swap(own)
     if rounds == 4:
         ahead = along(own, -1)
         moved, beside = lax.optimization_barrier((moved, beside))
         opposite = along(moved, 1)
         moved_beside = across(moved)
+        packed, ahead = lax.optimization_barrier((own, ahead))
+        other = swap(packed)
         ahead_beside = across(ahead)
         last = [along(moved_beside, 1)]
         unit, side, sums, mixed = first(own, other, beside, moved, moved_beside)
         sums, mixed = more(unit, side, sums, mixed, ahead, opposite, ahead_beside)
     else:
+        other = swap(own)
         unit, side, sums, mixed = first(own, other, beside)
 
         def turn(at, state):

time: 28.3 us -> 30.7 us (1.085)
  waiting for transfers between devices: 7.87 us -> 13 us
  starting transfers between devices: 14.5 us -> 11.7 us
    ppermute x4, waiting for transfers between devices: 4.98 us -> 11 us  [along(): return lax.ppermute(array, 'shard', pairs)]
    ppermute x4, starting transfers between devices: 9.89 us -> 7.13 us  [along(): return lax.ppermute(array, 'shard', pairs)]
    ppermute x3, waiting for transfers between devices: 1.96 us -> 1.03 us  [across(): return lax.ppermute(array, 'shard', [(at, at ^ 1) for at in range(shards)])]
  transfers between devices with their start and end apart: 9 -> 9, of which waited for: 6 -> 6; matrix products, arithmetic and copies ran while one was open for 0% -> 0% of each run, Pallas kernels for 10% -> 9%
where the time goes in v31:
time: 30.7 us; the launch traced here: 30.6 us
  waiting for transfers between devices  13 us (42%)
  starting transfers between devices  11.7 us (38%)
  Pallas kernels  4.27 us (14%)
  local copies, waits for them, and re-layouts  0.9 us (3%)
  between operations  0.7 us (2%)
    ppermute x4, waiting for transfers between devices, along(): return lax.ppermute(array, 'shard', pairs)  11 us
    ppermute x4, starting transfers between devices, along(): return lax.ppermute(array, 'shard', pairs)  7.13 us
    ppermute x3, starting transfers between devices, across(): return lax.ppermute(array, 'shard', [(at, at ^ 1) for at in range(shards)])  4.48 us
    pallas_call x1, Pallas kernels, first(): pl.pallas_call(first_kernel, out_shape=[shape(queries, width, dtype=bf16)...  1.19 us
    pallas_call x1, Pallas kernels, more(): pl.pallas_call(more_kernel, out_shape=[shape(queries, 128), shape(queries...  1.06 us
    ppermute x3, waiting for transfers between devices, across(): return lax.ppermute(array, 'shard', [(at, at ^ 1) for at in range(shards)])  1.03 us
    pallas_call x1, Pallas kernels, local(): pl.pallas_call(combine_kernel, out_shape=[shape(1, count), shape(count, w...  0.95 us
    ppermute x2, waiting for transfers between devices, swap(): lax.ppermute(array, 'owner', [(at, lanes - 1 - at) for at in range(lanes)])  0.93 us
  transfers between devices with their start and end apart: 9, of which 6 were waited for; matrix products, arithmetic and copies ran while one was open for 0% of the time, Pallas kernels for 9%

profile of v31, /device:TPU:0, one launch (start us, length us, event | category | flops | bytes accessed | tf_op | source)
XLA Modules:
  0.0 30.6 jit_solution(13069781566490964298)
XLA Ops:
  0.6 0.0 copy-start
  0.6 0.0 copy-start.1
  0.7 0.0 copy-start.2
  0.7 0.9 %copy-done = bf16[128,768]{1,0:T(8,128)(2,1)S(1)} copy-done((bf16[128,768]{1,0:T(8,128)(2,1)S(1)}, bf16[128,768]{1,0:T(8,128)(2,1)}, u32[]{:S(2)}) %copy-start) | copy-done | bytes 196632
  1.6 0.0 copy-done.1
  1.6 0.0 copy-done.2
  1.6 4.1 %collective-permute-start.2 = (bf16[97,8,128]{2,1,0:T(8,128)(2,1)S(1)}, bf16[97,8,128]{2,1,0:T(8,128)(2,1)S(1)}, u32[]{:S(2)}, u32[]{:S(2)}) collective-permute-start(bf16[97,8,128]{2,1,0:T(8,128)(2,1)S(1)} %pack.1.own_ref), channel_id=1, source_target_pairs={{0,8},{2,10},{8,12},{10,14},{12,4},{14,6},{4,0},{6,2},{1,9},{3,11}... | collective-permute-start | bytes 595976 | tf_op jit(solution)/shard_map/ppermute | solution.py:176
  5.7 1.5 %collective-permute-start.3 = (bf16[97,8,128]{2,1,0:T(8,128)(2,1)S(1)}, bf16[97,8,128]{2,1,0:T(8,128)(2,1)S(1)}, u32[]{:S(2)}, u32[]{:S(2)}) collective-permute-start(bf16[97,8,128]{2,1,0:T(8,128)(2,1)S(1)} %pack.1.own_ref), channel_id=1, source_target_pairs={{0,2},{2,0},{4,6},{6,4},{8,10},{10,8},{12,14},{14,12},{1,3},{3,1},... | collective-permute-start | bytes 595976 | tf_op jit(solution)/shard_map/ppermute | solution.py:179
  7.2 0.0 collective-permute-start
  7.2 3.9 %collective-permute-done.2.refs_1_ = bf16[97,8,128]{2,1,0:T(8,128)(2,1)S(1)} collective-permute-done((bf16[97,8,128]{2,1,0:T(8,128)(2,1)S(1)}, bf16[97,8,128]{2,1,0:T(8,128)(2,1)S(1)}, u32[]{:S(2)}, u32[]{:S(2)}) %collective-permute-start.2) | collective-permute-done | bytes 198688 | tf_op jit(solution)/shard_map/ppermute | solution.py:176
  11.1 1.0 %collective-permute-done.3.refs_0_ = bf16[97,8,128]{2,1,0:T(8,128)(2,1)S(1)} collective-permute-done((bf16[97,8,128]{2,1,0:T(8,128)(2,1)S(1)}, bf16[97,8,128]{2,1,0:T(8,128)(2,1)S(1)}, u32[]{:S(2)}, u32[]{:S(2)}) %collective-permute-start.3) | collective-permute-done | bytes 198688 | tf_op jit(solution)/shard_map/ppermute | solution.py:179
  12.1 1.5 %collective-permute-start.4 = (bf16[97,8,128]{2,1,0:T(8,128)(2,1)S(1)}, bf16[97,8,128]{2,1,0:T(8,128)(2,1)S(1)}, u32[]{:S(2)}, u32[]{:S(2)}) collective-permute-start(bf16[97,8,128]{2,1,0:T(8,128)(2,1)S(1)} %collective-permute-done.2.refs_1_), channel_id=1, source_target_pairs={{0,2},{2,0},{4,6},{6,4},{8,10},{10,8},{12,14},{14,12},{1,3},{3,1},... | collective-permute-start | bytes 595976 | tf_op jit(solution)/shard_map/ppermute | solution.py:179
  13.6 2.4 %collective-permute-done.refs_0_ = bf16[97,8,128]{2,1,0:T(8,128)(2,1)S(1)} collective-permute-done((bf16[97,8,128]{2,1,0:T(8,128)(2,1)S(1)}, bf16[97,8,128]{2,1,0:T(8,128)(2,1)S(1)}, u32[]{:S(2)}, u32[]{:S(2)}) %collective-permute-start) | collective-permute-done | bytes 198688 | tf_op jit(solution)/shard_map/ppermute | solution.py:176
  15.9 0.0 collective-permute-start.1
  15.9 0.6 %collective-permute-start.5 = (bf16[97,8,128]{2,1,0:T(8,128)(2,1)S(1)}, bf16[97,8,128]{2,1,0:T(8,128)(2,1)S(1)}, u32[]{:S(2)}, u32[]{:S(2)}) collective-permute-start(bf16[97,8,128]{2,1,0:T(8,128)(2,1)S(1)} %collective-permute-done.2.refs_1_), channel_id=1, source_target_pairs={{0,8},{2,10},{8,12},{10,14},{12,4},{14,6},{4,0},{6,2},{1,9},{3,11}... | collective-permute-start | bytes 595976 | tf_op jit(solution)/shard_map/ppermute | solution.py:176
  16.5 1.5 %collective-permute-start.6 = (bf16[97,8,128]{2,1,0:T(8,128)(2,1)S(1)}, bf16[97,8,128]{2,1,0:T(8,128)(2,1)S(1)}, u32[]{:S(2)}, u32[]{:S(2)}) collective-permute-start(bf16[97,8,128]{2,1,0:T(8,128)(2,1)S(1)} %collective-permute-done.refs_0_), channel_id=1, source_target_pairs={{0,2},{2,0},{4,6},{6,4},{8,10},{10,8},{12,14},{14,12},{1,3},{3,1},... | collective-permute-start | bytes 595976 | tf_op jit(solution)/shard_map/ppermute | solution.py:179
  18.0 0.0 collective-permute-done.4.refs_2_
  18.0 2.5 %collective-permute-start.7 = (bf16[97,8,128]{2,1,0:T(8,128)(2,1)S(1)}, bf16[97,8,128]{2,1,0:T(8,128)(2,1)S(1)}, u32[]{:S(2)}, u32[]{:S(2)}) collective-permute-start(bf16[97,8,128]{2,1,0:T(8,128)(2,1)S(1)} %collective-permute-done.4.refs_2_), channel_id=1, source_target_pairs={{0,8},{2,10},{8,12},{10,14},{12,4},{14,6},{4,0},{6,2},{1,9},{3,11}... | collective-permute-start | bytes 595976 | tf_op jit(solution)/shard_map/ppermute | solution.py:176
  20.5 0.0 collective-permute-done.1.other_ref
  20.5 1.2 %first_scores.1 = (bf16[256,768]{1,0:T(8,128)(2,1)S(1)}, f32[256,128]{1,0:T(8,128)S(1)}, f32[256,128]{1,0:T(8,128)S(1)}, f32[256,768]{1,0:T(8,128)S(1)}) custom-call(bf16[97,8,128]{2,1,0:T(8,128)(2,1)S(1)} %pack.1.own_ref, bf16[97,8,128]{2,1,0:T(8,128)(2,1)S(1)} %collective-permute-done.1.other_ref, bf16[97,8,128]{2,1,0:T(8,128)(2,1)S(1)} %collective-permute-done.3.refs_0_, ...), custom_call_target="tpu_custom_call" | custom-call | flops 40265318400 | bytes 2359296 | tf_op jit(solution)/shard_map/first_scores/pallas_call | solution.py:185
  21.7 2.0 %collective-permute-done.5.refs_1_ = bf16[97,8,128]{2,1,0:T(8,128)(2,1)S(1)} collective-permute-done((bf16[97,8,128]{2,1,0:T(8,128)(2,1)S(1)}, bf16[97,8,128]{2,1,0:T(8,128)(2,1)S(1)}, u32[]{:S(2)}, u32[]{:S(2)}) %collective-permute-start.5) | collective-permute-done | bytes 198688 | tf_op jit(solution)/shard_map/ppermute | solution.py:176
  23.7 0.0 collective-permute-done.6.refs_2_
  23.7 1.1 %more_scores.1 = (f32[256,128]{1,0:T(8,128)S(1)}, f32[256,768]{1,0:T(8,128)S(1)}) custom-call(bf16[256,768]{1,0:T(8,128)(2,1)S(1)} %get-tuple-element.19.unit_ref, f32[256,128]{1,0:T(8,128)S(1)} %get-tuple-element.20.side_ref, f32[256,128]{1,0:T(8,128)S(1)} %get-tuple-element.21.old_sums_ref, ...), custom_call_target="tpu_custom_call", output_to_operand_aliasing={{0}: (2, {}), {1}: (3, {})} | custom-call | flops 30198988800 | bytes 2162688 | tf_op jit(solution)/shard_map/more_scores/pallas_call | solution.py:199
  24.8 2.8 %collective-permute-done.7.refs_0_ = bf16[97,8,128]{2,1,0:T(8,128)(2,1)S(1)} collective-permute-done((bf16[97,8,128]{2,1,0:T(8,128)(2,1)S(1)}, bf16[97,8,128]{2,1,0:T(8,128)(2,1)S(1)}, u32[]{:S(2)}, u32[]{:S(2)}) %collective-permute-start.7) | collective-permute-done | bytes 198688 | tf_op jit(solution)/shard_map/ppermute | solution.py:176
  27.6 0.5 %send_scores.1 = bf16[136,768]{1,0:T(8,128)(2,1)S(1)} custom-call(bf16[256,768]{1,0:T(8,128)(2,1)S(1)} %get-tuple-element.19.unit_ref, f32[256,128]{1,0:T(8,128)S(1)} %get-tuple-element.20.side_ref, f32[256,128]{1,0:T(8,128)S(1)} %get-tuple-element.24.old_sums_ref, f32[256,768]{1,0:T(8,128)S(1)} %get-tuple-element.25.old_mixed_ref, ...), custom_call_target="tpu_custom_call" | custom-call | flops 5033164800 | bytes 983040 | tf_op jit(solution)/shard_map/send_scores/pallas_call | solution.py:209
  28.1 0.1 collective-permute-start.8
  28.2 0.5 %keep_scores.1 = (f32[128,128]{1,0:T(8,128)S(1)}, f32[128,768]{1,0:T(8,128)S(1)}) custom-call(bf16[256,768]{1,0:T(8,128)(2,1)S(1)} %get-tuple-element.19.unit_ref, f32[256,128]{1,0:T(8,128)S(1)} %get-tuple-element.20.side_ref, f32[256,128]{1,0:T(8,128)S(1)} %get-tuple-element.24.old_sums_ref, f32[256,768]{1,0:T(8,128)S(1)} %get-tuple-element.25.old_mixed_ref, ...), custom_call_target="tpu_custom_call" | custom-call | flops 5033164800 | bytes 983040 | tf_op jit(solution)/shard_map/keep_scores/pallas_call | solution.py:216
  28.7 0.9 %collective-permute-done.8.got_ref = bf16[136,768]{1,0:T(8,128)(2,1)S(1)} collective-permute-done((bf16[136,768]{1,0:T(8,128)(2,1)S(1)}, bf16[136,768]{1,0:T(8,128)(2,1)S(1)}, u32[]{:S(2)}, u32[]{:S(2)}) %collective-permute-start.8) | collective-permute-done | bytes 208928 | tf_op jit(solution)/shard_map/ppermute | solution.py:182
  29.6 1.0 %combine.1 = (f32[1,128]{1,0:T(1,128)}, f32[128,768]{1,0:T(8,128)}) custom-call(f32[128,128]{1,0:T(8,128)S(1)} %get-tuple-element.26.sums_ref, f32[128,768]{1,0:T(8,128)S(1)} %get-tuple-element.27.mixed_ref, bf16[136,768]{1,0:T(8,128)(2,1)S(1)} %collective-permute-done.8.got_ref), custom_call_target="tpu_custom_call" | custom-call | tf_op jit(solution)/shard_map/combine/pallas_call | solution.py:265
  (2 shorter events, 0.0 us)
Async XLA Ops:
  0.6 0.9 %copy-start = (bf16[128,768]{1,0:T(8,128)(2,1)S(1)}, bf16[128,768]{1,0:T(8,128)(2,1)}, u32[]{:S(2)}) copy-start(bf16[128,768]{1,0:T(8,128)(2,1)} %param.3) | copy-start | bytes 589828
  0.6 0.9 %copy-start.1 = (s32[128,1]{0,1:T(1,128)S(1)}, s32[128,1]{0,1:T(1,128)}, u32[]{:S(2)}) copy-start(s32[128,1]{0,1:T(1,128)} %param.4) | copy-start | bytes 1540
  0.7 0.9 %copy-start.2 = (s32[128]{0:T(128)S(1)}, s32[128]{0:T(128)}, u32[]{:S(2)}) copy-start(s32[128]{0:T(128)} %param.5) | copy-start | bytes 1540
  1.6 9.5 %collective-permute-start.2 = (bf16[97,8,128]{2,1,0:T(8,128)(2,1)S(1)}, bf16[97,8,128]{2,1,0:T(8,128)(2,1)S(1)}, u32[]{:S(2)}, u32[]{:S(2)}) collective-permute-start(bf16[97,8,128]{2,1,0:T(8,128)(2,1)S(1)} %pack.1.own_ref), channel_id=1, source_target_pairs={{0,8},{2,10},{8,12},{10,14},{12,4},{14,6},{4,0},{6,2},{1,9},{3,11}... | collective-permute-start | bytes 595976 | tf_op jit(solution)/shard_map/ppermute | solution.py:176
  5.7 6.4 %collective-permute-start.3 = (bf16[97,8,128]{2,1,0:T(8,128)(2,1)S(1)}, bf16[97,8,128]{2,1,0:T(8,128)(2,1)S(1)}, u32[]{:S(2)}, u32[]{:S(2)}) collective-permute-start(bf16[97,8,128]{2,1,0:T(8,128)(2,1)S(1)} %pack.1.own_ref), channel_id=1, source_target_pairs={{0,2},{2,0},{4,6},{6,4},{8,10},{10,8},{12,14},{14,12},{1,3},{3,1},... | collective-permute-start | bytes 595976 | tf_op jit(solution)/shard_map/ppermute | solution.py:179
  7.2 8.8 %collective-permute-start = (bf16[97,8,128]{2,1,0:T(8,128)(2,1)S(1)}, bf16[97,8,128]{2,1,0:T(8,128)(2,1)S(1)}, u32[]{:S(2)}, u32[]{:S(2)}) collective-permute-start(bf16[97,8,128]{2,1,0:T(8,128)(2,1)S(1)} %pack.1.own_ref), channel_id=1, source_target_pairs={{0,4},{2,6},{8,0},{10,2},{12,8},{14,10},{4,12},{6,14},{1,5},{3,7},... | collective-permute-start | bytes 595976 | tf_op jit(solution)/shard_map/ppermute | solution.py:176
  12.1 5.9 %collective-permute-start.4 = (bf16[97,8,128]{2,1,0:T(8,128)(2,1)S(1)}, bf16[97,8,128]{2,1,0:T(8,128)(2,1)S(1)}, u32[]{:S(2)}, u32[]{:S(2)}) collective-permute-start(bf16[97,8,128]{2,1,0:T(8,128)(2,1)S(1)} %collective-permute-done.2.refs_1_), channel_id=1, source_target_pairs={{0,2},{2,0},{4,6},{6,4},{8,10},{10,8},{12,14},{14,12},{1,3},{3,1},... | collective-permute-start | bytes 595976 | tf_op jit(solution)/shard_map/ppermute | solution.py:179
  15.9 4.6 %collective-permute-start.1 = (bf16[97,8,128]{2,1,0:T(8,128)(2,1)S(1)}, bf16[97,8,128]{2,1,0:T(8,128)(2,1)S(1)}, u32[]{:S(2)}, u32[]{:S(2)}) collective-permute-start(bf16[97,8,128]{2,1,0:T(8,128)(2,1)S(1)} %pack.1.own_ref), channel_id=1, source_target_pairs={{0,1},{1,0},{2,3},{3,2},{4,5},{5,4},{6,7},{7,6},{8,9},{9,8},{10,11... | collective-permute-start | bytes 595976 | tf_op jit(solution)/shard_map/ppermute | solution.py:182
  15.9 7.7 %collective-permute-start.5 = (bf16[97,8,128]{2,1,0:T(8,128)(2,1)S(1)}, bf16[97,8,128]{2,1,0:T(8,128)(2,1)S(1)}, u32[]{:S(2)}, u32[]{:S(2)}) collective-permute-start(bf16[97,8,128]{2,1,0:T(8,128)(2,1)S(1)} %collective-permute-done.2.refs_1_), channel_id=1, source_target_pairs={{0,8},{2,10},{8,12},{10,14},{12,4},{14,6},{4,0},{6,2},{1,9},{3,11}... | collective-permute-start | bytes 595976 | tf_op jit(solution)/shard_map/ppermute | solution.py:176
  16.5 7.2 %collective-permute-start.6 = (bf16[97,8,128]{2,1,0:T(8,128)(2,1)S(1)}, bf16[97,8,128]{2,1,0:T(8,128)(2,1)S(1)}, u32[]{:S(2)}, u32[]{:S(2)}) collective-permute-start(bf16[97,8,128]{2,1,0:T(8,128)(2,1)S(1)} %collective-permute-done.refs_0_), channel_id=1, source_target_pairs={{0,2},{2,0},{4,6},{6,4},{8,10},{10,8},{12,14},{14,12},{1,3},{3,1},... | collective-permute-start | bytes 595976 | tf_op jit(solution)/shard_map/ppermute | solution.py:179
  18.0 9.5 %collective-permute-start.7 = (bf16[97,8,128]{2,1,0:T(8,128)(2,1)S(1)}, bf16[97,8,128]{2,1,0:T(8,128)(2,1)S(1)}, u32[]{:S(2)}, u32[]{:S(2)}) collective-permute-start(bf16[97,8,128]{2,1,0:T(8,128)(2,1)S(1)} %collective-permute-done.4.refs_2_), channel_id=1, source_target_pairs={{0,8},{2,10},{8,12},{10,14},{12,4},{14,6},{4,0},{6,2},{1,9},{3,11}... | collective-permute-start | bytes 595976 | tf_op jit(solution)/shard_map/ppermute | solution.py:176
  28.1 1.5 %collective-permute-start.8 = (bf16[136,768]{1,0:T(8,128)(2,1)S(1)}, bf16[136,768]{1,0:T(8,128)(2,1)S(1)}, u32[]{:S(2)}, u32[]{:S(2)}) collective-permute-start(bf16[136,768]{1,0:T(8,128)(2,1)S(1)} %send_scores.1), channel_id=1, source_target_pairs={{0,1},{1,0},{2,3},{3,2},{4,5},{5,4},{6,7},{7,6},{8,9},{9,8},{10,11... | collective-permute-start | bytes 626696 | tf_op jit(solution)/shard_map/ppermute | solution.py:182

commit v32 on v23

--- a/solution.py
+++ b/solution.py
@@ -244,10 +244,8 @@
         moved, beside, other = lax.optimization_barrier((moved, beside, other))
         opposite = along(moved, 1)
         moved_beside = across(moved)
-        moved_beside, ahead = lax.optimization_barrier((moved_beside, ahead))
-        last_ = along(moved_beside, 1)
         ahead_beside = across(ahead)
-        last = [last_, ahead_beside]
+        last = [along(moved_beside, 1), ahead_beside]
         unit, side, sums, mixed = first(own, other, beside, moved, moved_beside)
         sums, mixed = more(unit, side, sums, mixed, ahead, opposite)
     else:

time: 29 us -> 28.4 us (0.979)
  waiting for transfers between devices: 9.72 us -> 7.8 us
  starting transfers between devices: 13.3 us -> 14.6 us
    ppermute x3, waiting for transfers between devices: 3.91 us -> 1.29 us  [across(): return lax.ppermute(array, 'shard', [(at, at ^ 1) for at in range(shards)])]
    ppermute x3, starting transfers between devices: 4.47 us -> 5.29 us  [across(): return lax.ppermute(array, 'shard', [(at, at ^ 1) for at in range(shards)])]
    ppermute x4, waiting for transfers between devices: 5 us -> 5.68 us  [along(): return lax.ppermute(array, 'shard', pairs)]
    ppermute x4, starting transfers between devices: 8.75 us -> 9.19 us  [along(): return lax.ppermute(array, 'shard', pairs)]
  transfers between devices with their start and end apart: 9 -> 9, of which waited for: 7 -> 6; matrix products, arithmetic and copies ran while one was open for 0% -> 0% of each run, Pallas kernels for 9% -> 9%
where the time goes in v32:
time: 28.4 us; the launch traced here: 28.2 us
  starting transfers between devices  14.6 us (51%)
  waiting for transfers between devices  7.8 us (27%)
  Pallas kernels  4.26 us (15%)
  local copies, waits for them, and re-layouts  0.9 us (3%)
  between operations  0.71 us (2%)
    ppermute x4, starting transfers between devices, along(): return lax.ppermute(array, 'shard', pairs)  9.19 us
    ppermute x4, waiting for transfers between devices, along(): return lax.ppermute(array, 'shard', pairs)  5.68 us
    ppermute x3, starting transfers between devices, across(): return lax.ppermute(array, 'shard', [(at, at ^ 1) for at in range(shards)])  5.29 us
    ppermute x3, waiting for transfers between devices, across(): return lax.ppermute(array, 'shard', [(at, at ^ 1) for at in range(shards)])  1.29 us
    pallas_call x1, Pallas kernels, first(): pl.pallas_call(first_kernel, out_shape=[shape(queries, width, dtype=bf16)...  1.18 us
    pallas_call x1, Pallas kernels, local(): pl.pallas_call(combine_kernel, out_shape=[shape(1, count), shape(count, w...  0.95 us
    unnamed x6, local copies, waits for them, and re-layouts  0.9 us
    pallas_call x1, Pallas kernels, more(): pl.pallas_call(more_kernel, out_shape=[shape(queries, 128), shape(queries...  0.86 us
  transfers between devices with their start and end apart: 9, of which 6 were waited for; matrix products, arithmetic and copies ran while one was open for 0% of the time, Pallas kernels for 9%

profile of v32, /device:TPU:0, one launch (start us, length us, event | category | flops | bytes accessed | tf_op | source)
XLA Modules:
  0.0 28.2 jit_solution(9967204121980237523)
XLA Ops:
  0.6 0.0 copy-start
  0.6 0.0 copy-start.1
  0.7 0.0 copy-start.2
  0.7 0.9 %copy-done = bf16[128,768]{1,0:T(8,128)(2,1)S(1)} copy-done((bf16[128,768]{1,0:T(8,128)(2,1)S(1)}, bf16[128,768]{1,0:T(8,128)(2,1)}, u32[]{:S(2)}) %copy-start) | copy-done | bytes 196632
  1.6 0.0 copy-done.1
  1.6 0.0 copy-done.2
  1.6 4.1 %collective-permute-start = (bf16[97,8,128]{2,1,0:T(8,128)(2,1)S(1)}, bf16[97,8,128]{2,1,0:T(8,128)(2,1)S(1)}, u32[]{:S(2)}, u32[]{:S(2)}) collective-permute-start(bf16[97,8,128]{2,1,0:T(8,128)(2,1)S(1)} %pack.1.own_ref), channel_id=1, source_target_pairs={{0,8},{2,10},{8,12},{10,14},{12,4},{14,6},{4,0},{6,2},{1,9},{3,11}... | collective-permute-start | bytes 595976 | tf_op jit(solution)/shard_map/ppermute | solution.py:176
  5.7 1.5 %collective-permute-start.1 = (bf16[97,8,128]{2,1,0:T(8,128)(2,1)S(1)}, bf16[97,8,128]{2,1,0:T(8,128)(2,1)S(1)}, u32[]{:S(2)}, u32[]{:S(2)}) collective-permute-start(bf16[97,8,128]{2,1,0:T(8,128)(2,1)S(1)} %pack.1.own_ref), channel_id=1, source_target_pairs={{0,2},{2,0},{4,6},{6,4},{8,10},{10,8},{12,14},{14,12},{1,3},{3,1},... | collective-permute-start | bytes 595976 | tf_op jit(solution)/shard_map/ppermute | solution.py:179
  7.2 0.0 collective-permute-start.2
  7.2 0.0 collective-permute-start.4
  7.2 3.9 %collective-permute-done.refs_1_ = bf16[97,8,128]{2,1,0:T(8,128)(2,1)S(1)} collective-permute-done((bf16[97,8,128]{2,1,0:T(8,128)(2,1)S(1)}, bf16[97,8,128]{2,1,0:T(8,128)(2,1)S(1)}, u32[]{:S(2)}, u32[]{:S(2)}) %collective-permute-start) | collective-permute-done | bytes 198688 | tf_op jit(solution)/shard_map/ppermute | solution.py:176
  11.0 1.1 %collective-permute-done.1.refs_0_ = bf16[97,8,128]{2,1,0:T(8,128)(2,1)S(1)} collective-permute-done((bf16[97,8,128]{2,1,0:T(8,128)(2,1)S(1)}, bf16[97,8,128]{2,1,0:T(8,128)(2,1)S(1)}, u32[]{:S(2)}, u32[]{:S(2)}) %collective-permute-start.1) | collective-permute-done | bytes 198688 | tf_op jit(solution)/shard_map/ppermute | solution.py:179
  12.1 0.0 collective-permute-done.2.other_ref
  12.1 1.5 %collective-permute-start.3 = (bf16[97,8,128]{2,1,0:T(8,128)(2,1)S(1)}, bf16[97,8,128]{2,1,0:T(8,128)(2,1)S(1)}, u32[]{:S(2)}, u32[]{:S(2)}) collective-permute-start(bf16[97,8,128]{2,1,0:T(8,128)(2,1)S(1)} %collective-permute-done.refs_1_), channel_id=1, source_target_pairs={{0,2},{2,0},{4,6},{6,4},{8,10},{10,8},{12,14},{14,12},{1,3},{3,1},... | collective-permute-start | bytes 595976 | tf_op jit(solution)/shard_map/ppermute | solution.py:179
  13.6 2.3 %collective-permute-start.5 = (bf16[97,8,128]{2,1,0:T(8,128)(2,1)S(1)}, bf16[97,8,128]{2,1,0:T(8,128)(2,1)S(1)}, u32[]{:S(2)}, u32[]{:S(2)}) collective-permute-start(bf16[97,8,128]{2,1,0:T(8,128)(2,1)S(1)} %collective-permute-done.refs_1_), channel_id=1, source_target_pairs={{0,8},{2,10},{8,12},{10,14},{12,4},{14,6},{4,0},{6,2},{1,9},{3,11}... | collective-permute-start | bytes 595976 | tf_op jit(solution)/shard_map/ppermute | solution.py:176
  15.9 0.4 %collective-permute-done.4.refs_0_ = bf16[97,8,128]{2,1,0:T(8,128)(2,1)S(1)} collective-permute-done((bf16[97,8,128]{2,1,0:T(8,128)(2,1)S(1)}, bf16[97,8,128]{2,1,0:T(8,128)(2,1)S(1)}, u32[]{:S(2)}, u32[]{:S(2)}) %collective-permute-start.4) | collective-permute-done | bytes 198688 | tf_op jit(solution)/shard_map/ppermute | solution.py:176
  16.3 2.3 %collective-permute-start.7 = (bf16[97,8,128]{2,1,0:T(8,128)(2,1)S(1)}, bf16[97,8,128]{2,1,0:T(8,128)(2,1)S(1)}, u32[]{:S(2)}, u32[]{:S(2)}) collective-permute-start(bf16[97,8,128]{2,1,0:T(8,128)(2,1)S(1)} %collective-permute-done.4.refs_0_), channel_id=1, source_target_pairs={{0,2},{2,0},{4,6},{6,4},{8,10},{10,8},{12,14},{14,12},{1,3},{3,1},... | collective-permute-start | bytes 595976 | tf_op jit(solution)/shard_map/ppermute | solution.py:179
  18.6 0.0 collective-permute-done.3.refs_2_
  18.6 2.8 %collective-permute-start.6 = (bf16[97,8,128]{2,1,0:T(8,128)(2,1)S(1)}, bf16[97,8,128]{2,1,0:T(8,128)(2,1)S(1)}, u32[]{:S(2)}, u32[]{:S(2)}) collective-permute-start(bf16[97,8,128]{2,1,0:T(8,128)(2,1)S(1)} %collective-permute-done.3.refs_2_), channel_id=1, source_target_pairs={{0,8},{2,10},{8,12},{10,14},{12,4},{14,6},{4,0},{6,2},{1,9},{3,11}... | collective-permute-start | bytes 595976 | tf_op jit(solution)/shard_map/ppermute | solution.py:176
  21.3 1.2 %first_scores.1 = (bf16[256,768]{1,0:T(8,128)(2,1)S(1)}, f32[256,128]{1,0:T(8,128)S(1)}, f32[256,128]{1,0:T(8,128)S(1)}, f32[256,768]{1,0:T(8,128)S(1)}) custom-call(bf16[97,8,128]{2,1,0:T(8,128)(2,1)S(1)} %pack.1.own_ref, bf16[97,8,128]{2,1,0:T(8,128)(2,1)S(1)} %collective-permute-done.2.other_ref, bf16[97,8,128]{2,1,0:T(8,128)(2,1)S(1)} %collective-permute-done.1.refs_0_, ...), custom_call_target="tpu_custom_call" | custom-call | flops 40265318400 | bytes 2359296 | tf_op jit(solution)/shard_map/first_scores/pallas_call | solution.py:185
  22.5 0.0 collective-permute-done.5.refs_1_
  22.5 0.9 %more_scores.1 = (f32[256,128]{1,0:T(8,128)S(1)}, f32[256,768]{1,0:T(8,128)S(1)}) custom-call(bf16[256,768]{1,0:T(8,128)(2,1)S(1)} %get-tuple-element.18.unit_ref, f32[256,128]{1,0:T(8,128)S(1)} %get-tuple-element.19.side_ref, f32[256,128]{1,0:T(8,128)S(1)} %get-tuple-element.20.old_sums_ref, ...), custom_call_target="tpu_custom_call", output_to_operand_aliasing={{0}: (2, {}), {1}: (3, {})} | custom-call | flops 20132659200 | bytes 1966080 | tf_op jit(solution)/shard_map/more_scores/pallas_call | solution.py:199
  23.4 0.2 collective-permute-done.7.refs_1_
  23.7 1.5 %collective-permute-done.6.refs_0_ = bf16[97,8,128]{2,1,0:T(8,128)(2,1)S(1)} collective-permute-done((bf16[97,8,128]{2,1,0:T(8,128)(2,1)S(1)}, bf16[97,8,128]{2,1,0:T(8,128)(2,1)S(1)}, u32[]{:S(2)}, u32[]{:S(2)}) %collective-permute-start.6) | collective-permute-done | bytes 198688 | tf_op jit(solution)/shard_map/ppermute | solution.py:176
  25.1 0.6 %send_scores.1 = bf16[136,768]{1,0:T(8,128)(2,1)S(1)} custom-call(bf16[256,768]{1,0:T(8,128)(2,1)S(1)} %get-tuple-element.18.unit_ref, f32[256,128]{1,0:T(8,128)S(1)} %get-tuple-element.19.side_ref, f32[256,128]{1,0:T(8,128)S(1)} %get-tuple-element.22.old_sums_ref, f32[256,768]{1,0:T(8,128)S(1)} %get-tuple-element.23.old_mixed_ref, ...), custom_call_target="tpu_custom_call" | custom-call | flops 10066329600 | bytes 1179648 | tf_op jit(solution)/shard_map/send_scores/pallas_call | solution.py:209
  25.7 0.1 collective-permute-start.8
  25.8 0.6 %keep_scores.1 = (f32[128,128]{1,0:T(8,128)S(1)}, f32[128,768]{1,0:T(8,128)S(1)}) custom-call(bf16[256,768]{1,0:T(8,128)(2,1)S(1)} %get-tuple-element.18.unit_ref, f32[256,128]{1,0:T(8,128)S(1)} %get-tuple-element.19.side_ref, f32[256,128]{1,0:T(8,128)S(1)} %get-tuple-element.22.old_sums_ref, f32[256,768]{1,0:T(8,128)S(1)} %get-tuple-element.23.old_mixed_ref, ...), custom_call_target="tpu_custom_call" | custom-call | flops 10066329600 | bytes 1179648 | tf_op jit(solution)/shard_map/keep_scores/pallas_call | solution.py:216
  26.5 0.8 %collective-permute-done.8.got_ref = bf16[136,768]{1,0:T(8,128)(2,1)S(1)} collective-permute-done((bf16[136,768]{1,0:T(8,128)(2,1)S(1)}, bf16[136,768]{1,0:T(8,128)(2,1)S(1)}, u32[]{:S(2)}, u32[]{:S(2)}) %collective-permute-start.8) | collective-permute-done | bytes 208928 | tf_op jit(solution)/shard_map/ppermute | solution.py:182
  27.3 1.0 %combine.1 = (f32[1,128]{1,0:T(1,128)}, f32[128,768]{1,0:T(8,128)}) custom-call(f32[128,128]{1,0:T(8,128)S(1)} %get-tuple-element.24.sums_ref, f32[128,768]{1,0:T(8,128)S(1)} %get-tuple-element.25.mixed_ref, bf16[136,768]{1,0:T(8,128)(2,1)S(1)} %collective-permute-done.8.got_ref), custom_call_target="tpu_custom_call" | custom-call | tf_op jit(solution)/shard_map/combine/pallas_call | solution.py:263
  (2 shorter events, 0.0 us)
Async XLA Ops:
  0.6 0.9 %copy-start = (bf16[128,768]{1,0:T(8,128)(2,1)S(1)}, bf16[128,768]{1,0:T(8,128)(2,1)}, u32[]{:S(2)}) copy-start(bf16[128,768]{1,0:T(8,128)(2,1)} %param.3) | copy-start | bytes 589828
  0.6 0.9 %copy-start.1 = (s32[128,1]{0,1:T(1,128)S(1)}, s32[128,1]{0,1:T(1,128)}, u32[]{:S(2)}) copy-start(s32[128,1]{0,1:T(1,128)} %param.4) | copy-start | bytes 1540
  0.7 0.9 %copy-start.2 = (s32[128]{0:T(128)S(1)}, s32[128]{0:T(128)}, u32[]{:S(2)}) copy-start(s32[128]{0:T(128)} %param.5) | copy-start | bytes 1540
  1.6 9.4 %collective-permute-start = (bf16[97,8,128]{2,1,0:T(8,128)(2,1)S(1)}, bf16[97,8,128]{2,1,0:T(8,128)(2,1)S(1)}, u32[]{:S(2)}, u32[]{:S(2)}) collective-permute-start(bf16[97,8,128]{2,1,0:T(8,128)(2,1)S(1)} %pack.1.own_ref), channel_id=1, source_target_pairs={{0,8},{2,10},{8,12},{10,14},{12,4},{14,6},{4,0},{6,2},{1,9},{3,11}... | collective-permute-start | bytes 595976 | tf_op jit(solution)/shard_map/ppermute | solution.py:176
  5.7 6.4 %collective-permute-start.1 = (bf16[97,8,128]{2,1,0:T(8,128)(2,1)S(1)}, bf16[97,8,128]{2,1,0:T(8,128)(2,1)S(1)}, u32[]{:S(2)}, u32[]{:S(2)}) collective-permute-start(bf16[97,8,128]{2,1,0:T(8,128)(2,1)S(1)} %pack.1.own_ref), channel_id=1, source_target_pairs={{0,2},{2,0},{4,6},{6,4},{8,10},{10,8},{12,14},{14,12},{1,3},{3,1},... | collective-permute-start | bytes 595976 | tf_op jit(solution)/shard_map/ppermute | solution.py:179
  7.2 4.9 %collective-permute-start.2 = (bf16[97,8,128]{2,1,0:T(8,128)(2,1)S(1)}, bf16[97,8,128]{2,1,0:T(8,128)(2,1)S(1)}, u32[]{:S(2)}, u32[]{:S(2)}) collective-permute-start(bf16[97,8,128]{2,1,0:T(8,128)(2,1)S(1)} %pack.1.own_ref), channel_id=1, source_target_pairs={{0,1},{1,0},{2,3},{3,2},{4,5},{5,4},{6,7},{7,6},{8,9},{9,8},{10,11... | collective-permute-start | bytes 595976 | tf_op jit(solution)/shard_map/ppermute | solution.py:182
  7.2 9.1 %collective-permute-start.4 = (bf16[97,8,128]{2,1,0:T(8,128)(2,1)S(1)}, bf16[97,8,128]{2,1,0:T(8,128)(2,1)S(1)}, u32[]{:S(2)}, u32[]{:S(2)}) collective-permute-start(bf16[97,8,128]{2,1,0:T(8,128)(2,1)S(1)} %pack.1.own_ref), channel_id=1, source_target_pairs={{0,4},{2,6},{8,0},{10,2},{12,8},{14,10},{4,12},{6,14},{1,5},{3,7},... | collective-permute-start | bytes 595976 | tf_op jit(solution)/shard_map/ppermute | solution.py:176
  12.1 6.5 %collective-permute-start.3 = (bf16[97,8,128]{2,1,0:T(8,128)(2,1)S(1)}, bf16[97,8,128]{2,1,0:T(8,128)(2,1)S(1)}, u32[]{:S(2)}, u32[]{:S(2)}) collective-permute-start(bf16[97,8,128]{2,1,0:T(8,128)(2,1)S(1)} %collective-permute-done.refs_1_), channel_id=1, source_target_pairs={{0,2},{2,0},{4,6},{6,4},{8,10},{10,8},{12,14},{14,12},{1,3},{3,1},... | collective-permute-start | bytes 595976 | tf_op jit(solution)/shard_map/ppermute | solution.py:179
  13.6 9.0 %collective-permute-start.5 = (bf16[97,8,128]{2,1,0:T(8,128)(2,1)S(1)}, bf16[97,8,128]{2,1,0:T(8,128)(2,1)S(1)}, u32[]{:S(2)}, u32[]{:S(2)}) collective-permute-start(bf16[97,8,128]{2,1,0:T(8,128)(2,1)S(1)} %collective-permute-done.refs_1_), channel_id=1, source_target_pairs={{0,8},{2,10},{8,12},{10,14},{12,4},{14,6},{4,0},{6,2},{1,9},{3,11}... | collective-permute-start | bytes 595976 | tf_op jit(solution)/shard_map/ppermute | solution.py:176
  16.3 7.4 %collective-permute-start.7 = (bf16[97,8,128]{2,1,0:T(8,128)(2,1)S(1)}, bf16[97,8,128]{2,1,0:T(8,128)(2,1)S(1)}, u32[]{:S(2)}, u32[]{:S(2)}) collective-permute-start(bf16[97,8,128]{2,1,0:T(8,128)(2,1)S(1)} %collective-permute-done.4.refs_0_), channel_id=1, source_target_pairs={{0,2},{2,0},{4,6},{6,4},{8,10},{10,8},{12,14},{14,12},{1,3},{3,1},... | collective-permute-start | bytes 595976 | tf_op jit(solution)/shard_map/ppermute | solution.py:179
  18.6 6.5 %collective-permute-start.6 = (bf16[97,8,128]{2,1,0:T(8,128)(2,1)S(1)}, bf16[97,8,128]{2,1,0:T(8,128)(2,1)S(1)}, u32[]{:S(2)}, u32[]{:S(2)}) collective-permute-start(bf16[97,8,128]{2,1,0:T(8,128)(2,1)S(1)} %collective-permute-done.3.refs_2_), channel_id=1, source_target_pairs={{0,8},{2,10},{8,12},{10,14},{12,4},{14,6},{4,0},{6,2},{1,9},{3,11}... | collective-permute-start | bytes 595976 | tf_op jit(solution)/shard_map/ppermute | solution.py:176
  25.7 1.5 %collective-permute-start.8 = (bf16[136,768]{1,0:T(8,128)(2,1)S(1)}, bf16[136,768]{1,0:T(8,128)(2,1)S(1)}, u32[]{:S(2)}, u32[]{:S(2)}) collective-permute-start(bf16[136,768]{1,0:T(8,128)(2,1)S(1)} %send_scores.1), channel_id=1, source_target_pairs={{0,1},{1,0},{2,3},{3,2},{4,5},{5,4},{6,7},{7,6},{8,9},{9,8},{10,11... | collective-permute-start | bytes 626696 | tf_op jit(solution)/shard_map/ppermute | solution.py:182

commit v33 on v32

--- a/solution.py
+++ b/solution.py
@@ -241,7 +241,7 @@
     other = swap(own)
     if rounds == 4:
         ahead = along(own, -1)
-        moved, beside, other = lax.optimization_barrier((moved, beside, other))
+        moved, beside = lax.optimization_barrier((moved, beside))
         opposite = along(moved, 1)
         moved_beside = across(moved)
         ahead_beside = across(ahead)

time: 28.4 us -> 28.4 us (level)
    ppermute x3, starting transfers between devices: 5.29 us -> 4.48 us  [across(): return lax.ppermute(array, 'shard', [(at, at ^ 1) for at in range(shards)])]
    ppermute x4, starting transfers between devices: 9.19 us -> 9.89 us  [along(): return lax.ppermute(array, 'shard', pairs)]
  transfers between devices with their start and end apart: 9 -> 9, of which waited for: 6 -> 5; matrix products, arithmetic and copies ran while one was open for 0% -> 0% of each run, Pallas kernels for 9% -> 9%
where the time goes in v33:
time: 28.4 us; the launch traced here: 28.3 us
  starting transfers between devices  14.5 us (51%)
  waiting for transfers between devices  7.95 us (28%)
  Pallas kernels  4.27 us (15%)
  local copies, waits for them, and re-layouts  0.9 us (3%)
  between operations  0.72 us (3%)
    ppermute x4, starting transfers between devices, along(): return lax.ppermute(array, 'shard', pairs)  9.89 us
    ppermute x4, waiting for transfers between devices, along(): return lax.ppermute(array, 'shard', pairs)  5.78 us
    ppermute x3, starting transfers between devices, across(): return lax.ppermute(array, 'shard', [(at, at ^ 1) for at in range(shards)])  4.48 us
    ppermute x3, waiting for transfers between devices, across(): return lax.ppermute(array, 'shard', [(at, at ^ 1) for at in range(shards)])  1.35 us
    pallas_call x1, Pallas kernels, first(): pl.pallas_call(first_kernel, out_shape=[shape(queries, width, dtype=bf16)...  1.19 us
    pallas_call x1, Pallas kernels, local(): pl.pallas_call(combine_kernel, out_shape=[shape(1, count), shape(count, w...  0.95 us
    unnamed x6, local copies, waits for them, and re-layouts  0.9 us
    pallas_call x1, Pallas kernels, more(): pl.pallas_call(more_kernel, out_shape=[shape(queries, 128), shape(queries...  0.86 us
  transfers between devices with their start and end apart: 9, of which 5 were waited for; matrix products, arithmetic and copies ran while one was open for 0% of the time, Pallas kernels for 9%

profile of v33, /device:TPU:0, one launch (start us, length us, event | category | flops | bytes accessed | tf_op | source)
XLA Modules:
  0.0 28.3 jit_solution(18272821385118584228)
XLA Ops:
  0.6 0.0 copy-start
  0.6 0.0 copy-start.1
  0.7 0.0 copy-start.2
  0.7 0.9 %copy-done = bf16[128,768]{1,0:T(8,128)(2,1)S(1)} copy-done((bf16[128,768]{1,0:T(8,128)(2,1)S(1)}, bf16[128,768]{1,0:T(8,128)(2,1)}, u32[]{:S(2)}) %copy-start) | copy-done | bytes 196632
  1.6 0.0 copy-done.1
  1.6 0.0 copy-done.2
  1.6 4.1 %collective-permute-start.1 = (bf16[97,8,128]{2,1,0:T(8,128)(2,1)S(1)}, bf16[97,8,128]{2,1,0:T(8,128)(2,1)S(1)}, u32[]{:S(2)}, u32[]{:S(2)}) collective-permute-start(bf16[97,8,128]{2,1,0:T(8,128)(2,1)S(1)} %pack.1.own_ref), channel_id=1, source_target_pairs={{0,8},{2,10},{8,12},{10,14},{12,4},{14,6},{4,0},{6,2},{1,9},{3,11}... | collective-permute-start | bytes 595976 | tf_op jit(solution)/shard_map/ppermute | solution.py:176
  5.7 1.5 %collective-permute-start.2 = (bf16[97,8,128]{2,1,0:T(8,128)(2,1)S(1)}, bf16[97,8,128]{2,1,0:T(8,128)(2,1)S(1)}, u32[]{:S(2)}, u32[]{:S(2)}) collective-permute-start(bf16[97,8,128]{2,1,0:T(8,128)(2,1)S(1)} %pack.1.own_ref), channel_id=1, source_target_pairs={{0,2},{2,0},{4,6},{6,4},{8,10},{10,8},{12,14},{14,12},{1,3},{3,1},... | collective-permute-start | bytes 595976 | tf_op jit(solution)/shard_map/ppermute | solution.py:179
  7.2 0.0 collective-permute-start.4
  7.2 3.9 %collective-permute-done.1.refs_1_ = bf16[97,8,128]{2,1,0:T(8,128)(2,1)S(1)} collective-permute-done((bf16[97,8,128]{2,1,0:T(8,128)(2,1)S(1)}, bf16[97,8,128]{2,1,0:T(8,128)(2,1)S(1)}, u32[]{:S(2)}, u32[]{:S(2)}) %collective-permute-start.1) | collective-permute-done | bytes 198688 | tf_op jit(solution)/shard_map/ppermute | solution.py:176
  11.1 1.0 %collective-permute-done.2.refs_0_ = bf16[97,8,128]{2,1,0:T(8,128)(2,1)S(1)} collective-permute-done((bf16[97,8,128]{2,1,0:T(8,128)(2,1)S(1)}, bf16[97,8,128]{2,1,0:T(8,128)(2,1)S(1)}, u32[]{:S(2)}, u32[]{:S(2)}) %collective-permute-start.2) | collective-permute-done | bytes 198688 | tf_op jit(solution)/shard_map/ppermute | solution.py:179
  12.1 1.5 %collective-permute-start.3 = (bf16[97,8,128]{2,1,0:T(8,128)(2,1)S(1)}, bf16[97,8,128]{2,1,0:T(8,128)(2,1)S(1)}, u32[]{:S(2)}, u32[]{:S(2)}) collective-permute-start(bf16[97,8,128]{2,1,0:T(8,128)(2,1)S(1)} %collective-permute-done.1.refs_1_), channel_id=1, source_target_pairs={{0,2},{2,0},{4,6},{6,4},{8,10},{10,8},{12,14},{14,12},{1,3},{3,1},... | collective-permute-start | bytes 595976 | tf_op jit(solution)/shard_map/ppermute | solution.py:179
  13.6 0.0 collective-permute-start
  13.6 2.4 %collective-permute-start.5 = (bf16[97,8,128]{2,1,0:T(8,128)(2,1)S(1)}, bf16[97,8,128]{2,1,0:T(8,128)(2,1)S(1)}, u32[]{:S(2)}, u32[]{:S(2)}) collective-permute-start(bf16[97,8,128]{2,1,0:T(8,128)(2,1)S(1)} %collective-permute-done.1.refs_1_), channel_id=1, source_target_pairs={{0,8},{2,10},{8,12},{10,14},{12,4},{14,6},{4,0},{6,2},{1,9},{3,11}... | collective-permute-start | bytes 595976 | tf_op jit(solution)/shard_map/ppermute | solution.py:176
  15.9 0.0 collective-permute-done.4.refs_0_
  16.0 1.5 %collective-permute-start.7 = (bf16[97,8,128]{2,1,0:T(8,128)(2,1)S(1)}, bf16[97,8,128]{2,1,0:T(8,128)(2,1)S(1)}, u32[]{:S(2)}, u32[]{:S(2)}) collective-permute-start(bf16[97,8,128]{2,1,0:T(8,128)(2,1)S(1)} %collective-permute-done.4.refs_0_), channel_id=1, source_target_pairs={{0,2},{2,0},{4,6},{6,4},{8,10},{10,8},{12,14},{14,12},{1,3},{3,1},... | collective-permute-start | bytes 595976 | tf_op jit(solution)/shard_map/ppermute | solution.py:179
  17.5 0.3 %collective-permute-done.3.refs_2_ = bf16[97,8,128]{2,1,0:T(8,128)(2,1)S(1)} collective-permute-done((bf16[97,8,128]{2,1,0:T(8,128)(2,1)S(1)}, bf16[97,8,128]{2,1,0:T(8,128)(2,1)S(1)}, u32[]{:S(2)}, u32[]{:S(2)}) %collective-permute-start.3) | collective-permute-done | bytes 198688 | tf_op jit(solution)/shard_map/ppermute | solution.py:179
  17.8 3.4 %collective-permute-start.6 = (bf16[97,8,128]{2,1,0:T(8,128)(2,1)S(1)}, bf16[97,8,128]{2,1,0:T(8,128)(2,1)S(1)}, u32[]{:S(2)}, u32[]{:S(2)}) collective-permute-start(bf16[97,8,128]{2,1,0:T(8,128)(2,1)S(1)} %collective-permute-done.3.refs_2_), channel_id=1, source_target_pairs={{0,8},{2,10},{8,12},{10,14},{12,4},{14,6},{4,0},{6,2},{1,9},{3,11}... | collective-permute-start | bytes 595976 | tf_op jit(solution)/shard_map/ppermute | solution.py:176
  21.2 0.0 collective-permute-done.other_ref
  21.2 1.2 %first_scores.1 = (bf16[256,768]{1,0:T(8,128)(2,1)S(1)}, f32[256,128]{1,0:T(8,128)S(1)}, f32[256,128]{1,0:T(8,128)S(1)}, f32[256,768]{1,0:T(8,128)S(1)}) custom-call(bf16[97,8,128]{2,1,0:T(8,128)(2,1)S(1)} %pack.1.own_ref, bf16[97,8,128]{2,1,0:T(8,128)(2,1)S(1)} %collective-permute-done.other_ref, bf16[97,8,128]{2,1,0:T(8,128)(2,1)S(1)} %collective-permute-done.2.refs_0_, ...), custom_call_target="tpu_custom_call" | custom-call | flops 40265318400 | bytes 2359296 | tf_op jit(solution)/shard_map/first_scores/pallas_call | solution.py:185
  22.4 0.0 collective-permute-done.5.refs_1_
  22.4 0.9 %more_scores.1 = (f32[256,128]{1,0:T(8,128)S(1)}, f32[256,768]{1,0:T(8,128)S(1)}) custom-call(bf16[256,768]{1,0:T(8,128)(2,1)S(1)} %get-tuple-element.16.unit_ref, f32[256,128]{1,0:T(8,128)S(1)} %get-tuple-element.17.side_ref, f32[256,128]{1,0:T(8,128)S(1)} %get-tuple-element.18.old_sums_ref, ...), custom_call_target="tpu_custom_call", output_to_operand_aliasing={{0}: (2, {}), {1}: (3, {})} | custom-call | flops 20132659200 | bytes 1966080 | tf_op jit(solution)/shard_map/more_scores/pallas_call | solution.py:199
  23.3 0.0 collective-permute-done.7.refs_1_
  23.3 1.9 %collective-permute-done.6.refs_0_ = bf16[97,8,128]{2,1,0:T(8,128)(2,1)S(1)} collective-permute-done((bf16[97,8,128]{2,1,0:T(8,128)(2,1)S(1)}, bf16[97,8,128]{2,1,0:T(8,128)(2,1)S(1)}, u32[]{:S(2)}, u32[]{:S(2)}) %collective-permute-start.6) | collective-permute-done | bytes 198688 | tf_op jit(solution)/shard_map/ppermute | solution.py:176
  25.2 0.6 %send_scores.1 = bf16[136,768]{1,0:T(8,128)(2,1)S(1)} custom-call(bf16[256,768]{1,0:T(8,128)(2,1)S(1)} %get-tuple-element.16.unit_ref, f32[256,128]{1,0:T(8,128)S(1)} %get-tuple-element.17.side_ref, f32[256,128]{1,0:T(8,128)S(1)} %get-tuple-element.20.old_sums_ref, f32[256,768]{1,0:T(8,128)S(1)} %get-tuple-element.21.old_mixed_ref, ...), custom_call_target="tpu_custom_call" | custom-call | flops 10066329600 | bytes 1179648 | tf_op jit(solution)/shard_map/send_scores/pallas_call | solution.py:209
  25.8 0.1 collective-permute-start.8
  25.9 0.6 %keep_scores.1 = (f32[128,128]{1,0:T(8,128)S(1)}, f32[128,768]{1,0:T(8,128)S(1)}) custom-call(bf16[256,768]{1,0:T(8,128)(2,1)S(1)} %get-tuple-element.16.unit_ref, f32[256,128]{1,0:T(8,128)S(1)} %get-tuple-element.17.side_ref, f32[256,128]{1,0:T(8,128)S(1)} %get-tuple-element.20.old_sums_ref, f32[256,768]{1,0:T(8,128)S(1)} %get-tuple-element.21.old_mixed_ref, ...), custom_call_target="tpu_custom_call" | custom-call | flops 10066329600 | bytes 1179648 | tf_op jit(solution)/shard_map/keep_scores/pallas_call | solution.py:216
  26.5 0.8 %collective-permute-done.8.got_ref = bf16[136,768]{1,0:T(8,128)(2,1)S(1)} collective-permute-done((bf16[136,768]{1,0:T(8,128)(2,1)S(1)}, bf16[136,768]{1,0:T(8,128)(2,1)S(1)}, u32[]{:S(2)}, u32[]{:S(2)}) %collective-permute-start.8) | collective-permute-done | bytes 208928 | tf_op jit(solution)/shard_map/ppermute | solution.py:182
  27.3 1.0 %combine.1 = (f32[1,128]{1,0:T(1,128)}, f32[128,768]{1,0:T(8,128)}) custom-call(f32[128,128]{1,0:T(8,128)S(1)} %get-tuple-element.22.sums_ref, f32[128,768]{1,0:T(8,128)S(1)} %get-tuple-element.23.mixed_ref, bf16[136,768]{1,0:T(8,128)(2,1)S(1)} %collective-permute-done.8.got_ref), custom_call_target="tpu_custom_call" | custom-call | tf_op jit(solution)/shard_map/combine/pallas_call | solution.py:263
  (2 shorter events, 0.0 us)
Async XLA Ops:
  0.6 0.9 %copy-start = (bf16[128,768]{1,0:T(8,128)(2,1)S(1)}, bf16[128,768]{1,0:T(8,128)(2,1)}, u32[]{:S(2)}) copy-start(bf16[128,768]{1,0:T(8,128)(2,1)} %param.3) | copy-start | bytes 589828
  0.6 0.9 %copy-start.1 = (s32[128,1]{0,1:T(1,128)S(1)}, s32[128,1]{0,1:T(1,128)}, u32[]{:S(2)}) copy-start(s32[128,1]{0,1:T(1,128)} %param.4) | copy-start | bytes 1540
  0.7 0.9 %copy-start.2 = (s32[128]{0:T(128)S(1)}, s32[128]{0:T(128)}, u32[]{:S(2)}) copy-start(s32[128]{0:T(128)} %param.5) | copy-start | bytes 1540
  1.6 9.5 %collective-permute-start.1 = (bf16[97,8,128]{2,1,0:T(8,128)(2,1)S(1)}, bf16[97,8,128]{2,1,0:T(8,128)(2,1)S(1)}, u32[]{:S(2)}, u32[]{:S(2)}) collective-permute-start(bf16[97,8,128]{2,1,0:T(8,128)(2,1)S(1)} %pack.1.own_ref), channel_id=1, source_target_pairs={{0,8},{2,10},{8,12},{10,14},{12,4},{14,6},{4,0},{6,2},{1,9},{3,11}... | collective-permute-start | bytes 595976 | tf_op jit(solution)/shard_map/ppermute | solution.py:176
  5.7 6.4 %collective-permute-start.2 = (bf16[97,8,128]{2,1,0:T(8,128)(2,1)S(1)}, bf16[97,8,128]{2,1,0:T(8,128)(2,1)S(1)}, u32[]{:S(2)}, u32[]{:S(2)}) collective-permute-start(bf16[97,8,128]{2,1,0:T(8,128)(2,1)S(1)} %pack.1.own_ref), channel_id=1, source_target_pairs={{0,2},{2,0},{4,6},{6,4},{8,10},{10,8},{12,14},{14,12},{1,3},{3,1},... | collective-permute-start | bytes 595976 | tf_op jit(solution)/shard_map/ppermute | solution.py:179
  7.2 8.8 %collective-permute-start.4 = (bf16[97,8,128]{2,1,0:T(8,128)(2,1)S(1)}, bf16[97,8,128]{2,1,0:T(8,128)(2,1)S(1)}, u32[]{:S(2)}, u32[]{:S(2)}) collective-permute-start(bf16[97,8,128]{2,1,0:T(8,128)(2,1)S(1)} %pack.1.own_ref), channel_id=1, source_target_pairs={{0,4},{2,6},{8,0},{10,2},{12,8},{14,10},{4,12},{6,14},{1,5},{3,7},... | collective-permute-start | bytes 595976 | tf_op jit(solution)/shard_map/ppermute | solution.py:176
  12.1 5.7 %collective-permute-start.3 = (bf16[97,8,128]{2,1,0:T(8,128)(2,1)S(1)}, bf16[97,8,128]{2,1,0:T(8,128)(2,1)S(1)}, u32[]{:S(2)}, u32[]{:S(2)}) collective-permute-start(bf16[97,8,128]{2,1,0:T(8,128)(2,1)S(1)} %collective-permute-done.1.refs_1_), channel_id=1, source_target_pairs={{0,2},{2,0},{4,6},{6,4},{8,10},{10,8},{12,14},{14,12},{1,3},{3,1},... | collective-permute-start | bytes 595976 | tf_op jit(solution)/shard_map/ppermute | solution.py:179
  13.6 7.6 %collective-permute-start = (bf16[97,8,128]{2,1,0:T(8,128)(2,1)S(1)}, bf16[97,8,128]{2,1,0:T(8,128)(2,1)S(1)}, u32[]{:S(2)}, u32[]{:S(2)}) collective-permute-start(bf16[97,8,128]{2,1,0:T(8,128)(2,1)S(1)} %pack.1.own_ref), channel_id=1, source_target_pairs={{0,1},{1,0},{2,3},{3,2},{4,5},{5,4},{6,7},{7,6},{8,9},{9,8},{10,11... | collective-permute-start | bytes 595976 | tf_op jit(solution)/shard_map/ppermute | solution.py:182
  13.6 8.8 %collective-permute-start.5 = (bf16[97,8,128]{2,1,0:T(8,128)(2,1)S(1)}, bf16[97,8,128]{2,1,0:T(8,128)(2,1)S(1)}, u32[]{:S(2)}, u32[]{:S(2)}) collective-permute-start(bf16[97,8,128]{2,1,0:T(8,128)(2,1)S(1)} %collective-permute-done.1.refs_1_), channel_id=1, source_target_pairs={{0,8},{2,10},{8,12},{10,14},{12,4},{14,6},{4,0},{6,2},{1,9},{3,11}... | collective-permute-start | bytes 595976 | tf_op jit(solution)/shard_map/ppermute | solution.py:176
  16.0 7.3 %collective-permute-start.7 = (bf16[97,8,128]{2,1,0:T(8,128)(2,1)S(1)}, bf16[97,8,128]{2,1,0:T(8,128)(2,1)S(1)}, u32[]{:S(2)}, u32[]{:S(2)}) collective-permute-start(bf16[97,8,128]{2,1,0:T(8,128)(2,1)S(1)} %collective-permute-done.4.refs_0_), channel_id=1, source_target_pairs={{0,2},{2,0},{4,6},{6,4},{8,10},{10,8},{12,14},{14,12},{1,3},{3,1},... | collective-permute-start | bytes 595976 | tf_op jit(solution)/shard_map/ppermute | solution.py:179
  17.8 7.4 %collective-permute-start.6 = (bf16[97,8,128]{2,1,0:T(8,128)(2,1)S(1)}, bf16[97,8,128]{2,1,0:T(8,128)(2,1)S(1)}, u32[]{:S(2)}, u32[]{:S(2)}) collective-permute-start(bf16[97,8,128]{2,1,0:T(8,128)(2,1)S(1)} %collective-permute-done.3.refs_2_), channel_id=1, source_target_pairs={{0,8},{2,10},{8,12},{10,14},{12,4},{14,6},{4,0},{6,2},{1,9},{3,11}... | collective-permute-start | bytes 595976 | tf_op jit(solution)/shard_map/ppermute | solution.py:176
  25.8 1.5 %collective-permute-start.8 = (bf16[136,768]{1,0:T(8,128)(2,1)S(1)}, bf16[136,768]{1,0:T(8,128)(2,1)S(1)}, u32[]{:S(2)}, u32[]{:S(2)}) collective-permute-start(bf16[136,768]{1,0:T(8,128)(2,1)S(1)} %send_scores.1), channel_id=1, source_target_pairs={{0,1},{1,0},{2,3},{3,2},{4,5},{5,4},{6,7},{7,6},{8,9},{9,8},{10,11... | collective-permute-start | bytes 626696 | tf_op jit(solution)/shard_map/ppermute | solution.py:182

commit v34 on v29

--- a/solution.py
+++ b/solution.py
@@ -241,7 +241,7 @@
     other = swap(own)
     if rounds == 4:
         ahead = along(own, -1)
-        moved, beside = lax.optimization_barrier((moved, beside))
+        beside, moved = lax.optimization_barrier((beside, moved))
         opposite = along(moved, 1)
         moved_beside = across(moved)
         ahead_beside = across(ahead)

time: 28.3 us -> 30.1 us (1.064)
  starting transfers between devices: 14.5 us -> 15.8 us
  waiting for transfers between devices: 7.87 us -> 8.22 us
    ppermute x4, starting transfers between devices: 9.89 us -> 11.4 us  [along(): return lax.ppermute(array, 'shard', pairs)]
    ppermute x3, waiting for transfers between devices: 1.96 us -> 2.63 us  [across(): return lax.ppermute(array, 'shard', [(at, at ^ 1) for at in range(shards)])]
    ppermute x4, waiting for transfers between devices: 4.98 us -> 4.66 us  [along(): return lax.ppermute(array, 'shard', pairs)]
  transfers between devices with their start and end apart: 9 -> 9, of which waited for: 6 -> 6; matrix products, arithmetic and copies ran while one was open for 0% -> 0% of each run, Pallas kernels for 10% -> 9%
where the time goes in v34:
time: 30.1 us; the launch traced here: 29.9 us
  starting transfers between devices  15.8 us (52%)
  waiting for transfers between devices  8.22 us (27%)
  Pallas kernels  4.27 us (14%)
  local copies, waits for them, and re-layouts  0.9 us (3%)
  between operations  0.72 us (2%)
    ppermute x4, starting transfers between devices, along(): return lax.ppermute(array, 'shard', pairs)  11.4 us
    ppermute x4, waiting for transfers between devices, along(): return lax.ppermute(array, 'shard', pairs)  4.66 us
    ppermute x3, starting transfers between devices, across(): return lax.ppermute(array, 'shard', [(at, at ^ 1) for at in range(shards)])  4.37 us
    ppermute x3, waiting for transfers between devices, across(): return lax.ppermute(array, 'shard', [(at, at ^ 1) for at in range(shards)])  2.63 us
    pallas_call x1, Pallas kernels, first(): pl.pallas_call(first_kernel, out_shape=[shape(queries, width, dtype=bf16)...  1.19 us
    pallas_call x1, Pallas kernels, more(): pl.pallas_call(more_kernel, out_shape=[shape(queries, 128), shape(queries...  1.06 us
    pallas_call x1, Pallas kernels, local(): pl.pallas_call(combine_kernel, out_shape=[shape(1, count), shape(count, w...  0.95 us
    ppermute x2, waiting for transfers between devices, swap(): lax.ppermute(array, 'owner', [(at, lanes - 1 - at) for at in range(lanes)])  0.93 us
  transfers between devices with their start and end apart: 9, of which 6 were waited for; matrix products, arithmetic and copies ran while one was open for 0% of the time, Pallas kernels for 9%

profile of v34, /device:TPU:0, one launch (start us, length us, event | category | flops | bytes accessed | tf_op | source)
XLA Modules:
  0.0 29.9 jit_solution(4725366440738243668)
XLA Ops:
  0.6 0.0 copy-start
  0.6 0.0 copy-start.1
  0.7 0.0 copy-start.2
  0.7 0.9 %copy-done = bf16[128,768]{1,0:T(8,128)(2,1)S(1)} copy-done((bf16[128,768]{1,0:T(8,128)(2,1)S(1)}, bf16[128,768]{1,0:T(8,128)(2,1)}, u32[]{:S(2)}) %copy-start) | copy-done | bytes 196632
  1.6 0.0 copy-done.1
  1.6 0.0 copy-done.2
  1.6 3.0 %collective-permute-start.1 = (bf16[97,8,128]{2,1,0:T(8,128)(2,1)S(1)}, bf16[97,8,128]{2,1,0:T(8,128)(2,1)S(1)}, u32[]{:S(2)}, u32[]{:S(2)}) collective-permute-start(bf16[97,8,128]{2,1,0:T(8,128)(2,1)S(1)} %pack.1.own_ref), channel_id=1, source_target_pairs={{0,2},{2,0},{4,6},{6,4},{8,10},{10,8},{12,14},{14,12},{1,3},{3,1},... | collective-permute-start | bytes 595976 | tf_op jit(solution)/shard_map/ppermute | solution.py:179
  4.6 2.6 %collective-permute-start.2 = (bf16[97,8,128]{2,1,0:T(8,128)(2,1)S(1)}, bf16[97,8,128]{2,1,0:T(8,128)(2,1)S(1)}, u32[]{:S(2)}, u32[]{:S(2)}) collective-permute-start(bf16[97,8,128]{2,1,0:T(8,128)(2,1)S(1)} %pack.1.own_ref), channel_id=1, source_target_pairs={{0,8},{2,10},{8,12},{10,14},{12,4},{14,6},{4,0},{6,2},{1,9},{3,11}... | collective-permute-start | bytes 595976 | tf_op jit(solution)/shard_map/ppermute | solution.py:176
  7.2 0.0 collective-permute-start.4
  7.2 2.4 %collective-permute-done.1.refs_0_ = bf16[97,8,128]{2,1,0:T(8,128)(2,1)S(1)} collective-permute-done((bf16[97,8,128]{2,1,0:T(8,128)(2,1)S(1)}, bf16[97,8,128]{2,1,0:T(8,128)(2,1)S(1)}, u32[]{:S(2)}, u32[]{:S(2)}) %collective-permute-start.1) | collective-permute-done | bytes 198688 | tf_op jit(solution)/shard_map/ppermute | solution.py:179
  9.5 3.1 %collective-permute-done.2.refs_1_ = bf16[97,8,128]{2,1,0:T(8,128)(2,1)S(1)} collective-permute-done((bf16[97,8,128]{2,1,0:T(8,128)(2,1)S(1)}, bf16[97,8,128]{2,1,0:T(8,128)(2,1)S(1)}, u32[]{:S(2)}, u32[]{:S(2)}) %collective-permute-start.2) | collective-permute-done | bytes 198688 | tf_op jit(solution)/shard_map/ppermute | solution.py:176
  12.6 0.5 %collective-permute-start.3 = (bf16[97,8,128]{2,1,0:T(8,128)(2,1)S(1)}, bf16[97,8,128]{2,1,0:T(8,128)(2,1)S(1)}, u32[]{:S(2)}, u32[]{:S(2)}) collective-permute-start(bf16[97,8,128]{2,1,0:T(8,128)(2,1)S(1)} %collective-permute-done.2.refs_1_), channel_id=1, source_target_pairs={{0,2},{2,0},{4,6},{6,4},{8,10},{10,8},{12,14},{14,12},{1,3},{3,1},... | collective-permute-start | bytes 595976 | tf_op jit(solution)/shard_map/ppermute | solution.py:179
  13.1 0.0 collective-permute-start
  13.1 3.4 %collective-permute-start.5 = (bf16[97,8,128]{2,1,0:T(8,128)(2,1)S(1)}, bf16[97,8,128]{2,1,0:T(8,128)(2,1)S(1)}, u32[]{:S(2)}, u32[]{:S(2)}) collective-permute-start(bf16[97,8,128]{2,1,0:T(8,128)(2,1)S(1)} %collective-permute-done.2.refs_1_), channel_id=1, source_target_pairs={{0,8},{2,10},{8,12},{10,14},{12,4},{14,6},{4,0},{6,2},{1,9},{3,11}... | collective-permute-start | bytes 595976 | tf_op jit(solution)/shard_map/ppermute | solution.py:176
  16.5 0.7 %collective-permute-done.4.refs_0_ = bf16[97,8,128]{2,1,0:T(8,128)(2,1)S(1)} collective-permute-done((bf16[97,8,128]{2,1,0:T(8,128)(2,1)S(1)}, bf16[97,8,128]{2,1,0:T(8,128)(2,1)S(1)}, u32[]{:S(2)}, u32[]{:S(2)}) %collective-permute-start.4) | collective-permute-done | bytes 198688 | tf_op jit(solution)/shard_map/ppermute | solution.py:176
  17.2 0.8 %collective-permute-start.6 = (bf16[97,8,128]{2,1,0:T(8,128)(2,1)S(1)}, bf16[97,8,128]{2,1,0:T(8,128)(2,1)S(1)}, u32[]{:S(2)}, u32[]{:S(2)}) collective-permute-start(bf16[97,8,128]{2,1,0:T(8,128)(2,1)S(1)} %collective-permute-done.4.refs_0_), channel_id=1, source_target_pairs={{0,2},{2,0},{4,6},{6,4},{8,10},{10,8},{12,14},{14,12},{1,3},{3,1},... | collective-permute-start | bytes 595976 | tf_op jit(solution)/shard_map/ppermute | solution.py:179
  18.0 0.3 collective-permute-done.3.refs_2_
  18.3 5.4 %collective-permute-start.7 = (bf16[97,8,128]{2,1,0:T(8,128)(2,1)S(1)}, bf16[97,8,128]{2,1,0:T(8,128)(2,1)S(1)}, u32[]{:S(2)}, u32[]{:S(2)}) collective-permute-start(bf16[97,8,128]{2,1,0:T(8,128)(2,1)S(1)} %collective-permute-done.3.refs_2_), channel_id=1, source_target_pairs={{0,8},{2,10},{8,12},{10,14},{12,4},{14,6},{4,0},{6,2},{1,9},{3,11}... | collective-permute-start | bytes 595976 | tf_op jit(solution)/shard_map/ppermute | solution.py:176
  23.7 0.0 collective-permute-done.other_ref
  23.7 1.2 %first_scores.1 = (bf16[256,768]{1,0:T(8,128)(2,1)S(1)}, f32[256,128]{1,0:T(8,128)S(1)}, f32[256,128]{1,0:T(8,128)S(1)}, f32[256,768]{1,0:T(8,128)S(1)}) custom-call(bf16[97,8,128]{2,1,0:T(8,128)(2,1)S(1)} %pack.1.own_ref, bf16[97,8,128]{2,1,0:T(8,128)(2,1)S(1)} %collective-permute-done.other_ref, bf16[97,8,128]{2,1,0:T(8,128)(2,1)S(1)} %collective-permute-done.1.refs_0_, ...), custom_call_target="tpu_custom_call" | custom-call | flops 40265318400 | bytes 2359296 | tf_op jit(solution)/shard_map/first_scores/pallas_call | solution.py:185
  24.9 0.0 collective-permute-done.5.refs_1_
  24.9 0.0 collective-permute-done.6.refs_2_
  24.9 1.1 %more_scores.1 = (f32[256,128]{1,0:T(8,128)S(1)}, f32[256,768]{1,0:T(8,128)S(1)}) custom-call(bf16[256,768]{1,0:T(8,128)(2,1)S(1)} %get-tuple-element.16.unit_ref, f32[256,128]{1,0:T(8,128)S(1)} %get-tuple-element.17.side_ref, f32[256,128]{1,0:T(8,128)S(1)} %get-tuple-element.18.old_sums_ref, ...), custom_call_target="tpu_custom_call", output_to_operand_aliasing={{0}: (2, {}), {1}: (3, {})} | custom-call | flops 30198988800 | bytes 2162688 | tf_op jit(solution)/shard_map/more_scores/pallas_call | solution.py:199
  26.0 0.9 %collective-permute-done.7.refs_0_ = bf16[97,8,128]{2,1,0:T(8,128)(2,1)S(1)} collective-permute-done((bf16[97,8,128]{2,1,0:T(8,128)(2,1)S(1)}, bf16[97,8,128]{2,1,0:T(8,128)(2,1)S(1)}, u32[]{:S(2)}, u32[]{:S(2)}) %collective-permute-start.7) | collective-permute-done | bytes 198688 | tf_op jit(solution)/shard_map/ppermute | solution.py:176
  26.9 0.5 %send_scores.1 = bf16[136,768]{1,0:T(8,128)(2,1)S(1)} custom-call(bf16[256,768]{1,0:T(8,128)(2,1)S(1)} %get-tuple-element.16.unit_ref, f32[256,128]{1,0:T(8,128)S(1)} %get-tuple-element.17.side_ref, f32[256,128]{1,0:T(8,128)S(1)} %get-tuple-element.20.old_sums_ref, f32[256,768]{1,0:T(8,128)S(1)} %get-tuple-element.21.old_mixed_ref, ...), custom_call_target="tpu_custom_call" | custom-call | flops 5033164800 | bytes 983040 | tf_op jit(solution)/shard_map/send_scores/pallas_call | solution.py:209
  27.5 0.1 collective-permute-start.8
  27.5 0.5 %keep_scores.1 = (f32[128,128]{1,0:T(8,128)S(1)}, f32[128,768]{1,0:T(8,128)S(1)}) custom-call(bf16[256,768]{1,0:T(8,128)(2,1)S(1)} %get-tuple-element.16.unit_ref, f32[256,128]{1,0:T(8,128)S(1)} %get-tuple-element.17.side_ref, f32[256,128]{1,0:T(8,128)S(1)} %get-tuple-element.20.old_sums_ref, f32[256,768]{1,0:T(8,128)S(1)} %get-tuple-element.21.old_mixed_ref, ...), custom_call_target="tpu_custom_call" | custom-call | flops 5033164800 | bytes 983040 | tf_op jit(solution)/shard_map/keep_scores/pallas_call | solution.py:216
  28.1 0.9 %collective-permute-done.8.got_ref = bf16[136,768]{1,0:T(8,128)(2,1)S(1)} collective-permute-done((bf16[136,768]{1,0:T(8,128)(2,1)S(1)}, bf16[136,768]{1,0:T(8,128)(2,1)S(1)}, u32[]{:S(2)}, u32[]{:S(2)}) %collective-permute-start.8) | collective-permute-done | bytes 208928 | tf_op jit(solution)/shard_map/ppermute | solution.py:182
  29.0 1.0 %combine.1 = (f32[1,128]{1,0:T(1,128)}, f32[128,768]{1,0:T(8,128)}) custom-call(f32[128,128]{1,0:T(8,128)S(1)} %get-tuple-element.22.sums_ref, f32[128,768]{1,0:T(8,128)S(1)} %get-tuple-element.23.mixed_ref, bf16[136,768]{1,0:T(8,128)(2,1)S(1)} %collective-permute-done.8.got_ref), custom_call_target="tpu_custom_call" | custom-call | tf_op jit(solution)/shard_map/combine/pallas_call | solution.py:263
  (2 shorter events, 0.0 us)
Async XLA Ops:
  0.6 0.9 %copy-start = (bf16[128,768]{1,0:T(8,128)(2,1)S(1)}, bf16[128,768]{1,0:T(8,128)(2,1)}, u32[]{:S(2)}) copy-start(bf16[128,768]{1,0:T(8,128)(2,1)} %param.3) | copy-start | bytes 589828
  0.6 0.9 %copy-start.1 = (s32[128,1]{0,1:T(1,128)S(1)}, s32[128,1]{0,1:T(1,128)}, u32[]{:S(2)}) copy-start(s32[128,1]{0,1:T(1,128)} %param.4) | copy-start | bytes 1540
  0.7 0.9 %copy-start.2 = (s32[128]{0:T(128)S(1)}, s32[128]{0:T(128)}, u32[]{:S(2)}) copy-start(s32[128]{0:T(128)} %param.5) | copy-start | bytes 1540
  1.6 7.9 %collective-permute-start.1 = (bf16[97,8,128]{2,1,0:T(8,128)(2,1)S(1)}, bf16[97,8,128]{2,1,0:T(8,128)(2,1)S(1)}, u32[]{:S(2)}, u32[]{:S(2)}) collective-permute-start(bf16[97,8,128]{2,1,0:T(8,128)(2,1)S(1)} %pack.1.own_ref), channel_id=1, source_target_pairs={{0,2},{2,0},{4,6},{6,4},{8,10},{10,8},{12,14},{14,12},{1,3},{3,1},... | collective-permute-start | bytes 595976 | tf_op jit(solution)/shard_map/ppermute | solution.py:179
  4.6 8.0 %collective-permute-start.2 = (bf16[97,8,128]{2,1,0:T(8,128)(2,1)S(1)}, bf16[97,8,128]{2,1,0:T(8,128)(2,1)S(1)}, u32[]{:S(2)}, u32[]{:S(2)}) collective-permute-start(bf16[97,8,128]{2,1,0:T(8,128)(2,1)S(1)} %pack.1.own_ref), channel_id=1, source_target_pairs={{0,8},{2,10},{8,12},{10,14},{12,4},{14,6},{4,0},{6,2},{1,9},{3,11}... | collective-permute-start | bytes 595976 | tf_op jit(solution)/shard_map/ppermute | solution.py:176
  7.2 10.0 %collective-permute-start.4 = (bf16[97,8,128]{2,1,0:T(8,128)(2,1)S(1)}, bf16[97,8,128]{2,1,0:T(8,128)(2,1)S(1)}, u32[]{:S(2)}, u32[]{:S(2)}) collective-permute-start(bf16[97,8,128]{2,1,0:T(8,128)(2,1)S(1)} %pack.1.own_ref), channel_id=1, source_target_pairs={{0,4},{2,6},{8,0},{10,2},{12,8},{14,10},{4,12},{6,14},{1,5},{3,7},... | collective-permute-start | bytes 595976 | tf_op jit(solution)/shard_map/ppermute | solution.py:176
  12.6 5.7 %collective-permute-start.3 = (bf16[97,8,128]{2,1,0:T(8,128)(2,1)S(1)}, bf16[97,8,128]{2,1,0:T(8,128)(2,1)S(1)}, u32[]{:S(2)}, u32[]{:S(2)}) collective-permute-start(bf16[97,8,128]{2,1,0:T(8,128)(2,1)S(1)} %collective-permute-done.2.refs_1_), channel_id=1, source_target_pairs={{0,2},{2,0},{4,6},{6,4},{8,10},{10,8},{12,14},{14,12},{1,3},{3,1},... | collective-permute-start | bytes 595976 | tf_op jit(solution)/shard_map/ppermute | solution.py:179
  13.1 10.6 %collective-permute-start = (bf16[97,8,128]{2,1,0:T(8,128)(2,1)S(1)}, bf16[97,8,128]{2,1,0:T(8,128)(2,1)S(1)}, u32[]{:S(2)}, u32[]{:S(2)}) collective-permute-start(bf16[97,8,128]{2,1,0:T(8,128)(2,1)S(1)} %pack.1.own_ref), channel_id=1, source_target_pairs={{0,1},{1,0},{2,3},{3,2},{4,5},{5,4},{6,7},{7,6},{8,9},{9,8},{10,11... | collective-permute-start | bytes 595976 | tf_op jit(solution)/shard_map/ppermute | solution.py:182
  13.1 11.8 %collective-permute-start.5 = (bf16[97,8,128]{2,1,0:T(8,128)(2,1)S(1)}, bf16[97,8,128]{2,1,0:T(8,128)(2,1)S(1)}, u32[]{:S(2)}, u32[]{:S(2)}) collective-permute-start(bf16[97,8,128]{2,1,0:T(8,128)(2,1)S(1)} %collective-permute-done.2.refs_1_), channel_id=1, source_target_pairs={{0,8},{2,10},{8,12},{10,14},{12,4},{14,6},{4,0},{6,2},{1,9},{3,11}... | collective-permute-start | bytes 595976 | tf_op jit(solution)/shard_map/ppermute | solution.py:176
  17.2 7.7 %collective-permute-start.6 = (bf16[97,8,128]{2,1,0:T(8,128)(2,1)S(1)}, bf16[97,8,128]{2,1,0:T(8,128)(2,1)S(1)}, u32[]{:S(2)}, u32[]{:S(2)}) collective-permute-start(bf16[97,8,128]{2,1,0:T(8,128)(2,1)S(1)} %collective-permute-done.4.refs_0_), channel_id=1, source_target_pairs={{0,2},{2,0},{4,6},{6,4},{8,10},{10,8},{12,14},{14,12},{1,3},{3,1},... | collective-permute-start | bytes 595976 | tf_op jit(solution)/shard_map/ppermute | solution.py:179
  18.3 8.6 %collective-permute-start.7 = (bf16[97,8,128]{2,1,0:T(8,128)(2,1)S(1)}, bf16[97,8,128]{2,1,0:T(8,128)(2,1)S(1)}, u32[]{:S(2)}, u32[]{:S(2)}) collective-permute-start(bf16[97,8,128]{2,1,0:T(8,128)(2,1)S(1)} %collective-permute-done.3.refs_2_), channel_id=1, source_target_pairs={{0,8},{2,10},{8,12},{10,14},{12,4},{14,6},{4,0},{6,2},{1,9},{3,11}... | collective-permute-start | bytes 595976 | tf_op jit(solution)/shard_map/ppermute | solution.py:176
  27.5 1.5 %collective-permute-start.8 = (bf16[136,768]{1,0:T(8,128)(2,1)S(1)}, bf16[136,768]{1,0:T(8,128)(2,1)S(1)}, u32[]{:S(2)}, u32[]{:S(2)}) collective-permute-start(bf16[136,768]{1,0:T(8,128)(2,1)S(1)} %send_scores.1), channel_id=1, source_target_pairs={{0,1},{1,0},{2,3},{3,2},{4,5},{5,4},{6,7},{7,6},{8,9},{9,8},{10,11... | collective-permute-start | bytes 626696 | tf_op jit(solution)/shard_map/ppermute | solution.py:182
